TPU v7x, 32 devices: a whole 2x2x4 slice. The times are simulated.
32 devices in a mesh: dp: 16 (over z, x, core), group: 2 (over y).
Axes of the slice: x: 2, y: 2, z: 4, core: 2. Of those that a mesh axis runs over, the one named last changes fastest.
Arguments:
- patches: bfloat16 [4, 8192, 512], P('group', 'dp'), may hold values from -6 to 6
- cotangents: bfloat16 [4, 8192, 512], P('group', 'dp'), may hold values from -6 to 6
- newton_counts: int32 [4, 2], P('group'), may hold values from 2 to 4
Outputs:
- update: bfloat16 [4, 512, 512], P(None, 'dp')
All inputs are finite; a program needn't handle non-finite values.
Results may differ from a plain program's by a relative error of at most 0.012.
The roundings to bfloat16 on the way count: a program that leaves them out, or rounds other values in their place, can miss the bound.
Values may be sent and summed in bfloat16 or wider, within the bound.
No kernel may reach another device: no remote copies, remote signals or barrier semaphores. Data moves between devices by JAX's collectives and lax.ppermute only.
A program may use at most 64 MiB of HBM per device.

v0:
```python
import jax
import jax.numpy as jnp
from jax import lax
from jax.sharding import PartitionSpec as P


def spread(x, axis, root):
    mine = lax.axis_index(axis) == root
    return lax.psum(jnp.where(mine, x, jnp.zeros_like(x)), axis)


def half_dot(left_mat, right_mat):
    return jnp.dot(
        left_mat.astype(jnp.bfloat16),
        right_mat.astype(jnp.bfloat16),
        preferred_element_type=jnp.float32,
    )


def newton_root(matrix, count):
    order = matrix.shape[0]
    eye = jnp.eye(order, dtype=jnp.float32)
    scale = 5.0 / (2.0 * jnp.sqrt(jnp.sum(matrix * matrix)))
    start = (scale**0.25 * eye, scale * matrix)

    def sweep(index, carry):
        current, moment = carry
        factor = (5.0 * eye - moment) / 4.0
        square = half_dot(factor, factor)
        fourth = half_dot(square, square)
        return (half_dot(current, factor), half_dot(fourth, moment))

    final, moment = lax.fori_loop(0, count, sweep, start)
    return final.astype(jnp.bfloat16)


def side_root(grad, side, count):
    order = grad.shape[0]
    eye = jnp.eye(order, dtype=jnp.float32)
    if side == 0:
        stats = jnp.dot(grad, grad.T, precision=lax.Precision.HIGHEST) + 0.1 * eye
    else:
        stats = jnp.dot(grad.T, grad, precision=lax.Precision.HIGHEST) + 0.1 * eye
    return newton_root(stats, count)


def shards(patches, cotangents, newton_counts):
    blocks = patches.shape[0]
    width = patches.shape[2]
    devices = lax.axis_size("dp")
    total_pix = patches.shape[1] * devices
    terms = jnp.einsum("kpi,kpj->kij", patches, cotangents, preferred_element_type=jnp.float32)
    terms = terms / jnp.sqrt(jnp.float32(total_pix * width))
    grads = lax.psum(terms, "dp")
    mine = lax.axis_index("dp")
    rows = width // devices
    start = mine * rows
    results = []
    for block in range(blocks):
        grad = grads[block]
        found = []
        for side in range(2):
            number = 2 * block + side
            count = newton_counts[block, side]
            local_root = lax.cond(
                mine == number,
                lambda: side_root(grad, side, count),
                lambda: jnp.zeros((width, width), jnp.bfloat16),
            )
            found.append(spread(local_root, "dp", number))
        left_rows = lax.dynamic_slice_in_dim(found[0], start, rows, 0)
        partial_value = jnp.dot(
            left_rows, grad.astype(jnp.bfloat16), preferred_element_type=jnp.float32
        ).astype(jnp.bfloat16)
        results.append(
            jnp.dot(partial_value, found[1], preferred_element_type=jnp.float32).astype(
                jnp.bfloat16
            )
        )
    stacked = jnp.stack(results, 0)
    return lax.all_gather(stacked, "group", axis=0, tiled=True)


def solution(mesh):
    placed = (P("group", "dp", None), P("group", "dp", None), P("group", None))
    return jax.shard_map(
        shards, mesh=mesh, in_specs=placed, out_specs=P(None, "dp", None), check_vma=False
    )
```

profile of v0, /device:TPU:0, one launch (start us, length us, event | category | flops | bytes accessed | tf_op | source)
XLA Modules:
  0.0 263.7 jit_solution(17821239501755863228)
XLA Ops:
  6.5 0.0 copy-start
  6.5 0.0 all-reduce.4.cloned.1.call-start
  6.5 1.2 copy-done
  7.8 3.3 %convolution_multiply_fusion = f32[2,512,512]{2,1,0:T(8,128)} fusion(bf16[2,512,512]{2,1,0:T(8,128)(2,1)S(1)} %copy-done, bf16[2,512,512]{2,1,0:T(8,128)(2,1)} %param.20), kind=kOutput, calls=%fused_computation.88 | convolution fusion | flops 537395200 | bytes 4194304 | tf_op jit(solution)/shard_map/kpi,kpj->kij/dot_general | solution.py:52
  11.1 0.0 all-reduce.4.cloned.1.call-update
  11.1 0.0 all-reduce.6.cloned.1.call-start
  11.1 0.0 copy-start.2
  11.2 100.6 %all-reduce.4.cloned.1.call-done = f32[2,512,512]{2,1,0:T(8,128)} async-done(((f32[2,512,512]{2,1,0:T(8,128)}), f32[2,512,512]{2,1,0:T(8,128)}) %all-reduce.4.cloned.1.call-update) | async-done | bytes 2097168 | tf_op jit(solution)/shard_map/psum | solution.py:54
  111.8 3.0 %slice_bitcast_fusion.1 = (f32[512,512]{1,0:T(8,128)}, f32[512,512]{1,0:T(8,128)}) fusion(f32[2,512,512]{2,1,0:T(8,128)} %all-reduce.4.cloned.1.call-done), kind=kLoop, calls=%fused_computation.96 | loop fusion | bytes 4194304 | tf_op jit(solution)/shard_map/squeeze | solution.py:60
  114.8 0.0 copy-done.2
  114.8 20.1 %conditional.4 = (bf16[512,512]{0,1:T(8,128)(2,1)}) conditional(s32[]{:T(128)} %convert_element_type.130, () %tuple.45, (f32[512,512]{1,0:T(8,128)}, s32[2,2]{1,0:T(2,128)S(1)}) %tuple.135), branch_computations={%region_1.0_spmd, %region_2.0_spmd} | conditional | flops 2689859584 | bytes 15204529 | solution.py:65
  114.8 4.2 %multiply_reduce_fusion = (f32[]{:T(128)}, f32[512,512]{1,0:T(8,128)S(1)}) fusion(f32[512,512]{1,0:T(8,128)} %get-tuple-element.128), kind=kOutput, calls=%fused_computation.21 | convolution fusion | flops 1611923456 | bytes 2097156 | tf_op jit(solution)/shard_map/cond/branch_1_fun/dot_general | solution.py:41
  119.7 0.1 broadcast_multiply_fusion
  119.9 1.0 copy.9
  120.9 0.5 slice.16
  121.4 13.5 %while.48 = (s32[]{:T(128)}, bf16[512,512]{0,1:T(8,128)(2,1)}, f32[512,512]{1,0:T(8,128)S(1)}, s32[]{:T(128)}, s32[]{:T(128)}) while((s32[]{:T(128)}, bf16[512,512]{0,1:T(8,128)(2,1)}, f32[512,512]{1,0:T(8,128)S(1)}, s32[]{:T(128)}, s32[]{:T(128)}) %tuple.119), condition=%wide.region_5.0_spmd.clone, body=%wide.region_4.0_spmd.clone.sunk | while | flops 1077149696 | bytes 9437245 | solution.py:33
  122.1 0.1 copy.88
  122.2 1.0 copy.87
  123.2 1.3 convolution_bitcast_fusion.11
  124.5 1.9 convolution_convert_fusion.19
  126.4 1.5 fusion.161
  128.5 0.1 copy.88
  128.6 1.0 copy.87
  129.6 1.3 convolution_bitcast_fusion.11
  130.9 1.9 convolution_convert_fusion.19
  132.8 1.5 fusion.161
  134.9 0.8 conditional.5
  134.9 0.8 broadcast.56
  135.8 2.1 broadcast_select_fusion.2
  137.9 0.8 conditional.6
  137.9 0.8 broadcast.61
  138.7 0.8 conditional.7
  138.7 0.8 broadcast.66
  139.5 0.0 copy-start.1
  139.5 1.1 broadcast_select_fusion
  140.6 0.0 all-reduce.6.cloned.1.call-update
  140.6 107.4 %all-reduce.6.cloned.1.call-done = (bf16[512,512]{0,1:T(8,128)(2,1)}, bf16[512,512]{0,1:T(8,128)(2,1)}, bf16[512,512]{0,1:T(8,128)(2,1)}, bf16[512,512]{0,1:T(8,128)(2,1)}) async-done(((bf16[512,512]{0,1:T(8,128)(2,1)}, bf16[512,512]{0,1:T(8,128)(2,1)}, bf16[512,512]{0,1:T(8,128)(2,1)}, bf16[512,512]{0,1:T(8,128)(2,1)}), (bf16[512,512]{0,1:T(8,128)(2,1)}, bf16[512,512]{0,1:T(8,128)(2,1)}, ...) | async-done | bytes 2097168 | tf_op jit(solution)/shard_map/psum | solution.py:9
  248.1 0.0 copy-done.1
  248.1 1.6 fusion.80
  249.6 1.6 fusion.81
  251.3 4.9 %all_gather.3 = bf16[4,32,512]{2,1,0:T(8,128)(2,1)S(1)} all-gather(bf16[2,32,512]{2,1,0:T(8,128)(2,1)S(1)} %pad_maximum_fusion), channel_id=1, replica_groups=mesh['dp'=16,'group'=2] {'group'}, dimensions={0}, use_global_device_ids=true | all-gather | bytes 196608 | tf_op jit(solution)/shard_map/all_gather | solution.py:81
  256.2 0.7 copy.89
  (2 shorter events, 0.1 us)
Async XLA Ops:
  6.5 1.2 copy-start
  6.5 105.2 %all-reduce.4.cloned.1.call-start = ((), (), s32[]{:S(2)}) async-start(), calls=%async_computation | async-start | bytes 4194304 | tf_op jit(solution)/shard_map/psum | solution.py:54
  11.1 237.0 %all-reduce.6.cloned.1.call-start = ((), (), s32[]{:S(2)}) async-start(), calls=%async_computation.1 | async-start | bytes 4194304 | tf_op jit(solution)/shard_map/psum | solution.py:9
  11.1 103.7 %copy-start.2 = (s32[2,2]{1,0:T(2,128)S(1)}, s32[2,2]{1,0:T(2,128)}, u32[]{:S(2)}) copy-start(s32[2,2]{1,0:T(2,128)} %param.21) | copy-start | bytes 52
  139.5 108.5 %copy-start.1 = (f32[2,512,512]{2,1,0:T(8,128)S(1)}, f32[2,512,512]{2,1,0:T(8,128)}, u32[]{:S(2)}) copy-start(f32[2,512,512]{2,1,0:T(8,128)} %all-reduce.4.cloned.1.call-done) | copy-start | bytes 6291460
Sparse Core Ops, SparseCore 0:
  11.2 100.5 all-reduce.3
  140.7 107.2 all-reduce.5
where the time goes:
time: 265 us; the launch traced here: 264 us
  waiting for transfers between devices  208 us (78%)
  matrix products  19.9 us (8%)
  between operations  13.4 us (5%)
  local copies, waits for them, and re-layouts  11.2 us (4%)
  blocking collectives  4.94 us (2%)
  other arithmetic  3.33 us (1%)
  loops' own time  2.77 us (1%)
    psum x1, waiting for transfers between devices, spread(): return lax.psum(jnp.where(mine, x, jnp.zeros_like(x)), axis)  107 us
    psum x1, waiting for transfers between devices, shards(): grads = lax.psum(terms, 'dp')  101 us
    dot_general x6, matrix products, half_dot(): jnp.dot(left_mat.astype(jnp.bfloat16), right_mat.astype(jnp.bfloat16), pr...  9.28 us
  transfers between devices with their start and end apart: 2, of which 2 were waited for; matrix products, arithmetic and copies ran while one was open for 0% of the time, Pallas kernels for 0%

commit v1 on v0

v1 whole, which is shorter than its diff:
```python
import functools

import jax
import jax.numpy as jnp
from jax import lax
from jax.experimental import pallas as pl
from jax.experimental.pallas import tpu as pltpu
from jax.sharding import PartitionSpec as P

F32 = jnp.float32
BF16 = jnp.bfloat16
VMEM = pl.BlockSpec(memory_space=pltpu.VMEM)
SMEM = pl.BlockSpec(memory_space=pltpu.SMEM)
ROWS_IN_COLS = (((0,), (0,)), ((), ()))
COLS_IN_COLS = (((1,), (1,)), ((), ()))


def params(limit):
    return pltpu.CompilerParams(vmem_limit_bytes=limit << 20)


def gram_kernel(scale, where_ref, patch_ref, cot_ref, out_ref):
    terms = lax.dot_general(patch_ref[0], cot_ref[0], ROWS_IN_COLS, preferred_element_type=F32)
    out_ref[0] = (terms * scale).astype(out_ref.dtype)


def gram(where, patches, cotangents, scale, dtype):
    count = where.shape[0]
    _, pix, width = patches.shape
    half = width // 2
    return pl.pallas_call(
        functools.partial(gram_kernel, scale),
        out_shape=jax.ShapeDtypeStruct((count, half, width), dtype),
        grid_spec=pltpu.PrefetchScalarGridSpec(
            num_scalar_prefetch=1,
            grid=(count,),
            in_specs=[
                pl.BlockSpec((1, pix, half), lambda m, where: (where[m, 0], 0, where[m, 1])),
                pl.BlockSpec((1, pix, width), lambda m, where: (where[m, 0], 0, 0)),
            ],
            out_specs=pl.BlockSpec((1, half, width), lambda m, where: (m, 0, 0)),
        ),
        compiler_params=params(16),
        cost_estimate=pl.CostEstimate(
            flops=2 * count * pix * half * width,
            bytes_accessed=2 * count * pix * (half + width),
            transcendentals=0,
        ),
    )(where, patches, cotangents)


def split_kernel(place_ref, kept_ref, came_ref, own_ref, *piece_refs):
    rows = own_ref.shape[0]
    place = place_ref[0]

    def piece(offset):
        where = pl.ds(pl.multiple_of((place ^ offset) * rows, rows), rows)
        return kept_ref[where, :] + came_ref[where, :].astype(F32)

    own_ref[...] = piece(0)
    for index, ref in enumerate(piece_refs):
        ref[...] = piece(index + 1).astype(BF16)


def split(place, kept, came, line):
    rows, width = kept.shape
    part = rows // line
    return pl.pallas_call(
        split_kernel,
        out_shape=[jax.ShapeDtypeStruct((part, width), F32)]
        + [jax.ShapeDtypeStruct((part, width), BF16)] * (line - 1),
        in_specs=[SMEM, VMEM, VMEM],
        out_specs=[VMEM] * line,
        compiler_params=params(16),
    )(place, kept, came)


def root_kernel(count_pieces, scalar_ref, *refs):
    pieces = refs[:count_pieces]
    out_ref, grad, q_left, q_right, m_left, m_right, x_left, x_right = refs[count_pieces:]
    part = pieces[0].shape[0]
    width = grad.shape[0]
    for index, ref in enumerate(pieces):
        grad[part * index : part * (index + 1), :] = ref[...]
    diagonal = lax.broadcasted_iota(jnp.int32, (width, width), 0) == lax.broadcasted_iota(
        jnp.int32, (width, width), 1
    )

    def dot(a, b):
        return jnp.dot(a, b, preferred_element_type=F32)

    def factor(moment):
        return (jnp.where(diagonal, 1.25, 0.0) - 0.25 * moment).astype(BF16)

    def begin(dims):
        stats = lax.dot_general(grad[...], grad[...], dims, preferred_element_type=F32)
        stats = stats + jnp.where(diagonal, 0.1, 0.0)
        scale = 2.5 / jnp.sqrt(jnp.sum(stats * stats, keepdims=True))
        first = jnp.sqrt(jnp.sqrt(scale)).astype(BF16).astype(F32)
        return scale * stats, first

    rows = pl.ds(pl.multiple_of(scalar_ref[2], part), part)
    moment, first = begin(COLS_IN_COLS)
    m_left[...] = moment.astype(BF16)
    q_left[...] = factor(moment)
    x_left[...] = (first * q_left[rows, :].astype(F32)).astype(BF16)
    moment, first = begin(ROWS_IN_COLS)
    m_right[...] = moment.astype(BF16)
    factor_value = factor(moment)
    q_right[...] = factor_value
    x_right[...] = (first * factor_value.astype(F32)).astype(BF16)

    count_left, count_right = scalar_ref[0], scalar_ref[1]

    def sweep(index, carry):
        second_left = dot(q_left[...], q_left[...]).astype(BF16)
        second_right = dot(q_right[...], q_right[...]).astype(BF16)
        fourth_left = dot(second_left, second_left).astype(BF16)
        fourth_right = dot(second_right, second_right).astype(BF16)
        moment_left = dot(fourth_left, m_left[...])
        moment_right = dot(fourth_right, m_right[...])
        m_left[...] = moment_left.astype(BF16)
        m_right[...] = moment_right.astype(BF16)
        factor_left = factor(moment_left)
        factor_right = factor(moment_right)
        q_left[...] = factor_left
        q_right[...] = factor_right

        @pl.when(index < count_left)
        def _():
            x_left[...] = dot(x_left[...], factor_left).astype(BF16)

        @pl.when(index < count_right)
        def _():
            x_right[...] = dot(x_right[...], factor_right).astype(BF16)

        return carry

    lax.fori_loop(1, jnp.maximum(count_left, count_right), sweep, 0)
    partial_value = dot(x_left[...], grad[...]).astype(BF16)
    out_ref[...] = dot(partial_value, x_right[...]).astype(BF16)


def root(scalars, pieces):
    part, width = pieces[0].shape
    square = pltpu.VMEM((width, width), BF16)
    return pl.pallas_call(
        functools.partial(root_kernel, len(pieces)),
        out_shape=jax.ShapeDtypeStruct((part, width), BF16),
        in_specs=[SMEM] + [VMEM] * len(pieces),
        out_specs=VMEM,
        scratch_shapes=[square] * 5 + [pltpu.VMEM((part, width), BF16), square],
        compiler_params=params(32),
    )(scalars, *pieces)


def shards(groups, patches, cotangents, newton_counts):
    blocks, pix, width = patches.shape
    devices = lax.axis_size("dp")
    line = devices // 4
    half = width // 2
    part = half // line
    rows = part // 2
    scale = 1.0 / float(pix * devices * width) ** 0.5
    mine = lax.axis_index("dp")
    core, column, place = mine % 2, mine // 2 % 2, mine // 4

    def swap(array, mask):
        return lax.ppermute(array, "dp", [(i, i ^ mask) for i in range(devices)])

    away = jnp.stack([jnp.stack([1 - column, 1 - core]), jnp.stack([column, 1 - core])])
    home = jnp.stack([jnp.stack([1 - column, core]), jnp.stack([column, core])])
    given = gram(away, patches, cotangents, scale, BF16)
    came_other = swap(given[0], 1)
    came_own = swap(given[1], 1)
    kept = gram(home, patches, cotangents, scale, F32)
    came_column = swap((kept[0] + came_other.astype(F32)).astype(BF16), 2)
    pair = kept[1] + came_own.astype(F32)
    own, *others = split(place[None], pair, came_column, line)
    for offset, piece in enumerate(others, 1):
        own = own + swap(piece, 4 * offset).astype(F32)
    own = own.astype(BF16)
    near = [own] + [swap(own, 4 * offset) for offset in range(1, line)]
    far = [swap(piece, 1) for piece in near]

    target = 2 * place + core
    start = ((target // line) ^ core) * half + ((target % line) ^ place) * part
    counts = lax.dynamic_index_in_dim(newton_counts, column, 0, keepdims=False)
    update = root(jnp.concatenate([counts, start[None]]), near + far)

    group = lax.axis_index("group")
    found = []
    for turn in range(groups):
        pair_found = []
        for flip in range(2):
            moves = []
            for index in range(devices):
                high, col, cor = index // 4, index // 2 % 2, index % 2
                to = 4 * high + 2 * cor + (col ^ flip)
                for g in range(groups):
                    moves.append((index * groups + g, to * groups + (g + turn) % groups))
            piece = lax.dynamic_slice_in_dim(update, (column ^ flip) * rows, rows, 0)
            pair_found.append(lax.ppermute(piece, ("dp", "group"), moves))
        found.append(
            jnp.stack(
                [
                    jnp.where(core == 0, pair_found[0], pair_found[1]),
                    jnp.where(core == 0, pair_found[1], pair_found[0]),
                ]
            )
        )
    ordered = jnp.stack(found[::-1])
    ordered = jnp.roll(ordered, group + 1, axis=0)
    return ordered.reshape(blocks * groups, rows, width)


def solution(mesh):
    placed = (P("group", "dp", None), P("group", "dp", None), P("group", None))
    return jax.shard_map(
        functools.partial(shards, mesh.shape["group"]),
        mesh=mesh,
        in_specs=placed,
        out_specs=P(None, "dp", None),
        check_vma=False,
    )
```

time: 265 us -> 54.1 us (0.20)
  waiting for transfers between devices: 208 us -> 18.7 us
  matrix products: 19.9 us -> 0 us
  starting transfers between devices: 0.04 us -> 18.2 us
  between operations: 13.4 us -> 0.19 us
  Pallas kernels: 0 us -> 12.4 us
  local copies, waits for them, and re-layouts: 11.2 us -> 3 us
  blocking collectives: 4.94 us -> 0 us
  loops' own time: 2.77 us -> 0 us
    psum x2 -> x0, waiting for transfers between devices: 208 us -> none  [the longest x1 107 us: spread(): return lax.psum(jnp.where(mine, x, jnp.zeros_like(x)), axis)]
    dot_general x10 -> x0, matrix products: 19.9 us -> none  [the longest x6 9.28 us: half_dot(): jnp.dot(left_mat.astype(jnp.bfloat16), right_mat.astype(jnp.bfloat16), pr...]
    ppermute x0 -> x17, waiting for transfers between devices: none -> 18.7 us  [the longest x13 16.6 us: swap(): return lax.ppermute(array, 'dp', [(i, i ^ mask) for i in range(devices)])]
    ppermute x0 -> x17, starting transfers between devices: none -> 18.2 us  [the longest x13 12.7 us: swap(): return lax.ppermute(array, 'dp', [(i, i ^ mask) for i in range(devices)])]
    pallas_call x0 -> x4, Pallas kernels: none -> 12.4 us  [the longest x1 9.8 us: root(): pl.pallas_call(functools.partial(root_kernel, len(pieces)), out_shape=jax...]
    all_gather x1 -> x0, blocking collectives: 4.94 us -> none  [shards(): return lax.all_gather(stacked, 'group', axis=0, tiled=True)]
    select_n x2 -> x0, other arithmetic: 3.17 us -> none  [spread(): return lax.psum(jnp.where(mine, x, jnp.zeros_like(x)), axis)]
    squeeze x1 -> x2, local copies, waits for them, and re-layouts: 3.04 us -> 0.04 us  [the longest x1 0.04 us: shards(): came_other = swap(given[0], 1)]
  transfers between devices with their start and end apart: 2 -> 17, of which waited for: 2 -> 8; matrix products, arithmetic and copies ran while one was open for 0% -> 0% of each run, Pallas kernels for 0% -> 2%
where the time goes in v1:
time: 54.1 us; the launch traced here: 53.7 us
  waiting for transfers between devices  18.7 us (35%)
  starting transfers between devices  18.2 us (34%)
  Pallas kernels  12.4 us (23%)
  local copies, waits for them, and re-layouts  3 us (6%)
  other arithmetic  1.23 us (2%)
    ppermute x13, waiting for transfers between devices, swap(): return lax.ppermute(array, 'dp', [(i, i ^ mask) for i in range(devices)])  16.6 us
    ppermute x13, starting transfers between devices, swap(): return lax.ppermute(array, 'dp', [(i, i ^ mask) for i in range(devices)])  12.7 us
    pallas_call x1, Pallas kernels, root(): pl.pallas_call(functools.partial(root_kernel, len(pieces)), out_shape=jax...  9.8 us
    ppermute x4, starting transfers between devices, shards(): pair_found.append(lax.ppermute(piece, ('dp', 'group'), moves))  5.54 us
    unnamed x10, local copies, waits for them, and re-layouts  2.94 us
    pallas_call x2, Pallas kernels, gram(): pl.pallas_call(functools.partial(gram_kernel, scale), out_shape=jax.Shape...  2.6 us
    ppermute x4, waiting for transfers between devices, shards(): pair_found.append(lax.ppermute(piece, ('dp', 'group'), moves))  2.09 us
  transfers between devices with their start and end apart: 17, of which 8 were waited for; matrix products, arithmetic and copies ran while one was open for 0% of the time, Pallas kernels for 2%

profile of v1, /device:TPU:0, one launch (start us, length us, event | category | flops | bytes accessed | tf_op | source)
XLA Modules:
  0.0 53.7 jit_solution(15359148609966221495)
XLA Ops:
  0.0 0.0 copy-start
  0.0 0.1 add_bitcast_fusion.2
  0.1 0.0 copy-start.1
  0.1 1.2 %copy-done.1 = bf16[2,512,512]{2,1,0:T(8,128)(2,1)S(1)} copy-done((bf16[2,512,512]{2,1,0:T(8,128)(2,1)S(1)}, bf16[2,512,512]{2,1,0:T(8,128)(2,1)}, u32[]{:S(2)}) %copy-start.1) | copy-done | bytes 1048600
  1.3 0.0 copy-start.3
  1.3 1.2 %copy-done.3 = bf16[2,512,512]{2,1,0:T(8,128)(2,1)S(1)} copy-done((bf16[2,512,512]{2,1,0:T(8,128)(2,1)S(1)}, bf16[2,512,512]{2,1,0:T(8,128)(2,1)}, u32[]{:S(2)}) %copy-start.3) | copy-done | bytes 1048600
  2.5 0.0 copy-start.4
  2.5 1.3 %shard_map.38 = bf16[2,256,512]{2,1,0:T(8,128)(2,1)S(1)} custom-call(s32[2,2]{1,0:T(2,128)S(1)} %pad_add_fusion.1.where_ref, bf16[2,512,512]{2,1,0:T(8,128)(2,1)S(1)} %copy-done.1, bf16[2,512,512]{2,1,0:T(8,128)(2,1)S(1)} %copy-done.3), custom_call_target="tpu_custom_call" | custom-call | flops 268435456 | bytes 1572864 | tf_op jit(solution)/shard_map/pallas_call | solution.py:31
  3.9 0.0 copy-start.2
  3.9 0.5 collective-permute-start.1
  4.4 0.1 collective-permute-start
  4.5 0.1 add_bitcast_fusion
  4.6 0.0 copy-done.4
  4.6 0.5 copy-done.2
  5.1 1.3 %shard_map.37 = f32[2,256,512]{2,1,0:T(8,128)S(1)} custom-call(s32[2,2]{1,0:T(2,128)S(1)} %pad_add_fusion.where_ref, bf16[2,512,512]{2,1,0:T(8,128)(2,1)S(1)} %copy-done.2, bf16[2,512,512]{2,1,0:T(8,128)(2,1)S(1)} %copy-done.4), custom_call_target="tpu_custom_call" | custom-call | flops 268435456 | bytes 1572864 | tf_op jit(solution)/shard_map/pallas_call | solution.py:31
  6.4 0.0 collective-permute-done.1
  6.4 0.0 collective-permute-done
  6.4 0.1 fusion.1
  6.6 3.0 %collective-permute-start.2 = (bf16[256,512]{1,0:T(8,128)(2,1)S(1)}, bf16[256,512]{1,0:T(8,128)(2,1)S(1)}, u32[]{:S(2)}, u32[]{:S(2)}) collective-permute-start(bf16[256,512]{1,0:T(8,128)(2,1)S(1)} %get-tuple-element.13), channel_id=1, source_target_pairs={{0,4},{2,6},{4,0},{6,2},{8,12},{10,14},{12,8},{14,10},{16,20},{18,... | collective-permute-start | bytes 786440 | tf_op jit(solution)/shard_map/ppermute | solution.py:169
  9.6 6.3 %collective-permute-done.2.came_ref = bf16[256,512]{1,0:T(8,128)(2,1)S(1)} collective-permute-done((bf16[256,512]{1,0:T(8,128)(2,1)S(1)}, bf16[256,512]{1,0:T(8,128)(2,1)S(1)}, u32[]{:S(2)}, u32[]{:S(2)}) %collective-permute-start.2) | collective-permute-done | bytes 262176 | tf_op jit(solution)/shard_map/ppermute | solution.py:169
  15.9 3.9 %collective-permute-start.5 = (bf16[64,512]{1,0:T(8,128)(2,1)S(1)}, bf16[64,512]{1,0:T(8,128)(2,1)S(1)}, u32[]{:S(2)}, u32[]{:S(2)}) collective-permute-start(bf16[64,512]{1,0:T(8,128)(2,1)S(1)} %get-tuple-element.12), channel_id=1, source_target_pairs={{0,24},{2,26},{4,28},{6,30},{8,16},{10,18},{12,20},{14,22},{16,8},... | collective-permute-start | bytes 196616 | tf_op jit(solution)/shard_map/ppermute | solution.py:169
  19.8 0.0 collective-permute-start.4
  19.8 0.6 %collective-permute-start.3 = (bf16[64,512]{1,0:T(8,128)(2,1)S(1)}, bf16[64,512]{1,0:T(8,128)(2,1)S(1)}, u32[]{:S(2)}, u32[]{:S(2)}) collective-permute-start(bf16[64,512]{1,0:T(8,128)(2,1)S(1)} %get-tuple-element.10), channel_id=1, source_target_pairs={{0,8},{2,10},{4,12},{6,14},{8,0},{10,2},{12,4},{14,6},{16,24},{18,... | collective-permute-start | bytes 196616 | tf_op jit(solution)/shard_map/ppermute | solution.py:169
  20.5 2.0 %collective-permute-done.5 = bf16[64,512]{1,0:T(8,128)(2,1)S(1)} collective-permute-done((bf16[64,512]{1,0:T(8,128)(2,1)S(1)}, bf16[64,512]{1,0:T(8,128)(2,1)S(1)}, u32[]{:S(2)}, u32[]{:S(2)}) %collective-permute-start.5) | collective-permute-done | bytes 65568 | tf_op jit(solution)/shard_map/ppermute | solution.py:169
  22.5 2.7 %collective-permute-done.4 = bf16[64,512]{1,0:T(8,128)(2,1)S(1)} collective-permute-done((bf16[64,512]{1,0:T(8,128)(2,1)S(1)}, bf16[64,512]{1,0:T(8,128)(2,1)S(1)}, u32[]{:S(2)}, u32[]{:S(2)}) %collective-permute-start.4) | collective-permute-done | bytes 65568 | tf_op jit(solution)/shard_map/ppermute | solution.py:169
  25.2 0.0 collective-permute-done.3
  25.2 0.5 collective-permute-start.6
  25.8 2.3 %collective-permute-start.7 = (bf16[64,512]{1,0:T(8,128)(2,1)S(1)}, bf16[64,512]{1,0:T(8,128)(2,1)S(1)}, u32[]{:S(2)}, u32[]{:S(2)}) collective-permute-start(bf16[64,512]{1,0:T(8,128)(2,1)S(1)} %add_convert_fusion.refs_0_), channel_id=1, source_target_pairs={{0,16},{2,18},{4,20},{6,22},{8,24},{10,26},{12,28},{14,30},{16,0},... | collective-permute-start | bytes 196616 | tf_op jit(solution)/shard_map/ppermute | solution.py:169
  28.1 1.6 %collective-permute-start.8 = (bf16[64,512]{1,0:T(8,128)(2,1)S(1)}, bf16[64,512]{1,0:T(8,128)(2,1)S(1)}, u32[]{:S(2)}, u32[]{:S(2)}) collective-permute-start(bf16[64,512]{1,0:T(8,128)(2,1)S(1)} %add_convert_fusion.refs_0_), channel_id=1, source_target_pairs={{0,24},{2,26},{4,28},{6,30},{8,16},{10,18},{12,20},{14,22},{16,8},... | collective-permute-start | bytes 196616 | tf_op jit(solution)/shard_map/ppermute | solution.py:169
  29.7 0.0 copy-done
  29.7 0.1 collective-permute-start.9
  29.8 0.6 %collective-permute-done.6.refs_1_ = bf16[64,512]{1,0:T(8,128)(2,1)S(1)} collective-permute-done((bf16[64,512]{1,0:T(8,128)(2,1)S(1)}, bf16[64,512]{1,0:T(8,128)(2,1)S(1)}, u32[]{:S(2)}, u32[]{:S(2)}) %collective-permute-start.6) | collective-permute-done | bytes 65568 | tf_op jit(solution)/shard_map/ppermute | solution.py:169
  30.3 0.0 collective-permute-start.10
  30.3 1.0 %collective-permute-done.7.refs_2_ = bf16[64,512]{1,0:T(8,128)(2,1)S(1)} collective-permute-done((bf16[64,512]{1,0:T(8,128)(2,1)S(1)}, bf16[64,512]{1,0:T(8,128)(2,1)S(1)}, u32[]{:S(2)}, u32[]{:S(2)}) %collective-permute-start.7) | collective-permute-done | bytes 65568 | tf_op jit(solution)/shard_map/ppermute | solution.py:169
  31.3 0.0 collective-permute-start.11
  31.3 2.8 %collective-permute-done.8.refs_3_ = bf16[64,512]{1,0:T(8,128)(2,1)S(1)} collective-permute-done((bf16[64,512]{1,0:T(8,128)(2,1)S(1)}, bf16[64,512]{1,0:T(8,128)(2,1)S(1)}, u32[]{:S(2)}, u32[]{:S(2)}) %collective-permute-start.8) | collective-permute-done | bytes 65568 | tf_op jit(solution)/shard_map/ppermute | solution.py:169
  34.1 0.0 collective-permute-start.12
  34.1 0.1 pad_add_fusion.2.scalar_ref
  34.2 0.0 collective-permute-done.9.refs_4_
  34.2 0.0 collective-permute-done.10.refs_5_
  34.2 0.0 collective-permute-done.11.refs_6_
  34.2 1.2 %collective-permute-done.12.refs_7_ = bf16[64,512]{1,0:T(8,128)(2,1)S(1)} collective-permute-done((bf16[64,512]{1,0:T(8,128)(2,1)S(1)}, bf16[64,512]{1,0:T(8,128)(2,1)S(1)}, u32[]{:S(2)}, u32[]{:S(2)}) %collective-permute-start.12) | collective-permute-done | bytes 65568 | tf_op jit(solution)/shard_map/ppermute | solution.py:169
  35.4 9.8 %shard_map.40 = bf16[64,512]{1,0:T(8,128)(2,1)S(1)} custom-call(s32[3]{0:T(128)S(1)} %pad_add_fusion.2.scalar_ref, bf16[64,512]{1,0:T(8,128)(2,1)S(1)} %add_convert_fusion.refs_0_, bf16[64,512]{1,0:T(8,128)(2,1)S(1)} %collective-permute-done.6.refs_1_, bf16[64,512]{1,0:T(8,128)(2,1)S(1)} %collective-permute-done.7.refs_2_, ...), custom_call_target="tpu_custom_call" | custom-call | tf_op jit(solution)/shard_map/pallas_call | solution.py:147
  45.2 0.1 collective-permute-start.13
  45.3 0.1 collective-permute-start.14
  45.4 0.7 %collective-permute-start.15 = (bf16[32,512]{1,0:T(8,128)(2,1)S(1)}, bf16[32,512]{1,0:T(8,128)(2,1)S(1)}, u32[]{:S(2)}, u32[]{:S(2)}) collective-permute-start(bf16[32,512]{1,0:T(8,128)(2,1)S(1)} %get-tuple-element.21), channel_id=1, source_target_pairs={{0,0},{1,1},{2,4},{3,5},{4,2},{5,3},{6,6},{7,7},{8,8},{9,9},{10,12... | collective-permute-start | bytes 98312 | tf_op jit(solution)/shard_map/ppermute | solution.py:203
  46.1 4.7 %collective-permute-start.16 = (bf16[32,512]{1,0:T(8,128)(2,1)S(1)}, bf16[32,512]{1,0:T(8,128)(2,1)S(1)}, u32[]{:S(2)}, u32[]{:S(2)}) collective-permute-start(bf16[32,512]{1,0:T(8,128)(2,1)S(1)} %get-tuple-element.22), channel_id=1, source_target_pairs={{0,2},{1,3},{2,6},{3,7},{4,0},{5,1},{6,4},{7,5},{8,10},{9,11},{10,... | collective-permute-start | bytes 98312 | tf_op jit(solution)/shard_map/ppermute | solution.py:203
  50.8 0.0 collective-permute-done.13
  50.8 0.0 collective-permute-done.14
  50.9 0.0 collective-permute-done.15
  50.9 2.1 %collective-permute-done.16 = bf16[32,512]{1,0:T(8,128)(2,1)S(1)} collective-permute-done((bf16[32,512]{1,0:T(8,128)(2,1)S(1)}, bf16[32,512]{1,0:T(8,128)(2,1)S(1)}, u32[]{:S(2)}, u32[]{:S(2)}) %collective-permute-start.16) | collective-permute-done | bytes 32800 | tf_op jit(solution)/shard_map/ppermute | solution.py:203
  53.0 0.8 %fusion.5 = bf16[2,2,32,512]{3,2,1,0:T(8,128)(2,1)} fusion(s32[]{:T(128)S(6)} %select_n.84, bf16[1,2,32,512]{3,2,1,0:T(8,128)(2,1)S(1)} %maximum_bitcast_fusion, bf16[1,2,32,512]{3,2,1,0:T(8,128)(2,1)S(1)} %maximum_bitcast_fusion.1), kind=kLoop, calls=%fused_computation.13 | loop fusion | flops 196608 | bytes 262148 | tf_op jit(solution)/shard_map/jit(_roll_dynamic)/concatenate | solution.py:213
  (11 shorter events, 0.2 us)
Async XLA Ops:
  0.0 29.7 %copy-start = (s32[2,2]{1,0:T(2,128)S(1)}, s32[2,2]{1,0:T(2,128)}, u32[]{:S(2)}) copy-start(s32[2,2]{1,0:T(2,128)} %param.5) | copy-start | bytes 52
  0.1 1.2 %copy-start.1 = (bf16[2,512,512]{2,1,0:T(8,128)(2,1)S(1)}, bf16[2,512,512]{2,1,0:T(8,128)(2,1)}, u32[]{:S(2)}) copy-start(bf16[2,512,512]{2,1,0:T(8,128)(2,1)} %patch_ref.3) | copy-start | bytes 3145732
  1.3 1.2 %copy-start.3 = (bf16[2,512,512]{2,1,0:T(8,128)(2,1)S(1)}, bf16[2,512,512]{2,1,0:T(8,128)(2,1)}, u32[]{:S(2)}) copy-start(bf16[2,512,512]{2,1,0:T(8,128)(2,1)} %cot_ref.3) | copy-start | bytes 3145732
  2.5 2.1 %copy-start.4 = (bf16[2,512,512]{2,1,0:T(8,128)(2,1)S(1)}, bf16[2,512,512]{2,1,0:T(8,128)(2,1)}, u32[]{:S(2)}) copy-start(bf16[2,512,512]{2,1,0:T(8,128)(2,1)} %cot_ref.3) | copy-start | bytes 3145732
  3.9 1.2 %copy-start.2 = (bf16[2,512,512]{2,1,0:T(8,128)(2,1)S(1)}, bf16[2,512,512]{2,1,0:T(8,128)(2,1)}, u32[]{:S(2)}) copy-start(bf16[2,512,512]{2,1,0:T(8,128)(2,1)} %patch_ref.3) | copy-start | bytes 3145732
  3.9 2.5 %collective-permute-start.1 = (bf16[256,512]{1,0:T(8,128)(2,1)S(1)}, bf16[256,512]{1,0:T(8,128)(2,1)S(1)}, u32[]{:S(2)}, u32[]{:S(2)}) collective-permute-start(bf16[256,512]{1,0:T(8,128)(2,1)S(1)} %get-tuple-element.15), channel_id=1, source_target_pairs={{0,2},{2,0},{4,6},{6,4},{8,10},{10,8},{12,14},{14,12},{16,18},{18,... | collective-permute-start | bytes 786440 | tf_op jit(solution)/shard_map/ppermute | solution.py:169
  4.4 2.0 %collective-permute-start = (bf16[256,512]{1,0:T(8,128)(2,1)S(1)}, bf16[256,512]{1,0:T(8,128)(2,1)S(1)}, u32[]{:S(2)}, u32[]{:S(2)}) collective-permute-start(bf16[256,512]{1,0:T(8,128)(2,1)S(1)} %get-tuple-element.16), channel_id=1, source_target_pairs={{0,2},{2,0},{4,6},{6,4},{8,10},{10,8},{12,14},{14,12},{16,18},{18,... | collective-permute-start | bytes 786440 | tf_op jit(solution)/shard_map/ppermute | solution.py:169
  6.6 9.3 %collective-permute-start.2 = (bf16[256,512]{1,0:T(8,128)(2,1)S(1)}, bf16[256,512]{1,0:T(8,128)(2,1)S(1)}, u32[]{:S(2)}, u32[]{:S(2)}) collective-permute-start(bf16[256,512]{1,0:T(8,128)(2,1)S(1)} %get-tuple-element.13), channel_id=1, source_target_pairs={{0,4},{2,6},{4,0},{6,2},{8,12},{10,14},{12,8},{14,10},{16,20},{18,... | collective-permute-start | bytes 786440 | tf_op jit(solution)/shard_map/ppermute | solution.py:169
  15.9 6.6 %collective-permute-start.5 = (bf16[64,512]{1,0:T(8,128)(2,1)S(1)}, bf16[64,512]{1,0:T(8,128)(2,1)S(1)}, u32[]{:S(2)}, u32[]{:S(2)}) collective-permute-start(bf16[64,512]{1,0:T(8,128)(2,1)S(1)} %get-tuple-element.12), channel_id=1, source_target_pairs={{0,24},{2,26},{4,28},{6,30},{8,16},{10,18},{12,20},{14,22},{16,8},... | collective-permute-start | bytes 196616 | tf_op jit(solution)/shard_map/ppermute | solution.py:169
  19.8 5.4 %collective-permute-start.4 = (bf16[64,512]{1,0:T(8,128)(2,1)S(1)}, bf16[64,512]{1,0:T(8,128)(2,1)S(1)}, u32[]{:S(2)}, u32[]{:S(2)}) collective-permute-start(bf16[64,512]{1,0:T(8,128)(2,1)S(1)} %get-tuple-element.11), channel_id=1, source_target_pairs={{0,16},{2,18},{4,20},{6,22},{8,24},{10,26},{12,28},{14,30},{16,0},... | collective-permute-start | bytes 196616 | tf_op jit(solution)/shard_map/ppermute | solution.py:169
  19.8 5.4 %collective-permute-start.3 = (bf16[64,512]{1,0:T(8,128)(2,1)S(1)}, bf16[64,512]{1,0:T(8,128)(2,1)S(1)}, u32[]{:S(2)}, u32[]{:S(2)}) collective-permute-start(bf16[64,512]{1,0:T(8,128)(2,1)S(1)} %get-tuple-element.10), channel_id=1, source_target_pairs={{0,8},{2,10},{4,12},{6,14},{8,0},{10,2},{12,4},{14,6},{16,24},{18,... | collective-permute-start | bytes 196616 | tf_op jit(solution)/shard_map/ppermute | solution.py:169
  25.2 5.1 %collective-permute-start.6 = (bf16[64,512]{1,0:T(8,128)(2,1)S(1)}, bf16[64,512]{1,0:T(8,128)(2,1)S(1)}, u32[]{:S(2)}, u32[]{:S(2)}) collective-permute-start(bf16[64,512]{1,0:T(8,128)(2,1)S(1)} %add_convert_fusion.refs_0_), channel_id=1, source_target_pairs={{0,8},{2,10},{4,12},{6,14},{8,0},{10,2},{12,4},{14,6},{16,24},{18,... | collective-permute-start | bytes 196616 | tf_op jit(solution)/shard_map/ppermute | solution.py:169
  25.8 5.6 %collective-permute-start.7 = (bf16[64,512]{1,0:T(8,128)(2,1)S(1)}, bf16[64,512]{1,0:T(8,128)(2,1)S(1)}, u32[]{:S(2)}, u32[]{:S(2)}) collective-permute-start(bf16[64,512]{1,0:T(8,128)(2,1)S(1)} %add_convert_fusion.refs_0_), channel_id=1, source_target_pairs={{0,16},{2,18},{4,20},{6,22},{8,24},{10,26},{12,28},{14,30},{16,0},... | collective-permute-start | bytes 196616 | tf_op jit(solution)/shard_map/ppermute | solution.py:169
  28.1 6.1 %collective-permute-start.8 = (bf16[64,512]{1,0:T(8,128)(2,1)S(1)}, bf16[64,512]{1,0:T(8,128)(2,1)S(1)}, u32[]{:S(2)}, u32[]{:S(2)}) collective-permute-start(bf16[64,512]{1,0:T(8,128)(2,1)S(1)} %add_convert_fusion.refs_0_), channel_id=1, source_target_pairs={{0,24},{2,26},{4,28},{6,30},{8,16},{10,18},{12,20},{14,22},{16,8},... | collective-permute-start | bytes 196616 | tf_op jit(solution)/shard_map/ppermute | solution.py:169
  29.7 4.5 %collective-permute-start.9 = (bf16[64,512]{1,0:T(8,128)(2,1)S(1)}, bf16[64,512]{1,0:T(8,128)(2,1)S(1)}, u32[]{:S(2)}, u32[]{:S(2)}) collective-permute-start(bf16[64,512]{1,0:T(8,128)(2,1)S(1)} %add_convert_fusion.refs_0_), channel_id=1, source_target_pairs={{0,2},{2,0},{4,6},{6,4},{8,10},{10,8},{12,14},{14,12},{16,18},{18,... | collective-permute-start | bytes 196616 | tf_op jit(solution)/shard_map/ppermute | solution.py:169
  30.3 3.9 %collective-permute-start.10 = (bf16[64,512]{1,0:T(8,128)(2,1)S(1)}, bf16[64,512]{1,0:T(8,128)(2,1)S(1)}, u32[]{:S(2)}, u32[]{:S(2)}) collective-permute-start(bf16[64,512]{1,0:T(8,128)(2,1)S(1)} %collective-permute-done.6.refs_1_), channel_id=1, source_target_pairs={{0,2},{2,0},{4,6},{6,4},{8,10},{10,8},{12,14},{14,12},{16,18},{18,... | collective-permute-start | bytes 196616 | tf_op jit(solution)/shard_map/ppermute | solution.py:169
  31.3 2.9 %collective-permute-start.11 = (bf16[64,512]{1,0:T(8,128)(2,1)S(1)}, bf16[64,512]{1,0:T(8,128)(2,1)S(1)}, u32[]{:S(2)}, u32[]{:S(2)}) collective-permute-start(bf16[64,512]{1,0:T(8,128)(2,1)S(1)} %collective-permute-done.7.refs_2_), channel_id=1, source_target_pairs={{0,2},{2,0},{4,6},{6,4},{8,10},{10,8},{12,14},{14,12},{16,18},{18,... | collective-permute-start | bytes 196616 | tf_op jit(solution)/shard_map/ppermute | solution.py:169
  34.1 1.3 %collective-permute-start.12 = (bf16[64,512]{1,0:T(8,128)(2,1)S(1)}, bf16[64,512]{1,0:T(8,128)(2,1)S(1)}, u32[]{:S(2)}, u32[]{:S(2)}) collective-permute-start(bf16[64,512]{1,0:T(8,128)(2,1)S(1)} %collective-permute-done.8.refs_3_), channel_id=1, source_target_pairs={{0,2},{2,0},{4,6},{6,4},{8,10},{10,8},{12,14},{14,12},{16,18},{18,... | collective-permute-start | bytes 196616 | tf_op jit(solution)/shard_map/ppermute | solution.py:169
  45.2 5.6 %collective-permute-start.13 = (bf16[32,512]{1,0:T(8,128)(2,1)S(1)}, bf16[32,512]{1,0:T(8,128)(2,1)S(1)}, u32[]{:S(2)}, u32[]{:S(2)}) collective-permute-start(bf16[32,512]{1,0:T(8,128)(2,1)S(1)} %get-tuple-element.21), channel_id=1, source_target_pairs={{0,1},{1,0},{2,5},{3,4},{4,3},{5,2},{6,7},{7,6},{8,9},{9,8},{10,13... | collective-permute-start | bytes 98312 | tf_op jit(solution)/shard_map/ppermute | solution.py:203
  45.3 5.5 %collective-permute-start.14 = (bf16[32,512]{1,0:T(8,128)(2,1)S(1)}, bf16[32,512]{1,0:T(8,128)(2,1)S(1)}, u32[]{:S(2)}, u32[]{:S(2)}) collective-permute-start(bf16[32,512]{1,0:T(8,128)(2,1)S(1)} %get-tuple-element.22), channel_id=1, source_target_pairs={{0,3},{1,2},{2,7},{3,6},{4,1},{5,0},{6,5},{7,4},{8,11},{9,10},{10,... | collective-permute-start | bytes 98312 | tf_op jit(solution)/shard_map/ppermute | solution.py:203
  45.4 5.5 %collective-permute-start.15 = (bf16[32,512]{1,0:T(8,128)(2,1)S(1)}, bf16[32,512]{1,0:T(8,128)(2,1)S(1)}, u32[]{:S(2)}, u32[]{:S(2)}) collective-permute-start(bf16[32,512]{1,0:T(8,128)(2,1)S(1)} %get-tuple-element.21), channel_id=1, source_target_pairs={{0,0},{1,1},{2,4},{3,5},{4,2},{5,3},{6,6},{7,7},{8,8},{9,9},{10,12... | collective-permute-start | bytes 98312 | tf_op jit(solution)/shard_map/ppermute | solution.py:203
  46.1 6.9 %collective-permute-start.16 = (bf16[32,512]{1,0:T(8,128)(2,1)S(1)}, bf16[32,512]{1,0:T(8,128)(2,1)S(1)}, u32[]{:S(2)}, u32[]{:S(2)}) collective-permute-start(bf16[32,512]{1,0:T(8,128)(2,1)S(1)} %get-tuple-element.22), channel_id=1, source_target_pairs={{0,2},{1,3},{2,6},{3,7},{4,0},{5,1},{6,4},{7,5},{8,10},{9,11},{10,... | collective-permute-start | bytes 98312 | tf_op jit(solution)/shard_map/ppermute | solution.py:203

commit v2 on v1

v2 whole, which is shorter than its diff:
```python
import functools

import jax
import jax.numpy as jnp
from jax import lax
from jax.experimental import pallas as pl
from jax.experimental.pallas import tpu as pltpu
from jax.sharding import PartitionSpec as P

F32 = jnp.float32
BF16 = jnp.bfloat16
VMEM = pl.BlockSpec(memory_space=pltpu.VMEM)
SMEM = pl.BlockSpec(memory_space=pltpu.SMEM)
HBM = pl.BlockSpec(memory_space=pltpu.HBM)
ROWS_IN_COLS = (((0,), (0,)), ((), ()))
COLS_IN_COLS = (((1,), (1,)), ((), ()))


def params(limit):
    return pltpu.CompilerParams(vmem_limit_bytes=limit << 20)


def gram_kernel(scale, pieces, *refs):
    count = len(pieces)
    scalar_ref, patch_hbm, cot_hbm = refs[:3]
    outs = refs[3 : 3 + count]
    patch, cot, patch_sems, cot_sems = refs[3 + count :]
    half = patch.shape[2]
    distinct = sorted({block for block, _, _ in pieces}, key=[p[0] for p in pieces].index)
    copies = {}
    for index, (block, side, _) in enumerate(pieces):
        number = scalar_ref[block]
        if block not in copies:
            slot = distinct.index(block)
            copies[block] = pltpu.make_async_copy(
                cot_hbm.at[number], cot.at[slot], cot_sems.at[slot]
            )
            copies[block].start()
        columns = pl.ds(pl.multiple_of(scalar_ref[2 + side] * half, half), half)
        copies[index, None] = pltpu.make_async_copy(
            patch_hbm.at[number, :, columns], patch.at[index], patch_sems.at[index]
        )
        copies[index, None].start()
    waited = set()
    for index, (block, _, dtype) in enumerate(pieces):
        if block not in waited:
            copies[block].wait()
            waited.add(block)
        copies[index, None].wait()
        terms = lax.dot_general(
            patch[index], cot[distinct.index(block)], ROWS_IN_COLS, preferred_element_type=F32
        )
        outs[index][...] = (terms * scale).astype(dtype)


def gram(scalars, patches, cotangents, scale, pieces):
    _, pix, width = patches.shape
    half = width // 2
    count = len(pieces)
    blocks = len({block for block, _, _ in pieces})
    return pl.pallas_call(
        functools.partial(gram_kernel, scale, pieces),
        out_shape=[jax.ShapeDtypeStruct((half, width), dtype) for _, _, dtype in pieces],
        in_specs=[SMEM, HBM, HBM],
        out_specs=[VMEM] * count,
        scratch_shapes=[
            pltpu.VMEM((count, pix, half), BF16),
            pltpu.VMEM((blocks, pix, width), BF16),
            pltpu.SemaphoreType.DMA((count,)),
            pltpu.SemaphoreType.DMA((blocks,)),
        ],
        compiler_params=params(16),
        cost_estimate=pl.CostEstimate(
            flops=2 * count * pix * half * width,
            bytes_accessed=2 * (count * pix * half + blocks * pix * width),
            transcendentals=0,
        ),
    )(scalars, patches, cotangents)


def split_kernel(place_ref, kept_ref, came_ref, own_ref, *piece_refs):
    rows = own_ref.shape[0]
    place = place_ref[0]

    def piece(offset):
        where = pl.ds(pl.multiple_of((place ^ offset) * rows, rows), rows)
        return kept_ref[where, :] + came_ref[where, :].astype(F32)

    own_ref[...] = piece(0)
    for index, ref in enumerate(piece_refs):
        ref[...] = piece(index + 1).astype(BF16)


def split(place, kept, came, line):
    rows, width = kept.shape
    part = rows // line
    return pl.pallas_call(
        split_kernel,
        out_shape=[jax.ShapeDtypeStruct((part, width), F32)]
        + [jax.ShapeDtypeStruct((part, width), BF16)] * (line - 1),
        in_specs=[SMEM, VMEM, VMEM],
        out_specs=[VMEM] * line,
        compiler_params=params(16),
    )(place, kept, came)


def root_kernel(count_pieces, scalar_ref, *refs):
    pieces = refs[:count_pieces]
    out_ref, grad, q_left, q_right, m_left, m_right, x_left, x_right = refs[count_pieces:]
    part = pieces[0].shape[0]
    width = grad.shape[0]
    for index, ref in enumerate(pieces):
        grad[part * index : part * (index + 1), :] = ref[...]
    diagonal = lax.broadcasted_iota(jnp.int32, (width, width), 0) == lax.broadcasted_iota(
        jnp.int32, (width, width), 1
    )

    def dot(a, b):
        return jnp.dot(a, b, preferred_element_type=F32)

    def factor(moment):
        return (jnp.where(diagonal, 1.25, 0.0) - 0.25 * moment).astype(BF16)

    def begin(dims):
        stats = lax.dot_general(grad[...], grad[...], dims, preferred_element_type=F32)
        stats = stats + jnp.where(diagonal, 0.1, 0.0)
        scale = 2.5 / jnp.sqrt(jnp.sum(stats * stats, keepdims=True))
        first = jnp.sqrt(jnp.sqrt(scale)).astype(BF16).astype(F32)
        return scale * stats, first

    line = lax.broadcasted_iota(jnp.int32, (part, width), 0)
    spot = lax.broadcasted_iota(jnp.int32, (part, width), 1)
    wanted = jnp.where(line < part // 2, scalar_ref[2] + line, scalar_ref[3] + line - part // 2)
    pick = jnp.where(spot == wanted, 1.0, 0.0).astype(BF16)
    moment, first = begin(COLS_IN_COLS)
    m_left[...] = moment.astype(BF16)
    factor_value = factor(moment)
    q_left[...] = factor_value
    x_left[...] = (first * dot(pick, factor_value)).astype(BF16)
    moment, first = begin(ROWS_IN_COLS)
    m_right[...] = moment.astype(BF16)
    factor_value = factor(moment)
    q_right[...] = factor_value
    x_right[...] = (first * factor_value.astype(F32)).astype(BF16)

    count_left, count_right = scalar_ref[0], scalar_ref[1]

    def sweep(index, carry):
        second_left = dot(q_left[...], q_left[...]).astype(BF16)
        second_right = dot(q_right[...], q_right[...]).astype(BF16)
        fourth_left = dot(second_left, second_left).astype(BF16)
        fourth_right = dot(second_right, second_right).astype(BF16)
        moment_left = dot(fourth_left, m_left[...])
        moment_right = dot(fourth_right, m_right[...])
        m_left[...] = moment_left.astype(BF16)
        m_right[...] = moment_right.astype(BF16)
        factor_left = factor(moment_left)
        factor_right = factor(moment_right)
        q_left[...] = factor_left
        q_right[...] = factor_right

        @pl.when(index < count_left)
        def _():
            x_left[...] = dot(x_left[...], factor_left).astype(BF16)

        @pl.when(index < count_right)
        def _():
            x_right[...] = dot(x_right[...], factor_right).astype(BF16)

        return carry

    lax.fori_loop(1, jnp.maximum(count_left, count_right), sweep, 0)
    partial_value = dot(x_left[...], grad[...]).astype(BF16)
    update = dot(partial_value, x_right[...]).astype(BF16)
    for group in range(out_ref.shape[0]):
        out_ref[group] = update


def root(scalars, pieces, groups):
    part, width = pieces[0].shape
    square = pltpu.VMEM((width, width), BF16)
    return pl.pallas_call(
        functools.partial(root_kernel, len(pieces)),
        out_shape=jax.ShapeDtypeStruct((groups, part, width), BF16),
        in_specs=[SMEM] + [VMEM] * len(pieces),
        out_specs=VMEM,
        scratch_shapes=[square] * 5 + [pltpu.VMEM((part, width), BF16), square],
        compiler_params=params(32),
    )(scalars, *pieces)


def shards(line, groups, patches, cotangents, newton_counts):
    blocks, pix, width = patches.shape
    half = width // 2
    part = half // line
    rows = part // 2
    scale = 1.0 / float(pix * 4 * line * width) ** 0.5
    place, column, core = (lax.axis_index(name) for name in ("z", "x", "core"))

    def swap(array, axis, mask=1):
        return lax.ppermute(array, axis, [(i, i ^ mask) for i in range(lax.axis_size(axis))])

    where = jnp.stack([1 - column, column, 1 - core, core])
    (given,) = gram(where, patches, cotangents, scale, ((0, 0, BF16),))
    came = swap(given, "core")
    kept_other, given, kept = gram(
        where, patches, cotangents, scale, ((0, 1, F32), (1, 0, BF16), (1, 1, F32))
    )
    came_column = swap((kept_other + came.astype(F32)).astype(BF16), "x")
    pair = kept + swap(given, "core").astype(F32)
    own, *others = split(place[None], pair, came_column, line)
    for offset, piece in enumerate(others, 1):
        own = own + swap(piece, "z", offset).astype(F32)
    own = own.astype(BF16)
    near = [own] + [swap(own, "z", offset) for offset in range(1, line)]
    far = [swap(piece, "core") for piece in near]

    starts = []
    for index in range(2):
        target = 2 * place + index
        starts.append(
            ((target // line) ^ core) * half + ((target % line) ^ place) * part + core * rows
        )
    counts = lax.dynamic_index_in_dim(newton_counts, column, 0, keepdims=False)
    update = root(jnp.concatenate([counts, jnp.stack(starts)]), near + far, groups)
    update = update.reshape(groups * 2, rows, width)
    return lax.all_to_all(update, ("group", "x"), 0, 0, tiled=True)


def solution(mesh):
    devices, groups = mesh.shape["dp"], mesh.shape["group"]
    line = devices // 4
    cut = jax.sharding.Mesh(
        mesh.devices.reshape(line, 2, 2, groups), ("z", "x", "core", "group")
    )
    dp = ("z", "x", "core")
    placed = (P("group", dp, None), P("group", dp, None), P("group", None))
    return jax.shard_map(
        functools.partial(shards, line, groups),
        mesh=cut,
        in_specs=placed,
        out_specs=P(None, dp, None),
        check_vma=False,
    )
```

time: 54.1 us -> 54 us (level)
  blocking collectives: 0 us -> 10.5 us
  starting transfers between devices: 18.2 us -> 13.2 us
  waiting for transfers between devices: 18.7 us -> 16.4 us
  Pallas kernels: 12.4 us -> 10.3 us
  other arithmetic: 1.23 us -> 0.33 us
    all_to_all x0 -> x1, blocking collectives: none -> 10.5 us  [shards(): return lax.all_to_all(update, ('group', 'x'), 0, 0, tiled=True)]
    ppermute x17 -> x13, starting transfers between devices: 18.2 us -> 13.2 us  [swap(): lax.ppermute(array, axis, [(i, i ^ mask) for i in range(lax.axis_size(axi...]
    ppermute x17 -> x13, waiting for transfers between devices: 18.7 us -> 16.4 us  [swap(): lax.ppermute(array, axis, [(i, i ^ mask) for i in range(lax.axis_size(axi...]
    pallas_call x1, Pallas kernels: 9.8 us -> 7.61 us  [root(): pl.pallas_call(functools.partial(root_kernel, len(pieces)), out_shape=jax...]
    concatenate x2 -> x1, other arithmetic: 0.84 us -> 0.08 us  [shards(): jnp.concatenate([counts, jnp.stack(starts)])]
    unnamed x10 -> x7, local copies, waits for them, and re-layouts: 2.94 us -> 3.11 us
  transfers between devices with their start and end apart: 17 -> 13, of which waited for: 8 -> 7; matrix products, arithmetic and copies ran while one was open for 0% -> 0% of each run, Pallas kernels for 2% -> 3%
where the time goes in v2:
time: 54 us; the launch traced here: 53.9 us
  waiting for transfers between devices  16.4 us (30%)
  starting transfers between devices  13.2 us (24%)
  blocking collectives  10.5 us (19%)
  Pallas kernels  10.3 us (19%)
  local copies, waits for them, and re-layouts  3.11 us (6%)
    ppermute x13, waiting for transfers between devices, swap(): lax.ppermute(array, axis, [(i, i ^ mask) for i in range(lax.axis_size(axi...  16.4 us
    ppermute x13, starting transfers between devices, swap(): lax.ppermute(array, axis, [(i, i ^ mask) for i in range(lax.axis_size(axi...  13.2 us
    all_to_all x1, blocking collectives, shards(): return lax.all_to_all(update, ('group', 'x'), 0, 0, tiled=True)  10.5 us
    pallas_call x1, Pallas kernels, root(): pl.pallas_call(functools.partial(root_kernel, len(pieces)), out_shape=jax...  7.61 us
    unnamed x7, local copies, waits for them, and re-layouts  3.11 us
    pallas_call x2, Pallas kernels, gram(): pl.pallas_call(functools.partial(gram_kernel, scale, pieces), out_shape=[...  2.66 us
  transfers between devices with their start and end apart: 13, of which 7 were waited for; matrix products, arithmetic and copies ran while one was open for 0% of the time, Pallas kernels for 3%

profile of v2, /device:TPU:0, one launch (start us, length us, event | category | flops | bytes accessed | tf_op | source)
XLA Modules:
  0.0 53.9 jit_solution(18325092704779538021)
XLA Ops:
  0.0 0.0 copy-start
  0.0 0.1 pad_add_fusion.1.refs_0_
  0.1 0.0 copy-start.1
  0.1 1.2 %copy-done.1 = bf16[2,512,512]{2,1,0:T(8,128)(2,1)S(1)} copy-done((bf16[2,512,512]{2,1,0:T(8,128)(2,1)S(1)}, bf16[2,512,512]{2,1,0:T(8,128)(2,1)}, u32[]{:S(2)}) %copy-start.1) | copy-done | bytes 1048600
  1.3 0.0 copy-start.2
  1.3 1.2 %copy-done.2 = bf16[2,512,512]{2,1,0:T(8,128)(2,1)S(1)} copy-done((bf16[2,512,512]{2,1,0:T(8,128)(2,1)S(1)}, bf16[2,512,512]{2,1,0:T(8,128)(2,1)}, u32[]{:S(2)}) %copy-start.2) | copy-done | bytes 1048600
  2.5 0.9 %shard_map.38 = bf16[256,512]{1,0:T(8,128)(2,1)S(1)} custom-call(s32[4]{0:T(128)S(1)} %pad_add_fusion.1.refs_0_, bf16[2,512,512]{2,1,0:T(8,128)(2,1)S(1)} %copy-done.1, bf16[2,512,512]{2,1,0:T(8,128)(2,1)S(1)} %copy-done.2), custom_call_target="tpu_custom_call" | custom-call | flops 134217728 | bytes 786432 | tf_op jit(solution)/shard_map/pallas_call | solution.py:61
  3.5 0.5 collective-permute-start.1
  4.0 1.7 %shard_map.37 = (f32[256,512]{1,0:T(8,128)S(1)}, bf16[256,512]{1,0:T(8,128)(2,1)S(1)}, f32[256,512]{1,0:T(8,128)S(1)}) custom-call(s32[4]{0:T(128)S(1)} %pad_add_fusion.1.refs_0_, bf16[2,512,512]{2,1,0:T(8,128)(2,1)S(1)} %copy-done.1, bf16[2,512,512]{2,1,0:T(8,128)(2,1)S(1)} %copy-done.2), custom_call_target="tpu_custom_call" | custom-call | flops 402653184 | bytes 1835008 | tf_op jit(solution)/shard_map/pallas_call | solution.py:61
  5.7 0.1 collective-permute-start
  5.9 0.0 collective-permute-done.1
  5.9 0.1 add_convert_fusion
  5.9 3.0 %collective-permute-start.2 = (bf16[256,512]{1,0:T(8,128)(2,1)S(1)}, bf16[256,512]{1,0:T(8,128)(2,1)S(1)}, u32[]{:S(2)}, u32[]{:S(2)}) collective-permute-start(bf16[256,512]{1,0:T(8,128)(2,1)S(1)} %add_convert_fusion), channel_id=1, source_target_pairs={{0,4},{4,0},{1,5},{5,1},{2,6},{6,2},{3,7},{7,3},{8,12},{12,8},{9,1... | collective-permute-start | bytes 786440 | tf_op jit(solution)/shard_map/ppermute | solution.py:201
  8.9 0.0 collective-permute-done
  8.9 0.1 convert_add_fusion.kept_ref
  9.0 6.4 %collective-permute-done.2.came_ref = bf16[256,512]{1,0:T(8,128)(2,1)S(1)} collective-permute-done((bf16[256,512]{1,0:T(8,128)(2,1)S(1)}, bf16[256,512]{1,0:T(8,128)(2,1)S(1)}, u32[]{:S(2)}, u32[]{:S(2)}) %collective-permute-start.2) | collective-permute-done | bytes 262176 | tf_op jit(solution)/shard_map/ppermute | solution.py:201
  15.5 1.9 %collective-permute-start.3 = (bf16[64,512]{1,0:T(8,128)(2,1)S(1)}, bf16[64,512]{1,0:T(8,128)(2,1)S(1)}, u32[]{:S(2)}, u32[]{:S(2)}) collective-permute-start(bf16[64,512]{1,0:T(8,128)(2,1)S(1)} %get-tuple-element.16), channel_id=1, source_target_pairs={{0,8},{8,0},{16,24},{24,16},{1,9},{9,1},{17,25},{25,17},{2,10},{10... | collective-permute-start | bytes 196616 | tf_op jit(solution)/shard_map/ppermute | solution.py:201
  17.4 2.6 %collective-permute-start.4 = (bf16[64,512]{1,0:T(8,128)(2,1)S(1)}, bf16[64,512]{1,0:T(8,128)(2,1)S(1)}, u32[]{:S(2)}, u32[]{:S(2)}) collective-permute-start(bf16[64,512]{1,0:T(8,128)(2,1)S(1)} %get-tuple-element.17), channel_id=1, source_target_pairs={{0,16},{8,24},{16,0},{24,8},{1,17},{9,25},{17,1},{25,9},{2,18},{10... | collective-permute-start | bytes 196616 | tf_op jit(solution)/shard_map/ppermute | solution.py:201
  20.0 0.0 collective-permute-start.5
  20.0 0.0 collective-permute-done.3
  20.0 4.0 %collective-permute-done.4 = bf16[64,512]{1,0:T(8,128)(2,1)S(1)} collective-permute-done((bf16[64,512]{1,0:T(8,128)(2,1)S(1)}, bf16[64,512]{1,0:T(8,128)(2,1)S(1)}, u32[]{:S(2)}, u32[]{:S(2)}) %collective-permute-start.4) | collective-permute-done | bytes 65568 | tf_op jit(solution)/shard_map/ppermute | solution.py:201
  24.0 2.2 %collective-permute-done.5 = bf16[64,512]{1,0:T(8,128)(2,1)S(1)} collective-permute-done((bf16[64,512]{1,0:T(8,128)(2,1)S(1)}, bf16[64,512]{1,0:T(8,128)(2,1)S(1)}, u32[]{:S(2)}, u32[]{:S(2)}) %collective-permute-start.5) | collective-permute-done | bytes 65568 | tf_op jit(solution)/shard_map/ppermute | solution.py:201
  26.2 1.1 %collective-permute-start.8 = (bf16[64,512]{1,0:T(8,128)(2,1)S(1)}, bf16[64,512]{1,0:T(8,128)(2,1)S(1)}, u32[]{:S(2)}, u32[]{:S(2)}) collective-permute-start(bf16[64,512]{1,0:T(8,128)(2,1)S(1)} %add_convert_fusion.1.refs_0_), channel_id=1, source_target_pairs={{0,24},{8,16},{16,8},{24,0},{1,25},{9,17},{17,9},{25,1},{2,26},{10... | collective-permute-start | bytes 196616 | tf_op jit(solution)/shard_map/ppermute | solution.py:201
  27.3 0.0 collective-permute-start.7
  27.3 3.3 %collective-permute-start.6 = (bf16[64,512]{1,0:T(8,128)(2,1)S(1)}, bf16[64,512]{1,0:T(8,128)(2,1)S(1)}, u32[]{:S(2)}, u32[]{:S(2)}) collective-permute-start(bf16[64,512]{1,0:T(8,128)(2,1)S(1)} %add_convert_fusion.1.refs_0_), channel_id=1, source_target_pairs={{0,8},{8,0},{16,24},{24,16},{1,9},{9,1},{17,25},{25,17},{2,10},{10... | collective-permute-start | bytes 196616 | tf_op jit(solution)/shard_map/ppermute | solution.py:201
  30.6 0.0 copy-done
  30.6 0.1 collective-permute-start.9
  30.7 1.7 %collective-permute-done.8.refs_3_ = bf16[64,512]{1,0:T(8,128)(2,1)S(1)} collective-permute-done((bf16[64,512]{1,0:T(8,128)(2,1)S(1)}, bf16[64,512]{1,0:T(8,128)(2,1)S(1)}, u32[]{:S(2)}, u32[]{:S(2)}) %collective-permute-start.8) | collective-permute-done | bytes 65568 | tf_op jit(solution)/shard_map/ppermute | solution.py:201
  32.4 0.0 collective-permute-start.12
  32.4 1.3 %collective-permute-done.7.refs_2_ = bf16[64,512]{1,0:T(8,128)(2,1)S(1)} collective-permute-done((bf16[64,512]{1,0:T(8,128)(2,1)S(1)}, bf16[64,512]{1,0:T(8,128)(2,1)S(1)}, u32[]{:S(2)}, u32[]{:S(2)}) %collective-permute-start.7) | collective-permute-done | bytes 65568 | tf_op jit(solution)/shard_map/ppermute | solution.py:201
  33.7 0.0 collective-permute-start.11
  33.7 0.0 collective-permute-done.6.refs_1_
  33.7 0.5 collective-permute-start.10
  34.2 0.1 pad_add_fusion.scalar_ref
  34.3 0.0 collective-permute-done.9.refs_4_
  34.3 0.0 collective-permute-done.12.refs_7_
  34.3 0.7 %collective-permute-done.11.refs_6_ = bf16[64,512]{1,0:T(8,128)(2,1)S(1)} collective-permute-done((bf16[64,512]{1,0:T(8,128)(2,1)S(1)}, bf16[64,512]{1,0:T(8,128)(2,1)S(1)}, u32[]{:S(2)}, u32[]{:S(2)}) %collective-permute-start.11) | collective-permute-done | bytes 65568 | tf_op jit(solution)/shard_map/ppermute | solution.py:201
  35.0 0.2 collective-permute-done.10.refs_5_
  35.1 7.6 %shard_map.40 = bf16[2,64,512]{2,1,0:T(8,128)(2,1)S(1)} custom-call(s32[4]{0:T(128)S(1)} %pad_add_fusion.scalar_ref, bf16[64,512]{1,0:T(8,128)(2,1)S(1)} %add_convert_fusion.1.refs_0_, bf16[64,512]{1,0:T(8,128)(2,1)S(1)} %collective-permute-done.6.refs_1_, bf16[64,512]{1,0:T(8,128)(2,1)S(1)} %collective-permute-done.7.refs_2_, ...), custom_call_target="tpu_custom_call" | custom-call | tf_op jit(solution)/shard_map/pallas_call | solution.py:182
  42.7 10.5 %all_to_all.5 = bf16[4,32,512]{2,1,0:T(8,128)(2,1)S(1)} all-to-all(bf16[4,32,512]{2,1,0:T(8,128)(2,1)S(1)} %bitcast.10), channel_id=1, replica_groups=mesh['z'=4,'x'=2,'core'=2,'group'=2] {'group','x'}, dimensions={0} | all-to-all | bytes 262144 | tf_op jit(solution)/shard_map/all_to_all | solution.py:227
  53.2 0.7 %copy.5 = bf16[4,32,512]{2,1,0:T(8,128)(2,1)} copy(bf16[4,32,512]{2,1,0:T(8,128)(2,1)S(1)} %all_to_all.5) | data formatting | bytes 262144
  (3 shorter events, 0.1 us)
Async XLA Ops:
  0.0 30.6 %copy-start = (s32[2,2]{1,0:T(2,128)S(1)}, s32[2,2]{1,0:T(2,128)}, u32[]{:S(2)}) copy-start(s32[2,2]{1,0:T(2,128)} %param.5) | copy-start | bytes 52
  0.1 1.2 %copy-start.1 = (bf16[2,512,512]{2,1,0:T(8,128)(2,1)S(1)}, bf16[2,512,512]{2,1,0:T(8,128)(2,1)}, u32[]{:S(2)}) copy-start(bf16[2,512,512]{2,1,0:T(8,128)(2,1)} %refs_1_.3) | copy-start | bytes 3145732
  1.3 1.2 %copy-start.2 = (bf16[2,512,512]{2,1,0:T(8,128)(2,1)S(1)}, bf16[2,512,512]{2,1,0:T(8,128)(2,1)}, u32[]{:S(2)}) copy-start(bf16[2,512,512]{2,1,0:T(8,128)(2,1)} %refs_2_.3) | copy-start | bytes 3145732
  3.5 2.4 %collective-permute-start.1 = (bf16[256,512]{1,0:T(8,128)(2,1)S(1)}, bf16[256,512]{1,0:T(8,128)(2,1)S(1)}, u32[]{:S(2)}, u32[]{:S(2)}) collective-permute-start(bf16[256,512]{1,0:T(8,128)(2,1)S(1)} %shard_map.38), channel_id=1, source_target_pairs={{0,2},{2,0},{1,3},{3,1},{4,6},{6,4},{5,7},{7,5},{8,10},{10,8},{9,1... | collective-permute-start | bytes 786440 | tf_op jit(solution)/shard_map/ppermute | solution.py:201
  5.7 3.2 %collective-permute-start = (bf16[256,512]{1,0:T(8,128)(2,1)S(1)}, bf16[256,512]{1,0:T(8,128)(2,1)S(1)}, u32[]{:S(2)}, u32[]{:S(2)}) collective-permute-start(bf16[256,512]{1,0:T(8,128)(2,1)S(1)} %get-tuple-element.13), channel_id=1, source_target_pairs={{0,2},{2,0},{1,3},{3,1},{4,6},{6,4},{5,7},{7,5},{8,10},{10,8},{9,1... | collective-permute-start | bytes 786440 | tf_op jit(solution)/shard_map/ppermute | solution.py:201
  5.9 9.5 %collective-permute-start.2 = (bf16[256,512]{1,0:T(8,128)(2,1)S(1)}, bf16[256,512]{1,0:T(8,128)(2,1)S(1)}, u32[]{:S(2)}, u32[]{:S(2)}) collective-permute-start(bf16[256,512]{1,0:T(8,128)(2,1)S(1)} %add_convert_fusion), channel_id=1, source_target_pairs={{0,4},{4,0},{1,5},{5,1},{2,6},{6,2},{3,7},{7,3},{8,12},{12,8},{9,1... | collective-permute-start | bytes 786440 | tf_op jit(solution)/shard_map/ppermute | solution.py:201
  15.5 4.5 %collective-permute-start.3 = (bf16[64,512]{1,0:T(8,128)(2,1)S(1)}, bf16[64,512]{1,0:T(8,128)(2,1)S(1)}, u32[]{:S(2)}, u32[]{:S(2)}) collective-permute-start(bf16[64,512]{1,0:T(8,128)(2,1)S(1)} %get-tuple-element.16), channel_id=1, source_target_pairs={{0,8},{8,0},{16,24},{24,16},{1,9},{9,1},{17,25},{25,17},{2,10},{10... | collective-permute-start | bytes 196616 | tf_op jit(solution)/shard_map/ppermute | solution.py:201
  17.4 6.6 %collective-permute-start.4 = (bf16[64,512]{1,0:T(8,128)(2,1)S(1)}, bf16[64,512]{1,0:T(8,128)(2,1)S(1)}, u32[]{:S(2)}, u32[]{:S(2)}) collective-permute-start(bf16[64,512]{1,0:T(8,128)(2,1)S(1)} %get-tuple-element.17), channel_id=1, source_target_pairs={{0,16},{8,24},{16,0},{24,8},{1,17},{9,25},{17,1},{25,9},{2,18},{10... | collective-permute-start | bytes 196616 | tf_op jit(solution)/shard_map/ppermute | solution.py:201
  20.0 6.2 %collective-permute-start.5 = (bf16[64,512]{1,0:T(8,128)(2,1)S(1)}, bf16[64,512]{1,0:T(8,128)(2,1)S(1)}, u32[]{:S(2)}, u32[]{:S(2)}) collective-permute-start(bf16[64,512]{1,0:T(8,128)(2,1)S(1)} %get-tuple-element.18), channel_id=1, source_target_pairs={{0,24},{8,16},{16,8},{24,0},{1,25},{9,17},{17,9},{25,1},{2,26},{10... | collective-permute-start | bytes 196616 | tf_op jit(solution)/shard_map/ppermute | solution.py:201
  26.2 6.2 %collective-permute-start.8 = (bf16[64,512]{1,0:T(8,128)(2,1)S(1)}, bf16[64,512]{1,0:T(8,128)(2,1)S(1)}, u32[]{:S(2)}, u32[]{:S(2)}) collective-permute-start(bf16[64,512]{1,0:T(8,128)(2,1)S(1)} %add_convert_fusion.1.refs_0_), channel_id=1, source_target_pairs={{0,24},{8,16},{16,8},{24,0},{1,25},{9,17},{17,9},{25,1},{2,26},{10... | collective-permute-start | bytes 196616 | tf_op jit(solution)/shard_map/ppermute | solution.py:201
  27.3 6.4 %collective-permute-start.7 = (bf16[64,512]{1,0:T(8,128)(2,1)S(1)}, bf16[64,512]{1,0:T(8,128)(2,1)S(1)}, u32[]{:S(2)}, u32[]{:S(2)}) collective-permute-start(bf16[64,512]{1,0:T(8,128)(2,1)S(1)} %add_convert_fusion.1.refs_0_), channel_id=1, source_target_pairs={{0,16},{8,24},{16,0},{24,8},{1,17},{9,25},{17,1},{25,9},{2,18},{10... | collective-permute-start | bytes 196616 | tf_op jit(solution)/shard_map/ppermute | solution.py:201
  27.3 6.4 %collective-permute-start.6 = (bf16[64,512]{1,0:T(8,128)(2,1)S(1)}, bf16[64,512]{1,0:T(8,128)(2,1)S(1)}, u32[]{:S(2)}, u32[]{:S(2)}) collective-permute-start(bf16[64,512]{1,0:T(8,128)(2,1)S(1)} %add_convert_fusion.1.refs_0_), channel_id=1, source_target_pairs={{0,8},{8,0},{16,24},{24,16},{1,9},{9,1},{17,25},{25,17},{2,10},{10... | collective-permute-start | bytes 196616 | tf_op jit(solution)/shard_map/ppermute | solution.py:201
  30.6 3.7 %collective-permute-start.9 = (bf16[64,512]{1,0:T(8,128)(2,1)S(1)}, bf16[64,512]{1,0:T(8,128)(2,1)S(1)}, u32[]{:S(2)}, u32[]{:S(2)}) collective-permute-start(bf16[64,512]{1,0:T(8,128)(2,1)S(1)} %add_convert_fusion.1.refs_0_), channel_id=1, source_target_pairs={{0,2},{2,0},{1,3},{3,1},{4,6},{6,4},{5,7},{7,5},{8,10},{10,8},{9,1... | collective-permute-start | bytes 196616 | tf_op jit(solution)/shard_map/ppermute | solution.py:201
  32.4 1.9 %collective-permute-start.12 = (bf16[64,512]{1,0:T(8,128)(2,1)S(1)}, bf16[64,512]{1,0:T(8,128)(2,1)S(1)}, u32[]{:S(2)}, u32[]{:S(2)}) collective-permute-start(bf16[64,512]{1,0:T(8,128)(2,1)S(1)} %collective-permute-done.8.refs_3_), channel_id=1, source_target_pairs={{0,2},{2,0},{1,3},{3,1},{4,6},{6,4},{5,7},{7,5},{8,10},{10,8},{9,1... | collective-permute-start | bytes 196616 | tf_op jit(solution)/shard_map/ppermute | solution.py:201
  33.7 1.3 %collective-permute-start.11 = (bf16[64,512]{1,0:T(8,128)(2,1)S(1)}, bf16[64,512]{1,0:T(8,128)(2,1)S(1)}, u32[]{:S(2)}, u32[]{:S(2)}) collective-permute-start(bf16[64,512]{1,0:T(8,128)(2,1)S(1)} %collective-permute-done.7.refs_2_), channel_id=1, source_target_pairs={{0,2},{2,0},{1,3},{3,1},{4,6},{6,4},{5,7},{7,5},{8,10},{10,8},{9,1... | collective-permute-start | bytes 196616 | tf_op jit(solution)/shard_map/ppermute | solution.py:201
  33.7 1.4 %collective-permute-start.10 = (bf16[64,512]{1,0:T(8,128)(2,1)S(1)}, bf16[64,512]{1,0:T(8,128)(2,1)S(1)}, u32[]{:S(2)}, u32[]{:S(2)}) collective-permute-start(bf16[64,512]{1,0:T(8,128)(2,1)S(1)} %collective-permute-done.6.refs_1_), channel_id=1, source_target_pairs={{0,2},{2,0},{1,3},{3,1},{4,6},{6,4},{5,7},{7,5},{8,10},{10,8},{9,1... | collective-permute-start | bytes 196616 | tf_op jit(solution)/shard_map/ppermute | solution.py:201

commit v3 on v2

v3 whole, which is shorter than its diff:
```python
import functools

import jax
import jax.numpy as jnp
from jax import lax
from jax.experimental import pallas as pl
from jax.experimental.pallas import tpu as pltpu
from jax.sharding import PartitionSpec as P

F32 = jnp.float32
BF16 = jnp.bfloat16
VMEM = pl.BlockSpec(memory_space=pltpu.VMEM)
SMEM = pl.BlockSpec(memory_space=pltpu.SMEM)
HBM = pl.BlockSpec(memory_space=pltpu.HBM)
ROWS_IN_COLS = (((0,), (0,)), ((), ()))
COLS_IN_COLS = (((1,), (1,)), ((), ()))


def params(limit):
    return pltpu.CompilerParams(vmem_limit_bytes=limit << 20)


def gram_kernel(scale, outputs, patch_hbm, cot_hbm, *refs):
    *outs, patch, cot, patch_sems, cot_sems = refs[-4 - len(outputs) :]
    half = cot.shape[2]
    column, core, parity = lax.axis_index("x"), lax.axis_index("core"), lax.axis_index("z") % 2
    pieces = [piece for _, group in outputs for piece in group]
    slots = {}
    copies = []
    for index, (block, columns, core_flip, parity_flip) in enumerate(pieces):
        number = column ^ block
        if (block, columns) not in slots:
            slot = len(slots)
            slots[block, columns] = slot
            copies.append(
                pltpu.make_async_copy(
                    cot_hbm.at[number, :, columns * half : (columns + 1) * half],
                    cot.at[slot],
                    cot_sems.at[slot],
                )
            )
            copies[-1].start()
        first = (core ^ core_flip) * half
        width = half
        if parity_flip is not None:
            width = half // 2
            first = first + (parity ^ parity_flip) * width
        copies.append(
            pltpu.make_async_copy(
                patch_hbm.at[number, :, pl.ds(pl.multiple_of(first, width), width)],
                patch.at[index, :, :width],
                patch_sems.at[index],
            )
        )
        copies[-1].start()
    index = 0
    waiting = iter(copies)
    ready = set()
    for (dtype, group), out in zip(outputs, outs):
        row = 0
        for block, columns, _, parity_flip in group:
            if (block, columns) not in ready:
                next(waiting).wait()
                ready.add((block, columns))
            next(waiting).wait()
            width = half if parity_flip is None else half // 2
            terms = lax.dot_general(
                patch[index, :, :width],
                cot[slots[block, columns]],
                ROWS_IN_COLS,
                preferred_element_type=F32,
            )
            out[row : row + width, :] = (terms * scale).astype(dtype)
            row += width
            index += 1


def gram(patches, cotangents, after, scale, *outputs):
    _, pix, width = patches.shape
    half = width // 2
    pieces = [piece for _, group in outputs for piece in group]
    sides = len({piece[:2] for piece in pieces})
    return pl.pallas_call(
        functools.partial(gram_kernel, scale, outputs),
        out_shape=[jax.ShapeDtypeStruct((2 * half, half), dtype) for dtype, _ in outputs],
        in_specs=[HBM, HBM] + [pl.BlockSpec(memory_space=pl.ANY)] * len(after),
        out_specs=[VMEM] * len(outputs),
        scratch_shapes=[
            pltpu.VMEM((len(pieces), pix, half), BF16),
            pltpu.VMEM((sides, pix, half), BF16),
            pltpu.SemaphoreType.DMA((len(pieces),)),
            pltpu.SemaphoreType.DMA((sides,)),
        ],
        compiler_params=params(16),
        cost_estimate=pl.CostEstimate(
            flops=4 * len(outputs) * pix * half * half,
            bytes_accessed=2 * (len(pieces) + sides) * pix * half,
            transcendentals=0,
        ),
    )(
        pltpu.with_memory_space_constraint(patches, pltpu.HBM),
        pltpu.with_memory_space_constraint(cotangents, pltpu.HBM),
        *after,
    )


def leave_kernel(kept_ref, came_ref, column_ref, line_ref):
    half = column_ref.shape[0]
    column_ref[...] = (kept_ref[:half, :] + came_ref[:half, :].astype(F32)).astype(BF16)
    line_ref[...] = (kept_ref[half:, :] + came_ref[half:, :].astype(F32)).astype(BF16)


def leave(kept, came):
    half = kept.shape[1]
    return pl.pallas_call(
        leave_kernel,
        out_shape=[jax.ShapeDtypeStruct((half, half), BF16)] * 2,
        in_specs=[VMEM] * 2,
        out_specs=[VMEM] * 2,
        compiler_params=params(16),
    )(kept, came)


def middle_kernel(kept_ref, given_ref, first_ref, second_ref, own_ref, line_ref, column_ref):
    rows, half = line_ref.shape
    parity = lax.axis_index("z") % 2

    def cut(flip):
        where = pl.ds(pl.multiple_of((parity ^ flip) * rows, rows), rows)
        total = kept_ref[where, :] + given_ref[where, :].astype(F32)
        return total + first_ref[where, :].astype(F32)

    def tail(block):
        where = slice((2 + block) * rows, (3 + block) * rows)
        total = kept_ref[where, :] + given_ref[where, :].astype(F32)
        return total + second_ref[block * rows : (block + 1) * rows, :].astype(F32)

    line_ref[...] = cut(1).astype(BF16)
    column_ref[...] = tail(0).astype(BF16)
    own_ref[:, :half] = cut(0)
    own_ref[:, half:] = tail(1)


def middle(kept, given, first, second):
    half = kept.shape[1]
    rows = half // 2
    return pl.pallas_call(
        middle_kernel,
        out_shape=[
            jax.ShapeDtypeStruct((rows, 2 * half), F32),
            jax.ShapeDtypeStruct((rows, half), BF16),
            jax.ShapeDtypeStruct((rows, half), BF16),
        ],
        in_specs=[VMEM] * 4,
        out_specs=[VMEM] * 3,
        compiler_params=params(16),
    )(kept, given, first, second)


def root_kernel(counts_ref, *refs):
    pieces = refs[:4]
    keep_ref, send_ref, grad, q_left, q_right, m_left, m_right, x_left, x_right = refs[4:]
    width = grad.shape[0]
    quarter = width // 4
    rows = keep_ref.shape[0]
    place, column, core = (lax.axis_index(name) for name in ("z", "x", "core"))
    for index, ref in enumerate(pieces):
        grad[quarter * index : quarter * (index + 1), :] = ref[...]
    diagonal = lax.broadcasted_iota(jnp.int32, (width, width), 0) == lax.broadcasted_iota(
        jnp.int32, (width, width), 1
    )

    def dot(a, b):
        return jnp.dot(a, b, preferred_element_type=F32)

    def factor(moment):
        return (jnp.where(diagonal, 1.25, 0.0) - 0.25 * moment).astype(BF16)

    def begin(dims):
        stats = lax.dot_general(grad[...], grad[...], dims, preferred_element_type=F32)
        stats = stats + jnp.where(diagonal, 0.1, 0.0)
        scale = 2.5 / jnp.sqrt(jnp.sum(stats * stats, keepdims=True))
        first = jnp.sqrt(jnp.sqrt(scale)).astype(BF16).astype(F32)
        return scale * stats, first

    def spot(flip):
        row = (4 * place + 2 * (column ^ flip) + core) * rows
        part = row // quarter
        return ((part // 2 ^ core) * 2 + (part % 2 ^ place % 2)) * quarter + row % quarter

    line = lax.broadcasted_iota(jnp.int32, (2 * rows, width), 0)
    wanted = jnp.where(line < rows, spot(0) + line, spot(1) + line - rows)
    pick = lax.broadcasted_iota(jnp.int32, (2 * rows, width), 1) == wanted
    pick = jnp.where(pick, 1.0, 0.0).astype(BF16)
    moment, first = begin(COLS_IN_COLS)
    m_left[...] = moment.astype(BF16)
    factor_value = factor(moment)
    q_left[...] = factor_value
    x_left[...] = (first * dot(pick, factor_value)).astype(BF16)
    moment, first = begin(ROWS_IN_COLS)
    m_right[...] = moment.astype(BF16)
    factor_value = factor(moment)
    q_right[...] = factor_value
    x_right[...] = (first * factor_value.astype(F32)).astype(BF16)

    count_left, count_right = counts_ref[column, 0], counts_ref[column, 1]

    def sweep(index, carry):
        second_left = dot(q_left[...], q_left[...]).astype(BF16)
        second_right = dot(q_right[...], q_right[...]).astype(BF16)
        fourth_left = dot(second_left, second_left).astype(BF16)
        fourth_right = dot(second_right, second_right).astype(BF16)
        moment_left = dot(fourth_left, m_left[...])
        moment_right = dot(fourth_right, m_right[...])
        m_left[...] = moment_left.astype(BF16)
        m_right[...] = moment_right.astype(BF16)
        factor_left = factor(moment_left)
        factor_right = factor(moment_right)
        q_left[...] = factor_left
        q_right[...] = factor_right
        next_left = dot(x_left[...], factor_left).astype(BF16)
        next_right = dot(x_right[...], factor_right).astype(BF16)
        x_left[...] = jnp.where(index < count_left, next_left, x_left[...])
        x_right[...] = jnp.where(index < count_right, next_right, x_right[...])
        return carry

    lax.fori_loop(1, jnp.maximum(count_left, count_right), sweep, 0)
    partial_value = dot(x_left[...], grad[...]).astype(BF16)
    update = dot(partial_value, x_right[...])
    keep_ref[...] = update[:rows, :].astype(BF16)
    send_ref[...] = update[rows:, :].astype(BF16)


def root(counts, pieces, rows):
    width = pieces[0].shape[1]
    square = pltpu.VMEM((width, width), BF16)
    out = jax.ShapeDtypeStruct((rows, width), BF16)
    return pl.pallas_call(
        root_kernel,
        out_shape=[out, out],
        in_specs=[SMEM] + [VMEM] * 4,
        out_specs=[VMEM] * 2,
        scratch_shapes=[square] * 5 + [pltpu.VMEM((2 * rows, width), BF16), square],
        compiler_params=params(32),
    )(counts, *pieces)


def shards(line, groups, patches, cotangents, newton_counts):
    blocks, pix, width = patches.shape
    half = width // 2
    rows = half // (2 * line)
    scale = 1.0 / float(pix * 4 * line * width) ** 0.5
    column, group = lax.axis_index("x"), lax.axis_index("group")

    def swap(array, axis, mask=1):
        return lax.ppermute(array, axis, [(i, i ^ mask) for i in range(lax.axis_size(axis))])

    def pieces(core_flip, leaves):
        if leaves:
            return ((1, 0, core_flip, None), (1, 1, core_flip, 1), (0, 1, core_flip, 1))
        return ((0, 0, core_flip, None), (1, 1, core_flip, 0), (0, 1, core_flip, 0))

    (given,) = gram(patches, cotangents, (), scale, (BF16, pieces(1, True)))
    came = swap(given, "core")
    kept, given_on = gram(
        patches, cotangents, (given,), scale, (F32, pieces(0, True)), (BF16, pieces(1, False))
    )
    came_on = swap(given_on, "core")
    to_column, to_line = leave(kept, came)
    came_first = swap(to_column, "x")
    came_second = swap(to_line, "z")
    (kept_on,) = gram(patches, cotangents, (to_column,), scale, (F32, pieces(0, False)))
    own, to_line, to_column = middle(kept_on, came_on, came_first, came_second)
    from_line = swap(to_line, "z")
    from_column = swap(to_column, "x")
    own = own + jnp.concatenate([from_line, from_column], 1).astype(F32)
    mask = 2
    while mask < line:
        own = own + swap(own.astype(BF16), "z", mask).astype(F32)
        mask *= 2
    own = own.astype(BF16)
    other = swap(own, "z")
    near = jnp.concatenate([own, other], 0)
    far = swap(near, "core")
    quarter = width // 4
    keep, send = root(newton_counts, [own, other, far[:quarter], far[quarter:]], rows)

    found = []
    for turn in range(groups):
        pair = []
        for flip in range(2):
            moves = [
                (c * groups + g, (c ^ flip) * groups + (g ^ turn))
                for c in range(2)
                for g in range(groups)
            ]
            piece = send if flip else keep
            pair.append(lax.ppermute(piece, ("x", "group"), moves) if turn or flip else piece)
        found.append(jnp.stack(pair))
    found = jnp.stack(found)
    found = jnp.where(column == 0, found, found[:, ::-1])
    bit = 1
    while bit < groups:
        shape = (groups // (2 * bit), 2, bit) + found.shape[1:]
        flipped = found.reshape(shape)[:, ::-1].reshape(found.shape)
        found = jnp.where(group & bit == 0, found, flipped)
        bit *= 2
    return found.reshape(blocks * groups, rows, width)


def solution(mesh):
    devices, groups = mesh.shape["dp"], mesh.shape["group"]
    line = devices // 4
    cut = jax.sharding.Mesh(
        mesh.devices.reshape(line, 2, 2, groups), ("z", "x", "core", "group")
    )
    dp = ("z", "x", "core")
    placed = (P("group", dp, None), P("group", dp, None), P("group", None))
    return jax.shard_map(
        functools.partial(shards, line, groups),
        mesh=cut,
        in_specs=placed,
        out_specs=P(None, dp, None),
        check_vma=False,
    )
```

time: 54 us -> 51.8 us (0.959)
  blocking collectives: 10.5 us -> 0 us
  Pallas kernels: 10.3 us -> 16.3 us
  waiting for transfers between devices: 16.4 us -> 20 us
  local copies, waits for them, and re-layouts: 3.11 us -> 0.69 us
    all_to_all x1 -> x0, blocking collectives: 10.5 us -> none  [shards(): return lax.all_to_all(update, ('group', 'x'), 0, 0, tiled=True)]
    pallas_call x4 -> x6, Pallas kernels: 10.3 us -> 16.3 us  [the longest x1 9.71 us: root(): pl.pallas_call(root_kernel, out_shape=[out, out], in_specs=[SMEM] + [VMEM...]
    ppermute x0 -> x3, starting transfers between devices: none -> 3.54 us  [shards(): lax.ppermute(piece, ('x', 'group'), moves)]
    ppermute x0 -> x3, waiting for transfers between devices: none -> 3.4 us  [shards(): lax.ppermute(piece, ('x', 'group'), moves)]
    ppermute x13 -> x9, starting transfers between devices: 13.2 us -> 10.2 us  [swap(): lax.ppermute(array, axis, [(i, i ^ mask) for i in range(lax.axis_size(axi...]
    unnamed x7 -> x2, local copies, waits for them, and re-layouts: 3.11 us -> 0.67 us
    select_n x0 -> x2, other arithmetic: none -> 0.71 us  [the longest x1 0.68 us: shards(): found = jnp.where(group & bit == 0, found, flipped)]
    ppermute x13 -> x9, waiting for transfers between devices: 16.4 us -> 16.6 us  [swap(): lax.ppermute(array, axis, [(i, i ^ mask) for i in range(lax.axis_size(axi...]
  transfers between devices with their start and end apart: 13 -> 12, of which waited for: 7 -> 9; matrix products, arithmetic and copies ran while one was open for 0% -> 0% of each run, Pallas kernels for 3% -> 9%
where the time goes in v3:
time: 51.8 us; the launch traced here: 51.6 us
  waiting for transfers between devices  20 us (39%)
  Pallas kernels  16.3 us (31%)
  starting transfers between devices  13.7 us (26%)
  other arithmetic  0.84 us (2%)
  local copies, waits for them, and re-layouts  0.69 us (1%)
    ppermute x9, waiting for transfers between devices, swap(): lax.ppermute(array, axis, [(i, i ^ mask) for i in range(lax.axis_size(axi...  16.6 us
    ppermute x9, starting transfers between devices, swap(): lax.ppermute(array, axis, [(i, i ^ mask) for i in range(lax.axis_size(axi...  10.2 us
    pallas_call x1, Pallas kernels, root(): pl.pallas_call(root_kernel, out_shape=[out, out], in_specs=[SMEM] + [VMEM...  9.71 us
    pallas_call x3, Pallas kernels, gram(): pl.pallas_call(functools.partial(gram_kernel, scale, outputs), out_shape=...  6.43 us
    ppermute x3, starting transfers between devices, shards(): lax.ppermute(piece, ('x', 'group'), moves)  3.54 us
    ppermute x3, waiting for transfers between devices, shards(): lax.ppermute(piece, ('x', 'group'), moves)  3.4 us
  transfers between devices with their start and end apart: 12, of which 9 were waited for; matrix products, arithmetic and copies ran while one was open for 0% of the time, Pallas kernels for 9%

profile of v3, /device:TPU:0, one launch (start us, length us, event | category | flops | bytes accessed | tf_op | source)
XLA Modules:
  0.0 51.6 jit_solution(6146553597296702459)
XLA Ops:
  0.0 1.9 %shard_map.37.refs_0_ = bf16[512,256]{1,0:T(8,128)(2,1)S(1)} custom-call(bf16[2,512,512]{2,1,0:T(8,128)(2,1)} %patch_hbm.5, bf16[2,512,512]{2,1,0:T(8,128)(2,1)} %cot_hbm.5), custom_call_target="tpu_custom_call" | custom-call | flops 134217728 | bytes 1572864 | tf_op jit(solution)/shard_map/pallas_call | solution.py:83
  1.9 0.5 %collective-permute-start = (bf16[512,256]{1,0:T(8,128)(2,1)S(1)}, bf16[512,256]{1,0:T(8,128)(2,1)S(1)}, u32[]{:S(2)}, u32[]{:S(2)}) collective-permute-start(bf16[512,256]{1,0:T(8,128)(2,1)S(1)} %shard_map.37.refs_0_), channel_id=1, source_target_pairs={{0,2},{2,0},{1,3},{3,1},{4,6},{6,4},{5,7},{7,5},{8,10},{10,8},{9,1... | collective-permute-start | bytes 786440 | tf_op jit(solution)/shard_map/ppermute | solution.py:256
  2.4 2.7 %shard_map.38 = (f32[512,256]{1,0:T(8,128)S(1)}, bf16[512,256]{1,0:T(8,128)(2,1)S(1)}) custom-call(bf16[2,512,512]{2,1,0:T(8,128)(2,1)} %patch_hbm.5, bf16[2,512,512]{2,1,0:T(8,128)(2,1)} %cot_hbm.5, bf16[512,256]{1,0:T(8,128)(2,1)S(1)} %shard_map.37.refs_0_), custom_call_target="tpu_custom_call" | custom-call | flops 268435456 | bytes 2621440 | tf_op jit(solution)/shard_map/pallas_call | solution.py:83
  5.1 0.1 collective-permute-start.1
  5.2 0.0 collective-permute-done.came_ref
  5.3 3.0 %collective-permute-start.2 = (bf16[256,256]{1,0:T(8,128)(2,1)S(1)}, bf16[256,256]{1,0:T(8,128)(2,1)S(1)}, u32[]{:S(2)}, u32[]{:S(2)}) collective-permute-start(bf16[256,256]{1,0:T(8,128)(2,1)S(1)} %get-tuple-element.15.refs_0_), channel_id=1, source_target_pairs={{0,4},{4,0},{1,5},{5,1},{2,6},{6,2},{3,7},{7,3},{8,12},{12,8},{9,1... | collective-permute-start | bytes 393224 | tf_op jit(solution)/shard_map/ppermute | solution.py:256
  8.3 1.6 %collective-permute-start.3 = (bf16[256,256]{1,0:T(8,128)(2,1)S(1)}, bf16[256,256]{1,0:T(8,128)(2,1)S(1)}, u32[]{:S(2)}, u32[]{:S(2)}) collective-permute-start(bf16[256,256]{1,0:T(8,128)(2,1)S(1)} %get-tuple-element.17), channel_id=1, source_target_pairs={{0,8},{8,0},{16,24},{24,16},{1,9},{9,1},{17,25},{25,17},{2,10},{10... | collective-permute-start | bytes 393224 | tf_op jit(solution)/shard_map/ppermute | solution.py:256
  9.9 1.9 %shard_map.40.kept_ref = f32[512,256]{1,0:T(8,128)S(1)} custom-call(bf16[2,512,512]{2,1,0:T(8,128)(2,1)} %patch_hbm.5, bf16[2,512,512]{2,1,0:T(8,128)(2,1)} %cot_hbm.5, bf16[256,256]{1,0:T(8,128)(2,1)S(1)} %get-tuple-element.15.refs_0_), custom_call_target="tpu_custom_call" | custom-call | flops 134217728 | bytes 1572864 | tf_op jit(solution)/shard_map/pallas_call | solution.py:83
  11.7 0.0 collective-permute-done.1.given_ref
  11.7 0.2 collective-permute-done.2.first_ref
  12.0 1.5 %collective-permute-done.3.second_ref = bf16[256,256]{1,0:T(8,128)(2,1)S(1)} collective-permute-done((bf16[256,256]{1,0:T(8,128)(2,1)S(1)}, bf16[256,256]{1,0:T(8,128)(2,1)S(1)}, u32[]{:S(2)}, u32[]{:S(2)}) %collective-permute-start.3) | collective-permute-done | bytes 131104 | tf_op jit(solution)/shard_map/ppermute | solution.py:256
  13.4 0.1 shard_map.41
  13.5 1.6 %collective-permute-start.4 = (bf16[128,256]{1,0:T(8,128)(2,1)S(1)}, bf16[128,256]{1,0:T(8,128)(2,1)S(1)}, u32[]{:S(2)}, u32[]{:S(2)}) collective-permute-start(bf16[128,256]{1,0:T(8,128)(2,1)S(1)} %get-tuple-element.19), channel_id=1, source_target_pairs={{0,8},{8,0},{16,24},{24,16},{1,9},{9,1},{17,25},{25,17},{2,10},{10... | collective-permute-start | bytes 196616 | tf_op jit(solution)/shard_map/ppermute | solution.py:256
  15.2 0.5 %collective-permute-start.5 = (bf16[128,256]{1,0:T(8,128)(2,1)S(1)}, bf16[128,256]{1,0:T(8,128)(2,1)S(1)}, u32[]{:S(2)}, u32[]{:S(2)}) collective-permute-start(bf16[128,256]{1,0:T(8,128)(2,1)S(1)} %get-tuple-element.20), channel_id=1, source_target_pairs={{0,4},{4,0},{1,5},{5,1},{2,6},{6,2},{3,7},{7,3},{8,12},{12,8},{9,1... | collective-permute-start | bytes 196616 | tf_op jit(solution)/shard_map/ppermute | solution.py:256
  15.7 2.2 %collective-permute-done.4 = bf16[128,256]{1,0:T(8,128)(2,1)S(1)} collective-permute-done((bf16[128,256]{1,0:T(8,128)(2,1)S(1)}, bf16[128,256]{1,0:T(8,128)(2,1)S(1)}, u32[]{:S(2)}, u32[]{:S(2)}) %collective-permute-start.4) | collective-permute-done | bytes 65568 | tf_op jit(solution)/shard_map/ppermute | solution.py:256
  17.8 1.6 %collective-permute-done.5 = bf16[128,256]{1,0:T(8,128)(2,1)S(1)} collective-permute-done((bf16[128,256]{1,0:T(8,128)(2,1)S(1)}, bf16[128,256]{1,0:T(8,128)(2,1)S(1)}, u32[]{:S(2)}, u32[]{:S(2)}) %collective-permute-start.5) | collective-permute-done | bytes 65568 | tf_op jit(solution)/shard_map/ppermute | solution.py:256
  19.5 2.7 %collective-permute-start.6 = (bf16[128,512]{1,0:T(8,128)(2,1)S(1)}, bf16[128,512]{1,0:T(8,128)(2,1)S(1)}, u32[]{:S(2)}, u32[]{:S(2)}) collective-permute-start(bf16[128,512]{1,0:T(8,128)(2,1)S(1)} %fusion), channel_id=1, source_target_pairs={{0,16},{8,24},{16,0},{24,8},{1,17},{9,25},{17,1},{25,9},{2,18},{10... | collective-permute-start | bytes 393224 | tf_op jit(solution)/shard_map/ppermute | solution.py:256
  22.1 4.7 %collective-permute-done.6 = bf16[128,512]{1,0:T(8,128)(2,1)S(1)} collective-permute-done((bf16[128,512]{1,0:T(8,128)(2,1)S(1)}, bf16[128,512]{1,0:T(8,128)(2,1)S(1)}, u32[]{:S(2)}, u32[]{:S(2)}) %collective-permute-start.6) | collective-permute-done | bytes 131104 | tf_op jit(solution)/shard_map/ppermute | solution.py:256
  26.8 0.1 add_convert_fusion.refs_0_
  26.8 0.1 collective-permute-start.7
  26.9 5.0 %collective-permute-done.7.refs_1_ = bf16[128,512]{1,0:T(8,128)(2,1)S(1)} collective-permute-done((bf16[128,512]{1,0:T(8,128)(2,1)S(1)}, bf16[128,512]{1,0:T(8,128)(2,1)S(1)}, u32[]{:S(2)}, u32[]{:S(2)}) %collective-permute-start.7) | collective-permute-done | bytes 131104 | tf_op jit(solution)/shard_map/ppermute | solution.py:256
  31.9 0.1 collective-permute-start.8
  32.0 1.5 %collective-permute-done.8 = bf16[256,512]{1,0:T(8,128)(2,1)S(1)} collective-permute-done((bf16[256,512]{1,0:T(8,128)(2,1)S(1)}, bf16[256,512]{1,0:T(8,128)(2,1)S(1)}, u32[]{:S(2)}, u32[]{:S(2)}) %collective-permute-start.8) | collective-permute-done | bytes 262176 | tf_op jit(solution)/shard_map/ppermute | solution.py:256
  33.5 0.0 copy-start
  33.5 0.7 %copy-done = s32[2,2]{1,0:T(2,128)S(1)} copy-done((s32[2,2]{1,0:T(2,128)S(1)}, s32[2,2]{1,0:T(2,128)}, u32[]{:S(2)}) %copy-start) | copy-done | bytes 40
  34.2 9.7 %shard_map.42 = (bf16[32,512]{1,0:T(8,128)(2,1)S(1)}, bf16[32,512]{1,0:T(8,128)(2,1)S(1)}) custom-call(s32[2,2]{1,0:T(2,128)S(1)} %copy-done, bf16[128,512]{1,0:T(8,128)(2,1)S(1)} %add_convert_fusion.refs_0_, bf16[128,512]{1,0:T(8,128)(2,1)S(1)} %collective-permute-done.7.refs_1_, bf16[128,512]{1,0:T(8,128)(2,1)S(1)} %get-tuple-element.24.refs_2_, ...), custom_call_target="tpu_custom_call" | custom-call | tf_op jit(solution)/shard_map/pallas_call | solution.py:238
  43.9 0.1 collective-permute-start.9
  44.0 3.0 %collective-permute-start.11 = (bf16[32,512]{1,0:T(8,128)(2,1)S(1)}, bf16[32,512]{1,0:T(8,128)(2,1)S(1)}, u32[]{:S(2)}, u32[]{:S(2)}) collective-permute-start(bf16[32,512]{1,0:T(8,128)(2,1)S(1)} %get-tuple-element.22), channel_id=1, source_target_pairs={{0,5},{1,4},{4,1},{5,0},{2,7},{3,6},{6,3},{7,2},{8,13},{9,12},{12,... | collective-permute-start | bytes 98312 | tf_op jit(solution)/shard_map/ppermute | solution.py:298
  47.0 0.5 collective-permute-start.10
  47.5 0.6 %collective-permute-done.9 = bf16[32,512]{1,0:T(8,128)(2,1)S(1)} collective-permute-done((bf16[32,512]{1,0:T(8,128)(2,1)S(1)}, bf16[32,512]{1,0:T(8,128)(2,1)S(1)}, u32[]{:S(2)}, u32[]{:S(2)}) %collective-permute-start.9) | collective-permute-done | bytes 32800 | tf_op jit(solution)/shard_map/ppermute | solution.py:298
  48.0 2.8 %collective-permute-done.10 = bf16[32,512]{1,0:T(8,128)(2,1)S(1)} collective-permute-done((bf16[32,512]{1,0:T(8,128)(2,1)S(1)}, bf16[32,512]{1,0:T(8,128)(2,1)S(1)}, u32[]{:S(2)}, u32[]{:S(2)}) %collective-permute-start.10) | collective-permute-done | bytes 32800 | tf_op jit(solution)/shard_map/ppermute | solution.py:298
  50.9 0.0 collective-permute-done.11
  51.0 0.7 %reverse_select_fusion = bf16[2,2,32,512]{3,2,1,0:T(8,128)(2,1)} fusion(bf16[2,2,32,512]{3,2,1,0:T(8,128)(2,1)S(1)} %reverse_select_fusion.1, pred[]{:T(512)S(6)} %eq.6), kind=kLoop, calls=%fused_computation.3 | loop fusion | flops 65536 | bytes 262145 | tf_op jit(solution)/shard_map/jit(_where)/select_n | solution.py:306
  (8 shorter events, 0.2 us)
Async XLA Ops:
  1.9 3.3 %collective-permute-start = (bf16[512,256]{1,0:T(8,128)(2,1)S(1)}, bf16[512,256]{1,0:T(8,128)(2,1)S(1)}, u32[]{:S(2)}, u32[]{:S(2)}) collective-permute-start(bf16[512,256]{1,0:T(8,128)(2,1)S(1)} %shard_map.37.refs_0_), channel_id=1, source_target_pairs={{0,2},{2,0},{1,3},{3,1},{4,6},{6,4},{5,7},{7,5},{8,10},{10,8},{9,1... | collective-permute-start | bytes 786440 | tf_op jit(solution)/shard_map/ppermute | solution.py:256
  5.1 6.6 %collective-permute-start.1 = (bf16[512,256]{1,0:T(8,128)(2,1)S(1)}, bf16[512,256]{1,0:T(8,128)(2,1)S(1)}, u32[]{:S(2)}, u32[]{:S(2)}) collective-permute-start(bf16[512,256]{1,0:T(8,128)(2,1)S(1)} %get-tuple-element.16), channel_id=1, source_target_pairs={{0,2},{2,0},{1,3},{3,1},{4,6},{6,4},{5,7},{7,5},{8,10},{10,8},{9,1... | collective-permute-start | bytes 786440 | tf_op jit(solution)/shard_map/ppermute | solution.py:256
  5.3 6.7 %collective-permute-start.2 = (bf16[256,256]{1,0:T(8,128)(2,1)S(1)}, bf16[256,256]{1,0:T(8,128)(2,1)S(1)}, u32[]{:S(2)}, u32[]{:S(2)}) collective-permute-start(bf16[256,256]{1,0:T(8,128)(2,1)S(1)} %get-tuple-element.15.refs_0_), channel_id=1, source_target_pairs={{0,4},{4,0},{1,5},{5,1},{2,6},{6,2},{3,7},{7,3},{8,12},{12,8},{9,1... | collective-permute-start | bytes 393224 | tf_op jit(solution)/shard_map/ppermute | solution.py:256
  8.3 5.2 %collective-permute-start.3 = (bf16[256,256]{1,0:T(8,128)(2,1)S(1)}, bf16[256,256]{1,0:T(8,128)(2,1)S(1)}, u32[]{:S(2)}, u32[]{:S(2)}) collective-permute-start(bf16[256,256]{1,0:T(8,128)(2,1)S(1)} %get-tuple-element.17), channel_id=1, source_target_pairs={{0,8},{8,0},{16,24},{24,16},{1,9},{9,1},{17,25},{25,17},{2,10},{10... | collective-permute-start | bytes 393224 | tf_op jit(solution)/shard_map/ppermute | solution.py:256
  13.5 4.3 %collective-permute-start.4 = (bf16[128,256]{1,0:T(8,128)(2,1)S(1)}, bf16[128,256]{1,0:T(8,128)(2,1)S(1)}, u32[]{:S(2)}, u32[]{:S(2)}) collective-permute-start(bf16[128,256]{1,0:T(8,128)(2,1)S(1)} %get-tuple-element.19), channel_id=1, source_target_pairs={{0,8},{8,0},{16,24},{24,16},{1,9},{9,1},{17,25},{25,17},{2,10},{10... | collective-permute-start | bytes 196616 | tf_op jit(solution)/shard_map/ppermute | solution.py:256
  15.2 4.3 %collective-permute-start.5 = (bf16[128,256]{1,0:T(8,128)(2,1)S(1)}, bf16[128,256]{1,0:T(8,128)(2,1)S(1)}, u32[]{:S(2)}, u32[]{:S(2)}) collective-permute-start(bf16[128,256]{1,0:T(8,128)(2,1)S(1)} %get-tuple-element.20), channel_id=1, source_target_pairs={{0,4},{4,0},{1,5},{5,1},{2,6},{6,2},{3,7},{7,3},{8,12},{12,8},{9,1... | collective-permute-start | bytes 196616 | tf_op jit(solution)/shard_map/ppermute | solution.py:256
  19.5 7.3 %collective-permute-start.6 = (bf16[128,512]{1,0:T(8,128)(2,1)S(1)}, bf16[128,512]{1,0:T(8,128)(2,1)S(1)}, u32[]{:S(2)}, u32[]{:S(2)}) collective-permute-start(bf16[128,512]{1,0:T(8,128)(2,1)S(1)} %fusion), channel_id=1, source_target_pairs={{0,16},{8,24},{16,0},{24,8},{1,17},{9,25},{17,1},{25,9},{2,18},{10... | collective-permute-start | bytes 393224 | tf_op jit(solution)/shard_map/ppermute | solution.py:256
  26.8 5.0 %collective-permute-start.7 = (bf16[128,512]{1,0:T(8,128)(2,1)S(1)}, bf16[128,512]{1,0:T(8,128)(2,1)S(1)}, u32[]{:S(2)}, u32[]{:S(2)}) collective-permute-start(bf16[128,512]{1,0:T(8,128)(2,1)S(1)} %add_convert_fusion.refs_0_), channel_id=1, source_target_pairs={{0,8},{8,0},{16,24},{24,16},{1,9},{9,1},{17,25},{25,17},{2,10},{10... | collective-permute-start | bytes 393224 | tf_op jit(solution)/shard_map/ppermute | solution.py:256
  31.9 1.6 %collective-permute-start.8 = (bf16[256,512]{1,0:T(8,128)(2,1)S(1)}, bf16[256,512]{1,0:T(8,128)(2,1)S(1)}, u32[]{:S(2)}, u32[]{:S(2)}) collective-permute-start(bf16[256,512]{1,0:T(8,128)(2,1)S(1)} %pad_maximum_fusion), channel_id=1, source_target_pairs={{0,2},{2,0},{1,3},{3,1},{4,6},{6,4},{5,7},{7,5},{8,10},{10,8},{9,1... | collective-permute-start | bytes 786440 | tf_op jit(solution)/shard_map/ppermute | solution.py:256
  33.5 0.7 %copy-start = (s32[2,2]{1,0:T(2,128)S(1)}, s32[2,2]{1,0:T(2,128)}, u32[]{:S(2)}) copy-start(s32[2,2]{1,0:T(2,128)} %counts_ref.1) | copy-start | bytes 52
  43.9 4.1 %collective-permute-start.9 = (bf16[32,512]{1,0:T(8,128)(2,1)S(1)}, bf16[32,512]{1,0:T(8,128)(2,1)S(1)}, u32[]{:S(2)}, u32[]{:S(2)}) collective-permute-start(bf16[32,512]{1,0:T(8,128)(2,1)S(1)} %get-tuple-element.22), channel_id=1, source_target_pairs={{0,4},{1,5},{4,0},{5,1},{2,6},{3,7},{6,2},{7,3},{8,12},{9,13},{12,... | collective-permute-start | bytes 98312 | tf_op jit(solution)/shard_map/ppermute | solution.py:298
  44.0 6.9 %collective-permute-start.11 = (bf16[32,512]{1,0:T(8,128)(2,1)S(1)}, bf16[32,512]{1,0:T(8,128)(2,1)S(1)}, u32[]{:S(2)}, u32[]{:S(2)}) collective-permute-start(bf16[32,512]{1,0:T(8,128)(2,1)S(1)} %get-tuple-element.22), channel_id=1, source_target_pairs={{0,5},{1,4},{4,1},{5,0},{2,7},{3,6},{6,3},{7,2},{8,13},{9,12},{12,... | collective-permute-start | bytes 98312 | tf_op jit(solution)/shard_map/ppermute | solution.py:298
  47.0 3.9 %collective-permute-start.10 = (bf16[32,512]{1,0:T(8,128)(2,1)S(1)}, bf16[32,512]{1,0:T(8,128)(2,1)S(1)}, u32[]{:S(2)}, u32[]{:S(2)}) collective-permute-start(bf16[32,512]{1,0:T(8,128)(2,1)S(1)} %get-tuple-element.21), channel_id=1, source_target_pairs={{0,1},{1,0},{4,5},{5,4},{2,3},{3,2},{6,7},{7,6},{8,9},{9,8},{12,13... | collective-permute-start | bytes 98312 | tf_op jit(solution)/shard_map/ppermute | solution.py:298

commit v4 on v3

v4 whole, which is shorter than its diff:
```python
import functools

import jax
import jax.numpy as jnp
from jax import lax
from jax.experimental import pallas as pl
from jax.experimental.pallas import tpu as pltpu
from jax.sharding import PartitionSpec as P

F32 = jnp.float32
BF16 = jnp.bfloat16
VMEM = pl.BlockSpec(memory_space=pltpu.VMEM)
SMEM = pl.BlockSpec(memory_space=pltpu.SMEM)
HBM = pl.BlockSpec(memory_space=pltpu.HBM)
ROWS_IN_COLS = (((0,), (0,)), ((), ()))
COLS_IN_COLS = (((1,), (1,)), ((), ()))


def params(limit):
    return pltpu.CompilerParams(vmem_limit_bytes=limit << 20)


def piece_sum(patch, cot, scale, piece):
    block, columns, side, quarter = piece
    half = patch.shape[3]
    rows = slice(None) if quarter is None else slice(quarter * half // 2, (quarter + 1) * half // 2)
    terms = lax.dot_general(
        patch[block, side, :, rows],
        cot[block, :, columns * half : (columns + 1) * half],
        ROWS_IN_COLS,
        preferred_element_type=F32,
    )
    return terms * scale


def write_pieces(patch, cot, scale, pieces, out):
    row = 0
    for piece in pieces:
        value = piece_sum(patch, cot, scale, piece)
        out[row : row + value.shape[0], :] = value.astype(out.dtype)
        row += value.shape[0]


def load_kernel(scale, pieces, patch_hbm, cot_hbm, out, patch, cot, sems):
    half = patch.shape[3]
    width = half // 2
    column, core, parity = lax.axis_index("x"), lax.axis_index("core"), lax.axis_index("z") % 2
    copies = []

    def fetch(source, target):
        copies.append(pltpu.make_async_copy(source, target, sems.at[len(copies)]))
        copies[-1].start()

    def fetch_patch(block, side):
        for quarter in range(2):
            first = (core ^ side) * half + (parity ^ quarter) * width
            fetch(
                patch_hbm.at[column ^ block, :, pl.ds(pl.multiple_of(first, width), width)],
                patch.at[block, side, :, quarter * width : (quarter + 1) * width],
            )

    for block in (1, 0):
        fetch(cot_hbm.at[column ^ block], cot.at[block])
        fetch_patch(block, 1)
    needed = len(copies)
    for block in (1, 0):
        fetch_patch(block, 0)
    for copy in copies[:needed]:
        copy.wait()
    write_pieces(patch, cot, scale, pieces, out)
    for copy in copies[needed:]:
        copy.wait()


def load(patches, cotangents, scale, pieces):
    blocks, pix, width = patches.shape
    half = width // 2
    return pl.pallas_call(
        functools.partial(load_kernel, scale, pieces),
        out_shape=[
            jax.ShapeDtypeStruct((2 * half, half), BF16),
            jax.ShapeDtypeStruct((blocks, 2, pix, half), BF16),
            jax.ShapeDtypeStruct((blocks, pix, width), BF16),
        ],
        in_specs=[HBM, HBM],
        out_specs=[VMEM] * 3,
        scratch_shapes=[pltpu.SemaphoreType.DMA((10,))],
        compiler_params=params(16),
    )(
        pltpu.with_memory_space_constraint(patches, pltpu.HBM),
        pltpu.with_memory_space_constraint(cotangents, pltpu.HBM),
    )


def gram_kernel(scale, outputs, patch, cot, *refs):
    for (_, pieces), out in zip(outputs, refs[-len(outputs) :]):
        write_pieces(patch, cot, scale, pieces, out)


def gram(patch, cot, after, scale, *outputs):
    pix, half = patch.shape[2:]
    return pl.pallas_call(
        functools.partial(gram_kernel, scale, outputs),
        out_shape=[jax.ShapeDtypeStruct((2 * half, half), dtype) for dtype, _ in outputs],
        in_specs=[VMEM, VMEM] + [pl.BlockSpec(memory_space=pl.ANY)] * len(after),
        out_specs=[VMEM] * len(outputs),
        compiler_params=params(16),
        cost_estimate=pl.CostEstimate(
            flops=4 * len(outputs) * pix * half * half,
            bytes_accessed=2 * (patch.size + cot.size),
            transcendentals=0,
        ),
    )(patch, cot, *after)


def add(*values):
    total = values[0]
    for value in values[1:]:
        total = total + value.astype(F32)
    return total


def root_kernel(counts_hbm, *refs):
    pieces = refs[:6]
    keep_ref, send_ref, grad, q_left, q_right, m_left, m_right, x_left, x_right, counts, sem = refs[6:]
    counts_copy = pltpu.make_async_copy(counts_hbm, counts, sem)
    counts_copy.start()
    width = grad.shape[0]
    half, quarter = width // 2, width // 4
    rows = keep_ref.shape[0]
    place, column, core = (lax.axis_index(name) for name in ("z", "x", "core"))
    for index in range(2):
        own, other, far = pieces[3 * index : 3 * index + 3]
        columns = slice(half * index, half * (index + 1))
        grad[:quarter, columns] = own[...]
        grad[quarter:half, columns] = other[...]
        grad[half:, columns] = far[...]
    diagonal = lax.broadcasted_iota(jnp.int32, (width, width), 0) == lax.broadcasted_iota(
        jnp.int32, (width, width), 1
    )

    def dot(a, b):
        return jnp.dot(a, b, preferred_element_type=F32)

    def factor(moment):
        return (jnp.where(diagonal, 1.25, 0.0) - 0.25 * moment).astype(BF16)

    def begin(dims):
        stats = lax.dot_general(grad[...], grad[...], dims, preferred_element_type=F32)
        stats = stats + jnp.where(diagonal, 0.1, 0.0)
        scale = 2.5 / jnp.sqrt(jnp.sum(stats * stats, keepdims=True))
        first = jnp.sqrt(jnp.sqrt(scale)).astype(BF16).astype(F32)
        return scale * stats, first

    def spot(flip):
        row = (4 * place + 2 * (column ^ flip) + core) * rows
        part = row // quarter
        return ((part // 2 ^ core) * 2 + (part % 2 ^ place % 2)) * quarter + row % quarter

    line = lax.broadcasted_iota(jnp.int32, (2 * rows, width), 0)
    wanted = jnp.where(line < rows, spot(0) + line, spot(1) + line - rows)
    pick = lax.broadcasted_iota(jnp.int32, (2 * rows, width), 1) == wanted
    pick = jnp.where(pick, 1.0, 0.0).astype(BF16)
    moment, first = begin(COLS_IN_COLS)
    m_left[...] = moment.astype(BF16)
    factor_value = factor(moment)
    q_left[...] = factor_value
    x_left[...] = (first * dot(pick, factor_value)).astype(BF16)
    moment, first = begin(ROWS_IN_COLS)
    m_right[...] = moment.astype(BF16)
    factor_value = factor(moment)
    q_right[...] = factor_value
    x_right[...] = (first * factor_value.astype(F32)).astype(BF16)

    counts_copy.wait()
    count_left, count_right = counts[column, 0], counts[column, 1]

    def sweep(index, carry):
        second_left = dot(q_left[...], q_left[...]).astype(BF16)
        second_right = dot(q_right[...], q_right[...]).astype(BF16)
        fourth_left = dot(second_left, second_left).astype(BF16)
        fourth_right = dot(second_right, second_right).astype(BF16)
        moment_left = dot(fourth_left, m_left[...])
        moment_right = dot(fourth_right, m_right[...])
        m_left[...] = moment_left.astype(BF16)
        m_right[...] = moment_right.astype(BF16)
        factor_left = factor(moment_left)
        factor_right = factor(moment_right)
        q_left[...] = factor_left
        q_right[...] = factor_right
        next_left = dot(x_left[...], factor_left).astype(BF16)
        next_right = dot(x_right[...], factor_right).astype(BF16)
        x_left[...] = jnp.where(index < count_left, next_left, x_left[...])
        x_right[...] = jnp.where(index < count_right, next_right, x_right[...])
        return carry

    lax.fori_loop(1, jnp.maximum(count_left, count_right), sweep, 0)
    partial_value = dot(x_left[...], grad[...]).astype(BF16)
    update = dot(partial_value, x_right[...])
    keep_ref[...] = update[:rows, :].astype(BF16)
    send_ref[...] = update[rows:, :].astype(BF16)


def root(counts, pieces, rows):
    width = 4 * pieces[0].shape[0]
    square = pltpu.VMEM((width, width), BF16)
    out = jax.ShapeDtypeStruct((rows, width), BF16)
    return pl.pallas_call(
        root_kernel,
        out_shape=[out, out],
        in_specs=[HBM] + [VMEM] * 6,
        out_specs=[VMEM] * 2,
        scratch_shapes=[square] * 5
        + [
            pltpu.VMEM((2 * rows, width), BF16),
            square,
            pltpu.SMEM(counts.shape, jnp.int32),
            pltpu.SemaphoreType.DMA(()),
        ],
        compiler_params=params(32),
    )(pltpu.with_memory_space_constraint(counts, pltpu.HBM), *pieces)


def shards(line, groups, patches, cotangents, newton_counts):
    blocks, pix, width = patches.shape
    half, quarter = width // 2, width // 4
    rows = half // (2 * line)
    scale = 1.0 / float(pix * 4 * line * width) ** 0.5
    column, group = lax.axis_index("x"), lax.axis_index("group")

    def swap(array, axis, mask=1):
        return lax.ppermute(array, axis, [(i, i ^ mask) for i in range(lax.axis_size(axis))])

    def leaving(side):
        return ((1, 0, side, None), (1, 1, side, 1), (0, 1, side, 1))

    def staying(side):
        return ((0, 0, side, None), (1, 1, side, 0), (0, 1, side, 0))

    given, patch, cot = load(patches, cotangents, scale, leaving(1))
    came = swap(given, "core")
    kept, given_on = gram(patch, cot, (), scale, (F32, leaving(0)), (BF16, staying(1)))
    came_on = swap(given_on, "core")
    to_column = add(kept[:half], came[:half]).astype(BF16)
    to_line = add(kept[half:], came[half:]).astype(BF16)
    from_column = swap(to_column, "x")
    from_line = swap(to_line, "z")
    (kept_on,) = gram(patch, cot, (to_column,), scale, (F32, staying(0)))
    left = add(kept_on[:half], came_on[:half], from_column)
    from_line_left = swap(left[quarter:].astype(BF16), "z")
    right = add(kept_on[half:], came_on[half:], from_line)
    from_column_right = swap(right[:quarter].astype(BF16), "x")
    streams = [add(left[:quarter], from_line_left), add(right[quarter:], from_column_right)]
    mask = 2
    while mask < line:
        streams = [add(own, swap(own.astype(BF16), "z", mask)) for own in streams]
        mask *= 2
    pieces = []
    for own in streams:
        own = own.astype(BF16)
        other = swap(own, "z")
        pieces += [own, other, swap(jnp.concatenate([own, other], 0), "core")]
    keep, send = root(newton_counts, pieces, rows)

    found = []
    for turn in range(groups):
        pair = []
        for flip in range(2):
            moves = [
                (c * groups + g, (c ^ flip) * groups + (g ^ turn))
                for c in range(2)
                for g in range(groups)
            ]
            piece = send if flip else keep
            pair.append(lax.ppermute(piece, ("x", "group"), moves) if turn or flip else piece)
        found.append(jnp.stack(pair))
    found = jnp.stack(found)
    found = jnp.where(column == 0, found, found[:, ::-1])
    bit = 1
    while bit < groups:
        shape = (groups // (2 * bit), 2, bit) + found.shape[1:]
        flipped = found.reshape(shape)[:, ::-1].reshape(found.shape)
        found = jnp.where(group & bit == 0, found, flipped)
        bit *= 2
    return found.reshape(blocks * groups, rows, width)


def solution(mesh):
    devices, groups = mesh.shape["dp"], mesh.shape["group"]
    line = devices // 4
    cut = jax.sharding.Mesh(
        mesh.devices.reshape(line, 2, 2, groups), ("z", "x", "core", "group")
    )
    dp = ("z", "x", "core")
    placed = (P("group", dp, None), P("group", dp, None), P("group", None))
    return jax.shard_map(
        functools.partial(shards, line, groups),
        mesh=cut,
        in_specs=placed,
        out_specs=P(None, dp, None),
        check_vma=False,
    )
```

time: 51.8 us -> 47.6 us (0.919)
  Pallas kernels: 16.3 us -> 11.8 us
  starting transfers between devices: 13.7 us -> 14.4 us
  local copies, waits for them, and re-layouts: 0.69 us -> 0.02 us
    pallas_call x3 -> x2, Pallas kernels: 6.43 us -> 0.82 us  [gram(): pl.pallas_call(functools.partial(gram_kernel, scale, outputs), out_shape=...]
    pallas_call x3 -> x2, Pallas kernels: 9.83 us -> 11 us  [the longest x1 9.19 us: root(): pl.pallas_call(root_kernel, out_shape=[out, out], in_specs=[HBM] + [VMEM]...]
    unnamed x2 -> x0, local copies, waits for them, and re-layouts: 0.67 us -> none
    ppermute x9 -> x12, starting transfers between devices: 10.2 us -> 10.8 us  [swap(): lax.ppermute(array, axis, [(i, i ^ mask) for i in range(lax.axis_size(axi...]
    ppermute x9 -> x12, waiting for transfers between devices: 16.6 us -> 17 us  [swap(): lax.ppermute(array, axis, [(i, i ^ mask) for i in range(lax.axis_size(axi...]
  transfers between devices with their start and end apart: 12 -> 15, of which waited for: 9 -> 12; matrix products, arithmetic and copies ran while one was open for 0% -> 0% of each run, Pallas kernels for 9% -> 2%
where the time goes in v4:
time: 47.6 us; the launch traced here: 47.2 us
  waiting for transfers between devices  19.9 us (42%)
  starting transfers between devices  14.4 us (30%)
  Pallas kernels  11.8 us (25%)
  other arithmetic  0.97 us (2%)
    ppermute x12, waiting for transfers between devices, swap(): lax.ppermute(array, axis, [(i, i ^ mask) for i in range(lax.axis_size(axi...  17 us
    ppermute x12, starting transfers between devices, swap(): lax.ppermute(array, axis, [(i, i ^ mask) for i in range(lax.axis_size(axi...  10.8 us
    pallas_call x1, Pallas kernels, root(): pl.pallas_call(root_kernel, out_shape=[out, out], in_specs=[HBM] + [VMEM]...  9.19 us
    ppermute x3, starting transfers between devices, shards(): lax.ppermute(piece, ('x', 'group'), moves)  3.55 us
    ppermute x3, waiting for transfers between devices, shards(): lax.ppermute(piece, ('x', 'group'), moves)  2.94 us
    pallas_call x1, Pallas kernels, load(): pl.pallas_call(functools.partial(load_kernel, scale, pieces), out_shape=[...  1.79 us
  transfers between devices with their start and end apart: 15, of which 12 were waited for; matrix products, arithmetic and copies ran while one was open for 0% of the time, Pallas kernels for 2%

profile of v4, /device:TPU:0, one launch (start us, length us, event | category | flops | bytes accessed | tf_op | source)
XLA Modules:
  0.0 47.2 jit_solution(3654570553578091863)
XLA Ops:
  0.0 1.8 %shard_map.37 = (bf16[512,256]{1,0:T(8,128)(2,1)S(1)}, bf16[2,2,512,256]{3,2,1,0:T(8,128)(2,1)S(1)}, bf16[2,512,512]{2,1,0:T(8,128)(2,1)S(1)}) custom-call(bf16[2,512,512]{2,1,0:T(8,128)(2,1)} %patch_hbm.1, bf16[2,512,512]{2,1,0:T(8,128)(2,1)} %cot_hbm.1), custom_call_target="tpu_custom_call" | custom-call | tf_op jit(solution)/shard_map/pallas_call | solution.py:78
  1.8 0.5 %collective-permute-start = (bf16[512,256]{1,0:T(8,128)(2,1)S(1)}, bf16[512,256]{1,0:T(8,128)(2,1)S(1)}, u32[]{:S(2)}, u32[]{:S(2)}) collective-permute-start(bf16[512,256]{1,0:T(8,128)(2,1)S(1)} %get-tuple-element.15), channel_id=1, source_target_pairs={{0,2},{2,0},{1,3},{3,1},{4,6},{6,4},{5,7},{7,5},{8,10},{10,8},{9,1... | collective-permute-start | bytes 786440 | tf_op jit(solution)/shard_map/ppermute | solution.py:232
  2.3 0.5 %shard_map.38 = (f32[512,256]{1,0:T(8,128)S(1)}, bf16[512,256]{1,0:T(8,128)(2,1)S(1)}) custom-call(bf16[2,2,512,256]{3,2,1,0:T(8,128)(2,1)S(1)} %get-tuple-element.12.patch, bf16[2,512,512]{2,1,0:T(8,128)(2,1)S(1)} %get-tuple-element.13.cot), custom_call_target="tpu_custom_call" | custom-call | flops 268435456 | bytes 2097152 | tf_op jit(solution)/shard_map/pallas_call | solution.py:102
  2.8 0.1 collective-permute-start.1
  2.9 0.5 %collective-permute-done = bf16[512,256]{1,0:T(8,128)(2,1)S(1)} collective-permute-done((bf16[512,256]{1,0:T(8,128)(2,1)S(1)}, bf16[512,256]{1,0:T(8,128)(2,1)S(1)}, u32[]{:S(2)}, u32[]{:S(2)}) %collective-permute-start) | collective-permute-done | bytes 262176 | tf_op jit(solution)/shard_map/ppermute | solution.py:232
  3.5 0.1 add_convert_fusion
  3.5 3.0 %collective-permute-start.7 = (bf16[256,256]{1,0:T(8,128)(2,1)S(1)}, bf16[256,256]{1,0:T(8,128)(2,1)S(1)}, u32[]{:S(2)}, u32[]{:S(2)}) collective-permute-start(bf16[256,256]{1,0:T(8,128)(2,1)S(1)} %get-tuple-element.21), channel_id=1, source_target_pairs={{0,8},{8,0},{16,24},{24,16},{1,9},{9,1},{17,25},{25,17},{2,10},{10... | collective-permute-start | bytes 393224 | tf_op jit(solution)/shard_map/ppermute | solution.py:232
  6.6 1.5 %collective-permute-start.2 = (bf16[256,256]{1,0:T(8,128)(2,1)S(1)}, bf16[256,256]{1,0:T(8,128)(2,1)S(1)}, u32[]{:S(2)}, u32[]{:S(2)}) collective-permute-start(bf16[256,256]{1,0:T(8,128)(2,1)S(1)} %get-tuple-element.22.refs_0_), channel_id=1, source_target_pairs={{0,4},{4,0},{1,5},{5,1},{2,6},{6,2},{3,7},{7,3},{8,12},{12,8},{9,1... | collective-permute-start | bytes 393224 | tf_op jit(solution)/shard_map/ppermute | solution.py:232
  8.0 0.3 shard_map.39
  8.4 0.0 collective-permute-done.1
  8.4 1.9 %collective-permute-done.7 = bf16[256,256]{1,0:T(8,128)(2,1)S(1)} collective-permute-done((bf16[256,256]{1,0:T(8,128)(2,1)S(1)}, bf16[256,256]{1,0:T(8,128)(2,1)S(1)}, u32[]{:S(2)}, u32[]{:S(2)}) %collective-permute-start.7) | collective-permute-done | bytes 131104 | tf_op jit(solution)/shard_map/ppermute | solution.py:232
  10.3 1.5 %collective-permute-done.2 = bf16[256,256]{1,0:T(8,128)(2,1)S(1)} collective-permute-done((bf16[256,256]{1,0:T(8,128)(2,1)S(1)}, bf16[256,256]{1,0:T(8,128)(2,1)S(1)}, u32[]{:S(2)}, u32[]{:S(2)}) %collective-permute-start.2) | collective-permute-done | bytes 131104 | tf_op jit(solution)/shard_map/ppermute | solution.py:232
  11.8 0.1 fusion
  11.9 0.4 collective-permute-start.3
  12.3 1.6 %collective-permute-start.8 = (bf16[128,256]{1,0:T(8,128)(2,1)S(1)}, bf16[128,256]{1,0:T(8,128)(2,1)S(1)}, u32[]{:S(2)}, u32[]{:S(2)}) collective-permute-start(bf16[128,256]{1,0:T(8,128)(2,1)S(1)} %slice.84), channel_id=1, source_target_pairs={{0,4},{4,0},{1,5},{5,1},{2,6},{6,2},{3,7},{7,3},{8,12},{12,8},{9,1... | collective-permute-start | bytes 196616 | tf_op jit(solution)/shard_map/ppermute | solution.py:232
  14.0 2.2 %collective-permute-done.3 = bf16[128,256]{1,0:T(8,128)(2,1)S(1)} collective-permute-done((bf16[128,256]{1,0:T(8,128)(2,1)S(1)}, bf16[128,256]{1,0:T(8,128)(2,1)S(1)}, u32[]{:S(2)}, u32[]{:S(2)}) %collective-permute-start.3) | collective-permute-done | bytes 65568 | tf_op jit(solution)/shard_map/ppermute | solution.py:232
  16.3 3.1 %collective-permute-start.4 = (bf16[128,256]{1,0:T(8,128)(2,1)S(1)}, bf16[128,256]{1,0:T(8,128)(2,1)S(1)}, u32[]{:S(2)}, u32[]{:S(2)}) collective-permute-start(bf16[128,256]{1,0:T(8,128)(2,1)S(1)} %fusion.2), channel_id=1, source_target_pairs={{0,16},{8,24},{16,0},{24,8},{1,17},{9,25},{17,1},{25,9},{2,18},{10... | collective-permute-start | bytes 196616 | tf_op jit(solution)/shard_map/ppermute | solution.py:232
  19.4 0.0 collective-permute-done.8
  19.4 0.1 collective-permute-start.9
  19.5 3.4 %collective-permute-done.4 = bf16[128,256]{1,0:T(8,128)(2,1)S(1)} collective-permute-done((bf16[128,256]{1,0:T(8,128)(2,1)S(1)}, bf16[128,256]{1,0:T(8,128)(2,1)S(1)}, u32[]{:S(2)}, u32[]{:S(2)}) %collective-permute-start.4) | collective-permute-done | bytes 65568 | tf_op jit(solution)/shard_map/ppermute | solution.py:232
  23.0 0.1 collective-permute-start.5
  23.1 1.9 %collective-permute-done.9 = bf16[128,256]{1,0:T(8,128)(2,1)S(1)} collective-permute-done((bf16[128,256]{1,0:T(8,128)(2,1)S(1)}, bf16[128,256]{1,0:T(8,128)(2,1)S(1)}, u32[]{:S(2)}, u32[]{:S(2)}) %collective-permute-start.9) | collective-permute-done | bytes 65568 | tf_op jit(solution)/shard_map/ppermute | solution.py:232
  25.0 0.2 collective-permute-start.10
  25.2 2.1 %collective-permute-done.5.refs_1_ = bf16[128,256]{1,0:T(8,128)(2,1)S(1)} collective-permute-done((bf16[128,256]{1,0:T(8,128)(2,1)S(1)}, bf16[128,256]{1,0:T(8,128)(2,1)S(1)}, u32[]{:S(2)}, u32[]{:S(2)}) %collective-permute-start.5) | collective-permute-done | bytes 65568 | tf_op jit(solution)/shard_map/ppermute | solution.py:232
  27.3 0.1 collective-permute-start.6
  27.4 1.9 %collective-permute-done.10.refs_4_ = bf16[128,256]{1,0:T(8,128)(2,1)S(1)} collective-permute-done((bf16[128,256]{1,0:T(8,128)(2,1)S(1)}, bf16[128,256]{1,0:T(8,128)(2,1)S(1)}, u32[]{:S(2)}, u32[]{:S(2)}) %collective-permute-start.10) | collective-permute-done | bytes 65568 | tf_op jit(solution)/shard_map/ppermute | solution.py:232
  29.4 0.1 collective-permute-start.11
  29.4 0.0 collective-permute-done.6.refs_2_
  29.5 1.3 %collective-permute-done.11.refs_5_ = bf16[256,256]{1,0:T(8,128)(2,1)S(1)} collective-permute-done((bf16[256,256]{1,0:T(8,128)(2,1)S(1)}, bf16[256,256]{1,0:T(8,128)(2,1)S(1)}, u32[]{:S(2)}, u32[]{:S(2)}) %collective-permute-start.11) | collective-permute-done | bytes 131104 | tf_op jit(solution)/shard_map/ppermute | solution.py:232
  30.8 9.2 %shard_map.40 = (bf16[32,512]{1,0:T(8,128)(2,1)S(1)}, bf16[32,512]{1,0:T(8,128)(2,1)S(1)}) custom-call(s32[2,2]{1,0:T(2,128)} %counts_hbm.1, bf16[128,256]{1,0:T(8,128)(2,1)S(1)} %add_convert_fusion.3.refs_0_, bf16[128,256]{1,0:T(8,128)(2,1)S(1)} %collective-permute-done.5.refs_1_, bf16[256,256]{1,0:T(8,128)(2,1)S(1)} %collective-permute-done.6.refs_2_, ...), custom_call_target="tpu_custom_call" | custom-call | tf_op jit(solution)/shard_map/pallas_call | solution.py:208
  40.0 0.1 collective-permute-start.13
  40.1 2.5 %collective-permute-start.14 = (bf16[32,512]{1,0:T(8,128)(2,1)S(1)}, bf16[32,512]{1,0:T(8,128)(2,1)S(1)}, u32[]{:S(2)}, u32[]{:S(2)}) collective-permute-start(bf16[32,512]{1,0:T(8,128)(2,1)S(1)} %get-tuple-element.18), channel_id=1, source_target_pairs={{0,5},{1,4},{4,1},{5,0},{2,7},{3,6},{6,3},{7,2},{8,13},{9,12},{12,... | collective-permute-start | bytes 98312 | tf_op jit(solution)/shard_map/ppermute | solution.py:275
  42.6 1.0 %collective-permute-start.12 = (bf16[32,512]{1,0:T(8,128)(2,1)S(1)}, bf16[32,512]{1,0:T(8,128)(2,1)S(1)}, u32[]{:S(2)}, u32[]{:S(2)}) collective-permute-start(bf16[32,512]{1,0:T(8,128)(2,1)S(1)} %get-tuple-element.18), channel_id=1, source_target_pairs={{0,4},{1,5},{4,0},{5,1},{2,6},{3,7},{6,2},{7,3},{8,12},{9,13},{12,... | collective-permute-start | bytes 98312 | tf_op jit(solution)/shard_map/ppermute | solution.py:275
  43.5 0.8 %collective-permute-done.13 = bf16[32,512]{1,0:T(8,128)(2,1)S(1)} collective-permute-done((bf16[32,512]{1,0:T(8,128)(2,1)S(1)}, bf16[32,512]{1,0:T(8,128)(2,1)S(1)}, u32[]{:S(2)}, u32[]{:S(2)}) %collective-permute-start.13) | collective-permute-done | bytes 32800 | tf_op jit(solution)/shard_map/ppermute | solution.py:275
  44.3 0.6 %collective-permute-done.14 = bf16[32,512]{1,0:T(8,128)(2,1)S(1)} collective-permute-done((bf16[32,512]{1,0:T(8,128)(2,1)S(1)}, bf16[32,512]{1,0:T(8,128)(2,1)S(1)}, u32[]{:S(2)}, u32[]{:S(2)}) %collective-permute-start.14) | collective-permute-done | bytes 32800 | tf_op jit(solution)/shard_map/ppermute | solution.py:275
  44.9 1.5 %collective-permute-done.12 = bf16[32,512]{1,0:T(8,128)(2,1)S(1)} collective-permute-done((bf16[32,512]{1,0:T(8,128)(2,1)S(1)}, bf16[32,512]{1,0:T(8,128)(2,1)S(1)}, u32[]{:S(2)}, u32[]{:S(2)}) %collective-permute-start.12) | collective-permute-done | bytes 32800 | tf_op jit(solution)/shard_map/ppermute | solution.py:275
  46.6 0.7 %reverse_select_fusion = bf16[2,2,32,512]{3,2,1,0:T(8,128)(2,1)} fusion(bf16[2,2,32,512]{3,2,1,0:T(8,128)(2,1)S(1)} %reverse_select_fusion.1, pred[]{:T(512)S(6)} %eq.6), kind=kLoop, calls=%fused_computation.6 | loop fusion | flops 65536 | bytes 262145 | tf_op jit(solution)/shard_map/jit(_where)/select_n | solution.py:283
  (12 shorter events, 0.2 us)
Async XLA Ops:
  1.8 1.7 %collective-permute-start = (bf16[512,256]{1,0:T(8,128)(2,1)S(1)}, bf16[512,256]{1,0:T(8,128)(2,1)S(1)}, u32[]{:S(2)}, u32[]{:S(2)}) collective-permute-start(bf16[512,256]{1,0:T(8,128)(2,1)S(1)} %get-tuple-element.15), channel_id=1, source_target_pairs={{0,2},{2,0},{1,3},{3,1},{4,6},{6,4},{5,7},{7,5},{8,10},{10,8},{9,1... | collective-permute-start | bytes 786440 | tf_op jit(solution)/shard_map/ppermute | solution.py:232
  2.8 5.6 %collective-permute-start.1 = (bf16[512,256]{1,0:T(8,128)(2,1)S(1)}, bf16[512,256]{1,0:T(8,128)(2,1)S(1)}, u32[]{:S(2)}, u32[]{:S(2)}) collective-permute-start(bf16[512,256]{1,0:T(8,128)(2,1)S(1)} %get-tuple-element.16), channel_id=1, source_target_pairs={{0,2},{2,0},{1,3},{3,1},{4,6},{6,4},{5,7},{7,5},{8,10},{10,8},{9,1... | collective-permute-start | bytes 786440 | tf_op jit(solution)/shard_map/ppermute | solution.py:232
  3.5 6.8 %collective-permute-start.7 = (bf16[256,256]{1,0:T(8,128)(2,1)S(1)}, bf16[256,256]{1,0:T(8,128)(2,1)S(1)}, u32[]{:S(2)}, u32[]{:S(2)}) collective-permute-start(bf16[256,256]{1,0:T(8,128)(2,1)S(1)} %get-tuple-element.21), channel_id=1, source_target_pairs={{0,8},{8,0},{16,24},{24,16},{1,9},{9,1},{17,25},{25,17},{2,10},{10... | collective-permute-start | bytes 393224 | tf_op jit(solution)/shard_map/ppermute | solution.py:232
  6.6 5.3 %collective-permute-start.2 = (bf16[256,256]{1,0:T(8,128)(2,1)S(1)}, bf16[256,256]{1,0:T(8,128)(2,1)S(1)}, u32[]{:S(2)}, u32[]{:S(2)}) collective-permute-start(bf16[256,256]{1,0:T(8,128)(2,1)S(1)} %get-tuple-element.22.refs_0_), channel_id=1, source_target_pairs={{0,4},{4,0},{1,5},{5,1},{2,6},{6,2},{3,7},{7,3},{8,12},{12,8},{9,1... | collective-permute-start | bytes 393224 | tf_op jit(solution)/shard_map/ppermute | solution.py:232
  11.9 4.3 %collective-permute-start.3 = (bf16[128,256]{1,0:T(8,128)(2,1)S(1)}, bf16[128,256]{1,0:T(8,128)(2,1)S(1)}, u32[]{:S(2)}, u32[]{:S(2)}) collective-permute-start(bf16[128,256]{1,0:T(8,128)(2,1)S(1)} %slice.85), channel_id=1, source_target_pairs={{0,8},{8,0},{16,24},{24,16},{1,9},{9,1},{17,25},{25,17},{2,10},{10... | collective-permute-start | bytes 196616 | tf_op jit(solution)/shard_map/ppermute | solution.py:232
  12.3 7.1 %collective-permute-start.8 = (bf16[128,256]{1,0:T(8,128)(2,1)S(1)}, bf16[128,256]{1,0:T(8,128)(2,1)S(1)}, u32[]{:S(2)}, u32[]{:S(2)}) collective-permute-start(bf16[128,256]{1,0:T(8,128)(2,1)S(1)} %slice.84), channel_id=1, source_target_pairs={{0,4},{4,0},{1,5},{5,1},{2,6},{6,2},{3,7},{7,3},{8,12},{12,8},{9,1... | collective-permute-start | bytes 196616 | tf_op jit(solution)/shard_map/ppermute | solution.py:232
  16.3 6.7 %collective-permute-start.4 = (bf16[128,256]{1,0:T(8,128)(2,1)S(1)}, bf16[128,256]{1,0:T(8,128)(2,1)S(1)}, u32[]{:S(2)}, u32[]{:S(2)}) collective-permute-start(bf16[128,256]{1,0:T(8,128)(2,1)S(1)} %fusion.2), channel_id=1, source_target_pairs={{0,16},{8,24},{16,0},{24,8},{1,17},{9,25},{17,1},{25,9},{2,18},{10... | collective-permute-start | bytes 196616 | tf_op jit(solution)/shard_map/ppermute | solution.py:232
  19.4 5.6 %collective-permute-start.9 = (bf16[128,256]{1,0:T(8,128)(2,1)S(1)}, bf16[128,256]{1,0:T(8,128)(2,1)S(1)}, u32[]{:S(2)}, u32[]{:S(2)}) collective-permute-start(bf16[128,256]{1,0:T(8,128)(2,1)S(1)} %fusion.3), channel_id=1, source_target_pairs={{0,16},{8,24},{16,0},{24,8},{1,17},{9,25},{17,1},{25,9},{2,18},{10... | collective-permute-start | bytes 196616 | tf_op jit(solution)/shard_map/ppermute | solution.py:232
  23.0 4.3 %collective-permute-start.5 = (bf16[128,256]{1,0:T(8,128)(2,1)S(1)}, bf16[128,256]{1,0:T(8,128)(2,1)S(1)}, u32[]{:S(2)}, u32[]{:S(2)}) collective-permute-start(bf16[128,256]{1,0:T(8,128)(2,1)S(1)} %add_convert_fusion.3.refs_0_), channel_id=1, source_target_pairs={{0,8},{8,0},{16,24},{24,16},{1,9},{9,1},{17,25},{25,17},{2,10},{10... | collective-permute-start | bytes 196616 | tf_op jit(solution)/shard_map/ppermute | solution.py:232
  25.0 4.3 %collective-permute-start.10 = (bf16[128,256]{1,0:T(8,128)(2,1)S(1)}, bf16[128,256]{1,0:T(8,128)(2,1)S(1)}, u32[]{:S(2)}, u32[]{:S(2)}) collective-permute-start(bf16[128,256]{1,0:T(8,128)(2,1)S(1)} %add_convert_fusion.2.refs_3_), channel_id=1, source_target_pairs={{0,8},{8,0},{16,24},{24,16},{1,9},{9,1},{17,25},{25,17},{2,10},{10... | collective-permute-start | bytes 196616 | tf_op jit(solution)/shard_map/ppermute | solution.py:232
  27.3 2.1 %collective-permute-start.6 = (bf16[256,256]{1,0:T(8,128)(2,1)S(1)}, bf16[256,256]{1,0:T(8,128)(2,1)S(1)}, u32[]{:S(2)}, u32[]{:S(2)}) collective-permute-start(bf16[256,256]{1,0:T(8,128)(2,1)S(1)} %pad_maximum_fusion), channel_id=1, source_target_pairs={{0,2},{2,0},{1,3},{3,1},{4,6},{6,4},{5,7},{7,5},{8,10},{10,8},{9,1... | collective-permute-start | bytes 393224 | tf_op jit(solution)/shard_map/ppermute | solution.py:232
  29.4 1.4 %collective-permute-start.11 = (bf16[256,256]{1,0:T(8,128)(2,1)S(1)}, bf16[256,256]{1,0:T(8,128)(2,1)S(1)}, u32[]{:S(2)}, u32[]{:S(2)}) collective-permute-start(bf16[256,256]{1,0:T(8,128)(2,1)S(1)} %pad_maximum_fusion.1), channel_id=1, source_target_pairs={{0,2},{2,0},{1,3},{3,1},{4,6},{6,4},{5,7},{7,5},{8,10},{10,8},{9,1... | collective-permute-start | bytes 393224 | tf_op jit(solution)/shard_map/ppermute | solution.py:232
  40.0 4.3 %collective-permute-start.13 = (bf16[32,512]{1,0:T(8,128)(2,1)S(1)}, bf16[32,512]{1,0:T(8,128)(2,1)S(1)}, u32[]{:S(2)}, u32[]{:S(2)}) collective-permute-start(bf16[32,512]{1,0:T(8,128)(2,1)S(1)} %get-tuple-element.17), channel_id=1, source_target_pairs={{0,1},{1,0},{4,5},{5,4},{2,3},{3,2},{6,7},{7,6},{8,9},{9,8},{12,13... | collective-permute-start | bytes 98312 | tf_op jit(solution)/shard_map/ppermute | solution.py:275
  40.1 4.9 %collective-permute-start.14 = (bf16[32,512]{1,0:T(8,128)(2,1)S(1)}, bf16[32,512]{1,0:T(8,128)(2,1)S(1)}, u32[]{:S(2)}, u32[]{:S(2)}) collective-permute-start(bf16[32,512]{1,0:T(8,128)(2,1)S(1)} %get-tuple-element.18), channel_id=1, source_target_pairs={{0,5},{1,4},{4,1},{5,0},{2,7},{3,6},{6,3},{7,2},{8,13},{9,12},{12,... | collective-permute-start | bytes 98312 | tf_op jit(solution)/shard_map/ppermute | solution.py:275
  42.6 3.9 %collective-permute-start.12 = (bf16[32,512]{1,0:T(8,128)(2,1)S(1)}, bf16[32,512]{1,0:T(8,128)(2,1)S(1)}, u32[]{:S(2)}, u32[]{:S(2)}) collective-permute-start(bf16[32,512]{1,0:T(8,128)(2,1)S(1)} %get-tuple-element.18), channel_id=1, source_target_pairs={{0,4},{1,5},{4,0},{5,1},{2,6},{3,7},{6,2},{7,3},{8,12},{9,13},{12,... | collective-permute-start | bytes 98312 | tf_op jit(solution)/shard_map/ppermute | solution.py:275

commit v5 on v4

v5 whole, which is shorter than its diff:
```python
import functools

import jax
import jax.numpy as jnp
from jax import lax
from jax.experimental import pallas as pl
from jax.experimental.pallas import tpu as pltpu
from jax.sharding import PartitionSpec as P

F32 = jnp.float32
BF16 = jnp.bfloat16
VMEM = pl.BlockSpec(memory_space=pltpu.VMEM)
SMEM = pl.BlockSpec(memory_space=pltpu.SMEM)
HBM = pl.BlockSpec(memory_space=pltpu.HBM)
ROWS_IN_COLS = (((0,), (0,)), ((), ()))
COLS_IN_COLS = (((1,), (1,)), ((), ()))


def params(limit):
    return pltpu.CompilerParams(vmem_limit_bytes=limit << 20)


def piece_place(kind, stage, index):
    early = 1 - stage
    block = jnp.where(kind == 0, early, index)
    rows = jnp.where(kind == 0, index, early)
    return block, rows


def write_pieces(patch, cot, scale, kind, columns, stage, out):
    half = patch.shape[3]
    for index in range(2):
        block, rows = piece_place(kind, stage, index)
        terms = lax.dot_general(
            patch[block, rows], cot[block, columns], ROWS_IN_COLS, preferred_element_type=F32
        )
        out[index * half : (index + 1) * half, :] = (terms * scale).astype(out.dtype)


def load_kernel(scale, patch_hbm, cot_hbm, out, patch, cot, sems):
    half = patch.shape[3]
    column, core, parity = lax.axis_index("x"), lax.axis_index("core"), lax.axis_index("z") % 2
    copies = []

    def fetch(source, target):
        copies.append(pltpu.make_async_copy(source, target, sems.at[len(copies)]))
        copies[-1].start()

    def part(array, block, number):
        first = pl.multiple_of(number * half, half)
        return array.at[column ^ block, :, pl.ds(first, half)]

    def fetch_patch(stage):
        for index in range(2):
            block, rows = piece_place(1 - core, stage, index)
            fetch(part(patch_hbm, block, parity ^ rows), patch.at[block, rows])

    def fetch_cot(columns):
        for block in (1, 0):
            fetch(part(cot_hbm, block, core ^ columns), cot.at[block, columns])

    fetch_patch(0)
    fetch_cot(1)
    needed = len(copies)
    fetch_patch(1)
    fetch_cot(0)
    for copy in copies[:needed]:
        copy.wait()
    write_pieces(patch, cot, scale, 1 - core, 1, 0, out)
    for copy in copies[needed:]:
        copy.wait()


def load(patches, cotangents, scale):
    blocks, pix, width = patches.shape
    half = width // 2
    return pl.pallas_call(
        functools.partial(load_kernel, scale),
        out_shape=[
            jax.ShapeDtypeStruct((width, half), BF16),
            jax.ShapeDtypeStruct((blocks, 2, pix, half), BF16),
            jax.ShapeDtypeStruct((blocks, 2, pix, half), BF16),
        ],
        in_specs=[HBM, HBM],
        out_specs=[VMEM] * 3,
        scratch_shapes=[pltpu.SemaphoreType.DMA((8,))],
        compiler_params=params(16),
    )(
        pltpu.with_memory_space_constraint(patches, pltpu.HBM),
        pltpu.with_memory_space_constraint(cotangents, pltpu.HBM),
    )


def gram_kernel(scale, outputs, patch, cot, *refs):
    core = lax.axis_index("core")
    for (_, columns, stage), out in zip(outputs, refs[-len(outputs) :]):
        write_pieces(patch, cot, scale, core ^ columns, columns, stage, out)


def gram(patch, cot, after, scale, *outputs):
    pix, half = patch.shape[2:]
    return pl.pallas_call(
        functools.partial(gram_kernel, scale, outputs),
        out_shape=[jax.ShapeDtypeStruct((2 * half, half), dtype) for dtype, _, _ in outputs],
        in_specs=[VMEM, VMEM] + [pl.BlockSpec(memory_space=pl.ANY)] * len(after),
        out_specs=[VMEM] * len(outputs),
        compiler_params=params(16),
        cost_estimate=pl.CostEstimate(
            flops=4 * len(outputs) * pix * half * half,
            bytes_accessed=2 * (patch.size + cot.size),
            transcendentals=0,
        ),
    )(patch, cot, *after)


def add(*values):
    total = values[0]
    for value in values[1:]:
        total = total + value.astype(F32)
    return total


def root_kernel(counts_hbm, own, other, far, out, grad, *refs):
    q_left, q_right, m_left, m_right, x_left, x_right, counts, sem = refs
    counts_copy = pltpu.make_async_copy(counts_hbm, counts, sem)
    counts_copy.start()
    width = grad.shape[0]
    half = width // 2
    rows = out.shape[0] // 2
    place, column, core = (lax.axis_index(name) for name in ("z", "x", "core"))
    for index, ref in enumerate((own, other)):
        where = slice(half * index, half * (index + 1))
        grad[where, :half] = jnp.where(core == 0, ref[...], far[where, :])
        grad[where, half:] = jnp.where(core == 0, far[where, :], ref[...])
    diagonal = lax.broadcasted_iota(jnp.int32, (width, width), 0) == lax.broadcasted_iota(
        jnp.int32, (width, width), 1
    )

    def dot(a, b):
        return jnp.dot(a, b, preferred_element_type=F32)

    def factor(moment):
        return (jnp.where(diagonal, 1.25, 0.0) - 0.25 * moment).astype(BF16)

    def begin(dims):
        stats = lax.dot_general(grad[...], grad[...], dims, preferred_element_type=F32)
        stats = stats + jnp.where(diagonal, 0.1, 0.0)
        scale = 2.5 / jnp.sqrt(jnp.sum(stats * stats, keepdims=True))
        first = jnp.sqrt(jnp.sqrt(scale)).astype(BF16).astype(F32)
        return scale * stats, first

    def spot(flip):
        row = (4 * place + 2 * (column ^ flip) + core) * rows
        return (row // half ^ place % 2) * half + row % half

    line = lax.broadcasted_iota(jnp.int32, (2 * rows, width), 0)
    wanted = jnp.where(line < rows, spot(1) + line, spot(0) + line - rows)
    pick = lax.broadcasted_iota(jnp.int32, (2 * rows, width), 1) == wanted
    pick = jnp.where(pick, 1.0, 0.0).astype(BF16)
    moment, first = begin(COLS_IN_COLS)
    m_left[...] = moment.astype(BF16)
    factor_value = factor(moment)
    q_left[...] = factor_value
    x_left[...] = (first * dot(pick, factor_value)).astype(BF16)
    moment, first = begin(ROWS_IN_COLS)
    m_right[...] = moment.astype(BF16)
    factor_value = factor(moment)
    q_right[...] = factor_value
    x_right[...] = (first * factor_value.astype(F32)).astype(BF16)

    counts_copy.wait()
    count_left, count_right = counts[column, 0], counts[column, 1]

    def sweep(index, carry):
        second_left = dot(q_left[...], q_left[...]).astype(BF16)
        second_right = dot(q_right[...], q_right[...]).astype(BF16)
        fourth_left = dot(second_left, second_left).astype(BF16)
        fourth_right = dot(second_right, second_right).astype(BF16)
        moment_left = dot(fourth_left, m_left[...])
        moment_right = dot(fourth_right, m_right[...])
        m_left[...] = moment_left.astype(BF16)
        m_right[...] = moment_right.astype(BF16)
        factor_left = factor(moment_left)
        factor_right = factor(moment_right)
        q_left[...] = factor_left
        q_right[...] = factor_right
        next_left = dot(x_left[...], factor_left).astype(BF16)
        next_right = dot(x_right[...], factor_right).astype(BF16)
        x_left[...] = jnp.where(index < count_left, next_left, x_left[...])
        x_right[...] = jnp.where(index < count_right, next_right, x_right[...])
        return carry

    lax.fori_loop(1, jnp.maximum(count_left, count_right), sweep, 0)
    partial_value = dot(x_left[...], grad[...]).astype(BF16)
    out[...] = dot(partial_value, x_right[...]).astype(BF16)


def root(counts, own, other, far, rows):
    width = far.shape[0]
    square = pltpu.VMEM((width, width), BF16)
    return pl.pallas_call(
        root_kernel,
        out_shape=jax.ShapeDtypeStruct((2 * rows, width), BF16),
        in_specs=[HBM] + [VMEM] * 3,
        out_specs=VMEM,
        scratch_shapes=[square] * 5
        + [
            pltpu.VMEM((2 * rows, width), BF16),
            square,
            pltpu.SMEM(counts.shape, jnp.int32),
            pltpu.SemaphoreType.DMA(()),
        ],
        compiler_params=params(32),
    )(pltpu.with_memory_space_constraint(counts, pltpu.HBM), own, other, far)


def spread_rows(groups, both):
    rows = both.shape[0] // 2
    send, keep = both[:rows], both[rows:]
    core = lax.axis_index("core")
    if groups == 2:
        moves = []
        for kinds in ((0, 1), (1, 0)):
            kind_moves = []
            for c in range(2):
                for k in range(2):
                    for g in range(2):
                        to = (c ^ 1, k, g) if kinds[k] == 0 else (c, k, g ^ 1)
                        kind_moves.append((4 * c + 2 * k + g, 4 * to[0] + 2 * to[1] + to[2]))
            moves.append(kind_moves)
        axes = ("x", "core", "group")
        first = lax.ppermute(both, axes, moves[0])
        passed = jnp.concatenate([jnp.where(core == 0, keep, send), first[:rows]], 0)
        second = lax.ppermute(passed, axes, moves[1])
        beside = jnp.where(core == 0, first[:rows], second[:rows])
        across = jnp.where(core == 0, second[:rows], first[rows:])
        return jnp.stack([jnp.stack([keep, beside]), jnp.stack([across, second[rows:]])])
    found = []
    for turn in range(groups):
        pair = []
        for flip in range(2):
            moves = [
                (c * groups + g, (c ^ flip) * groups + (g ^ turn))
                for c in range(2)
                for g in range(groups)
            ]
            piece = send if flip else keep
            pair.append(lax.ppermute(piece, ("x", "group"), moves) if turn or flip else piece)
        found.append(jnp.stack(pair))
    return jnp.stack(found)


def shards(line, groups, patches, cotangents, newton_counts):
    blocks, pix, width = patches.shape
    half = width // 2
    rows = half // (2 * line)
    scale = 1.0 / float(pix * 4 * line * width) ** 0.5
    column, group = lax.axis_index("x"), lax.axis_index("group")

    def swap(array, axis, mask=1):
        return lax.ppermute(array, axis, [(i, i ^ mask) for i in range(lax.axis_size(axis))])

    def cross(array, over_x):
        moves = []
        for z in range(line):
            for x in range(2):
                for core in range(2):
                    to = (z, x ^ 1) if core == over_x else (z ^ 1, x)
                    moves.append((4 * z + 2 * x + core, 4 * to[0] + 2 * to[1] + core))
        return lax.ppermute(array, ("z", "x", "core"), moves)

    given, patch, cot = load(patches, cotangents, scale)
    came = swap(given, "core")
    kept, given_on = gram(patch, cot, (), scale, (F32, 0, 0), (BF16, 1, 1))
    came_on = swap(given_on, "core")
    leaving = add(kept, came).astype(BF16)
    crossed = cross(leaving, 0)
    (kept_on,) = gram(patch, cot, (leaving,), scale, (F32, 0, 1))
    own = add(kept_on, came_on, crossed)
    own = add(own[:half], cross(own[half:].astype(BF16), 1))
    mask = 2
    while mask < line:
        own = add(own, swap(own.astype(BF16), "z", mask))
        mask *= 2
    own = own.astype(BF16)
    other = swap(own, "z")
    far = swap(jnp.concatenate([own, other], 0), "core")
    both = root(newton_counts, own, other, far, rows)

    found = spread_rows(groups, both)
    found = jnp.where(column == 0, found, found[:, ::-1])
    bit = 1
    while bit < groups:
        shape = (groups // (2 * bit), 2, bit) + found.shape[1:]
        flipped = found.reshape(shape)[:, ::-1].reshape(found.shape)
        found = jnp.where(group & bit == 0, found, flipped)
        bit *= 2
    return found.reshape(blocks * groups, rows, width)


def solution(mesh):
    devices, groups = mesh.shape["dp"], mesh.shape["group"]
    line = devices // 4
    cut = jax.sharding.Mesh(
        mesh.devices.reshape(line, 2, 2, groups), ("z", "x", "core", "group")
    )
    dp = ("z", "x", "core")
    placed = (P("group", dp, None), P("group", dp, None), P("group", None))
    return jax.shard_map(
        functools.partial(shards, line, groups),
        mesh=cut,
        in_specs=placed,
        out_specs=P(None, dp, None),
        check_vma=False,
    )
```

time: 47.6 us -> 49.1 us (1.032)
  waiting for transfers between devices: 19.9 us -> 24.6 us
  starting transfers between devices: 14.4 us -> 11.6 us
    ppermute x3 -> x4, waiting for transfers between devices: 2.94 us -> 13.7 us  [the longest x2 6.94 us: cross(): return lax.ppermute(array, ('z', 'x', 'core'), moves)]
    ppermute x12 -> x5, starting transfers between devices: 10.8 us -> 4.62 us  [swap(): lax.ppermute(array, axis, [(i, i ^ mask) for i in range(lax.axis_size(axi...]
    ppermute x12 -> x5, waiting for transfers between devices: 17 us -> 10.9 us  [swap(): lax.ppermute(array, axis, [(i, i ^ mask) for i in range(lax.axis_size(axi...]
    ppermute x3 -> x4, starting transfers between devices: 3.55 us -> 6.95 us  [the longest x2 5.1 us: cross(): return lax.ppermute(array, ('z', 'x', 'core'), moves)]
  transfers between devices with their start and end apart: 15 -> 9, of which waited for: 12 -> 8; matrix products, arithmetic and copies ran while one was open for 0% -> 0% of each run, Pallas kernels for 2% -> 2%
where the time goes in v5:
time: 49.1 us; the launch traced here: 49 us
  waiting for transfers between devices  24.6 us (50%)
  Pallas kernels  11.6 us (24%)
  starting transfers between devices  11.6 us (24%)
  other arithmetic  0.99 us (2%)
    ppermute x5, waiting for transfers between devices, swap(): lax.ppermute(array, axis, [(i, i ^ mask) for i in range(lax.axis_size(axi...  10.9 us
    pallas_call x1, Pallas kernels, root(): pl.pallas_call(root_kernel, out_shape=jax.ShapeDtypeStruct((2 * rows, wid...  9.21 us
    ppermute x2, waiting for transfers between devices, cross(): return lax.ppermute(array, ('z', 'x', 'core'), moves)  6.94 us
    ppermute x2, starting transfers between devices, cross(): return lax.ppermute(array, ('z', 'x', 'core'), moves)  5.1 us
    ppermute x5, starting transfers between devices, swap(): lax.ppermute(array, axis, [(i, i ^ mask) for i in range(lax.axis_size(axi...  4.62 us
    ppermute x1, waiting for transfers between devices, spread_rows(): first = lax.ppermute(both, axes, moves[0])  4.24 us
    ppermute x1, waiting for transfers between devices, spread_rows(): second = lax.ppermute(passed, axes, moves[1])  2.55 us
    ppermute x1, starting transfers between devices, spread_rows(): second = lax.ppermute(passed, axes, moves[1])  1.78 us
  transfers between devices with their start and end apart: 9, of which 8 were waited for; matrix products, arithmetic and copies ran while one was open for 0% of the time, Pallas kernels for 2%

profile of v5, /device:TPU:0, one launch (start us, length us, event | category | flops | bytes accessed | tf_op | source)
XLA Modules:
  0.0 49.0 jit_solution(14090829006304178395)
XLA Ops:
  0.0 1.6 %shard_map.37 = (bf16[512,256]{1,0:T(8,128)(2,1)S(1)}, bf16[2,2,512,256]{3,2,1,0:T(8,128)(2,1)S(1)}, bf16[2,2,512,256]{3,2,1,0:T(8,128)(2,1)S(1)}) custom-call(bf16[2,512,512]{2,1,0:T(8,128)(2,1)} %patch_hbm.1, bf16[2,512,512]{2,1,0:T(8,128)(2,1)} %cot_hbm.1), custom_call_target="tpu_custom_call" | custom-call | tf_op jit(solution)/shard_map/pallas_call | solution.py:77
  1.6 0.5 %collective-permute-start = (bf16[512,256]{1,0:T(8,128)(2,1)S(1)}, bf16[512,256]{1,0:T(8,128)(2,1)S(1)}, u32[]{:S(2)}, u32[]{:S(2)}) collective-permute-start(bf16[512,256]{1,0:T(8,128)(2,1)S(1)} %get-tuple-element.13), channel_id=1, source_target_pairs={{0,2},{2,0},{1,3},{3,1},{4,6},{6,4},{5,7},{7,5},{8,10},{10,8},{9,1... | collective-permute-start | bytes 786440 | tf_op jit(solution)/shard_map/ppermute | solution.py:261
  2.1 0.5 shard_map.38
  2.6 0.1 collective-permute-start.1
  2.8 0.5 %collective-permute-done = bf16[512,256]{1,0:T(8,128)(2,1)S(1)} collective-permute-done((bf16[512,256]{1,0:T(8,128)(2,1)S(1)}, bf16[512,256]{1,0:T(8,128)(2,1)S(1)}, u32[]{:S(2)}, u32[]{:S(2)}) %collective-permute-start) | collective-permute-done | bytes 262176 | tf_op jit(solution)/shard_map/ppermute | solution.py:261
  3.3 0.1 add_convert_fusion.refs_0_
  3.4 2.9 %collective-permute-start.2 = (bf16[512,256]{1,0:T(8,128)(2,1)S(1)}, bf16[512,256]{1,0:T(8,128)(2,1)S(1)}, u32[]{:S(2)}, u32[]{:S(2)}) collective-permute-start(bf16[512,256]{1,0:T(8,128)(2,1)S(1)} %add_convert_fusion.refs_0_), channel_id=1, source_target_pairs={{0,4},{2,10},{4,0},{6,14},{8,12},{10,2},{12,8},{14,6},{16,20},{18,... | collective-permute-start | bytes 786440 | tf_op jit(solution)/shard_map/ppermute | solution.py:270
  6.3 0.3 shard_map.39
  6.6 0.0 collective-permute-done.1
  6.6 4.0 %collective-permute-done.2 = bf16[512,256]{1,0:T(8,128)(2,1)S(1)} collective-permute-done((bf16[512,256]{1,0:T(8,128)(2,1)S(1)}, bf16[512,256]{1,0:T(8,128)(2,1)S(1)}, u32[]{:S(2)}, u32[]{:S(2)}) %collective-permute-start.2) | collective-permute-done | bytes 262176 | tf_op jit(solution)/shard_map/ppermute | solution.py:270
  10.6 0.1 convert_add_fusion
  10.7 2.2 %collective-permute-start.3 = (bf16[256,256]{1,0:T(8,128)(2,1)S(1)}, bf16[256,256]{1,0:T(8,128)(2,1)S(1)}, u32[]{:S(2)}, u32[]{:S(2)}) collective-permute-start(bf16[256,256]{1,0:T(8,128)(2,1)S(1)} %slice.59), channel_id=1, source_target_pairs={{0,8},{2,6},{4,12},{6,2},{8,0},{10,14},{12,4},{14,10},{16,24},{18,... | collective-permute-start | bytes 393224 | tf_op jit(solution)/shard_map/ppermute | solution.py:270
  12.9 2.9 %collective-permute-done.3 = bf16[256,256]{1,0:T(8,128)(2,1)S(1)} collective-permute-done((bf16[256,256]{1,0:T(8,128)(2,1)S(1)}, bf16[256,256]{1,0:T(8,128)(2,1)S(1)}, u32[]{:S(2)}, u32[]{:S(2)}) %collective-permute-start.3) | collective-permute-done | bytes 131104 | tf_op jit(solution)/shard_map/ppermute | solution.py:270
  15.9 3.1 %collective-permute-start.4 = (bf16[256,256]{1,0:T(8,128)(2,1)S(1)}, bf16[256,256]{1,0:T(8,128)(2,1)S(1)}, u32[]{:S(2)}, u32[]{:S(2)}) collective-permute-start(bf16[256,256]{1,0:T(8,128)(2,1)S(1)} %fusion), channel_id=1, source_target_pairs={{0,16},{8,24},{16,0},{24,8},{1,17},{9,25},{17,1},{25,9},{2,18},{10... | collective-permute-start | bytes 393224 | tf_op jit(solution)/shard_map/ppermute | solution.py:261
  19.0 4.6 %collective-permute-done.4 = bf16[256,256]{1,0:T(8,128)(2,1)S(1)} collective-permute-done((bf16[256,256]{1,0:T(8,128)(2,1)S(1)}, bf16[256,256]{1,0:T(8,128)(2,1)S(1)}, u32[]{:S(2)}, u32[]{:S(2)}) %collective-permute-start.4) | collective-permute-done | bytes 131104 | tf_op jit(solution)/shard_map/ppermute | solution.py:261
  23.6 0.8 %collective-permute-start.5 = (bf16[256,256]{1,0:T(8,128)(2,1)S(1)}, bf16[256,256]{1,0:T(8,128)(2,1)S(1)}, u32[]{:S(2)}, u32[]{:S(2)}) collective-permute-start(bf16[256,256]{1,0:T(8,128)(2,1)S(1)} %add_convert_fusion.1.own), channel_id=1, source_target_pairs={{0,8},{8,0},{16,24},{24,16},{1,9},{9,1},{17,25},{25,17},{2,10},{10... | collective-permute-start | bytes 393224 | tf_op jit(solution)/shard_map/ppermute | solution.py:261
  24.5 4.2 %collective-permute-done.5.other = bf16[256,256]{1,0:T(8,128)(2,1)S(1)} collective-permute-done((bf16[256,256]{1,0:T(8,128)(2,1)S(1)}, bf16[256,256]{1,0:T(8,128)(2,1)S(1)}, u32[]{:S(2)}, u32[]{:S(2)}) %collective-permute-start.5) | collective-permute-done | bytes 131104 | tf_op jit(solution)/shard_map/ppermute | solution.py:261
  28.7 0.1 collective-permute-start.6
  28.8 1.5 %collective-permute-done.6.far = bf16[512,256]{1,0:T(8,128)(2,1)S(1)} collective-permute-done((bf16[512,256]{1,0:T(8,128)(2,1)S(1)}, bf16[512,256]{1,0:T(8,128)(2,1)S(1)}, u32[]{:S(2)}, u32[]{:S(2)}) %collective-permute-start.6) | collective-permute-done | bytes 262176 | tf_op jit(solution)/shard_map/ppermute | solution.py:261
  30.3 9.2 %shard_map.40 = bf16[64,512]{1,0:T(8,128)(2,1)S(1)} custom-call(s32[2,2]{1,0:T(2,128)} %counts_hbm.1, bf16[256,256]{1,0:T(8,128)(2,1)S(1)} %add_convert_fusion.1.own, bf16[256,256]{1,0:T(8,128)(2,1)S(1)} %collective-permute-done.5.other, bf16[512,256]{1,0:T(8,128)(2,1)S(1)} %collective-permute-done.6.far), custom_call_target="tpu_custom_call" | custom-call | tf_op jit(solution)/shard_map/pallas_call | solution.py:201
  39.5 0.1 collective-permute-start.7
  39.6 4.2 %collective-permute-done.7 = bf16[64,512]{1,0:T(8,128)(2,1)S(1)} collective-permute-done((bf16[64,512]{1,0:T(8,128)(2,1)S(1)}, bf16[64,512]{1,0:T(8,128)(2,1)S(1)}, u32[]{:S(2)}, u32[]{:S(2)}) %collective-permute-start.7) | collective-permute-done | bytes 65568 | tf_op jit(solution)/shard_map/ppermute | solution.py:232
  43.9 1.8 %collective-permute-start.8 = (bf16[64,512]{1,0:T(8,128)(2,1)S(1)}, bf16[64,512]{1,0:T(8,128)(2,1)S(1)}, u32[]{:S(2)}, u32[]{:S(2)}) collective-permute-start(bf16[64,512]{1,0:T(8,128)(2,1)S(1)} %pad_maximum_fusion.2), channel_id=1, source_target_pairs={{0,1},{1,0},{2,6},{3,7},{4,5},{5,4},{6,2},{7,3},{8,9},{9,8},{10,14... | collective-permute-start | bytes 196616 | tf_op jit(solution)/shard_map/ppermute | solution.py:234
  45.6 2.5 %collective-permute-done.8 = bf16[64,512]{1,0:T(8,128)(2,1)S(1)} collective-permute-done((bf16[64,512]{1,0:T(8,128)(2,1)S(1)}, bf16[64,512]{1,0:T(8,128)(2,1)S(1)}, u32[]{:S(2)}, u32[]{:S(2)}) %collective-permute-start.8) | collective-permute-done | bytes 65568 | tf_op jit(solution)/shard_map/ppermute | solution.py:234
  48.3 0.7 %reverse_select_fusion = bf16[2,2,32,512]{3,2,1,0:T(8,128)(2,1)} fusion(bf16[2,2,32,512]{3,2,1,0:T(8,128)(2,1)S(1)} %reverse_select_fusion.1, pred[]{:T(512)S(6)} %eq.11), kind=kLoop, calls=%fused_computation.6 | loop fusion | flops 65536 | bytes 262145 | tf_op jit(solution)/shard_map/jit(_where)/select_n | solution.py:296
  (11 shorter events, 0.2 us)
Async XLA Ops:
  1.6 1.7 %collective-permute-start = (bf16[512,256]{1,0:T(8,128)(2,1)S(1)}, bf16[512,256]{1,0:T(8,128)(2,1)S(1)}, u32[]{:S(2)}, u32[]{:S(2)}) collective-permute-start(bf16[512,256]{1,0:T(8,128)(2,1)S(1)} %get-tuple-element.13), channel_id=1, source_target_pairs={{0,2},{2,0},{1,3},{3,1},{4,6},{6,4},{5,7},{7,5},{8,10},{10,8},{9,1... | collective-permute-start | bytes 786440 | tf_op jit(solution)/shard_map/ppermute | solution.py:261
  2.6 4.0 %collective-permute-start.1 = (bf16[512,256]{1,0:T(8,128)(2,1)S(1)}, bf16[512,256]{1,0:T(8,128)(2,1)S(1)}, u32[]{:S(2)}, u32[]{:S(2)}) collective-permute-start(bf16[512,256]{1,0:T(8,128)(2,1)S(1)} %get-tuple-element.14), channel_id=1, source_target_pairs={{0,2},{2,0},{1,3},{3,1},{4,6},{6,4},{5,7},{7,5},{8,10},{10,8},{9,1... | collective-permute-start | bytes 786440 | tf_op jit(solution)/shard_map/ppermute | solution.py:261
  3.4 7.3 %collective-permute-start.2 = (bf16[512,256]{1,0:T(8,128)(2,1)S(1)}, bf16[512,256]{1,0:T(8,128)(2,1)S(1)}, u32[]{:S(2)}, u32[]{:S(2)}) collective-permute-start(bf16[512,256]{1,0:T(8,128)(2,1)S(1)} %add_convert_fusion.refs_0_), channel_id=1, source_target_pairs={{0,4},{2,10},{4,0},{6,14},{8,12},{10,2},{12,8},{14,6},{16,20},{18,... | collective-permute-start | bytes 786440 | tf_op jit(solution)/shard_map/ppermute | solution.py:270
  10.7 5.1 %collective-permute-start.3 = (bf16[256,256]{1,0:T(8,128)(2,1)S(1)}, bf16[256,256]{1,0:T(8,128)(2,1)S(1)}, u32[]{:S(2)}, u32[]{:S(2)}) collective-permute-start(bf16[256,256]{1,0:T(8,128)(2,1)S(1)} %slice.59), channel_id=1, source_target_pairs={{0,8},{2,6},{4,12},{6,2},{8,0},{10,14},{12,4},{14,10},{16,24},{18,... | collective-permute-start | bytes 393224 | tf_op jit(solution)/shard_map/ppermute | solution.py:270
  15.9 7.7 %collective-permute-start.4 = (bf16[256,256]{1,0:T(8,128)(2,1)S(1)}, bf16[256,256]{1,0:T(8,128)(2,1)S(1)}, u32[]{:S(2)}, u32[]{:S(2)}) collective-permute-start(bf16[256,256]{1,0:T(8,128)(2,1)S(1)} %fusion), channel_id=1, source_target_pairs={{0,16},{8,24},{16,0},{24,8},{1,17},{9,25},{17,1},{25,9},{2,18},{10... | collective-permute-start | bytes 393224 | tf_op jit(solution)/shard_map/ppermute | solution.py:261
  23.6 5.0 %collective-permute-start.5 = (bf16[256,256]{1,0:T(8,128)(2,1)S(1)}, bf16[256,256]{1,0:T(8,128)(2,1)S(1)}, u32[]{:S(2)}, u32[]{:S(2)}) collective-permute-start(bf16[256,256]{1,0:T(8,128)(2,1)S(1)} %add_convert_fusion.1.own), channel_id=1, source_target_pairs={{0,8},{8,0},{16,24},{24,16},{1,9},{9,1},{17,25},{25,17},{2,10},{10... | collective-permute-start | bytes 393224 | tf_op jit(solution)/shard_map/ppermute | solution.py:261
  28.7 1.6 %collective-permute-start.6 = (bf16[512,256]{1,0:T(8,128)(2,1)S(1)}, bf16[512,256]{1,0:T(8,128)(2,1)S(1)}, u32[]{:S(2)}, u32[]{:S(2)}) collective-permute-start(bf16[512,256]{1,0:T(8,128)(2,1)S(1)} %pad_maximum_fusion), channel_id=1, source_target_pairs={{0,2},{2,0},{1,3},{3,1},{4,6},{6,4},{5,7},{7,5},{8,10},{10,8},{9,1... | collective-permute-start | bytes 786440 | tf_op jit(solution)/shard_map/ppermute | solution.py:261
  39.5 4.3 %collective-permute-start.7 = (bf16[64,512]{1,0:T(8,128)(2,1)S(1)}, bf16[64,512]{1,0:T(8,128)(2,1)S(1)}, u32[]{:S(2)}, u32[]{:S(2)}) collective-permute-start(bf16[64,512]{1,0:T(8,128)(2,1)S(1)} %shard_map.40), channel_id=1, source_target_pairs={{0,4},{1,5},{2,3},{3,2},{4,0},{5,1},{6,7},{7,6},{8,12},{9,13},{10,... | collective-permute-start | bytes 196616 | tf_op jit(solution)/shard_map/ppermute | solution.py:232
  43.9 4.3 %collective-permute-start.8 = (bf16[64,512]{1,0:T(8,128)(2,1)S(1)}, bf16[64,512]{1,0:T(8,128)(2,1)S(1)}, u32[]{:S(2)}, u32[]{:S(2)}) collective-permute-start(bf16[64,512]{1,0:T(8,128)(2,1)S(1)} %pad_maximum_fusion.2), channel_id=1, source_target_pairs={{0,1},{1,0},{2,6},{3,7},{4,5},{5,4},{6,2},{7,3},{8,9},{9,8},{10,14... | collective-permute-start | bytes 196616 | tf_op jit(solution)/shard_map/ppermute | solution.py:234

commit v6 on v4

--- a/solution.py
+++ b/solution.py
@@ -120,9 +120,9 @@
     return total
 
 
-def root_kernel(counts_hbm, *refs):
+def root_kernel(most, counts_hbm, *refs):
     pieces = refs[:6]
-    keep_ref, send_ref, grad, q_left, q_right, m_left, m_right, x_left, x_right, counts, sem = refs[6:]
+    keep_ref, send_ref, grad, left, right, m_left, m_right, counts, sem = refs[6:]
     counts_copy = pltpu.make_async_copy(counts_hbm, counts, sem)
     counts_copy.start()
     width = grad.shape[0]
@@ -164,60 +164,67 @@
     moment, first = begin(COLS_IN_COLS)
     m_left[...] = moment.astype(BF16)
     factor_value = factor(moment)
-    q_left[...] = factor_value
-    x_left[...] = (first * dot(pick, factor_value)).astype(BF16)
+    left[2 * rows :, :] = factor_value
+    left[: 2 * rows, :] = (first * dot(pick, factor_value)).astype(BF16)
     moment, first = begin(ROWS_IN_COLS)
     m_right[...] = moment.astype(BF16)
     factor_value = factor(moment)
-    q_right[...] = factor_value
-    x_right[...] = (first * factor_value.astype(F32)).astype(BF16)
+    right[width:, :] = factor_value
+    right[:width, :] = (first * factor_value.astype(F32)).astype(BF16)
 
     counts_copy.wait()
-    count_left, count_right = counts[column, 0], counts[column, 1]
-
-    def sweep(index, carry):
-        second_left = dot(q_left[...], q_left[...]).astype(BF16)
-        second_right = dot(q_right[...], q_right[...]).astype(BF16)
-        fourth_left = dot(second_left, second_left).astype(BF16)
-        fourth_right = dot(second_right, second_right).astype(BF16)
-        moment_left = dot(fourth_left, m_left[...])
-        moment_right = dot(fourth_right, m_right[...])
-        m_left[...] = moment_left.astype(BF16)
-        m_right[...] = moment_right.astype(BF16)
-        factor_left = factor(moment_left)
-        factor_right = factor(moment_right)
-        q_left[...] = factor_left
-        q_right[...] = factor_right
-        next_left = dot(x_left[...], factor_left).astype(BF16)
-        next_right = dot(x_right[...], factor_right).astype(BF16)
-        x_left[...] = jnp.where(index < count_left, next_left, x_left[...])
-        x_right[...] = jnp.where(index < count_right, next_right, x_right[...])
-        return carry
-
-    lax.fori_loop(1, jnp.maximum(count_left, count_right), sweep, 0)
-    partial_value = dot(x_left[...], grad[...]).astype(BF16)
-    update = dot(partial_value, x_right[...])
+    sides = (
+        (left, m_left, 2 * rows, counts[column, 0]),
+        (right, m_right, width, counts[column, 1]),
+    )
+    for index in range(1, most):
+        seconds = []
+        for stacked, _, size, count in sides:
+            if index == 1:
+                factor_value = stacked[size:, :]
+                seconds.append(dot(factor_value, factor_value).astype(BF16))
+            else:
+                product = dot(stacked[...], stacked[size:, :]).astype(BF16)
+                if index > 2:
+                    stacked[:size, :] = jnp.where(index <= count, product[:size], stacked[:size, :])
+                else:
+                    stacked[:size, :] = product[:size]
+                seconds.append(product[size:])
+        fourths = [dot(second, second).astype(BF16) for second in seconds]
+        for (stacked, moment_ref, size, _), fourth in zip(sides, fourths):
+            moment = dot(fourth, moment_ref[...])
+            if index < most - 1:
+                moment_ref[...] = moment.astype(BF16)
+            stacked[size:, :] = factor(moment)
+    finals = []
+    for stacked, _, size, count in sides:
+        product = dot(stacked[:size, :], stacked[size:, :]).astype(BF16)
+        finals.append(jnp.where(most <= count, product, stacked[:size, :]))
+    partial_value = dot(finals[0], grad[...]).astype(BF16)
+    update = dot(partial_value, finals[1])
     keep_ref[...] = update[:rows, :].astype(BF16)
     send_ref[...] = update[rows:, :].astype(BF16)
 
 
-def root(counts, pieces, rows):
+def root(counts, pieces, rows, most=4):
     width = 4 * pieces[0].shape[0]
     square = pltpu.VMEM((width, width), BF16)
     out = jax.ShapeDtypeStruct((rows, width), BF16)
     return pl.pallas_call(
-        root_kernel,
+        functools.partial(root_kernel, most),
         out_shape=[out, out],
         in_specs=[HBM] + [VMEM] * 6,
         out_specs=[VMEM] * 2,
-        scratch_shapes=[square] * 5
-        + [
-            pltpu.VMEM((2 * rows, width), BF16),
+        scratch_shapes=[
+            square,
+            pltpu.VMEM((2 * rows + width, width), BF16),
+            pltpu.VMEM((2 * width, width), BF16),
+            square,
             square,
             pltpu.SMEM(counts.shape, jnp.int32),
             pltpu.SemaphoreType.DMA(()),
         ],
-        compiler_params=params(32),
+        compiler_params=params(40),
     )(pltpu.with_memory_space_constraint(counts, pltpu.HBM), *pieces)
 
 

time: 47.6 us -> 47 us (0.987)
  Pallas kernels: 11.8 us -> 10.9 us
  waiting for transfers between devices: 19.9 us -> 20.4 us
    pallas_call x1, Pallas kernels: 9.19 us -> 8.33 us  [root(): pl.pallas_call(functools.partial(root_kernel, most), out_shape=[out, out]...]
where the time goes in v6:
time: 47 us; the launch traced here: 46.8 us
  waiting for transfers between devices  20.4 us (43%)
  starting transfers between devices  14.4 us (31%)
  Pallas kernels  10.9 us (23%)
  other arithmetic  0.97 us (2%)
    ppermute x12, waiting for transfers between devices, swap(): lax.ppermute(array, axis, [(i, i ^ mask) for i in range(lax.axis_size(axi...  17 us
    ppermute x12, starting transfers between devices, swap(): lax.ppermute(array, axis, [(i, i ^ mask) for i in range(lax.axis_size(axi...  10.8 us
    pallas_call x1, Pallas kernels, root(): pl.pallas_call(functools.partial(root_kernel, most), out_shape=[out, out]...  8.33 us
    ppermute x3, starting transfers between devices, shards(): lax.ppermute(piece, ('x', 'group'), moves)  3.55 us
    ppermute x3, waiting for transfers between devices, shards(): lax.ppermute(piece, ('x', 'group'), moves)  3.38 us
    pallas_call x1, Pallas kernels, load(): pl.pallas_call(functools.partial(load_kernel, scale, pieces), out_shape=[...  1.79 us
  transfers between devices with their start and end apart: 15, of which 12 were waited for; matrix products, arithmetic and copies ran while one was open for 0% of the time, Pallas kernels for 2%

profile of v6, /device:TPU:0, one launch (start us, length us, event | category | flops | bytes accessed | tf_op | source)
XLA Modules:
  0.0 46.8 jit_solution(10936711374867720187)
XLA Ops:
  0.0 1.8 %shard_map.37 = (bf16[512,256]{1,0:T(8,128)(2,1)S(1)}, bf16[2,2,512,256]{3,2,1,0:T(8,128)(2,1)S(1)}, bf16[2,512,512]{2,1,0:T(8,128)(2,1)S(1)}) custom-call(bf16[2,512,512]{2,1,0:T(8,128)(2,1)} %patch_hbm.1, bf16[2,512,512]{2,1,0:T(8,128)(2,1)} %cot_hbm.1), custom_call_target="tpu_custom_call" | custom-call | tf_op jit(solution)/shard_map/pallas_call | solution.py:78
  1.8 0.5 %collective-permute-start = (bf16[512,256]{1,0:T(8,128)(2,1)S(1)}, bf16[512,256]{1,0:T(8,128)(2,1)S(1)}, u32[]{:S(2)}, u32[]{:S(2)}) collective-permute-start(bf16[512,256]{1,0:T(8,128)(2,1)S(1)} %get-tuple-element.15), channel_id=1, source_target_pairs={{0,2},{2,0},{1,3},{3,1},{4,6},{6,4},{5,7},{7,5},{8,10},{10,8},{9,1... | collective-permute-start | bytes 786440 | tf_op jit(solution)/shard_map/ppermute | solution.py:239
  2.3 0.5 %shard_map.38 = (f32[512,256]{1,0:T(8,128)S(1)}, bf16[512,256]{1,0:T(8,128)(2,1)S(1)}) custom-call(bf16[2,2,512,256]{3,2,1,0:T(8,128)(2,1)S(1)} %get-tuple-element.12.patch, bf16[2,512,512]{2,1,0:T(8,128)(2,1)S(1)} %get-tuple-element.13.cot), custom_call_target="tpu_custom_call" | custom-call | flops 268435456 | bytes 2097152 | tf_op jit(solution)/shard_map/pallas_call | solution.py:102
  2.8 0.1 collective-permute-start.1
  2.9 0.5 %collective-permute-done = bf16[512,256]{1,0:T(8,128)(2,1)S(1)} collective-permute-done((bf16[512,256]{1,0:T(8,128)(2,1)S(1)}, bf16[512,256]{1,0:T(8,128)(2,1)S(1)}, u32[]{:S(2)}, u32[]{:S(2)}) %collective-permute-start) | collective-permute-done | bytes 262176 | tf_op jit(solution)/shard_map/ppermute | solution.py:239
  3.5 0.1 add_convert_fusion
  3.5 3.0 %collective-permute-start.7 = (bf16[256,256]{1,0:T(8,128)(2,1)S(1)}, bf16[256,256]{1,0:T(8,128)(2,1)S(1)}, u32[]{:S(2)}, u32[]{:S(2)}) collective-permute-start(bf16[256,256]{1,0:T(8,128)(2,1)S(1)} %get-tuple-element.21), channel_id=1, source_target_pairs={{0,8},{8,0},{16,24},{24,16},{1,9},{9,1},{17,25},{25,17},{2,10},{10... | collective-permute-start | bytes 393224 | tf_op jit(solution)/shard_map/ppermute | solution.py:239
  6.6 1.5 %collective-permute-start.2 = (bf16[256,256]{1,0:T(8,128)(2,1)S(1)}, bf16[256,256]{1,0:T(8,128)(2,1)S(1)}, u32[]{:S(2)}, u32[]{:S(2)}) collective-permute-start(bf16[256,256]{1,0:T(8,128)(2,1)S(1)} %get-tuple-element.22.refs_0_), channel_id=1, source_target_pairs={{0,4},{4,0},{1,5},{5,1},{2,6},{6,2},{3,7},{7,3},{8,12},{12,8},{9,1... | collective-permute-start | bytes 393224 | tf_op jit(solution)/shard_map/ppermute | solution.py:239
  8.0 0.3 shard_map.39
  8.4 0.0 collective-permute-done.1
  8.4 1.9 %collective-permute-done.7 = bf16[256,256]{1,0:T(8,128)(2,1)S(1)} collective-permute-done((bf16[256,256]{1,0:T(8,128)(2,1)S(1)}, bf16[256,256]{1,0:T(8,128)(2,1)S(1)}, u32[]{:S(2)}, u32[]{:S(2)}) %collective-permute-start.7) | collective-permute-done | bytes 131104 | tf_op jit(solution)/shard_map/ppermute | solution.py:239
  10.3 1.5 %collective-permute-done.2 = bf16[256,256]{1,0:T(8,128)(2,1)S(1)} collective-permute-done((bf16[256,256]{1,0:T(8,128)(2,1)S(1)}, bf16[256,256]{1,0:T(8,128)(2,1)S(1)}, u32[]{:S(2)}, u32[]{:S(2)}) %collective-permute-start.2) | collective-permute-done | bytes 131104 | tf_op jit(solution)/shard_map/ppermute | solution.py:239
  11.8 0.1 fusion
  11.9 0.4 collective-permute-start.3
  12.3 1.6 %collective-permute-start.8 = (bf16[128,256]{1,0:T(8,128)(2,1)S(1)}, bf16[128,256]{1,0:T(8,128)(2,1)S(1)}, u32[]{:S(2)}, u32[]{:S(2)}) collective-permute-start(bf16[128,256]{1,0:T(8,128)(2,1)S(1)} %slice.84), channel_id=1, source_target_pairs={{0,4},{4,0},{1,5},{5,1},{2,6},{6,2},{3,7},{7,3},{8,12},{12,8},{9,1... | collective-permute-start | bytes 196616 | tf_op jit(solution)/shard_map/ppermute | solution.py:239
  14.0 2.2 %collective-permute-done.3 = bf16[128,256]{1,0:T(8,128)(2,1)S(1)} collective-permute-done((bf16[128,256]{1,0:T(8,128)(2,1)S(1)}, bf16[128,256]{1,0:T(8,128)(2,1)S(1)}, u32[]{:S(2)}, u32[]{:S(2)}) %collective-permute-start.3) | collective-permute-done | bytes 65568 | tf_op jit(solution)/shard_map/ppermute | solution.py:239
  16.3 3.1 %collective-permute-start.4 = (bf16[128,256]{1,0:T(8,128)(2,1)S(1)}, bf16[128,256]{1,0:T(8,128)(2,1)S(1)}, u32[]{:S(2)}, u32[]{:S(2)}) collective-permute-start(bf16[128,256]{1,0:T(8,128)(2,1)S(1)} %fusion.2), channel_id=1, source_target_pairs={{0,16},{8,24},{16,0},{24,8},{1,17},{9,25},{17,1},{25,9},{2,18},{10... | collective-permute-start | bytes 196616 | tf_op jit(solution)/shard_map/ppermute | solution.py:239
  19.4 0.0 collective-permute-done.8
  19.4 0.1 collective-permute-start.9
  19.5 3.4 %collective-permute-done.4 = bf16[128,256]{1,0:T(8,128)(2,1)S(1)} collective-permute-done((bf16[128,256]{1,0:T(8,128)(2,1)S(1)}, bf16[128,256]{1,0:T(8,128)(2,1)S(1)}, u32[]{:S(2)}, u32[]{:S(2)}) %collective-permute-start.4) | collective-permute-done | bytes 65568 | tf_op jit(solution)/shard_map/ppermute | solution.py:239
  23.0 0.1 collective-permute-start.5
  23.1 1.9 %collective-permute-done.9 = bf16[128,256]{1,0:T(8,128)(2,1)S(1)} collective-permute-done((bf16[128,256]{1,0:T(8,128)(2,1)S(1)}, bf16[128,256]{1,0:T(8,128)(2,1)S(1)}, u32[]{:S(2)}, u32[]{:S(2)}) %collective-permute-start.9) | collective-permute-done | bytes 65568 | tf_op jit(solution)/shard_map/ppermute | solution.py:239
  25.0 0.2 collective-permute-start.10
  25.2 2.1 %collective-permute-done.5.refs_1_ = bf16[128,256]{1,0:T(8,128)(2,1)S(1)} collective-permute-done((bf16[128,256]{1,0:T(8,128)(2,1)S(1)}, bf16[128,256]{1,0:T(8,128)(2,1)S(1)}, u32[]{:S(2)}, u32[]{:S(2)}) %collective-permute-start.5) | collective-permute-done | bytes 65568 | tf_op jit(solution)/shard_map/ppermute | solution.py:239
  27.3 0.1 collective-permute-start.6
  27.4 1.9 %collective-permute-done.10.refs_4_ = bf16[128,256]{1,0:T(8,128)(2,1)S(1)} collective-permute-done((bf16[128,256]{1,0:T(8,128)(2,1)S(1)}, bf16[128,256]{1,0:T(8,128)(2,1)S(1)}, u32[]{:S(2)}, u32[]{:S(2)}) %collective-permute-start.10) | collective-permute-done | bytes 65568 | tf_op jit(solution)/shard_map/ppermute | solution.py:239
  29.4 0.1 collective-permute-start.11
  29.4 0.0 collective-permute-done.6.refs_2_
  29.5 1.3 %collective-permute-done.11.refs_5_ = bf16[256,256]{1,0:T(8,128)(2,1)S(1)} collective-permute-done((bf16[256,256]{1,0:T(8,128)(2,1)S(1)}, bf16[256,256]{1,0:T(8,128)(2,1)S(1)}, u32[]{:S(2)}, u32[]{:S(2)}) %collective-permute-start.11) | collective-permute-done | bytes 131104 | tf_op jit(solution)/shard_map/ppermute | solution.py:239
  30.8 8.3 %shard_map.40 = (bf16[32,512]{1,0:T(8,128)(2,1)S(1)}, bf16[32,512]{1,0:T(8,128)(2,1)S(1)}) custom-call(s32[2,2]{1,0:T(2,128)} %counts_hbm.1, bf16[128,256]{1,0:T(8,128)(2,1)S(1)} %add_convert_fusion.3.refs_0_, bf16[128,256]{1,0:T(8,128)(2,1)S(1)} %collective-permute-done.5.refs_1_, bf16[256,256]{1,0:T(8,128)(2,1)S(1)} %collective-permute-done.6.refs_2_, ...), custom_call_target="tpu_custom_call" | custom-call | tf_op jit(solution)/shard_map/pallas_call | solution.py:213
  39.1 1.6 %collective-permute-start.13 = (bf16[32,512]{1,0:T(8,128)(2,1)S(1)}, bf16[32,512]{1,0:T(8,128)(2,1)S(1)}, u32[]{:S(2)}, u32[]{:S(2)}) collective-permute-start(bf16[32,512]{1,0:T(8,128)(2,1)S(1)} %get-tuple-element.17), channel_id=1, source_target_pairs={{0,1},{1,0},{4,5},{5,4},{2,3},{3,2},{6,7},{7,6},{8,9},{9,8},{12,13... | collective-permute-start | bytes 98312 | tf_op jit(solution)/shard_map/ppermute | solution.py:282
  40.7 1.4 %collective-permute-start.14 = (bf16[32,512]{1,0:T(8,128)(2,1)S(1)}, bf16[32,512]{1,0:T(8,128)(2,1)S(1)}, u32[]{:S(2)}, u32[]{:S(2)}) collective-permute-start(bf16[32,512]{1,0:T(8,128)(2,1)S(1)} %get-tuple-element.18), channel_id=1, source_target_pairs={{0,5},{1,4},{4,1},{5,0},{2,7},{3,6},{6,3},{7,2},{8,13},{9,12},{12,... | collective-permute-start | bytes 98312 | tf_op jit(solution)/shard_map/ppermute | solution.py:282
  42.1 0.5 %collective-permute-start.12 = (bf16[32,512]{1,0:T(8,128)(2,1)S(1)}, bf16[32,512]{1,0:T(8,128)(2,1)S(1)}, u32[]{:S(2)}, u32[]{:S(2)}) collective-permute-start(bf16[32,512]{1,0:T(8,128)(2,1)S(1)} %get-tuple-element.18), channel_id=1, source_target_pairs={{0,4},{1,5},{4,0},{5,1},{2,6},{3,7},{6,2},{7,3},{8,12},{9,13},{12,... | collective-permute-start | bytes 98312 | tf_op jit(solution)/shard_map/ppermute | solution.py:282
  42.7 0.4 collective-permute-done.13
  43.1 2.7 %collective-permute-done.14 = bf16[32,512]{1,0:T(8,128)(2,1)S(1)} collective-permute-done((bf16[32,512]{1,0:T(8,128)(2,1)S(1)}, bf16[32,512]{1,0:T(8,128)(2,1)S(1)}, u32[]{:S(2)}, u32[]{:S(2)}) %collective-permute-start.14) | collective-permute-done | bytes 32800 | tf_op jit(solution)/shard_map/ppermute | solution.py:282
  45.8 0.3 collective-permute-done.12
  46.1 0.7 %reverse_select_fusion = bf16[2,2,32,512]{3,2,1,0:T(8,128)(2,1)} fusion(bf16[2,2,32,512]{3,2,1,0:T(8,128)(2,1)S(1)} %reverse_select_fusion.1, pred[]{:T(512)S(6)} %eq.6), kind=kLoop, calls=%fused_computation.6 | loop fusion | flops 65536 | bytes 262145 | tf_op jit(solution)/shard_map/jit(_where)/select_n | solution.py:290
  (12 shorter events, 0.2 us)
Async XLA Ops:
  1.8 1.7 %collective-permute-start = (bf16[512,256]{1,0:T(8,128)(2,1)S(1)}, bf16[512,256]{1,0:T(8,128)(2,1)S(1)}, u32[]{:S(2)}, u32[]{:S(2)}) collective-permute-start(bf16[512,256]{1,0:T(8,128)(2,1)S(1)} %get-tuple-element.15), channel_id=1, source_target_pairs={{0,2},{2,0},{1,3},{3,1},{4,6},{6,4},{5,7},{7,5},{8,10},{10,8},{9,1... | collective-permute-start | bytes 786440 | tf_op jit(solution)/shard_map/ppermute | solution.py:239
  2.8 5.6 %collective-permute-start.1 = (bf16[512,256]{1,0:T(8,128)(2,1)S(1)}, bf16[512,256]{1,0:T(8,128)(2,1)S(1)}, u32[]{:S(2)}, u32[]{:S(2)}) collective-permute-start(bf16[512,256]{1,0:T(8,128)(2,1)S(1)} %get-tuple-element.16), channel_id=1, source_target_pairs={{0,2},{2,0},{1,3},{3,1},{4,6},{6,4},{5,7},{7,5},{8,10},{10,8},{9,1... | collective-permute-start | bytes 786440 | tf_op jit(solution)/shard_map/ppermute | solution.py:239
  3.5 6.8 %collective-permute-start.7 = (bf16[256,256]{1,0:T(8,128)(2,1)S(1)}, bf16[256,256]{1,0:T(8,128)(2,1)S(1)}, u32[]{:S(2)}, u32[]{:S(2)}) collective-permute-start(bf16[256,256]{1,0:T(8,128)(2,1)S(1)} %get-tuple-element.21), channel_id=1, source_target_pairs={{0,8},{8,0},{16,24},{24,16},{1,9},{9,1},{17,25},{25,17},{2,10},{10... | collective-permute-start | bytes 393224 | tf_op jit(solution)/shard_map/ppermute | solution.py:239
  6.6 5.3 %collective-permute-start.2 = (bf16[256,256]{1,0:T(8,128)(2,1)S(1)}, bf16[256,256]{1,0:T(8,128)(2,1)S(1)}, u32[]{:S(2)}, u32[]{:S(2)}) collective-permute-start(bf16[256,256]{1,0:T(8,128)(2,1)S(1)} %get-tuple-element.22.refs_0_), channel_id=1, source_target_pairs={{0,4},{4,0},{1,5},{5,1},{2,6},{6,2},{3,7},{7,3},{8,12},{12,8},{9,1... | collective-permute-start | bytes 393224 | tf_op jit(solution)/shard_map/ppermute | solution.py:239
  11.9 4.3 %collective-permute-start.3 = (bf16[128,256]{1,0:T(8,128)(2,1)S(1)}, bf16[128,256]{1,0:T(8,128)(2,1)S(1)}, u32[]{:S(2)}, u32[]{:S(2)}) collective-permute-start(bf16[128,256]{1,0:T(8,128)(2,1)S(1)} %slice.85), channel_id=1, source_target_pairs={{0,8},{8,0},{16,24},{24,16},{1,9},{9,1},{17,25},{25,17},{2,10},{10... | collective-permute-start | bytes 196616 | tf_op jit(solution)/shard_map/ppermute | solution.py:239
  12.3 7.1 %collective-permute-start.8 = (bf16[128,256]{1,0:T(8,128)(2,1)S(1)}, bf16[128,256]{1,0:T(8,128)(2,1)S(1)}, u32[]{:S(2)}, u32[]{:S(2)}) collective-permute-start(bf16[128,256]{1,0:T(8,128)(2,1)S(1)} %slice.84), channel_id=1, source_target_pairs={{0,4},{4,0},{1,5},{5,1},{2,6},{6,2},{3,7},{7,3},{8,12},{12,8},{9,1... | collective-permute-start | bytes 196616 | tf_op jit(solution)/shard_map/ppermute | solution.py:239
  16.3 6.7 %collective-permute-start.4 = (bf16[128,256]{1,0:T(8,128)(2,1)S(1)}, bf16[128,256]{1,0:T(8,128)(2,1)S(1)}, u32[]{:S(2)}, u32[]{:S(2)}) collective-permute-start(bf16[128,256]{1,0:T(8,128)(2,1)S(1)} %fusion.2), channel_id=1, source_target_pairs={{0,16},{8,24},{16,0},{24,8},{1,17},{9,25},{17,1},{25,9},{2,18},{10... | collective-permute-start | bytes 196616 | tf_op jit(solution)/shard_map/ppermute | solution.py:239
  19.4 5.6 %collective-permute-start.9 = (bf16[128,256]{1,0:T(8,128)(2,1)S(1)}, bf16[128,256]{1,0:T(8,128)(2,1)S(1)}, u32[]{:S(2)}, u32[]{:S(2)}) collective-permute-start(bf16[128,256]{1,0:T(8,128)(2,1)S(1)} %fusion.3), channel_id=1, source_target_pairs={{0,16},{8,24},{16,0},{24,8},{1,17},{9,25},{17,1},{25,9},{2,18},{10... | collective-permute-start | bytes 196616 | tf_op jit(solution)/shard_map/ppermute | solution.py:239
  23.0 4.3 %collective-permute-start.5 = (bf16[128,256]{1,0:T(8,128)(2,1)S(1)}, bf16[128,256]{1,0:T(8,128)(2,1)S(1)}, u32[]{:S(2)}, u32[]{:S(2)}) collective-permute-start(bf16[128,256]{1,0:T(8,128)(2,1)S(1)} %add_convert_fusion.3.refs_0_), channel_id=1, source_target_pairs={{0,8},{8,0},{16,24},{24,16},{1,9},{9,1},{17,25},{25,17},{2,10},{10... | collective-permute-start | bytes 196616 | tf_op jit(solution)/shard_map/ppermute | solution.py:239
  25.0 4.3 %collective-permute-start.10 = (bf16[128,256]{1,0:T(8,128)(2,1)S(1)}, bf16[128,256]{1,0:T(8,128)(2,1)S(1)}, u32[]{:S(2)}, u32[]{:S(2)}) collective-permute-start(bf16[128,256]{1,0:T(8,128)(2,1)S(1)} %add_convert_fusion.2.refs_3_), channel_id=1, source_target_pairs={{0,8},{8,0},{16,24},{24,16},{1,9},{9,1},{17,25},{25,17},{2,10},{10... | collective-permute-start | bytes 196616 | tf_op jit(solution)/shard_map/ppermute | solution.py:239
  27.3 2.1 %collective-permute-start.6 = (bf16[256,256]{1,0:T(8,128)(2,1)S(1)}, bf16[256,256]{1,0:T(8,128)(2,1)S(1)}, u32[]{:S(2)}, u32[]{:S(2)}) collective-permute-start(bf16[256,256]{1,0:T(8,128)(2,1)S(1)} %pad_maximum_fusion), channel_id=1, source_target_pairs={{0,2},{2,0},{1,3},{3,1},{4,6},{6,4},{5,7},{7,5},{8,10},{10,8},{9,1... | collective-permute-start | bytes 393224 | tf_op jit(solution)/shard_map/ppermute | solution.py:239
  29.4 1.4 %collective-permute-start.11 = (bf16[256,256]{1,0:T(8,128)(2,1)S(1)}, bf16[256,256]{1,0:T(8,128)(2,1)S(1)}, u32[]{:S(2)}, u32[]{:S(2)}) collective-permute-start(bf16[256,256]{1,0:T(8,128)(2,1)S(1)} %pad_maximum_fusion.1), channel_id=1, source_target_pairs={{0,2},{2,0},{1,3},{3,1},{4,6},{6,4},{5,7},{7,5},{8,10},{10,8},{9,1... | collective-permute-start | bytes 393224 | tf_op jit(solution)/shard_map/ppermute | solution.py:239
  39.1 4.0 %collective-permute-start.13 = (bf16[32,512]{1,0:T(8,128)(2,1)S(1)}, bf16[32,512]{1,0:T(8,128)(2,1)S(1)}, u32[]{:S(2)}, u32[]{:S(2)}) collective-permute-start(bf16[32,512]{1,0:T(8,128)(2,1)S(1)} %get-tuple-element.17), channel_id=1, source_target_pairs={{0,1},{1,0},{4,5},{5,4},{2,3},{3,2},{6,7},{7,6},{8,9},{9,8},{12,13... | collective-permute-start | bytes 98312 | tf_op jit(solution)/shard_map/ppermute | solution.py:282
  40.7 5.0 %collective-permute-start.14 = (bf16[32,512]{1,0:T(8,128)(2,1)S(1)}, bf16[32,512]{1,0:T(8,128)(2,1)S(1)}, u32[]{:S(2)}, u32[]{:S(2)}) collective-permute-start(bf16[32,512]{1,0:T(8,128)(2,1)S(1)} %get-tuple-element.18), channel_id=1, source_target_pairs={{0,5},{1,4},{4,1},{5,0},{2,7},{3,6},{6,3},{7,2},{8,13},{9,12},{12,... | collective-permute-start | bytes 98312 | tf_op jit(solution)/shard_map/ppermute | solution.py:282
  42.1 3.9 %collective-permute-start.12 = (bf16[32,512]{1,0:T(8,128)(2,1)S(1)}, bf16[32,512]{1,0:T(8,128)(2,1)S(1)}, u32[]{:S(2)}, u32[]{:S(2)}) collective-permute-start(bf16[32,512]{1,0:T(8,128)(2,1)S(1)} %get-tuple-element.18), channel_id=1, source_target_pairs={{0,4},{1,5},{4,0},{5,1},{2,6},{3,7},{6,2},{7,3},{8,12},{9,13},{12,... | collective-permute-start | bytes 98312 | tf_op jit(solution)/shard_map/ppermute | solution.py:282

commit v7 on v6

--- a/solution.py
+++ b/solution.py
@@ -20,97 +20,102 @@
     return pltpu.CompilerParams(vmem_limit_bytes=limit << 20)
 
 
-def piece_sum(patch, cot, scale, piece):
-    block, columns, side, quarter = piece
-    half = patch.shape[3]
-    rows = slice(None) if quarter is None else slice(quarter * half // 2, (quarter + 1) * half // 2)
-    terms = lax.dot_general(
-        patch[block, side, :, rows],
-        cot[block, :, columns * half : (columns + 1) * half],
-        ROWS_IN_COLS,
-        preferred_element_type=F32,
-    )
-    return terms * scale
-
-
-def write_pieces(patch, cot, scale, pieces, out):
-    row = 0
-    for piece in pieces:
-        value = piece_sum(patch, cot, scale, piece)
-        out[row : row + value.shape[0], :] = value.astype(out.dtype)
-        row += value.shape[0]
-
-
-def load_kernel(scale, pieces, patch_hbm, cot_hbm, out, patch, cot, sems):
-    half = patch.shape[3]
+def fetch_block(block, side_order, hbm, buffers, sems):
+    patch_hbm, cot_hbm = hbm
+    patch, cot = buffers
+    half = patch.shape[2]
     width = half // 2
     column, core, parity = lax.axis_index("x"), lax.axis_index("core"), lax.axis_index("z") % 2
-    copies = []
-
-    def fetch(source, target):
-        copies.append(pltpu.make_async_copy(source, target, sems.at[len(copies)]))
-        copies[-1].start()
-
-    def fetch_patch(block, side):
+    copies = [pltpu.make_async_copy(cot_hbm.at[column ^ block], cot, sems.at[0])]
+    for side in side_order:
         for quarter in range(2):
             first = (core ^ side) * half + (parity ^ quarter) * width
-            fetch(
-                patch_hbm.at[column ^ block, :, pl.ds(pl.multiple_of(first, width), width)],
-                patch.at[block, side, :, quarter * width : (quarter + 1) * width],
+            copies.append(
+                pltpu.make_async_copy(
+                    patch_hbm.at[column ^ block, :, pl.ds(pl.multiple_of(first, width), width)],
+                    patch.at[side, :, quarter * width : (quarter + 1) * width],
+                    sems.at[len(copies)],
+                )
             )
-
-    for block in (1, 0):
-        fetch(cot_hbm.at[column ^ block], cot.at[block])
-        fetch_patch(block, 1)
-    needed = len(copies)
-    for block in (1, 0):
-        fetch_patch(block, 0)
-    for copy in copies[:needed]:
+    for copy in copies:
+        copy.start()
+    return copies
+
+
+def half_sum(patch, cot, side, scale):
+    terms = lax.dot_general(patch[side], cot[...], ROWS_IN_COLS, preferred_element_type=F32)
+    return terms * scale
+
+
+def first_kernel(scale, patch_hbm, cot_hbm, given, patch, cot, sems):
+    copies = fetch_block(1, (1, 0), (patch_hbm, cot_hbm), (patch, cot), sems)
+    for copy in copies[:3]:
         copy.wait()
-    write_pieces(patch, cot, scale, pieces, out)
-    for copy in copies[needed:]:
+    given[...] = half_sum(patch, cot, 1, scale).astype(BF16)
+    for copy in copies[3:]:
         copy.wait()
 
 
-def load(patches, cotangents, scale, pieces):
-    blocks, pix, width = patches.shape
+def second_kernel(scale, patch_hbm, cot_hbm, other_patch, other_cot, kept, given, patch, cot, sems):
+    copies = fetch_block(0, (1, 0), (patch_hbm, cot_hbm), (patch, cot), sems)
+    kept[...] = half_sum(other_patch, other_cot, 0, scale)
+    for copy in copies[:3]:
+        copy.wait()
+    given[...] = half_sum(patch, cot, 1, scale).astype(BF16)
+    for copy in copies[3:]:
+        copy.wait()
+
+
+def third_kernel(scale, patch, cot, _, kept):
+    kept[...] = half_sum(patch, cot, 0, scale)
+
+
+def pixel_sums(kernel, scale, shape, sums, loads, *operands):
+    pix, width = shape
     half = width // 2
+    out_shape = [jax.ShapeDtypeStruct((half, width), dtype) for dtype in sums]
+    if loads:
+        out_shape.append(jax.ShapeDtypeStruct((2, pix, half), BF16))
+        out_shape.append(jax.ShapeDtypeStruct((pix, width), BF16))
     return pl.pallas_call(
-        functools.partial(load_kernel, scale, pieces),
-        out_shape=[
-            jax.ShapeDtypeStruct((2 * half, half), BF16),
-            jax.ShapeDtypeStruct((blocks, 2, pix, half), BF16),
-            jax.ShapeDtypeStruct((blocks, pix, width), BF16),
-        ],
-        in_specs=[HBM, HBM],
-        out_specs=[VMEM] * 3,
-        scratch_shapes=[pltpu.SemaphoreType.DMA((10,))],
-        compiler_params=params(16),
-    )(
-        pltpu.with_memory_space_constraint(patches, pltpu.HBM),
-        pltpu.with_memory_space_constraint(cotangents, pltpu.HBM),
-    )
-
-
-def gram_kernel(scale, outputs, patch, cot, *refs):
-    for (_, pieces), out in zip(outputs, refs[-len(outputs) :]):
-        write_pieces(patch, cot, scale, pieces, out)
-
-
-def gram(patch, cot, after, scale, *outputs):
-    pix, half = patch.shape[2:]
-    return pl.pallas_call(
-        functools.partial(gram_kernel, scale, outputs),
-        out_shape=[jax.ShapeDtypeStruct((2 * half, half), dtype) for dtype, _ in outputs],
-        in_specs=[VMEM, VMEM] + [pl.BlockSpec(memory_space=pl.ANY)] * len(after),
-        out_specs=[VMEM] * len(outputs),
+        functools.partial(kernel, scale),
+        out_shape=out_shape,
+        in_specs=[HBM if loads and index < 2 else VMEM for index in range(len(operands))],
+        out_specs=[VMEM] * len(out_shape),
+        scratch_shapes=[pltpu.SemaphoreType.DMA((5,))] if loads else [],
         compiler_params=params(16),
         cost_estimate=pl.CostEstimate(
-            flops=4 * len(outputs) * pix * half * half,
-            bytes_accessed=2 * (patch.size + cot.size),
+            flops=2 * len(sums) * pix * half * width,
+            bytes_accessed=4 * pix * width,
             transcendentals=0,
         ),
-    )(patch, cot, *after)
+    )(*operands)
+
+
+def collect_kernel(own, *refs):
+    *came, keep_left, keep_right, send_left, send_right = refs
+    half = keep_left.shape[1]
+    for columns, keep, send in (
+        (slice(0, half), keep_left, send_left),
+        (slice(half, 2 * half), keep_right, send_right),
+    ):
+        total = own[: keep.shape[0], columns]
+        for ref in came:
+            total = total + ref[:, columns].astype(F32)
+        keep[...] = total
+        send[...] = total.astype(BF16)
+
+
+def collect(own, *came):
+    rows, width = came[0].shape
+    shape = (rows, width // 2)
+    return pl.pallas_call(
+        collect_kernel,
+        out_shape=[jax.ShapeDtypeStruct(shape, F32)] * 2 + [jax.ShapeDtypeStruct(shape, BF16)] * 2,
+        in_specs=[VMEM] * (1 + len(came)),
+        out_specs=[VMEM] * 4,
+        compiler_params=params(16),
+    )(own, *came)
 
 
 def add(*values):
@@ -238,33 +243,35 @@
     def swap(array, axis, mask=1):
         return lax.ppermute(array, axis, [(i, i ^ mask) for i in range(lax.axis_size(axis))])
 
-    def leaving(side):
-        return ((1, 0, side, None), (1, 1, side, 1), (0, 1, side, 1))
-
-    def staying(side):
-        return ((0, 0, side, None), (1, 1, side, 0), (0, 1, side, 0))
-
-    given, patch, cot = load(patches, cotangents, scale, leaving(1))
+    def swap_diagonal(array):
+        moves = [(2 * z + x, 2 * (z ^ 1) + (x ^ 1)) for z in range(line) for x in range(2)]
+        return lax.ppermute(array, ("z", "x"), moves)
+
+    patches = pltpu.with_memory_space_constraint(patches, pltpu.HBM)
+    cotangents = pltpu.with_memory_space_constraint(cotangents, pltpu.HBM)
+    shape = (pix, width)
+    given, *loaded = pixel_sums(first_kernel, scale, shape, (BF16,), True, patches, cotangents)
     came = swap(given, "core")
-    kept, given_on = gram(patch, cot, (), scale, (F32, leaving(0)), (BF16, staying(1)))
+    kept, given_on, *loaded = pixel_sums(
+        second_kernel, scale, shape, (F32, BF16), True, patches, cotangents, *loaded
+    )
     came_on = swap(given_on, "core")
-    to_column = add(kept[:half], came[:half]).astype(BF16)
-    to_line = add(kept[half:], came[half:]).astype(BF16)
+    leaving = add(kept, came).astype(BF16)
+    to_diagonal, to_column = leaving[quarter:], leaving[:quarter]
+    from_diagonal = swap_diagonal(to_diagonal)
     from_column = swap(to_column, "x")
-    from_line = swap(to_line, "z")
-    (kept_on,) = gram(patch, cot, (to_column,), scale, (F32, staying(0)))
-    left = add(kept_on[:half], came_on[:half], from_column)
-    from_line_left = swap(left[quarter:].astype(BF16), "z")
-    right = add(kept_on[half:], came_on[half:], from_line)
-    from_column_right = swap(right[:quarter].astype(BF16), "x")
-    streams = [add(left[:quarter], from_line_left), add(right[quarter:], from_column_right)]
-    mask = 2
-    while mask < line:
-        streams = [add(own, swap(own.astype(BF16), "z", mask)) for own in streams]
-        mask *= 2
+    (kept_on,) = pixel_sums(third_kernel, scale, shape, (F32,), False, *loaded, to_diagonal)
+    own = add(kept_on, came_on)
+    from_line = swap(own[quarter:].astype(BF16), "z")
+    left, right, send_left, send_right = collect(own, from_diagonal, from_column, from_line)
     pieces = []
-    for own in streams:
-        own = own.astype(BF16)
+    for own, send in ((left, send_left), (right, send_right)):
+        mask = 2
+        while mask < line:
+            own = add(own, swap(send, "z", mask))
+            send = own.astype(BF16)
+            mask *= 2
+        own = send
         other = swap(own, "z")
         pieces += [own, other, swap(jnp.concatenate([own, other], 0), "core")]
     keep, send = root(newton_counts, pieces, rows)

time: 47 us -> 45.6 us (0.970)
  waiting for transfers between devices: 20.4 us -> 15.2 us
  starting transfers between devices: 14.4 us -> 17.3 us
  Pallas kernels: 10.9 us -> 11.8 us
    ppermute x12 -> x10, waiting for transfers between devices: 17 us -> 11.6 us  [swap(): lax.ppermute(array, axis, [(i, i ^ mask) for i in range(lax.axis_size(axi...]
    ppermute x0 -> x1, starting transfers between devices: none -> 4.02 us  [swap_diagonal(): return lax.ppermute(array, ('z', 'x'), moves)]
    ppermute x12 -> x10, starting transfers between devices: 10.8 us -> 9.09 us  [swap(): lax.ppermute(array, axis, [(i, i ^ mask) for i in range(lax.axis_size(axi...]
    pallas_call x3 -> x4, Pallas kernels: 2.62 us -> 3.42 us  [the longest x3 3.36 us: pixel_sums(): pl.pallas_call(functools.partial(kernel, scale), out_shape=out_shape, in_...]
    ppermute x3, starting transfers between devices: 3.55 us -> 4.24 us  [shards(): lax.ppermute(piece, ('x', 'group'), moves)]
  transfers between devices with their start and end apart: 15 -> 14, of which waited for: 12 -> 7; matrix products, arithmetic and copies ran while one was open for 0% -> 1% of each run, Pallas kernels for 2% -> 4%
where the time goes in v7:
time: 45.6 us; the launch traced here: 45.4 us
  starting transfers between devices  17.3 us (38%)
  waiting for transfers between devices  15.2 us (33%)
  Pallas kernels  11.8 us (26%)
  other arithmetic  0.93 us (2%)
    ppermute x10, waiting for transfers between devices, swap(): lax.ppermute(array, axis, [(i, i ^ mask) for i in range(lax.axis_size(axi...  11.6 us
    ppermute x10, starting transfers between devices, swap(): lax.ppermute(array, axis, [(i, i ^ mask) for i in range(lax.axis_size(axi...  9.09 us
    pallas_call x1, Pallas kernels, root(): pl.pallas_call(functools.partial(root_kernel, most), out_shape=[out, out]...  8.33 us
    ppermute x3, starting transfers between devices, shards(): lax.ppermute(piece, ('x', 'group'), moves)  4.24 us
    ppermute x1, starting transfers between devices, swap_diagonal(): return lax.ppermute(array, ('z', 'x'), moves)  4.02 us
    ppermute x3, waiting for transfers between devices, shards(): lax.ppermute(piece, ('x', 'group'), moves)  3.61 us
    pallas_call x3, Pallas kernels, pixel_sums(): pl.pallas_call(functools.partial(kernel, scale), out_shape=out_shape, in_...  3.36 us
  transfers between devices with their start and end apart: 14, of which 7 were waited for; matrix products, arithmetic and copies ran while one was open for 1% of the time, Pallas kernels for 4%

profile of v7, /device:TPU:0, one launch (start us, length us, event | category | flops | bytes accessed | tf_op | source)
XLA Modules:
  0.0 45.4 jit_solution(10074926740356344307)
XLA Ops:
  0.0 1.5 %shard_map.37 = (bf16[256,512]{1,0:T(8,128)(2,1)S(1)}, bf16[2,512,256]{2,1,0:T(8,128)(2,1)S(1)}, bf16[512,512]{1,0:T(8,128)(2,1)S(1)}) custom-call(bf16[2,512,512]{2,1,0:T(8,128)(2,1)} %patch_hbm.3, bf16[2,512,512]{2,1,0:T(8,128)(2,1)} %cot_hbm.3), custom_call_target="tpu_custom_call" | custom-call | flops 134217728 | bytes 1048576 | tf_op jit(solution)/shard_map/pallas_call | solution.py:80
  1.5 0.5 %collective-permute-start = (bf16[256,512]{1,0:T(8,128)(2,1)S(1)}, bf16[256,512]{1,0:T(8,128)(2,1)S(1)}, u32[]{:S(2)}, u32[]{:S(2)}) collective-permute-start(bf16[256,512]{1,0:T(8,128)(2,1)S(1)} %get-tuple-element.23), channel_id=1, source_target_pairs={{0,2},{2,0},{1,3},{3,1},{4,6},{6,4},{5,7},{7,5},{8,10},{10,8},{9,1... | collective-permute-start | bytes 786440 | tf_op jit(solution)/shard_map/ppermute | solution.py:244
  2.0 1.6 %shard_map.38 = (f32[256,512]{1,0:T(8,128)S(1)}, bf16[256,512]{1,0:T(8,128)(2,1)S(1)}, bf16[2,512,256]{2,1,0:T(8,128)(2,1)S(1)}, bf16[512,512]{1,0:T(8,128)(2,1)S(1)}) custom-call(bf16[2,512,512]{2,1,0:T(8,128)(2,1)} %patch_hbm.3, bf16[2,512,512]{2,1,0:T(8,128)(2,1)} %cot_hbm.3, bf16[2,512,256]{2,1,0:T(8,128)(2,1)S(1)} %get-tuple-element.18.other_patch, ...), custom_call_target="tpu_custom_call" | custom-call | flops 268435456 | bytes 1048576 | tf_op jit(solution)/shard_map/pallas_call | solution.py:80
  3.6 0.1 collective-permute-start.1
  3.7 0.0 collective-permute-done
  3.7 0.1 add_convert_fusion
  3.8 4.0 %collective-permute-start.2 = (bf16[128,512]{1,0:T(8,128)(2,1)S(1)}, bf16[128,512]{1,0:T(8,128)(2,1)S(1)}, u32[]{:S(2)}, u32[]{:S(2)}) collective-permute-start(bf16[128,512]{1,0:T(8,128)(2,1)S(1)} %get-tuple-element.32._), channel_id=1, source_target_pairs={{0,12},{4,8},{8,4},{12,0},{16,28},{20,24},{24,20},{28,16},{1,13},{... | collective-permute-start | bytes 393224 | tf_op jit(solution)/shard_map/ppermute | solution.py:248
  7.8 0.3 shard_map.39
  8.1 0.0 collective-permute-done.1
  8.2 0.1 convert_add_fusion.own
  8.3 0.5 %collective-permute-start.4 = (bf16[128,512]{1,0:T(8,128)(2,1)S(1)}, bf16[128,512]{1,0:T(8,128)(2,1)S(1)}, u32[]{:S(2)}, u32[]{:S(2)}) collective-permute-start(bf16[128,512]{1,0:T(8,128)(2,1)S(1)} %slice.17), channel_id=1, source_target_pairs={{0,8},{8,0},{16,24},{24,16},{1,9},{9,1},{17,25},{25,17},{2,10},{10... | collective-permute-start | bytes 393224 | tf_op jit(solution)/shard_map/ppermute | solution.py:244
  8.8 0.8 %collective-permute-start.3 = (bf16[128,512]{1,0:T(8,128)(2,1)S(1)}, bf16[128,512]{1,0:T(8,128)(2,1)S(1)}, u32[]{:S(2)}, u32[]{:S(2)}) collective-permute-start(bf16[128,512]{1,0:T(8,128)(2,1)S(1)} %get-tuple-element.31), channel_id=1, source_target_pairs={{0,4},{4,0},{1,5},{5,1},{2,6},{6,2},{3,7},{7,3},{8,12},{12,8},{9,1... | collective-permute-start | bytes 393224 | tf_op jit(solution)/shard_map/ppermute | solution.py:244
  9.6 4.9 %collective-permute-done.4.refs_2_ = bf16[128,512]{1,0:T(8,128)(2,1)S(1)} collective-permute-done((bf16[128,512]{1,0:T(8,128)(2,1)S(1)}, bf16[128,512]{1,0:T(8,128)(2,1)S(1)}, u32[]{:S(2)}, u32[]{:S(2)}) %collective-permute-start.4) | collective-permute-done | bytes 131104 | tf_op jit(solution)/shard_map/ppermute | solution.py:244
  14.5 0.0 collective-permute-done.2.refs_0_
  14.5 0.0 collective-permute-done.3.refs_1_
  14.5 0.1 shard_map.40
  14.6 2.7 %collective-permute-start.8 = (bf16[128,256]{1,0:T(8,128)(2,1)S(1)}, bf16[128,256]{1,0:T(8,128)(2,1)S(1)}, u32[]{:S(2)}, u32[]{:S(2)}) collective-permute-start(bf16[128,256]{1,0:T(8,128)(2,1)S(1)} %get-tuple-element.28), channel_id=1, source_target_pairs={{0,16},{8,24},{16,0},{24,8},{1,17},{9,25},{17,1},{25,9},{2,18},{10... | collective-permute-start | bytes 196616 | tf_op jit(solution)/shard_map/ppermute | solution.py:244
  17.2 0.3 collective-permute-start.5
  17.5 2.5 %collective-permute-done.8 = bf16[128,256]{1,0:T(8,128)(2,1)S(1)} collective-permute-done((bf16[128,256]{1,0:T(8,128)(2,1)S(1)}, bf16[128,256]{1,0:T(8,128)(2,1)S(1)}, u32[]{:S(2)}, u32[]{:S(2)}) %collective-permute-start.8) | collective-permute-done | bytes 65568 | tf_op jit(solution)/shard_map/ppermute | solution.py:244
  20.0 2.6 %collective-permute-start.9 = (bf16[128,256]{1,0:T(8,128)(2,1)S(1)}, bf16[128,256]{1,0:T(8,128)(2,1)S(1)}, u32[]{:S(2)}, u32[]{:S(2)}) collective-permute-start(bf16[128,256]{1,0:T(8,128)(2,1)S(1)} %add_convert_fusion.1.refs_3_), channel_id=1, source_target_pairs={{0,8},{8,0},{16,24},{24,16},{1,9},{9,1},{17,25},{25,17},{2,10},{10... | collective-permute-start | bytes 196616 | tf_op jit(solution)/shard_map/ppermute | solution.py:244
  22.7 0.0 collective-permute-done.5
  22.7 1.4 %collective-permute-start.6 = (bf16[128,256]{1,0:T(8,128)(2,1)S(1)}, bf16[128,256]{1,0:T(8,128)(2,1)S(1)}, u32[]{:S(2)}, u32[]{:S(2)}) collective-permute-start(bf16[128,256]{1,0:T(8,128)(2,1)S(1)} %add_convert_fusion.2.refs_0_), channel_id=1, source_target_pairs={{0,8},{8,0},{16,24},{24,16},{1,9},{9,1},{17,25},{25,17},{2,10},{10... | collective-permute-start | bytes 196616 | tf_op jit(solution)/shard_map/ppermute | solution.py:244
  24.1 1.1 %collective-permute-done.9.refs_4_ = bf16[128,256]{1,0:T(8,128)(2,1)S(1)} collective-permute-done((bf16[128,256]{1,0:T(8,128)(2,1)S(1)}, bf16[128,256]{1,0:T(8,128)(2,1)S(1)}, u32[]{:S(2)}, u32[]{:S(2)}) %collective-permute-start.9) | collective-permute-done | bytes 65568 | tf_op jit(solution)/shard_map/ppermute | solution.py:244
  25.2 0.1 collective-permute-start.10
  25.2 1.8 %collective-permute-done.6.refs_1_ = bf16[128,256]{1,0:T(8,128)(2,1)S(1)} collective-permute-done((bf16[128,256]{1,0:T(8,128)(2,1)S(1)}, bf16[128,256]{1,0:T(8,128)(2,1)S(1)}, u32[]{:S(2)}, u32[]{:S(2)}) %collective-permute-start.6) | collective-permute-done | bytes 65568 | tf_op jit(solution)/shard_map/ppermute | solution.py:244
  27.0 0.1 collective-permute-start.7
  27.1 0.0 collective-permute-done.10.refs_5_
  27.1 1.3 %collective-permute-done.7.refs_2_ = bf16[256,256]{1,0:T(8,128)(2,1)S(1)} collective-permute-done((bf16[256,256]{1,0:T(8,128)(2,1)S(1)}, bf16[256,256]{1,0:T(8,128)(2,1)S(1)}, u32[]{:S(2)}, u32[]{:S(2)}) %collective-permute-start.7) | collective-permute-done | bytes 131104 | tf_op jit(solution)/shard_map/ppermute | solution.py:244
  28.5 8.3 %shard_map.41 = (bf16[32,512]{1,0:T(8,128)(2,1)S(1)}, bf16[32,512]{1,0:T(8,128)(2,1)S(1)}) custom-call(s32[2,2]{1,0:T(2,128)} %counts_hbm.1, bf16[128,256]{1,0:T(8,128)(2,1)S(1)} %add_convert_fusion.2.refs_0_, bf16[128,256]{1,0:T(8,128)(2,1)S(1)} %collective-permute-done.6.refs_1_, bf16[256,256]{1,0:T(8,128)(2,1)S(1)} %collective-permute-done.7.refs_2_, ...), custom_call_target="tpu_custom_call" | custom-call | tf_op jit(solution)/shard_map/pallas_call | solution.py:218
  36.8 2.7 %collective-permute-start.11 = (bf16[32,512]{1,0:T(8,128)(2,1)S(1)}, bf16[32,512]{1,0:T(8,128)(2,1)S(1)}, u32[]{:S(2)}, u32[]{:S(2)}) collective-permute-start(bf16[32,512]{1,0:T(8,128)(2,1)S(1)} %get-tuple-element.30), channel_id=1, source_target_pairs={{0,4},{1,5},{4,0},{5,1},{2,6},{3,7},{6,2},{7,3},{8,12},{9,13},{12,... | collective-permute-start | bytes 98312 | tf_op jit(solution)/shard_map/ppermute | solution.py:289
  39.5 1.0 %collective-permute-start.13 = (bf16[32,512]{1,0:T(8,128)(2,1)S(1)}, bf16[32,512]{1,0:T(8,128)(2,1)S(1)}, u32[]{:S(2)}, u32[]{:S(2)}) collective-permute-start(bf16[32,512]{1,0:T(8,128)(2,1)S(1)} %get-tuple-element.30), channel_id=1, source_target_pairs={{0,5},{1,4},{4,1},{5,0},{2,7},{3,6},{6,3},{7,2},{8,13},{9,12},{12,... | collective-permute-start | bytes 98312 | tf_op jit(solution)/shard_map/ppermute | solution.py:289
  40.5 0.5 %collective-permute-start.12 = (bf16[32,512]{1,0:T(8,128)(2,1)S(1)}, bf16[32,512]{1,0:T(8,128)(2,1)S(1)}, u32[]{:S(2)}, u32[]{:S(2)}) collective-permute-start(bf16[32,512]{1,0:T(8,128)(2,1)S(1)} %get-tuple-element.29), channel_id=1, source_target_pairs={{0,1},{1,0},{4,5},{5,4},{2,3},{3,2},{6,7},{7,6},{8,9},{9,8},{12,13... | collective-permute-start | bytes 98312 | tf_op jit(solution)/shard_map/ppermute | solution.py:289
  41.0 0.3 collective-permute-done.11
  41.4 3.3 %collective-permute-done.12 = bf16[32,512]{1,0:T(8,128)(2,1)S(1)} collective-permute-done((bf16[32,512]{1,0:T(8,128)(2,1)S(1)}, bf16[32,512]{1,0:T(8,128)(2,1)S(1)}, u32[]{:S(2)}, u32[]{:S(2)}) %collective-permute-start.12) | collective-permute-done | bytes 32800 | tf_op jit(solution)/shard_map/ppermute | solution.py:289
  44.6 0.0 collective-permute-done.13
  44.7 0.7 %reverse_select_fusion = bf16[2,2,32,512]{3,2,1,0:T(8,128)(2,1)} fusion(bf16[2,2,32,512]{3,2,1,0:T(8,128)(2,1)S(1)} %reverse_select_fusion.1, pred[]{:T(512)S(6)} %eq.6), kind=kLoop, calls=%fused_computation.3 | loop fusion | flops 65536 | bytes 262145 | tf_op jit(solution)/shard_map/jit(_where)/select_n | solution.py:297
  (10 shorter events, 0.1 us)
Async XLA Ops:
  1.5 2.2 %collective-permute-start = (bf16[256,512]{1,0:T(8,128)(2,1)S(1)}, bf16[256,512]{1,0:T(8,128)(2,1)S(1)}, u32[]{:S(2)}, u32[]{:S(2)}) collective-permute-start(bf16[256,512]{1,0:T(8,128)(2,1)S(1)} %get-tuple-element.23), channel_id=1, source_target_pairs={{0,2},{2,0},{1,3},{3,1},{4,6},{6,4},{5,7},{7,5},{8,10},{10,8},{9,1... | collective-permute-start | bytes 786440 | tf_op jit(solution)/shard_map/ppermute | solution.py:244
  3.6 4.6 %collective-permute-start.1 = (bf16[256,512]{1,0:T(8,128)(2,1)S(1)}, bf16[256,512]{1,0:T(8,128)(2,1)S(1)}, u32[]{:S(2)}, u32[]{:S(2)}) collective-permute-start(bf16[256,512]{1,0:T(8,128)(2,1)S(1)} %get-tuple-element.24), channel_id=1, source_target_pairs={{0,2},{2,0},{1,3},{3,1},{4,6},{6,4},{5,7},{7,5},{8,10},{10,8},{9,1... | collective-permute-start | bytes 786440 | tf_op jit(solution)/shard_map/ppermute | solution.py:244
  3.8 10.7 %collective-permute-start.2 = (bf16[128,512]{1,0:T(8,128)(2,1)S(1)}, bf16[128,512]{1,0:T(8,128)(2,1)S(1)}, u32[]{:S(2)}, u32[]{:S(2)}) collective-permute-start(bf16[128,512]{1,0:T(8,128)(2,1)S(1)} %get-tuple-element.32._), channel_id=1, source_target_pairs={{0,12},{4,8},{8,4},{12,0},{16,28},{20,24},{24,20},{28,16},{1,13},{... | collective-permute-start | bytes 393224 | tf_op jit(solution)/shard_map/ppermute | solution.py:248
  8.3 6.2 %collective-permute-start.4 = (bf16[128,512]{1,0:T(8,128)(2,1)S(1)}, bf16[128,512]{1,0:T(8,128)(2,1)S(1)}, u32[]{:S(2)}, u32[]{:S(2)}) collective-permute-start(bf16[128,512]{1,0:T(8,128)(2,1)S(1)} %slice.17), channel_id=1, source_target_pairs={{0,8},{8,0},{16,24},{24,16},{1,9},{9,1},{17,25},{25,17},{2,10},{10... | collective-permute-start | bytes 393224 | tf_op jit(solution)/shard_map/ppermute | solution.py:244
  8.8 5.7 %collective-permute-start.3 = (bf16[128,512]{1,0:T(8,128)(2,1)S(1)}, bf16[128,512]{1,0:T(8,128)(2,1)S(1)}, u32[]{:S(2)}, u32[]{:S(2)}) collective-permute-start(bf16[128,512]{1,0:T(8,128)(2,1)S(1)} %get-tuple-element.31), channel_id=1, source_target_pairs={{0,4},{4,0},{1,5},{5,1},{2,6},{6,2},{3,7},{7,3},{8,12},{12,8},{9,1... | collective-permute-start | bytes 393224 | tf_op jit(solution)/shard_map/ppermute | solution.py:244
  14.6 5.4 %collective-permute-start.8 = (bf16[128,256]{1,0:T(8,128)(2,1)S(1)}, bf16[128,256]{1,0:T(8,128)(2,1)S(1)}, u32[]{:S(2)}, u32[]{:S(2)}) collective-permute-start(bf16[128,256]{1,0:T(8,128)(2,1)S(1)} %get-tuple-element.28), channel_id=1, source_target_pairs={{0,16},{8,24},{16,0},{24,8},{1,17},{9,25},{17,1},{25,9},{2,18},{10... | collective-permute-start | bytes 196616 | tf_op jit(solution)/shard_map/ppermute | solution.py:244
  17.2 5.4 %collective-permute-start.5 = (bf16[128,256]{1,0:T(8,128)(2,1)S(1)}, bf16[128,256]{1,0:T(8,128)(2,1)S(1)}, u32[]{:S(2)}, u32[]{:S(2)}) collective-permute-start(bf16[128,256]{1,0:T(8,128)(2,1)S(1)} %get-tuple-element.26), channel_id=1, source_target_pairs={{0,16},{8,24},{16,0},{24,8},{1,17},{9,25},{17,1},{25,9},{2,18},{10... | collective-permute-start | bytes 196616 | tf_op jit(solution)/shard_map/ppermute | solution.py:244
  20.0 5.1 %collective-permute-start.9 = (bf16[128,256]{1,0:T(8,128)(2,1)S(1)}, bf16[128,256]{1,0:T(8,128)(2,1)S(1)}, u32[]{:S(2)}, u32[]{:S(2)}) collective-permute-start(bf16[128,256]{1,0:T(8,128)(2,1)S(1)} %add_convert_fusion.1.refs_3_), channel_id=1, source_target_pairs={{0,8},{8,0},{16,24},{24,16},{1,9},{9,1},{17,25},{25,17},{2,10},{10... | collective-permute-start | bytes 196616 | tf_op jit(solution)/shard_map/ppermute | solution.py:244
  22.7 4.3 %collective-permute-start.6 = (bf16[128,256]{1,0:T(8,128)(2,1)S(1)}, bf16[128,256]{1,0:T(8,128)(2,1)S(1)}, u32[]{:S(2)}, u32[]{:S(2)}) collective-permute-start(bf16[128,256]{1,0:T(8,128)(2,1)S(1)} %add_convert_fusion.2.refs_0_), channel_id=1, source_target_pairs={{0,8},{8,0},{16,24},{24,16},{1,9},{9,1},{17,25},{25,17},{2,10},{10... | collective-permute-start | bytes 196616 | tf_op jit(solution)/shard_map/ppermute | solution.py:244
  25.2 2.0 %collective-permute-start.10 = (bf16[256,256]{1,0:T(8,128)(2,1)S(1)}, bf16[256,256]{1,0:T(8,128)(2,1)S(1)}, u32[]{:S(2)}, u32[]{:S(2)}) collective-permute-start(bf16[256,256]{1,0:T(8,128)(2,1)S(1)} %pad_maximum_fusion.1), channel_id=1, source_target_pairs={{0,2},{2,0},{1,3},{3,1},{4,6},{6,4},{5,7},{7,5},{8,10},{10,8},{9,1... | collective-permute-start | bytes 393224 | tf_op jit(solution)/shard_map/ppermute | solution.py:244
  27.0 1.4 %collective-permute-start.7 = (bf16[256,256]{1,0:T(8,128)(2,1)S(1)}, bf16[256,256]{1,0:T(8,128)(2,1)S(1)}, u32[]{:S(2)}, u32[]{:S(2)}) collective-permute-start(bf16[256,256]{1,0:T(8,128)(2,1)S(1)} %pad_maximum_fusion), channel_id=1, source_target_pairs={{0,2},{2,0},{1,3},{3,1},{4,6},{6,4},{5,7},{7,5},{8,10},{10,8},{9,1... | collective-permute-start | bytes 393224 | tf_op jit(solution)/shard_map/ppermute | solution.py:244
  36.8 4.6 %collective-permute-start.11 = (bf16[32,512]{1,0:T(8,128)(2,1)S(1)}, bf16[32,512]{1,0:T(8,128)(2,1)S(1)}, u32[]{:S(2)}, u32[]{:S(2)}) collective-permute-start(bf16[32,512]{1,0:T(8,128)(2,1)S(1)} %get-tuple-element.30), channel_id=1, source_target_pairs={{0,4},{1,5},{4,0},{5,1},{2,6},{3,7},{6,2},{7,3},{8,12},{9,13},{12,... | collective-permute-start | bytes 98312 | tf_op jit(solution)/shard_map/ppermute | solution.py:289
  39.5 5.2 %collective-permute-start.13 = (bf16[32,512]{1,0:T(8,128)(2,1)S(1)}, bf16[32,512]{1,0:T(8,128)(2,1)S(1)}, u32[]{:S(2)}, u32[]{:S(2)}) collective-permute-start(bf16[32,512]{1,0:T(8,128)(2,1)S(1)} %get-tuple-element.30), channel_id=1, source_target_pairs={{0,5},{1,4},{4,1},{5,0},{2,7},{3,6},{6,3},{7,2},{8,13},{9,12},{12,... | collective-permute-start | bytes 98312 | tf_op jit(solution)/shard_map/ppermute | solution.py:289
  40.5 4.1 %collective-permute-start.12 = (bf16[32,512]{1,0:T(8,128)(2,1)S(1)}, bf16[32,512]{1,0:T(8,128)(2,1)S(1)}, u32[]{:S(2)}, u32[]{:S(2)}) collective-permute-start(bf16[32,512]{1,0:T(8,128)(2,1)S(1)} %get-tuple-element.29), channel_id=1, source_target_pairs={{0,1},{1,0},{4,5},{5,4},{2,3},{3,2},{6,7},{7,6},{8,9},{9,8},{12,13... | collective-permute-start | bytes 98312 | tf_op jit(solution)/shard_map/ppermute | solution.py:289

commit v8 on v7

--- a/solution.py
+++ b/solution.py
@@ -127,12 +127,13 @@
 
 def root_kernel(most, counts_hbm, *refs):
     pieces = refs[:6]
-    keep_ref, send_ref, grad, left, right, m_left, m_right, counts, sem = refs[6:]
+    keep_ref, send_ref, grad, left, right, m_left, m_right, s_left, s_right, counts, sem = refs[6:]
     counts_copy = pltpu.make_async_copy(counts_hbm, counts, sem)
     counts_copy.start()
     width = grad.shape[0]
     half, quarter = width // 2, width // 4
     rows = keep_ref.shape[0]
+    low, high = slice(0, half), slice(half, width)
     place, column, core = (lax.axis_index(name) for name in ("z", "x", "core"))
     for index in range(2):
         own, other, far = pieces[3 * index : 3 * index + 3]
@@ -140,22 +141,36 @@
         grad[:quarter, columns] = own[...]
         grad[quarter:half, columns] = other[...]
         grad[half:, columns] = far[...]
-    diagonal = lax.broadcasted_iota(jnp.int32, (width, width), 0) == lax.broadcasted_iota(
-        jnp.int32, (width, width), 1
+    diagonal = lax.broadcasted_iota(jnp.int32, (half, half), 0) == lax.broadcasted_iota(
+        jnp.int32, (half, half), 1
     )
 
     def dot(a, b):
         return jnp.dot(a, b, preferred_element_type=F32)
 
-    def factor(moment):
-        return (jnp.where(diagonal, 1.25, 0.0) - 0.25 * moment).astype(BF16)
-
-    def begin(dims):
-        stats = lax.dot_general(grad[...], grad[...], dims, preferred_element_type=F32)
-        stats = stats + jnp.where(diagonal, 0.1, 0.0)
-        scale = 2.5 / jnp.sqrt(jnp.sum(stats * stats, keepdims=True))
+    def fill(ref, start, tiles):
+        upper_left, upper_right, lower_right = (tile.astype(BF16) for tile in tiles)
+        ref[start : start + half, low] = upper_left
+        ref[start : start + half, high] = upper_right
+        ref[start + half : start + width, low] = upper_right.T
+        ref[start + half : start + width, high] = lower_right
+
+    def factor(tiles):
+        upper_left, upper_right, lower_right = tiles
+        five = jnp.where(diagonal, 1.25, 0.0)
+        return five - 0.25 * upper_left, -0.25 * upper_right, five - 0.25 * lower_right
+
+    def begin(dims, upper, lower):
+        tenth = jnp.where(diagonal, 0.1, 0.0)
+        tiles = [
+            lax.dot_general(a, b, dims, preferred_element_type=F32)
+            for a, b in ((upper, upper), (upper, lower), (lower, lower))
+        ]
+        tiles = [tiles[0] + tenth, tiles[1], tiles[2] + tenth]
+        squares = tiles[0] * tiles[0] + 2.0 * (tiles[1] * tiles[1]) + tiles[2] * tiles[2]
+        scale = 2.5 / jnp.sqrt(jnp.sum(squares, keepdims=True))
         first = jnp.sqrt(jnp.sqrt(scale)).astype(BF16).astype(F32)
-        return scale * stats, first
+        return [scale * tile for tile in tiles], first
 
     def spot(flip):
         row = (4 * place + 2 * (column ^ flip) + core) * rows
@@ -166,47 +181,82 @@
     wanted = jnp.where(line < rows, spot(0) + line, spot(1) + line - rows)
     pick = lax.broadcasted_iota(jnp.int32, (2 * rows, width), 1) == wanted
     pick = jnp.where(pick, 1.0, 0.0).astype(BF16)
-    moment, first = begin(COLS_IN_COLS)
-    m_left[...] = moment.astype(BF16)
-    factor_value = factor(moment)
-    left[2 * rows :, :] = factor_value
-    left[: 2 * rows, :] = (first * dot(pick, factor_value)).astype(BF16)
-    moment, first = begin(ROWS_IN_COLS)
-    m_right[...] = moment.astype(BF16)
-    factor_value = factor(moment)
-    right[width:, :] = factor_value
-    right[:width, :] = (first * factor_value.astype(F32)).astype(BF16)
+    picked = 2 * rows
+    tiles, first = begin(COLS_IN_COLS, grad[low, :], grad[high, :])
+    fill(m_left, 0, tiles)
+    fill(left, picked, factor(tiles))
+    left[:picked, :] = (first * dot(pick, left[picked:, :])).astype(BF16)
+    tiles, first = begin(ROWS_IN_COLS, grad[:, low], grad[:, high])
+    fill(m_right, 0, tiles)
+    tiles = [tile.astype(BF16) for tile in factor(tiles)]
+    fill(right, width, tiles)
+    tiles = [(first * tile.astype(F32)).astype(BF16) for tile in tiles]
+    right[half:width, low] = tiles[0]
+    right[half:width, high] = tiles[1]
+    right[:half, low] = tiles[1].T
+    right[:half, high] = tiles[2]
+
+    def square(ref):
+        by_high = dot(ref[...], ref[:, high])
+        return dot(ref[low, :], ref[:, low]), by_high[low], by_high[high]
 
     counts_copy.wait()
-    sides = (
-        (left, m_left, 2 * rows, counts[column, 0]),
-        (right, m_right, width, counts[column, 1]),
-    )
+    count_left, count_right = counts[column, 0], counts[column, 1]
     for index in range(1, most):
-        seconds = []
-        for stacked, _, size, count in sides:
-            if index == 1:
-                factor_value = stacked[size:, :]
-                seconds.append(dot(factor_value, factor_value).astype(BF16))
-            else:
-                product = dot(stacked[...], stacked[size:, :]).astype(BF16)
-                if index > 2:
-                    stacked[:size, :] = jnp.where(index <= count, product[:size], stacked[:size, :])
-                else:
-                    stacked[:size, :] = product[:size]
-                seconds.append(product[size:])
-        fourths = [dot(second, second).astype(BF16) for second in seconds]
-        for (stacked, moment_ref, size, _), fourth in zip(sides, fourths):
-            moment = dot(fourth, moment_ref[...])
+        q_left, q_right = left.at[picked:, :], right.at[width:, :]
+        if index == 1:
+            fill(s_left, 0, square(q_left))
+            fill(s_right, 0, square(q_right))
+        else:
+            by_high = dot(left[...], q_left[:, high])
+            by_low = dot(left[: picked + half, :], q_left[:, low])
+            right_by_high = dot(right[...], q_right[:, high])
+            right_by_low = dot(right[half : width + half, :], q_right[:, low])
+            fill(s_left, 0, (by_low[picked:], by_high[picked : picked + half], by_high[picked + half :]))
+            fill(
+                s_right,
+                0,
+                (right_by_low[half:], right_by_high[width : width + half], right_by_high[width + half :]),
+            )
+
+            def keep_if(ref, value, goes_on):
+                value = value.astype(BF16)
+                return value if index == 2 else jnp.where(goes_on, value, ref)
+
+            left[:picked, low] = keep_if(left[:picked, low], by_low[:picked], index <= count_left)
+            left[:picked, high] = keep_if(left[:picked, high], by_high[:picked], index <= count_left)
+            goes_on = index <= count_right
+            upper_right = keep_if(right[half:width, high], right_by_high[half:width], goes_on)
+            right[half:width, low] = keep_if(right[half:width, low], right_by_low[:half], goes_on)
+            right[half:width, high] = upper_right
+            right[:half, low] = upper_right.T
+            right[:half, high] = keep_if(right[:half, high], right_by_high[:half], goes_on)
+        fourths = square(s_left), square(s_right)
+        fill(s_left, 0, fourths[0])
+        fill(s_right, 0, fourths[1])
+        for fourth, moment_ref, ref, start in (
+            (s_left, m_left, left, picked),
+            (s_right, m_right, right, width),
+        ):
+            by_high = dot(fourth[...], moment_ref[:, high])
+            tiles = (dot(fourth[low, :], moment_ref[:, low]), by_high[low], by_high[high])
             if index < most - 1:
-                moment_ref[...] = moment.astype(BF16)
-            stacked[size:, :] = factor(moment)
-    finals = []
-    for stacked, _, size, count in sides:
-        product = dot(stacked[:size, :], stacked[size:, :]).astype(BF16)
-        finals.append(jnp.where(most <= count, product, stacked[:size, :]))
-    partial_value = dot(finals[0], grad[...]).astype(BF16)
-    update = dot(partial_value, finals[1])
+                fill(moment_ref, 0, tiles)
+            fill(ref, start, factor(tiles))
+    final_left = dot(left[:picked, :], left[picked:, :]).astype(BF16)
+    final_left = jnp.where(most <= count_left, final_left, left[:picked, :])
+    by_high = dot(right[:width, :], right[width:, high])
+    by_low = dot(right[half:width, :], right[width:, low])
+    goes_on = most <= count_right
+    upper_right = jnp.where(goes_on, by_high[half:].astype(BF16), right[half:width, high])
+    right[half:width, low] = jnp.where(goes_on, by_low.astype(BF16), right[half:width, low])
+    right[half:width, high] = upper_right
+    right[:half, low] = upper_right.T
+    right[:half, high] = jnp.where(goes_on, by_high[:half].astype(BF16), right[:half, high])
+    partial_value = dot(final_left, grad[...]).astype(BF16)
+    update = dot(partial_value[:, low], right[half:width, :]) + dot(
+        partial_value[:, high], right[:half, :]
+    )
     keep_ref[...] = update[:rows, :].astype(BF16)
     send_ref[...] = update[rows:, :].astype(BF16)
 
@@ -224,6 +274,8 @@
             square,
             pltpu.VMEM((2 * rows + width, width), BF16),
             pltpu.VMEM((2 * width, width), BF16),
+            square,
+            square,
             square,
             square,
             pltpu.SMEM(counts.shape, jnp.int32),

time: 45.6 us -> 43.8 us (0.961)
  Pallas kernels: 11.8 us -> 9.97 us
    pallas_call x1, Pallas kernels: 8.33 us -> 6.55 us  [root(): pl.pallas_call(functools.partial(root_kernel, most), out_shape=[out, out]...]
where the time goes in v8:
time: 43.8 us; the launch traced here: 43.6 us
  starting transfers between devices  17.3 us (39%)
  waiting for transfers between devices  15.2 us (35%)
  Pallas kernels  9.97 us (23%)
  other arithmetic  0.93 us (2%)
    ppermute x10, waiting for transfers between devices, swap(): lax.ppermute(array, axis, [(i, i ^ mask) for i in range(lax.axis_size(axi...  11.6 us
    ppermute x10, starting transfers between devices, swap(): lax.ppermute(array, axis, [(i, i ^ mask) for i in range(lax.axis_size(axi...  9.09 us
    pallas_call x1, Pallas kernels, root(): pl.pallas_call(functools.partial(root_kernel, most), out_shape=[out, out]...  6.55 us
    ppermute x3, starting transfers between devices, shards(): lax.ppermute(piece, ('x', 'group'), moves)  4.23 us
    ppermute x1, starting transfers between devices, swap_diagonal(): return lax.ppermute(array, ('z', 'x'), moves)  4.02 us
    ppermute x3, waiting for transfers between devices, shards(): lax.ppermute(piece, ('x', 'group'), moves)  3.61 us
    pallas_call x3, Pallas kernels, pixel_sums(): pl.pallas_call(functools.partial(kernel, scale), out_shape=out_shape, in_...  3.36 us
  transfers between devices with their start and end apart: 14, of which 7 were waited for; matrix products, arithmetic and copies ran while one was open for 1% of the time, Pallas kernels for 4%

profile of v8, /device:TPU:0, one launch (start us, length us, event | category | flops | bytes accessed | tf_op | source)
XLA Modules:
  0.0 43.6 jit_solution(13293336783775410941)
XLA Ops:
  0.0 1.5 %shard_map.37 = (bf16[256,512]{1,0:T(8,128)(2,1)S(1)}, bf16[2,512,256]{2,1,0:T(8,128)(2,1)S(1)}, bf16[512,512]{1,0:T(8,128)(2,1)S(1)}) custom-call(bf16[2,512,512]{2,1,0:T(8,128)(2,1)} %patch_hbm.3, bf16[2,512,512]{2,1,0:T(8,128)(2,1)} %cot_hbm.3), custom_call_target="tpu_custom_call" | custom-call | flops 134217728 | bytes 1048576 | tf_op jit(solution)/shard_map/pallas_call | solution.py:80
  1.5 0.5 %collective-permute-start = (bf16[256,512]{1,0:T(8,128)(2,1)S(1)}, bf16[256,512]{1,0:T(8,128)(2,1)S(1)}, u32[]{:S(2)}, u32[]{:S(2)}) collective-permute-start(bf16[256,512]{1,0:T(8,128)(2,1)S(1)} %get-tuple-element.23), channel_id=1, source_target_pairs={{0,2},{2,0},{1,3},{3,1},{4,6},{6,4},{5,7},{7,5},{8,10},{10,8},{9,1... | collective-permute-start | bytes 786440 | tf_op jit(solution)/shard_map/ppermute | solution.py:296
  2.0 1.6 %shard_map.38 = (f32[256,512]{1,0:T(8,128)S(1)}, bf16[256,512]{1,0:T(8,128)(2,1)S(1)}, bf16[2,512,256]{2,1,0:T(8,128)(2,1)S(1)}, bf16[512,512]{1,0:T(8,128)(2,1)S(1)}) custom-call(bf16[2,512,512]{2,1,0:T(8,128)(2,1)} %patch_hbm.3, bf16[2,512,512]{2,1,0:T(8,128)(2,1)} %cot_hbm.3, bf16[2,512,256]{2,1,0:T(8,128)(2,1)S(1)} %get-tuple-element.18.other_patch, ...), custom_call_target="tpu_custom_call" | custom-call | flops 268435456 | bytes 1048576 | tf_op jit(solution)/shard_map/pallas_call | solution.py:80
  3.6 0.1 collective-permute-start.1
  3.7 0.0 collective-permute-done
  3.7 0.1 add_convert_fusion
  3.8 4.0 %collective-permute-start.2 = (bf16[128,512]{1,0:T(8,128)(2,1)S(1)}, bf16[128,512]{1,0:T(8,128)(2,1)S(1)}, u32[]{:S(2)}, u32[]{:S(2)}) collective-permute-start(bf16[128,512]{1,0:T(8,128)(2,1)S(1)} %get-tuple-element.32._), channel_id=1, source_target_pairs={{0,12},{4,8},{8,4},{12,0},{16,28},{20,24},{24,20},{28,16},{1,13},{... | collective-permute-start | bytes 393224 | tf_op jit(solution)/shard_map/ppermute | solution.py:300
  7.8 0.3 shard_map.39
  8.1 0.0 collective-permute-done.1
  8.2 0.1 convert_add_fusion.own
  8.3 0.5 %collective-permute-start.4 = (bf16[128,512]{1,0:T(8,128)(2,1)S(1)}, bf16[128,512]{1,0:T(8,128)(2,1)S(1)}, u32[]{:S(2)}, u32[]{:S(2)}) collective-permute-start(bf16[128,512]{1,0:T(8,128)(2,1)S(1)} %slice.17), channel_id=1, source_target_pairs={{0,8},{8,0},{16,24},{24,16},{1,9},{9,1},{17,25},{25,17},{2,10},{10... | collective-permute-start | bytes 393224 | tf_op jit(solution)/shard_map/ppermute | solution.py:296
  8.8 0.8 %collective-permute-start.3 = (bf16[128,512]{1,0:T(8,128)(2,1)S(1)}, bf16[128,512]{1,0:T(8,128)(2,1)S(1)}, u32[]{:S(2)}, u32[]{:S(2)}) collective-permute-start(bf16[128,512]{1,0:T(8,128)(2,1)S(1)} %get-tuple-element.31), channel_id=1, source_target_pairs={{0,4},{4,0},{1,5},{5,1},{2,6},{6,2},{3,7},{7,3},{8,12},{12,8},{9,1... | collective-permute-start | bytes 393224 | tf_op jit(solution)/shard_map/ppermute | solution.py:296
  9.6 4.9 %collective-permute-done.4.refs_2_ = bf16[128,512]{1,0:T(8,128)(2,1)S(1)} collective-permute-done((bf16[128,512]{1,0:T(8,128)(2,1)S(1)}, bf16[128,512]{1,0:T(8,128)(2,1)S(1)}, u32[]{:S(2)}, u32[]{:S(2)}) %collective-permute-start.4) | collective-permute-done | bytes 131104 | tf_op jit(solution)/shard_map/ppermute | solution.py:296
  14.5 0.0 collective-permute-done.2.refs_0_
  14.5 0.0 collective-permute-done.3.refs_1_
  14.5 0.1 shard_map.40
  14.6 2.7 %collective-permute-start.8 = (bf16[128,256]{1,0:T(8,128)(2,1)S(1)}, bf16[128,256]{1,0:T(8,128)(2,1)S(1)}, u32[]{:S(2)}, u32[]{:S(2)}) collective-permute-start(bf16[128,256]{1,0:T(8,128)(2,1)S(1)} %get-tuple-element.28), channel_id=1, source_target_pairs={{0,16},{8,24},{16,0},{24,8},{1,17},{9,25},{17,1},{25,9},{2,18},{10... | collective-permute-start | bytes 196616 | tf_op jit(solution)/shard_map/ppermute | solution.py:296
  17.2 0.3 collective-permute-start.5
  17.5 2.5 %collective-permute-done.8 = bf16[128,256]{1,0:T(8,128)(2,1)S(1)} collective-permute-done((bf16[128,256]{1,0:T(8,128)(2,1)S(1)}, bf16[128,256]{1,0:T(8,128)(2,1)S(1)}, u32[]{:S(2)}, u32[]{:S(2)}) %collective-permute-start.8) | collective-permute-done | bytes 65568 | tf_op jit(solution)/shard_map/ppermute | solution.py:296
  20.0 2.6 %collective-permute-start.9 = (bf16[128,256]{1,0:T(8,128)(2,1)S(1)}, bf16[128,256]{1,0:T(8,128)(2,1)S(1)}, u32[]{:S(2)}, u32[]{:S(2)}) collective-permute-start(bf16[128,256]{1,0:T(8,128)(2,1)S(1)} %add_convert_fusion.1.refs_3_), channel_id=1, source_target_pairs={{0,8},{8,0},{16,24},{24,16},{1,9},{9,1},{17,25},{25,17},{2,10},{10... | collective-permute-start | bytes 196616 | tf_op jit(solution)/shard_map/ppermute | solution.py:296
  22.7 0.0 collective-permute-done.5
  22.7 1.4 %collective-permute-start.6 = (bf16[128,256]{1,0:T(8,128)(2,1)S(1)}, bf16[128,256]{1,0:T(8,128)(2,1)S(1)}, u32[]{:S(2)}, u32[]{:S(2)}) collective-permute-start(bf16[128,256]{1,0:T(8,128)(2,1)S(1)} %add_convert_fusion.2.refs_0_), channel_id=1, source_target_pairs={{0,8},{8,0},{16,24},{24,16},{1,9},{9,1},{17,25},{25,17},{2,10},{10... | collective-permute-start | bytes 196616 | tf_op jit(solution)/shard_map/ppermute | solution.py:296
  24.1 1.1 %collective-permute-done.9.refs_4_ = bf16[128,256]{1,0:T(8,128)(2,1)S(1)} collective-permute-done((bf16[128,256]{1,0:T(8,128)(2,1)S(1)}, bf16[128,256]{1,0:T(8,128)(2,1)S(1)}, u32[]{:S(2)}, u32[]{:S(2)}) %collective-permute-start.9) | collective-permute-done | bytes 65568 | tf_op jit(solution)/shard_map/ppermute | solution.py:296
  25.2 0.1 collective-permute-start.10
  25.2 1.8 %collective-permute-done.6.refs_1_ = bf16[128,256]{1,0:T(8,128)(2,1)S(1)} collective-permute-done((bf16[128,256]{1,0:T(8,128)(2,1)S(1)}, bf16[128,256]{1,0:T(8,128)(2,1)S(1)}, u32[]{:S(2)}, u32[]{:S(2)}) %collective-permute-start.6) | collective-permute-done | bytes 65568 | tf_op jit(solution)/shard_map/ppermute | solution.py:296
  27.0 0.1 collective-permute-start.7
  27.1 0.0 collective-permute-done.10.refs_5_
  27.1 1.3 %collective-permute-done.7.refs_2_ = bf16[256,256]{1,0:T(8,128)(2,1)S(1)} collective-permute-done((bf16[256,256]{1,0:T(8,128)(2,1)S(1)}, bf16[256,256]{1,0:T(8,128)(2,1)S(1)}, u32[]{:S(2)}, u32[]{:S(2)}) %collective-permute-start.7) | collective-permute-done | bytes 131104 | tf_op jit(solution)/shard_map/ppermute | solution.py:296
  28.5 6.5 %shard_map.41 = (bf16[32,512]{1,0:T(8,128)(2,1)S(1)}, bf16[32,512]{1,0:T(8,128)(2,1)S(1)}) custom-call(s32[2,2]{1,0:T(2,128)} %counts_hbm.1, bf16[128,256]{1,0:T(8,128)(2,1)S(1)} %add_convert_fusion.2.refs_0_, bf16[128,256]{1,0:T(8,128)(2,1)S(1)} %collective-permute-done.6.refs_1_, bf16[256,256]{1,0:T(8,128)(2,1)S(1)} %collective-permute-done.7.refs_2_, ...), custom_call_target="tpu_custom_call" | custom-call | tf_op jit(solution)/shard_map/pallas_call | solution.py:268
  35.0 2.7 %collective-permute-start.11 = (bf16[32,512]{1,0:T(8,128)(2,1)S(1)}, bf16[32,512]{1,0:T(8,128)(2,1)S(1)}, u32[]{:S(2)}, u32[]{:S(2)}) collective-permute-start(bf16[32,512]{1,0:T(8,128)(2,1)S(1)} %get-tuple-element.30), channel_id=1, source_target_pairs={{0,4},{1,5},{4,0},{5,1},{2,6},{3,7},{6,2},{7,3},{8,12},{9,13},{12,... | collective-permute-start | bytes 98312 | tf_op jit(solution)/shard_map/ppermute | solution.py:341
  37.7 1.0 %collective-permute-start.13 = (bf16[32,512]{1,0:T(8,128)(2,1)S(1)}, bf16[32,512]{1,0:T(8,128)(2,1)S(1)}, u32[]{:S(2)}, u32[]{:S(2)}) collective-permute-start(bf16[32,512]{1,0:T(8,128)(2,1)S(1)} %get-tuple-element.30), channel_id=1, source_target_pairs={{0,5},{1,4},{4,1},{5,0},{2,7},{3,6},{6,3},{7,2},{8,13},{9,12},{12,... | collective-permute-start | bytes 98312 | tf_op jit(solution)/shard_map/ppermute | solution.py:341
  38.7 0.5 %collective-permute-start.12 = (bf16[32,512]{1,0:T(8,128)(2,1)S(1)}, bf16[32,512]{1,0:T(8,128)(2,1)S(1)}, u32[]{:S(2)}, u32[]{:S(2)}) collective-permute-start(bf16[32,512]{1,0:T(8,128)(2,1)S(1)} %get-tuple-element.29), channel_id=1, source_target_pairs={{0,1},{1,0},{4,5},{5,4},{2,3},{3,2},{6,7},{7,6},{8,9},{9,8},{12,13... | collective-permute-start | bytes 98312 | tf_op jit(solution)/shard_map/ppermute | solution.py:341
  39.2 0.3 collective-permute-done.11
  39.6 3.3 %collective-permute-done.12 = bf16[32,512]{1,0:T(8,128)(2,1)S(1)} collective-permute-done((bf16[32,512]{1,0:T(8,128)(2,1)S(1)}, bf16[32,512]{1,0:T(8,128)(2,1)S(1)}, u32[]{:S(2)}, u32[]{:S(2)}) %collective-permute-start.12) | collective-permute-done | bytes 32800 | tf_op jit(solution)/shard_map/ppermute | solution.py:341
  42.9 0.0 collective-permute-done.13
  42.9 0.7 %reverse_select_fusion = bf16[2,2,32,512]{3,2,1,0:T(8,128)(2,1)} fusion(bf16[2,2,32,512]{3,2,1,0:T(8,128)(2,1)S(1)} %reverse_select_fusion.1, pred[]{:T(512)S(6)} %eq.6), kind=kLoop, calls=%fused_computation.3 | loop fusion | flops 65536 | bytes 262145 | tf_op jit(solution)/shard_map/jit(_where)/select_n | solution.py:349
  (10 shorter events, 0.1 us)
Async XLA Ops:
  1.5 2.2 %collective-permute-start = (bf16[256,512]{1,0:T(8,128)(2,1)S(1)}, bf16[256,512]{1,0:T(8,128)(2,1)S(1)}, u32[]{:S(2)}, u32[]{:S(2)}) collective-permute-start(bf16[256,512]{1,0:T(8,128)(2,1)S(1)} %get-tuple-element.23), channel_id=1, source_target_pairs={{0,2},{2,0},{1,3},{3,1},{4,6},{6,4},{5,7},{7,5},{8,10},{10,8},{9,1... | collective-permute-start | bytes 786440 | tf_op jit(solution)/shard_map/ppermute | solution.py:296
  3.6 4.6 %collective-permute-start.1 = (bf16[256,512]{1,0:T(8,128)(2,1)S(1)}, bf16[256,512]{1,0:T(8,128)(2,1)S(1)}, u32[]{:S(2)}, u32[]{:S(2)}) collective-permute-start(bf16[256,512]{1,0:T(8,128)(2,1)S(1)} %get-tuple-element.24), channel_id=1, source_target_pairs={{0,2},{2,0},{1,3},{3,1},{4,6},{6,4},{5,7},{7,5},{8,10},{10,8},{9,1... | collective-permute-start | bytes 786440 | tf_op jit(solution)/shard_map/ppermute | solution.py:296
  3.8 10.7 %collective-permute-start.2 = (bf16[128,512]{1,0:T(8,128)(2,1)S(1)}, bf16[128,512]{1,0:T(8,128)(2,1)S(1)}, u32[]{:S(2)}, u32[]{:S(2)}) collective-permute-start(bf16[128,512]{1,0:T(8,128)(2,1)S(1)} %get-tuple-element.32._), channel_id=1, source_target_pairs={{0,12},{4,8},{8,4},{12,0},{16,28},{20,24},{24,20},{28,16},{1,13},{... | collective-permute-start | bytes 393224 | tf_op jit(solution)/shard_map/ppermute | solution.py:300
  8.3 6.2 %collective-permute-start.4 = (bf16[128,512]{1,0:T(8,128)(2,1)S(1)}, bf16[128,512]{1,0:T(8,128)(2,1)S(1)}, u32[]{:S(2)}, u32[]{:S(2)}) collective-permute-start(bf16[128,512]{1,0:T(8,128)(2,1)S(1)} %slice.17), channel_id=1, source_target_pairs={{0,8},{8,0},{16,24},{24,16},{1,9},{9,1},{17,25},{25,17},{2,10},{10... | collective-permute-start | bytes 393224 | tf_op jit(solution)/shard_map/ppermute | solution.py:296
  8.8 5.7 %collective-permute-start.3 = (bf16[128,512]{1,0:T(8,128)(2,1)S(1)}, bf16[128,512]{1,0:T(8,128)(2,1)S(1)}, u32[]{:S(2)}, u32[]{:S(2)}) collective-permute-start(bf16[128,512]{1,0:T(8,128)(2,1)S(1)} %get-tuple-element.31), channel_id=1, source_target_pairs={{0,4},{4,0},{1,5},{5,1},{2,6},{6,2},{3,7},{7,3},{8,12},{12,8},{9,1... | collective-permute-start | bytes 393224 | tf_op jit(solution)/shard_map/ppermute | solution.py:296
  14.6 5.4 %collective-permute-start.8 = (bf16[128,256]{1,0:T(8,128)(2,1)S(1)}, bf16[128,256]{1,0:T(8,128)(2,1)S(1)}, u32[]{:S(2)}, u32[]{:S(2)}) collective-permute-start(bf16[128,256]{1,0:T(8,128)(2,1)S(1)} %get-tuple-element.28), channel_id=1, source_target_pairs={{0,16},{8,24},{16,0},{24,8},{1,17},{9,25},{17,1},{25,9},{2,18},{10... | collective-permute-start | bytes 196616 | tf_op jit(solution)/shard_map/ppermute | solution.py:296
  17.2 5.4 %collective-permute-start.5 = (bf16[128,256]{1,0:T(8,128)(2,1)S(1)}, bf16[128,256]{1,0:T(8,128)(2,1)S(1)}, u32[]{:S(2)}, u32[]{:S(2)}) collective-permute-start(bf16[128,256]{1,0:T(8,128)(2,1)S(1)} %get-tuple-element.26), channel_id=1, source_target_pairs={{0,16},{8,24},{16,0},{24,8},{1,17},{9,25},{17,1},{25,9},{2,18},{10... | collective-permute-start | bytes 196616 | tf_op jit(solution)/shard_map/ppermute | solution.py:296
  20.0 5.1 %collective-permute-start.9 = (bf16[128,256]{1,0:T(8,128)(2,1)S(1)}, bf16[128,256]{1,0:T(8,128)(2,1)S(1)}, u32[]{:S(2)}, u32[]{:S(2)}) collective-permute-start(bf16[128,256]{1,0:T(8,128)(2,1)S(1)} %add_convert_fusion.1.refs_3_), channel_id=1, source_target_pairs={{0,8},{8,0},{16,24},{24,16},{1,9},{9,1},{17,25},{25,17},{2,10},{10... | collective-permute-start | bytes 196616 | tf_op jit(solution)/shard_map/ppermute | solution.py:296
  22.7 4.3 %collective-permute-start.6 = (bf16[128,256]{1,0:T(8,128)(2,1)S(1)}, bf16[128,256]{1,0:T(8,128)(2,1)S(1)}, u32[]{:S(2)}, u32[]{:S(2)}) collective-permute-start(bf16[128,256]{1,0:T(8,128)(2,1)S(1)} %add_convert_fusion.2.refs_0_), channel_id=1, source_target_pairs={{0,8},{8,0},{16,24},{24,16},{1,9},{9,1},{17,25},{25,17},{2,10},{10... | collective-permute-start | bytes 196616 | tf_op jit(solution)/shard_map/ppermute | solution.py:296
  25.2 2.0 %collective-permute-start.10 = (bf16[256,256]{1,0:T(8,128)(2,1)S(1)}, bf16[256,256]{1,0:T(8,128)(2,1)S(1)}, u32[]{:S(2)}, u32[]{:S(2)}) collective-permute-start(bf16[256,256]{1,0:T(8,128)(2,1)S(1)} %pad_maximum_fusion.1), channel_id=1, source_target_pairs={{0,2},{2,0},{1,3},{3,1},{4,6},{6,4},{5,7},{7,5},{8,10},{10,8},{9,1... | collective-permute-start | bytes 393224 | tf_op jit(solution)/shard_map/ppermute | solution.py:296
  27.0 1.4 %collective-permute-start.7 = (bf16[256,256]{1,0:T(8,128)(2,1)S(1)}, bf16[256,256]{1,0:T(8,128)(2,1)S(1)}, u32[]{:S(2)}, u32[]{:S(2)}) collective-permute-start(bf16[256,256]{1,0:T(8,128)(2,1)S(1)} %pad_maximum_fusion), channel_id=1, source_target_pairs={{0,2},{2,0},{1,3},{3,1},{4,6},{6,4},{5,7},{7,5},{8,10},{10,8},{9,1... | collective-permute-start | bytes 393224 | tf_op jit(solution)/shard_map/ppermute | solution.py:296
  35.0 4.6 %collective-permute-start.11 = (bf16[32,512]{1,0:T(8,128)(2,1)S(1)}, bf16[32,512]{1,0:T(8,128)(2,1)S(1)}, u32[]{:S(2)}, u32[]{:S(2)}) collective-permute-start(bf16[32,512]{1,0:T(8,128)(2,1)S(1)} %get-tuple-element.30), channel_id=1, source_target_pairs={{0,4},{1,5},{4,0},{5,1},{2,6},{3,7},{6,2},{7,3},{8,12},{9,13},{12,... | collective-permute-start | bytes 98312 | tf_op jit(solution)/shard_map/ppermute | solution.py:341
  37.7 5.2 %collective-permute-start.13 = (bf16[32,512]{1,0:T(8,128)(2,1)S(1)}, bf16[32,512]{1,0:T(8,128)(2,1)S(1)}, u32[]{:S(2)}, u32[]{:S(2)}) collective-permute-start(bf16[32,512]{1,0:T(8,128)(2,1)S(1)} %get-tuple-element.30), channel_id=1, source_target_pairs={{0,5},{1,4},{4,1},{5,0},{2,7},{3,6},{6,3},{7,2},{8,13},{9,12},{12,... | collective-permute-start | bytes 98312 | tf_op jit(solution)/shard_map/ppermute | solution.py:341
  38.7 4.1 %collective-permute-start.12 = (bf16[32,512]{1,0:T(8,128)(2,1)S(1)}, bf16[32,512]{1,0:T(8,128)(2,1)S(1)}, u32[]{:S(2)}, u32[]{:S(2)}) collective-permute-start(bf16[32,512]{1,0:T(8,128)(2,1)S(1)} %get-tuple-element.29), channel_id=1, source_target_pairs={{0,1},{1,0},{4,5},{5,4},{2,3},{3,2},{6,7},{7,6},{8,9},{9,8},{12,13... | collective-permute-start | bytes 98312 | tf_op jit(solution)/shard_map/ppermute | solution.py:341

commit v9 on v8

--- a/solution.py
+++ b/solution.py
@@ -14,6 +14,7 @@
 HBM = pl.BlockSpec(memory_space=pltpu.HBM)
 ROWS_IN_COLS = (((0,), (0,)), ((), ()))
 COLS_IN_COLS = (((1,), (1,)), ((), ()))
+QUICK = pl.CostEstimate(flops=1, bytes_accessed=1, transcendentals=0)
 
 
 def params(limit):
@@ -84,38 +85,31 @@
         out_specs=[VMEM] * len(out_shape),
         scratch_shapes=[pltpu.SemaphoreType.DMA((5,))] if loads else [],
         compiler_params=params(16),
-        cost_estimate=pl.CostEstimate(
-            flops=2 * len(sums) * pix * half * width,
-            bytes_accessed=4 * pix * width,
-            transcendentals=0,
-        ),
+        cost_estimate=QUICK,
     )(*operands)
 
 
-def collect_kernel(own, *refs):
-    *came, keep_left, keep_right, send_left, send_right = refs
-    half = keep_left.shape[1]
-    for columns, keep, send in (
-        (slice(0, half), keep_left, send_left),
-        (slice(half, 2 * half), keep_right, send_right),
-    ):
-        total = own[: keep.shape[0], columns]
-        for ref in came:
-            total = total + ref[:, columns].astype(F32)
-        keep[...] = total
-        send[...] = total.astype(BF16)
-
-
-def collect(own, *came):
-    rows, width = came[0].shape
-    shape = (rows, width // 2)
+def cut_kernel(columns, dtypes, mine, theirs, *refs):
+    half = mine.shape[1] // 2
+    where = slice(columns * half, (columns + 1) * half)
+    outs = refs[-2:]
+    rows = outs[0].shape[0]
+    for index, out in enumerate(outs):
+        lines = slice(index * rows, (index + 1) * rows)
+        total = mine[lines, where] + theirs[lines, where].astype(F32)
+        out[...] = total.astype(out.dtype)
+
+
+def cut(mine, theirs, columns, dtypes, after=()):
+    rows, width = mine.shape
     return pl.pallas_call(
-        collect_kernel,
-        out_shape=[jax.ShapeDtypeStruct(shape, F32)] * 2 + [jax.ShapeDtypeStruct(shape, BF16)] * 2,
-        in_specs=[VMEM] * (1 + len(came)),
-        out_specs=[VMEM] * 4,
+        functools.partial(cut_kernel, columns, dtypes),
+        out_shape=[jax.ShapeDtypeStruct((rows // 2, width // 2), dtype) for dtype in dtypes],
+        in_specs=[VMEM] * 2 + [pl.BlockSpec(memory_space=pl.ANY)] * len(after),
+        out_specs=[VMEM] * 2,
         compiler_params=params(16),
-    )(own, *came)
+        cost_estimate=QUICK,
+    )(mine, theirs, *after)
 
 
 def add(*values):
@@ -287,7 +281,7 @@
 
 def shards(line, groups, patches, cotangents, newton_counts):
     blocks, pix, width = patches.shape
-    half, quarter = width // 2, width // 4
+    half = width // 2
     rows = half // (2 * line)
     scale = 1.0 / float(pix * 4 * line * width) ** 0.5
     column, group = lax.axis_index("x"), lax.axis_index("group")
@@ -308,22 +302,23 @@
         second_kernel, scale, shape, (F32, BF16), True, patches, cotangents, *loaded
     )
     came_on = swap(given_on, "core")
-    leaving = add(kept, came).astype(BF16)
-    to_diagonal, to_column = leaving[quarter:], leaving[:quarter]
+    to_column, to_diagonal = cut(kept, came, 0, (BF16, BF16))
     from_diagonal = swap_diagonal(to_diagonal)
     from_column = swap(to_column, "x")
     (kept_on,) = pixel_sums(third_kernel, scale, shape, (F32,), False, *loaded, to_diagonal)
-    own = add(kept_on, came_on)
-    from_line = swap(own[quarter:].astype(BF16), "z")
-    left, right, send_left, send_right = collect(own, from_diagonal, from_column, from_line)
+    left, to_line = cut(kept_on, came_on, 0, (F32, BF16))
+    left = add(left, from_diagonal, from_column, swap(to_line, "z"))
+    to_column, to_diagonal = cut(kept, came, 1, (BF16, BF16), (from_diagonal,))
+    right, to_line = cut(kept_on, came_on, 1, (F32, BF16), (to_diagonal,))
+    from_diagonal = swap_diagonal(to_diagonal)
+    right = add(right, from_diagonal, swap(to_column, "x"), swap(to_line, "z"))
     pieces = []
-    for own, send in ((left, send_left), (right, send_right)):
+    for own in (left, right):
         mask = 2
         while mask < line:
-            own = add(own, swap(send, "z", mask))
-            send = own.astype(BF16)
+            own = add(own, swap(own.astype(BF16), "z", mask))
             mask *= 2
-        own = send
+        own = own.astype(BF16)
         other = swap(own, "z")
         pieces += [own, other, swap(jnp.concatenate([own, other], 0), "core")]
     keep, send = root(newton_counts, pieces, rows)

time: 43.8 us -> 43.5 us (level)
  waiting for transfers between devices: 15.2 us -> 9.9 us
  starting transfers between devices: 17.3 us -> 22.4 us
    ppermute x10 -> x12, waiting for transfers between devices: 11.6 us -> 5.96 us  [swap(): lax.ppermute(array, axis, [(i, i ^ mask) for i in range(lax.axis_size(axi...]
    ppermute x1 -> x2, starting transfers between devices: 4.02 us -> 7.53 us  [swap_diagonal(): return lax.ppermute(array, ('z', 'x'), moves)]
    ppermute x10 -> x12, starting transfers between devices: 9.09 us -> 11.3 us  [swap(): lax.ppermute(array, axis, [(i, i ^ mask) for i in range(lax.axis_size(axi...]
    ppermute x3, starting transfers between devices: 4.23 us -> 3.55 us  [shards(): lax.ppermute(piece, ('x', 'group'), moves)]
    ppermute x1 -> x2, waiting for transfers between devices: 0.01 us -> 0.55 us  [swap_diagonal(): return lax.ppermute(array, ('z', 'x'), moves)]
  transfers between devices with their start and end apart: 14 -> 17, of which waited for: 7 -> 10; matrix products, arithmetic and copies ran while one was open for 1% -> 0% of each run, Pallas kernels for 4% -> 5%
where the time goes in v9:
time: 43.5 us; the launch traced here: 43.4 us
  starting transfers between devices  22.4 us (51%)
  Pallas kernels  10 us (23%)
  waiting for transfers between devices  9.9 us (23%)
  other arithmetic  0.9 us (2%)
    ppermute x12, starting transfers between devices, swap(): lax.ppermute(array, axis, [(i, i ^ mask) for i in range(lax.axis_size(axi...  11.3 us
    ppermute x2, starting transfers between devices, swap_diagonal(): return lax.ppermute(array, ('z', 'x'), moves)  7.53 us
    pallas_call x1, Pallas kernels, root(): pl.pallas_call(functools.partial(root_kernel, most), out_shape=[out, out]...  6.55 us
    ppermute x12, waiting for transfers between devices, swap(): lax.ppermute(array, axis, [(i, i ^ mask) for i in range(lax.axis_size(axi...  5.96 us
    ppermute x3, starting transfers between devices, shards(): lax.ppermute(piece, ('x', 'group'), moves)  3.55 us
    ppermute x3, waiting for transfers between devices, shards(): lax.ppermute(piece, ('x', 'group'), moves)  3.4 us
    pallas_call x3, Pallas kernels, pixel_sums(): pl.pallas_call(functools.partial(kernel, scale), out_shape=out_shape, in_...  3.36 us
  transfers between devices with their start and end apart: 17, of which 10 were waited for; matrix products, arithmetic and copies ran while one was open for 0% of the time, Pallas kernels for 5%

profile of v9, /device:TPU:0, one launch (start us, length us, event | category | flops | bytes accessed | tf_op | source)
XLA Modules:
  0.0 43.4 jit_solution(5881673889369315799)
XLA Ops:
  0.0 1.5 %shard_map.37 = (bf16[256,512]{1,0:T(8,128)(2,1)S(1)}, bf16[2,512,256]{2,1,0:T(8,128)(2,1)S(1)}, bf16[512,512]{1,0:T(8,128)(2,1)S(1)}) custom-call(bf16[2,512,512]{2,1,0:T(8,128)(2,1)} %patch_hbm.3, bf16[2,512,512]{2,1,0:T(8,128)(2,1)} %cot_hbm.3), custom_call_target="tpu_custom_call" | custom-call | flops 1 | bytes 1 | tf_op jit(solution)/shard_map/pallas_call | solution.py:81
  1.5 0.5 %collective-permute-start = (bf16[256,512]{1,0:T(8,128)(2,1)S(1)}, bf16[256,512]{1,0:T(8,128)(2,1)S(1)}, u32[]{:S(2)}, u32[]{:S(2)}) collective-permute-start(bf16[256,512]{1,0:T(8,128)(2,1)S(1)} %get-tuple-element.27), channel_id=1, source_target_pairs={{0,2},{2,0},{1,3},{3,1},{4,6},{6,4},{5,7},{7,5},{8,10},{10,8},{9,1... | collective-permute-start | bytes 786440 | tf_op jit(solution)/shard_map/ppermute | solution.py:290
  2.0 1.6 %shard_map.38 = (f32[256,512]{1,0:T(8,128)S(1)}, bf16[256,512]{1,0:T(8,128)(2,1)S(1)}, bf16[2,512,256]{2,1,0:T(8,128)(2,1)S(1)}, bf16[512,512]{1,0:T(8,128)(2,1)S(1)}) custom-call(bf16[2,512,512]{2,1,0:T(8,128)(2,1)} %patch_hbm.3, bf16[2,512,512]{2,1,0:T(8,128)(2,1)} %cot_hbm.3, bf16[2,512,256]{2,1,0:T(8,128)(2,1)S(1)} %get-tuple-element.22.other_patch, ...), custom_call_target="tpu_custom_call" | custom-call | flops 1 | bytes 1 | tf_op jit(solution)/shard_map/pallas_call | solution.py:81
  3.6 0.1 collective-permute-start.1
  3.7 0.0 collective-permute-done.theirs
  3.7 4.0 %collective-permute-start.2 = (bf16[128,256]{1,0:T(8,128)(2,1)S(1)}, bf16[128,256]{1,0:T(8,128)(2,1)S(1)}, u32[]{:S(2)}, u32[]{:S(2)}) collective-permute-start(bf16[128,256]{1,0:T(8,128)(2,1)S(1)} %get-tuple-element.28._), channel_id=1, source_target_pairs={{0,12},{4,8},{8,4},{12,0},{16,28},{20,24},{24,20},{28,16},{1,13},{... | collective-permute-start | bytes 196616 | tf_op jit(solution)/shard_map/ppermute | solution.py:294
  7.8 0.3 shard_map.40.mine
  8.1 0.0 collective-permute-done.1.theirs
  8.1 0.5 %collective-permute-start.4 = (bf16[128,256]{1,0:T(8,128)(2,1)S(1)}, bf16[128,256]{1,0:T(8,128)(2,1)S(1)}, u32[]{:S(2)}, u32[]{:S(2)}) collective-permute-start(bf16[128,256]{1,0:T(8,128)(2,1)S(1)} %get-tuple-element.32), channel_id=1, source_target_pairs={{0,8},{8,0},{16,24},{24,16},{1,9},{9,1},{17,25},{25,17},{2,10},{10... | collective-permute-start | bytes 196616 | tf_op jit(solution)/shard_map/ppermute | solution.py:290
  8.6 0.8 %collective-permute-start.3 = (bf16[128,256]{1,0:T(8,128)(2,1)S(1)}, bf16[128,256]{1,0:T(8,128)(2,1)S(1)}, u32[]{:S(2)}, u32[]{:S(2)}) collective-permute-start(bf16[128,256]{1,0:T(8,128)(2,1)S(1)} %get-tuple-element.31), channel_id=1, source_target_pairs={{0,4},{4,0},{1,5},{5,1},{2,6},{6,2},{3,7},{7,3},{8,12},{12,8},{9,1... | collective-permute-start | bytes 196616 | tf_op jit(solution)/shard_map/ppermute | solution.py:290
  9.5 0.5 %collective-permute-done.2.refs_0_ = bf16[128,256]{1,0:T(8,128)(2,1)S(1)} collective-permute-done((bf16[128,256]{1,0:T(8,128)(2,1)S(1)}, bf16[128,256]{1,0:T(8,128)(2,1)S(1)}, u32[]{:S(2)}, u32[]{:S(2)}) %collective-permute-start.2) | collective-permute-done | bytes 65568 | tf_op jit(solution)/shard_map/ppermute | solution.py:294
  10.1 3.5 %collective-permute-start.8 = (bf16[128,256]{1,0:T(8,128)(2,1)S(1)}, bf16[128,256]{1,0:T(8,128)(2,1)S(1)}, u32[]{:S(2)}, u32[]{:S(2)}) collective-permute-start(bf16[128,256]{1,0:T(8,128)(2,1)S(1)} %get-tuple-element.33.refs_0_), channel_id=1, source_target_pairs={{0,12},{4,8},{8,4},{12,0},{16,28},{20,24},{24,20},{28,16},{1,13},{... | collective-permute-start | bytes 196616 | tf_op jit(solution)/shard_map/ppermute | solution.py:294
  13.6 0.1 collective-permute-start.10
  13.7 0.6 %collective-permute-start.9 = (bf16[128,256]{1,0:T(8,128)(2,1)S(1)}, bf16[128,256]{1,0:T(8,128)(2,1)S(1)}, u32[]{:S(2)}, u32[]{:S(2)}) collective-permute-start(bf16[128,256]{1,0:T(8,128)(2,1)S(1)} %get-tuple-element.35), channel_id=1, source_target_pairs={{0,4},{4,0},{1,5},{5,1},{2,6},{6,2},{3,7},{7,3},{8,12},{12,8},{9,1... | collective-permute-start | bytes 196616 | tf_op jit(solution)/shard_map/ppermute | solution.py:290
  14.3 0.0 collective-permute-done.4
  14.3 0.0 collective-permute-done.3
  14.3 2.7 %collective-permute-start.5 = (bf16[128,256]{1,0:T(8,128)(2,1)S(1)}, bf16[128,256]{1,0:T(8,128)(2,1)S(1)}, u32[]{:S(2)}, u32[]{:S(2)}) collective-permute-start(bf16[128,256]{1,0:T(8,128)(2,1)S(1)} %fusion), channel_id=1, source_target_pairs={{0,16},{8,24},{16,0},{24,8},{1,17},{9,25},{17,1},{25,9},{2,18},{10... | collective-permute-start | bytes 196616 | tf_op jit(solution)/shard_map/ppermute | solution.py:290
  17.0 1.0 %collective-permute-done.10 = bf16[128,256]{1,0:T(8,128)(2,1)S(1)} collective-permute-done((bf16[128,256]{1,0:T(8,128)(2,1)S(1)}, bf16[128,256]{1,0:T(8,128)(2,1)S(1)}, u32[]{:S(2)}, u32[]{:S(2)}) %collective-permute-start.10) | collective-permute-done | bytes 65568 | tf_op jit(solution)/shard_map/ppermute | solution.py:290
  17.9 0.0 collective-permute-done.8
  18.0 0.1 collective-permute-done.9
  18.1 2.7 %collective-permute-start.11 = (bf16[128,256]{1,0:T(8,128)(2,1)S(1)}, bf16[128,256]{1,0:T(8,128)(2,1)S(1)}, u32[]{:S(2)}, u32[]{:S(2)}) collective-permute-start(bf16[128,256]{1,0:T(8,128)(2,1)S(1)} %fusion.1), channel_id=1, source_target_pairs={{0,16},{8,24},{16,0},{24,8},{1,17},{9,25},{17,1},{25,9},{2,18},{10... | collective-permute-start | bytes 196616 | tf_op jit(solution)/shard_map/ppermute | solution.py:290
  20.8 0.8 %collective-permute-done.5 = bf16[128,256]{1,0:T(8,128)(2,1)S(1)} collective-permute-done((bf16[128,256]{1,0:T(8,128)(2,1)S(1)}, bf16[128,256]{1,0:T(8,128)(2,1)S(1)}, u32[]{:S(2)}, u32[]{:S(2)}) %collective-permute-start.5) | collective-permute-done | bytes 65568 | tf_op jit(solution)/shard_map/ppermute | solution.py:290
  21.6 1.1 %collective-permute-start.6 = (bf16[128,256]{1,0:T(8,128)(2,1)S(1)}, bf16[128,256]{1,0:T(8,128)(2,1)S(1)}, u32[]{:S(2)}, u32[]{:S(2)}) collective-permute-start(bf16[128,256]{1,0:T(8,128)(2,1)S(1)} %add_convert_fusion.1.refs_0_), channel_id=1, source_target_pairs={{0,8},{8,0},{16,24},{24,16},{1,9},{9,1},{17,25},{25,17},{2,10},{10... | collective-permute-start | bytes 196616 | tf_op jit(solution)/shard_map/ppermute | solution.py:290
  22.8 0.5 %collective-permute-done.11 = bf16[128,256]{1,0:T(8,128)(2,1)S(1)} collective-permute-done((bf16[128,256]{1,0:T(8,128)(2,1)S(1)}, bf16[128,256]{1,0:T(8,128)(2,1)S(1)}, u32[]{:S(2)}, u32[]{:S(2)}) %collective-permute-start.11) | collective-permute-done | bytes 65568 | tf_op jit(solution)/shard_map/ppermute | solution.py:290
  23.3 2.0 %collective-permute-start.12 = (bf16[128,256]{1,0:T(8,128)(2,1)S(1)}, bf16[128,256]{1,0:T(8,128)(2,1)S(1)}, u32[]{:S(2)}, u32[]{:S(2)}) collective-permute-start(bf16[128,256]{1,0:T(8,128)(2,1)S(1)} %add_convert_fusion.refs_3_), channel_id=1, source_target_pairs={{0,8},{8,0},{16,24},{24,16},{1,9},{9,1},{17,25},{25,17},{2,10},{10... | collective-permute-start | bytes 196616 | tf_op jit(solution)/shard_map/ppermute | solution.py:290
  25.4 0.6 %collective-permute-done.6.refs_1_ = bf16[128,256]{1,0:T(8,128)(2,1)S(1)} collective-permute-done((bf16[128,256]{1,0:T(8,128)(2,1)S(1)}, bf16[128,256]{1,0:T(8,128)(2,1)S(1)}, u32[]{:S(2)}, u32[]{:S(2)}) %collective-permute-start.6) | collective-permute-done | bytes 65568 | tf_op jit(solution)/shard_map/ppermute | solution.py:290
  26.0 0.1 collective-permute-start.7
  26.1 1.6 %collective-permute-done.12.refs_4_ = bf16[128,256]{1,0:T(8,128)(2,1)S(1)} collective-permute-done((bf16[128,256]{1,0:T(8,128)(2,1)S(1)}, bf16[128,256]{1,0:T(8,128)(2,1)S(1)}, u32[]{:S(2)}, u32[]{:S(2)}) %collective-permute-start.12) | collective-permute-done | bytes 65568 | tf_op jit(solution)/shard_map/ppermute | solution.py:290
  27.7 0.1 collective-permute-start.13
  27.8 0.0 collective-permute-done.7.refs_2_
  27.8 1.3 %collective-permute-done.13.refs_5_ = bf16[256,256]{1,0:T(8,128)(2,1)S(1)} collective-permute-done((bf16[256,256]{1,0:T(8,128)(2,1)S(1)}, bf16[256,256]{1,0:T(8,128)(2,1)S(1)}, u32[]{:S(2)}, u32[]{:S(2)}) %collective-permute-start.13) | collective-permute-done | bytes 131104 | tf_op jit(solution)/shard_map/ppermute | solution.py:290
  29.1 6.6 %shard_map.44 = (bf16[32,512]{1,0:T(8,128)(2,1)S(1)}, bf16[32,512]{1,0:T(8,128)(2,1)S(1)}) custom-call(s32[2,2]{1,0:T(2,128)} %counts_hbm.1, bf16[128,256]{1,0:T(8,128)(2,1)S(1)} %add_convert_fusion.1.refs_0_, bf16[128,256]{1,0:T(8,128)(2,1)S(1)} %collective-permute-done.6.refs_1_, bf16[256,256]{1,0:T(8,128)(2,1)S(1)} %collective-permute-done.7.refs_2_, ...), custom_call_target="tpu_custom_call" | custom-call | tf_op jit(solution)/shard_map/pallas_call | solution.py:262
  35.7 0.8 %collective-permute-start.14 = (bf16[32,512]{1,0:T(8,128)(2,1)S(1)}, bf16[32,512]{1,0:T(8,128)(2,1)S(1)}, u32[]{:S(2)}, u32[]{:S(2)}) collective-permute-start(bf16[32,512]{1,0:T(8,128)(2,1)S(1)} %get-tuple-element.38), channel_id=1, source_target_pairs={{0,4},{1,5},{4,0},{5,1},{2,6},{3,7},{6,2},{7,3},{8,12},{9,13},{12,... | collective-permute-start | bytes 98312 | tf_op jit(solution)/shard_map/ppermute | solution.py:336
  36.4 2.3 %collective-permute-start.16 = (bf16[32,512]{1,0:T(8,128)(2,1)S(1)}, bf16[32,512]{1,0:T(8,128)(2,1)S(1)}, u32[]{:S(2)}, u32[]{:S(2)}) collective-permute-start(bf16[32,512]{1,0:T(8,128)(2,1)S(1)} %get-tuple-element.38), channel_id=1, source_target_pairs={{0,5},{1,4},{4,1},{5,0},{2,7},{3,6},{6,3},{7,2},{8,13},{9,12},{12,... | collective-permute-start | bytes 98312 | tf_op jit(solution)/shard_map/ppermute | solution.py:336
  38.7 0.5 %collective-permute-start.15 = (bf16[32,512]{1,0:T(8,128)(2,1)S(1)}, bf16[32,512]{1,0:T(8,128)(2,1)S(1)}, u32[]{:S(2)}, u32[]{:S(2)}) collective-permute-start(bf16[32,512]{1,0:T(8,128)(2,1)S(1)} %get-tuple-element.37), channel_id=1, source_target_pairs={{0,1},{1,0},{4,5},{5,4},{2,3},{3,2},{6,7},{7,6},{8,9},{9,8},{12,13... | collective-permute-start | bytes 98312 | tf_op jit(solution)/shard_map/ppermute | solution.py:336
  39.2 0.4 collective-permute-done.14
  39.6 3.0 %collective-permute-done.15 = bf16[32,512]{1,0:T(8,128)(2,1)S(1)} collective-permute-done((bf16[32,512]{1,0:T(8,128)(2,1)S(1)}, bf16[32,512]{1,0:T(8,128)(2,1)S(1)}, u32[]{:S(2)}, u32[]{:S(2)}) %collective-permute-start.15) | collective-permute-done | bytes 32800 | tf_op jit(solution)/shard_map/ppermute | solution.py:336
  42.6 0.0 collective-permute-done.16
  42.7 0.7 %reverse_select_fusion = bf16[2,2,32,512]{3,2,1,0:T(8,128)(2,1)} fusion(bf16[2,2,32,512]{3,2,1,0:T(8,128)(2,1)S(1)} %reverse_select_fusion.1, pred[]{:T(512)S(6)} %eq.6), kind=kLoop, calls=%fused_computation | loop fusion | flops 65536 | bytes 262145 | tf_op jit(solution)/shard_map/jit(_where)/select_n | solution.py:344
  (14 shorter events, 0.3 us)
Async XLA Ops:
  1.5 2.2 %collective-permute-start = (bf16[256,512]{1,0:T(8,128)(2,1)S(1)}, bf16[256,512]{1,0:T(8,128)(2,1)S(1)}, u32[]{:S(2)}, u32[]{:S(2)}) collective-permute-start(bf16[256,512]{1,0:T(8,128)(2,1)S(1)} %get-tuple-element.27), channel_id=1, source_target_pairs={{0,2},{2,0},{1,3},{3,1},{4,6},{6,4},{5,7},{7,5},{8,10},{10,8},{9,1... | collective-permute-start | bytes 786440 | tf_op jit(solution)/shard_map/ppermute | solution.py:290
  3.6 4.5 %collective-permute-start.1 = (bf16[256,512]{1,0:T(8,128)(2,1)S(1)}, bf16[256,512]{1,0:T(8,128)(2,1)S(1)}, u32[]{:S(2)}, u32[]{:S(2)}) collective-permute-start(bf16[256,512]{1,0:T(8,128)(2,1)S(1)} %get-tuple-element.29), channel_id=1, source_target_pairs={{0,2},{2,0},{1,3},{3,1},{4,6},{6,4},{5,7},{7,5},{8,10},{10,8},{9,1... | collective-permute-start | bytes 786440 | tf_op jit(solution)/shard_map/ppermute | solution.py:290
  3.7 6.3 %collective-permute-start.2 = (bf16[128,256]{1,0:T(8,128)(2,1)S(1)}, bf16[128,256]{1,0:T(8,128)(2,1)S(1)}, u32[]{:S(2)}, u32[]{:S(2)}) collective-permute-start(bf16[128,256]{1,0:T(8,128)(2,1)S(1)} %get-tuple-element.28._), channel_id=1, source_target_pairs={{0,12},{4,8},{8,4},{12,0},{16,28},{20,24},{24,20},{28,16},{1,13},{... | collective-permute-start | bytes 196616 | tf_op jit(solution)/shard_map/ppermute | solution.py:294
  8.1 6.1 %collective-permute-start.4 = (bf16[128,256]{1,0:T(8,128)(2,1)S(1)}, bf16[128,256]{1,0:T(8,128)(2,1)S(1)}, u32[]{:S(2)}, u32[]{:S(2)}) collective-permute-start(bf16[128,256]{1,0:T(8,128)(2,1)S(1)} %get-tuple-element.32), channel_id=1, source_target_pairs={{0,8},{8,0},{16,24},{24,16},{1,9},{9,1},{17,25},{25,17},{2,10},{10... | collective-permute-start | bytes 196616 | tf_op jit(solution)/shard_map/ppermute | solution.py:290
  8.6 5.6 %collective-permute-start.3 = (bf16[128,256]{1,0:T(8,128)(2,1)S(1)}, bf16[128,256]{1,0:T(8,128)(2,1)S(1)}, u32[]{:S(2)}, u32[]{:S(2)}) collective-permute-start(bf16[128,256]{1,0:T(8,128)(2,1)S(1)} %get-tuple-element.31), channel_id=1, source_target_pairs={{0,4},{4,0},{1,5},{5,1},{2,6},{6,2},{3,7},{7,3},{8,12},{12,8},{9,1... | collective-permute-start | bytes 196616 | tf_op jit(solution)/shard_map/ppermute | solution.py:290
  10.1 7.9 %collective-permute-start.8 = (bf16[128,256]{1,0:T(8,128)(2,1)S(1)}, bf16[128,256]{1,0:T(8,128)(2,1)S(1)}, u32[]{:S(2)}, u32[]{:S(2)}) collective-permute-start(bf16[128,256]{1,0:T(8,128)(2,1)S(1)} %get-tuple-element.33.refs_0_), channel_id=1, source_target_pairs={{0,12},{4,8},{8,4},{12,0},{16,28},{20,24},{24,20},{28,16},{1,13},{... | collective-permute-start | bytes 196616 | tf_op jit(solution)/shard_map/ppermute | solution.py:294
  13.6 4.3 %collective-permute-start.10 = (bf16[128,256]{1,0:T(8,128)(2,1)S(1)}, bf16[128,256]{1,0:T(8,128)(2,1)S(1)}, u32[]{:S(2)}, u32[]{:S(2)}) collective-permute-start(bf16[128,256]{1,0:T(8,128)(2,1)S(1)} %get-tuple-element.36), channel_id=1, source_target_pairs={{0,8},{8,0},{16,24},{24,16},{1,9},{9,1},{17,25},{25,17},{2,10},{10... | collective-permute-start | bytes 196616 | tf_op jit(solution)/shard_map/ppermute | solution.py:290
  13.7 4.3 %collective-permute-start.9 = (bf16[128,256]{1,0:T(8,128)(2,1)S(1)}, bf16[128,256]{1,0:T(8,128)(2,1)S(1)}, u32[]{:S(2)}, u32[]{:S(2)}) collective-permute-start(bf16[128,256]{1,0:T(8,128)(2,1)S(1)} %get-tuple-element.35), channel_id=1, source_target_pairs={{0,4},{4,0},{1,5},{5,1},{2,6},{6,2},{3,7},{7,3},{8,12},{12,8},{9,1... | collective-permute-start | bytes 196616 | tf_op jit(solution)/shard_map/ppermute | solution.py:290
  14.3 7.3 %collective-permute-start.5 = (bf16[128,256]{1,0:T(8,128)(2,1)S(1)}, bf16[128,256]{1,0:T(8,128)(2,1)S(1)}, u32[]{:S(2)}, u32[]{:S(2)}) collective-permute-start(bf16[128,256]{1,0:T(8,128)(2,1)S(1)} %fusion), channel_id=1, source_target_pairs={{0,16},{8,24},{16,0},{24,8},{1,17},{9,25},{17,1},{25,9},{2,18},{10... | collective-permute-start | bytes 196616 | tf_op jit(solution)/shard_map/ppermute | solution.py:290
  18.1 5.2 %collective-permute-start.11 = (bf16[128,256]{1,0:T(8,128)(2,1)S(1)}, bf16[128,256]{1,0:T(8,128)(2,1)S(1)}, u32[]{:S(2)}, u32[]{:S(2)}) collective-permute-start(bf16[128,256]{1,0:T(8,128)(2,1)S(1)} %fusion.1), channel_id=1, source_target_pairs={{0,16},{8,24},{16,0},{24,8},{1,17},{9,25},{17,1},{25,9},{2,18},{10... | collective-permute-start | bytes 196616 | tf_op jit(solution)/shard_map/ppermute | solution.py:290
  21.6 4.3 %collective-permute-start.6 = (bf16[128,256]{1,0:T(8,128)(2,1)S(1)}, bf16[128,256]{1,0:T(8,128)(2,1)S(1)}, u32[]{:S(2)}, u32[]{:S(2)}) collective-permute-start(bf16[128,256]{1,0:T(8,128)(2,1)S(1)} %add_convert_fusion.1.refs_0_), channel_id=1, source_target_pairs={{0,8},{8,0},{16,24},{24,16},{1,9},{9,1},{17,25},{25,17},{2,10},{10... | collective-permute-start | bytes 196616 | tf_op jit(solution)/shard_map/ppermute | solution.py:290
  23.3 4.3 %collective-permute-start.12 = (bf16[128,256]{1,0:T(8,128)(2,1)S(1)}, bf16[128,256]{1,0:T(8,128)(2,1)S(1)}, u32[]{:S(2)}, u32[]{:S(2)}) collective-permute-start(bf16[128,256]{1,0:T(8,128)(2,1)S(1)} %add_convert_fusion.refs_3_), channel_id=1, source_target_pairs={{0,8},{8,0},{16,24},{24,16},{1,9},{9,1},{17,25},{25,17},{2,10},{10... | collective-permute-start | bytes 196616 | tf_op jit(solution)/shard_map/ppermute | solution.py:290
  26.0 1.8 %collective-permute-start.7 = (bf16[256,256]{1,0:T(8,128)(2,1)S(1)}, bf16[256,256]{1,0:T(8,128)(2,1)S(1)}, u32[]{:S(2)}, u32[]{:S(2)}) collective-permute-start(bf16[256,256]{1,0:T(8,128)(2,1)S(1)} %pad_maximum_fusion), channel_id=1, source_target_pairs={{0,2},{2,0},{1,3},{3,1},{4,6},{6,4},{5,7},{7,5},{8,10},{10,8},{9,1... | collective-permute-start | bytes 393224 | tf_op jit(solution)/shard_map/ppermute | solution.py:290
  27.7 1.4 %collective-permute-start.13 = (bf16[256,256]{1,0:T(8,128)(2,1)S(1)}, bf16[256,256]{1,0:T(8,128)(2,1)S(1)}, u32[]{:S(2)}, u32[]{:S(2)}) collective-permute-start(bf16[256,256]{1,0:T(8,128)(2,1)S(1)} %pad_maximum_fusion.1), channel_id=1, source_target_pairs={{0,2},{2,0},{1,3},{3,1},{4,6},{6,4},{5,7},{7,5},{8,10},{10,8},{9,1... | collective-permute-start | bytes 393224 | tf_op jit(solution)/shard_map/ppermute | solution.py:290
  35.7 4.0 %collective-permute-start.14 = (bf16[32,512]{1,0:T(8,128)(2,1)S(1)}, bf16[32,512]{1,0:T(8,128)(2,1)S(1)}, u32[]{:S(2)}, u32[]{:S(2)}) collective-permute-start(bf16[32,512]{1,0:T(8,128)(2,1)S(1)} %get-tuple-element.38), channel_id=1, source_target_pairs={{0,4},{1,5},{4,0},{5,1},{2,6},{3,7},{6,2},{7,3},{8,12},{9,13},{12,... | collective-permute-start | bytes 98312 | tf_op jit(solution)/shard_map/ppermute | solution.py:336
  36.4 6.2 %collective-permute-start.16 = (bf16[32,512]{1,0:T(8,128)(2,1)S(1)}, bf16[32,512]{1,0:T(8,128)(2,1)S(1)}, u32[]{:S(2)}, u32[]{:S(2)}) collective-permute-start(bf16[32,512]{1,0:T(8,128)(2,1)S(1)} %get-tuple-element.38), channel_id=1, source_target_pairs={{0,5},{1,4},{4,1},{5,0},{2,7},{3,6},{6,3},{7,2},{8,13},{9,12},{12,... | collective-permute-start | bytes 98312 | tf_op jit(solution)/shard_map/ppermute | solution.py:336
  38.7 3.9 %collective-permute-start.15 = (bf16[32,512]{1,0:T(8,128)(2,1)S(1)}, bf16[32,512]{1,0:T(8,128)(2,1)S(1)}, u32[]{:S(2)}, u32[]{:S(2)}) collective-permute-start(bf16[32,512]{1,0:T(8,128)(2,1)S(1)} %get-tuple-element.37), channel_id=1, source_target_pairs={{0,1},{1,0},{4,5},{5,4},{2,3},{3,2},{6,7},{7,6},{8,9},{9,8},{12,13... | collective-permute-start | bytes 98312 | tf_op jit(solution)/shard_map/ppermute | solution.py:336

commit v10 on v8

--- a/solution.py
+++ b/solution.py
@@ -92,32 +92,6 @@
     )(*operands)
 
 
-def collect_kernel(own, *refs):
-    *came, keep_left, keep_right, send_left, send_right = refs
-    half = keep_left.shape[1]
-    for columns, keep, send in (
-        (slice(0, half), keep_left, send_left),
-        (slice(half, 2 * half), keep_right, send_right),
-    ):
-        total = own[: keep.shape[0], columns]
-        for ref in came:
-            total = total + ref[:, columns].astype(F32)
-        keep[...] = total
-        send[...] = total.astype(BF16)
-
-
-def collect(own, *came):
-    rows, width = came[0].shape
-    shape = (rows, width // 2)
-    return pl.pallas_call(
-        collect_kernel,
-        out_shape=[jax.ShapeDtypeStruct(shape, F32)] * 2 + [jax.ShapeDtypeStruct(shape, BF16)] * 2,
-        in_specs=[VMEM] * (1 + len(came)),
-        out_specs=[VMEM] * 4,
-        compiler_params=params(16),
-    )(own, *came)
-
-
 def add(*values):
     total = values[0]
     for value in values[1:]:
@@ -125,9 +99,8 @@
     return total
 
 
-def root_kernel(most, counts_hbm, *refs):
-    pieces = refs[:6]
-    keep_ref, send_ref, grad, left, right, m_left, m_right, s_left, s_right, counts, sem = refs[6:]
+def root_kernel(most, counts_hbm, near, far, keep_ref, send_ref, *refs):
+    grad, left, right, m_left, m_right, s_left, s_right, counts, sem = refs
     counts_copy = pltpu.make_async_copy(counts_hbm, counts, sem)
     counts_copy.start()
     width = grad.shape[0]
@@ -135,12 +108,8 @@
     rows = keep_ref.shape[0]
     low, high = slice(0, half), slice(half, width)
     place, column, core = (lax.axis_index(name) for name in ("z", "x", "core"))
-    for index in range(2):
-        own, other, far = pieces[3 * index : 3 * index + 3]
-        columns = slice(half * index, half * (index + 1))
-        grad[:quarter, columns] = own[...]
-        grad[quarter:half, columns] = other[...]
-        grad[half:, columns] = far[...]
+    grad[low, :] = near[...]
+    grad[high, :] = far[...]
     diagonal = lax.broadcasted_iota(jnp.int32, (half, half), 0) == lax.broadcasted_iota(
         jnp.int32, (half, half), 1
     )
@@ -182,78 +151,93 @@
     pick = lax.broadcasted_iota(jnp.int32, (2 * rows, width), 1) == wanted
     pick = jnp.where(pick, 1.0, 0.0).astype(BF16)
     picked = 2 * rows
-    tiles, first = begin(COLS_IN_COLS, grad[low, :], grad[high, :])
-    fill(m_left, 0, tiles)
-    fill(left, picked, factor(tiles))
-    left[:picked, :] = (first * dot(pick, left[picked:, :])).astype(BF16)
-    tiles, first = begin(ROWS_IN_COLS, grad[:, low], grad[:, high])
-    fill(m_right, 0, tiles)
-    tiles = [tile.astype(BF16) for tile in factor(tiles)]
-    fill(right, width, tiles)
-    tiles = [(first * tile.astype(F32)).astype(BF16) for tile in tiles]
-    right[half:width, low] = tiles[0]
-    right[half:width, high] = tiles[1]
-    right[:half, low] = tiles[1].T
-    right[:half, high] = tiles[2]
+    counts_copy.wait()
+    count_left, count_right = counts[column, 0], counts[column, 1]
 
     def square(ref):
         by_high = dot(ref[...], ref[:, high])
         return dot(ref[low, :], ref[:, low]), by_high[low], by_high[high]
 
-    counts_copy.wait()
-    count_left, count_right = counts[column, 0], counts[column, 1]
-    for index in range(1, most):
-        q_left, q_right = left.at[picked:, :], right.at[width:, :]
-        if index == 1:
-            fill(s_left, 0, square(q_left))
-            fill(s_right, 0, square(q_right))
-        else:
-            by_high = dot(left[...], q_left[:, high])
-            by_low = dot(left[: picked + half, :], q_left[:, low])
-            right_by_high = dot(right[...], q_right[:, high])
-            right_by_low = dot(right[half : width + half, :], q_right[:, low])
-            fill(s_left, 0, (by_low[picked:], by_high[picked : picked + half], by_high[picked + half :]))
-            fill(
-                s_right,
-                0,
-                (right_by_low[half:], right_by_high[width : width + half], right_by_high[width + half :]),
-            )
-
-            def keep_if(ref, value, goes_on):
-                value = value.astype(BF16)
-                return value if index == 2 else jnp.where(goes_on, value, ref)
-
-            left[:picked, low] = keep_if(left[:picked, low], by_low[:picked], index <= count_left)
-            left[:picked, high] = keep_if(left[:picked, high], by_high[:picked], index <= count_left)
-            goes_on = index <= count_right
-            upper_right = keep_if(right[half:width, high], right_by_high[half:width], goes_on)
-            right[half:width, low] = keep_if(right[half:width, low], right_by_low[:half], goes_on)
+    def keep_if(old, value, goes_on):
+        return jnp.where(goes_on, value.astype(BF16), old)
+
+    def end_sweep(index, second, moment_ref, ref, start):
+        fill(second, 0, square(second))
+        yield
+        by_high = dot(second[...], moment_ref[:, high])
+        tiles = (dot(second[low, :], moment_ref[:, low]), by_high[low], by_high[high])
+        if index < most - 1:
+            fill(moment_ref, 0, tiles)
+        fill(ref, start, factor(tiles))
+        yield
+
+    def left_steps():
+        tiles, first = begin(COLS_IN_COLS, grad[low, :], grad[high, :])
+        fill(m_left, 0, tiles)
+        fill(left, picked, factor(tiles))
+        left[:picked, :] = (first * dot(pick, left[picked:, :])).astype(BF16)
+        yield
+        factor_ref = left.at[picked:, :]
+        for index in range(1, most):
+            if index == 1:
+                fill(s_left, 0, square(factor_ref))
+            else:
+                goes_on = index <= count_left
+                by_high = dot(left[...], factor_ref[:, high])
+                by_low = dot(left[: picked + half, :], factor_ref[:, low])
+                second = by_high[picked:]
+                fill(s_left, 0, (by_low[picked:], second[low], second[high]))
+                left[:picked, low] = keep_if(left[:picked, low], by_low[:picked], goes_on)
+                left[:picked, high] = keep_if(left[:picked, high], by_high[:picked], goes_on)
+            yield
+            yield from end_sweep(index, s_left, m_left, left, picked)
+        product = dot(left[:picked, :], factor_ref[...])
+        left[:picked, :] = keep_if(left[:picked, :], product, most <= count_left)
+        yield
+        left[:picked, :] = dot(left[:picked, :], grad[...]).astype(BF16)
+        yield
+
+    def right_steps():
+        def keep_x(by_low, by_high, goes_on):
+            upper_right = keep_if(right[half:width, high], by_high[high], goes_on)
+            right[half:width, low] = keep_if(right[half:width, low], by_low, goes_on)
             right[half:width, high] = upper_right
             right[:half, low] = upper_right.T
-            right[:half, high] = keep_if(right[:half, high], right_by_high[:half], goes_on)
-        fourths = square(s_left), square(s_right)
-        fill(s_left, 0, fourths[0])
-        fill(s_right, 0, fourths[1])
-        for fourth, moment_ref, ref, start in (
-            (s_left, m_left, left, picked),
-            (s_right, m_right, right, width),
-        ):
-            by_high = dot(fourth[...], moment_ref[:, high])
-            tiles = (dot(fourth[low, :], moment_ref[:, low]), by_high[low], by_high[high])
-            if index < most - 1:
-                fill(moment_ref, 0, tiles)
-            fill(ref, start, factor(tiles))
-    final_left = dot(left[:picked, :], left[picked:, :]).astype(BF16)
-    final_left = jnp.where(most <= count_left, final_left, left[:picked, :])
-    by_high = dot(right[:width, :], right[width:, high])
-    by_low = dot(right[half:width, :], right[width:, low])
-    goes_on = most <= count_right
-    upper_right = jnp.where(goes_on, by_high[half:].astype(BF16), right[half:width, high])
-    right[half:width, low] = jnp.where(goes_on, by_low.astype(BF16), right[half:width, low])
-    right[half:width, high] = upper_right
-    right[:half, low] = upper_right.T
-    right[:half, high] = jnp.where(goes_on, by_high[:half].astype(BF16), right[:half, high])
-    partial_value = dot(final_left, grad[...]).astype(BF16)
+            right[:half, high] = keep_if(right[:half, high], by_high[low], goes_on)
+
+        tiles, first = begin(ROWS_IN_COLS, grad[:, low], grad[:, high])
+        fill(m_right, 0, tiles)
+        tiles = [tile.astype(BF16) for tile in factor(tiles)]
+        fill(right, width, tiles)
+        tiles = [(first * tile.astype(F32)).astype(BF16) for tile in tiles]
+        right[half:width, low] = tiles[0]
+        right[half:width, high] = tiles[1]
+        right[:half, low] = tiles[1].T
+        right[:half, high] = tiles[2]
+        yield
+        factor_ref = right.at[width:, :]
+        for index in range(1, most):
+            if index == 1:
+                fill(s_right, 0, square(factor_ref))
+            else:
+                by_high = dot(right[...], factor_ref[:, high])
+                by_low = dot(right[half : width + half, :], factor_ref[:, low])
+                second = by_high[width:]
+                fill(s_right, 0, (by_low[half:], second[low], second[high]))
+                keep_x(by_low[:half], by_high[:width], index <= count_right)
+            yield
+            yield from end_sweep(index, s_right, m_right, right, width)
+        by_high = dot(right[:width, :], factor_ref[:, high])
+        keep_x(dot(right[half:width, :], factor_ref[:, low]), by_high, most <= count_right)
+        yield
+
+    lefts, rights = left_steps(), right_steps()
+    next(lefts)
+    going = True
+    while going:
+        going = next(lefts, True) is None
+        going = (next(rights, True) is None) or going
+    partial_value = left[:picked, :]
     update = dot(partial_value[:, low], right[half:width, :]) + dot(
         partial_value[:, high], right[:half, :]
     )
@@ -261,14 +245,14 @@
     send_ref[...] = update[rows:, :].astype(BF16)
 
 
-def root(counts, pieces, rows, most=4):
-    width = 4 * pieces[0].shape[0]
+def root(counts, near, far, rows, most=4):
+    width = near.shape[1]
     square = pltpu.VMEM((width, width), BF16)
     out = jax.ShapeDtypeStruct((rows, width), BF16)
     return pl.pallas_call(
         functools.partial(root_kernel, most),
         out_shape=[out, out],
-        in_specs=[HBM] + [VMEM] * 6,
+        in_specs=[HBM] + [VMEM] * 2,
         out_specs=[VMEM] * 2,
         scratch_shapes=[
             square,
@@ -282,7 +266,7 @@
             pltpu.SemaphoreType.DMA(()),
         ],
         compiler_params=params(40),
-    )(pltpu.with_memory_space_constraint(counts, pltpu.HBM), *pieces)
+    )(pltpu.with_memory_space_constraint(counts, pltpu.HBM), near, far)
 
 
 def shards(line, groups, patches, cotangents, newton_counts):
@@ -315,18 +299,14 @@
     (kept_on,) = pixel_sums(third_kernel, scale, shape, (F32,), False, *loaded, to_diagonal)
     own = add(kept_on, came_on)
     from_line = swap(own[quarter:].astype(BF16), "z")
-    left, right, send_left, send_right = collect(own, from_diagonal, from_column, from_line)
-    pieces = []
-    for own, send in ((left, send_left), (right, send_right)):
-        mask = 2
-        while mask < line:
-            own = add(own, swap(send, "z", mask))
-            send = own.astype(BF16)
-            mask *= 2
-        own = send
-        other = swap(own, "z")
-        pieces += [own, other, swap(jnp.concatenate([own, other], 0), "core")]
-    keep, send = root(newton_counts, pieces, rows)
+    own = add(own[:quarter], from_diagonal, from_column, from_line)
+    mask = 2
+    while mask < line:
+        own = add(own, swap(own.astype(BF16), "z", mask))
+        mask *= 2
+    own = own.astype(BF16)
+    near = jnp.concatenate([own, swap(own, "z")], 0)
+    keep, send = root(newton_counts, near, swap(near, "core"), rows)
 
     found = []
     for turn in range(groups):

time: 43.8 us -> 44.8 us (1.023)
  waiting for transfers between devices: 15.2 us -> 20 us
  starting transfers between devices: 17.3 us -> 13 us
    ppermute x10 -> x7, waiting for transfers between devices: 11.6 us -> 16.5 us  [swap(): lax.ppermute(array, axis, [(i, i ^ mask) for i in range(lax.axis_size(axi...]
    ppermute x10 -> x7, starting transfers between devices: 9.09 us -> 5.48 us  [swap(): lax.ppermute(array, axis, [(i, i ^ mask) for i in range(lax.axis_size(axi...]
    ppermute x3, starting transfers between devices: 4.23 us -> 3.55 us  [shards(): lax.ppermute(piece, ('x', 'group'), moves)]
  transfers between devices with their start and end apart: 14 -> 11, of which waited for: 7 -> 6; matrix products, arithmetic and copies ran while one was open for 1% -> 0% of each run, Pallas kernels for 4% -> 4%
where the time goes in v10:
time: 44.8 us; the launch traced here: 44.6 us
  waiting for transfers between devices  20 us (45%)
  starting transfers between devices  13 us (29%)
  Pallas kernels  10.3 us (23%)
  other arithmetic  1.06 us (2%)
    ppermute x7, waiting for transfers between devices, swap(): lax.ppermute(array, axis, [(i, i ^ mask) for i in range(lax.axis_size(axi...  16.5 us
    pallas_call x1, Pallas kernels, root(): pl.pallas_call(functools.partial(root_kernel, most), out_shape=[out, out]...  6.98 us
    ppermute x7, starting transfers between devices, swap(): lax.ppermute(array, axis, [(i, i ^ mask) for i in range(lax.axis_size(axi...  5.48 us
    ppermute x1, starting transfers between devices, swap_diagonal(): return lax.ppermute(array, ('z', 'x'), moves)  4.02 us
    ppermute x3, starting transfers between devices, shards(): lax.ppermute(piece, ('x', 'group'), moves)  3.55 us
    ppermute x3, waiting for transfers between devices, shards(): lax.ppermute(piece, ('x', 'group'), moves)  3.54 us
    pallas_call x3, Pallas kernels, pixel_sums(): pl.pallas_call(functools.partial(kernel, scale), out_shape=out_shape, in_...  3.36 us
  transfers between devices with their start and end apart: 11, of which 6 were waited for; matrix products, arithmetic and copies ran while one was open for 0% of the time, Pallas kernels for 4%

profile of v10, /device:TPU:0, one launch (start us, length us, event | category | flops | bytes accessed | tf_op | source)
XLA Modules:
  0.0 44.6 jit_solution(10183701886516703000)
XLA Ops:
  0.0 1.5 %shard_map.37 = (bf16[256,512]{1,0:T(8,128)(2,1)S(1)}, bf16[2,512,256]{2,1,0:T(8,128)(2,1)S(1)}, bf16[512,512]{1,0:T(8,128)(2,1)S(1)}) custom-call(bf16[2,512,512]{2,1,0:T(8,128)(2,1)} %patch_hbm.3, bf16[2,512,512]{2,1,0:T(8,128)(2,1)} %cot_hbm.3), custom_call_target="tpu_custom_call" | custom-call | flops 134217728 | bytes 1048576 | tf_op jit(solution)/shard_map/pallas_call | solution.py:80
  1.5 0.5 %collective-permute-start = (bf16[256,512]{1,0:T(8,128)(2,1)S(1)}, bf16[256,512]{1,0:T(8,128)(2,1)S(1)}, u32[]{:S(2)}, u32[]{:S(2)}) collective-permute-start(bf16[256,512]{1,0:T(8,128)(2,1)S(1)} %get-tuple-element.19), channel_id=1, source_target_pairs={{0,2},{2,0},{1,3},{3,1},{4,6},{6,4},{5,7},{7,5},{8,10},{10,8},{9,1... | collective-permute-start | bytes 786440 | tf_op jit(solution)/shard_map/ppermute | solution.py:280
  2.0 1.6 %shard_map.38 = (f32[256,512]{1,0:T(8,128)S(1)}, bf16[256,512]{1,0:T(8,128)(2,1)S(1)}, bf16[2,512,256]{2,1,0:T(8,128)(2,1)S(1)}, bf16[512,512]{1,0:T(8,128)(2,1)S(1)}) custom-call(bf16[2,512,512]{2,1,0:T(8,128)(2,1)} %patch_hbm.3, bf16[2,512,512]{2,1,0:T(8,128)(2,1)} %cot_hbm.3, bf16[2,512,256]{2,1,0:T(8,128)(2,1)S(1)} %get-tuple-element.14.other_patch, ...), custom_call_target="tpu_custom_call" | custom-call | flops 268435456 | bytes 1048576 | tf_op jit(solution)/shard_map/pallas_call | solution.py:80
  3.6 0.1 collective-permute-start.1
  3.7 0.0 collective-permute-done
  3.7 0.1 add_convert_fusion
  3.8 4.0 %collective-permute-start.2 = (bf16[128,512]{1,0:T(8,128)(2,1)S(1)}, bf16[128,512]{1,0:T(8,128)(2,1)S(1)}, u32[]{:S(2)}, u32[]{:S(2)}) collective-permute-start(bf16[128,512]{1,0:T(8,128)(2,1)S(1)} %get-tuple-element.24._), channel_id=1, source_target_pairs={{0,12},{4,8},{8,4},{12,0},{16,28},{20,24},{24,20},{28,16},{1,13},{... | collective-permute-start | bytes 393224 | tf_op jit(solution)/shard_map/ppermute | solution.py:284
  7.8 0.3 shard_map.39
  8.1 0.0 collective-permute-done.1
  8.2 0.1 convert_add_fusion
  8.3 0.5 %collective-permute-start.4 = (bf16[128,512]{1,0:T(8,128)(2,1)S(1)}, bf16[128,512]{1,0:T(8,128)(2,1)S(1)}, u32[]{:S(2)}, u32[]{:S(2)}) collective-permute-start(bf16[128,512]{1,0:T(8,128)(2,1)S(1)} %slice.31), channel_id=1, source_target_pairs={{0,8},{8,0},{16,24},{24,16},{1,9},{9,1},{17,25},{25,17},{2,10},{10... | collective-permute-start | bytes 393224 | tf_op jit(solution)/shard_map/ppermute | solution.py:280
  8.8 0.8 %collective-permute-start.3 = (bf16[128,512]{1,0:T(8,128)(2,1)S(1)}, bf16[128,512]{1,0:T(8,128)(2,1)S(1)}, u32[]{:S(2)}, u32[]{:S(2)}) collective-permute-start(bf16[128,512]{1,0:T(8,128)(2,1)S(1)} %get-tuple-element.23), channel_id=1, source_target_pairs={{0,4},{4,0},{1,5},{5,1},{2,6},{6,2},{3,7},{7,3},{8,12},{12,8},{9,1... | collective-permute-start | bytes 393224 | tf_op jit(solution)/shard_map/ppermute | solution.py:280
  9.6 4.9 %collective-permute-done.4 = bf16[128,512]{1,0:T(8,128)(2,1)S(1)} collective-permute-done((bf16[128,512]{1,0:T(8,128)(2,1)S(1)}, bf16[128,512]{1,0:T(8,128)(2,1)S(1)}, u32[]{:S(2)}, u32[]{:S(2)}) %collective-permute-start.4) | collective-permute-done | bytes 131104 | tf_op jit(solution)/shard_map/ppermute | solution.py:280
  14.5 0.0 collective-permute-done.2
  14.5 0.0 collective-permute-done.3
  14.5 0.1 fusion.2
  14.6 2.7 %collective-permute-start.5 = (bf16[128,512]{1,0:T(8,128)(2,1)S(1)}, bf16[128,512]{1,0:T(8,128)(2,1)S(1)}, u32[]{:S(2)}, u32[]{:S(2)}) collective-permute-start(bf16[128,512]{1,0:T(8,128)(2,1)S(1)} %fusion.2), channel_id=1, source_target_pairs={{0,16},{8,24},{16,0},{24,8},{1,17},{9,25},{17,1},{25,9},{2,18},{10... | collective-permute-start | bytes 393224 | tf_op jit(solution)/shard_map/ppermute | solution.py:280
  17.3 5.8 %collective-permute-done.5 = bf16[128,512]{1,0:T(8,128)(2,1)S(1)} collective-permute-done((bf16[128,512]{1,0:T(8,128)(2,1)S(1)}, bf16[128,512]{1,0:T(8,128)(2,1)S(1)}, u32[]{:S(2)}, u32[]{:S(2)}) %collective-permute-start.5) | collective-permute-done | bytes 131104 | tf_op jit(solution)/shard_map/ppermute | solution.py:280
  23.0 0.1 add_convert_fusion.1
  23.1 0.8 %collective-permute-start.6 = (bf16[128,512]{1,0:T(8,128)(2,1)S(1)}, bf16[128,512]{1,0:T(8,128)(2,1)S(1)}, u32[]{:S(2)}, u32[]{:S(2)}) collective-permute-start(bf16[128,512]{1,0:T(8,128)(2,1)S(1)} %add_convert_fusion.1), channel_id=1, source_target_pairs={{0,8},{8,0},{16,24},{24,16},{1,9},{9,1},{17,25},{25,17},{2,10},{10... | collective-permute-start | bytes 393224 | tf_op jit(solution)/shard_map/ppermute | solution.py:280
  23.9 4.2 %collective-permute-done.6 = bf16[128,512]{1,0:T(8,128)(2,1)S(1)} collective-permute-done((bf16[128,512]{1,0:T(8,128)(2,1)S(1)}, bf16[128,512]{1,0:T(8,128)(2,1)S(1)}, u32[]{:S(2)}, u32[]{:S(2)}) %collective-permute-start.6) | collective-permute-done | bytes 131104 | tf_op jit(solution)/shard_map/ppermute | solution.py:280
  28.2 0.1 collective-permute-start.7
  28.2 1.5 %collective-permute-done.7.far = bf16[256,512]{1,0:T(8,128)(2,1)S(1)} collective-permute-done((bf16[256,512]{1,0:T(8,128)(2,1)S(1)}, bf16[256,512]{1,0:T(8,128)(2,1)S(1)}, u32[]{:S(2)}, u32[]{:S(2)}) %collective-permute-start.7) | collective-permute-done | bytes 262176 | tf_op jit(solution)/shard_map/ppermute | solution.py:280
  29.8 7.0 %shard_map.40 = (bf16[32,512]{1,0:T(8,128)(2,1)S(1)}, bf16[32,512]{1,0:T(8,128)(2,1)S(1)}) custom-call(s32[2,2]{1,0:T(2,128)} %counts_hbm.1, bf16[256,512]{1,0:T(8,128)(2,1)S(1)} %pad_maximum_fusion.near, bf16[256,512]{1,0:T(8,128)(2,1)S(1)} %collective-permute-done.7.far), custom_call_target="tpu_custom_call" | custom-call | tf_op jit(solution)/shard_map/pallas_call | solution.py:252
  36.8 1.9 %collective-permute-start.8 = (bf16[32,512]{1,0:T(8,128)(2,1)S(1)}, bf16[32,512]{1,0:T(8,128)(2,1)S(1)}, u32[]{:S(2)}, u32[]{:S(2)}) collective-permute-start(bf16[32,512]{1,0:T(8,128)(2,1)S(1)} %get-tuple-element.22), channel_id=1, source_target_pairs={{0,4},{1,5},{4,0},{5,1},{2,6},{3,7},{6,2},{7,3},{8,12},{9,13},{12,... | collective-permute-start | bytes 98312 | tf_op jit(solution)/shard_map/ppermute | solution.py:321
  38.7 1.2 %collective-permute-start.10 = (bf16[32,512]{1,0:T(8,128)(2,1)S(1)}, bf16[32,512]{1,0:T(8,128)(2,1)S(1)}, u32[]{:S(2)}, u32[]{:S(2)}) collective-permute-start(bf16[32,512]{1,0:T(8,128)(2,1)S(1)} %get-tuple-element.22), channel_id=1, source_target_pairs={{0,5},{1,4},{4,1},{5,0},{2,7},{3,6},{6,3},{7,2},{8,13},{9,12},{12,... | collective-permute-start | bytes 98312 | tf_op jit(solution)/shard_map/ppermute | solution.py:321
  39.9 0.5 %collective-permute-start.9 = (bf16[32,512]{1,0:T(8,128)(2,1)S(1)}, bf16[32,512]{1,0:T(8,128)(2,1)S(1)}, u32[]{:S(2)}, u32[]{:S(2)}) collective-permute-start(bf16[32,512]{1,0:T(8,128)(2,1)S(1)} %get-tuple-element.21), channel_id=1, source_target_pairs={{0,1},{1,0},{4,5},{5,4},{2,3},{3,2},{6,7},{7,6},{8,9},{9,8},{12,13... | collective-permute-start | bytes 98312 | tf_op jit(solution)/shard_map/ppermute | solution.py:321
  40.3 0.4 collective-permute-done.8
  40.7 3.1 %collective-permute-done.9 = bf16[32,512]{1,0:T(8,128)(2,1)S(1)} collective-permute-done((bf16[32,512]{1,0:T(8,128)(2,1)S(1)}, bf16[32,512]{1,0:T(8,128)(2,1)S(1)}, u32[]{:S(2)}, u32[]{:S(2)}) %collective-permute-start.9) | collective-permute-done | bytes 32800 | tf_op jit(solution)/shard_map/ppermute | solution.py:321
  43.9 0.0 collective-permute-done.10
  43.9 0.7 %reverse_select_fusion = bf16[2,2,32,512]{3,2,1,0:T(8,128)(2,1)} fusion(bf16[2,2,32,512]{3,2,1,0:T(8,128)(2,1)S(1)} %reverse_select_fusion.1, pred[]{:T(512)S(6)} %eq.6), kind=kLoop, calls=%fused_computation.8 | loop fusion | flops 65536 | bytes 262145 | tf_op jit(solution)/shard_map/jit(_where)/select_n | solution.py:329
  (7 shorter events, 0.1 us)
Async XLA Ops:
  1.5 2.2 %collective-permute-start = (bf16[256,512]{1,0:T(8,128)(2,1)S(1)}, bf16[256,512]{1,0:T(8,128)(2,1)S(1)}, u32[]{:S(2)}, u32[]{:S(2)}) collective-permute-start(bf16[256,512]{1,0:T(8,128)(2,1)S(1)} %get-tuple-element.19), channel_id=1, source_target_pairs={{0,2},{2,0},{1,3},{3,1},{4,6},{6,4},{5,7},{7,5},{8,10},{10,8},{9,1... | collective-permute-start | bytes 786440 | tf_op jit(solution)/shard_map/ppermute | solution.py:280
  3.6 4.6 %collective-permute-start.1 = (bf16[256,512]{1,0:T(8,128)(2,1)S(1)}, bf16[256,512]{1,0:T(8,128)(2,1)S(1)}, u32[]{:S(2)}, u32[]{:S(2)}) collective-permute-start(bf16[256,512]{1,0:T(8,128)(2,1)S(1)} %get-tuple-element.20), channel_id=1, source_target_pairs={{0,2},{2,0},{1,3},{3,1},{4,6},{6,4},{5,7},{7,5},{8,10},{10,8},{9,1... | collective-permute-start | bytes 786440 | tf_op jit(solution)/shard_map/ppermute | solution.py:280
  3.8 10.7 %collective-permute-start.2 = (bf16[128,512]{1,0:T(8,128)(2,1)S(1)}, bf16[128,512]{1,0:T(8,128)(2,1)S(1)}, u32[]{:S(2)}, u32[]{:S(2)}) collective-permute-start(bf16[128,512]{1,0:T(8,128)(2,1)S(1)} %get-tuple-element.24._), channel_id=1, source_target_pairs={{0,12},{4,8},{8,4},{12,0},{16,28},{20,24},{24,20},{28,16},{1,13},{... | collective-permute-start | bytes 393224 | tf_op jit(solution)/shard_map/ppermute | solution.py:284
  8.3 6.2 %collective-permute-start.4 = (bf16[128,512]{1,0:T(8,128)(2,1)S(1)}, bf16[128,512]{1,0:T(8,128)(2,1)S(1)}, u32[]{:S(2)}, u32[]{:S(2)}) collective-permute-start(bf16[128,512]{1,0:T(8,128)(2,1)S(1)} %slice.31), channel_id=1, source_target_pairs={{0,8},{8,0},{16,24},{24,16},{1,9},{9,1},{17,25},{25,17},{2,10},{10... | collective-permute-start | bytes 393224 | tf_op jit(solution)/shard_map/ppermute | solution.py:280
  8.8 5.7 %collective-permute-start.3 = (bf16[128,512]{1,0:T(8,128)(2,1)S(1)}, bf16[128,512]{1,0:T(8,128)(2,1)S(1)}, u32[]{:S(2)}, u32[]{:S(2)}) collective-permute-start(bf16[128,512]{1,0:T(8,128)(2,1)S(1)} %get-tuple-element.23), channel_id=1, source_target_pairs={{0,4},{4,0},{1,5},{5,1},{2,6},{6,2},{3,7},{7,3},{8,12},{12,8},{9,1... | collective-permute-start | bytes 393224 | tf_op jit(solution)/shard_map/ppermute | solution.py:280
  14.6 8.5 %collective-permute-start.5 = (bf16[128,512]{1,0:T(8,128)(2,1)S(1)}, bf16[128,512]{1,0:T(8,128)(2,1)S(1)}, u32[]{:S(2)}, u32[]{:S(2)}) collective-permute-start(bf16[128,512]{1,0:T(8,128)(2,1)S(1)} %fusion.2), channel_id=1, source_target_pairs={{0,16},{8,24},{16,0},{24,8},{1,17},{9,25},{17,1},{25,9},{2,18},{10... | collective-permute-start | bytes 393224 | tf_op jit(solution)/shard_map/ppermute | solution.py:280
  23.1 5.0 %collective-permute-start.6 = (bf16[128,512]{1,0:T(8,128)(2,1)S(1)}, bf16[128,512]{1,0:T(8,128)(2,1)S(1)}, u32[]{:S(2)}, u32[]{:S(2)}) collective-permute-start(bf16[128,512]{1,0:T(8,128)(2,1)S(1)} %add_convert_fusion.1), channel_id=1, source_target_pairs={{0,8},{8,0},{16,24},{24,16},{1,9},{9,1},{17,25},{25,17},{2,10},{10... | collective-permute-start | bytes 393224 | tf_op jit(solution)/shard_map/ppermute | solution.py:280
  28.2 1.6 %collective-permute-start.7 = (bf16[256,512]{1,0:T(8,128)(2,1)S(1)}, bf16[256,512]{1,0:T(8,128)(2,1)S(1)}, u32[]{:S(2)}, u32[]{:S(2)}) collective-permute-start(bf16[256,512]{1,0:T(8,128)(2,1)S(1)} %pad_maximum_fusion.near), channel_id=1, source_target_pairs={{0,2},{2,0},{1,3},{3,1},{4,6},{6,4},{5,7},{7,5},{8,10},{10,8},{9,1... | collective-permute-start | bytes 786440 | tf_op jit(solution)/shard_map/ppermute | solution.py:280
  36.8 4.0 %collective-permute-start.8 = (bf16[32,512]{1,0:T(8,128)(2,1)S(1)}, bf16[32,512]{1,0:T(8,128)(2,1)S(1)}, u32[]{:S(2)}, u32[]{:S(2)}) collective-permute-start(bf16[32,512]{1,0:T(8,128)(2,1)S(1)} %get-tuple-element.22), channel_id=1, source_target_pairs={{0,4},{1,5},{4,0},{5,1},{2,6},{3,7},{6,2},{7,3},{8,12},{9,13},{12,... | collective-permute-start | bytes 98312 | tf_op jit(solution)/shard_map/ppermute | solution.py:321
  38.7 5.2 %collective-permute-start.10 = (bf16[32,512]{1,0:T(8,128)(2,1)S(1)}, bf16[32,512]{1,0:T(8,128)(2,1)S(1)}, u32[]{:S(2)}, u32[]{:S(2)}) collective-permute-start(bf16[32,512]{1,0:T(8,128)(2,1)S(1)} %get-tuple-element.22), channel_id=1, source_target_pairs={{0,5},{1,4},{4,1},{5,0},{2,7},{3,6},{6,3},{7,2},{8,13},{9,12},{12,... | collective-permute-start | bytes 98312 | tf_op jit(solution)/shard_map/ppermute | solution.py:321
  39.9 4.0 %collective-permute-start.9 = (bf16[32,512]{1,0:T(8,128)(2,1)S(1)}, bf16[32,512]{1,0:T(8,128)(2,1)S(1)}, u32[]{:S(2)}, u32[]{:S(2)}) collective-permute-start(bf16[32,512]{1,0:T(8,128)(2,1)S(1)} %get-tuple-element.21), channel_id=1, source_target_pairs={{0,1},{1,0},{4,5},{5,4},{2,3},{3,2},{6,7},{7,6},{8,9},{9,8},{12,13... | collective-permute-start | bytes 98312 | tf_op jit(solution)/shard_map/ppermute | solution.py:321

commit v11 on v8

--- a/solution.py
+++ b/solution.py
@@ -20,76 +20,84 @@
     return pltpu.CompilerParams(vmem_limit_bytes=limit << 20)
 
 
-def fetch_block(block, side_order, hbm, buffers, sems):
-    patch_hbm, cot_hbm = hbm
-    patch, cot = buffers
-    half = patch.shape[2]
+def half_sum(patch, cot, block, side, scale):
+    terms = lax.dot_general(
+        patch[block, side], cot[block], ROWS_IN_COLS, preferred_element_type=F32
+    )
+    return terms * scale
+
+
+def load_kernel(scale, patch_hbm, cot_hbm, given, patch, cot, sems):
+    half = patch.shape[3]
     width = half // 2
     column, core, parity = lax.axis_index("x"), lax.axis_index("core"), lax.axis_index("z") % 2
-    copies = [pltpu.make_async_copy(cot_hbm.at[column ^ block], cot, sems.at[0])]
-    for side in side_order:
+    copies = []
+
+    def fetch(source, target):
+        copies.append(pltpu.make_async_copy(source, target, sems.at[len(copies)]))
+        copies[-1].start()
+
+    def fetch_patch(block, side):
         for quarter in range(2):
             first = (core ^ side) * half + (parity ^ quarter) * width
-            copies.append(
-                pltpu.make_async_copy(
-                    patch_hbm.at[column ^ block, :, pl.ds(pl.multiple_of(first, width), width)],
-                    patch.at[side, :, quarter * width : (quarter + 1) * width],
-                    sems.at[len(copies)],
-                )
+            fetch(
+                patch_hbm.at[column ^ block, :, pl.ds(pl.multiple_of(first, width), width)],
+                patch.at[block, side, :, quarter * width : (quarter + 1) * width],
             )
-    for copy in copies:
-        copy.start()
-    return copies
-
-
-def half_sum(patch, cot, side, scale):
-    terms = lax.dot_general(patch[side], cot[...], ROWS_IN_COLS, preferred_element_type=F32)
-    return terms * scale
-
-
-def first_kernel(scale, patch_hbm, cot_hbm, given, patch, cot, sems):
-    copies = fetch_block(1, (1, 0), (patch_hbm, cot_hbm), (patch, cot), sems)
-    for copy in copies[:3]:
+
+    fetch(cot_hbm.at[column ^ 1], cot.at[1])
+    fetch_patch(1, 1)
+    needed = len(copies)
+    fetch_patch(1, 0)
+    fetch(cot_hbm.at[column], cot.at[0])
+    fetch_patch(0, 1)
+    fetch_patch(0, 0)
+    for copy in copies[:needed]:
         copy.wait()
-    given[...] = half_sum(patch, cot, 1, scale).astype(BF16)
-    for copy in copies[3:]:
+    given[...] = half_sum(patch, cot, 1, 1, scale).astype(BF16)
+    for copy in copies[needed:]:
         copy.wait()
 
 
-def second_kernel(scale, patch_hbm, cot_hbm, other_patch, other_cot, kept, given, patch, cot, sems):
-    copies = fetch_block(0, (1, 0), (patch_hbm, cot_hbm), (patch, cot), sems)
-    kept[...] = half_sum(other_patch, other_cot, 0, scale)
-    for copy in copies[:3]:
-        copy.wait()
-    given[...] = half_sum(patch, cot, 1, scale).astype(BF16)
-    for copy in copies[3:]:
-        copy.wait()
-
-
-def third_kernel(scale, patch, cot, _, kept):
-    kept[...] = half_sum(patch, cot, 0, scale)
-
-
-def pixel_sums(kernel, scale, shape, sums, loads, *operands):
-    pix, width = shape
+def load(scale, patches, cotangents):
+    blocks, pix, width = patches.shape
     half = width // 2
-    out_shape = [jax.ShapeDtypeStruct((half, width), dtype) for dtype in sums]
-    if loads:
-        out_shape.append(jax.ShapeDtypeStruct((2, pix, half), BF16))
-        out_shape.append(jax.ShapeDtypeStruct((pix, width), BF16))
-    return pl.pallas_call(
-        functools.partial(kernel, scale),
-        out_shape=out_shape,
-        in_specs=[HBM if loads and index < 2 else VMEM for index in range(len(operands))],
-        out_specs=[VMEM] * len(out_shape),
-        scratch_shapes=[pltpu.SemaphoreType.DMA((5,))] if loads else [],
+    return pl.pallas_call(
+        functools.partial(load_kernel, scale),
+        out_shape=[
+            jax.ShapeDtypeStruct((half, width), BF16),
+            jax.ShapeDtypeStruct((blocks, 2, pix, half), BF16),
+            jax.ShapeDtypeStruct((blocks, pix, width), BF16),
+        ],
+        in_specs=[HBM] * 2,
+        out_specs=[VMEM] * 3,
+        scratch_shapes=[pltpu.SemaphoreType.DMA((10,))],
+        compiler_params=params(16),
+    )(
+        pltpu.with_memory_space_constraint(patches, pltpu.HBM),
+        pltpu.with_memory_space_constraint(cotangents, pltpu.HBM),
+    )
+
+
+def sums_kernel(scale, wanted, patch, cot, *refs):
+    for (block, side, dtype), out in zip(wanted, refs[-len(wanted) :]):
+        out[...] = half_sum(patch, cot, block, side, scale).astype(dtype)
+
+
+def sums(scale, patch, cot, after, *wanted):
+    pix, half = patch.shape[2:]
+    return pl.pallas_call(
+        functools.partial(sums_kernel, scale, wanted),
+        out_shape=[jax.ShapeDtypeStruct((half, 2 * half), dtype) for _, _, dtype in wanted],
+        in_specs=[VMEM] * 2 + [pl.BlockSpec(memory_space=pl.ANY)] * len(after),
+        out_specs=[VMEM] * len(wanted),
         compiler_params=params(16),
         cost_estimate=pl.CostEstimate(
-            flops=2 * len(sums) * pix * half * width,
-            bytes_accessed=4 * pix * width,
+            flops=4 * len(wanted) * pix * half * half,
+            bytes_accessed=8 * pix * half,
             transcendentals=0,
         ),
-    )(*operands)
+    )(patch, cot, *after)
 
 
 def collect_kernel(own, *refs):
@@ -160,17 +168,13 @@
         five = jnp.where(diagonal, 1.25, 0.0)
         return five - 0.25 * upper_left, -0.25 * upper_right, five - 0.25 * lower_right
 
-    def begin(dims, upper, lower):
-        tenth = jnp.where(diagonal, 0.1, 0.0)
+    def statistics(dims, upper, lower):
         tiles = [
             lax.dot_general(a, b, dims, preferred_element_type=F32)
             for a, b in ((upper, upper), (upper, lower), (lower, lower))
         ]
-        tiles = [tiles[0] + tenth, tiles[1], tiles[2] + tenth]
-        squares = tiles[0] * tiles[0] + 2.0 * (tiles[1] * tiles[1]) + tiles[2] * tiles[2]
-        scale = 2.5 / jnp.sqrt(jnp.sum(squares, keepdims=True))
-        first = jnp.sqrt(jnp.sqrt(scale)).astype(BF16).astype(F32)
-        return [scale * tile for tile in tiles], first
+        tenth = jnp.where(diagonal, 0.1, 0.0)
+        return tiles[0] + tenth, tiles[1], tiles[2] + tenth
 
     def spot(flip):
         row = (4 * place + 2 * (column ^ flip) + core) * rows
@@ -182,11 +186,17 @@
     pick = lax.broadcasted_iota(jnp.int32, (2 * rows, width), 1) == wanted
     pick = jnp.where(pick, 1.0, 0.0).astype(BF16)
     picked = 2 * rows
-    tiles, first = begin(COLS_IN_COLS, grad[low, :], grad[high, :])
+    stats_left = statistics(COLS_IN_COLS, grad[low, :], grad[high, :])
+    stats_right = statistics(ROWS_IN_COLS, grad[:, low], grad[:, high])
+    squares = [tile * tile for tile in stats_left]
+    norm = jnp.sqrt(jnp.sum(squares[0] + 2.0 * squares[1] + squares[2], keepdims=True))
+    scale = 2.5 / norm
+    first = jnp.sqrt(jnp.sqrt(scale)).astype(BF16).astype(F32)
+    tiles = [scale * tile for tile in stats_left]
     fill(m_left, 0, tiles)
     fill(left, picked, factor(tiles))
     left[:picked, :] = (first * dot(pick, left[picked:, :])).astype(BF16)
-    tiles, first = begin(ROWS_IN_COLS, grad[:, low], grad[:, high])
+    tiles = [scale * tile for tile in stats_right]
     fill(m_right, 0, tiles)
     tiles = [tile.astype(BF16) for tile in factor(tiles)]
     fill(right, width, tiles)
@@ -285,12 +295,35 @@
     )(pltpu.with_memory_space_constraint(counts, pltpu.HBM), *pieces)
 
 
+def place_kernel(*refs):
+    *pieces, out, sems = refs
+    column, group = lax.axis_index("x"), lax.axis_index("group")
+    copies = []
+    for index, piece in enumerate(pieces):
+        number = 2 * (group ^ (index // 2)) + (column ^ (index % 2))
+        copies.append(pltpu.make_async_copy(piece, out.at[number], sems.at[index]))
+        copies[-1].start()
+    for copy in copies:
+        copy.wait()
+
+
+def place(pieces):
+    rows, width = pieces[0].shape
+    return pl.pallas_call(
+        place_kernel,
+        out_shape=jax.ShapeDtypeStruct((len(pieces), rows, width), BF16),
+        in_specs=[VMEM] * len(pieces),
+        out_specs=HBM,
+        scratch_shapes=[pltpu.SemaphoreType.DMA((len(pieces),))],
+        compiler_params=params(16),
+    )(*pieces)
+
+
 def shards(line, groups, patches, cotangents, newton_counts):
     blocks, pix, width = patches.shape
     half, quarter = width // 2, width // 4
     rows = half // (2 * line)
     scale = 1.0 / float(pix * 4 * line * width) ** 0.5
-    column, group = lax.axis_index("x"), lax.axis_index("group")
 
     def swap(array, axis, mask=1):
         return lax.ppermute(array, axis, [(i, i ^ mask) for i in range(lax.axis_size(axis))])
@@ -299,20 +332,15 @@
         moves = [(2 * z + x, 2 * (z ^ 1) + (x ^ 1)) for z in range(line) for x in range(2)]
         return lax.ppermute(array, ("z", "x"), moves)
 
-    patches = pltpu.with_memory_space_constraint(patches, pltpu.HBM)
-    cotangents = pltpu.with_memory_space_constraint(cotangents, pltpu.HBM)
-    shape = (pix, width)
-    given, *loaded = pixel_sums(first_kernel, scale, shape, (BF16,), True, patches, cotangents)
+    given, patch, cot = load(scale, patches, cotangents)
     came = swap(given, "core")
-    kept, given_on, *loaded = pixel_sums(
-        second_kernel, scale, shape, (F32, BF16), True, patches, cotangents, *loaded
-    )
+    kept, given_on = sums(scale, patch, cot, (), (1, 0, F32), (0, 1, BF16))
     came_on = swap(given_on, "core")
     leaving = add(kept, came).astype(BF16)
     to_diagonal, to_column = leaving[quarter:], leaving[:quarter]
     from_diagonal = swap_diagonal(to_diagonal)
     from_column = swap(to_column, "x")
-    (kept_on,) = pixel_sums(third_kernel, scale, shape, (F32,), False, *loaded, to_diagonal)
+    (kept_on,) = sums(scale, patch, cot, (to_diagonal,), (0, 0, F32))
     own = add(kept_on, came_on)
     from_line = swap(own[quarter:].astype(BF16), "z")
     left, right, send_left, send_right = collect(own, from_diagonal, from_column, from_line)
@@ -328,9 +356,8 @@
         pieces += [own, other, swap(jnp.concatenate([own, other], 0), "core")]
     keep, send = root(newton_counts, pieces, rows)
 
-    found = []
+    pieces = []
     for turn in range(groups):
-        pair = []
         for flip in range(2):
             moves = [
                 (c * groups + g, (c ^ flip) * groups + (g ^ turn))
@@ -338,17 +365,8 @@
                 for g in range(groups)
             ]
             piece = send if flip else keep
-            pair.append(lax.ppermute(piece, ("x", "group"), moves) if turn or flip else piece)
-        found.append(jnp.stack(pair))
-    found = jnp.stack(found)
-    found = jnp.where(column == 0, found, found[:, ::-1])
-    bit = 1
-    while bit < groups:
-        shape = (groups // (2 * bit), 2, bit) + found.shape[1:]
-        flipped = found.reshape(shape)[:, ::-1].reshape(found.shape)
-        found = jnp.where(group & bit == 0, found, flipped)
-        bit *= 2
-    return found.reshape(blocks * groups, rows, width)
+            pieces.append(lax.ppermute(piece, ("x", "group"), moves) if turn or flip else piece)
+    return place(pieces)
 
 
 def solution(mesh):

time: 43.8 us -> 42.4 us (0.968)
  waiting for transfers between devices: 15.2 us -> 16.7 us
  starting transfers between devices: 17.3 us -> 16 us
  other arithmetic: 0.93 us -> 0.19 us
  Pallas kernels: 9.97 us -> 9.29 us
    ppermute x1, starting transfers between devices: 4.02 us -> 1.55 us  [swap_diagonal(): return lax.ppermute(array, ('z', 'x'), moves)]
    ppermute x10, starting transfers between devices: 9.09 us -> 10.9 us  [swap(): lax.ppermute(array, axis, [(i, i ^ mask) for i in range(lax.axis_size(axi...]
    ppermute x1, waiting for transfers between devices: 0.01 us -> 1.4 us  [swap_diagonal(): return lax.ppermute(array, ('z', 'x'), moves)]
    select_n x2 -> x0, other arithmetic: 0.71 us -> none  [the longest x1 0.68 us: shards(): found = jnp.where(group & bit == 0, found, flipped)]
    ppermute x3, starting transfers between devices: 4.23 us -> 3.55 us  [shards(): lax.ppermute(piece, ('x', 'group'), moves)]
    pallas_call x3 -> x4, Pallas kernels: 3.36 us -> 3.07 us  [the longest x1 1.61 us: load(): pl.pallas_call(functools.partial(load_kernel, scale), out_shape=[jax.Shap...]
  transfers between devices with their start and end apart: 14 -> 14, of which waited for: 7 -> 11; matrix products, arithmetic and copies ran while one was open for 1% -> 1% of each run, Pallas kernels for 4% -> 2%
where the time goes in v11:
time: 42.4 us; the launch traced here: 42.3 us
  waiting for transfers between devices  16.7 us (39%)
  starting transfers between devices  16 us (38%)
  Pallas kernels  9.29 us (22%)
    ppermute x10, waiting for transfers between devices, swap(): lax.ppermute(array, axis, [(i, i ^ mask) for i in range(lax.axis_size(axi...  11.9 us
    ppermute x10, starting transfers between devices, swap(): lax.ppermute(array, axis, [(i, i ^ mask) for i in range(lax.axis_size(axi...  10.9 us
    pallas_call x1, Pallas kernels, root(): pl.pallas_call(functools.partial(root_kernel, most), out_shape=[out, out]...  6.17 us
    ppermute x3, starting transfers between devices, shards(): lax.ppermute(piece, ('x', 'group'), moves)  3.55 us
    ppermute x3, waiting for transfers between devices, shards(): lax.ppermute(piece, ('x', 'group'), moves)  3.38 us
    pallas_call x1, Pallas kernels, load(): pl.pallas_call(functools.partial(load_kernel, scale), out_shape=[jax.Shap...  1.61 us
    ppermute x1, starting transfers between devices, swap_diagonal(): return lax.ppermute(array, ('z', 'x'), moves)  1.55 us
    ppermute x1, waiting for transfers between devices, swap_diagonal(): return lax.ppermute(array, ('z', 'x'), moves)  1.4 us
  transfers between devices with their start and end apart: 14, of which 11 were waited for; matrix products, arithmetic and copies ran while one was open for 1% of the time, Pallas kernels for 2%

profile of v11, /device:TPU:0, one launch (start us, length us, event | category | flops | bytes accessed | tf_op | source)
XLA Modules:
  0.0 42.3 jit_solution(15640377993886387542)
XLA Ops:
  0.0 1.6 %shard_map.37 = (bf16[256,512]{1,0:T(8,128)(2,1)S(1)}, bf16[2,2,512,256]{3,2,1,0:T(8,128)(2,1)S(1)}, bf16[2,512,512]{2,1,0:T(8,128)(2,1)S(1)}) custom-call(bf16[2,512,512]{2,1,0:T(8,128)(2,1)} %patch_hbm.1, bf16[2,512,512]{2,1,0:T(8,128)(2,1)} %cot_hbm.1), custom_call_target="tpu_custom_call" | custom-call | tf_op jit(solution)/shard_map/pallas_call | solution.py:65
  1.6 0.5 %collective-permute-start = (bf16[256,512]{1,0:T(8,128)(2,1)S(1)}, bf16[256,512]{1,0:T(8,128)(2,1)S(1)}, u32[]{:S(2)}, u32[]{:S(2)}) collective-permute-start(bf16[256,512]{1,0:T(8,128)(2,1)S(1)} %get-tuple-element.19), channel_id=1, source_target_pairs={{0,2},{2,0},{1,3},{3,1},{4,6},{6,4},{5,7},{7,5},{8,10},{10,8},{9,1... | collective-permute-start | bytes 786440 | tf_op jit(solution)/shard_map/ppermute | solution.py:329
  2.1 0.5 %shard_map.38 = (f32[256,512]{1,0:T(8,128)S(1)}, bf16[256,512]{1,0:T(8,128)(2,1)S(1)}) custom-call(bf16[2,2,512,256]{3,2,1,0:T(8,128)(2,1)S(1)} %get-tuple-element.16.patch, bf16[2,512,512]{2,1,0:T(8,128)(2,1)S(1)} %get-tuple-element.17.cot), custom_call_target="tpu_custom_call" | custom-call | flops 268435456 | bytes 1048576 | tf_op jit(solution)/shard_map/pallas_call | solution.py:89
  2.6 0.1 collective-permute-start.1
  2.7 0.6 %collective-permute-done = bf16[256,512]{1,0:T(8,128)(2,1)S(1)} collective-permute-done((bf16[256,512]{1,0:T(8,128)(2,1)S(1)}, bf16[256,512]{1,0:T(8,128)(2,1)S(1)}, u32[]{:S(2)}, u32[]{:S(2)}) %collective-permute-start) | collective-permute-done | bytes 262176 | tf_op jit(solution)/shard_map/ppermute | solution.py:329
  3.3 0.1 add_convert_fusion
  3.4 2.9 %collective-permute-start.3 = (bf16[128,512]{1,0:T(8,128)(2,1)S(1)}, bf16[128,512]{1,0:T(8,128)(2,1)S(1)}, u32[]{:S(2)}, u32[]{:S(2)}) collective-permute-start(bf16[128,512]{1,0:T(8,128)(2,1)S(1)} %get-tuple-element.27), channel_id=1, source_target_pairs={{0,4},{4,0},{1,5},{5,1},{2,6},{6,2},{3,7},{7,3},{8,12},{12,8},{9,1... | collective-permute-start | bytes 393224 | tf_op jit(solution)/shard_map/ppermute | solution.py:329
  6.3 1.5 %collective-permute-start.2 = (bf16[128,512]{1,0:T(8,128)(2,1)S(1)}, bf16[128,512]{1,0:T(8,128)(2,1)S(1)}, u32[]{:S(2)}, u32[]{:S(2)}) collective-permute-start(bf16[128,512]{1,0:T(8,128)(2,1)S(1)} %get-tuple-element.28.refs_0_), channel_id=1, source_target_pairs={{0,12},{4,8},{8,4},{12,0},{16,28},{20,24},{24,20},{28,16},{1,13},{... | collective-permute-start | bytes 393224 | tf_op jit(solution)/shard_map/ppermute | solution.py:333
  7.9 0.3 shard_map.39
  8.2 0.0 collective-permute-done.1
  8.2 0.1 convert_add_fusion.own
  8.3 0.1 collective-permute-start.4
  8.4 3.8 %collective-permute-done.3.refs_1_ = bf16[128,512]{1,0:T(8,128)(2,1)S(1)} collective-permute-done((bf16[128,512]{1,0:T(8,128)(2,1)S(1)}, bf16[128,512]{1,0:T(8,128)(2,1)S(1)}, u32[]{:S(2)}, u32[]{:S(2)}) %collective-permute-start.3) | collective-permute-done | bytes 131104 | tf_op jit(solution)/shard_map/ppermute | solution.py:329
  12.2 1.4 %collective-permute-done.2.refs_0_ = bf16[128,512]{1,0:T(8,128)(2,1)S(1)} collective-permute-done((bf16[128,512]{1,0:T(8,128)(2,1)S(1)}, bf16[128,512]{1,0:T(8,128)(2,1)S(1)}, u32[]{:S(2)}, u32[]{:S(2)}) %collective-permute-start.2) | collective-permute-done | bytes 131104 | tf_op jit(solution)/shard_map/ppermute | solution.py:333
  13.6 0.6 %collective-permute-done.4.refs_2_ = bf16[128,512]{1,0:T(8,128)(2,1)S(1)} collective-permute-done((bf16[128,512]{1,0:T(8,128)(2,1)S(1)}, bf16[128,512]{1,0:T(8,128)(2,1)S(1)}, u32[]{:S(2)}, u32[]{:S(2)}) %collective-permute-start.4) | collective-permute-done | bytes 131104 | tf_op jit(solution)/shard_map/ppermute | solution.py:329
  14.3 0.1 shard_map.40
  14.3 2.8 %collective-permute-start.5 = (bf16[128,256]{1,0:T(8,128)(2,1)S(1)}, bf16[128,256]{1,0:T(8,128)(2,1)S(1)}, u32[]{:S(2)}, u32[]{:S(2)}) collective-permute-start(bf16[128,256]{1,0:T(8,128)(2,1)S(1)} %get-tuple-element.22), channel_id=1, source_target_pairs={{0,16},{8,24},{16,0},{24,8},{1,17},{9,25},{17,1},{25,9},{2,18},{10... | collective-permute-start | bytes 196616 | tf_op jit(solution)/shard_map/ppermute | solution.py:329
  17.1 0.2 collective-permute-start.8
  17.3 2.5 %collective-permute-done.5 = bf16[128,256]{1,0:T(8,128)(2,1)S(1)} collective-permute-done((bf16[128,256]{1,0:T(8,128)(2,1)S(1)}, bf16[128,256]{1,0:T(8,128)(2,1)S(1)}, u32[]{:S(2)}, u32[]{:S(2)}) %collective-permute-start.5) | collective-permute-done | bytes 65568 | tf_op jit(solution)/shard_map/ppermute | solution.py:329
  19.9 2.9 %collective-permute-start.6 = (bf16[128,256]{1,0:T(8,128)(2,1)S(1)}, bf16[128,256]{1,0:T(8,128)(2,1)S(1)}, u32[]{:S(2)}, u32[]{:S(2)}) collective-permute-start(bf16[128,256]{1,0:T(8,128)(2,1)S(1)} %add_convert_fusion.2.refs_0_), channel_id=1, source_target_pairs={{0,8},{8,0},{16,24},{24,16},{1,9},{9,1},{17,25},{25,17},{2,10},{10... | collective-permute-start | bytes 196616 | tf_op jit(solution)/shard_map/ppermute | solution.py:329
  22.7 0.0 collective-permute-done.8
  22.7 1.2 %collective-permute-start.9 = (bf16[128,256]{1,0:T(8,128)(2,1)S(1)}, bf16[128,256]{1,0:T(8,128)(2,1)S(1)}, u32[]{:S(2)}, u32[]{:S(2)}) collective-permute-start(bf16[128,256]{1,0:T(8,128)(2,1)S(1)} %add_convert_fusion.1.refs_3_), channel_id=1, source_target_pairs={{0,8},{8,0},{16,24},{24,16},{1,9},{9,1},{17,25},{25,17},{2,10},{10... | collective-permute-start | bytes 196616 | tf_op jit(solution)/shard_map/ppermute | solution.py:329
  24.0 1.5 %collective-permute-done.6.refs_1_ = bf16[128,256]{1,0:T(8,128)(2,1)S(1)} collective-permute-done((bf16[128,256]{1,0:T(8,128)(2,1)S(1)}, bf16[128,256]{1,0:T(8,128)(2,1)S(1)}, u32[]{:S(2)}, u32[]{:S(2)}) %collective-permute-start.6) | collective-permute-done | bytes 65568 | tf_op jit(solution)/shard_map/ppermute | solution.py:329
  25.5 0.1 collective-permute-start.7
  25.6 1.5 %collective-permute-done.9.refs_4_ = bf16[128,256]{1,0:T(8,128)(2,1)S(1)} collective-permute-done((bf16[128,256]{1,0:T(8,128)(2,1)S(1)}, bf16[128,256]{1,0:T(8,128)(2,1)S(1)}, u32[]{:S(2)}, u32[]{:S(2)}) %collective-permute-start.9) | collective-permute-done | bytes 65568 | tf_op jit(solution)/shard_map/ppermute | solution.py:329
  27.1 0.1 collective-permute-start.10
  27.2 0.0 collective-permute-done.7.refs_2_
  27.2 1.3 %collective-permute-done.10.refs_5_ = bf16[256,256]{1,0:T(8,128)(2,1)S(1)} collective-permute-done((bf16[256,256]{1,0:T(8,128)(2,1)S(1)}, bf16[256,256]{1,0:T(8,128)(2,1)S(1)}, u32[]{:S(2)}, u32[]{:S(2)}) %collective-permute-start.10) | collective-permute-done | bytes 131104 | tf_op jit(solution)/shard_map/ppermute | solution.py:329
  28.5 6.2 %shard_map.41 = (bf16[32,512]{1,0:T(8,128)(2,1)S(1)}, bf16[32,512]{1,0:T(8,128)(2,1)S(1)}) custom-call(s32[2,2]{1,0:T(2,128)} %counts_hbm.1, bf16[128,256]{1,0:T(8,128)(2,1)S(1)} %add_convert_fusion.2.refs_0_, bf16[128,256]{1,0:T(8,128)(2,1)S(1)} %collective-permute-done.6.refs_1_, bf16[256,256]{1,0:T(8,128)(2,1)S(1)} %collective-permute-done.7.refs_2_, ...), custom_call_target="tpu_custom_call" | custom-call | tf_op jit(solution)/shard_map/pallas_call | solution.py:278
  34.7 1.6 %collective-permute-start.12 = (bf16[32,512]{1,0:T(8,128)(2,1)S(1)}, bf16[32,512]{1,0:T(8,128)(2,1)S(1)}, u32[]{:S(2)}, u32[]{:S(2)}) collective-permute-start(bf16[32,512]{1,0:T(8,128)(2,1)S(1)} %get-tuple-element.25.refs_0_), channel_id=1, source_target_pairs={{0,1},{1,0},{4,5},{5,4},{2,3},{3,2},{6,7},{7,6},{8,9},{9,8},{12,13... | collective-permute-start | bytes 98312 | tf_op jit(solution)/shard_map/ppermute | solution.py:368
  36.3 1.4 %collective-permute-start.13 = (bf16[32,512]{1,0:T(8,128)(2,1)S(1)}, bf16[32,512]{1,0:T(8,128)(2,1)S(1)}, u32[]{:S(2)}, u32[]{:S(2)}) collective-permute-start(bf16[32,512]{1,0:T(8,128)(2,1)S(1)} %get-tuple-element.26), channel_id=1, source_target_pairs={{0,5},{1,4},{4,1},{5,0},{2,7},{3,6},{6,3},{7,2},{8,13},{9,12},{12,... | collective-permute-start | bytes 98312 | tf_op jit(solution)/shard_map/ppermute | solution.py:368
  37.7 0.5 %collective-permute-start.11 = (bf16[32,512]{1,0:T(8,128)(2,1)S(1)}, bf16[32,512]{1,0:T(8,128)(2,1)S(1)}, u32[]{:S(2)}, u32[]{:S(2)}) collective-permute-start(bf16[32,512]{1,0:T(8,128)(2,1)S(1)} %get-tuple-element.26), channel_id=1, source_target_pairs={{0,4},{1,5},{4,0},{5,1},{2,6},{3,7},{6,2},{7,3},{8,12},{9,13},{12,... | collective-permute-start | bytes 98312 | tf_op jit(solution)/shard_map/ppermute | solution.py:368
  38.2 0.4 %collective-permute-done.12.refs_2_ = bf16[32,512]{1,0:T(8,128)(2,1)S(1)} collective-permute-done((bf16[32,512]{1,0:T(8,128)(2,1)S(1)}, bf16[32,512]{1,0:T(8,128)(2,1)S(1)}, u32[]{:S(2)}, u32[]{:S(2)}) %collective-permute-start.12) | collective-permute-done | bytes 32800 | tf_op jit(solution)/shard_map/ppermute | solution.py:368
  38.7 2.7 %collective-permute-done.13.refs_3_ = bf16[32,512]{1,0:T(8,128)(2,1)S(1)} collective-permute-done((bf16[32,512]{1,0:T(8,128)(2,1)S(1)}, bf16[32,512]{1,0:T(8,128)(2,1)S(1)}, u32[]{:S(2)}, u32[]{:S(2)}) %collective-permute-start.13) | collective-permute-done | bytes 32800 | tf_op jit(solution)/shard_map/ppermute | solution.py:368
  41.3 0.3 collective-permute-done.11.refs_1_
  41.6 0.7 %shard_map.42 = bf16[4,32,512]{2,1,0:T(8,128)(2,1)} custom-call(bf16[32,512]{1,0:T(8,128)(2,1)S(1)} %get-tuple-element.25.refs_0_, bf16[32,512]{1,0:T(8,128)(2,1)S(1)} %collective-permute-done.11.refs_1_, bf16[32,512]{1,0:T(8,128)(2,1)S(1)} %collective-permute-done.12.refs_2_, bf16[32,512]{1,0:T(8,128)(2,1)S(1)} %collective-permute-done.13.refs_3_), custom_call_target="tpu_custom_call" | custom-call | tf_op jit(solution)/shard_map/pallas_call | solution.py:312
  (6 shorter events, 0.1 us)
Async XLA Ops:
  1.6 1.7 %collective-permute-start = (bf16[256,512]{1,0:T(8,128)(2,1)S(1)}, bf16[256,512]{1,0:T(8,128)(2,1)S(1)}, u32[]{:S(2)}, u32[]{:S(2)}) collective-permute-start(bf16[256,512]{1,0:T(8,128)(2,1)S(1)} %get-tuple-element.19), channel_id=1, source_target_pairs={{0,2},{2,0},{1,3},{3,1},{4,6},{6,4},{5,7},{7,5},{8,10},{10,8},{9,1... | collective-permute-start | bytes 786440 | tf_op jit(solution)/shard_map/ppermute | solution.py:329
  2.6 5.6 %collective-permute-start.1 = (bf16[256,512]{1,0:T(8,128)(2,1)S(1)}, bf16[256,512]{1,0:T(8,128)(2,1)S(1)}, u32[]{:S(2)}, u32[]{:S(2)}) collective-permute-start(bf16[256,512]{1,0:T(8,128)(2,1)S(1)} %get-tuple-element.20), channel_id=1, source_target_pairs={{0,2},{2,0},{1,3},{3,1},{4,6},{6,4},{5,7},{7,5},{8,10},{10,8},{9,1... | collective-permute-start | bytes 786440 | tf_op jit(solution)/shard_map/ppermute | solution.py:329
  3.4 8.8 %collective-permute-start.3 = (bf16[128,512]{1,0:T(8,128)(2,1)S(1)}, bf16[128,512]{1,0:T(8,128)(2,1)S(1)}, u32[]{:S(2)}, u32[]{:S(2)}) collective-permute-start(bf16[128,512]{1,0:T(8,128)(2,1)S(1)} %get-tuple-element.27), channel_id=1, source_target_pairs={{0,4},{4,0},{1,5},{5,1},{2,6},{6,2},{3,7},{7,3},{8,12},{12,8},{9,1... | collective-permute-start | bytes 393224 | tf_op jit(solution)/shard_map/ppermute | solution.py:329
  6.3 7.3 %collective-permute-start.2 = (bf16[128,512]{1,0:T(8,128)(2,1)S(1)}, bf16[128,512]{1,0:T(8,128)(2,1)S(1)}, u32[]{:S(2)}, u32[]{:S(2)}) collective-permute-start(bf16[128,512]{1,0:T(8,128)(2,1)S(1)} %get-tuple-element.28.refs_0_), channel_id=1, source_target_pairs={{0,12},{4,8},{8,4},{12,0},{16,28},{20,24},{24,20},{28,16},{1,13},{... | collective-permute-start | bytes 393224 | tf_op jit(solution)/shard_map/ppermute | solution.py:333
  8.3 6.0 %collective-permute-start.4 = (bf16[128,512]{1,0:T(8,128)(2,1)S(1)}, bf16[128,512]{1,0:T(8,128)(2,1)S(1)}, u32[]{:S(2)}, u32[]{:S(2)}) collective-permute-start(bf16[128,512]{1,0:T(8,128)(2,1)S(1)} %slice.17), channel_id=1, source_target_pairs={{0,8},{8,0},{16,24},{24,16},{1,9},{9,1},{17,25},{25,17},{2,10},{10... | collective-permute-start | bytes 393224 | tf_op jit(solution)/shard_map/ppermute | solution.py:329
  14.3 5.5 %collective-permute-start.5 = (bf16[128,256]{1,0:T(8,128)(2,1)S(1)}, bf16[128,256]{1,0:T(8,128)(2,1)S(1)}, u32[]{:S(2)}, u32[]{:S(2)}) collective-permute-start(bf16[128,256]{1,0:T(8,128)(2,1)S(1)} %get-tuple-element.22), channel_id=1, source_target_pairs={{0,16},{8,24},{16,0},{24,8},{1,17},{9,25},{17,1},{25,9},{2,18},{10... | collective-permute-start | bytes 196616 | tf_op jit(solution)/shard_map/ppermute | solution.py:329
  17.1 5.6 %collective-permute-start.8 = (bf16[128,256]{1,0:T(8,128)(2,1)S(1)}, bf16[128,256]{1,0:T(8,128)(2,1)S(1)}, u32[]{:S(2)}, u32[]{:S(2)}) collective-permute-start(bf16[128,256]{1,0:T(8,128)(2,1)S(1)} %get-tuple-element.24), channel_id=1, source_target_pairs={{0,16},{8,24},{16,0},{24,8},{1,17},{9,25},{17,1},{25,9},{2,18},{10... | collective-permute-start | bytes 196616 | tf_op jit(solution)/shard_map/ppermute | solution.py:329
  19.9 5.6 %collective-permute-start.6 = (bf16[128,256]{1,0:T(8,128)(2,1)S(1)}, bf16[128,256]{1,0:T(8,128)(2,1)S(1)}, u32[]{:S(2)}, u32[]{:S(2)}) collective-permute-start(bf16[128,256]{1,0:T(8,128)(2,1)S(1)} %add_convert_fusion.2.refs_0_), channel_id=1, source_target_pairs={{0,8},{8,0},{16,24},{24,16},{1,9},{9,1},{17,25},{25,17},{2,10},{10... | collective-permute-start | bytes 196616 | tf_op jit(solution)/shard_map/ppermute | solution.py:329
  22.7 4.3 %collective-permute-start.9 = (bf16[128,256]{1,0:T(8,128)(2,1)S(1)}, bf16[128,256]{1,0:T(8,128)(2,1)S(1)}, u32[]{:S(2)}, u32[]{:S(2)}) collective-permute-start(bf16[128,256]{1,0:T(8,128)(2,1)S(1)} %add_convert_fusion.1.refs_3_), channel_id=1, source_target_pairs={{0,8},{8,0},{16,24},{24,16},{1,9},{9,1},{17,25},{25,17},{2,10},{10... | collective-permute-start | bytes 196616 | tf_op jit(solution)/shard_map/ppermute | solution.py:329
  25.5 1.7 %collective-permute-start.7 = (bf16[256,256]{1,0:T(8,128)(2,1)S(1)}, bf16[256,256]{1,0:T(8,128)(2,1)S(1)}, u32[]{:S(2)}, u32[]{:S(2)}) collective-permute-start(bf16[256,256]{1,0:T(8,128)(2,1)S(1)} %pad_maximum_fusion), channel_id=1, source_target_pairs={{0,2},{2,0},{1,3},{3,1},{4,6},{6,4},{5,7},{7,5},{8,10},{10,8},{9,1... | collective-permute-start | bytes 393224 | tf_op jit(solution)/shard_map/ppermute | solution.py:329
  27.1 1.4 %collective-permute-start.10 = (bf16[256,256]{1,0:T(8,128)(2,1)S(1)}, bf16[256,256]{1,0:T(8,128)(2,1)S(1)}, u32[]{:S(2)}, u32[]{:S(2)}) collective-permute-start(bf16[256,256]{1,0:T(8,128)(2,1)S(1)} %pad_maximum_fusion.1), channel_id=1, source_target_pairs={{0,2},{2,0},{1,3},{3,1},{4,6},{6,4},{5,7},{7,5},{8,10},{10,8},{9,1... | collective-permute-start | bytes 393224 | tf_op jit(solution)/shard_map/ppermute | solution.py:329
  34.7 4.0 %collective-permute-start.12 = (bf16[32,512]{1,0:T(8,128)(2,1)S(1)}, bf16[32,512]{1,0:T(8,128)(2,1)S(1)}, u32[]{:S(2)}, u32[]{:S(2)}) collective-permute-start(bf16[32,512]{1,0:T(8,128)(2,1)S(1)} %get-tuple-element.25.refs_0_), channel_id=1, source_target_pairs={{0,1},{1,0},{4,5},{5,4},{2,3},{3,2},{6,7},{7,6},{8,9},{9,8},{12,13... | collective-permute-start | bytes 98312 | tf_op jit(solution)/shard_map/ppermute | solution.py:368
  36.3 5.1 %collective-permute-start.13 = (bf16[32,512]{1,0:T(8,128)(2,1)S(1)}, bf16[32,512]{1,0:T(8,128)(2,1)S(1)}, u32[]{:S(2)}, u32[]{:S(2)}) collective-permute-start(bf16[32,512]{1,0:T(8,128)(2,1)S(1)} %get-tuple-element.26), channel_id=1, source_target_pairs={{0,5},{1,4},{4,1},{5,0},{2,7},{3,6},{6,3},{7,2},{8,13},{9,12},{12,... | collective-permute-start | bytes 98312 | tf_op jit(solution)/shard_map/ppermute | solution.py:368
  37.7 3.9 %collective-permute-start.11 = (bf16[32,512]{1,0:T(8,128)(2,1)S(1)}, bf16[32,512]{1,0:T(8,128)(2,1)S(1)}, u32[]{:S(2)}, u32[]{:S(2)}) collective-permute-start(bf16[32,512]{1,0:T(8,128)(2,1)S(1)} %get-tuple-element.26), channel_id=1, source_target_pairs={{0,4},{1,5},{4,0},{5,1},{2,6},{3,7},{6,2},{7,3},{8,12},{9,13},{12,... | collective-permute-start | bytes 98312 | tf_op jit(solution)/shard_map/ppermute | solution.py:368

commit v12 on v11

--- a/solution.py
+++ b/solution.py
@@ -39,18 +39,18 @@
 
     def fetch_patch(block, side):
         for quarter in range(2):
-            first = (core ^ side) * half + (parity ^ quarter) * width
+            first = (column ^ side) * half + (parity ^ quarter) * width
             fetch(
-                patch_hbm.at[column ^ block, :, pl.ds(pl.multiple_of(first, width), width)],
+                patch_hbm.at[core ^ block, :, pl.ds(pl.multiple_of(first, width), width)],
                 patch.at[block, side, :, quarter * width : (quarter + 1) * width],
             )
 
-    fetch(cot_hbm.at[column ^ 1], cot.at[1])
+    fetch(cot_hbm.at[core ^ 1], cot.at[1])
     fetch_patch(1, 1)
     needed = len(copies)
+    fetch(cot_hbm.at[core], cot.at[0])
+    fetch_patch(0, 1)
     fetch_patch(1, 0)
-    fetch(cot_hbm.at[column], cot.at[0])
-    fetch_patch(0, 1)
     fetch_patch(0, 0)
     for copy in copies[:needed]:
         copy.wait()
@@ -134,8 +134,8 @@
 
 
 def root_kernel(most, counts_hbm, *refs):
-    pieces = refs[:6]
-    keep_ref, send_ref, grad, left, right, m_left, m_right, s_left, s_right, counts, sem = refs[6:]
+    pieces = refs[:8]
+    keep_ref, send_ref, grad, left, right, m_left, m_right, s_left, s_right, counts, sem = refs[8:]
     counts_copy = pltpu.make_async_copy(counts_hbm, counts, sem)
     counts_copy.start()
     width = grad.shape[0]
@@ -143,12 +143,10 @@
     rows = keep_ref.shape[0]
     low, high = slice(0, half), slice(half, width)
     place, column, core = (lax.axis_index(name) for name in ("z", "x", "core"))
-    for index in range(2):
-        own, other, far = pieces[3 * index : 3 * index + 3]
-        columns = slice(half * index, half * (index + 1))
-        grad[:quarter, columns] = own[...]
-        grad[quarter:half, columns] = other[...]
-        grad[half:, columns] = far[...]
+    for index, piece in enumerate(pieces):
+        column_half, part = index // 4, index % 4
+        columns = slice(half * column_half, half * (column_half + 1))
+        grad[quarter * part : quarter * (part + 1), columns] = piece[...]
     diagonal = lax.broadcasted_iota(jnp.int32, (half, half), 0) == lax.broadcasted_iota(
         jnp.int32, (half, half), 1
     )
@@ -177,9 +175,9 @@
         return tiles[0] + tenth, tiles[1], tiles[2] + tenth
 
     def spot(flip):
-        row = (4 * place + 2 * (column ^ flip) + core) * rows
+        row = (4 * place + 2 * column + (core ^ flip)) * rows
         part = row // quarter
-        return ((part // 2 ^ core) * 2 + (part % 2 ^ place % 2)) * quarter + row % quarter
+        return ((part // 2 ^ column) * 2 + (part % 2 ^ place % 2)) * quarter + row % quarter
 
     line = lax.broadcasted_iota(jnp.int32, (2 * rows, width), 0)
     wanted = jnp.where(line < rows, spot(0) + line, spot(1) + line - rows)
@@ -211,7 +209,7 @@
         return dot(ref[low, :], ref[:, low]), by_high[low], by_high[high]
 
     counts_copy.wait()
-    count_left, count_right = counts[column, 0], counts[column, 1]
+    count_left, count_right = counts[core, 0], counts[core, 1]
     for index in range(1, most):
         q_left, q_right = left.at[picked:, :], right.at[width:, :]
         if index == 1:
@@ -278,7 +276,7 @@
     return pl.pallas_call(
         functools.partial(root_kernel, most),
         out_shape=[out, out],
-        in_specs=[HBM] + [VMEM] * 6,
+        in_specs=[HBM] + [VMEM] * 8,
         out_specs=[VMEM] * 2,
         scratch_shapes=[
             square,
@@ -297,10 +295,10 @@
 
 def place_kernel(*refs):
     *pieces, out, sems = refs
-    column, group = lax.axis_index("x"), lax.axis_index("group")
+    core, group = lax.axis_index("core"), lax.axis_index("group")
     copies = []
     for index, piece in enumerate(pieces):
-        number = 2 * (group ^ (index // 2)) + (column ^ (index % 2))
+        number = 2 * (group ^ (index // 2)) + (core ^ (index % 2))
         copies.append(pltpu.make_async_copy(piece, out.at[number], sems.at[index]))
         copies[-1].start()
     for copy in copies:
@@ -334,7 +332,7 @@
 
     given, patch, cot = load(scale, patches, cotangents)
     came = swap(given, "core")
-    kept, given_on = sums(scale, patch, cot, (), (1, 0, F32), (0, 1, BF16))
+    kept, given_on = sums(scale, patch, cot, (), (0, 1, F32), (1, 0, BF16))
     came_on = swap(given_on, "core")
     leaving = add(kept, came).astype(BF16)
     to_diagonal, to_column = leaving[quarter:], leaving[:quarter]
@@ -351,9 +349,7 @@
             own = add(own, swap(send, "z", mask))
             send = own.astype(BF16)
             mask *= 2
-        own = send
-        other = swap(own, "z")
-        pieces += [own, other, swap(jnp.concatenate([own, other], 0), "core")]
+        pieces += [send, swap(send, "z"), swap(send, "x"), swap_diagonal(send)]
     keep, send = root(newton_counts, pieces, rows)
 
     pieces = []
@@ -365,7 +361,7 @@
                 for g in range(groups)
             ]
             piece = send if flip else keep
-            pieces.append(lax.ppermute(piece, ("x", "group"), moves) if turn or flip else piece)
+            pieces.append(lax.ppermute(piece, ("core", "group"), moves) if turn or flip else piece)
     return place(pieces)
 
 

time: 42.4 us -> 43.9 us (1.035)
  starting transfers between devices: 16 us -> 18.8 us
  waiting for transfers between devices: 16.7 us -> 15.5 us
    ppermute x1 -> x3, starting transfers between devices: 1.55 us -> 7.89 us  [swap_diagonal(): return lax.ppermute(array, ('z', 'x'), moves)]
    ppermute x10, starting transfers between devices: 10.9 us -> 8.66 us  [swap(): lax.ppermute(array, axis, [(i, i ^ mask) for i in range(lax.axis_size(axi...]
    ppermute x10, waiting for transfers between devices: 11.9 us -> 9.81 us  [swap(): lax.ppermute(array, axis, [(i, i ^ mask) for i in range(lax.axis_size(axi...]
    ppermute x1 -> x3, waiting for transfers between devices: 1.4 us -> 2.94 us  [swap_diagonal(): return lax.ppermute(array, ('z', 'x'), moves)]
    ppermute x3, starting transfers between devices: 3.55 us -> 2.21 us  [shards(): lax.ppermute(piece, ('core', 'group'), moves)]
    ppermute x3, waiting for transfers between devices: 3.38 us -> 2.72 us  [shards(): lax.ppermute(piece, ('core', 'group'), moves)]
  transfers between devices with their start and end apart: 14 -> 16, of which waited for: 11 -> 11; matrix products, arithmetic and copies ran while one was open for 1% -> 0% of each run, Pallas kernels for 2% -> 2%
where the time goes in v12:
time: 43.9 us; the launch traced here: 43.7 us
  starting transfers between devices  18.8 us (43%)
  waiting for transfers between devices  15.5 us (35%)
  Pallas kernels  9.2 us (21%)
    ppermute x10, waiting for transfers between devices, swap(): lax.ppermute(array, axis, [(i, i ^ mask) for i in range(lax.axis_size(axi...  9.81 us
    ppermute x10, starting transfers between devices, swap(): lax.ppermute(array, axis, [(i, i ^ mask) for i in range(lax.axis_size(axi...  8.66 us
    ppermute x3, starting transfers between devices, swap_diagonal(): return lax.ppermute(array, ('z', 'x'), moves)  7.89 us
    pallas_call x1, Pallas kernels, root(): pl.pallas_call(functools.partial(root_kernel, most), out_shape=[out, out]...  6.07 us
    ppermute x3, waiting for transfers between devices, swap_diagonal(): return lax.ppermute(array, ('z', 'x'), moves)  2.94 us
    ppermute x3, waiting for transfers between devices, shards(): lax.ppermute(piece, ('core', 'group'), moves)  2.72 us
    ppermute x3, starting transfers between devices, shards(): lax.ppermute(piece, ('core', 'group'), moves)  2.21 us
    pallas_call x1, Pallas kernels, load(): pl.pallas_call(functools.partial(load_kernel, scale), out_shape=[jax.Shap...  1.61 us
  transfers between devices with their start and end apart: 16, of which 11 were waited for; matrix products, arithmetic and copies ran while one was open for 0% of the time, Pallas kernels for 2%

profile of v12, /device:TPU:0, one launch (start us, length us, event | category | flops | bytes accessed | tf_op | source)
XLA Modules:
  0.0 43.7 jit_solution(9557193594413650437)
XLA Ops:
  0.0 1.6 %shard_map.37 = (bf16[256,512]{1,0:T(8,128)(2,1)S(1)}, bf16[2,2,512,256]{3,2,1,0:T(8,128)(2,1)S(1)}, bf16[2,512,512]{2,1,0:T(8,128)(2,1)S(1)}) custom-call(bf16[2,512,512]{2,1,0:T(8,128)(2,1)} %patch_hbm.1, bf16[2,512,512]{2,1,0:T(8,128)(2,1)} %cot_hbm.1), custom_call_target="tpu_custom_call" | custom-call | tf_op jit(solution)/shard_map/pallas_call | solution.py:65
  1.6 0.5 %collective-permute-start = (bf16[256,512]{1,0:T(8,128)(2,1)S(1)}, bf16[256,512]{1,0:T(8,128)(2,1)S(1)}, u32[]{:S(2)}, u32[]{:S(2)}) collective-permute-start(bf16[256,512]{1,0:T(8,128)(2,1)S(1)} %get-tuple-element.19), channel_id=1, source_target_pairs={{0,2},{2,0},{1,3},{3,1},{4,6},{6,4},{5,7},{7,5},{8,10},{10,8},{9,1... | collective-permute-start | bytes 786440 | tf_op jit(solution)/shard_map/ppermute | solution.py:327
  2.1 0.5 %shard_map.38 = (f32[256,512]{1,0:T(8,128)S(1)}, bf16[256,512]{1,0:T(8,128)(2,1)S(1)}) custom-call(bf16[2,2,512,256]{3,2,1,0:T(8,128)(2,1)S(1)} %get-tuple-element.16.patch, bf16[2,512,512]{2,1,0:T(8,128)(2,1)S(1)} %get-tuple-element.17.cot), custom_call_target="tpu_custom_call" | custom-call | flops 268435456 | bytes 1048576 | tf_op jit(solution)/shard_map/pallas_call | solution.py:89
  2.6 0.1 collective-permute-start.1
  2.7 0.6 %collective-permute-done = bf16[256,512]{1,0:T(8,128)(2,1)S(1)} collective-permute-done((bf16[256,512]{1,0:T(8,128)(2,1)S(1)}, bf16[256,512]{1,0:T(8,128)(2,1)S(1)}, u32[]{:S(2)}, u32[]{:S(2)}) %collective-permute-start) | collective-permute-done | bytes 262176 | tf_op jit(solution)/shard_map/ppermute | solution.py:327
  3.3 0.1 add_convert_fusion
  3.4 2.9 %collective-permute-start.3 = (bf16[128,512]{1,0:T(8,128)(2,1)S(1)}, bf16[128,512]{1,0:T(8,128)(2,1)S(1)}, u32[]{:S(2)}, u32[]{:S(2)}) collective-permute-start(bf16[128,512]{1,0:T(8,128)(2,1)S(1)} %get-tuple-element.27), channel_id=1, source_target_pairs={{0,4},{4,0},{1,5},{5,1},{2,6},{6,2},{3,7},{7,3},{8,12},{12,8},{9,1... | collective-permute-start | bytes 393224 | tf_op jit(solution)/shard_map/ppermute | solution.py:327
  6.3 1.5 %collective-permute-start.2 = (bf16[128,512]{1,0:T(8,128)(2,1)S(1)}, bf16[128,512]{1,0:T(8,128)(2,1)S(1)}, u32[]{:S(2)}, u32[]{:S(2)}) collective-permute-start(bf16[128,512]{1,0:T(8,128)(2,1)S(1)} %get-tuple-element.28.refs_0_), channel_id=1, source_target_pairs={{0,12},{4,8},{8,4},{12,0},{16,28},{20,24},{24,20},{28,16},{1,13},{... | collective-permute-start | bytes 393224 | tf_op jit(solution)/shard_map/ppermute | solution.py:331
  7.9 0.3 shard_map.39
  8.2 0.0 collective-permute-done.1
  8.2 0.1 convert_add_fusion.own
  8.3 0.1 collective-permute-start.4
  8.4 3.8 %collective-permute-done.3.refs_1_ = bf16[128,512]{1,0:T(8,128)(2,1)S(1)} collective-permute-done((bf16[128,512]{1,0:T(8,128)(2,1)S(1)}, bf16[128,512]{1,0:T(8,128)(2,1)S(1)}, u32[]{:S(2)}, u32[]{:S(2)}) %collective-permute-start.3) | collective-permute-done | bytes 131104 | tf_op jit(solution)/shard_map/ppermute | solution.py:327
  12.2 1.4 %collective-permute-done.2.refs_0_ = bf16[128,512]{1,0:T(8,128)(2,1)S(1)} collective-permute-done((bf16[128,512]{1,0:T(8,128)(2,1)S(1)}, bf16[128,512]{1,0:T(8,128)(2,1)S(1)}, u32[]{:S(2)}, u32[]{:S(2)}) %collective-permute-start.2) | collective-permute-done | bytes 131104 | tf_op jit(solution)/shard_map/ppermute | solution.py:331
  13.6 0.6 %collective-permute-done.4.refs_2_ = bf16[128,512]{1,0:T(8,128)(2,1)S(1)} collective-permute-done((bf16[128,512]{1,0:T(8,128)(2,1)S(1)}, bf16[128,512]{1,0:T(8,128)(2,1)S(1)}, u32[]{:S(2)}, u32[]{:S(2)}) %collective-permute-start.4) | collective-permute-done | bytes 131104 | tf_op jit(solution)/shard_map/ppermute | solution.py:327
  14.3 0.1 shard_map.40
  14.3 2.8 %collective-permute-start.5 = (bf16[128,256]{1,0:T(8,128)(2,1)S(1)}, bf16[128,256]{1,0:T(8,128)(2,1)S(1)}, u32[]{:S(2)}, u32[]{:S(2)}) collective-permute-start(bf16[128,256]{1,0:T(8,128)(2,1)S(1)} %get-tuple-element.22), channel_id=1, source_target_pairs={{0,16},{8,24},{16,0},{24,8},{1,17},{9,25},{17,1},{25,9},{2,18},{10... | collective-permute-start | bytes 196616 | tf_op jit(solution)/shard_map/ppermute | solution.py:327
  17.1 0.2 collective-permute-start.9
  17.3 2.5 %collective-permute-done.5 = bf16[128,256]{1,0:T(8,128)(2,1)S(1)} collective-permute-done((bf16[128,256]{1,0:T(8,128)(2,1)S(1)}, bf16[128,256]{1,0:T(8,128)(2,1)S(1)}, u32[]{:S(2)}, u32[]{:S(2)}) %collective-permute-start.5) | collective-permute-done | bytes 65568 | tf_op jit(solution)/shard_map/ppermute | solution.py:327
  19.9 3.8 %collective-permute-start.8 = (bf16[128,256]{1,0:T(8,128)(2,1)S(1)}, bf16[128,256]{1,0:T(8,128)(2,1)S(1)}, u32[]{:S(2)}, u32[]{:S(2)}) collective-permute-start(bf16[128,256]{1,0:T(8,128)(2,1)S(1)} %add_convert_fusion.2.refs_0_), channel_id=1, source_target_pairs={{0,12},{4,8},{8,4},{12,0},{16,28},{20,24},{24,20},{28,16},{1,13},{... | collective-permute-start | bytes 196616 | tf_op jit(solution)/shard_map/ppermute | solution.py:331
  23.6 0.5 %collective-permute-start.7 = (bf16[128,256]{1,0:T(8,128)(2,1)S(1)}, bf16[128,256]{1,0:T(8,128)(2,1)S(1)}, u32[]{:S(2)}, u32[]{:S(2)}) collective-permute-start(bf16[128,256]{1,0:T(8,128)(2,1)S(1)} %add_convert_fusion.2.refs_0_), channel_id=1, source_target_pairs={{0,4},{4,0},{1,5},{5,1},{2,6},{6,2},{3,7},{7,3},{8,12},{12,8},{9,1... | collective-permute-start | bytes 196616 | tf_op jit(solution)/shard_map/ppermute | solution.py:327
  24.2 0.5 %collective-permute-start.6 = (bf16[128,256]{1,0:T(8,128)(2,1)S(1)}, bf16[128,256]{1,0:T(8,128)(2,1)S(1)}, u32[]{:S(2)}, u32[]{:S(2)}) collective-permute-start(bf16[128,256]{1,0:T(8,128)(2,1)S(1)} %add_convert_fusion.2.refs_0_), channel_id=1, source_target_pairs={{0,8},{8,0},{16,24},{24,16},{1,9},{9,1},{17,25},{25,17},{2,10},{10... | collective-permute-start | bytes 196616 | tf_op jit(solution)/shard_map/ppermute | solution.py:327
  24.7 0.0 collective-permute-done.9
  24.7 2.6 %collective-permute-start.12 = (bf16[128,256]{1,0:T(8,128)(2,1)S(1)}, bf16[128,256]{1,0:T(8,128)(2,1)S(1)}, u32[]{:S(2)}, u32[]{:S(2)}) collective-permute-start(bf16[128,256]{1,0:T(8,128)(2,1)S(1)} %add_convert_fusion.1.refs_4_), channel_id=1, source_target_pairs={{0,12},{4,8},{8,4},{12,0},{16,28},{20,24},{24,20},{28,16},{1,13},{... | collective-permute-start | bytes 196616 | tf_op jit(solution)/shard_map/ppermute | solution.py:331
  27.2 0.5 %collective-permute-start.11 = (bf16[128,256]{1,0:T(8,128)(2,1)S(1)}, bf16[128,256]{1,0:T(8,128)(2,1)S(1)}, u32[]{:S(2)}, u32[]{:S(2)}) collective-permute-start(bf16[128,256]{1,0:T(8,128)(2,1)S(1)} %add_convert_fusion.1.refs_4_), channel_id=1, source_target_pairs={{0,4},{4,0},{1,5},{5,1},{2,6},{6,2},{3,7},{7,3},{8,12},{12,8},{9,1... | collective-permute-start | bytes 196616 | tf_op jit(solution)/shard_map/ppermute | solution.py:327
  27.8 0.0 collective-permute-done.8.refs_3_
  27.8 0.5 %collective-permute-start.10 = (bf16[128,256]{1,0:T(8,128)(2,1)S(1)}, bf16[128,256]{1,0:T(8,128)(2,1)S(1)}, u32[]{:S(2)}, u32[]{:S(2)}) collective-permute-start(bf16[128,256]{1,0:T(8,128)(2,1)S(1)} %add_convert_fusion.1.refs_4_), channel_id=1, source_target_pairs={{0,8},{8,0},{16,24},{24,16},{1,9},{9,1},{17,25},{25,17},{2,10},{10... | collective-permute-start | bytes 196616 | tf_op jit(solution)/shard_map/ppermute | solution.py:327
  28.2 0.0 collective-permute-done.7.refs_2_
  28.2 0.3 collective-permute-done.6.refs_1_
  28.5 1.5 %collective-permute-done.12.refs_7_ = bf16[128,256]{1,0:T(8,128)(2,1)S(1)} collective-permute-done((bf16[128,256]{1,0:T(8,128)(2,1)S(1)}, bf16[128,256]{1,0:T(8,128)(2,1)S(1)}, u32[]{:S(2)}, u32[]{:S(2)}) %collective-permute-start.12) | collective-permute-done | bytes 65568 | tf_op jit(solution)/shard_map/ppermute | solution.py:331
  30.1 1.4 %collective-permute-done.11.refs_6_ = bf16[128,256]{1,0:T(8,128)(2,1)S(1)} collective-permute-done((bf16[128,256]{1,0:T(8,128)(2,1)S(1)}, bf16[128,256]{1,0:T(8,128)(2,1)S(1)}, u32[]{:S(2)}, u32[]{:S(2)}) %collective-permute-start.11) | collective-permute-done | bytes 65568 | tf_op jit(solution)/shard_map/ppermute | solution.py:327
  31.5 0.5 %collective-permute-done.10.refs_5_ = bf16[128,256]{1,0:T(8,128)(2,1)S(1)} collective-permute-done((bf16[128,256]{1,0:T(8,128)(2,1)S(1)}, bf16[128,256]{1,0:T(8,128)(2,1)S(1)}, u32[]{:S(2)}, u32[]{:S(2)}) %collective-permute-start.10) | collective-permute-done | bytes 65568 | tf_op jit(solution)/shard_map/ppermute | solution.py:327
  32.0 6.1 %shard_map.41 = (bf16[32,512]{1,0:T(8,128)(2,1)S(1)}, bf16[32,512]{1,0:T(8,128)(2,1)S(1)}) custom-call(s32[2,2]{1,0:T(2,128)} %counts_hbm.1, bf16[128,256]{1,0:T(8,128)(2,1)S(1)} %add_convert_fusion.2.refs_0_, bf16[128,256]{1,0:T(8,128)(2,1)S(1)} %collective-permute-done.6.refs_1_, bf16[128,256]{1,0:T(8,128)(2,1)S(1)} %collective-permute-done.7.refs_2_, ...), custom_call_target="tpu_custom_call" | custom-call | tf_op jit(solution)/shard_map/pallas_call | solution.py:276
  38.1 1.6 %collective-permute-start.14 = (bf16[32,512]{1,0:T(8,128)(2,1)S(1)}, bf16[32,512]{1,0:T(8,128)(2,1)S(1)}, u32[]{:S(2)}, u32[]{:S(2)}) collective-permute-start(bf16[32,512]{1,0:T(8,128)(2,1)S(1)} %get-tuple-element.25.refs_0_), channel_id=1, source_target_pairs={{0,1},{1,0},{2,3},{3,2},{4,5},{5,4},{6,7},{7,6},{8,9},{9,8},{10,11... | collective-permute-start | bytes 98312 | tf_op jit(solution)/shard_map/ppermute | solution.py:364
  39.7 0.0 collective-permute-start.15
  39.7 0.6 %collective-permute-start.13 = (bf16[32,512]{1,0:T(8,128)(2,1)S(1)}, bf16[32,512]{1,0:T(8,128)(2,1)S(1)}, u32[]{:S(2)}, u32[]{:S(2)}) collective-permute-start(bf16[32,512]{1,0:T(8,128)(2,1)S(1)} %get-tuple-element.26), channel_id=1, source_target_pairs={{0,2},{1,3},{2,0},{3,1},{4,6},{5,7},{6,4},{7,5},{8,10},{9,11},{10,... | collective-permute-start | bytes 98312 | tf_op jit(solution)/shard_map/ppermute | solution.py:364
  40.3 1.8 %collective-permute-done.14.refs_2_ = bf16[32,512]{1,0:T(8,128)(2,1)S(1)} collective-permute-done((bf16[32,512]{1,0:T(8,128)(2,1)S(1)}, bf16[32,512]{1,0:T(8,128)(2,1)S(1)}, u32[]{:S(2)}, u32[]{:S(2)}) %collective-permute-start.14) | collective-permute-done | bytes 32800 | tf_op jit(solution)/shard_map/ppermute | solution.py:364
  42.1 0.9 %collective-permute-done.15.refs_3_ = bf16[32,512]{1,0:T(8,128)(2,1)S(1)} collective-permute-done((bf16[32,512]{1,0:T(8,128)(2,1)S(1)}, bf16[32,512]{1,0:T(8,128)(2,1)S(1)}, u32[]{:S(2)}, u32[]{:S(2)}) %collective-permute-start.15) | collective-permute-done | bytes 32800 | tf_op jit(solution)/shard_map/ppermute | solution.py:364
  43.0 0.0 collective-permute-done.13.refs_1_
  43.0 0.7 %shard_map.42 = bf16[4,32,512]{2,1,0:T(8,128)(2,1)} custom-call(bf16[32,512]{1,0:T(8,128)(2,1)S(1)} %get-tuple-element.25.refs_0_, bf16[32,512]{1,0:T(8,128)(2,1)S(1)} %collective-permute-done.13.refs_1_, bf16[32,512]{1,0:T(8,128)(2,1)S(1)} %collective-permute-done.14.refs_2_, bf16[32,512]{1,0:T(8,128)(2,1)S(1)} %collective-permute-done.15.refs_3_), custom_call_target="tpu_custom_call" | custom-call | tf_op jit(solution)/shard_map/pallas_call | solution.py:310
  (4 shorter events, 0.1 us)
Async XLA Ops:
  1.6 1.7 %collective-permute-start = (bf16[256,512]{1,0:T(8,128)(2,1)S(1)}, bf16[256,512]{1,0:T(8,128)(2,1)S(1)}, u32[]{:S(2)}, u32[]{:S(2)}) collective-permute-start(bf16[256,512]{1,0:T(8,128)(2,1)S(1)} %get-tuple-element.19), channel_id=1, source_target_pairs={{0,2},{2,0},{1,3},{3,1},{4,6},{6,4},{5,7},{7,5},{8,10},{10,8},{9,1... | collective-permute-start | bytes 786440 | tf_op jit(solution)/shard_map/ppermute | solution.py:327
  2.6 5.6 %collective-permute-start.1 = (bf16[256,512]{1,0:T(8,128)(2,1)S(1)}, bf16[256,512]{1,0:T(8,128)(2,1)S(1)}, u32[]{:S(2)}, u32[]{:S(2)}) collective-permute-start(bf16[256,512]{1,0:T(8,128)(2,1)S(1)} %get-tuple-element.20), channel_id=1, source_target_pairs={{0,2},{2,0},{1,3},{3,1},{4,6},{6,4},{5,7},{7,5},{8,10},{10,8},{9,1... | collective-permute-start | bytes 786440 | tf_op jit(solution)/shard_map/ppermute | solution.py:327
  3.4 8.8 %collective-permute-start.3 = (bf16[128,512]{1,0:T(8,128)(2,1)S(1)}, bf16[128,512]{1,0:T(8,128)(2,1)S(1)}, u32[]{:S(2)}, u32[]{:S(2)}) collective-permute-start(bf16[128,512]{1,0:T(8,128)(2,1)S(1)} %get-tuple-element.27), channel_id=1, source_target_pairs={{0,4},{4,0},{1,5},{5,1},{2,6},{6,2},{3,7},{7,3},{8,12},{12,8},{9,1... | collective-permute-start | bytes 393224 | tf_op jit(solution)/shard_map/ppermute | solution.py:327
  6.3 7.3 %collective-permute-start.2 = (bf16[128,512]{1,0:T(8,128)(2,1)S(1)}, bf16[128,512]{1,0:T(8,128)(2,1)S(1)}, u32[]{:S(2)}, u32[]{:S(2)}) collective-permute-start(bf16[128,512]{1,0:T(8,128)(2,1)S(1)} %get-tuple-element.28.refs_0_), channel_id=1, source_target_pairs={{0,12},{4,8},{8,4},{12,0},{16,28},{20,24},{24,20},{28,16},{1,13},{... | collective-permute-start | bytes 393224 | tf_op jit(solution)/shard_map/ppermute | solution.py:331
  8.3 6.0 %collective-permute-start.4 = (bf16[128,512]{1,0:T(8,128)(2,1)S(1)}, bf16[128,512]{1,0:T(8,128)(2,1)S(1)}, u32[]{:S(2)}, u32[]{:S(2)}) collective-permute-start(bf16[128,512]{1,0:T(8,128)(2,1)S(1)} %slice.17), channel_id=1, source_target_pairs={{0,8},{8,0},{16,24},{24,16},{1,9},{9,1},{17,25},{25,17},{2,10},{10... | collective-permute-start | bytes 393224 | tf_op jit(solution)/shard_map/ppermute | solution.py:327
  14.3 5.5 %collective-permute-start.5 = (bf16[128,256]{1,0:T(8,128)(2,1)S(1)}, bf16[128,256]{1,0:T(8,128)(2,1)S(1)}, u32[]{:S(2)}, u32[]{:S(2)}) collective-permute-start(bf16[128,256]{1,0:T(8,128)(2,1)S(1)} %get-tuple-element.22), channel_id=1, source_target_pairs={{0,16},{8,24},{16,0},{24,8},{1,17},{9,25},{17,1},{25,9},{2,18},{10... | collective-permute-start | bytes 196616 | tf_op jit(solution)/shard_map/ppermute | solution.py:327
  17.1 7.5 %collective-permute-start.9 = (bf16[128,256]{1,0:T(8,128)(2,1)S(1)}, bf16[128,256]{1,0:T(8,128)(2,1)S(1)}, u32[]{:S(2)}, u32[]{:S(2)}) collective-permute-start(bf16[128,256]{1,0:T(8,128)(2,1)S(1)} %get-tuple-element.24), channel_id=1, source_target_pairs={{0,16},{8,24},{16,0},{24,8},{1,17},{9,25},{17,1},{25,9},{2,18},{10... | collective-permute-start | bytes 196616 | tf_op jit(solution)/shard_map/ppermute | solution.py:327
  19.9 7.9 %collective-permute-start.8 = (bf16[128,256]{1,0:T(8,128)(2,1)S(1)}, bf16[128,256]{1,0:T(8,128)(2,1)S(1)}, u32[]{:S(2)}, u32[]{:S(2)}) collective-permute-start(bf16[128,256]{1,0:T(8,128)(2,1)S(1)} %add_convert_fusion.2.refs_0_), channel_id=1, source_target_pairs={{0,12},{4,8},{8,4},{12,0},{16,28},{20,24},{24,20},{28,16},{1,13},{... | collective-permute-start | bytes 196616 | tf_op jit(solution)/shard_map/ppermute | solution.py:331
  23.6 4.6 %collective-permute-start.7 = (bf16[128,256]{1,0:T(8,128)(2,1)S(1)}, bf16[128,256]{1,0:T(8,128)(2,1)S(1)}, u32[]{:S(2)}, u32[]{:S(2)}) collective-permute-start(bf16[128,256]{1,0:T(8,128)(2,1)S(1)} %add_convert_fusion.2.refs_0_), channel_id=1, source_target_pairs={{0,4},{4,0},{1,5},{5,1},{2,6},{6,2},{3,7},{7,3},{8,12},{12,8},{9,1... | collective-permute-start | bytes 196616 | tf_op jit(solution)/shard_map/ppermute | solution.py:327
  24.2 4.4 %collective-permute-start.6 = (bf16[128,256]{1,0:T(8,128)(2,1)S(1)}, bf16[128,256]{1,0:T(8,128)(2,1)S(1)}, u32[]{:S(2)}, u32[]{:S(2)}) collective-permute-start(bf16[128,256]{1,0:T(8,128)(2,1)S(1)} %add_convert_fusion.2.refs_0_), channel_id=1, source_target_pairs={{0,8},{8,0},{16,24},{24,16},{1,9},{9,1},{17,25},{25,17},{2,10},{10... | collective-permute-start | bytes 196616 | tf_op jit(solution)/shard_map/ppermute | solution.py:327
  24.7 5.4 %collective-permute-start.12 = (bf16[128,256]{1,0:T(8,128)(2,1)S(1)}, bf16[128,256]{1,0:T(8,128)(2,1)S(1)}, u32[]{:S(2)}, u32[]{:S(2)}) collective-permute-start(bf16[128,256]{1,0:T(8,128)(2,1)S(1)} %add_convert_fusion.1.refs_4_), channel_id=1, source_target_pairs={{0,12},{4,8},{8,4},{12,0},{16,28},{20,24},{24,20},{28,16},{1,13},{... | collective-permute-start | bytes 196616 | tf_op jit(solution)/shard_map/ppermute | solution.py:331
  27.2 4.3 %collective-permute-start.11 = (bf16[128,256]{1,0:T(8,128)(2,1)S(1)}, bf16[128,256]{1,0:T(8,128)(2,1)S(1)}, u32[]{:S(2)}, u32[]{:S(2)}) collective-permute-start(bf16[128,256]{1,0:T(8,128)(2,1)S(1)} %add_convert_fusion.1.refs_4_), channel_id=1, source_target_pairs={{0,4},{4,0},{1,5},{5,1},{2,6},{6,2},{3,7},{7,3},{8,12},{12,8},{9,1... | collective-permute-start | bytes 196616 | tf_op jit(solution)/shard_map/ppermute | solution.py:327
  27.8 4.3 %collective-permute-start.10 = (bf16[128,256]{1,0:T(8,128)(2,1)S(1)}, bf16[128,256]{1,0:T(8,128)(2,1)S(1)}, u32[]{:S(2)}, u32[]{:S(2)}) collective-permute-start(bf16[128,256]{1,0:T(8,128)(2,1)S(1)} %add_convert_fusion.1.refs_4_), channel_id=1, source_target_pairs={{0,8},{8,0},{16,24},{24,16},{1,9},{9,1},{17,25},{25,17},{2,10},{10... | collective-permute-start | bytes 196616 | tf_op jit(solution)/shard_map/ppermute | solution.py:327
  38.1 4.0 %collective-permute-start.14 = (bf16[32,512]{1,0:T(8,128)(2,1)S(1)}, bf16[32,512]{1,0:T(8,128)(2,1)S(1)}, u32[]{:S(2)}, u32[]{:S(2)}) collective-permute-start(bf16[32,512]{1,0:T(8,128)(2,1)S(1)} %get-tuple-element.25.refs_0_), channel_id=1, source_target_pairs={{0,1},{1,0},{2,3},{3,2},{4,5},{5,4},{6,7},{7,6},{8,9},{9,8},{10,11... | collective-permute-start | bytes 98312 | tf_op jit(solution)/shard_map/ppermute | solution.py:364
  39.7 3.3 %collective-permute-start.15 = (bf16[32,512]{1,0:T(8,128)(2,1)S(1)}, bf16[32,512]{1,0:T(8,128)(2,1)S(1)}, u32[]{:S(2)}, u32[]{:S(2)}) collective-permute-start(bf16[32,512]{1,0:T(8,128)(2,1)S(1)} %get-tuple-element.26), channel_id=1, source_target_pairs={{0,3},{1,2},{2,1},{3,0},{4,7},{5,6},{6,5},{7,4},{8,11},{9,10},{10,... | collective-permute-start | bytes 98312 | tf_op jit(solution)/shard_map/ppermute | solution.py:364
  39.7 3.3 %collective-permute-start.13 = (bf16[32,512]{1,0:T(8,128)(2,1)S(1)}, bf16[32,512]{1,0:T(8,128)(2,1)S(1)}, u32[]{:S(2)}, u32[]{:S(2)}) collective-permute-start(bf16[32,512]{1,0:T(8,128)(2,1)S(1)} %get-tuple-element.26), channel_id=1, source_target_pairs={{0,2},{1,3},{2,0},{3,1},{4,6},{5,7},{6,4},{7,5},{8,10},{9,11},{10,... | collective-permute-start | bytes 98312 | tf_op jit(solution)/shard_map/ppermute | solution.py:364

commit v13 on v11

--- a/solution.py
+++ b/solution.py
@@ -13,7 +13,6 @@
 SMEM = pl.BlockSpec(memory_space=pltpu.SMEM)
 HBM = pl.BlockSpec(memory_space=pltpu.HBM)
 ROWS_IN_COLS = (((0,), (0,)), ((), ()))
-COLS_IN_COLS = (((1,), (1,)), ((), ()))
 
 
 def params(limit):
@@ -102,10 +101,10 @@
 
 def collect_kernel(own, *refs):
     *came, keep_left, keep_right, send_left, send_right = refs
-    half = keep_left.shape[1]
+    split = keep_left.shape[1]
     for columns, keep, send in (
-        (slice(0, half), keep_left, send_left),
-        (slice(half, 2 * half), keep_right, send_right),
+        (slice(0, split), keep_left, send_left),
+        (slice(split, own.shape[1]), keep_right, send_right),
     ):
         total = own[: keep.shape[0], columns]
         for ref in came:
@@ -114,12 +113,13 @@
         send[...] = total.astype(BF16)
 
 
-def collect(own, *came):
+def collect(split, own, *came):
     rows, width = came[0].shape
-    shape = (rows, width // 2)
+    shapes = [(rows, split), (rows, width - split)]
     return pl.pallas_call(
         collect_kernel,
-        out_shape=[jax.ShapeDtypeStruct(shape, F32)] * 2 + [jax.ShapeDtypeStruct(shape, BF16)] * 2,
+        out_shape=[jax.ShapeDtypeStruct(shape, F32) for shape in shapes]
+        + [jax.ShapeDtypeStruct(shape, BF16) for shape in shapes],
         in_specs=[VMEM] * (1 + len(came)),
         out_specs=[VMEM] * 4,
         compiler_params=params(16),
@@ -135,7 +135,7 @@
 
 def root_kernel(most, counts_hbm, *refs):
     pieces = refs[:6]
-    keep_ref, send_ref, grad, left, right, m_left, m_right, s_left, s_right, counts, sem = refs[6:]
+    keep_ref, send_ref, grad, turned, left, right, m_left, m_right, s_left, s_right, counts, sem = refs[6:]
     counts_copy = pltpu.make_async_copy(counts_hbm, counts, sem)
     counts_copy.start()
     width = grad.shape[0]
@@ -143,12 +143,15 @@
     rows = keep_ref.shape[0]
     low, high = slice(0, half), slice(half, width)
     place, column, core = (lax.axis_index(name) for name in ("z", "x", "core"))
+    column_start = 0
     for index in range(2):
         own, other, far = pieces[3 * index : 3 * index + 3]
-        columns = slice(half * index, half * (index + 1))
+        columns = slice(column_start, column_start + own.shape[1])
+        column_start += own.shape[1]
         grad[:quarter, columns] = own[...]
         grad[quarter:half, columns] = other[...]
         grad[half:, columns] = far[...]
+    turned[...] = grad[...].T
     diagonal = lax.broadcasted_iota(jnp.int32, (half, half), 0) == lax.broadcasted_iota(
         jnp.int32, (half, half), 1
     )
@@ -168,10 +171,9 @@
         five = jnp.where(diagonal, 1.25, 0.0)
         return five - 0.25 * upper_left, -0.25 * upper_right, five - 0.25 * lower_right
 
-    def statistics(dims, upper, lower):
+    def statistics(first, second):
         tiles = [
-            lax.dot_general(a, b, dims, preferred_element_type=F32)
-            for a, b in ((upper, upper), (upper, lower), (lower, lower))
+            dot(first[a, :], second[:, b]) for a, b in ((low, low), (low, high), (high, high))
         ]
         tenth = jnp.where(diagonal, 0.1, 0.0)
         return tiles[0] + tenth, tiles[1], tiles[2] + tenth
@@ -186,8 +188,8 @@
     pick = lax.broadcasted_iota(jnp.int32, (2 * rows, width), 1) == wanted
     pick = jnp.where(pick, 1.0, 0.0).astype(BF16)
     picked = 2 * rows
-    stats_left = statistics(COLS_IN_COLS, grad[low, :], grad[high, :])
-    stats_right = statistics(ROWS_IN_COLS, grad[:, low], grad[:, high])
+    stats_left = statistics(grad, turned)
+    stats_right = statistics(turned, grad)
     squares = [tile * tile for tile in stats_left]
     norm = jnp.sqrt(jnp.sum(squares[0] + 2.0 * squares[1] + squares[2], keepdims=True))
     scale = 2.5 / norm
@@ -282,6 +284,7 @@
         out_specs=[VMEM] * 2,
         scratch_shapes=[
             square,
+            square,
             pltpu.VMEM((2 * rows + width, width), BF16),
             pltpu.VMEM((2 * width, width), BF16),
             square,
@@ -343,7 +346,9 @@
     (kept_on,) = sums(scale, patch, cot, (to_diagonal,), (0, 0, F32))
     own = add(kept_on, came_on)
     from_line = swap(own[quarter:].astype(BF16), "z")
-    left, right, send_left, send_right = collect(own, from_diagonal, from_column, from_line)
+    left, right, send_left, send_right = collect(
+        width * 3 // 4, own, from_diagonal, from_column, from_line
+    )
     pieces = []
     for own, send in ((left, send_left), (right, send_right)):
         mask = 2

time: 42.4 us -> 42.3 us (level)
  starting transfers between devices: 16 us -> 14.3 us
  waiting for transfers between devices: 16.7 us -> 18.2 us
    ppermute x10, starting transfers between devices: 10.9 us -> 9.2 us  [swap(): lax.ppermute(array, axis, [(i, i ^ mask) for i in range(lax.axis_size(axi...]
    ppermute x10, waiting for transfers between devices: 11.9 us -> 13.5 us  [swap(): lax.ppermute(array, axis, [(i, i ^ mask) for i in range(lax.axis_size(axi...]
where the time goes in v13:
time: 42.3 us; the launch traced here: 42.1 us
  waiting for transfers between devices  18.2 us (43%)
  starting transfers between devices  14.3 us (34%)
  Pallas kernels  9.29 us (22%)
    ppermute x10, waiting for transfers between devices, swap(): lax.ppermute(array, axis, [(i, i ^ mask) for i in range(lax.axis_size(axi...  13.5 us
    ppermute x10, starting transfers between devices, swap(): lax.ppermute(array, axis, [(i, i ^ mask) for i in range(lax.axis_size(axi...  9.2 us
    pallas_call x1, Pallas kernels, root(): pl.pallas_call(functools.partial(root_kernel, most), out_shape=[out, out]...  6.15 us
    ppermute x3, starting transfers between devices, shards(): lax.ppermute(piece, ('x', 'group'), moves)  3.55 us
    ppermute x3, waiting for transfers between devices, shards(): lax.ppermute(piece, ('x', 'group'), moves)  3.26 us
    pallas_call x1, Pallas kernels, load(): pl.pallas_call(functools.partial(load_kernel, scale), out_shape=[jax.Shap...  1.61 us
    ppermute x1, starting transfers between devices, swap_diagonal(): return lax.ppermute(array, ('z', 'x'), moves)  1.55 us
    ppermute x1, waiting for transfers between devices, swap_diagonal(): return lax.ppermute(array, ('z', 'x'), moves)  1.4 us
  transfers between devices with their start and end apart: 14, of which 11 were waited for; matrix products, arithmetic and copies ran while one was open for 1% of the time, Pallas kernels for 2%

profile of v13, /device:TPU:0, one launch (start us, length us, event | category | flops | bytes accessed | tf_op | source)
XLA Modules:
  0.0 42.1 jit_solution(16400011811437975057)
XLA Ops:
  0.0 1.6 %shard_map.37 = (bf16[256,512]{1,0:T(8,128)(2,1)S(1)}, bf16[2,2,512,256]{3,2,1,0:T(8,128)(2,1)S(1)}, bf16[2,512,512]{2,1,0:T(8,128)(2,1)S(1)}) custom-call(bf16[2,512,512]{2,1,0:T(8,128)(2,1)} %patch_hbm.1, bf16[2,512,512]{2,1,0:T(8,128)(2,1)} %cot_hbm.1), custom_call_target="tpu_custom_call" | custom-call | tf_op jit(solution)/shard_map/pallas_call | solution.py:64
  1.6 0.5 %collective-permute-start = (bf16[256,512]{1,0:T(8,128)(2,1)S(1)}, bf16[256,512]{1,0:T(8,128)(2,1)S(1)}, u32[]{:S(2)}, u32[]{:S(2)}) collective-permute-start(bf16[256,512]{1,0:T(8,128)(2,1)S(1)} %get-tuple-element.19), channel_id=1, source_target_pairs={{0,2},{2,0},{1,3},{3,1},{4,6},{6,4},{5,7},{7,5},{8,10},{10,8},{9,1... | collective-permute-start | bytes 786440 | tf_op jit(solution)/shard_map/ppermute | solution.py:332
  2.1 0.5 %shard_map.38 = (f32[256,512]{1,0:T(8,128)S(1)}, bf16[256,512]{1,0:T(8,128)(2,1)S(1)}) custom-call(bf16[2,2,512,256]{3,2,1,0:T(8,128)(2,1)S(1)} %get-tuple-element.16.patch, bf16[2,512,512]{2,1,0:T(8,128)(2,1)S(1)} %get-tuple-element.17.cot), custom_call_target="tpu_custom_call" | custom-call | flops 268435456 | bytes 1048576 | tf_op jit(solution)/shard_map/pallas_call | solution.py:88
  2.6 0.1 collective-permute-start.1
  2.7 0.6 %collective-permute-done = bf16[256,512]{1,0:T(8,128)(2,1)S(1)} collective-permute-done((bf16[256,512]{1,0:T(8,128)(2,1)S(1)}, bf16[256,512]{1,0:T(8,128)(2,1)S(1)}, u32[]{:S(2)}, u32[]{:S(2)}) %collective-permute-start) | collective-permute-done | bytes 262176 | tf_op jit(solution)/shard_map/ppermute | solution.py:332
  3.3 0.1 add_convert_fusion
  3.4 2.9 %collective-permute-start.3 = (bf16[128,512]{1,0:T(8,128)(2,1)S(1)}, bf16[128,512]{1,0:T(8,128)(2,1)S(1)}, u32[]{:S(2)}, u32[]{:S(2)}) collective-permute-start(bf16[128,512]{1,0:T(8,128)(2,1)S(1)} %get-tuple-element.27), channel_id=1, source_target_pairs={{0,4},{4,0},{1,5},{5,1},{2,6},{6,2},{3,7},{7,3},{8,12},{12,8},{9,1... | collective-permute-start | bytes 393224 | tf_op jit(solution)/shard_map/ppermute | solution.py:332
  6.3 1.5 %collective-permute-start.2 = (bf16[128,512]{1,0:T(8,128)(2,1)S(1)}, bf16[128,512]{1,0:T(8,128)(2,1)S(1)}, u32[]{:S(2)}, u32[]{:S(2)}) collective-permute-start(bf16[128,512]{1,0:T(8,128)(2,1)S(1)} %get-tuple-element.28.refs_0_), channel_id=1, source_target_pairs={{0,12},{4,8},{8,4},{12,0},{16,28},{20,24},{24,20},{28,16},{1,13},{... | collective-permute-start | bytes 393224 | tf_op jit(solution)/shard_map/ppermute | solution.py:336
  7.9 0.3 shard_map.39
  8.2 0.0 collective-permute-done.1
  8.2 0.1 convert_add_fusion.own
  8.3 0.1 collective-permute-start.4
  8.4 3.8 %collective-permute-done.3.refs_1_ = bf16[128,512]{1,0:T(8,128)(2,1)S(1)} collective-permute-done((bf16[128,512]{1,0:T(8,128)(2,1)S(1)}, bf16[128,512]{1,0:T(8,128)(2,1)S(1)}, u32[]{:S(2)}, u32[]{:S(2)}) %collective-permute-start.3) | collective-permute-done | bytes 131104 | tf_op jit(solution)/shard_map/ppermute | solution.py:332
  12.2 1.4 %collective-permute-done.2.refs_0_ = bf16[128,512]{1,0:T(8,128)(2,1)S(1)} collective-permute-done((bf16[128,512]{1,0:T(8,128)(2,1)S(1)}, bf16[128,512]{1,0:T(8,128)(2,1)S(1)}, u32[]{:S(2)}, u32[]{:S(2)}) %collective-permute-start.2) | collective-permute-done | bytes 131104 | tf_op jit(solution)/shard_map/ppermute | solution.py:336
  13.6 0.6 %collective-permute-done.4.refs_2_ = bf16[128,512]{1,0:T(8,128)(2,1)S(1)} collective-permute-done((bf16[128,512]{1,0:T(8,128)(2,1)S(1)}, bf16[128,512]{1,0:T(8,128)(2,1)S(1)}, u32[]{:S(2)}, u32[]{:S(2)}) %collective-permute-start.4) | collective-permute-done | bytes 131104 | tf_op jit(solution)/shard_map/ppermute | solution.py:332
  14.3 0.1 shard_map.40
  14.3 2.8 %collective-permute-start.5 = (bf16[128,384]{1,0:T(8,128)(2,1)S(1)}, bf16[128,384]{1,0:T(8,128)(2,1)S(1)}, u32[]{:S(2)}, u32[]{:S(2)}) collective-permute-start(bf16[128,384]{1,0:T(8,128)(2,1)S(1)} %get-tuple-element.22), channel_id=1, source_target_pairs={{0,16},{8,24},{16,0},{24,8},{1,17},{9,25},{17,1},{25,9},{2,18},{10... | collective-permute-start | bytes 294920 | tf_op jit(solution)/shard_map/ppermute | solution.py:332
  17.1 0.2 collective-permute-start.8
  17.3 4.8 %collective-permute-done.5 = bf16[128,384]{1,0:T(8,128)(2,1)S(1)} collective-permute-done((bf16[128,384]{1,0:T(8,128)(2,1)S(1)}, bf16[128,384]{1,0:T(8,128)(2,1)S(1)}, u32[]{:S(2)}, u32[]{:S(2)}) %collective-permute-start.5) | collective-permute-done | bytes 98336 | tf_op jit(solution)/shard_map/ppermute | solution.py:332
  22.2 0.9 %collective-permute-start.6 = (bf16[128,384]{1,0:T(8,128)(2,1)S(1)}, bf16[128,384]{1,0:T(8,128)(2,1)S(1)}, u32[]{:S(2)}, u32[]{:S(2)}) collective-permute-start(bf16[128,384]{1,0:T(8,128)(2,1)S(1)} %add_convert_fusion.1.refs_0_), channel_id=1, source_target_pairs={{0,8},{8,0},{16,24},{24,16},{1,9},{9,1},{17,25},{25,17},{2,10},{10... | collective-permute-start | bytes 294920 | tf_op jit(solution)/shard_map/ppermute | solution.py:332
  23.1 0.0 collective-permute-done.8
  23.1 1.2 %collective-permute-start.9 = (bf16[128,128]{1,0:T(8,128)(2,1)S(1)}, bf16[128,128]{1,0:T(8,128)(2,1)S(1)}, u32[]{:S(2)}, u32[]{:S(2)}) collective-permute-start(bf16[128,128]{1,0:T(8,128)(2,1)S(1)} %add_convert_fusion.2.refs_3_), channel_id=1, source_target_pairs={{0,8},{8,0},{16,24},{24,16},{1,9},{9,1},{17,25},{25,17},{2,10},{10... | collective-permute-start | bytes 98312 | tf_op jit(solution)/shard_map/ppermute | solution.py:332
  24.3 2.5 %collective-permute-done.6.refs_1_ = bf16[128,384]{1,0:T(8,128)(2,1)S(1)} collective-permute-done((bf16[128,384]{1,0:T(8,128)(2,1)S(1)}, bf16[128,384]{1,0:T(8,128)(2,1)S(1)}, u32[]{:S(2)}, u32[]{:S(2)}) %collective-permute-start.6) | collective-permute-done | bytes 98336 | tf_op jit(solution)/shard_map/ppermute | solution.py:332
  26.9 0.1 collective-permute-start.7
  26.9 0.2 collective-permute-done.9.refs_4_
  27.2 0.3 collective-permute-start.10
  27.5 0.9 %collective-permute-done.10.refs_5_ = bf16[256,128]{1,0:T(8,128)(2,1)S(1)} collective-permute-done((bf16[256,128]{1,0:T(8,128)(2,1)S(1)}, bf16[256,128]{1,0:T(8,128)(2,1)S(1)}, u32[]{:S(2)}, u32[]{:S(2)}) %collective-permute-start.10) | collective-permute-done | bytes 65568 | tf_op jit(solution)/shard_map/ppermute | solution.py:332
  28.5 0.0 collective-permute-done.7.refs_2_
  28.5 6.2 %shard_map.41 = (bf16[32,512]{1,0:T(8,128)(2,1)S(1)}, bf16[32,512]{1,0:T(8,128)(2,1)S(1)}) custom-call(s32[2,2]{1,0:T(2,128)} %counts_hbm.1, bf16[128,384]{1,0:T(8,128)(2,1)S(1)} %add_convert_fusion.1.refs_0_, bf16[128,384]{1,0:T(8,128)(2,1)S(1)} %collective-permute-done.6.refs_1_, bf16[256,384]{1,0:T(8,128)(2,1)S(1)} %collective-permute-done.7.refs_2_, ...), custom_call_target="tpu_custom_call" | custom-call | tf_op jit(solution)/shard_map/pallas_call | solution.py:280
  34.6 1.5 %collective-permute-start.12 = (bf16[32,512]{1,0:T(8,128)(2,1)S(1)}, bf16[32,512]{1,0:T(8,128)(2,1)S(1)}, u32[]{:S(2)}, u32[]{:S(2)}) collective-permute-start(bf16[32,512]{1,0:T(8,128)(2,1)S(1)} %get-tuple-element.25.refs_0_), channel_id=1, source_target_pairs={{0,1},{1,0},{4,5},{5,4},{2,3},{3,2},{6,7},{7,6},{8,9},{9,8},{12,13... | collective-permute-start | bytes 98312 | tf_op jit(solution)/shard_map/ppermute | solution.py:373
  36.1 1.4 %collective-permute-start.13 = (bf16[32,512]{1,0:T(8,128)(2,1)S(1)}, bf16[32,512]{1,0:T(8,128)(2,1)S(1)}, u32[]{:S(2)}, u32[]{:S(2)}) collective-permute-start(bf16[32,512]{1,0:T(8,128)(2,1)S(1)} %get-tuple-element.26), channel_id=1, source_target_pairs={{0,5},{1,4},{4,1},{5,0},{2,7},{3,6},{6,3},{7,2},{8,13},{9,12},{12,... | collective-permute-start | bytes 98312 | tf_op jit(solution)/shard_map/ppermute | solution.py:373
  37.5 0.7 %collective-permute-start.11 = (bf16[32,512]{1,0:T(8,128)(2,1)S(1)}, bf16[32,512]{1,0:T(8,128)(2,1)S(1)}, u32[]{:S(2)}, u32[]{:S(2)}) collective-permute-start(bf16[32,512]{1,0:T(8,128)(2,1)S(1)} %get-tuple-element.26), channel_id=1, source_target_pairs={{0,4},{1,5},{4,0},{5,1},{2,6},{3,7},{6,2},{7,3},{8,12},{9,13},{12,... | collective-permute-start | bytes 98312 | tf_op jit(solution)/shard_map/ppermute | solution.py:373
  38.2 0.4 %collective-permute-done.12.refs_2_ = bf16[32,512]{1,0:T(8,128)(2,1)S(1)} collective-permute-done((bf16[32,512]{1,0:T(8,128)(2,1)S(1)}, bf16[32,512]{1,0:T(8,128)(2,1)S(1)}, u32[]{:S(2)}, u32[]{:S(2)}) %collective-permute-start.12) | collective-permute-done | bytes 32800 | tf_op jit(solution)/shard_map/ppermute | solution.py:373
  38.6 2.4 %collective-permute-done.13.refs_3_ = bf16[32,512]{1,0:T(8,128)(2,1)S(1)} collective-permute-done((bf16[32,512]{1,0:T(8,128)(2,1)S(1)}, bf16[32,512]{1,0:T(8,128)(2,1)S(1)}, u32[]{:S(2)}, u32[]{:S(2)}) %collective-permute-start.13) | collective-permute-done | bytes 32800 | tf_op jit(solution)/shard_map/ppermute | solution.py:373
  41.0 0.4 collective-permute-done.11.refs_1_
  41.4 0.7 %shard_map.42 = bf16[4,32,512]{2,1,0:T(8,128)(2,1)} custom-call(bf16[32,512]{1,0:T(8,128)(2,1)S(1)} %get-tuple-element.25.refs_0_, bf16[32,512]{1,0:T(8,128)(2,1)S(1)} %collective-permute-done.11.refs_1_, bf16[32,512]{1,0:T(8,128)(2,1)S(1)} %collective-permute-done.12.refs_2_, bf16[32,512]{1,0:T(8,128)(2,1)S(1)} %collective-permute-done.13.refs_3_), custom_call_target="tpu_custom_call" | custom-call | tf_op jit(solution)/shard_map/pallas_call | solution.py:315
  (6 shorter events, 0.1 us)
Async XLA Ops:
  1.6 1.7 %collective-permute-start = (bf16[256,512]{1,0:T(8,128)(2,1)S(1)}, bf16[256,512]{1,0:T(8,128)(2,1)S(1)}, u32[]{:S(2)}, u32[]{:S(2)}) collective-permute-start(bf16[256,512]{1,0:T(8,128)(2,1)S(1)} %get-tuple-element.19), channel_id=1, source_target_pairs={{0,2},{2,0},{1,3},{3,1},{4,6},{6,4},{5,7},{7,5},{8,10},{10,8},{9,1... | collective-permute-start | bytes 786440 | tf_op jit(solution)/shard_map/ppermute | solution.py:332
  2.6 5.6 %collective-permute-start.1 = (bf16[256,512]{1,0:T(8,128)(2,1)S(1)}, bf16[256,512]{1,0:T(8,128)(2,1)S(1)}, u32[]{:S(2)}, u32[]{:S(2)}) collective-permute-start(bf16[256,512]{1,0:T(8,128)(2,1)S(1)} %get-tuple-element.20), channel_id=1, source_target_pairs={{0,2},{2,0},{1,3},{3,1},{4,6},{6,4},{5,7},{7,5},{8,10},{10,8},{9,1... | collective-permute-start | bytes 786440 | tf_op jit(solution)/shard_map/ppermute | solution.py:332
  3.4 8.8 %collective-permute-start.3 = (bf16[128,512]{1,0:T(8,128)(2,1)S(1)}, bf16[128,512]{1,0:T(8,128)(2,1)S(1)}, u32[]{:S(2)}, u32[]{:S(2)}) collective-permute-start(bf16[128,512]{1,0:T(8,128)(2,1)S(1)} %get-tuple-element.27), channel_id=1, source_target_pairs={{0,4},{4,0},{1,5},{5,1},{2,6},{6,2},{3,7},{7,3},{8,12},{12,8},{9,1... | collective-permute-start | bytes 393224 | tf_op jit(solution)/shard_map/ppermute | solution.py:332
  6.3 7.3 %collective-permute-start.2 = (bf16[128,512]{1,0:T(8,128)(2,1)S(1)}, bf16[128,512]{1,0:T(8,128)(2,1)S(1)}, u32[]{:S(2)}, u32[]{:S(2)}) collective-permute-start(bf16[128,512]{1,0:T(8,128)(2,1)S(1)} %get-tuple-element.28.refs_0_), channel_id=1, source_target_pairs={{0,12},{4,8},{8,4},{12,0},{16,28},{20,24},{24,20},{28,16},{1,13},{... | collective-permute-start | bytes 393224 | tf_op jit(solution)/shard_map/ppermute | solution.py:336
  8.3 6.0 %collective-permute-start.4 = (bf16[128,512]{1,0:T(8,128)(2,1)S(1)}, bf16[128,512]{1,0:T(8,128)(2,1)S(1)}, u32[]{:S(2)}, u32[]{:S(2)}) collective-permute-start(bf16[128,512]{1,0:T(8,128)(2,1)S(1)} %slice.17), channel_id=1, source_target_pairs={{0,8},{8,0},{16,24},{24,16},{1,9},{9,1},{17,25},{25,17},{2,10},{10... | collective-permute-start | bytes 393224 | tf_op jit(solution)/shard_map/ppermute | solution.py:332
  14.3 7.8 %collective-permute-start.5 = (bf16[128,384]{1,0:T(8,128)(2,1)S(1)}, bf16[128,384]{1,0:T(8,128)(2,1)S(1)}, u32[]{:S(2)}, u32[]{:S(2)}) collective-permute-start(bf16[128,384]{1,0:T(8,128)(2,1)S(1)} %get-tuple-element.22), channel_id=1, source_target_pairs={{0,16},{8,24},{16,0},{24,8},{1,17},{9,25},{17,1},{25,9},{2,18},{10... | collective-permute-start | bytes 294920 | tf_op jit(solution)/shard_map/ppermute | solution.py:332
  17.1 6.0 %collective-permute-start.8 = (bf16[128,128]{1,0:T(8,128)(2,1)S(1)}, bf16[128,128]{1,0:T(8,128)(2,1)S(1)}, u32[]{:S(2)}, u32[]{:S(2)}) collective-permute-start(bf16[128,128]{1,0:T(8,128)(2,1)S(1)} %get-tuple-element.24), channel_id=1, source_target_pairs={{0,16},{8,24},{16,0},{24,8},{1,17},{9,25},{17,1},{25,9},{2,18},{10... | collective-permute-start | bytes 98312 | tf_op jit(solution)/shard_map/ppermute | solution.py:332
  22.2 4.7 %collective-permute-start.6 = (bf16[128,384]{1,0:T(8,128)(2,1)S(1)}, bf16[128,384]{1,0:T(8,128)(2,1)S(1)}, u32[]{:S(2)}, u32[]{:S(2)}) collective-permute-start(bf16[128,384]{1,0:T(8,128)(2,1)S(1)} %add_convert_fusion.1.refs_0_), channel_id=1, source_target_pairs={{0,8},{8,0},{16,24},{24,16},{1,9},{9,1},{17,25},{25,17},{2,10},{10... | collective-permute-start | bytes 294920 | tf_op jit(solution)/shard_map/ppermute | solution.py:332
  23.1 4.1 %collective-permute-start.9 = (bf16[128,128]{1,0:T(8,128)(2,1)S(1)}, bf16[128,128]{1,0:T(8,128)(2,1)S(1)}, u32[]{:S(2)}, u32[]{:S(2)}) collective-permute-start(bf16[128,128]{1,0:T(8,128)(2,1)S(1)} %add_convert_fusion.2.refs_3_), channel_id=1, source_target_pairs={{0,8},{8,0},{16,24},{24,16},{1,9},{9,1},{17,25},{25,17},{2,10},{10... | collective-permute-start | bytes 98312 | tf_op jit(solution)/shard_map/ppermute | solution.py:332
  26.9 1.6 %collective-permute-start.7 = (bf16[256,384]{1,0:T(8,128)(2,1)S(1)}, bf16[256,384]{1,0:T(8,128)(2,1)S(1)}, u32[]{:S(2)}, u32[]{:S(2)}) collective-permute-start(bf16[256,384]{1,0:T(8,128)(2,1)S(1)} %pad_maximum_fusion), channel_id=1, source_target_pairs={{0,2},{2,0},{1,3},{3,1},{4,6},{6,4},{5,7},{7,5},{8,10},{10,8},{9,1... | collective-permute-start | bytes 589832 | tf_op jit(solution)/shard_map/ppermute | solution.py:332
  27.2 1.3 %collective-permute-start.10 = (bf16[256,128]{1,0:T(8,128)(2,1)S(1)}, bf16[256,128]{1,0:T(8,128)(2,1)S(1)}, u32[]{:S(2)}, u32[]{:S(2)}) collective-permute-start(bf16[256,128]{1,0:T(8,128)(2,1)S(1)} %pad_maximum_fusion.1), channel_id=1, source_target_pairs={{0,2},{2,0},{1,3},{3,1},{4,6},{6,4},{5,7},{7,5},{8,10},{10,8},{9,1... | collective-permute-start | bytes 196616 | tf_op jit(solution)/shard_map/ppermute | solution.py:332
  34.6 4.0 %collective-permute-start.12 = (bf16[32,512]{1,0:T(8,128)(2,1)S(1)}, bf16[32,512]{1,0:T(8,128)(2,1)S(1)}, u32[]{:S(2)}, u32[]{:S(2)}) collective-permute-start(bf16[32,512]{1,0:T(8,128)(2,1)S(1)} %get-tuple-element.25.refs_0_), channel_id=1, source_target_pairs={{0,1},{1,0},{4,5},{5,4},{2,3},{3,2},{6,7},{7,6},{8,9},{9,8},{12,13... | collective-permute-start | bytes 98312 | tf_op jit(solution)/shard_map/ppermute | solution.py:373
  36.1 4.9 %collective-permute-start.13 = (bf16[32,512]{1,0:T(8,128)(2,1)S(1)}, bf16[32,512]{1,0:T(8,128)(2,1)S(1)}, u32[]{:S(2)}, u32[]{:S(2)}) collective-permute-start(bf16[32,512]{1,0:T(8,128)(2,1)S(1)} %get-tuple-element.26), channel_id=1, source_target_pairs={{0,5},{1,4},{4,1},{5,0},{2,7},{3,6},{6,3},{7,2},{8,13},{9,12},{12,... | collective-permute-start | bytes 98312 | tf_op jit(solution)/shard_map/ppermute | solution.py:373
  37.5 3.9 %collective-permute-start.11 = (bf16[32,512]{1,0:T(8,128)(2,1)S(1)}, bf16[32,512]{1,0:T(8,128)(2,1)S(1)}, u32[]{:S(2)}, u32[]{:S(2)}) collective-permute-start(bf16[32,512]{1,0:T(8,128)(2,1)S(1)} %get-tuple-element.26), channel_id=1, source_target_pairs={{0,4},{1,5},{4,0},{5,1},{2,6},{3,7},{6,2},{7,3},{8,12},{9,13},{12,... | collective-permute-start | bytes 98312 | tf_op jit(solution)/shard_map/ppermute | solution.py:373

commit v14 on v13

--- a/solution.py
+++ b/solution.py
@@ -188,84 +188,112 @@
     pick = lax.broadcasted_iota(jnp.int32, (2 * rows, width), 1) == wanted
     pick = jnp.where(pick, 1.0, 0.0).astype(BF16)
     picked = 2 * rows
-    stats_left = statistics(grad, turned)
-    stats_right = statistics(turned, grad)
-    squares = [tile * tile for tile in stats_left]
-    norm = jnp.sqrt(jnp.sum(squares[0] + 2.0 * squares[1] + squares[2], keepdims=True))
-    scale = 2.5 / norm
-    first = jnp.sqrt(jnp.sqrt(scale)).astype(BF16).astype(F32)
-    tiles = [scale * tile for tile in stats_left]
-    fill(m_left, 0, tiles)
-    fill(left, picked, factor(tiles))
-    left[:picked, :] = (first * dot(pick, left[picked:, :])).astype(BF16)
-    tiles = [scale * tile for tile in stats_right]
-    fill(m_right, 0, tiles)
-    tiles = [tile.astype(BF16) for tile in factor(tiles)]
-    fill(right, width, tiles)
-    tiles = [(first * tile.astype(F32)).astype(BF16) for tile in tiles]
-    right[half:width, low] = tiles[0]
-    right[half:width, high] = tiles[1]
-    right[:half, low] = tiles[1].T
-    right[:half, high] = tiles[2]
-
-    def square(ref):
-        by_high = dot(ref[...], ref[:, high])
-        return dot(ref[low, :], ref[:, low]), by_high[low], by_high[high]
-
     counts_copy.wait()
     count_left, count_right = counts[column, 0], counts[column, 1]
-    for index in range(1, most):
-        q_left, q_right = left.at[picked:, :], right.at[width:, :]
-        if index == 1:
-            fill(s_left, 0, square(q_left))
-            fill(s_right, 0, square(q_right))
-        else:
-            by_high = dot(left[...], q_left[:, high])
-            by_low = dot(left[: picked + half, :], q_left[:, low])
-            right_by_high = dot(right[...], q_right[:, high])
-            right_by_low = dot(right[half : width + half, :], q_right[:, low])
-            fill(s_left, 0, (by_low[picked:], by_high[picked : picked + half], by_high[picked + half :]))
-            fill(
-                s_right,
-                0,
-                (right_by_low[half:], right_by_high[width : width + half], right_by_high[width + half :]),
-            )
-
-            def keep_if(ref, value, goes_on):
-                value = value.astype(BF16)
-                return value if index == 2 else jnp.where(goes_on, value, ref)
-
-            left[:picked, low] = keep_if(left[:picked, low], by_low[:picked], index <= count_left)
-            left[:picked, high] = keep_if(left[:picked, high], by_high[:picked], index <= count_left)
-            goes_on = index <= count_right
-            upper_right = keep_if(right[half:width, high], right_by_high[half:width], goes_on)
-            right[half:width, low] = keep_if(right[half:width, low], right_by_low[:half], goes_on)
-            right[half:width, high] = upper_right
-            right[:half, low] = upper_right.T
-            right[:half, high] = keep_if(right[:half, high], right_by_high[:half], goes_on)
-        fourths = square(s_left), square(s_right)
-        fill(s_left, 0, fourths[0])
-        fill(s_right, 0, fourths[1])
-        for fourth, moment_ref, ref, start in (
-            (s_left, m_left, left, picked),
-            (s_right, m_right, right, width),
-        ):
-            by_high = dot(fourth[...], moment_ref[:, high])
-            tiles = (dot(fourth[low, :], moment_ref[:, low]), by_high[low], by_high[high])
+
+    def by_tiles(first, second):
+        by_high = dot(first[...], second[:, high])
+        return dot(first[low, :], second[:, low]), by_high[low], by_high[high]
+
+    def keep_if(old, value, goes_on):
+        return jnp.where(goes_on, value.astype(BF16), old)
+
+    def steps(stats, shared, stacked, second, moment_ref, start, first_x, next_x):
+        tiles = statistics(*stats)
+        yield
+        if not shared:
+            squares = [tile * tile for tile in tiles]
+            total = jnp.sum(squares[0] + 2.0 * squares[1] + squares[2], keepdims=True)
+            scale = 2.5 / jnp.sqrt(total)
+            shared += [scale, jnp.sqrt(jnp.sqrt(scale)).astype(BF16).astype(F32)]
+        scale, first = shared
+        tiles = [scale * tile for tile in tiles]
+        fill(moment_ref, 0, tiles)
+        tiles = [tile.astype(BF16) for tile in factor(tiles)]
+        fill(stacked, start, tiles)
+        factor_ref = stacked.at[start : start + width, :]
+        tiles_x = first_x(first, tiles, factor_ref)
+        products = by_tiles(factor_ref, factor_ref)
+        yield
+        tiles_x()
+        for index in range(1, most):
+            if index > 1:
+                products = next_x(products, index)
+            fill(second, 0, products)
+            products = by_tiles(second, second)
+            yield
+            fill(second, 0, products)
+            products = by_tiles(second, moment_ref)
+            yield
             if index < most - 1:
-                fill(moment_ref, 0, tiles)
-            fill(ref, start, factor(tiles))
-    final_left = dot(left[:picked, :], left[picked:, :]).astype(BF16)
-    final_left = jnp.where(most <= count_left, final_left, left[:picked, :])
-    by_high = dot(right[:width, :], right[width:, high])
-    by_low = dot(right[half:width, :], right[width:, low])
-    goes_on = most <= count_right
-    upper_right = jnp.where(goes_on, by_high[half:].astype(BF16), right[half:width, high])
-    right[half:width, low] = jnp.where(goes_on, by_low.astype(BF16), right[half:width, low])
-    right[half:width, high] = upper_right
-    right[:half, low] = upper_right.T
-    right[:half, high] = jnp.where(goes_on, by_high[:half].astype(BF16), right[:half, high])
-    partial_value = dot(final_left, grad[...]).astype(BF16)
+                fill(moment_ref, 0, products)
+            fill(stacked, start, factor(products))
+            if index < most - 1:
+                products = dot(stacked[...], factor_ref[:, high]), dot(
+                    stacked[max(start - half, 0) : start + half, :], factor_ref[:, low]
+                )
+                yield
+
+    def first_left(first, tiles, factor_ref):
+        product = first * dot(pick, factor_ref[...])
+
+        def store():
+            left[:picked, :] = product.astype(BF16)
+
+        return store
+
+    def next_left(products, index):
+        by_high, by_low = products
+        goes_on = index <= count_left
+        left[:picked, low] = keep_if(left[:picked, low], by_low[:picked], goes_on)
+        left[:picked, high] = keep_if(left[:picked, high], by_high[:picked], goes_on)
+        return by_low[picked:], by_high[picked : picked + half], by_high[picked + half :]
+
+    def first_right(first, tiles, factor_ref):
+        def store():
+            values = [(first * tile.astype(F32)).astype(BF16) for tile in tiles]
+            right[half:width, low] = values[0]
+            right[half:width, high] = values[1]
+            right[:half, low] = values[1].T
+            right[:half, high] = values[2]
+
+        return store
+
+    def keep_right(by_low, by_high, goes_on):
+        upper_right = keep_if(right[half:width, high], by_high[half:width], goes_on)
+        right[half:width, low] = keep_if(right[half:width, low], by_low[:half], goes_on)
+        right[half:width, high] = upper_right
+        right[:half, low] = upper_right.T
+        right[:half, high] = keep_if(right[:half, high], by_high[:half], goes_on)
+
+    def next_right(products, index):
+        by_high, by_low = products
+        keep_right(by_low, by_high, index <= count_right)
+        return by_low[half:], by_high[width : width + half], by_high[width + half :]
+
+    def left_steps(shared):
+        yield from steps((grad, turned), shared, left, s_left, m_left, picked, first_left, next_left)
+        product = dot(left[:picked, :], left[picked:, :])
+        yield
+        left[:picked, :] = keep_if(left[:picked, :], product, most <= count_left)
+        product = dot(left[:picked, :], grad[...])
+        yield
+        left[:picked, :] = product.astype(BF16)
+
+    def right_steps(shared):
+        yield from steps(
+            (turned, grad), shared, right, s_right, m_right, width, first_right, next_right
+        )
+        by_high = dot(right[:width, :], right[width:, high])
+        by_low = dot(right[half:width, :], right[width:, low])
+        yield
+        keep_right(by_low, by_high, most <= count_right)
+
+    shared = []
+    sides = [left_steps(shared), right_steps(shared)]
+    while sides:
+        sides = [side for side in sides if next(side, True) is None]
+    partial_value = left[:picked, :]
     update = dot(partial_value[:, low], right[half:width, :]) + dot(
         partial_value[:, high], right[:half, :]
     )

time: 42.3 us -> 42.7 us (level)
  no operation moved by 1% of the time
where the time goes in v14:
time: 42.7 us; the launch traced here: 42.5 us
  waiting for transfers between devices  18.2 us (43%)
  starting transfers between devices  14.3 us (33%)
  Pallas kernels  9.71 us (23%)
    ppermute x10, waiting for transfers between devices, swap(): lax.ppermute(array, axis, [(i, i ^ mask) for i in range(lax.axis_size(axi...  13.5 us
    ppermute x10, starting transfers between devices, swap(): lax.ppermute(array, axis, [(i, i ^ mask) for i in range(lax.axis_size(axi...  9.2 us
    pallas_call x1, Pallas kernels, root(): pl.pallas_call(functools.partial(root_kernel, most), out_shape=[out, out]...  6.57 us
    ppermute x3, starting transfers between devices, shards(): lax.ppermute(piece, ('x', 'group'), moves)  3.55 us
    ppermute x3, waiting for transfers between devices, shards(): lax.ppermute(piece, ('x', 'group'), moves)  3.26 us
    pallas_call x1, Pallas kernels, load(): pl.pallas_call(functools.partial(load_kernel, scale), out_shape=[jax.Shap...  1.61 us
    ppermute x1, starting transfers between devices, swap_diagonal(): return lax.ppermute(array, ('z', 'x'), moves)  1.55 us
    ppermute x1, waiting for transfers between devices, swap_diagonal(): return lax.ppermute(array, ('z', 'x'), moves)  1.4 us
  transfers between devices with their start and end apart: 14, of which 11 were waited for; matrix products, arithmetic and copies ran while one was open for 1% of the time, Pallas kernels for 2%

profile of v14, /device:TPU:0, one launch (start us, length us, event | category | flops | bytes accessed | tf_op | source)
XLA Modules:
  0.0 42.5 jit_solution(114925942139822777)
XLA Ops:
  0.0 1.6 %shard_map.37 = (bf16[256,512]{1,0:T(8,128)(2,1)S(1)}, bf16[2,2,512,256]{3,2,1,0:T(8,128)(2,1)S(1)}, bf16[2,512,512]{2,1,0:T(8,128)(2,1)S(1)}) custom-call(bf16[2,512,512]{2,1,0:T(8,128)(2,1)} %patch_hbm.1, bf16[2,512,512]{2,1,0:T(8,128)(2,1)} %cot_hbm.1), custom_call_target="tpu_custom_call" | custom-call | tf_op jit(solution)/shard_map/pallas_call | solution.py:64
  1.6 0.5 %collective-permute-start = (bf16[256,512]{1,0:T(8,128)(2,1)S(1)}, bf16[256,512]{1,0:T(8,128)(2,1)S(1)}, u32[]{:S(2)}, u32[]{:S(2)}) collective-permute-start(bf16[256,512]{1,0:T(8,128)(2,1)S(1)} %get-tuple-element.19), channel_id=1, source_target_pairs={{0,2},{2,0},{1,3},{3,1},{4,6},{6,4},{5,7},{7,5},{8,10},{10,8},{9,1... | collective-permute-start | bytes 786440 | tf_op jit(solution)/shard_map/ppermute | solution.py:360
  2.1 0.5 %shard_map.38 = (f32[256,512]{1,0:T(8,128)S(1)}, bf16[256,512]{1,0:T(8,128)(2,1)S(1)}) custom-call(bf16[2,2,512,256]{3,2,1,0:T(8,128)(2,1)S(1)} %get-tuple-element.16.patch, bf16[2,512,512]{2,1,0:T(8,128)(2,1)S(1)} %get-tuple-element.17.cot), custom_call_target="tpu_custom_call" | custom-call | flops 268435456 | bytes 1048576 | tf_op jit(solution)/shard_map/pallas_call | solution.py:88
  2.6 0.1 collective-permute-start.1
  2.7 0.6 %collective-permute-done = bf16[256,512]{1,0:T(8,128)(2,1)S(1)} collective-permute-done((bf16[256,512]{1,0:T(8,128)(2,1)S(1)}, bf16[256,512]{1,0:T(8,128)(2,1)S(1)}, u32[]{:S(2)}, u32[]{:S(2)}) %collective-permute-start) | collective-permute-done | bytes 262176 | tf_op jit(solution)/shard_map/ppermute | solution.py:360
  3.3 0.1 add_convert_fusion
  3.4 2.9 %collective-permute-start.3 = (bf16[128,512]{1,0:T(8,128)(2,1)S(1)}, bf16[128,512]{1,0:T(8,128)(2,1)S(1)}, u32[]{:S(2)}, u32[]{:S(2)}) collective-permute-start(bf16[128,512]{1,0:T(8,128)(2,1)S(1)} %get-tuple-element.27), channel_id=1, source_target_pairs={{0,4},{4,0},{1,5},{5,1},{2,6},{6,2},{3,7},{7,3},{8,12},{12,8},{9,1... | collective-permute-start | bytes 393224 | tf_op jit(solution)/shard_map/ppermute | solution.py:360
  6.3 1.5 %collective-permute-start.2 = (bf16[128,512]{1,0:T(8,128)(2,1)S(1)}, bf16[128,512]{1,0:T(8,128)(2,1)S(1)}, u32[]{:S(2)}, u32[]{:S(2)}) collective-permute-start(bf16[128,512]{1,0:T(8,128)(2,1)S(1)} %get-tuple-element.28.refs_0_), channel_id=1, source_target_pairs={{0,12},{4,8},{8,4},{12,0},{16,28},{20,24},{24,20},{28,16},{1,13},{... | collective-permute-start | bytes 393224 | tf_op jit(solution)/shard_map/ppermute | solution.py:364
  7.9 0.3 shard_map.39
  8.2 0.0 collective-permute-done.1
  8.2 0.1 convert_add_fusion.own
  8.3 0.1 collective-permute-start.4
  8.4 3.8 %collective-permute-done.3.refs_1_ = bf16[128,512]{1,0:T(8,128)(2,1)S(1)} collective-permute-done((bf16[128,512]{1,0:T(8,128)(2,1)S(1)}, bf16[128,512]{1,0:T(8,128)(2,1)S(1)}, u32[]{:S(2)}, u32[]{:S(2)}) %collective-permute-start.3) | collective-permute-done | bytes 131104 | tf_op jit(solution)/shard_map/ppermute | solution.py:360
  12.2 1.4 %collective-permute-done.2.refs_0_ = bf16[128,512]{1,0:T(8,128)(2,1)S(1)} collective-permute-done((bf16[128,512]{1,0:T(8,128)(2,1)S(1)}, bf16[128,512]{1,0:T(8,128)(2,1)S(1)}, u32[]{:S(2)}, u32[]{:S(2)}) %collective-permute-start.2) | collective-permute-done | bytes 131104 | tf_op jit(solution)/shard_map/ppermute | solution.py:364
  13.6 0.6 %collective-permute-done.4.refs_2_ = bf16[128,512]{1,0:T(8,128)(2,1)S(1)} collective-permute-done((bf16[128,512]{1,0:T(8,128)(2,1)S(1)}, bf16[128,512]{1,0:T(8,128)(2,1)S(1)}, u32[]{:S(2)}, u32[]{:S(2)}) %collective-permute-start.4) | collective-permute-done | bytes 131104 | tf_op jit(solution)/shard_map/ppermute | solution.py:360
  14.3 0.1 shard_map.40
  14.3 2.8 %collective-permute-start.5 = (bf16[128,384]{1,0:T(8,128)(2,1)S(1)}, bf16[128,384]{1,0:T(8,128)(2,1)S(1)}, u32[]{:S(2)}, u32[]{:S(2)}) collective-permute-start(bf16[128,384]{1,0:T(8,128)(2,1)S(1)} %get-tuple-element.22), channel_id=1, source_target_pairs={{0,16},{8,24},{16,0},{24,8},{1,17},{9,25},{17,1},{25,9},{2,18},{10... | collective-permute-start | bytes 294920 | tf_op jit(solution)/shard_map/ppermute | solution.py:360
  17.1 0.2 collective-permute-start.8
  17.3 4.8 %collective-permute-done.5 = bf16[128,384]{1,0:T(8,128)(2,1)S(1)} collective-permute-done((bf16[128,384]{1,0:T(8,128)(2,1)S(1)}, bf16[128,384]{1,0:T(8,128)(2,1)S(1)}, u32[]{:S(2)}, u32[]{:S(2)}) %collective-permute-start.5) | collective-permute-done | bytes 98336 | tf_op jit(solution)/shard_map/ppermute | solution.py:360
  22.2 0.9 %collective-permute-start.6 = (bf16[128,384]{1,0:T(8,128)(2,1)S(1)}, bf16[128,384]{1,0:T(8,128)(2,1)S(1)}, u32[]{:S(2)}, u32[]{:S(2)}) collective-permute-start(bf16[128,384]{1,0:T(8,128)(2,1)S(1)} %add_convert_fusion.1.refs_0_), channel_id=1, source_target_pairs={{0,8},{8,0},{16,24},{24,16},{1,9},{9,1},{17,25},{25,17},{2,10},{10... | collective-permute-start | bytes 294920 | tf_op jit(solution)/shard_map/ppermute | solution.py:360
  23.1 0.0 collective-permute-done.8
  23.1 1.2 %collective-permute-start.9 = (bf16[128,128]{1,0:T(8,128)(2,1)S(1)}, bf16[128,128]{1,0:T(8,128)(2,1)S(1)}, u32[]{:S(2)}, u32[]{:S(2)}) collective-permute-start(bf16[128,128]{1,0:T(8,128)(2,1)S(1)} %add_convert_fusion.2.refs_3_), channel_id=1, source_target_pairs={{0,8},{8,0},{16,24},{24,16},{1,9},{9,1},{17,25},{25,17},{2,10},{10... | collective-permute-start | bytes 98312 | tf_op jit(solution)/shard_map/ppermute | solution.py:360
  24.3 2.5 %collective-permute-done.6.refs_1_ = bf16[128,384]{1,0:T(8,128)(2,1)S(1)} collective-permute-done((bf16[128,384]{1,0:T(8,128)(2,1)S(1)}, bf16[128,384]{1,0:T(8,128)(2,1)S(1)}, u32[]{:S(2)}, u32[]{:S(2)}) %collective-permute-start.6) | collective-permute-done | bytes 98336 | tf_op jit(solution)/shard_map/ppermute | solution.py:360
  26.9 0.1 collective-permute-start.7
  26.9 0.2 collective-permute-done.9.refs_4_
  27.2 0.3 collective-permute-start.10
  27.5 0.9 %collective-permute-done.10.refs_5_ = bf16[256,128]{1,0:T(8,128)(2,1)S(1)} collective-permute-done((bf16[256,128]{1,0:T(8,128)(2,1)S(1)}, bf16[256,128]{1,0:T(8,128)(2,1)S(1)}, u32[]{:S(2)}, u32[]{:S(2)}) %collective-permute-start.10) | collective-permute-done | bytes 65568 | tf_op jit(solution)/shard_map/ppermute | solution.py:360
  28.5 0.0 collective-permute-done.7.refs_2_
  28.5 6.6 %shard_map.41 = (bf16[32,512]{1,0:T(8,128)(2,1)S(1)}, bf16[32,512]{1,0:T(8,128)(2,1)S(1)}) custom-call(s32[2,2]{1,0:T(2,128)} %counts_hbm.1, bf16[128,384]{1,0:T(8,128)(2,1)S(1)} %add_convert_fusion.1.refs_0_, bf16[128,384]{1,0:T(8,128)(2,1)S(1)} %collective-permute-done.6.refs_1_, bf16[256,384]{1,0:T(8,128)(2,1)S(1)} %collective-permute-done.7.refs_2_, ...), custom_call_target="tpu_custom_call" | custom-call | tf_op jit(solution)/shard_map/pallas_call | solution.py:308
  35.0 1.5 %collective-permute-start.12 = (bf16[32,512]{1,0:T(8,128)(2,1)S(1)}, bf16[32,512]{1,0:T(8,128)(2,1)S(1)}, u32[]{:S(2)}, u32[]{:S(2)}) collective-permute-start(bf16[32,512]{1,0:T(8,128)(2,1)S(1)} %get-tuple-element.25.refs_0_), channel_id=1, source_target_pairs={{0,1},{1,0},{4,5},{5,4},{2,3},{3,2},{6,7},{7,6},{8,9},{9,8},{12,13... | collective-permute-start | bytes 98312 | tf_op jit(solution)/shard_map/ppermute | solution.py:401
  36.5 1.4 %collective-permute-start.13 = (bf16[32,512]{1,0:T(8,128)(2,1)S(1)}, bf16[32,512]{1,0:T(8,128)(2,1)S(1)}, u32[]{:S(2)}, u32[]{:S(2)}) collective-permute-start(bf16[32,512]{1,0:T(8,128)(2,1)S(1)} %get-tuple-element.26), channel_id=1, source_target_pairs={{0,5},{1,4},{4,1},{5,0},{2,7},{3,6},{6,3},{7,2},{8,13},{9,12},{12,... | collective-permute-start | bytes 98312 | tf_op jit(solution)/shard_map/ppermute | solution.py:401
  37.9 0.7 %collective-permute-start.11 = (bf16[32,512]{1,0:T(8,128)(2,1)S(1)}, bf16[32,512]{1,0:T(8,128)(2,1)S(1)}, u32[]{:S(2)}, u32[]{:S(2)}) collective-permute-start(bf16[32,512]{1,0:T(8,128)(2,1)S(1)} %get-tuple-element.26), channel_id=1, source_target_pairs={{0,4},{1,5},{4,0},{5,1},{2,6},{3,7},{6,2},{7,3},{8,12},{9,13},{12,... | collective-permute-start | bytes 98312 | tf_op jit(solution)/shard_map/ppermute | solution.py:401
  38.6 0.4 collective-permute-done.12.refs_2_
  39.0 2.4 %collective-permute-done.13.refs_3_ = bf16[32,512]{1,0:T(8,128)(2,1)S(1)} collective-permute-done((bf16[32,512]{1,0:T(8,128)(2,1)S(1)}, bf16[32,512]{1,0:T(8,128)(2,1)S(1)}, u32[]{:S(2)}, u32[]{:S(2)}) %collective-permute-start.13) | collective-permute-done | bytes 32800 | tf_op jit(solution)/shard_map/ppermute | solution.py:401
  41.5 0.4 collective-permute-done.11.refs_1_
  41.9 0.7 %shard_map.42 = bf16[4,32,512]{2,1,0:T(8,128)(2,1)} custom-call(bf16[32,512]{1,0:T(8,128)(2,1)S(1)} %get-tuple-element.25.refs_0_, bf16[32,512]{1,0:T(8,128)(2,1)S(1)} %collective-permute-done.11.refs_1_, bf16[32,512]{1,0:T(8,128)(2,1)S(1)} %collective-permute-done.12.refs_2_, bf16[32,512]{1,0:T(8,128)(2,1)S(1)} %collective-permute-done.13.refs_3_), custom_call_target="tpu_custom_call" | custom-call | tf_op jit(solution)/shard_map/pallas_call | solution.py:343
  (6 shorter events, 0.1 us)
Async XLA Ops:
  1.6 1.7 %collective-permute-start = (bf16[256,512]{1,0:T(8,128)(2,1)S(1)}, bf16[256,512]{1,0:T(8,128)(2,1)S(1)}, u32[]{:S(2)}, u32[]{:S(2)}) collective-permute-start(bf16[256,512]{1,0:T(8,128)(2,1)S(1)} %get-tuple-element.19), channel_id=1, source_target_pairs={{0,2},{2,0},{1,3},{3,1},{4,6},{6,4},{5,7},{7,5},{8,10},{10,8},{9,1... | collective-permute-start | bytes 786440 | tf_op jit(solution)/shard_map/ppermute | solution.py:360
  2.6 5.6 %collective-permute-start.1 = (bf16[256,512]{1,0:T(8,128)(2,1)S(1)}, bf16[256,512]{1,0:T(8,128)(2,1)S(1)}, u32[]{:S(2)}, u32[]{:S(2)}) collective-permute-start(bf16[256,512]{1,0:T(8,128)(2,1)S(1)} %get-tuple-element.20), channel_id=1, source_target_pairs={{0,2},{2,0},{1,3},{3,1},{4,6},{6,4},{5,7},{7,5},{8,10},{10,8},{9,1... | collective-permute-start | bytes 786440 | tf_op jit(solution)/shard_map/ppermute | solution.py:360
  3.4 8.8 %collective-permute-start.3 = (bf16[128,512]{1,0:T(8,128)(2,1)S(1)}, bf16[128,512]{1,0:T(8,128)(2,1)S(1)}, u32[]{:S(2)}, u32[]{:S(2)}) collective-permute-start(bf16[128,512]{1,0:T(8,128)(2,1)S(1)} %get-tuple-element.27), channel_id=1, source_target_pairs={{0,4},{4,0},{1,5},{5,1},{2,6},{6,2},{3,7},{7,3},{8,12},{12,8},{9,1... | collective-permute-start | bytes 393224 | tf_op jit(solution)/shard_map/ppermute | solution.py:360
  6.3 7.3 %collective-permute-start.2 = (bf16[128,512]{1,0:T(8,128)(2,1)S(1)}, bf16[128,512]{1,0:T(8,128)(2,1)S(1)}, u32[]{:S(2)}, u32[]{:S(2)}) collective-permute-start(bf16[128,512]{1,0:T(8,128)(2,1)S(1)} %get-tuple-element.28.refs_0_), channel_id=1, source_target_pairs={{0,12},{4,8},{8,4},{12,0},{16,28},{20,24},{24,20},{28,16},{1,13},{... | collective-permute-start | bytes 393224 | tf_op jit(solution)/shard_map/ppermute | solution.py:364
  8.3 6.0 %collective-permute-start.4 = (bf16[128,512]{1,0:T(8,128)(2,1)S(1)}, bf16[128,512]{1,0:T(8,128)(2,1)S(1)}, u32[]{:S(2)}, u32[]{:S(2)}) collective-permute-start(bf16[128,512]{1,0:T(8,128)(2,1)S(1)} %slice.17), channel_id=1, source_target_pairs={{0,8},{8,0},{16,24},{24,16},{1,9},{9,1},{17,25},{25,17},{2,10},{10... | collective-permute-start | bytes 393224 | tf_op jit(solution)/shard_map/ppermute | solution.py:360
  14.3 7.8 %collective-permute-start.5 = (bf16[128,384]{1,0:T(8,128)(2,1)S(1)}, bf16[128,384]{1,0:T(8,128)(2,1)S(1)}, u32[]{:S(2)}, u32[]{:S(2)}) collective-permute-start(bf16[128,384]{1,0:T(8,128)(2,1)S(1)} %get-tuple-element.22), channel_id=1, source_target_pairs={{0,16},{8,24},{16,0},{24,8},{1,17},{9,25},{17,1},{25,9},{2,18},{10... | collective-permute-start | bytes 294920 | tf_op jit(solution)/shard_map/ppermute | solution.py:360
  17.1 6.0 %collective-permute-start.8 = (bf16[128,128]{1,0:T(8,128)(2,1)S(1)}, bf16[128,128]{1,0:T(8,128)(2,1)S(1)}, u32[]{:S(2)}, u32[]{:S(2)}) collective-permute-start(bf16[128,128]{1,0:T(8,128)(2,1)S(1)} %get-tuple-element.24), channel_id=1, source_target_pairs={{0,16},{8,24},{16,0},{24,8},{1,17},{9,25},{17,1},{25,9},{2,18},{10... | collective-permute-start | bytes 98312 | tf_op jit(solution)/shard_map/ppermute | solution.py:360
  22.2 4.7 %collective-permute-start.6 = (bf16[128,384]{1,0:T(8,128)(2,1)S(1)}, bf16[128,384]{1,0:T(8,128)(2,1)S(1)}, u32[]{:S(2)}, u32[]{:S(2)}) collective-permute-start(bf16[128,384]{1,0:T(8,128)(2,1)S(1)} %add_convert_fusion.1.refs_0_), channel_id=1, source_target_pairs={{0,8},{8,0},{16,24},{24,16},{1,9},{9,1},{17,25},{25,17},{2,10},{10... | collective-permute-start | bytes 294920 | tf_op jit(solution)/shard_map/ppermute | solution.py:360
  23.1 4.1 %collective-permute-start.9 = (bf16[128,128]{1,0:T(8,128)(2,1)S(1)}, bf16[128,128]{1,0:T(8,128)(2,1)S(1)}, u32[]{:S(2)}, u32[]{:S(2)}) collective-permute-start(bf16[128,128]{1,0:T(8,128)(2,1)S(1)} %add_convert_fusion.2.refs_3_), channel_id=1, source_target_pairs={{0,8},{8,0},{16,24},{24,16},{1,9},{9,1},{17,25},{25,17},{2,10},{10... | collective-permute-start | bytes 98312 | tf_op jit(solution)/shard_map/ppermute | solution.py:360
  26.9 1.6 %collective-permute-start.7 = (bf16[256,384]{1,0:T(8,128)(2,1)S(1)}, bf16[256,384]{1,0:T(8,128)(2,1)S(1)}, u32[]{:S(2)}, u32[]{:S(2)}) collective-permute-start(bf16[256,384]{1,0:T(8,128)(2,1)S(1)} %pad_maximum_fusion), channel_id=1, source_target_pairs={{0,2},{2,0},{1,3},{3,1},{4,6},{6,4},{5,7},{7,5},{8,10},{10,8},{9,1... | collective-permute-start | bytes 589832 | tf_op jit(solution)/shard_map/ppermute | solution.py:360
  27.2 1.3 %collective-permute-start.10 = (bf16[256,128]{1,0:T(8,128)(2,1)S(1)}, bf16[256,128]{1,0:T(8,128)(2,1)S(1)}, u32[]{:S(2)}, u32[]{:S(2)}) collective-permute-start(bf16[256,128]{1,0:T(8,128)(2,1)S(1)} %pad_maximum_fusion.1), channel_id=1, source_target_pairs={{0,2},{2,0},{1,3},{3,1},{4,6},{6,4},{5,7},{7,5},{8,10},{10,8},{9,1... | collective-permute-start | bytes 196616 | tf_op jit(solution)/shard_map/ppermute | solution.py:360
  35.0 4.0 %collective-permute-start.12 = (bf16[32,512]{1,0:T(8,128)(2,1)S(1)}, bf16[32,512]{1,0:T(8,128)(2,1)S(1)}, u32[]{:S(2)}, u32[]{:S(2)}) collective-permute-start(bf16[32,512]{1,0:T(8,128)(2,1)S(1)} %get-tuple-element.25.refs_0_), channel_id=1, source_target_pairs={{0,1},{1,0},{4,5},{5,4},{2,3},{3,2},{6,7},{7,6},{8,9},{9,8},{12,13... | collective-permute-start | bytes 98312 | tf_op jit(solution)/shard_map/ppermute | solution.py:401
  36.5 4.9 %collective-permute-start.13 = (bf16[32,512]{1,0:T(8,128)(2,1)S(1)}, bf16[32,512]{1,0:T(8,128)(2,1)S(1)}, u32[]{:S(2)}, u32[]{:S(2)}) collective-permute-start(bf16[32,512]{1,0:T(8,128)(2,1)S(1)} %get-tuple-element.26), channel_id=1, source_target_pairs={{0,5},{1,4},{4,1},{5,0},{2,7},{3,6},{6,3},{7,2},{8,13},{9,12},{12,... | collective-permute-start | bytes 98312 | tf_op jit(solution)/shard_map/ppermute | solution.py:401
  37.9 3.9 %collective-permute-start.11 = (bf16[32,512]{1,0:T(8,128)(2,1)S(1)}, bf16[32,512]{1,0:T(8,128)(2,1)S(1)}, u32[]{:S(2)}, u32[]{:S(2)}) collective-permute-start(bf16[32,512]{1,0:T(8,128)(2,1)S(1)} %get-tuple-element.26), channel_id=1, source_target_pairs={{0,4},{1,5},{4,0},{5,1},{2,6},{3,7},{6,2},{7,3},{8,12},{9,13},{12,... | collective-permute-start | bytes 98312 | tf_op jit(solution)/shard_map/ppermute | solution.py:401

commit v15 on v13

--- a/solution.py
+++ b/solution.py
@@ -133,25 +133,54 @@
     return total
 
 
+def near_kernel(left_own, left_other, right_own, right_other, near, turned, *tiles):
+    quarter, split = left_own.shape
+    for first, columns in ((left_own, slice(0, split)), (right_own, slice(split, None))):
+        near[:quarter, columns] = first[...]
+    for second, columns in ((left_other, slice(0, split)), (right_other, slice(split, None))):
+        near[quarter:, columns] = second[...]
+    turned[...] = near[...].T
+    *inner, outer = tiles
+    half = near.shape[0]
+    low, high = slice(0, half), slice(half, 2 * half)
+    for (a, b), tile in zip(((low, low), (low, high), (high, high)), inner):
+        tile[...] = jnp.dot(turned[a, :], near[:, b], preferred_element_type=F32)
+    outer[...] = jnp.dot(near[...], turned[...], preferred_element_type=F32)
+
+
+def near_part(*pieces):
+    half = 2 * pieces[0].shape[0]
+    tile = jax.ShapeDtypeStruct((half, half), F32)
+    return pl.pallas_call(
+        near_kernel,
+        out_shape=[
+            jax.ShapeDtypeStruct((half, 2 * half), BF16),
+            jax.ShapeDtypeStruct((2 * half, half), BF16),
+        ]
+        + [tile] * 4,
+        in_specs=[VMEM] * 4,
+        out_specs=[VMEM] * 6,
+        compiler_params=params(16),
+        cost_estimate=pl.CostEstimate(
+            flops=10 * half**3, bytes_accessed=16 * half**2, transcendentals=0
+        ),
+    )(*pieces)
+
+
 def root_kernel(most, counts_hbm, *refs):
-    pieces = refs[:6]
-    keep_ref, send_ref, grad, turned, left, right, m_left, m_right, s_left, s_right, counts, sem = refs[6:]
+    near, near_turned, *near_tiles, near_outer, left_far, right_far, keep_ref, send_ref = refs[:10]
+    far, far_turned, left, right, m_left, m_right, s_left, s_right, counts, sem = refs[10:]
     counts_copy = pltpu.make_async_copy(counts_hbm, counts, sem)
     counts_copy.start()
-    width = grad.shape[0]
-    half, quarter = width // 2, width // 4
+    width = far.shape[1]
+    half = width // 2
     rows = keep_ref.shape[0]
     low, high = slice(0, half), slice(half, width)
     place, column, core = (lax.axis_index(name) for name in ("z", "x", "core"))
-    column_start = 0
-    for index in range(2):
-        own, other, far = pieces[3 * index : 3 * index + 3]
-        columns = slice(column_start, column_start + own.shape[1])
-        column_start += own.shape[1]
-        grad[:quarter, columns] = own[...]
-        grad[quarter:half, columns] = other[...]
-        grad[half:, columns] = far[...]
-    turned[...] = grad[...].T
+    split = left_far.shape[1]
+    far[:, :split] = left_far[...]
+    far[:, split:] = right_far[...]
+    far_turned[...] = far[...].T
     diagonal = lax.broadcasted_iota(jnp.int32, (half, half), 0) == lax.broadcasted_iota(
         jnp.int32, (half, half), 1
     )
@@ -171,25 +200,30 @@
         five = jnp.where(diagonal, 1.25, 0.0)
         return five - 0.25 * upper_left, -0.25 * upper_right, five - 0.25 * lower_right
 
-    def statistics(first, second):
-        tiles = [
-            dot(first[a, :], second[:, b]) for a, b in ((low, low), (low, high), (high, high))
-        ]
+    def damped(tiles):
         tenth = jnp.where(diagonal, 0.1, 0.0)
         return tiles[0] + tenth, tiles[1], tiles[2] + tenth
 
     def spot(flip):
         row = (4 * place + 2 * (column ^ flip) + core) * rows
-        part = row // quarter
-        return ((part // 2 ^ core) * 2 + (part % 2 ^ place % 2)) * quarter + row % quarter
+        part = row // (half // 2)
+        start = ((part // 2 ^ core) * 2 + (part % 2 ^ place % 2)) * (half // 2)
+        return start + row % (half // 2)
 
     line = lax.broadcasted_iota(jnp.int32, (2 * rows, width), 0)
     wanted = jnp.where(line < rows, spot(0) + line, spot(1) + line - rows)
     pick = lax.broadcasted_iota(jnp.int32, (2 * rows, width), 1) == wanted
     pick = jnp.where(pick, 1.0, 0.0).astype(BF16)
     picked = 2 * rows
-    stats_left = statistics(grad, turned)
-    stats_right = statistics(turned, grad)
+    stats_left = damped(
+        (near_outer[...], dot(near[...], far_turned[...]), dot(far[...], far_turned[...]))
+    )
+    stats_right = damped(
+        [
+            tile[...] + dot(far_turned[a, :], far[:, b])
+            for (a, b), tile in zip(((low, low), (low, high), (high, high)), near_tiles)
+        ]
+    )
     squares = [tile * tile for tile in stats_left]
     norm = jnp.sqrt(jnp.sum(squares[0] + 2.0 * squares[1] + squares[2], keepdims=True))
     scale = 2.5 / norm
@@ -265,7 +299,8 @@
     right[half:width, high] = upper_right
     right[:half, low] = upper_right.T
     right[:half, high] = jnp.where(goes_on, by_high[:half].astype(BF16), right[:half, high])
-    partial_value = dot(final_left, grad[...]).astype(BF16)
+    partial_value = dot(final_left[:, low], near[...]) + dot(final_left[:, high], far[...])
+    partial_value = partial_value.astype(BF16)
     update = dot(partial_value[:, low], right[half:width, :]) + dot(
         partial_value[:, high], right[:half, :]
     )
@@ -273,18 +308,18 @@
     send_ref[...] = update[rows:, :].astype(BF16)
 
 
-def root(counts, pieces, rows, most=4):
-    width = 4 * pieces[0].shape[0]
+def root(counts, early, fars, rows, most=4):
+    width = early[0].shape[1]
     square = pltpu.VMEM((width, width), BF16)
     out = jax.ShapeDtypeStruct((rows, width), BF16)
     return pl.pallas_call(
         functools.partial(root_kernel, most),
         out_shape=[out, out],
-        in_specs=[HBM] + [VMEM] * 6,
+        in_specs=[HBM] + [VMEM] * 8,
         out_specs=[VMEM] * 2,
         scratch_shapes=[
-            square,
-            square,
+            pltpu.VMEM((width // 2, width), BF16),
+            pltpu.VMEM((width, width // 2), BF16),
             pltpu.VMEM((2 * rows + width, width), BF16),
             pltpu.VMEM((2 * width, width), BF16),
             square,
@@ -295,7 +330,7 @@
             pltpu.SemaphoreType.DMA(()),
         ],
         compiler_params=params(40),
-    )(pltpu.with_memory_space_constraint(counts, pltpu.HBM), *pieces)
+    )(pltpu.with_memory_space_constraint(counts, pltpu.HBM), *early, *fars)
 
 
 def place_kernel(*refs):
@@ -349,7 +384,7 @@
     left, right, send_left, send_right = collect(
         width * 3 // 4, own, from_diagonal, from_column, from_line
     )
-    pieces = []
+    pieces, fars = [], []
     for own, send in ((left, send_left), (right, send_right)):
         mask = 2
         while mask < line:
@@ -358,8 +393,9 @@
             mask *= 2
         own = send
         other = swap(own, "z")
-        pieces += [own, other, swap(jnp.concatenate([own, other], 0), "core")]
-    keep, send = root(newton_counts, pieces, rows)
+        pieces += [own, other]
+        fars.append(swap(jnp.concatenate([own, other], 0), "core"))
+    keep, send = root(newton_counts, near_part(*pieces), fars, rows)
 
     pieces = []
     for turn in range(groups):

time: 42.3 us -> 42.5 us (level)
  Pallas kernels: 9.29 us -> 9.86 us
  transfers between devices with their start and end apart: 14 -> 14, of which waited for: 11 -> 11; matrix products, arithmetic and copies ran while one was open for 1% -> 1% of each run, Pallas kernels for 2% -> 3%
where the time goes in v15:
time: 42.5 us; the launch traced here: 42.3 us
  waiting for transfers between devices  17.8 us (42%)
  starting transfers between devices  14.3 us (34%)
  Pallas kernels  9.86 us (23%)
    ppermute x10, waiting for transfers between devices, swap(): lax.ppermute(array, axis, [(i, i ^ mask) for i in range(lax.axis_size(axi...  13.2 us
    ppermute x10, starting transfers between devices, swap(): lax.ppermute(array, axis, [(i, i ^ mask) for i in range(lax.axis_size(axi...  9.2 us
    pallas_call x1, Pallas kernels, root(): pl.pallas_call(functools.partial(root_kernel, most), out_shape=[out, out]...  6.35 us
    ppermute x3, starting transfers between devices, shards(): lax.ppermute(piece, ('x', 'group'), moves)  3.55 us
    ppermute x3, waiting for transfers between devices, shards(): lax.ppermute(piece, ('x', 'group'), moves)  3.26 us
    pallas_call x1, Pallas kernels, load(): pl.pallas_call(functools.partial(load_kernel, scale), out_shape=[jax.Shap...  1.61 us
    ppermute x1, starting transfers between devices, swap_diagonal(): return lax.ppermute(array, ('z', 'x'), moves)  1.55 us
    ppermute x1, waiting for transfers between devices, swap_diagonal(): return lax.ppermute(array, ('z', 'x'), moves)  1.4 us
  transfers between devices with their start and end apart: 14, of which 11 were waited for; matrix products, arithmetic and copies ran while one was open for 1% of the time, Pallas kernels for 3%

profile of v15, /device:TPU:0, one launch (start us, length us, event | category | flops | bytes accessed | tf_op | source)
XLA Modules:
  0.0 42.3 jit_solution(10705481638074151693)
XLA Ops:
  0.0 1.6 %shard_map.37 = (bf16[256,512]{1,0:T(8,128)(2,1)S(1)}, bf16[2,2,512,256]{3,2,1,0:T(8,128)(2,1)S(1)}, bf16[2,512,512]{2,1,0:T(8,128)(2,1)S(1)}) custom-call(bf16[2,512,512]{2,1,0:T(8,128)(2,1)} %patch_hbm.1, bf16[2,512,512]{2,1,0:T(8,128)(2,1)} %cot_hbm.1), custom_call_target="tpu_custom_call" | custom-call | tf_op jit(solution)/shard_map/pallas_call | solution.py:64
  1.6 0.5 %collective-permute-start = (bf16[256,512]{1,0:T(8,128)(2,1)S(1)}, bf16[256,512]{1,0:T(8,128)(2,1)S(1)}, u32[]{:S(2)}, u32[]{:S(2)}) collective-permute-start(bf16[256,512]{1,0:T(8,128)(2,1)S(1)} %get-tuple-element.25), channel_id=1, source_target_pairs={{0,2},{2,0},{1,3},{3,1},{4,6},{6,4},{5,7},{7,5},{8,10},{10,8},{9,1... | collective-permute-start | bytes 786440 | tf_op jit(solution)/shard_map/ppermute | solution.py:367
  2.1 0.5 %shard_map.38 = (f32[256,512]{1,0:T(8,128)S(1)}, bf16[256,512]{1,0:T(8,128)(2,1)S(1)}) custom-call(bf16[2,2,512,256]{3,2,1,0:T(8,128)(2,1)S(1)} %get-tuple-element.22.patch, bf16[2,512,512]{2,1,0:T(8,128)(2,1)S(1)} %get-tuple-element.23.cot), custom_call_target="tpu_custom_call" | custom-call | flops 268435456 | bytes 1048576 | tf_op jit(solution)/shard_map/pallas_call | solution.py:88
  2.6 0.1 collective-permute-start.1
  2.7 0.6 %collective-permute-done = bf16[256,512]{1,0:T(8,128)(2,1)S(1)} collective-permute-done((bf16[256,512]{1,0:T(8,128)(2,1)S(1)}, bf16[256,512]{1,0:T(8,128)(2,1)S(1)}, u32[]{:S(2)}, u32[]{:S(2)}) %collective-permute-start) | collective-permute-done | bytes 262176 | tf_op jit(solution)/shard_map/ppermute | solution.py:367
  3.3 0.1 add_convert_fusion
  3.4 2.9 %collective-permute-start.3 = (bf16[128,512]{1,0:T(8,128)(2,1)S(1)}, bf16[128,512]{1,0:T(8,128)(2,1)S(1)}, u32[]{:S(2)}, u32[]{:S(2)}) collective-permute-start(bf16[128,512]{1,0:T(8,128)(2,1)S(1)} %get-tuple-element.39), channel_id=1, source_target_pairs={{0,4},{4,0},{1,5},{5,1},{2,6},{6,2},{3,7},{7,3},{8,12},{12,8},{9,1... | collective-permute-start | bytes 393224 | tf_op jit(solution)/shard_map/ppermute | solution.py:367
  6.3 1.5 %collective-permute-start.2 = (bf16[128,512]{1,0:T(8,128)(2,1)S(1)}, bf16[128,512]{1,0:T(8,128)(2,1)S(1)}, u32[]{:S(2)}, u32[]{:S(2)}) collective-permute-start(bf16[128,512]{1,0:T(8,128)(2,1)S(1)} %get-tuple-element.40.refs_0_), channel_id=1, source_target_pairs={{0,12},{4,8},{8,4},{12,0},{16,28},{20,24},{24,20},{28,16},{1,13},{... | collective-permute-start | bytes 393224 | tf_op jit(solution)/shard_map/ppermute | solution.py:371
  7.9 0.3 shard_map.39
  8.2 0.0 collective-permute-done.1
  8.2 0.1 convert_add_fusion.own
  8.3 0.1 collective-permute-start.4
  8.4 3.8 %collective-permute-done.3.refs_1_ = bf16[128,512]{1,0:T(8,128)(2,1)S(1)} collective-permute-done((bf16[128,512]{1,0:T(8,128)(2,1)S(1)}, bf16[128,512]{1,0:T(8,128)(2,1)S(1)}, u32[]{:S(2)}, u32[]{:S(2)}) %collective-permute-start.3) | collective-permute-done | bytes 131104 | tf_op jit(solution)/shard_map/ppermute | solution.py:367
  12.2 1.4 %collective-permute-done.2.refs_0_ = bf16[128,512]{1,0:T(8,128)(2,1)S(1)} collective-permute-done((bf16[128,512]{1,0:T(8,128)(2,1)S(1)}, bf16[128,512]{1,0:T(8,128)(2,1)S(1)}, u32[]{:S(2)}, u32[]{:S(2)}) %collective-permute-start.2) | collective-permute-done | bytes 131104 | tf_op jit(solution)/shard_map/ppermute | solution.py:371
  13.6 0.6 %collective-permute-done.4.refs_2_ = bf16[128,512]{1,0:T(8,128)(2,1)S(1)} collective-permute-done((bf16[128,512]{1,0:T(8,128)(2,1)S(1)}, bf16[128,512]{1,0:T(8,128)(2,1)S(1)}, u32[]{:S(2)}, u32[]{:S(2)}) %collective-permute-start.4) | collective-permute-done | bytes 131104 | tf_op jit(solution)/shard_map/ppermute | solution.py:367
  14.3 0.1 shard_map.40
  14.3 2.8 %collective-permute-start.5 = (bf16[128,384]{1,0:T(8,128)(2,1)S(1)}, bf16[128,384]{1,0:T(8,128)(2,1)S(1)}, u32[]{:S(2)}, u32[]{:S(2)}) collective-permute-start(bf16[128,384]{1,0:T(8,128)(2,1)S(1)} %get-tuple-element.28), channel_id=1, source_target_pairs={{0,16},{8,24},{16,0},{24,8},{1,17},{9,25},{17,1},{25,9},{2,18},{10... | collective-permute-start | bytes 294920 | tf_op jit(solution)/shard_map/ppermute | solution.py:367
  17.1 0.2 collective-permute-start.7
  17.3 4.8 %collective-permute-done.5 = bf16[128,384]{1,0:T(8,128)(2,1)S(1)} collective-permute-done((bf16[128,384]{1,0:T(8,128)(2,1)S(1)}, bf16[128,384]{1,0:T(8,128)(2,1)S(1)}, u32[]{:S(2)}, u32[]{:S(2)}) %collective-permute-start.5) | collective-permute-done | bytes 98336 | tf_op jit(solution)/shard_map/ppermute | solution.py:367
  22.1 0.9 %collective-permute-start.6 = (bf16[128,384]{1,0:T(8,128)(2,1)S(1)}, bf16[128,384]{1,0:T(8,128)(2,1)S(1)}, u32[]{:S(2)}, u32[]{:S(2)}) collective-permute-start(bf16[128,384]{1,0:T(8,128)(2,1)S(1)} %add_convert_fusion.1.left_own), channel_id=1, source_target_pairs={{0,8},{8,0},{16,24},{24,16},{1,9},{9,1},{17,25},{25,17},{2,10},{10... | collective-permute-start | bytes 294920 | tf_op jit(solution)/shard_map/ppermute | solution.py:367
  23.1 0.0 collective-permute-done.7
  23.1 1.2 %collective-permute-start.8 = (bf16[128,128]{1,0:T(8,128)(2,1)S(1)}, bf16[128,128]{1,0:T(8,128)(2,1)S(1)}, u32[]{:S(2)}, u32[]{:S(2)}) collective-permute-start(bf16[128,128]{1,0:T(8,128)(2,1)S(1)} %add_convert_fusion.2.right_own), channel_id=1, source_target_pairs={{0,8},{8,0},{16,24},{24,16},{1,9},{9,1},{17,25},{25,17},{2,10},{10... | collective-permute-start | bytes 98312 | tf_op jit(solution)/shard_map/ppermute | solution.py:367
  24.3 2.5 %collective-permute-done.6.left_other = bf16[128,384]{1,0:T(8,128)(2,1)S(1)} collective-permute-done((bf16[128,384]{1,0:T(8,128)(2,1)S(1)}, bf16[128,384]{1,0:T(8,128)(2,1)S(1)}, u32[]{:S(2)}, u32[]{:S(2)}) %collective-permute-start.6) | collective-permute-done | bytes 98336 | tf_op jit(solution)/shard_map/ppermute | solution.py:367
  26.9 0.1 collective-permute-start.9
  26.9 0.2 collective-permute-done.8.right_other
  27.2 0.3 collective-permute-start.10
  27.5 0.4 shard_map.41
  27.9 0.6 %collective-permute-done.10.refs_7_ = bf16[256,128]{1,0:T(8,128)(2,1)S(1)} collective-permute-done((bf16[256,128]{1,0:T(8,128)(2,1)S(1)}, bf16[256,128]{1,0:T(8,128)(2,1)S(1)}, u32[]{:S(2)}, u32[]{:S(2)}) %collective-permute-start.10) | collective-permute-done | bytes 65568 | tf_op jit(solution)/shard_map/ppermute | solution.py:367
  28.5 0.0 collective-permute-done.9.refs_6_
  28.5 6.3 %shard_map.42 = (bf16[32,512]{1,0:T(8,128)(2,1)S(1)}, bf16[32,512]{1,0:T(8,128)(2,1)S(1)}) custom-call(s32[2,2]{1,0:T(2,128)} %counts_hbm.1, bf16[256,512]{1,0:T(8,128)(2,1)S(1)} %get-tuple-element.31.refs_0_, bf16[512,256]{1,0:T(8,128)(2,1)S(1)} %get-tuple-element.32.refs_1_, f32[256,256]{1,0:T(8,128)S(1)} %get-tuple-element.33.refs_2_, ...), custom_call_target="tpu_custom_call" | custom-call | tf_op jit(solution)/shard_map/pallas_call | solution.py:315
  34.8 1.5 %collective-permute-start.12 = (bf16[32,512]{1,0:T(8,128)(2,1)S(1)}, bf16[32,512]{1,0:T(8,128)(2,1)S(1)}, u32[]{:S(2)}, u32[]{:S(2)}) collective-permute-start(bf16[32,512]{1,0:T(8,128)(2,1)S(1)} %get-tuple-element.37.refs_0_), channel_id=1, source_target_pairs={{0,1},{1,0},{4,5},{5,4},{2,3},{3,2},{6,7},{7,6},{8,9},{9,8},{12,13... | collective-permute-start | bytes 98312 | tf_op jit(solution)/shard_map/ppermute | solution.py:409
  36.3 1.4 %collective-permute-start.13 = (bf16[32,512]{1,0:T(8,128)(2,1)S(1)}, bf16[32,512]{1,0:T(8,128)(2,1)S(1)}, u32[]{:S(2)}, u32[]{:S(2)}) collective-permute-start(bf16[32,512]{1,0:T(8,128)(2,1)S(1)} %get-tuple-element.38), channel_id=1, source_target_pairs={{0,5},{1,4},{4,1},{5,0},{2,7},{3,6},{6,3},{7,2},{8,13},{9,12},{12,... | collective-permute-start | bytes 98312 | tf_op jit(solution)/shard_map/ppermute | solution.py:409
  37.7 0.7 %collective-permute-start.11 = (bf16[32,512]{1,0:T(8,128)(2,1)S(1)}, bf16[32,512]{1,0:T(8,128)(2,1)S(1)}, u32[]{:S(2)}, u32[]{:S(2)}) collective-permute-start(bf16[32,512]{1,0:T(8,128)(2,1)S(1)} %get-tuple-element.38), channel_id=1, source_target_pairs={{0,4},{1,5},{4,0},{5,1},{2,6},{3,7},{6,2},{7,3},{8,12},{9,13},{12,... | collective-permute-start | bytes 98312 | tf_op jit(solution)/shard_map/ppermute | solution.py:409
  38.4 0.4 %collective-permute-done.12.refs_2_ = bf16[32,512]{1,0:T(8,128)(2,1)S(1)} collective-permute-done((bf16[32,512]{1,0:T(8,128)(2,1)S(1)}, bf16[32,512]{1,0:T(8,128)(2,1)S(1)}, u32[]{:S(2)}, u32[]{:S(2)}) %collective-permute-start.12) | collective-permute-done | bytes 32800 | tf_op jit(solution)/shard_map/ppermute | solution.py:409
  38.8 2.4 %collective-permute-done.13.refs_3_ = bf16[32,512]{1,0:T(8,128)(2,1)S(1)} collective-permute-done((bf16[32,512]{1,0:T(8,128)(2,1)S(1)}, bf16[32,512]{1,0:T(8,128)(2,1)S(1)}, u32[]{:S(2)}, u32[]{:S(2)}) %collective-permute-start.13) | collective-permute-done | bytes 32800 | tf_op jit(solution)/shard_map/ppermute | solution.py:409
  41.2 0.4 collective-permute-done.11.refs_1_
  41.6 0.7 %shard_map.43 = bf16[4,32,512]{2,1,0:T(8,128)(2,1)} custom-call(bf16[32,512]{1,0:T(8,128)(2,1)S(1)} %get-tuple-element.37.refs_0_, bf16[32,512]{1,0:T(8,128)(2,1)S(1)} %collective-permute-done.11.refs_1_, bf16[32,512]{1,0:T(8,128)(2,1)S(1)} %collective-permute-done.12.refs_2_, bf16[32,512]{1,0:T(8,128)(2,1)S(1)} %collective-permute-done.13.refs_3_), custom_call_target="tpu_custom_call" | custom-call | tf_op jit(solution)/shard_map/pallas_call | solution.py:350
  (6 shorter events, 0.1 us)
Async XLA Ops:
  1.6 1.7 %collective-permute-start = (bf16[256,512]{1,0:T(8,128)(2,1)S(1)}, bf16[256,512]{1,0:T(8,128)(2,1)S(1)}, u32[]{:S(2)}, u32[]{:S(2)}) collective-permute-start(bf16[256,512]{1,0:T(8,128)(2,1)S(1)} %get-tuple-element.25), channel_id=1, source_target_pairs={{0,2},{2,0},{1,3},{3,1},{4,6},{6,4},{5,7},{7,5},{8,10},{10,8},{9,1... | collective-permute-start | bytes 786440 | tf_op jit(solution)/shard_map/ppermute | solution.py:367
  2.6 5.6 %collective-permute-start.1 = (bf16[256,512]{1,0:T(8,128)(2,1)S(1)}, bf16[256,512]{1,0:T(8,128)(2,1)S(1)}, u32[]{:S(2)}, u32[]{:S(2)}) collective-permute-start(bf16[256,512]{1,0:T(8,128)(2,1)S(1)} %get-tuple-element.26), channel_id=1, source_target_pairs={{0,2},{2,0},{1,3},{3,1},{4,6},{6,4},{5,7},{7,5},{8,10},{10,8},{9,1... | collective-permute-start | bytes 786440 | tf_op jit(solution)/shard_map/ppermute | solution.py:367
  3.4 8.8 %collective-permute-start.3 = (bf16[128,512]{1,0:T(8,128)(2,1)S(1)}, bf16[128,512]{1,0:T(8,128)(2,1)S(1)}, u32[]{:S(2)}, u32[]{:S(2)}) collective-permute-start(bf16[128,512]{1,0:T(8,128)(2,1)S(1)} %get-tuple-element.39), channel_id=1, source_target_pairs={{0,4},{4,0},{1,5},{5,1},{2,6},{6,2},{3,7},{7,3},{8,12},{12,8},{9,1... | collective-permute-start | bytes 393224 | tf_op jit(solution)/shard_map/ppermute | solution.py:367
  6.3 7.3 %collective-permute-start.2 = (bf16[128,512]{1,0:T(8,128)(2,1)S(1)}, bf16[128,512]{1,0:T(8,128)(2,1)S(1)}, u32[]{:S(2)}, u32[]{:S(2)}) collective-permute-start(bf16[128,512]{1,0:T(8,128)(2,1)S(1)} %get-tuple-element.40.refs_0_), channel_id=1, source_target_pairs={{0,12},{4,8},{8,4},{12,0},{16,28},{20,24},{24,20},{28,16},{1,13},{... | collective-permute-start | bytes 393224 | tf_op jit(solution)/shard_map/ppermute | solution.py:371
  8.3 6.0 %collective-permute-start.4 = (bf16[128,512]{1,0:T(8,128)(2,1)S(1)}, bf16[128,512]{1,0:T(8,128)(2,1)S(1)}, u32[]{:S(2)}, u32[]{:S(2)}) collective-permute-start(bf16[128,512]{1,0:T(8,128)(2,1)S(1)} %slice.17), channel_id=1, source_target_pairs={{0,8},{8,0},{16,24},{24,16},{1,9},{9,1},{17,25},{25,17},{2,10},{10... | collective-permute-start | bytes 393224 | tf_op jit(solution)/shard_map/ppermute | solution.py:367
  14.3 7.8 %collective-permute-start.5 = (bf16[128,384]{1,0:T(8,128)(2,1)S(1)}, bf16[128,384]{1,0:T(8,128)(2,1)S(1)}, u32[]{:S(2)}, u32[]{:S(2)}) collective-permute-start(bf16[128,384]{1,0:T(8,128)(2,1)S(1)} %get-tuple-element.28), channel_id=1, source_target_pairs={{0,16},{8,24},{16,0},{24,8},{1,17},{9,25},{17,1},{25,9},{2,18},{10... | collective-permute-start | bytes 294920 | tf_op jit(solution)/shard_map/ppermute | solution.py:367
  17.1 6.0 %collective-permute-start.7 = (bf16[128,128]{1,0:T(8,128)(2,1)S(1)}, bf16[128,128]{1,0:T(8,128)(2,1)S(1)}, u32[]{:S(2)}, u32[]{:S(2)}) collective-permute-start(bf16[128,128]{1,0:T(8,128)(2,1)S(1)} %get-tuple-element.30), channel_id=1, source_target_pairs={{0,16},{8,24},{16,0},{24,8},{1,17},{9,25},{17,1},{25,9},{2,18},{10... | collective-permute-start | bytes 98312 | tf_op jit(solution)/shard_map/ppermute | solution.py:367
  22.1 4.7 %collective-permute-start.6 = (bf16[128,384]{1,0:T(8,128)(2,1)S(1)}, bf16[128,384]{1,0:T(8,128)(2,1)S(1)}, u32[]{:S(2)}, u32[]{:S(2)}) collective-permute-start(bf16[128,384]{1,0:T(8,128)(2,1)S(1)} %add_convert_fusion.1.left_own), channel_id=1, source_target_pairs={{0,8},{8,0},{16,24},{24,16},{1,9},{9,1},{17,25},{25,17},{2,10},{10... | collective-permute-start | bytes 294920 | tf_op jit(solution)/shard_map/ppermute | solution.py:367
  23.1 4.1 %collective-permute-start.8 = (bf16[128,128]{1,0:T(8,128)(2,1)S(1)}, bf16[128,128]{1,0:T(8,128)(2,1)S(1)}, u32[]{:S(2)}, u32[]{:S(2)}) collective-permute-start(bf16[128,128]{1,0:T(8,128)(2,1)S(1)} %add_convert_fusion.2.right_own), channel_id=1, source_target_pairs={{0,8},{8,0},{16,24},{24,16},{1,9},{9,1},{17,25},{25,17},{2,10},{10... | collective-permute-start | bytes 98312 | tf_op jit(solution)/shard_map/ppermute | solution.py:367
  26.9 1.6 %collective-permute-start.9 = (bf16[256,384]{1,0:T(8,128)(2,1)S(1)}, bf16[256,384]{1,0:T(8,128)(2,1)S(1)}, u32[]{:S(2)}, u32[]{:S(2)}) collective-permute-start(bf16[256,384]{1,0:T(8,128)(2,1)S(1)} %pad_maximum_fusion), channel_id=1, source_target_pairs={{0,2},{2,0},{1,3},{3,1},{4,6},{6,4},{5,7},{7,5},{8,10},{10,8},{9,1... | collective-permute-start | bytes 589832 | tf_op jit(solution)/shard_map/ppermute | solution.py:367
  27.2 1.3 %collective-permute-start.10 = (bf16[256,128]{1,0:T(8,128)(2,1)S(1)}, bf16[256,128]{1,0:T(8,128)(2,1)S(1)}, u32[]{:S(2)}, u32[]{:S(2)}) collective-permute-start(bf16[256,128]{1,0:T(8,128)(2,1)S(1)} %pad_maximum_fusion.1), channel_id=1, source_target_pairs={{0,2},{2,0},{1,3},{3,1},{4,6},{6,4},{5,7},{7,5},{8,10},{10,8},{9,1... | collective-permute-start | bytes 196616 | tf_op jit(solution)/shard_map/ppermute | solution.py:367
  34.8 4.0 %collective-permute-start.12 = (bf16[32,512]{1,0:T(8,128)(2,1)S(1)}, bf16[32,512]{1,0:T(8,128)(2,1)S(1)}, u32[]{:S(2)}, u32[]{:S(2)}) collective-permute-start(bf16[32,512]{1,0:T(8,128)(2,1)S(1)} %get-tuple-element.37.refs_0_), channel_id=1, source_target_pairs={{0,1},{1,0},{4,5},{5,4},{2,3},{3,2},{6,7},{7,6},{8,9},{9,8},{12,13... | collective-permute-start | bytes 98312 | tf_op jit(solution)/shard_map/ppermute | solution.py:409
  36.3 4.9 %collective-permute-start.13 = (bf16[32,512]{1,0:T(8,128)(2,1)S(1)}, bf16[32,512]{1,0:T(8,128)(2,1)S(1)}, u32[]{:S(2)}, u32[]{:S(2)}) collective-permute-start(bf16[32,512]{1,0:T(8,128)(2,1)S(1)} %get-tuple-element.38), channel_id=1, source_target_pairs={{0,5},{1,4},{4,1},{5,0},{2,7},{3,6},{6,3},{7,2},{8,13},{9,12},{12,... | collective-permute-start | bytes 98312 | tf_op jit(solution)/shard_map/ppermute | solution.py:409
  37.7 3.9 %collective-permute-start.11 = (bf16[32,512]{1,0:T(8,128)(2,1)S(1)}, bf16[32,512]{1,0:T(8,128)(2,1)S(1)}, u32[]{:S(2)}, u32[]{:S(2)}) collective-permute-start(bf16[32,512]{1,0:T(8,128)(2,1)S(1)} %get-tuple-element.38), channel_id=1, source_target_pairs={{0,4},{1,5},{4,0},{5,1},{2,6},{3,7},{6,2},{7,3},{8,12},{9,13},{12,... | collective-permute-start | bytes 98312 | tf_op jit(solution)/shard_map/ppermute | solution.py:409

commit v16 on v13

--- a/solution.py
+++ b/solution.py
@@ -214,35 +214,9 @@
 
     counts_copy.wait()
     count_left, count_right = counts[column, 0], counts[column, 1]
-    for index in range(1, most):
-        q_left, q_right = left.at[picked:, :], right.at[width:, :]
-        if index == 1:
-            fill(s_left, 0, square(q_left))
-            fill(s_right, 0, square(q_right))
-        else:
-            by_high = dot(left[...], q_left[:, high])
-            by_low = dot(left[: picked + half, :], q_left[:, low])
-            right_by_high = dot(right[...], q_right[:, high])
-            right_by_low = dot(right[half : width + half, :], q_right[:, low])
-            fill(s_left, 0, (by_low[picked:], by_high[picked : picked + half], by_high[picked + half :]))
-            fill(
-                s_right,
-                0,
-                (right_by_low[half:], right_by_high[width : width + half], right_by_high[width + half :]),
-            )
-
-            def keep_if(ref, value, goes_on):
-                value = value.astype(BF16)
-                return value if index == 2 else jnp.where(goes_on, value, ref)
-
-            left[:picked, low] = keep_if(left[:picked, low], by_low[:picked], index <= count_left)
-            left[:picked, high] = keep_if(left[:picked, high], by_high[:picked], index <= count_left)
-            goes_on = index <= count_right
-            upper_right = keep_if(right[half:width, high], right_by_high[half:width], goes_on)
-            right[half:width, low] = keep_if(right[half:width, low], right_by_low[:half], goes_on)
-            right[half:width, high] = upper_right
-            right[:half, low] = upper_right.T
-            right[:half, high] = keep_if(right[:half, high], right_by_high[:half], goes_on)
+    q_left, q_right = left.at[picked:, :], right.at[width:, :]
+
+    def finish_sweep(last):
         fourths = square(s_left), square(s_right)
         fill(s_left, 0, fourths[0])
         fill(s_right, 0, fourths[1])
@@ -252,9 +226,40 @@
         ):
             by_high = dot(fourth[...], moment_ref[:, high])
             tiles = (dot(fourth[low, :], moment_ref[:, low]), by_high[low], by_high[high])
-            if index < most - 1:
+            if not last:
                 fill(moment_ref, 0, tiles)
             fill(ref, start, factor(tiles))
+
+    def keep_if(old, value, goes_on):
+        return jnp.where(goes_on, value.astype(BF16), old)
+
+    def sweep(index, carry):
+        finish_sweep(False)
+        by_high = dot(left[...], q_left[:, high])
+        by_low = dot(left[: picked + half, :], q_left[:, low])
+        right_by_high = dot(right[...], q_right[:, high])
+        right_by_low = dot(right[half : width + half, :], q_right[:, low])
+        fill(s_left, 0, (by_low[picked:], by_high[picked : picked + half], by_high[picked + half :]))
+        fill(
+            s_right,
+            0,
+            (right_by_low[half:], right_by_high[width : width + half], right_by_high[width + half :]),
+        )
+        goes_on = index <= count_left
+        left[:picked, low] = keep_if(left[:picked, low], by_low[:picked], goes_on)
+        left[:picked, high] = keep_if(left[:picked, high], by_high[:picked], goes_on)
+        goes_on = index <= count_right
+        upper_right = keep_if(right[half:width, high], right_by_high[half:width], goes_on)
+        right[half:width, low] = keep_if(right[half:width, low], right_by_low[:half], goes_on)
+        right[half:width, high] = upper_right
+        right[:half, low] = upper_right.T
+        right[:half, high] = keep_if(right[:half, high], right_by_high[:half], goes_on)
+        return carry
+
+    fill(s_left, 0, square(q_left))
+    fill(s_right, 0, square(q_right))
+    lax.fori_loop(2, most, sweep, 0)
+    finish_sweep(True)
     final_left = dot(left[:picked, :], left[picked:, :]).astype(BF16)
     final_left = jnp.where(most <= count_left, final_left, left[:picked, :])
     by_high = dot(right[:width, :], right[width:, high])

time: 42.3 us -> 42.9 us (1.014)
  Pallas kernels: 9.29 us -> 9.96 us
    pallas_call x1, Pallas kernels: 6.15 us -> 6.83 us  [root(): pl.pallas_call(functools.partial(root_kernel, most), out_shape=[out, out]...]
where the time goes in v16:
time: 42.9 us; the launch traced here: 42.8 us
  waiting for transfers between devices  18.2 us (42%)
  starting transfers between devices  14.3 us (33%)
  Pallas kernels  9.96 us (23%)
    ppermute x10, waiting for transfers between devices, swap(): lax.ppermute(array, axis, [(i, i ^ mask) for i in range(lax.axis_size(axi...  13.5 us
    ppermute x10, starting transfers between devices, swap(): lax.ppermute(array, axis, [(i, i ^ mask) for i in range(lax.axis_size(axi...  9.2 us
    pallas_call x1, Pallas kernels, root(): pl.pallas_call(functools.partial(root_kernel, most), out_shape=[out, out]...  6.83 us
    ppermute x3, starting transfers between devices, shards(): lax.ppermute(piece, ('x', 'group'), moves)  3.55 us
    ppermute x3, waiting for transfers between devices, shards(): lax.ppermute(piece, ('x', 'group'), moves)  3.26 us
    pallas_call x1, Pallas kernels, load(): pl.pallas_call(functools.partial(load_kernel, scale), out_shape=[jax.Shap...  1.61 us
    ppermute x1, starting transfers between devices, swap_diagonal(): return lax.ppermute(array, ('z', 'x'), moves)  1.55 us
    ppermute x1, waiting for transfers between devices, swap_diagonal(): return lax.ppermute(array, ('z', 'x'), moves)  1.4 us
  transfers between devices with their start and end apart: 14, of which 11 were waited for; matrix products, arithmetic and copies ran while one was open for 1% of the time, Pallas kernels for 2%

profile of v16, /device:TPU:0, one launch (start us, length us, event | category | flops | bytes accessed | tf_op | source)
XLA Modules:
  0.0 42.8 jit_solution(12722153237669896753)
XLA Ops:
  0.0 1.6 %shard_map.37 = (bf16[256,512]{1,0:T(8,128)(2,1)S(1)}, bf16[2,2,512,256]{3,2,1,0:T(8,128)(2,1)S(1)}, bf16[2,512,512]{2,1,0:T(8,128)(2,1)S(1)}) custom-call(bf16[2,512,512]{2,1,0:T(8,128)(2,1)} %patch_hbm.1, bf16[2,512,512]{2,1,0:T(8,128)(2,1)} %cot_hbm.1), custom_call_target="tpu_custom_call" | custom-call | tf_op jit(solution)/shard_map/pallas_call | solution.py:64
  1.6 0.5 %collective-permute-start = (bf16[256,512]{1,0:T(8,128)(2,1)S(1)}, bf16[256,512]{1,0:T(8,128)(2,1)S(1)}, u32[]{:S(2)}, u32[]{:S(2)}) collective-permute-start(bf16[256,512]{1,0:T(8,128)(2,1)S(1)} %get-tuple-element.19), channel_id=1, source_target_pairs={{0,2},{2,0},{1,3},{3,1},{4,6},{6,4},{5,7},{7,5},{8,10},{10,8},{9,1... | collective-permute-start | bytes 786440 | tf_op jit(solution)/shard_map/ppermute | solution.py:337
  2.1 0.5 %shard_map.38 = (f32[256,512]{1,0:T(8,128)S(1)}, bf16[256,512]{1,0:T(8,128)(2,1)S(1)}) custom-call(bf16[2,2,512,256]{3,2,1,0:T(8,128)(2,1)S(1)} %get-tuple-element.16.patch, bf16[2,512,512]{2,1,0:T(8,128)(2,1)S(1)} %get-tuple-element.17.cot), custom_call_target="tpu_custom_call" | custom-call | flops 268435456 | bytes 1048576 | tf_op jit(solution)/shard_map/pallas_call | solution.py:88
  2.6 0.1 collective-permute-start.1
  2.7 0.6 %collective-permute-done = bf16[256,512]{1,0:T(8,128)(2,1)S(1)} collective-permute-done((bf16[256,512]{1,0:T(8,128)(2,1)S(1)}, bf16[256,512]{1,0:T(8,128)(2,1)S(1)}, u32[]{:S(2)}, u32[]{:S(2)}) %collective-permute-start) | collective-permute-done | bytes 262176 | tf_op jit(solution)/shard_map/ppermute | solution.py:337
  3.3 0.1 add_convert_fusion
  3.4 2.9 %collective-permute-start.3 = (bf16[128,512]{1,0:T(8,128)(2,1)S(1)}, bf16[128,512]{1,0:T(8,128)(2,1)S(1)}, u32[]{:S(2)}, u32[]{:S(2)}) collective-permute-start(bf16[128,512]{1,0:T(8,128)(2,1)S(1)} %get-tuple-element.27), channel_id=1, source_target_pairs={{0,4},{4,0},{1,5},{5,1},{2,6},{6,2},{3,7},{7,3},{8,12},{12,8},{9,1... | collective-permute-start | bytes 393224 | tf_op jit(solution)/shard_map/ppermute | solution.py:337
  6.3 1.5 %collective-permute-start.2 = (bf16[128,512]{1,0:T(8,128)(2,1)S(1)}, bf16[128,512]{1,0:T(8,128)(2,1)S(1)}, u32[]{:S(2)}, u32[]{:S(2)}) collective-permute-start(bf16[128,512]{1,0:T(8,128)(2,1)S(1)} %get-tuple-element.28.refs_0_), channel_id=1, source_target_pairs={{0,12},{4,8},{8,4},{12,0},{16,28},{20,24},{24,20},{28,16},{1,13},{... | collective-permute-start | bytes 393224 | tf_op jit(solution)/shard_map/ppermute | solution.py:341
  7.9 0.3 shard_map.39
  8.2 0.0 collective-permute-done.1
  8.2 0.1 convert_add_fusion.own
  8.3 0.1 collective-permute-start.4
  8.4 3.8 %collective-permute-done.3.refs_1_ = bf16[128,512]{1,0:T(8,128)(2,1)S(1)} collective-permute-done((bf16[128,512]{1,0:T(8,128)(2,1)S(1)}, bf16[128,512]{1,0:T(8,128)(2,1)S(1)}, u32[]{:S(2)}, u32[]{:S(2)}) %collective-permute-start.3) | collective-permute-done | bytes 131104 | tf_op jit(solution)/shard_map/ppermute | solution.py:337
  12.2 1.4 %collective-permute-done.2.refs_0_ = bf16[128,512]{1,0:T(8,128)(2,1)S(1)} collective-permute-done((bf16[128,512]{1,0:T(8,128)(2,1)S(1)}, bf16[128,512]{1,0:T(8,128)(2,1)S(1)}, u32[]{:S(2)}, u32[]{:S(2)}) %collective-permute-start.2) | collective-permute-done | bytes 131104 | tf_op jit(solution)/shard_map/ppermute | solution.py:341
  13.6 0.6 %collective-permute-done.4.refs_2_ = bf16[128,512]{1,0:T(8,128)(2,1)S(1)} collective-permute-done((bf16[128,512]{1,0:T(8,128)(2,1)S(1)}, bf16[128,512]{1,0:T(8,128)(2,1)S(1)}, u32[]{:S(2)}, u32[]{:S(2)}) %collective-permute-start.4) | collective-permute-done | bytes 131104 | tf_op jit(solution)/shard_map/ppermute | solution.py:337
  14.3 0.1 shard_map.40
  14.3 2.8 %collective-permute-start.5 = (bf16[128,384]{1,0:T(8,128)(2,1)S(1)}, bf16[128,384]{1,0:T(8,128)(2,1)S(1)}, u32[]{:S(2)}, u32[]{:S(2)}) collective-permute-start(bf16[128,384]{1,0:T(8,128)(2,1)S(1)} %get-tuple-element.22), channel_id=1, source_target_pairs={{0,16},{8,24},{16,0},{24,8},{1,17},{9,25},{17,1},{25,9},{2,18},{10... | collective-permute-start | bytes 294920 | tf_op jit(solution)/shard_map/ppermute | solution.py:337
  17.1 0.2 collective-permute-start.8
  17.3 4.8 %collective-permute-done.5 = bf16[128,384]{1,0:T(8,128)(2,1)S(1)} collective-permute-done((bf16[128,384]{1,0:T(8,128)(2,1)S(1)}, bf16[128,384]{1,0:T(8,128)(2,1)S(1)}, u32[]{:S(2)}, u32[]{:S(2)}) %collective-permute-start.5) | collective-permute-done | bytes 98336 | tf_op jit(solution)/shard_map/ppermute | solution.py:337
  22.2 0.9 %collective-permute-start.6 = (bf16[128,384]{1,0:T(8,128)(2,1)S(1)}, bf16[128,384]{1,0:T(8,128)(2,1)S(1)}, u32[]{:S(2)}, u32[]{:S(2)}) collective-permute-start(bf16[128,384]{1,0:T(8,128)(2,1)S(1)} %add_convert_fusion.1.refs_0_), channel_id=1, source_target_pairs={{0,8},{8,0},{16,24},{24,16},{1,9},{9,1},{17,25},{25,17},{2,10},{10... | collective-permute-start | bytes 294920 | tf_op jit(solution)/shard_map/ppermute | solution.py:337
  23.1 0.0 collective-permute-done.8
  23.1 1.2 %collective-permute-start.9 = (bf16[128,128]{1,0:T(8,128)(2,1)S(1)}, bf16[128,128]{1,0:T(8,128)(2,1)S(1)}, u32[]{:S(2)}, u32[]{:S(2)}) collective-permute-start(bf16[128,128]{1,0:T(8,128)(2,1)S(1)} %add_convert_fusion.2.refs_3_), channel_id=1, source_target_pairs={{0,8},{8,0},{16,24},{24,16},{1,9},{9,1},{17,25},{25,17},{2,10},{10... | collective-permute-start | bytes 98312 | tf_op jit(solution)/shard_map/ppermute | solution.py:337
  24.3 2.5 %collective-permute-done.6.refs_1_ = bf16[128,384]{1,0:T(8,128)(2,1)S(1)} collective-permute-done((bf16[128,384]{1,0:T(8,128)(2,1)S(1)}, bf16[128,384]{1,0:T(8,128)(2,1)S(1)}, u32[]{:S(2)}, u32[]{:S(2)}) %collective-permute-start.6) | collective-permute-done | bytes 98336 | tf_op jit(solution)/shard_map/ppermute | solution.py:337
  26.9 0.1 collective-permute-start.7
  26.9 0.2 collective-permute-done.9.refs_4_
  27.2 0.3 collective-permute-start.10
  27.5 0.9 %collective-permute-done.10.refs_5_ = bf16[256,128]{1,0:T(8,128)(2,1)S(1)} collective-permute-done((bf16[256,128]{1,0:T(8,128)(2,1)S(1)}, bf16[256,128]{1,0:T(8,128)(2,1)S(1)}, u32[]{:S(2)}, u32[]{:S(2)}) %collective-permute-start.10) | collective-permute-done | bytes 65568 | tf_op jit(solution)/shard_map/ppermute | solution.py:337
  28.5 0.0 collective-permute-done.7.refs_2_
  28.5 6.8 %shard_map.41 = (bf16[32,512]{1,0:T(8,128)(2,1)S(1)}, bf16[32,512]{1,0:T(8,128)(2,1)S(1)}) custom-call(s32[2,2]{1,0:T(2,128)} %counts_hbm.1, bf16[128,384]{1,0:T(8,128)(2,1)S(1)} %add_convert_fusion.1.refs_0_, bf16[128,384]{1,0:T(8,128)(2,1)S(1)} %collective-permute-done.6.refs_1_, bf16[256,384]{1,0:T(8,128)(2,1)S(1)} %collective-permute-done.7.refs_2_, ...), custom_call_target="tpu_custom_call" | custom-call | tf_op jit(solution)/shard_map/pallas_call | solution.py:285
  35.3 1.5 %collective-permute-start.12 = (bf16[32,512]{1,0:T(8,128)(2,1)S(1)}, bf16[32,512]{1,0:T(8,128)(2,1)S(1)}, u32[]{:S(2)}, u32[]{:S(2)}) collective-permute-start(bf16[32,512]{1,0:T(8,128)(2,1)S(1)} %get-tuple-element.25.refs_0_), channel_id=1, source_target_pairs={{0,1},{1,0},{4,5},{5,4},{2,3},{3,2},{6,7},{7,6},{8,9},{9,8},{12,13... | collective-permute-start | bytes 98312 | tf_op jit(solution)/shard_map/ppermute | solution.py:378
  36.8 1.4 %collective-permute-start.13 = (bf16[32,512]{1,0:T(8,128)(2,1)S(1)}, bf16[32,512]{1,0:T(8,128)(2,1)S(1)}, u32[]{:S(2)}, u32[]{:S(2)}) collective-permute-start(bf16[32,512]{1,0:T(8,128)(2,1)S(1)} %get-tuple-element.26), channel_id=1, source_target_pairs={{0,5},{1,4},{4,1},{5,0},{2,7},{3,6},{6,3},{7,2},{8,13},{9,12},{12,... | collective-permute-start | bytes 98312 | tf_op jit(solution)/shard_map/ppermute | solution.py:378
  38.2 0.7 %collective-permute-start.11 = (bf16[32,512]{1,0:T(8,128)(2,1)S(1)}, bf16[32,512]{1,0:T(8,128)(2,1)S(1)}, u32[]{:S(2)}, u32[]{:S(2)}) collective-permute-start(bf16[32,512]{1,0:T(8,128)(2,1)S(1)} %get-tuple-element.26), channel_id=1, source_target_pairs={{0,4},{1,5},{4,0},{5,1},{2,6},{3,7},{6,2},{7,3},{8,12},{9,13},{12,... | collective-permute-start | bytes 98312 | tf_op jit(solution)/shard_map/ppermute | solution.py:378
  38.9 0.4 collective-permute-done.12.refs_2_
  39.3 2.4 %collective-permute-done.13.refs_3_ = bf16[32,512]{1,0:T(8,128)(2,1)S(1)} collective-permute-done((bf16[32,512]{1,0:T(8,128)(2,1)S(1)}, bf16[32,512]{1,0:T(8,128)(2,1)S(1)}, u32[]{:S(2)}, u32[]{:S(2)}) %collective-permute-start.13) | collective-permute-done | bytes 32800 | tf_op jit(solution)/shard_map/ppermute | solution.py:378
  41.7 0.4 collective-permute-done.11.refs_1_
  42.1 0.7 %shard_map.42 = bf16[4,32,512]{2,1,0:T(8,128)(2,1)} custom-call(bf16[32,512]{1,0:T(8,128)(2,1)S(1)} %get-tuple-element.25.refs_0_, bf16[32,512]{1,0:T(8,128)(2,1)S(1)} %collective-permute-done.11.refs_1_, bf16[32,512]{1,0:T(8,128)(2,1)S(1)} %collective-permute-done.12.refs_2_, bf16[32,512]{1,0:T(8,128)(2,1)S(1)} %collective-permute-done.13.refs_3_), custom_call_target="tpu_custom_call" | custom-call | tf_op jit(solution)/shard_map/pallas_call | solution.py:320
  (6 shorter events, 0.1 us)
Async XLA Ops:
  1.6 1.7 %collective-permute-start = (bf16[256,512]{1,0:T(8,128)(2,1)S(1)}, bf16[256,512]{1,0:T(8,128)(2,1)S(1)}, u32[]{:S(2)}, u32[]{:S(2)}) collective-permute-start(bf16[256,512]{1,0:T(8,128)(2,1)S(1)} %get-tuple-element.19), channel_id=1, source_target_pairs={{0,2},{2,0},{1,3},{3,1},{4,6},{6,4},{5,7},{7,5},{8,10},{10,8},{9,1... | collective-permute-start | bytes 786440 | tf_op jit(solution)/shard_map/ppermute | solution.py:337
  2.6 5.6 %collective-permute-start.1 = (bf16[256,512]{1,0:T(8,128)(2,1)S(1)}, bf16[256,512]{1,0:T(8,128)(2,1)S(1)}, u32[]{:S(2)}, u32[]{:S(2)}) collective-permute-start(bf16[256,512]{1,0:T(8,128)(2,1)S(1)} %get-tuple-element.20), channel_id=1, source_target_pairs={{0,2},{2,0},{1,3},{3,1},{4,6},{6,4},{5,7},{7,5},{8,10},{10,8},{9,1... | collective-permute-start | bytes 786440 | tf_op jit(solution)/shard_map/ppermute | solution.py:337
  3.4 8.8 %collective-permute-start.3 = (bf16[128,512]{1,0:T(8,128)(2,1)S(1)}, bf16[128,512]{1,0:T(8,128)(2,1)S(1)}, u32[]{:S(2)}, u32[]{:S(2)}) collective-permute-start(bf16[128,512]{1,0:T(8,128)(2,1)S(1)} %get-tuple-element.27), channel_id=1, source_target_pairs={{0,4},{4,0},{1,5},{5,1},{2,6},{6,2},{3,7},{7,3},{8,12},{12,8},{9,1... | collective-permute-start | bytes 393224 | tf_op jit(solution)/shard_map/ppermute | solution.py:337
  6.3 7.3 %collective-permute-start.2 = (bf16[128,512]{1,0:T(8,128)(2,1)S(1)}, bf16[128,512]{1,0:T(8,128)(2,1)S(1)}, u32[]{:S(2)}, u32[]{:S(2)}) collective-permute-start(bf16[128,512]{1,0:T(8,128)(2,1)S(1)} %get-tuple-element.28.refs_0_), channel_id=1, source_target_pairs={{0,12},{4,8},{8,4},{12,0},{16,28},{20,24},{24,20},{28,16},{1,13},{... | collective-permute-start | bytes 393224 | tf_op jit(solution)/shard_map/ppermute | solution.py:341
  8.3 6.0 %collective-permute-start.4 = (bf16[128,512]{1,0:T(8,128)(2,1)S(1)}, bf16[128,512]{1,0:T(8,128)(2,1)S(1)}, u32[]{:S(2)}, u32[]{:S(2)}) collective-permute-start(bf16[128,512]{1,0:T(8,128)(2,1)S(1)} %slice.17), channel_id=1, source_target_pairs={{0,8},{8,0},{16,24},{24,16},{1,9},{9,1},{17,25},{25,17},{2,10},{10... | collective-permute-start | bytes 393224 | tf_op jit(solution)/shard_map/ppermute | solution.py:337
  14.3 7.8 %collective-permute-start.5 = (bf16[128,384]{1,0:T(8,128)(2,1)S(1)}, bf16[128,384]{1,0:T(8,128)(2,1)S(1)}, u32[]{:S(2)}, u32[]{:S(2)}) collective-permute-start(bf16[128,384]{1,0:T(8,128)(2,1)S(1)} %get-tuple-element.22), channel_id=1, source_target_pairs={{0,16},{8,24},{16,0},{24,8},{1,17},{9,25},{17,1},{25,9},{2,18},{10... | collective-permute-start | bytes 294920 | tf_op jit(solution)/shard_map/ppermute | solution.py:337
  17.1 6.0 %collective-permute-start.8 = (bf16[128,128]{1,0:T(8,128)(2,1)S(1)}, bf16[128,128]{1,0:T(8,128)(2,1)S(1)}, u32[]{:S(2)}, u32[]{:S(2)}) collective-permute-start(bf16[128,128]{1,0:T(8,128)(2,1)S(1)} %get-tuple-element.24), channel_id=1, source_target_pairs={{0,16},{8,24},{16,0},{24,8},{1,17},{9,25},{17,1},{25,9},{2,18},{10... | collective-permute-start | bytes 98312 | tf_op jit(solution)/shard_map/ppermute | solution.py:337
  22.2 4.7 %collective-permute-start.6 = (bf16[128,384]{1,0:T(8,128)(2,1)S(1)}, bf16[128,384]{1,0:T(8,128)(2,1)S(1)}, u32[]{:S(2)}, u32[]{:S(2)}) collective-permute-start(bf16[128,384]{1,0:T(8,128)(2,1)S(1)} %add_convert_fusion.1.refs_0_), channel_id=1, source_target_pairs={{0,8},{8,0},{16,24},{24,16},{1,9},{9,1},{17,25},{25,17},{2,10},{10... | collective-permute-start | bytes 294920 | tf_op jit(solution)/shard_map/ppermute | solution.py:337
  23.1 4.1 %collective-permute-start.9 = (bf16[128,128]{1,0:T(8,128)(2,1)S(1)}, bf16[128,128]{1,0:T(8,128)(2,1)S(1)}, u32[]{:S(2)}, u32[]{:S(2)}) collective-permute-start(bf16[128,128]{1,0:T(8,128)(2,1)S(1)} %add_convert_fusion.2.refs_3_), channel_id=1, source_target_pairs={{0,8},{8,0},{16,24},{24,16},{1,9},{9,1},{17,25},{25,17},{2,10},{10... | collective-permute-start | bytes 98312 | tf_op jit(solution)/shard_map/ppermute | solution.py:337
  26.9 1.6 %collective-permute-start.7 = (bf16[256,384]{1,0:T(8,128)(2,1)S(1)}, bf16[256,384]{1,0:T(8,128)(2,1)S(1)}, u32[]{:S(2)}, u32[]{:S(2)}) collective-permute-start(bf16[256,384]{1,0:T(8,128)(2,1)S(1)} %pad_maximum_fusion), channel_id=1, source_target_pairs={{0,2},{2,0},{1,3},{3,1},{4,6},{6,4},{5,7},{7,5},{8,10},{10,8},{9,1... | collective-permute-start | bytes 589832 | tf_op jit(solution)/shard_map/ppermute | solution.py:337
  27.2 1.3 %collective-permute-start.10 = (bf16[256,128]{1,0:T(8,128)(2,1)S(1)}, bf16[256,128]{1,0:T(8,128)(2,1)S(1)}, u32[]{:S(2)}, u32[]{:S(2)}) collective-permute-start(bf16[256,128]{1,0:T(8,128)(2,1)S(1)} %pad_maximum_fusion.1), channel_id=1, source_target_pairs={{0,2},{2,0},{1,3},{3,1},{4,6},{6,4},{5,7},{7,5},{8,10},{10,8},{9,1... | collective-permute-start | bytes 196616 | tf_op jit(solution)/shard_map/ppermute | solution.py:337
  35.3 4.0 %collective-permute-start.12 = (bf16[32,512]{1,0:T(8,128)(2,1)S(1)}, bf16[32,512]{1,0:T(8,128)(2,1)S(1)}, u32[]{:S(2)}, u32[]{:S(2)}) collective-permute-start(bf16[32,512]{1,0:T(8,128)(2,1)S(1)} %get-tuple-element.25.refs_0_), channel_id=1, source_target_pairs={{0,1},{1,0},{4,5},{5,4},{2,3},{3,2},{6,7},{7,6},{8,9},{9,8},{12,13... | collective-permute-start | bytes 98312 | tf_op jit(solution)/shard_map/ppermute | solution.py:378
  36.8 4.9 %collective-permute-start.13 = (bf16[32,512]{1,0:T(8,128)(2,1)S(1)}, bf16[32,512]{1,0:T(8,128)(2,1)S(1)}, u32[]{:S(2)}, u32[]{:S(2)}) collective-permute-start(bf16[32,512]{1,0:T(8,128)(2,1)S(1)} %get-tuple-element.26), channel_id=1, source_target_pairs={{0,5},{1,4},{4,1},{5,0},{2,7},{3,6},{6,3},{7,2},{8,13},{9,12},{12,... | collective-permute-start | bytes 98312 | tf_op jit(solution)/shard_map/ppermute | solution.py:378
  38.2 3.9 %collective-permute-start.11 = (bf16[32,512]{1,0:T(8,128)(2,1)S(1)}, bf16[32,512]{1,0:T(8,128)(2,1)S(1)}, u32[]{:S(2)}, u32[]{:S(2)}) collective-permute-start(bf16[32,512]{1,0:T(8,128)(2,1)S(1)} %get-tuple-element.26), channel_id=1, source_target_pairs={{0,4},{1,5},{4,0},{5,1},{2,6},{3,7},{6,2},{7,3},{8,12},{9,13},{12,... | collective-permute-start | bytes 98312 | tf_op jit(solution)/shard_map/ppermute | solution.py:378

commit v17 on v13

--- a/solution.py
+++ b/solution.py
@@ -19,18 +19,21 @@
     return pltpu.CompilerParams(vmem_limit_bytes=limit << 20)
 
 
-def half_sum(patch, cot, block, side, scale):
+def half_sum(patch, cot, block, side, scale, part=None):
+    quarter = patch.shape[3] // 2
+    rows = slice(None) if part is None else slice(part * quarter, (part + 1) * quarter)
     terms = lax.dot_general(
-        patch[block, side], cot[block], ROWS_IN_COLS, preferred_element_type=F32
+        patch[block, side, :, rows], cot[block], ROWS_IN_COLS, preferred_element_type=F32
     )
     return terms * scale
 
 
-def load_kernel(scale, patch_hbm, cot_hbm, given, patch, cot, sems):
+def load_kernel(scale, patch_hbm, cot_hbm, given_near, given_far, patch, cot, sems):
     half = patch.shape[3]
     width = half // 2
     column, core, parity = lax.axis_index("x"), lax.axis_index("core"), lax.axis_index("z") % 2
     copies = []
+    quarter = given_near.shape[0]
 
     def fetch(source, target):
         copies.append(pltpu.make_async_copy(source, target, sems.at[len(copies)]))
@@ -53,7 +56,9 @@
     fetch_patch(0, 0)
     for copy in copies[:needed]:
         copy.wait()
-    given[...] = half_sum(patch, cot, 1, 1, scale).astype(BF16)
+    terms = half_sum(patch, cot, 1, 1, scale).astype(BF16)
+    given_near[...] = terms[:quarter]
+    given_far[...] = terms[quarter:]
     for copy in copies[needed:]:
         copy.wait()
 
@@ -64,12 +69,13 @@
     return pl.pallas_call(
         functools.partial(load_kernel, scale),
         out_shape=[
-            jax.ShapeDtypeStruct((half, width), BF16),
+            jax.ShapeDtypeStruct((half // 2, width), BF16),
+            jax.ShapeDtypeStruct((half // 2, width), BF16),
             jax.ShapeDtypeStruct((blocks, 2, pix, half), BF16),
             jax.ShapeDtypeStruct((blocks, pix, width), BF16),
         ],
         in_specs=[HBM] * 2,
-        out_specs=[VMEM] * 3,
+        out_specs=[VMEM] * 4,
         scratch_shapes=[pltpu.SemaphoreType.DMA((10,))],
         compiler_params=params(16),
     )(
@@ -79,15 +85,18 @@
 
 
 def sums_kernel(scale, wanted, patch, cot, *refs):
-    for (block, side, dtype), out in zip(wanted, refs[-len(wanted) :]):
-        out[...] = half_sum(patch, cot, block, side, scale).astype(dtype)
+    for (block, side, part, dtype), out in zip(wanted, refs[-len(wanted) :]):
+        out[...] = half_sum(patch, cot, block, side, scale, part).astype(dtype)
 
 
 def sums(scale, patch, cot, after, *wanted):
     pix, half = patch.shape[2:]
     return pl.pallas_call(
         functools.partial(sums_kernel, scale, wanted),
-        out_shape=[jax.ShapeDtypeStruct((half, 2 * half), dtype) for _, _, dtype in wanted],
+        out_shape=[
+            jax.ShapeDtypeStruct((half if part is None else half // 2, 2 * half), dtype)
+            for _, _, part, dtype in wanted
+        ],
         in_specs=[VMEM] * 2 + [pl.BlockSpec(memory_space=pl.ANY)] * len(after),
         out_specs=[VMEM] * len(wanted),
         compiler_params=params(16),
@@ -298,22 +307,23 @@
     )(pltpu.with_memory_space_constraint(counts, pltpu.HBM), *pieces)
 
 
-def place_kernel(*refs):
+def place_kernel(origins, *refs):
     *pieces, out, sems = refs
     column, group = lax.axis_index("x"), lax.axis_index("group")
     copies = []
-    for index, piece in enumerate(pieces):
-        number = 2 * (group ^ (index // 2)) + (column ^ (index % 2))
+    for index, (piece, (turn, flip)) in enumerate(zip(pieces, origins)):
+        number = 2 * (group ^ turn) + (column ^ flip)
         copies.append(pltpu.make_async_copy(piece, out.at[number], sems.at[index]))
         copies[-1].start()
     for copy in copies:
         copy.wait()
 
 
-def place(pieces):
+def place(found):
+    origins, pieces = zip(*found.items())
     rows, width = pieces[0].shape
     return pl.pallas_call(
-        place_kernel,
+        functools.partial(place_kernel, origins),
         out_shape=jax.ShapeDtypeStruct((len(pieces), rows, width), BF16),
         in_specs=[VMEM] * len(pieces),
         out_specs=HBM,
@@ -335,15 +345,17 @@
         moves = [(2 * z + x, 2 * (z ^ 1) + (x ^ 1)) for z in range(line) for x in range(2)]
         return lax.ppermute(array, ("z", "x"), moves)
 
-    given, patch, cot = load(scale, patches, cotangents)
-    came = swap(given, "core")
-    kept, given_on = sums(scale, patch, cot, (), (1, 0, F32), (0, 1, BF16))
+    given_near, given_far, patch, cot = load(scale, patches, cotangents)
+    came_near, came_far = swap(given_near, "core"), swap(given_far, "core")
+    kept_near, kept_far, given_on = sums(
+        scale, patch, cot, (), (1, 0, 0, F32), (1, 0, 1, F32), (0, 1, None, BF16)
+    )
     came_on = swap(given_on, "core")
-    leaving = add(kept, came).astype(BF16)
-    to_diagonal, to_column = leaving[quarter:], leaving[:quarter]
+    to_column = add(kept_near, came_near).astype(BF16)
+    to_diagonal = add(kept_far, came_far).astype(BF16)
     from_diagonal = swap_diagonal(to_diagonal)
     from_column = swap(to_column, "x")
-    (kept_on,) = sums(scale, patch, cot, (to_diagonal,), (0, 0, F32))
+    (kept_on,) = sums(scale, patch, cot, (to_diagonal,), (0, 0, None, F32))
     own = add(kept_on, came_on)
     from_line = swap(own[quarter:].astype(BF16), "z")
     left, right, send_left, send_right = collect(
@@ -361,17 +373,18 @@
         pieces += [own, other, swap(jnp.concatenate([own, other], 0), "core")]
     keep, send = root(newton_counts, pieces, rows)
 
-    pieces = []
-    for turn in range(groups):
-        for flip in range(2):
-            moves = [
-                (c * groups + g, (c ^ flip) * groups + (g ^ turn))
-                for c in range(2)
-                for g in range(groups)
-            ]
-            piece = send if flip else keep
-            pieces.append(lax.ppermute(piece, ("x", "group"), moves) if turn or flip else piece)
-    return place(pieces)
+    def pass_on(turn, flip):
+        moves = [
+            (c * groups + g, (c ^ flip) * groups + (g ^ turn))
+            for c in range(2)
+            for g in range(groups)
+        ]
+        return lax.ppermute(send if flip else keep, ("x", "group"), moves)
+
+    others = [(turn, flip) for turn in range(groups) for flip in range(2) if turn or flip]
+    found = {(turn, flip): pass_on(turn, flip) for turn, flip in others}
+    found[0, 0] = keep
+    return place(found)
 
 
 def solution(mesh):

time: 42.3 us -> 43.1 us (1.019)
  starting transfers between devices: 14.3 us -> 14.8 us
    ppermute x1, starting transfers between devices: 1.55 us -> 3.86 us  [swap_diagonal(): return lax.ppermute(array, ('z', 'x'), moves)]
    ppermute x10 -> x11, starting transfers between devices: 9.2 us -> 7.41 us  [swap(): lax.ppermute(array, axis, [(i, i ^ mask) for i in range(lax.axis_size(axi...]
    ppermute x1, waiting for transfers between devices: 1.4 us -> 2.72 us  [swap_diagonal(): return lax.ppermute(array, ('z', 'x'), moves)]
    ppermute x10 -> x11, waiting for transfers between devices: 13.5 us -> 12.4 us  [swap(): lax.ppermute(array, axis, [(i, i ^ mask) for i in range(lax.axis_size(axi...]
  transfers between devices with their start and end apart: 14 -> 15, of which waited for: 11 -> 10; matrix products, arithmetic and copies ran while one was open for 1% -> 0% of each run, Pallas kernels for 2% -> 2%
where the time goes in v17:
time: 43.1 us; the launch traced here: 42.9 us
  waiting for transfers between devices  18.5 us (43%)
  starting transfers between devices  14.8 us (34%)
  Pallas kernels  9.28 us (22%)
    ppermute x11, waiting for transfers between devices, swap(): lax.ppermute(array, axis, [(i, i ^ mask) for i in range(lax.axis_size(axi...  12.4 us
    ppermute x11, starting transfers between devices, swap(): lax.ppermute(array, axis, [(i, i ^ mask) for i in range(lax.axis_size(axi...  7.41 us
    pallas_call x1, Pallas kernels, root(): pl.pallas_call(functools.partial(root_kernel, most), out_shape=[out, out]...  6.15 us
    ppermute x1, starting transfers between devices, swap_diagonal(): return lax.ppermute(array, ('z', 'x'), moves)  3.86 us
    ppermute x3, starting transfers between devices, pass_on(): return lax.ppermute(send if flip else keep, ('x', 'group'), moves)  3.55 us
    ppermute x3, waiting for transfers between devices, pass_on(): return lax.ppermute(send if flip else keep, ('x', 'group'), moves)  3.45 us
    ppermute x1, waiting for transfers between devices, swap_diagonal(): return lax.ppermute(array, ('z', 'x'), moves)  2.72 us
    pallas_call x1, Pallas kernels, load(): pl.pallas_call(functools.partial(load_kernel, scale), out_shape=[jax.Shap...  1.61 us
  transfers between devices with their start and end apart: 15, of which 10 were waited for; matrix products, arithmetic and copies ran while one was open for 0% of the time, Pallas kernels for 2%

profile of v17, /device:TPU:0, one launch (start us, length us, event | category | flops | bytes accessed | tf_op | source)
XLA Modules:
  0.0 42.9 jit_solution(1577350100245022549)
XLA Ops:
  0.0 1.6 %shard_map.37 = (bf16[128,512]{1,0:T(8,128)(2,1)S(1)}, bf16[128,512]{1,0:T(8,128)(2,1)S(1)}, bf16[2,2,512,256]{3,2,1,0:T(8,128)(2,1)S(1)}, bf16[2,512,512]{2,1,0:T(8,128)(2,1)S(1)}) custom-call(bf16[2,512,512]{2,1,0:T(8,128)(2,1)} %patch_hbm.1, bf16[2,512,512]{2,1,0:T(8,128)(2,1)} %cot_hbm.1), custom_call_target="tpu_custom_call" | custom-call | tf_op jit(solution)/shard_map/pallas_call | solution.py:69
  1.6 0.5 %collective-permute-start = (bf16[128,512]{1,0:T(8,128)(2,1)S(1)}, bf16[128,512]{1,0:T(8,128)(2,1)S(1)}, u32[]{:S(2)}, u32[]{:S(2)}) collective-permute-start(bf16[128,512]{1,0:T(8,128)(2,1)S(1)} %get-tuple-element.21), channel_id=1, source_target_pairs={{0,2},{2,0},{1,3},{3,1},{4,6},{6,4},{5,7},{7,5},{8,10},{10,8},{9,1... | collective-permute-start | bytes 393224 | tf_op jit(solution)/shard_map/ppermute | solution.py:342
  2.1 0.1 collective-permute-start.3
  2.2 0.5 %shard_map.38 = (f32[128,512]{1,0:T(8,128)S(1)}, f32[128,512]{1,0:T(8,128)S(1)}, bf16[256,512]{1,0:T(8,128)(2,1)S(1)}) custom-call(bf16[2,2,512,256]{3,2,1,0:T(8,128)(2,1)S(1)} %get-tuple-element.18.patch, bf16[2,512,512]{2,1,0:T(8,128)(2,1)S(1)} %get-tuple-element.19.cot), custom_call_target="tpu_custom_call" | custom-call | flops 402653184 | bytes 1048576 | tf_op jit(solution)/shard_map/pallas_call | solution.py:94
  2.7 0.5 %collective-permute-start.1 = (bf16[256,512]{1,0:T(8,128)(2,1)S(1)}, bf16[256,512]{1,0:T(8,128)(2,1)S(1)}, u32[]{:S(2)}, u32[]{:S(2)}) collective-permute-start(bf16[256,512]{1,0:T(8,128)(2,1)S(1)} %get-tuple-element.22), channel_id=1, source_target_pairs={{0,2},{2,0},{1,3},{3,1},{4,6},{6,4},{5,7},{7,5},{8,10},{10,8},{9,1... | collective-permute-start | bytes 786440 | tf_op jit(solution)/shard_map/ppermute | solution.py:342
  3.2 0.0 collective-permute-done
  3.2 3.9 %collective-permute-start.2 = (bf16[128,512]{1,0:T(8,128)(2,1)S(1)}, bf16[128,512]{1,0:T(8,128)(2,1)S(1)}, u32[]{:S(2)}, u32[]{:S(2)}) collective-permute-start(bf16[128,512]{1,0:T(8,128)(2,1)S(1)} %add_convert_fusion.1.refs_0_), channel_id=1, source_target_pairs={{0,12},{4,8},{8,4},{12,0},{16,28},{20,24},{24,20},{28,16},{1,13},{... | collective-permute-start | bytes 393224 | tf_op jit(solution)/shard_map/ppermute | solution.py:346
  7.1 0.0 collective-permute-done.3
  7.1 0.6 %collective-permute-start.4 = (bf16[128,512]{1,0:T(8,128)(2,1)S(1)}, bf16[128,512]{1,0:T(8,128)(2,1)S(1)}, u32[]{:S(2)}, u32[]{:S(2)}) collective-permute-start(bf16[128,512]{1,0:T(8,128)(2,1)S(1)} %add_convert_fusion), channel_id=1, source_target_pairs={{0,4},{4,0},{1,5},{5,1},{2,6},{6,2},{3,7},{7,3},{8,12},{12,8},{9,1... | collective-permute-start | bytes 393224 | tf_op jit(solution)/shard_map/ppermute | solution.py:342
  7.7 0.3 shard_map.39
  8.0 0.0 collective-permute-done.1
  8.0 0.1 convert_add_fusion.own
  8.2 0.2 collective-permute-start.5
  8.3 2.7 %collective-permute-done.2.refs_0_ = bf16[128,512]{1,0:T(8,128)(2,1)S(1)} collective-permute-done((bf16[128,512]{1,0:T(8,128)(2,1)S(1)}, bf16[128,512]{1,0:T(8,128)(2,1)S(1)}, u32[]{:S(2)}, u32[]{:S(2)}) %collective-permute-start.2) | collective-permute-done | bytes 131104 | tf_op jit(solution)/shard_map/ppermute | solution.py:346
  11.1 2.7 %collective-permute-done.4.refs_1_ = bf16[128,512]{1,0:T(8,128)(2,1)S(1)} collective-permute-done((bf16[128,512]{1,0:T(8,128)(2,1)S(1)}, bf16[128,512]{1,0:T(8,128)(2,1)S(1)}, u32[]{:S(2)}, u32[]{:S(2)}) %collective-permute-start.4) | collective-permute-done | bytes 131104 | tf_op jit(solution)/shard_map/ppermute | solution.py:342
  13.8 0.2 collective-permute-done.5.refs_2_
  14.0 0.1 shard_map.40
  14.0 2.7 %collective-permute-start.6 = (bf16[128,384]{1,0:T(8,128)(2,1)S(1)}, bf16[128,384]{1,0:T(8,128)(2,1)S(1)}, u32[]{:S(2)}, u32[]{:S(2)}) collective-permute-start(bf16[128,384]{1,0:T(8,128)(2,1)S(1)} %get-tuple-element.26), channel_id=1, source_target_pairs={{0,16},{8,24},{16,0},{24,8},{1,17},{9,25},{17,1},{25,9},{2,18},{10... | collective-permute-start | bytes 294920 | tf_op jit(solution)/shard_map/ppermute | solution.py:342
  16.7 0.3 collective-permute-start.9
  17.0 5.8 %collective-permute-done.6 = bf16[128,384]{1,0:T(8,128)(2,1)S(1)} collective-permute-done((bf16[128,384]{1,0:T(8,128)(2,1)S(1)}, bf16[128,384]{1,0:T(8,128)(2,1)S(1)}, u32[]{:S(2)}, u32[]{:S(2)}) %collective-permute-start.6) | collective-permute-done | bytes 98336 | tf_op jit(solution)/shard_map/ppermute | solution.py:342
  22.8 0.5 %collective-permute-start.7 = (bf16[128,384]{1,0:T(8,128)(2,1)S(1)}, bf16[128,384]{1,0:T(8,128)(2,1)S(1)}, u32[]{:S(2)}, u32[]{:S(2)}) collective-permute-start(bf16[128,384]{1,0:T(8,128)(2,1)S(1)} %add_convert_fusion.2.refs_0_), channel_id=1, source_target_pairs={{0,8},{8,0},{16,24},{24,16},{1,9},{9,1},{17,25},{25,17},{2,10},{10... | collective-permute-start | bytes 294920 | tf_op jit(solution)/shard_map/ppermute | solution.py:342
  23.3 0.0 collective-permute-done.9
  23.3 1.6 %collective-permute-start.10 = (bf16[128,128]{1,0:T(8,128)(2,1)S(1)}, bf16[128,128]{1,0:T(8,128)(2,1)S(1)}, u32[]{:S(2)}, u32[]{:S(2)}) collective-permute-start(bf16[128,128]{1,0:T(8,128)(2,1)S(1)} %add_convert_fusion.3.refs_3_), channel_id=1, source_target_pairs={{0,8},{8,0},{16,24},{24,16},{1,9},{9,1},{17,25},{25,17},{2,10},{10... | collective-permute-start | bytes 98312 | tf_op jit(solution)/shard_map/ppermute | solution.py:342
  25.0 2.5 %collective-permute-done.7.refs_1_ = bf16[128,384]{1,0:T(8,128)(2,1)S(1)} collective-permute-done((bf16[128,384]{1,0:T(8,128)(2,1)S(1)}, bf16[128,384]{1,0:T(8,128)(2,1)S(1)}, u32[]{:S(2)}, u32[]{:S(2)}) %collective-permute-start.7) | collective-permute-done | bytes 98336 | tf_op jit(solution)/shard_map/ppermute | solution.py:342
  27.5 0.1 collective-permute-start.8
  27.6 0.2 collective-permute-done.10.refs_4_
  27.8 0.3 collective-permute-start.11
  28.2 0.9 %collective-permute-done.11.refs_5_ = bf16[256,128]{1,0:T(8,128)(2,1)S(1)} collective-permute-done((bf16[256,128]{1,0:T(8,128)(2,1)S(1)}, bf16[256,128]{1,0:T(8,128)(2,1)S(1)}, u32[]{:S(2)}, u32[]{:S(2)}) %collective-permute-start.11) | collective-permute-done | bytes 65568 | tf_op jit(solution)/shard_map/ppermute | solution.py:342
  29.1 0.0 collective-permute-done.8.refs_2_
  29.1 6.1 %shard_map.41 = (bf16[32,512]{1,0:T(8,128)(2,1)S(1)}, bf16[32,512]{1,0:T(8,128)(2,1)S(1)}) custom-call(s32[2,2]{1,0:T(2,128)} %counts_hbm.1, bf16[128,384]{1,0:T(8,128)(2,1)S(1)} %add_convert_fusion.2.refs_0_, bf16[128,384]{1,0:T(8,128)(2,1)S(1)} %collective-permute-done.7.refs_1_, bf16[256,384]{1,0:T(8,128)(2,1)S(1)} %collective-permute-done.8.refs_2_, ...), custom_call_target="tpu_custom_call" | custom-call | tf_op jit(solution)/shard_map/pallas_call | solution.py:289
  35.3 2.5 %collective-permute-start.14 = (bf16[32,512]{1,0:T(8,128)(2,1)S(1)}, bf16[32,512]{1,0:T(8,128)(2,1)S(1)}, u32[]{:S(2)}, u32[]{:S(2)}) collective-permute-start(bf16[32,512]{1,0:T(8,128)(2,1)S(1)} %get-tuple-element.29), channel_id=1, source_target_pairs={{0,5},{1,4},{4,1},{5,0},{2,7},{3,6},{6,3},{7,2},{8,13},{9,12},{12,... | collective-permute-start | bytes 98312 | tf_op jit(solution)/shard_map/ppermute | solution.py:382
  37.7 0.6 %collective-permute-start.12 = (bf16[32,512]{1,0:T(8,128)(2,1)S(1)}, bf16[32,512]{1,0:T(8,128)(2,1)S(1)}, u32[]{:S(2)}, u32[]{:S(2)}) collective-permute-start(bf16[32,512]{1,0:T(8,128)(2,1)S(1)} %get-tuple-element.29), channel_id=1, source_target_pairs={{0,4},{1,5},{4,0},{5,1},{2,6},{3,7},{6,2},{7,3},{8,12},{9,13},{12,... | collective-permute-start | bytes 98312 | tf_op jit(solution)/shard_map/ppermute | solution.py:382
  38.4 0.5 %collective-permute-start.13 = (bf16[32,512]{1,0:T(8,128)(2,1)S(1)}, bf16[32,512]{1,0:T(8,128)(2,1)S(1)}, u32[]{:S(2)}, u32[]{:S(2)}) collective-permute-start(bf16[32,512]{1,0:T(8,128)(2,1)S(1)} %get-tuple-element.30.refs_3_), channel_id=1, source_target_pairs={{0,1},{1,0},{4,5},{5,4},{2,3},{3,2},{6,7},{7,6},{8,9},{9,8},{12,13... | collective-permute-start | bytes 98312 | tf_op jit(solution)/shard_map/ppermute | solution.py:382
  38.8 1.3 %collective-permute-done.14.refs_2_ = bf16[32,512]{1,0:T(8,128)(2,1)S(1)} collective-permute-done((bf16[32,512]{1,0:T(8,128)(2,1)S(1)}, bf16[32,512]{1,0:T(8,128)(2,1)S(1)}, u32[]{:S(2)}, u32[]{:S(2)}) %collective-permute-start.14) | collective-permute-done | bytes 32800 | tf_op jit(solution)/shard_map/ppermute | solution.py:382
  40.1 1.5 %collective-permute-done.12.refs_0_ = bf16[32,512]{1,0:T(8,128)(2,1)S(1)} collective-permute-done((bf16[32,512]{1,0:T(8,128)(2,1)S(1)}, bf16[32,512]{1,0:T(8,128)(2,1)S(1)}, u32[]{:S(2)}, u32[]{:S(2)}) %collective-permute-start.12) | collective-permute-done | bytes 32800 | tf_op jit(solution)/shard_map/ppermute | solution.py:382
  41.7 0.6 %collective-permute-done.13.refs_1_ = bf16[32,512]{1,0:T(8,128)(2,1)S(1)} collective-permute-done((bf16[32,512]{1,0:T(8,128)(2,1)S(1)}, bf16[32,512]{1,0:T(8,128)(2,1)S(1)}, u32[]{:S(2)}, u32[]{:S(2)}) %collective-permute-start.13) | collective-permute-done | bytes 32800 | tf_op jit(solution)/shard_map/ppermute | solution.py:382
  42.3 0.7 %shard_map.42 = bf16[4,32,512]{2,1,0:T(8,128)(2,1)} custom-call(bf16[32,512]{1,0:T(8,128)(2,1)S(1)} %collective-permute-done.12.refs_0_, bf16[32,512]{1,0:T(8,128)(2,1)S(1)} %collective-permute-done.13.refs_1_, bf16[32,512]{1,0:T(8,128)(2,1)S(1)} %collective-permute-done.14.refs_2_, bf16[32,512]{1,0:T(8,128)(2,1)S(1)} %get-tuple-element.30.refs_3_), custom_call_target="tpu_custom_call" | custom-call | tf_op jit(solution)/shard_map/pallas_call | solution.py:325
  (7 shorter events, 0.1 us)
Async XLA Ops:
  1.6 1.6 %collective-permute-start = (bf16[128,512]{1,0:T(8,128)(2,1)S(1)}, bf16[128,512]{1,0:T(8,128)(2,1)S(1)}, u32[]{:S(2)}, u32[]{:S(2)}) collective-permute-start(bf16[128,512]{1,0:T(8,128)(2,1)S(1)} %get-tuple-element.21), channel_id=1, source_target_pairs={{0,2},{2,0},{1,3},{3,1},{4,6},{6,4},{5,7},{7,5},{8,10},{10,8},{9,1... | collective-permute-start | bytes 393224 | tf_op jit(solution)/shard_map/ppermute | solution.py:342
  2.1 4.9 %collective-permute-start.3 = (bf16[128,512]{1,0:T(8,128)(2,1)S(1)}, bf16[128,512]{1,0:T(8,128)(2,1)S(1)}, u32[]{:S(2)}, u32[]{:S(2)}) collective-permute-start(bf16[128,512]{1,0:T(8,128)(2,1)S(1)} %get-tuple-element.24), channel_id=1, source_target_pairs={{0,2},{2,0},{1,3},{3,1},{4,6},{6,4},{5,7},{7,5},{8,10},{10,8},{9,1... | collective-permute-start | bytes 393224 | tf_op jit(solution)/shard_map/ppermute | solution.py:342
  2.7 5.4 %collective-permute-start.1 = (bf16[256,512]{1,0:T(8,128)(2,1)S(1)}, bf16[256,512]{1,0:T(8,128)(2,1)S(1)}, u32[]{:S(2)}, u32[]{:S(2)}) collective-permute-start(bf16[256,512]{1,0:T(8,128)(2,1)S(1)} %get-tuple-element.22), channel_id=1, source_target_pairs={{0,2},{2,0},{1,3},{3,1},{4,6},{6,4},{5,7},{7,5},{8,10},{10,8},{9,1... | collective-permute-start | bytes 786440 | tf_op jit(solution)/shard_map/ppermute | solution.py:342
  3.2 7.8 %collective-permute-start.2 = (bf16[128,512]{1,0:T(8,128)(2,1)S(1)}, bf16[128,512]{1,0:T(8,128)(2,1)S(1)}, u32[]{:S(2)}, u32[]{:S(2)}) collective-permute-start(bf16[128,512]{1,0:T(8,128)(2,1)S(1)} %add_convert_fusion.1.refs_0_), channel_id=1, source_target_pairs={{0,12},{4,8},{8,4},{12,0},{16,28},{20,24},{24,20},{28,16},{1,13},{... | collective-permute-start | bytes 393224 | tf_op jit(solution)/shard_map/ppermute | solution.py:346
  7.1 6.6 %collective-permute-start.4 = (bf16[128,512]{1,0:T(8,128)(2,1)S(1)}, bf16[128,512]{1,0:T(8,128)(2,1)S(1)}, u32[]{:S(2)}, u32[]{:S(2)}) collective-permute-start(bf16[128,512]{1,0:T(8,128)(2,1)S(1)} %add_convert_fusion), channel_id=1, source_target_pairs={{0,4},{4,0},{1,5},{5,1},{2,6},{6,2},{3,7},{7,3},{8,12},{12,8},{9,1... | collective-permute-start | bytes 393224 | tf_op jit(solution)/shard_map/ppermute | solution.py:342
  8.2 5.8 %collective-permute-start.5 = (bf16[128,512]{1,0:T(8,128)(2,1)S(1)}, bf16[128,512]{1,0:T(8,128)(2,1)S(1)}, u32[]{:S(2)}, u32[]{:S(2)}) collective-permute-start(bf16[128,512]{1,0:T(8,128)(2,1)S(1)} %slice.7), channel_id=1, source_target_pairs={{0,8},{8,0},{16,24},{24,16},{1,9},{9,1},{17,25},{25,17},{2,10},{10... | collective-permute-start | bytes 393224 | tf_op jit(solution)/shard_map/ppermute | solution.py:342
  14.0 8.7 %collective-permute-start.6 = (bf16[128,384]{1,0:T(8,128)(2,1)S(1)}, bf16[128,384]{1,0:T(8,128)(2,1)S(1)}, u32[]{:S(2)}, u32[]{:S(2)}) collective-permute-start(bf16[128,384]{1,0:T(8,128)(2,1)S(1)} %get-tuple-element.26), channel_id=1, source_target_pairs={{0,16},{8,24},{16,0},{24,8},{1,17},{9,25},{17,1},{25,9},{2,18},{10... | collective-permute-start | bytes 294920 | tf_op jit(solution)/shard_map/ppermute | solution.py:342
  16.7 6.6 %collective-permute-start.9 = (bf16[128,128]{1,0:T(8,128)(2,1)S(1)}, bf16[128,128]{1,0:T(8,128)(2,1)S(1)}, u32[]{:S(2)}, u32[]{:S(2)}) collective-permute-start(bf16[128,128]{1,0:T(8,128)(2,1)S(1)} %get-tuple-element.28), channel_id=1, source_target_pairs={{0,16},{8,24},{16,0},{24,8},{1,17},{9,25},{17,1},{25,9},{2,18},{10... | collective-permute-start | bytes 98312 | tf_op jit(solution)/shard_map/ppermute | solution.py:342
  22.8 4.7 %collective-permute-start.7 = (bf16[128,384]{1,0:T(8,128)(2,1)S(1)}, bf16[128,384]{1,0:T(8,128)(2,1)S(1)}, u32[]{:S(2)}, u32[]{:S(2)}) collective-permute-start(bf16[128,384]{1,0:T(8,128)(2,1)S(1)} %add_convert_fusion.2.refs_0_), channel_id=1, source_target_pairs={{0,8},{8,0},{16,24},{24,16},{1,9},{9,1},{17,25},{25,17},{2,10},{10... | collective-permute-start | bytes 294920 | tf_op jit(solution)/shard_map/ppermute | solution.py:342
  23.3 4.5 %collective-permute-start.10 = (bf16[128,128]{1,0:T(8,128)(2,1)S(1)}, bf16[128,128]{1,0:T(8,128)(2,1)S(1)}, u32[]{:S(2)}, u32[]{:S(2)}) collective-permute-start(bf16[128,128]{1,0:T(8,128)(2,1)S(1)} %add_convert_fusion.3.refs_3_), channel_id=1, source_target_pairs={{0,8},{8,0},{16,24},{24,16},{1,9},{9,1},{17,25},{25,17},{2,10},{10... | collective-permute-start | bytes 98312 | tf_op jit(solution)/shard_map/ppermute | solution.py:342
  27.5 1.6 %collective-permute-start.8 = (bf16[256,384]{1,0:T(8,128)(2,1)S(1)}, bf16[256,384]{1,0:T(8,128)(2,1)S(1)}, u32[]{:S(2)}, u32[]{:S(2)}) collective-permute-start(bf16[256,384]{1,0:T(8,128)(2,1)S(1)} %pad_maximum_fusion), channel_id=1, source_target_pairs={{0,2},{2,0},{1,3},{3,1},{4,6},{6,4},{5,7},{7,5},{8,10},{10,8},{9,1... | collective-permute-start | bytes 589832 | tf_op jit(solution)/shard_map/ppermute | solution.py:342
  27.8 1.3 %collective-permute-start.11 = (bf16[256,128]{1,0:T(8,128)(2,1)S(1)}, bf16[256,128]{1,0:T(8,128)(2,1)S(1)}, u32[]{:S(2)}, u32[]{:S(2)}) collective-permute-start(bf16[256,128]{1,0:T(8,128)(2,1)S(1)} %pad_maximum_fusion.1), channel_id=1, source_target_pairs={{0,2},{2,0},{1,3},{3,1},{4,6},{6,4},{5,7},{7,5},{8,10},{10,8},{9,1... | collective-permute-start | bytes 196616 | tf_op jit(solution)/shard_map/ppermute | solution.py:342
  35.3 4.9 %collective-permute-start.14 = (bf16[32,512]{1,0:T(8,128)(2,1)S(1)}, bf16[32,512]{1,0:T(8,128)(2,1)S(1)}, u32[]{:S(2)}, u32[]{:S(2)}) collective-permute-start(bf16[32,512]{1,0:T(8,128)(2,1)S(1)} %get-tuple-element.29), channel_id=1, source_target_pairs={{0,5},{1,4},{4,1},{5,0},{2,7},{3,6},{6,3},{7,2},{8,13},{9,12},{12,... | collective-permute-start | bytes 98312 | tf_op jit(solution)/shard_map/ppermute | solution.py:382
  37.7 3.9 %collective-permute-start.12 = (bf16[32,512]{1,0:T(8,128)(2,1)S(1)}, bf16[32,512]{1,0:T(8,128)(2,1)S(1)}, u32[]{:S(2)}, u32[]{:S(2)}) collective-permute-start(bf16[32,512]{1,0:T(8,128)(2,1)S(1)} %get-tuple-element.29), channel_id=1, source_target_pairs={{0,4},{1,5},{4,0},{5,1},{2,6},{3,7},{6,2},{7,3},{8,12},{9,13},{12,... | collective-permute-start | bytes 98312 | tf_op jit(solution)/shard_map/ppermute | solution.py:382
  38.4 3.9 %collective-permute-start.13 = (bf16[32,512]{1,0:T(8,128)(2,1)S(1)}, bf16[32,512]{1,0:T(8,128)(2,1)S(1)}, u32[]{:S(2)}, u32[]{:S(2)}) collective-permute-start(bf16[32,512]{1,0:T(8,128)(2,1)S(1)} %get-tuple-element.30.refs_3_), channel_id=1, source_target_pairs={{0,1},{1,0},{4,5},{5,4},{2,3},{3,2},{6,7},{7,6},{8,9},{9,8},{12,13... | collective-permute-start | bytes 98312 | tf_op jit(solution)/shard_map/ppermute | solution.py:382

commit v18 on v17

--- a/solution.py
+++ b/solution.py
@@ -355,7 +355,7 @@
     to_diagonal = add(kept_far, came_far).astype(BF16)
     from_diagonal = swap_diagonal(to_diagonal)
     from_column = swap(to_column, "x")
-    (kept_on,) = sums(scale, patch, cot, (to_diagonal,), (0, 0, None, F32))
+    (kept_on,) = sums(scale, patch, cot, (to_column,), (0, 0, None, F32))
     own = add(kept_on, came_on)
     from_line = swap(own[quarter:].astype(BF16), "z")
     left, right, send_left, send_right = collect(
@@ -381,7 +381,7 @@
         ]
         return lax.ppermute(send if flip else keep, ("x", "group"), moves)
 
-    others = [(turn, flip) for turn in range(groups) for flip in range(2) if turn or flip]
+    others = [(turn, flip) for flip in (0, 1) for turn in range(groups) if turn or flip]
     found = {(turn, flip): pass_on(turn, flip) for turn, flip in others}
     found[0, 0] = keep
     return place(found)

time: 43.1 us -> 42.3 us (0.981)
  waiting for transfers between devices: 18.5 us -> 17.8 us
    ppermute x1, starting transfers between devices: 3.86 us -> 1.61 us  [swap_diagonal(): return lax.ppermute(array, ('z', 'x'), moves)]
    ppermute x11, starting transfers between devices: 7.41 us -> 9.59 us  [swap(): lax.ppermute(array, axis, [(i, i ^ mask) for i in range(lax.axis_size(axi...]
    ppermute x1, waiting for transfers between devices: 2.72 us -> 1.39 us  [swap_diagonal(): return lax.ppermute(array, ('z', 'x'), moves)]
    ppermute x11, waiting for transfers between devices: 12.4 us -> 13.3 us  [swap(): lax.ppermute(array, axis, [(i, i ^ mask) for i in range(lax.axis_size(axi...]
where the time goes in v18:
time: 42.3 us; the launch traced here: 42.1 us
  waiting for transfers between devices  17.8 us (42%)
  starting transfers between devices  14.8 us (35%)
  Pallas kernels  9.29 us (22%)
    ppermute x11, waiting for transfers between devices, swap(): lax.ppermute(array, axis, [(i, i ^ mask) for i in range(lax.axis_size(axi...  13.3 us
    ppermute x11, starting transfers between devices, swap(): lax.ppermute(array, axis, [(i, i ^ mask) for i in range(lax.axis_size(axi...  9.59 us
    pallas_call x1, Pallas kernels, root(): pl.pallas_call(functools.partial(root_kernel, most), out_shape=[out, out]...  6.15 us
    ppermute x3, starting transfers between devices, pass_on(): return lax.ppermute(send if flip else keep, ('x', 'group'), moves)  3.55 us
    ppermute x3, waiting for transfers between devices, pass_on(): return lax.ppermute(send if flip else keep, ('x', 'group'), moves)  3.09 us
    ppermute x1, starting transfers between devices, swap_diagonal(): return lax.ppermute(array, ('z', 'x'), moves)  1.61 us
    pallas_call x1, Pallas kernels, load(): pl.pallas_call(functools.partial(load_kernel, scale), out_shape=[jax.Shap...  1.61 us
    ppermute x1, waiting for transfers between devices, swap_diagonal(): return lax.ppermute(array, ('z', 'x'), moves)  1.39 us
  transfers between devices with their start and end apart: 15, of which 10 were waited for; matrix products, arithmetic and copies ran while one was open for 0% of the time, Pallas kernels for 2%

profile of v18, /device:TPU:0, one launch (start us, length us, event | category | flops | bytes accessed | tf_op | source)
XLA Modules:
  0.0 42.1 jit_solution(1307939210094426468)
XLA Ops:
  0.0 1.6 %shard_map.37 = (bf16[128,512]{1,0:T(8,128)(2,1)S(1)}, bf16[128,512]{1,0:T(8,128)(2,1)S(1)}, bf16[2,2,512,256]{3,2,1,0:T(8,128)(2,1)S(1)}, bf16[2,512,512]{2,1,0:T(8,128)(2,1)S(1)}) custom-call(bf16[2,512,512]{2,1,0:T(8,128)(2,1)} %patch_hbm.1, bf16[2,512,512]{2,1,0:T(8,128)(2,1)} %cot_hbm.1), custom_call_target="tpu_custom_call" | custom-call | tf_op jit(solution)/shard_map/pallas_call | solution.py:69
  1.6 0.5 %collective-permute-start = (bf16[128,512]{1,0:T(8,128)(2,1)S(1)}, bf16[128,512]{1,0:T(8,128)(2,1)S(1)}, u32[]{:S(2)}, u32[]{:S(2)}) collective-permute-start(bf16[128,512]{1,0:T(8,128)(2,1)S(1)} %get-tuple-element.21), channel_id=1, source_target_pairs={{0,2},{2,0},{1,3},{3,1},{4,6},{6,4},{5,7},{7,5},{8,10},{10,8},{9,1... | collective-permute-start | bytes 393224 | tf_op jit(solution)/shard_map/ppermute | solution.py:342
  2.1 0.1 collective-permute-start.2
  2.2 0.5 %shard_map.38 = (f32[128,512]{1,0:T(8,128)S(1)}, f32[128,512]{1,0:T(8,128)S(1)}, bf16[256,512]{1,0:T(8,128)(2,1)S(1)}) custom-call(bf16[2,2,512,256]{3,2,1,0:T(8,128)(2,1)S(1)} %get-tuple-element.18.patch, bf16[2,512,512]{2,1,0:T(8,128)(2,1)S(1)} %get-tuple-element.19.cot), custom_call_target="tpu_custom_call" | custom-call | flops 402653184 | bytes 1048576 | tf_op jit(solution)/shard_map/pallas_call | solution.py:94
  2.7 0.5 %collective-permute-start.1 = (bf16[256,512]{1,0:T(8,128)(2,1)S(1)}, bf16[256,512]{1,0:T(8,128)(2,1)S(1)}, u32[]{:S(2)}, u32[]{:S(2)}) collective-permute-start(bf16[256,512]{1,0:T(8,128)(2,1)S(1)} %get-tuple-element.22), channel_id=1, source_target_pairs={{0,2},{2,0},{1,3},{3,1},{4,6},{6,4},{5,7},{7,5},{8,10},{10,8},{9,1... | collective-permute-start | bytes 786440 | tf_op jit(solution)/shard_map/ppermute | solution.py:342
  3.2 0.0 collective-permute-done
  3.2 2.9 %collective-permute-start.4 = (bf16[128,512]{1,0:T(8,128)(2,1)S(1)}, bf16[128,512]{1,0:T(8,128)(2,1)S(1)}, u32[]{:S(2)}, u32[]{:S(2)}) collective-permute-start(bf16[128,512]{1,0:T(8,128)(2,1)S(1)} %add_convert_fusion.1.refs_0_), channel_id=1, source_target_pairs={{0,4},{4,0},{1,5},{5,1},{2,6},{6,2},{3,7},{7,3},{8,12},{12,8},{9,1... | collective-permute-start | bytes 393224 | tf_op jit(solution)/shard_map/ppermute | solution.py:342
  6.1 0.0 collective-permute-done.2
  6.1 1.6 %collective-permute-start.3 = (bf16[128,512]{1,0:T(8,128)(2,1)S(1)}, bf16[128,512]{1,0:T(8,128)(2,1)S(1)}, u32[]{:S(2)}, u32[]{:S(2)}) collective-permute-start(bf16[128,512]{1,0:T(8,128)(2,1)S(1)} %add_convert_fusion), channel_id=1, source_target_pairs={{0,12},{4,8},{8,4},{12,0},{16,28},{20,24},{24,20},{28,16},{1,13},{... | collective-permute-start | bytes 393224 | tf_op jit(solution)/shard_map/ppermute | solution.py:346
  7.7 0.3 shard_map.39
  8.0 0.0 collective-permute-done.1
  8.0 0.1 convert_add_fusion.own
  8.2 0.1 collective-permute-start.5
  8.3 3.8 %collective-permute-done.4.refs_1_ = bf16[128,512]{1,0:T(8,128)(2,1)S(1)} collective-permute-done((bf16[128,512]{1,0:T(8,128)(2,1)S(1)}, bf16[128,512]{1,0:T(8,128)(2,1)S(1)}, u32[]{:S(2)}, u32[]{:S(2)}) %collective-permute-start.4) | collective-permute-done | bytes 131104 | tf_op jit(solution)/shard_map/ppermute | solution.py:342
  12.1 1.4 %collective-permute-done.3.refs_0_ = bf16[128,512]{1,0:T(8,128)(2,1)S(1)} collective-permute-done((bf16[128,512]{1,0:T(8,128)(2,1)S(1)}, bf16[128,512]{1,0:T(8,128)(2,1)S(1)}, u32[]{:S(2)}, u32[]{:S(2)}) %collective-permute-start.3) | collective-permute-done | bytes 131104 | tf_op jit(solution)/shard_map/ppermute | solution.py:346
  13.4 0.8 %collective-permute-done.5.refs_2_ = bf16[128,512]{1,0:T(8,128)(2,1)S(1)} collective-permute-done((bf16[128,512]{1,0:T(8,128)(2,1)S(1)}, bf16[128,512]{1,0:T(8,128)(2,1)S(1)}, u32[]{:S(2)}, u32[]{:S(2)}) %collective-permute-start.5) | collective-permute-done | bytes 131104 | tf_op jit(solution)/shard_map/ppermute | solution.py:342
  14.3 0.1 shard_map.40
  14.3 2.7 %collective-permute-start.6 = (bf16[128,384]{1,0:T(8,128)(2,1)S(1)}, bf16[128,384]{1,0:T(8,128)(2,1)S(1)}, u32[]{:S(2)}, u32[]{:S(2)}) collective-permute-start(bf16[128,384]{1,0:T(8,128)(2,1)S(1)} %get-tuple-element.26), channel_id=1, source_target_pairs={{0,16},{8,24},{16,0},{24,8},{1,17},{9,25},{17,1},{25,9},{2,18},{10... | collective-permute-start | bytes 294920 | tf_op jit(solution)/shard_map/ppermute | solution.py:342
  17.0 0.3 collective-permute-start.9
  17.3 5.0 %collective-permute-done.6 = bf16[128,384]{1,0:T(8,128)(2,1)S(1)} collective-permute-done((bf16[128,384]{1,0:T(8,128)(2,1)S(1)}, bf16[128,384]{1,0:T(8,128)(2,1)S(1)}, u32[]{:S(2)}, u32[]{:S(2)}) %collective-permute-start.6) | collective-permute-done | bytes 98336 | tf_op jit(solution)/shard_map/ppermute | solution.py:342
  22.3 0.8 %collective-permute-start.7 = (bf16[128,384]{1,0:T(8,128)(2,1)S(1)}, bf16[128,384]{1,0:T(8,128)(2,1)S(1)}, u32[]{:S(2)}, u32[]{:S(2)}) collective-permute-start(bf16[128,384]{1,0:T(8,128)(2,1)S(1)} %add_convert_fusion.2.refs_0_), channel_id=1, source_target_pairs={{0,8},{8,0},{16,24},{24,16},{1,9},{9,1},{17,25},{25,17},{2,10},{10... | collective-permute-start | bytes 294920 | tf_op jit(solution)/shard_map/ppermute | solution.py:342
  23.1 0.0 collective-permute-done.9
  23.1 1.4 %collective-permute-start.10 = (bf16[128,128]{1,0:T(8,128)(2,1)S(1)}, bf16[128,128]{1,0:T(8,128)(2,1)S(1)}, u32[]{:S(2)}, u32[]{:S(2)}) collective-permute-start(bf16[128,128]{1,0:T(8,128)(2,1)S(1)} %add_convert_fusion.3.refs_3_), channel_id=1, source_target_pairs={{0,8},{8,0},{16,24},{24,16},{1,9},{9,1},{17,25},{25,17},{2,10},{10... | collective-permute-start | bytes 98312 | tf_op jit(solution)/shard_map/ppermute | solution.py:342
  24.5 2.5 %collective-permute-done.7.refs_1_ = bf16[128,384]{1,0:T(8,128)(2,1)S(1)} collective-permute-done((bf16[128,384]{1,0:T(8,128)(2,1)S(1)}, bf16[128,384]{1,0:T(8,128)(2,1)S(1)}, u32[]{:S(2)}, u32[]{:S(2)}) %collective-permute-start.7) | collective-permute-done | bytes 98336 | tf_op jit(solution)/shard_map/ppermute | solution.py:342
  27.0 0.1 collective-permute-start.8
  27.1 0.2 collective-permute-done.10.refs_4_
  27.4 0.3 collective-permute-start.11
  27.7 0.9 %collective-permute-done.11.refs_5_ = bf16[256,128]{1,0:T(8,128)(2,1)S(1)} collective-permute-done((bf16[256,128]{1,0:T(8,128)(2,1)S(1)}, bf16[256,128]{1,0:T(8,128)(2,1)S(1)}, u32[]{:S(2)}, u32[]{:S(2)}) %collective-permute-start.11) | collective-permute-done | bytes 65568 | tf_op jit(solution)/shard_map/ppermute | solution.py:342
  28.6 0.0 collective-permute-done.8.refs_2_
  28.6 6.2 %shard_map.41 = (bf16[32,512]{1,0:T(8,128)(2,1)S(1)}, bf16[32,512]{1,0:T(8,128)(2,1)S(1)}) custom-call(s32[2,2]{1,0:T(2,128)} %counts_hbm.1, bf16[128,384]{1,0:T(8,128)(2,1)S(1)} %add_convert_fusion.2.refs_0_, bf16[128,384]{1,0:T(8,128)(2,1)S(1)} %collective-permute-done.7.refs_1_, bf16[256,384]{1,0:T(8,128)(2,1)S(1)} %collective-permute-done.8.refs_2_, ...), custom_call_target="tpu_custom_call" | custom-call | tf_op jit(solution)/shard_map/pallas_call | solution.py:289
  34.8 1.3 %collective-permute-start.12 = (bf16[32,512]{1,0:T(8,128)(2,1)S(1)}, bf16[32,512]{1,0:T(8,128)(2,1)S(1)}, u32[]{:S(2)}, u32[]{:S(2)}) collective-permute-start(bf16[32,512]{1,0:T(8,128)(2,1)S(1)} %get-tuple-element.29.refs_3_), channel_id=1, source_target_pairs={{0,1},{1,0},{4,5},{5,4},{2,3},{3,2},{6,7},{7,6},{8,9},{9,8},{12,13... | collective-permute-start | bytes 98312 | tf_op jit(solution)/shard_map/ppermute | solution.py:382
  36.1 1.4 %collective-permute-start.14 = (bf16[32,512]{1,0:T(8,128)(2,1)S(1)}, bf16[32,512]{1,0:T(8,128)(2,1)S(1)}, u32[]{:S(2)}, u32[]{:S(2)}) collective-permute-start(bf16[32,512]{1,0:T(8,128)(2,1)S(1)} %get-tuple-element.30), channel_id=1, source_target_pairs={{0,5},{1,4},{4,1},{5,0},{2,7},{3,6},{6,3},{7,2},{8,13},{9,12},{12,... | collective-permute-start | bytes 98312 | tf_op jit(solution)/shard_map/ppermute | solution.py:382
  37.5 0.8 %collective-permute-start.13 = (bf16[32,512]{1,0:T(8,128)(2,1)S(1)}, bf16[32,512]{1,0:T(8,128)(2,1)S(1)}, u32[]{:S(2)}, u32[]{:S(2)}) collective-permute-start(bf16[32,512]{1,0:T(8,128)(2,1)S(1)} %get-tuple-element.30), channel_id=1, source_target_pairs={{0,4},{1,5},{4,0},{5,1},{2,6},{3,7},{6,2},{7,3},{8,12},{9,13},{12,... | collective-permute-start | bytes 98312 | tf_op jit(solution)/shard_map/ppermute | solution.py:382
  38.4 0.4 %collective-permute-done.12.refs_0_ = bf16[32,512]{1,0:T(8,128)(2,1)S(1)} collective-permute-done((bf16[32,512]{1,0:T(8,128)(2,1)S(1)}, bf16[32,512]{1,0:T(8,128)(2,1)S(1)}, u32[]{:S(2)}, u32[]{:S(2)}) %collective-permute-start.12) | collective-permute-done | bytes 32800 | tf_op jit(solution)/shard_map/ppermute | solution.py:382
  38.8 2.3 %collective-permute-done.14.refs_2_ = bf16[32,512]{1,0:T(8,128)(2,1)S(1)} collective-permute-done((bf16[32,512]{1,0:T(8,128)(2,1)S(1)}, bf16[32,512]{1,0:T(8,128)(2,1)S(1)}, u32[]{:S(2)}, u32[]{:S(2)}) %collective-permute-start.14) | collective-permute-done | bytes 32800 | tf_op jit(solution)/shard_map/ppermute | solution.py:382
  41.0 0.4 collective-permute-done.13.refs_1_
  41.4 0.7 %shard_map.42 = bf16[4,32,512]{2,1,0:T(8,128)(2,1)} custom-call(bf16[32,512]{1,0:T(8,128)(2,1)S(1)} %collective-permute-done.12.refs_0_, bf16[32,512]{1,0:T(8,128)(2,1)S(1)} %collective-permute-done.13.refs_1_, bf16[32,512]{1,0:T(8,128)(2,1)S(1)} %collective-permute-done.14.refs_2_, bf16[32,512]{1,0:T(8,128)(2,1)S(1)} %get-tuple-element.29.refs_3_), custom_call_target="tpu_custom_call" | custom-call | tf_op jit(solution)/shard_map/pallas_call | solution.py:325
  (7 shorter events, 0.1 us)
Async XLA Ops:
  1.6 1.6 %collective-permute-start = (bf16[128,512]{1,0:T(8,128)(2,1)S(1)}, bf16[128,512]{1,0:T(8,128)(2,1)S(1)}, u32[]{:S(2)}, u32[]{:S(2)}) collective-permute-start(bf16[128,512]{1,0:T(8,128)(2,1)S(1)} %get-tuple-element.21), channel_id=1, source_target_pairs={{0,2},{2,0},{1,3},{3,1},{4,6},{6,4},{5,7},{7,5},{8,10},{10,8},{9,1... | collective-permute-start | bytes 393224 | tf_op jit(solution)/shard_map/ppermute | solution.py:342
  2.1 3.9 %collective-permute-start.2 = (bf16[128,512]{1,0:T(8,128)(2,1)S(1)}, bf16[128,512]{1,0:T(8,128)(2,1)S(1)}, u32[]{:S(2)}, u32[]{:S(2)}) collective-permute-start(bf16[128,512]{1,0:T(8,128)(2,1)S(1)} %get-tuple-element.24), channel_id=1, source_target_pairs={{0,2},{2,0},{1,3},{3,1},{4,6},{6,4},{5,7},{7,5},{8,10},{10,8},{9,1... | collective-permute-start | bytes 393224 | tf_op jit(solution)/shard_map/ppermute | solution.py:342
  2.7 5.4 %collective-permute-start.1 = (bf16[256,512]{1,0:T(8,128)(2,1)S(1)}, bf16[256,512]{1,0:T(8,128)(2,1)S(1)}, u32[]{:S(2)}, u32[]{:S(2)}) collective-permute-start(bf16[256,512]{1,0:T(8,128)(2,1)S(1)} %get-tuple-element.22), channel_id=1, source_target_pairs={{0,2},{2,0},{1,3},{3,1},{4,6},{6,4},{5,7},{7,5},{8,10},{10,8},{9,1... | collective-permute-start | bytes 786440 | tf_op jit(solution)/shard_map/ppermute | solution.py:342
  3.2 8.8 %collective-permute-start.4 = (bf16[128,512]{1,0:T(8,128)(2,1)S(1)}, bf16[128,512]{1,0:T(8,128)(2,1)S(1)}, u32[]{:S(2)}, u32[]{:S(2)}) collective-permute-start(bf16[128,512]{1,0:T(8,128)(2,1)S(1)} %add_convert_fusion.1.refs_0_), channel_id=1, source_target_pairs={{0,4},{4,0},{1,5},{5,1},{2,6},{6,2},{3,7},{7,3},{8,12},{12,8},{9,1... | collective-permute-start | bytes 393224 | tf_op jit(solution)/shard_map/ppermute | solution.py:342
  6.1 7.3 %collective-permute-start.3 = (bf16[128,512]{1,0:T(8,128)(2,1)S(1)}, bf16[128,512]{1,0:T(8,128)(2,1)S(1)}, u32[]{:S(2)}, u32[]{:S(2)}) collective-permute-start(bf16[128,512]{1,0:T(8,128)(2,1)S(1)} %add_convert_fusion), channel_id=1, source_target_pairs={{0,12},{4,8},{8,4},{12,0},{16,28},{20,24},{24,20},{28,16},{1,13},{... | collective-permute-start | bytes 393224 | tf_op jit(solution)/shard_map/ppermute | solution.py:346
  8.2 6.1 %collective-permute-start.5 = (bf16[128,512]{1,0:T(8,128)(2,1)S(1)}, bf16[128,512]{1,0:T(8,128)(2,1)S(1)}, u32[]{:S(2)}, u32[]{:S(2)}) collective-permute-start(bf16[128,512]{1,0:T(8,128)(2,1)S(1)} %slice.7), channel_id=1, source_target_pairs={{0,8},{8,0},{16,24},{24,16},{1,9},{9,1},{17,25},{25,17},{2,10},{10... | collective-permute-start | bytes 393224 | tf_op jit(solution)/shard_map/ppermute | solution.py:342
  14.3 8.0 %collective-permute-start.6 = (bf16[128,384]{1,0:T(8,128)(2,1)S(1)}, bf16[128,384]{1,0:T(8,128)(2,1)S(1)}, u32[]{:S(2)}, u32[]{:S(2)}) collective-permute-start(bf16[128,384]{1,0:T(8,128)(2,1)S(1)} %get-tuple-element.26), channel_id=1, source_target_pairs={{0,16},{8,24},{16,0},{24,8},{1,17},{9,25},{17,1},{25,9},{2,18},{10... | collective-permute-start | bytes 294920 | tf_op jit(solution)/shard_map/ppermute | solution.py:342
  17.0 6.0 %collective-permute-start.9 = (bf16[128,128]{1,0:T(8,128)(2,1)S(1)}, bf16[128,128]{1,0:T(8,128)(2,1)S(1)}, u32[]{:S(2)}, u32[]{:S(2)}) collective-permute-start(bf16[128,128]{1,0:T(8,128)(2,1)S(1)} %get-tuple-element.28), channel_id=1, source_target_pairs={{0,16},{8,24},{16,0},{24,8},{1,17},{9,25},{17,1},{25,9},{2,18},{10... | collective-permute-start | bytes 98312 | tf_op jit(solution)/shard_map/ppermute | solution.py:342
  22.3 4.7 %collective-permute-start.7 = (bf16[128,384]{1,0:T(8,128)(2,1)S(1)}, bf16[128,384]{1,0:T(8,128)(2,1)S(1)}, u32[]{:S(2)}, u32[]{:S(2)}) collective-permute-start(bf16[128,384]{1,0:T(8,128)(2,1)S(1)} %add_convert_fusion.2.refs_0_), channel_id=1, source_target_pairs={{0,8},{8,0},{16,24},{24,16},{1,9},{9,1},{17,25},{25,17},{2,10},{10... | collective-permute-start | bytes 294920 | tf_op jit(solution)/shard_map/ppermute | solution.py:342
  23.1 4.2 %collective-permute-start.10 = (bf16[128,128]{1,0:T(8,128)(2,1)S(1)}, bf16[128,128]{1,0:T(8,128)(2,1)S(1)}, u32[]{:S(2)}, u32[]{:S(2)}) collective-permute-start(bf16[128,128]{1,0:T(8,128)(2,1)S(1)} %add_convert_fusion.3.refs_3_), channel_id=1, source_target_pairs={{0,8},{8,0},{16,24},{24,16},{1,9},{9,1},{17,25},{25,17},{2,10},{10... | collective-permute-start | bytes 98312 | tf_op jit(solution)/shard_map/ppermute | solution.py:342
  27.0 1.6 %collective-permute-start.8 = (bf16[256,384]{1,0:T(8,128)(2,1)S(1)}, bf16[256,384]{1,0:T(8,128)(2,1)S(1)}, u32[]{:S(2)}, u32[]{:S(2)}) collective-permute-start(bf16[256,384]{1,0:T(8,128)(2,1)S(1)} %pad_maximum_fusion), channel_id=1, source_target_pairs={{0,2},{2,0},{1,3},{3,1},{4,6},{6,4},{5,7},{7,5},{8,10},{10,8},{9,1... | collective-permute-start | bytes 589832 | tf_op jit(solution)/shard_map/ppermute | solution.py:342
  27.4 1.3 %collective-permute-start.11 = (bf16[256,128]{1,0:T(8,128)(2,1)S(1)}, bf16[256,128]{1,0:T(8,128)(2,1)S(1)}, u32[]{:S(2)}, u32[]{:S(2)}) collective-permute-start(bf16[256,128]{1,0:T(8,128)(2,1)S(1)} %pad_maximum_fusion.1), channel_id=1, source_target_pairs={{0,2},{2,0},{1,3},{3,1},{4,6},{6,4},{5,7},{7,5},{8,10},{10,8},{9,1... | collective-permute-start | bytes 196616 | tf_op jit(solution)/shard_map/ppermute | solution.py:342
  34.8 4.0 %collective-permute-start.12 = (bf16[32,512]{1,0:T(8,128)(2,1)S(1)}, bf16[32,512]{1,0:T(8,128)(2,1)S(1)}, u32[]{:S(2)}, u32[]{:S(2)}) collective-permute-start(bf16[32,512]{1,0:T(8,128)(2,1)S(1)} %get-tuple-element.29.refs_3_), channel_id=1, source_target_pairs={{0,1},{1,0},{4,5},{5,4},{2,3},{3,2},{6,7},{7,6},{8,9},{9,8},{12,13... | collective-permute-start | bytes 98312 | tf_op jit(solution)/shard_map/ppermute | solution.py:382
  36.1 4.9 %collective-permute-start.14 = (bf16[32,512]{1,0:T(8,128)(2,1)S(1)}, bf16[32,512]{1,0:T(8,128)(2,1)S(1)}, u32[]{:S(2)}, u32[]{:S(2)}) collective-permute-start(bf16[32,512]{1,0:T(8,128)(2,1)S(1)} %get-tuple-element.30), channel_id=1, source_target_pairs={{0,5},{1,4},{4,1},{5,0},{2,7},{3,6},{6,3},{7,2},{8,13},{9,12},{12,... | collective-permute-start | bytes 98312 | tf_op jit(solution)/shard_map/ppermute | solution.py:382
  37.5 3.9 %collective-permute-start.13 = (bf16[32,512]{1,0:T(8,128)(2,1)S(1)}, bf16[32,512]{1,0:T(8,128)(2,1)S(1)}, u32[]{:S(2)}, u32[]{:S(2)}) collective-permute-start(bf16[32,512]{1,0:T(8,128)(2,1)S(1)} %get-tuple-element.30), channel_id=1, source_target_pairs={{0,4},{1,5},{4,0},{5,1},{2,6},{3,7},{6,2},{7,3},{8,12},{9,13},{12,... | collective-permute-start | bytes 98312 | tf_op jit(solution)/shard_map/ppermute | solution.py:382

commit v19 on v18

--- a/solution.py
+++ b/solution.py
@@ -19,46 +19,47 @@
     return pltpu.CompilerParams(vmem_limit_bytes=limit << 20)
 
 
-def half_sum(patch, cot, block, side, scale, part=None):
+def piece_sum(patch, cot, scale, block, side, part):
     quarter = patch.shape[3] // 2
-    rows = slice(None) if part is None else slice(part * quarter, (part + 1) * quarter)
+    rows = slice(part * quarter, (part + 1) * quarter)
     terms = lax.dot_general(
         patch[block, side, :, rows], cot[block], ROWS_IN_COLS, preferred_element_type=F32
     )
     return terms * scale
 
 
-def load_kernel(scale, patch_hbm, cot_hbm, given_near, given_far, patch, cot, sems):
+def load_kernel(scale, patch_hbm, cot_hbm, given_column, given_line, patch, cot, sems):
     half = patch.shape[3]
     width = half // 2
     column, core, parity = lax.axis_index("x"), lax.axis_index("core"), lax.axis_index("z") % 2
     copies = []
-    quarter = given_near.shape[0]
 
     def fetch(source, target):
         copies.append(pltpu.make_async_copy(source, target, sems.at[len(copies)]))
         copies[-1].start()
 
-    def fetch_patch(block, side):
-        for quarter in range(2):
-            first = (core ^ side) * half + (parity ^ quarter) * width
-            fetch(
-                patch_hbm.at[column ^ block, :, pl.ds(pl.multiple_of(first, width), width)],
-                patch.at[block, side, :, quarter * width : (quarter + 1) * width],
-            )
+    def fetch_patch(block, side, part):
+        first = (core ^ side) * half + (parity ^ part) * width
+        fetch(
+            patch_hbm.at[column ^ block, :, pl.ds(pl.multiple_of(first, width), width)],
+            patch.at[block, side, :, part * width : (part + 1) * width],
+        )
 
     fetch(cot_hbm.at[column ^ 1], cot.at[1])
-    fetch_patch(1, 1)
+    fetch_patch(1, 1, 0)
+    fetch(cot_hbm.at[column], cot.at[0])
+    fetch_patch(0, 1, 1)
     needed = len(copies)
-    fetch_patch(1, 0)
-    fetch(cot_hbm.at[column], cot.at[0])
-    fetch_patch(0, 1)
-    fetch_patch(0, 0)
-    for copy in copies[:needed]:
+    for side in range(2):
+        for block, part in ((1, 0), (0, 1), (1, 1), (0, 0)):
+            if side == 0 or block == part:
+                fetch_patch(block, side, part)
+    for copy in copies[:2]:
         copy.wait()
-    terms = half_sum(patch, cot, 1, 1, scale).astype(BF16)
-    given_near[...] = terms[:quarter]
-    given_far[...] = terms[quarter:]
+    given_column[...] = piece_sum(patch, cot, scale, 1, 1, 0).astype(BF16)
+    for copy in copies[2:needed]:
+        copy.wait()
+    given_line[...] = piece_sum(patch, cot, scale, 0, 1, 1).astype(BF16)
     for copy in copies[needed:]:
         copy.wait()
 
@@ -85,8 +86,11 @@
 
 
 def sums_kernel(scale, wanted, patch, cot, *refs):
-    for (block, side, part, dtype), out in zip(wanted, refs[-len(wanted) :]):
-        out[...] = half_sum(patch, cot, block, side, scale, part).astype(dtype)
+    for (dtype, pieces), out in zip(wanted, refs[-len(wanted) :]):
+        rows = out.shape[0] // len(pieces)
+        for index, piece in enumerate(pieces):
+            value = piece_sum(patch, cot, scale, *piece).astype(dtype)
+            out[index * rows : (index + 1) * rows, :] = value
 
 
 def sums(scale, patch, cot, after, *wanted):
@@ -94,8 +98,8 @@
     return pl.pallas_call(
         functools.partial(sums_kernel, scale, wanted),
         out_shape=[
-            jax.ShapeDtypeStruct((half if part is None else half // 2, 2 * half), dtype)
-            for _, _, part, dtype in wanted
+            jax.ShapeDtypeStruct((len(pieces) * half // 2, 2 * half), dtype)
+            for dtype, pieces in wanted
         ],
         in_specs=[VMEM] * 2 + [pl.BlockSpec(memory_space=pl.ANY)] * len(after),
         out_specs=[VMEM] * len(wanted),
@@ -334,7 +338,7 @@
 
 def shards(line, groups, patches, cotangents, newton_counts):
     blocks, pix, width = patches.shape
-    half, quarter = width // 2, width // 4
+    half = width // 2
     rows = half // (2 * line)
     scale = 1.0 / float(pix * 4 * line * width) ** 0.5
 
@@ -345,19 +349,29 @@
         moves = [(2 * z + x, 2 * (z ^ 1) + (x ^ 1)) for z in range(line) for x in range(2)]
         return lax.ppermute(array, ("z", "x"), moves)
 
-    given_near, given_far, patch, cot = load(scale, patches, cotangents)
-    came_near, came_far = swap(given_near, "core"), swap(given_far, "core")
-    kept_near, kept_far, given_on = sums(
-        scale, patch, cot, (), (1, 0, 0, F32), (1, 0, 1, F32), (0, 1, None, BF16)
-    )
-    came_on = swap(given_on, "core")
-    to_column = add(kept_near, came_near).astype(BF16)
-    to_diagonal = add(kept_far, came_far).astype(BF16)
+    given_column, given_line, patch, cot = load(scale, patches, cotangents)
+    came_column, came_line = swap(given_column, "core"), swap(given_line, "core")
+    kept_column, kept_line, given_rest = sums(
+        scale,
+        patch,
+        cot,
+        (),
+        (F32, ((1, 0, 0),)),
+        (F32, ((0, 0, 1),)),
+        (BF16, ((1, 1, 1), (0, 1, 0))),
+    )
+    came_rest = swap(given_rest, "core")
+    to_column = add(kept_column, came_column).astype(BF16)
+    from_column = swap(to_column, "x")
+    to_line = add(kept_line, came_line).astype(BF16)
+    from_line = swap(to_line, "z")
+    kept_diagonal, own = sums(
+        scale, patch, cot, (to_line,), (F32, ((1, 0, 1),)), (F32, ((0, 0, 0),))
+    )
+    quarter = own.shape[0]
+    to_diagonal = add(kept_diagonal, came_rest[:quarter]).astype(BF16)
+    own = add(own, came_rest[quarter:])
     from_diagonal = swap_diagonal(to_diagonal)
-    from_column = swap(to_column, "x")
-    (kept_on,) = sums(scale, patch, cot, (to_column,), (0, 0, None, F32))
-    own = add(kept_on, came_on)
-    from_line = swap(own[quarter:].astype(BF16), "z")
     left, right, send_left, send_right = collect(
         width * 3 // 4, own, from_diagonal, from_column, from_line
     )

time: 42.3 us -> 42.7 us (level)
    ppermute x11, starting transfers between devices: 9.59 us -> 11.1 us  [swap(): lax.ppermute(array, axis, [(i, i ^ mask) for i in range(lax.axis_size(axi...]
    ppermute x1, starting transfers between devices: 1.61 us -> 0.19 us  [swap_diagonal(): return lax.ppermute(array, ('z', 'x'), moves)]
    ppermute x1, waiting for transfers between devices: 1.39 us -> 0.01 us  [swap_diagonal(): return lax.ppermute(array, ('z', 'x'), moves)]
    ppermute x11, waiting for transfers between devices: 13.3 us -> 14.1 us  [swap(): lax.ppermute(array, axis, [(i, i ^ mask) for i in range(lax.axis_size(axi...]
    ppermute x3, waiting for transfers between devices: 3.09 us -> 3.85 us  [pass_on(): return lax.ppermute(send if flip else keep, ('x', 'group'), moves)]
  transfers between devices with their start and end apart: 15 -> 15, of which waited for: 10 -> 9; matrix products, arithmetic and copies ran while one was open for 0% -> 0% of each run, Pallas kernels for 2% -> 2%
where the time goes in v19:
time: 42.7 us; the launch traced here: 42.5 us
  waiting for transfers between devices  18 us (42%)
  starting transfers between devices  14.9 us (35%)
  Pallas kernels  9.35 us (22%)
    ppermute x11, waiting for transfers between devices, swap(): lax.ppermute(array, axis, [(i, i ^ mask) for i in range(lax.axis_size(axi...  14.1 us
    ppermute x11, starting transfers between devices, swap(): lax.ppermute(array, axis, [(i, i ^ mask) for i in range(lax.axis_size(axi...  11.1 us
    pallas_call x1, Pallas kernels, root(): pl.pallas_call(functools.partial(root_kernel, most), out_shape=[out, out]...  6.15 us
    ppermute x3, waiting for transfers between devices, pass_on(): return lax.ppermute(send if flip else keep, ('x', 'group'), moves)  3.85 us
    ppermute x3, starting transfers between devices, pass_on(): return lax.ppermute(send if flip else keep, ('x', 'group'), moves)  3.62 us
    pallas_call x1, Pallas kernels, load(): pl.pallas_call(functools.partial(load_kernel, scale), out_shape=[jax.Shap...  1.67 us
  transfers between devices with their start and end apart: 15, of which 9 were waited for; matrix products, arithmetic and copies ran while one was open for 0% of the time, Pallas kernels for 2%

profile of v19, /device:TPU:0, one launch (start us, length us, event | category | flops | bytes accessed | tf_op | source)
XLA Modules:
  0.0 42.5 jit_solution(16715599012248761850)
XLA Ops:
  0.0 1.7 %shard_map.37 = (bf16[128,512]{1,0:T(8,128)(2,1)S(1)}, bf16[128,512]{1,0:T(8,128)(2,1)S(1)}, bf16[2,2,512,256]{3,2,1,0:T(8,128)(2,1)S(1)}, bf16[2,512,512]{2,1,0:T(8,128)(2,1)S(1)}) custom-call(bf16[2,512,512]{2,1,0:T(8,128)(2,1)} %patch_hbm.1, bf16[2,512,512]{2,1,0:T(8,128)(2,1)} %cot_hbm.1), custom_call_target="tpu_custom_call" | custom-call | tf_op jit(solution)/shard_map/pallas_call | solution.py:70
  1.7 0.5 %collective-permute-start = (bf16[128,512]{1,0:T(8,128)(2,1)S(1)}, bf16[128,512]{1,0:T(8,128)(2,1)S(1)}, u32[]{:S(2)}, u32[]{:S(2)}) collective-permute-start(bf16[128,512]{1,0:T(8,128)(2,1)S(1)} %get-tuple-element.23), channel_id=1, source_target_pairs={{0,2},{2,0},{1,3},{3,1},{4,6},{6,4},{5,7},{7,5},{8,10},{10,8},{9,1... | collective-permute-start | bytes 393224 | tf_op jit(solution)/shard_map/ppermute | solution.py:346
  2.2 0.1 collective-permute-start.3
  2.3 0.5 %shard_map.38 = (f32[128,512]{1,0:T(8,128)S(1)}, f32[128,512]{1,0:T(8,128)S(1)}, bf16[256,512]{1,0:T(8,128)(2,1)S(1)}) custom-call(bf16[2,2,512,256]{3,2,1,0:T(8,128)(2,1)S(1)} %get-tuple-element.20.patch, bf16[2,512,512]{2,1,0:T(8,128)(2,1)S(1)} %get-tuple-element.21.cot), custom_call_target="tpu_custom_call" | custom-call | flops 402653184 | bytes 1048576 | tf_op jit(solution)/shard_map/pallas_call | solution.py:98
  2.7 0.5 %collective-permute-start.1 = (bf16[256,512]{1,0:T(8,128)(2,1)S(1)}, bf16[256,512]{1,0:T(8,128)(2,1)S(1)}, u32[]{:S(2)}, u32[]{:S(2)}) collective-permute-start(bf16[256,512]{1,0:T(8,128)(2,1)S(1)} %get-tuple-element.25), channel_id=1, source_target_pairs={{0,2},{2,0},{1,3},{3,1},{4,6},{6,4},{5,7},{7,5},{8,10},{10,8},{9,1... | collective-permute-start | bytes 786440 | tf_op jit(solution)/shard_map/ppermute | solution.py:346
  3.2 0.0 collective-permute-done
  3.3 2.9 %collective-permute-start.5 = (bf16[128,512]{1,0:T(8,128)(2,1)S(1)}, bf16[128,512]{1,0:T(8,128)(2,1)S(1)}, u32[]{:S(2)}, u32[]{:S(2)}) collective-permute-start(bf16[128,512]{1,0:T(8,128)(2,1)S(1)} %add_convert_fusion.2.refs_0_), channel_id=1, source_target_pairs={{0,8},{8,0},{16,24},{24,16},{1,9},{9,1},{17,25},{25,17},{2,10},{10... | collective-permute-start | bytes 393224 | tf_op jit(solution)/shard_map/ppermute | solution.py:346
  6.2 0.0 collective-permute-done.3
  6.3 1.6 %collective-permute-start.4 = (bf16[128,512]{1,0:T(8,128)(2,1)S(1)}, bf16[128,512]{1,0:T(8,128)(2,1)S(1)}, u32[]{:S(2)}, u32[]{:S(2)}) collective-permute-start(bf16[128,512]{1,0:T(8,128)(2,1)S(1)} %add_convert_fusion), channel_id=1, source_target_pairs={{0,4},{4,0},{1,5},{5,1},{2,6},{6,2},{3,7},{7,3},{8,12},{12,8},{9,1... | collective-permute-start | bytes 393224 | tf_op jit(solution)/shard_map/ppermute | solution.py:346
  7.8 0.3 shard_map.39
  8.1 0.0 collective-permute-done.1
  8.1 0.1 add_convert_fusion.1
  8.2 0.2 collective-permute-start.2
  8.4 1.7 %collective-permute-done.5.refs_2_ = bf16[128,512]{1,0:T(8,128)(2,1)S(1)} collective-permute-done((bf16[128,512]{1,0:T(8,128)(2,1)S(1)}, bf16[128,512]{1,0:T(8,128)(2,1)S(1)}, u32[]{:S(2)}, u32[]{:S(2)}) %collective-permute-start.5) | collective-permute-done | bytes 131104 | tf_op jit(solution)/shard_map/ppermute | solution.py:346
  10.1 4.4 %collective-permute-done.4.refs_1_ = bf16[128,512]{1,0:T(8,128)(2,1)S(1)} collective-permute-done((bf16[128,512]{1,0:T(8,128)(2,1)S(1)}, bf16[128,512]{1,0:T(8,128)(2,1)S(1)}, u32[]{:S(2)}, u32[]{:S(2)}) %collective-permute-start.4) | collective-permute-done | bytes 131104 | tf_op jit(solution)/shard_map/ppermute | solution.py:346
  14.5 0.0 collective-permute-done.2.refs_0_
  14.5 0.1 shard_map.40
  14.5 2.7 %collective-permute-start.6 = (bf16[128,384]{1,0:T(8,128)(2,1)S(1)}, bf16[128,384]{1,0:T(8,128)(2,1)S(1)}, u32[]{:S(2)}, u32[]{:S(2)}) collective-permute-start(bf16[128,384]{1,0:T(8,128)(2,1)S(1)} %get-tuple-element.30), channel_id=1, source_target_pairs={{0,16},{8,24},{16,0},{24,8},{1,17},{9,25},{17,1},{25,9},{2,18},{10... | collective-permute-start | bytes 294920 | tf_op jit(solution)/shard_map/ppermute | solution.py:346
  17.2 0.3 collective-permute-start.9
  17.5 4.4 %collective-permute-done.6 = bf16[128,384]{1,0:T(8,128)(2,1)S(1)} collective-permute-done((bf16[128,384]{1,0:T(8,128)(2,1)S(1)}, bf16[128,384]{1,0:T(8,128)(2,1)S(1)}, u32[]{:S(2)}, u32[]{:S(2)}) %collective-permute-start.6) | collective-permute-done | bytes 98336 | tf_op jit(solution)/shard_map/ppermute | solution.py:346
  21.9 0.8 %collective-permute-start.7 = (bf16[128,384]{1,0:T(8,128)(2,1)S(1)}, bf16[128,384]{1,0:T(8,128)(2,1)S(1)}, u32[]{:S(2)}, u32[]{:S(2)}) collective-permute-start(bf16[128,384]{1,0:T(8,128)(2,1)S(1)} %add_convert_fusion.3.refs_0_), channel_id=1, source_target_pairs={{0,8},{8,0},{16,24},{24,16},{1,9},{9,1},{17,25},{25,17},{2,10},{10... | collective-permute-start | bytes 294920 | tf_op jit(solution)/shard_map/ppermute | solution.py:346
  22.7 0.0 collective-permute-done.9
  22.8 1.3 %collective-permute-start.10 = (bf16[128,128]{1,0:T(8,128)(2,1)S(1)}, bf16[128,128]{1,0:T(8,128)(2,1)S(1)}, u32[]{:S(2)}, u32[]{:S(2)}) collective-permute-start(bf16[128,128]{1,0:T(8,128)(2,1)S(1)} %add_convert_fusion.4.refs_3_), channel_id=1, source_target_pairs={{0,8},{8,0},{16,24},{24,16},{1,9},{9,1},{17,25},{25,17},{2,10},{10... | collective-permute-start | bytes 98312 | tf_op jit(solution)/shard_map/ppermute | solution.py:346
  24.1 2.5 %collective-permute-done.7.refs_1_ = bf16[128,384]{1,0:T(8,128)(2,1)S(1)} collective-permute-done((bf16[128,384]{1,0:T(8,128)(2,1)S(1)}, bf16[128,384]{1,0:T(8,128)(2,1)S(1)}, u32[]{:S(2)}, u32[]{:S(2)}) %collective-permute-start.7) | collective-permute-done | bytes 98336 | tf_op jit(solution)/shard_map/ppermute | solution.py:346
  26.6 0.1 collective-permute-start.8
  26.7 0.2 collective-permute-done.10.refs_4_
  26.9 0.3 collective-permute-start.11
  27.3 0.9 %collective-permute-done.11.refs_5_ = bf16[256,128]{1,0:T(8,128)(2,1)S(1)} collective-permute-done((bf16[256,128]{1,0:T(8,128)(2,1)S(1)}, bf16[256,128]{1,0:T(8,128)(2,1)S(1)}, u32[]{:S(2)}, u32[]{:S(2)}) %collective-permute-start.11) | collective-permute-done | bytes 65568 | tf_op jit(solution)/shard_map/ppermute | solution.py:346
  28.2 0.0 collective-permute-done.8.refs_2_
  28.2 6.1 %shard_map.41 = (bf16[32,512]{1,0:T(8,128)(2,1)S(1)}, bf16[32,512]{1,0:T(8,128)(2,1)S(1)}) custom-call(s32[2,2]{1,0:T(2,128)} %counts_hbm.1, bf16[128,384]{1,0:T(8,128)(2,1)S(1)} %add_convert_fusion.3.refs_0_, bf16[128,384]{1,0:T(8,128)(2,1)S(1)} %collective-permute-done.7.refs_1_, bf16[256,384]{1,0:T(8,128)(2,1)S(1)} %collective-permute-done.8.refs_2_, ...), custom_call_target="tpu_custom_call" | custom-call | tf_op jit(solution)/shard_map/pallas_call | solution.py:293
  34.4 1.6 %collective-permute-start.12 = (bf16[32,512]{1,0:T(8,128)(2,1)S(1)}, bf16[32,512]{1,0:T(8,128)(2,1)S(1)}, u32[]{:S(2)}, u32[]{:S(2)}) collective-permute-start(bf16[32,512]{1,0:T(8,128)(2,1)S(1)} %get-tuple-element.33.refs_3_), channel_id=1, source_target_pairs={{0,1},{1,0},{4,5},{5,4},{2,3},{3,2},{6,7},{7,6},{8,9},{9,8},{12,13... | collective-permute-start | bytes 98312 | tf_op jit(solution)/shard_map/ppermute | solution.py:396
  36.0 2.0 %collective-permute-start.14 = (bf16[32,512]{1,0:T(8,128)(2,1)S(1)}, bf16[32,512]{1,0:T(8,128)(2,1)S(1)}, u32[]{:S(2)}, u32[]{:S(2)}) collective-permute-start(bf16[32,512]{1,0:T(8,128)(2,1)S(1)} %get-tuple-element.34), channel_id=1, source_target_pairs={{0,5},{1,4},{4,1},{5,0},{2,7},{3,6},{6,3},{7,2},{8,13},{9,12},{12,... | collective-permute-start | bytes 98312 | tf_op jit(solution)/shard_map/ppermute | solution.py:396
  37.9 0.1 collective-permute-start.13
  38.0 0.4 collective-permute-done.12.refs_0_
  38.4 2.4 %collective-permute-done.14.refs_2_ = bf16[32,512]{1,0:T(8,128)(2,1)S(1)} collective-permute-done((bf16[32,512]{1,0:T(8,128)(2,1)S(1)}, bf16[32,512]{1,0:T(8,128)(2,1)S(1)}, u32[]{:S(2)}, u32[]{:S(2)}) %collective-permute-start.14) | collective-permute-done | bytes 32800 | tf_op jit(solution)/shard_map/ppermute | solution.py:396
  40.8 1.1 %collective-permute-done.13.refs_1_ = bf16[32,512]{1,0:T(8,128)(2,1)S(1)} collective-permute-done((bf16[32,512]{1,0:T(8,128)(2,1)S(1)}, bf16[32,512]{1,0:T(8,128)(2,1)S(1)}, u32[]{:S(2)}, u32[]{:S(2)}) %collective-permute-start.13) | collective-permute-done | bytes 32800 | tf_op jit(solution)/shard_map/ppermute | solution.py:396
  41.9 0.7 %shard_map.42 = bf16[4,32,512]{2,1,0:T(8,128)(2,1)} custom-call(bf16[32,512]{1,0:T(8,128)(2,1)S(1)} %collective-permute-done.12.refs_0_, bf16[32,512]{1,0:T(8,128)(2,1)S(1)} %collective-permute-done.13.refs_1_, bf16[32,512]{1,0:T(8,128)(2,1)S(1)} %collective-permute-done.14.refs_2_, bf16[32,512]{1,0:T(8,128)(2,1)S(1)} %get-tuple-element.33.refs_3_), custom_call_target="tpu_custom_call" | custom-call | tf_op jit(solution)/shard_map/pallas_call | solution.py:329
  (6 shorter events, 0.1 us)
Async XLA Ops:
  1.7 1.6 %collective-permute-start = (bf16[128,512]{1,0:T(8,128)(2,1)S(1)}, bf16[128,512]{1,0:T(8,128)(2,1)S(1)}, u32[]{:S(2)}, u32[]{:S(2)}) collective-permute-start(bf16[128,512]{1,0:T(8,128)(2,1)S(1)} %get-tuple-element.23), channel_id=1, source_target_pairs={{0,2},{2,0},{1,3},{3,1},{4,6},{6,4},{5,7},{7,5},{8,10},{10,8},{9,1... | collective-permute-start | bytes 393224 | tf_op jit(solution)/shard_map/ppermute | solution.py:346
  2.2 4.0 %collective-permute-start.3 = (bf16[128,512]{1,0:T(8,128)(2,1)S(1)}, bf16[128,512]{1,0:T(8,128)(2,1)S(1)}, u32[]{:S(2)}, u32[]{:S(2)}) collective-permute-start(bf16[128,512]{1,0:T(8,128)(2,1)S(1)} %get-tuple-element.28), channel_id=1, source_target_pairs={{0,2},{2,0},{1,3},{3,1},{4,6},{6,4},{5,7},{7,5},{8,10},{10,8},{9,1... | collective-permute-start | bytes 393224 | tf_op jit(solution)/shard_map/ppermute | solution.py:346
  2.7 5.4 %collective-permute-start.1 = (bf16[256,512]{1,0:T(8,128)(2,1)S(1)}, bf16[256,512]{1,0:T(8,128)(2,1)S(1)}, u32[]{:S(2)}, u32[]{:S(2)}) collective-permute-start(bf16[256,512]{1,0:T(8,128)(2,1)S(1)} %get-tuple-element.25), channel_id=1, source_target_pairs={{0,2},{2,0},{1,3},{3,1},{4,6},{6,4},{5,7},{7,5},{8,10},{10,8},{9,1... | collective-permute-start | bytes 786440 | tf_op jit(solution)/shard_map/ppermute | solution.py:346
  3.3 6.8 %collective-permute-start.5 = (bf16[128,512]{1,0:T(8,128)(2,1)S(1)}, bf16[128,512]{1,0:T(8,128)(2,1)S(1)}, u32[]{:S(2)}, u32[]{:S(2)}) collective-permute-start(bf16[128,512]{1,0:T(8,128)(2,1)S(1)} %add_convert_fusion.2.refs_0_), channel_id=1, source_target_pairs={{0,8},{8,0},{16,24},{24,16},{1,9},{9,1},{17,25},{25,17},{2,10},{10... | collective-permute-start | bytes 393224 | tf_op jit(solution)/shard_map/ppermute | solution.py:346
  6.3 8.2 %collective-permute-start.4 = (bf16[128,512]{1,0:T(8,128)(2,1)S(1)}, bf16[128,512]{1,0:T(8,128)(2,1)S(1)}, u32[]{:S(2)}, u32[]{:S(2)}) collective-permute-start(bf16[128,512]{1,0:T(8,128)(2,1)S(1)} %add_convert_fusion), channel_id=1, source_target_pairs={{0,4},{4,0},{1,5},{5,1},{2,6},{6,2},{3,7},{7,3},{8,12},{12,8},{9,1... | collective-permute-start | bytes 393224 | tf_op jit(solution)/shard_map/ppermute | solution.py:346
  8.2 6.2 %collective-permute-start.2 = (bf16[128,512]{1,0:T(8,128)(2,1)S(1)}, bf16[128,512]{1,0:T(8,128)(2,1)S(1)}, u32[]{:S(2)}, u32[]{:S(2)}) collective-permute-start(bf16[128,512]{1,0:T(8,128)(2,1)S(1)} %get-tuple-element.35), channel_id=1, source_target_pairs={{0,12},{4,8},{8,4},{12,0},{16,28},{20,24},{24,20},{28,16},{1,13},{... | collective-permute-start | bytes 393224 | tf_op jit(solution)/shard_map/ppermute | solution.py:350
  14.5 7.3 %collective-permute-start.6 = (bf16[128,384]{1,0:T(8,128)(2,1)S(1)}, bf16[128,384]{1,0:T(8,128)(2,1)S(1)}, u32[]{:S(2)}, u32[]{:S(2)}) collective-permute-start(bf16[128,384]{1,0:T(8,128)(2,1)S(1)} %get-tuple-element.30), channel_id=1, source_target_pairs={{0,16},{8,24},{16,0},{24,8},{1,17},{9,25},{17,1},{25,9},{2,18},{10... | collective-permute-start | bytes 294920 | tf_op jit(solution)/shard_map/ppermute | solution.py:346
  17.2 5.6 %collective-permute-start.9 = (bf16[128,128]{1,0:T(8,128)(2,1)S(1)}, bf16[128,128]{1,0:T(8,128)(2,1)S(1)}, u32[]{:S(2)}, u32[]{:S(2)}) collective-permute-start(bf16[128,128]{1,0:T(8,128)(2,1)S(1)} %get-tuple-element.32), channel_id=1, source_target_pairs={{0,16},{8,24},{16,0},{24,8},{1,17},{9,25},{17,1},{25,9},{2,18},{10... | collective-permute-start | bytes 98312 | tf_op jit(solution)/shard_map/ppermute | solution.py:346
  21.9 4.7 %collective-permute-start.7 = (bf16[128,384]{1,0:T(8,128)(2,1)S(1)}, bf16[128,384]{1,0:T(8,128)(2,1)S(1)}, u32[]{:S(2)}, u32[]{:S(2)}) collective-permute-start(bf16[128,384]{1,0:T(8,128)(2,1)S(1)} %add_convert_fusion.3.refs_0_), channel_id=1, source_target_pairs={{0,8},{8,0},{16,24},{24,16},{1,9},{9,1},{17,25},{25,17},{2,10},{10... | collective-permute-start | bytes 294920 | tf_op jit(solution)/shard_map/ppermute | solution.py:346
  22.8 4.2 %collective-permute-start.10 = (bf16[128,128]{1,0:T(8,128)(2,1)S(1)}, bf16[128,128]{1,0:T(8,128)(2,1)S(1)}, u32[]{:S(2)}, u32[]{:S(2)}) collective-permute-start(bf16[128,128]{1,0:T(8,128)(2,1)S(1)} %add_convert_fusion.4.refs_3_), channel_id=1, source_target_pairs={{0,8},{8,0},{16,24},{24,16},{1,9},{9,1},{17,25},{25,17},{2,10},{10... | collective-permute-start | bytes 98312 | tf_op jit(solution)/shard_map/ppermute | solution.py:346
  26.6 1.6 %collective-permute-start.8 = (bf16[256,384]{1,0:T(8,128)(2,1)S(1)}, bf16[256,384]{1,0:T(8,128)(2,1)S(1)}, u32[]{:S(2)}, u32[]{:S(2)}) collective-permute-start(bf16[256,384]{1,0:T(8,128)(2,1)S(1)} %pad_maximum_fusion), channel_id=1, source_target_pairs={{0,2},{2,0},{1,3},{3,1},{4,6},{6,4},{5,7},{7,5},{8,10},{10,8},{9,1... | collective-permute-start | bytes 589832 | tf_op jit(solution)/shard_map/ppermute | solution.py:346
  26.9 1.3 %collective-permute-start.11 = (bf16[256,128]{1,0:T(8,128)(2,1)S(1)}, bf16[256,128]{1,0:T(8,128)(2,1)S(1)}, u32[]{:S(2)}, u32[]{:S(2)}) collective-permute-start(bf16[256,128]{1,0:T(8,128)(2,1)S(1)} %pad_maximum_fusion.1), channel_id=1, source_target_pairs={{0,2},{2,0},{1,3},{3,1},{4,6},{6,4},{5,7},{7,5},{8,10},{10,8},{9,1... | collective-permute-start | bytes 196616 | tf_op jit(solution)/shard_map/ppermute | solution.py:346
  34.4 4.0 %collective-permute-start.12 = (bf16[32,512]{1,0:T(8,128)(2,1)S(1)}, bf16[32,512]{1,0:T(8,128)(2,1)S(1)}, u32[]{:S(2)}, u32[]{:S(2)}) collective-permute-start(bf16[32,512]{1,0:T(8,128)(2,1)S(1)} %get-tuple-element.33.refs_3_), channel_id=1, source_target_pairs={{0,1},{1,0},{4,5},{5,4},{2,3},{3,2},{6,7},{7,6},{8,9},{9,8},{12,13... | collective-permute-start | bytes 98312 | tf_op jit(solution)/shard_map/ppermute | solution.py:396
  36.0 4.8 %collective-permute-start.14 = (bf16[32,512]{1,0:T(8,128)(2,1)S(1)}, bf16[32,512]{1,0:T(8,128)(2,1)S(1)}, u32[]{:S(2)}, u32[]{:S(2)}) collective-permute-start(bf16[32,512]{1,0:T(8,128)(2,1)S(1)} %get-tuple-element.34), channel_id=1, source_target_pairs={{0,5},{1,4},{4,1},{5,0},{2,7},{3,6},{6,3},{7,2},{8,13},{9,12},{12,... | collective-permute-start | bytes 98312 | tf_op jit(solution)/shard_map/ppermute | solution.py:396
  37.9 3.9 %collective-permute-start.13 = (bf16[32,512]{1,0:T(8,128)(2,1)S(1)}, bf16[32,512]{1,0:T(8,128)(2,1)S(1)}, u32[]{:S(2)}, u32[]{:S(2)}) collective-permute-start(bf16[32,512]{1,0:T(8,128)(2,1)S(1)} %get-tuple-element.34), channel_id=1, source_target_pairs={{0,4},{1,5},{4,0},{5,1},{2,6},{3,7},{6,2},{7,3},{8,12},{9,13},{12,... | collective-permute-start | bytes 98312 | tf_op jit(solution)/shard_map/ppermute | solution.py:396

commit v20 on v19

--- a/solution.py
+++ b/solution.py
@@ -395,7 +395,7 @@
         ]
         return lax.ppermute(send if flip else keep, ("x", "group"), moves)
 
-    others = [(turn, flip) for flip in (0, 1) for turn in range(groups) if turn or flip]
+    others = [(turn, flip) for turn in range(groups) for flip in range(2) if turn or flip]
     found = {(turn, flip): pass_on(turn, flip) for turn, flip in others}
     found[0, 0] = keep
     return place(found)

time: 42.7 us -> 42.2 us (0.988)
  waiting for transfers between devices: 18 us -> 17.4 us
    ppermute x3, waiting for transfers between devices: 3.85 us -> 3.27 us  [pass_on(): return lax.ppermute(send if flip else keep, ('x', 'group'), moves)]
  transfers between devices with their start and end apart: 15 -> 15, of which waited for: 9 -> 8; matrix products, arithmetic and copies ran while one was open for 0% -> 0% of each run, Pallas kernels for 2% -> 2%
where the time goes in v20:
time: 42.2 us; the launch traced here: 42 us
  waiting for transfers between devices  17.4 us (41%)
  starting transfers between devices  15 us (36%)
  Pallas kernels  9.35 us (22%)
    ppermute x11, waiting for transfers between devices, swap(): lax.ppermute(array, axis, [(i, i ^ mask) for i in range(lax.axis_size(axi...  14.1 us
    ppermute x11, starting transfers between devices, swap(): lax.ppermute(array, axis, [(i, i ^ mask) for i in range(lax.axis_size(axi...  11.1 us
    pallas_call x1, Pallas kernels, root(): pl.pallas_call(functools.partial(root_kernel, most), out_shape=[out, out]...  6.15 us
    ppermute x3, starting transfers between devices, pass_on(): return lax.ppermute(send if flip else keep, ('x', 'group'), moves)  3.69 us
    ppermute x3, waiting for transfers between devices, pass_on(): return lax.ppermute(send if flip else keep, ('x', 'group'), moves)  3.27 us
    pallas_call x1, Pallas kernels, load(): pl.pallas_call(functools.partial(load_kernel, scale), out_shape=[jax.Shap...  1.67 us
  transfers between devices with their start and end apart: 15, of which 8 were waited for; matrix products, arithmetic and copies ran while one was open for 0% of the time, Pallas kernels for 2%

profile of v20, /device:TPU:0, one launch (start us, length us, event | category | flops | bytes accessed | tf_op | source)
XLA Modules:
  0.0 42.0 jit_solution(6537581196188938777)
XLA Ops:
  0.0 1.7 %shard_map.37 = (bf16[128,512]{1,0:T(8,128)(2,1)S(1)}, bf16[128,512]{1,0:T(8,128)(2,1)S(1)}, bf16[2,2,512,256]{3,2,1,0:T(8,128)(2,1)S(1)}, bf16[2,512,512]{2,1,0:T(8,128)(2,1)S(1)}) custom-call(bf16[2,512,512]{2,1,0:T(8,128)(2,1)} %patch_hbm.1, bf16[2,512,512]{2,1,0:T(8,128)(2,1)} %cot_hbm.1), custom_call_target="tpu_custom_call" | custom-call | tf_op jit(solution)/shard_map/pallas_call | solution.py:70
  1.7 0.5 %collective-permute-start = (bf16[128,512]{1,0:T(8,128)(2,1)S(1)}, bf16[128,512]{1,0:T(8,128)(2,1)S(1)}, u32[]{:S(2)}, u32[]{:S(2)}) collective-permute-start(bf16[128,512]{1,0:T(8,128)(2,1)S(1)} %get-tuple-element.23), channel_id=1, source_target_pairs={{0,2},{2,0},{1,3},{3,1},{4,6},{6,4},{5,7},{7,5},{8,10},{10,8},{9,1... | collective-permute-start | bytes 393224 | tf_op jit(solution)/shard_map/ppermute | solution.py:346
  2.2 0.1 collective-permute-start.3
  2.3 0.5 %shard_map.38 = (f32[128,512]{1,0:T(8,128)S(1)}, f32[128,512]{1,0:T(8,128)S(1)}, bf16[256,512]{1,0:T(8,128)(2,1)S(1)}) custom-call(bf16[2,2,512,256]{3,2,1,0:T(8,128)(2,1)S(1)} %get-tuple-element.20.patch, bf16[2,512,512]{2,1,0:T(8,128)(2,1)S(1)} %get-tuple-element.21.cot), custom_call_target="tpu_custom_call" | custom-call | flops 402653184 | bytes 1048576 | tf_op jit(solution)/shard_map/pallas_call | solution.py:98
  2.7 0.5 %collective-permute-start.1 = (bf16[256,512]{1,0:T(8,128)(2,1)S(1)}, bf16[256,512]{1,0:T(8,128)(2,1)S(1)}, u32[]{:S(2)}, u32[]{:S(2)}) collective-permute-start(bf16[256,512]{1,0:T(8,128)(2,1)S(1)} %get-tuple-element.25), channel_id=1, source_target_pairs={{0,2},{2,0},{1,3},{3,1},{4,6},{6,4},{5,7},{7,5},{8,10},{10,8},{9,1... | collective-permute-start | bytes 786440 | tf_op jit(solution)/shard_map/ppermute | solution.py:346
  3.2 0.0 collective-permute-done
  3.3 2.9 %collective-permute-start.5 = (bf16[128,512]{1,0:T(8,128)(2,1)S(1)}, bf16[128,512]{1,0:T(8,128)(2,1)S(1)}, u32[]{:S(2)}, u32[]{:S(2)}) collective-permute-start(bf16[128,512]{1,0:T(8,128)(2,1)S(1)} %add_convert_fusion.2.refs_0_), channel_id=1, source_target_pairs={{0,8},{8,0},{16,24},{24,16},{1,9},{9,1},{17,25},{25,17},{2,10},{10... | collective-permute-start | bytes 393224 | tf_op jit(solution)/shard_map/ppermute | solution.py:346
  6.2 0.0 collective-permute-done.3
  6.3 1.6 %collective-permute-start.4 = (bf16[128,512]{1,0:T(8,128)(2,1)S(1)}, bf16[128,512]{1,0:T(8,128)(2,1)S(1)}, u32[]{:S(2)}, u32[]{:S(2)}) collective-permute-start(bf16[128,512]{1,0:T(8,128)(2,1)S(1)} %add_convert_fusion), channel_id=1, source_target_pairs={{0,4},{4,0},{1,5},{5,1},{2,6},{6,2},{3,7},{7,3},{8,12},{12,8},{9,1... | collective-permute-start | bytes 393224 | tf_op jit(solution)/shard_map/ppermute | solution.py:346
  7.8 0.3 shard_map.39
  8.1 0.0 collective-permute-done.1
  8.1 0.1 add_convert_fusion.1
  8.2 0.2 collective-permute-start.2
  8.4 1.7 %collective-permute-done.5.refs_2_ = bf16[128,512]{1,0:T(8,128)(2,1)S(1)} collective-permute-done((bf16[128,512]{1,0:T(8,128)(2,1)S(1)}, bf16[128,512]{1,0:T(8,128)(2,1)S(1)}, u32[]{:S(2)}, u32[]{:S(2)}) %collective-permute-start.5) | collective-permute-done | bytes 131104 | tf_op jit(solution)/shard_map/ppermute | solution.py:346
  10.1 4.4 %collective-permute-done.4.refs_1_ = bf16[128,512]{1,0:T(8,128)(2,1)S(1)} collective-permute-done((bf16[128,512]{1,0:T(8,128)(2,1)S(1)}, bf16[128,512]{1,0:T(8,128)(2,1)S(1)}, u32[]{:S(2)}, u32[]{:S(2)}) %collective-permute-start.4) | collective-permute-done | bytes 131104 | tf_op jit(solution)/shard_map/ppermute | solution.py:346
  14.5 0.0 collective-permute-done.2.refs_0_
  14.5 0.1 shard_map.40
  14.5 2.7 %collective-permute-start.6 = (bf16[128,384]{1,0:T(8,128)(2,1)S(1)}, bf16[128,384]{1,0:T(8,128)(2,1)S(1)}, u32[]{:S(2)}, u32[]{:S(2)}) collective-permute-start(bf16[128,384]{1,0:T(8,128)(2,1)S(1)} %get-tuple-element.30), channel_id=1, source_target_pairs={{0,16},{8,24},{16,0},{24,8},{1,17},{9,25},{17,1},{25,9},{2,18},{10... | collective-permute-start | bytes 294920 | tf_op jit(solution)/shard_map/ppermute | solution.py:346
  17.2 0.3 collective-permute-start.9
  17.5 4.4 %collective-permute-done.6 = bf16[128,384]{1,0:T(8,128)(2,1)S(1)} collective-permute-done((bf16[128,384]{1,0:T(8,128)(2,1)S(1)}, bf16[128,384]{1,0:T(8,128)(2,1)S(1)}, u32[]{:S(2)}, u32[]{:S(2)}) %collective-permute-start.6) | collective-permute-done | bytes 98336 | tf_op jit(solution)/shard_map/ppermute | solution.py:346
  21.9 0.8 %collective-permute-start.7 = (bf16[128,384]{1,0:T(8,128)(2,1)S(1)}, bf16[128,384]{1,0:T(8,128)(2,1)S(1)}, u32[]{:S(2)}, u32[]{:S(2)}) collective-permute-start(bf16[128,384]{1,0:T(8,128)(2,1)S(1)} %add_convert_fusion.3.refs_0_), channel_id=1, source_target_pairs={{0,8},{8,0},{16,24},{24,16},{1,9},{9,1},{17,25},{25,17},{2,10},{10... | collective-permute-start | bytes 294920 | tf_op jit(solution)/shard_map/ppermute | solution.py:346
  22.7 0.0 collective-permute-done.9
  22.8 1.3 %collective-permute-start.10 = (bf16[128,128]{1,0:T(8,128)(2,1)S(1)}, bf16[128,128]{1,0:T(8,128)(2,1)S(1)}, u32[]{:S(2)}, u32[]{:S(2)}) collective-permute-start(bf16[128,128]{1,0:T(8,128)(2,1)S(1)} %add_convert_fusion.4.refs_3_), channel_id=1, source_target_pairs={{0,8},{8,0},{16,24},{24,16},{1,9},{9,1},{17,25},{25,17},{2,10},{10... | collective-permute-start | bytes 98312 | tf_op jit(solution)/shard_map/ppermute | solution.py:346
  24.1 2.5 %collective-permute-done.7.refs_1_ = bf16[128,384]{1,0:T(8,128)(2,1)S(1)} collective-permute-done((bf16[128,384]{1,0:T(8,128)(2,1)S(1)}, bf16[128,384]{1,0:T(8,128)(2,1)S(1)}, u32[]{:S(2)}, u32[]{:S(2)}) %collective-permute-start.7) | collective-permute-done | bytes 98336 | tf_op jit(solution)/shard_map/ppermute | solution.py:346
  26.6 0.1 collective-permute-start.8
  26.7 0.2 collective-permute-done.10.refs_4_
  26.9 0.3 collective-permute-start.11
  27.3 0.9 %collective-permute-done.11.refs_5_ = bf16[256,128]{1,0:T(8,128)(2,1)S(1)} collective-permute-done((bf16[256,128]{1,0:T(8,128)(2,1)S(1)}, bf16[256,128]{1,0:T(8,128)(2,1)S(1)}, u32[]{:S(2)}, u32[]{:S(2)}) %collective-permute-start.11) | collective-permute-done | bytes 65568 | tf_op jit(solution)/shard_map/ppermute | solution.py:346
  28.2 0.0 collective-permute-done.8.refs_2_
  28.2 6.1 %shard_map.41 = (bf16[32,512]{1,0:T(8,128)(2,1)S(1)}, bf16[32,512]{1,0:T(8,128)(2,1)S(1)}) custom-call(s32[2,2]{1,0:T(2,128)} %counts_hbm.1, bf16[128,384]{1,0:T(8,128)(2,1)S(1)} %add_convert_fusion.3.refs_0_, bf16[128,384]{1,0:T(8,128)(2,1)S(1)} %collective-permute-done.7.refs_1_, bf16[256,384]{1,0:T(8,128)(2,1)S(1)} %collective-permute-done.8.refs_2_, ...), custom_call_target="tpu_custom_call" | custom-call | tf_op jit(solution)/shard_map/pallas_call | solution.py:293
  34.4 3.1 %collective-permute-start.14 = (bf16[32,512]{1,0:T(8,128)(2,1)S(1)}, bf16[32,512]{1,0:T(8,128)(2,1)S(1)}, u32[]{:S(2)}, u32[]{:S(2)}) collective-permute-start(bf16[32,512]{1,0:T(8,128)(2,1)S(1)} %get-tuple-element.33), channel_id=1, source_target_pairs={{0,5},{1,4},{4,1},{5,0},{2,7},{3,6},{6,3},{7,2},{8,13},{9,12},{12,... | collective-permute-start | bytes 98312 | tf_op jit(solution)/shard_map/ppermute | solution.py:396
  37.4 0.0 collective-permute-start.12
  37.4 0.6 %collective-permute-start.13 = (bf16[32,512]{1,0:T(8,128)(2,1)S(1)}, bf16[32,512]{1,0:T(8,128)(2,1)S(1)}, u32[]{:S(2)}, u32[]{:S(2)}) collective-permute-start(bf16[32,512]{1,0:T(8,128)(2,1)S(1)} %get-tuple-element.34.refs_3_), channel_id=1, source_target_pairs={{0,1},{1,0},{4,5},{5,4},{2,3},{3,2},{6,7},{7,6},{8,9},{9,8},{12,13... | collective-permute-start | bytes 98312 | tf_op jit(solution)/shard_map/ppermute | solution.py:396
  38.1 1.3 %collective-permute-done.14.refs_2_ = bf16[32,512]{1,0:T(8,128)(2,1)S(1)} collective-permute-done((bf16[32,512]{1,0:T(8,128)(2,1)S(1)}, bf16[32,512]{1,0:T(8,128)(2,1)S(1)}, u32[]{:S(2)}, u32[]{:S(2)}) %collective-permute-start.14) | collective-permute-done | bytes 32800 | tf_op jit(solution)/shard_map/ppermute | solution.py:396
  39.3 2.0 %collective-permute-done.12.refs_0_ = bf16[32,512]{1,0:T(8,128)(2,1)S(1)} collective-permute-done((bf16[32,512]{1,0:T(8,128)(2,1)S(1)}, bf16[32,512]{1,0:T(8,128)(2,1)S(1)}, u32[]{:S(2)}, u32[]{:S(2)}) %collective-permute-start.12) | collective-permute-done | bytes 32800 | tf_op jit(solution)/shard_map/ppermute | solution.py:396
  41.3 0.0 collective-permute-done.13.refs_1_
  41.3 0.7 %shard_map.42 = bf16[4,32,512]{2,1,0:T(8,128)(2,1)} custom-call(bf16[32,512]{1,0:T(8,128)(2,1)S(1)} %collective-permute-done.12.refs_0_, bf16[32,512]{1,0:T(8,128)(2,1)S(1)} %collective-permute-done.13.refs_1_, bf16[32,512]{1,0:T(8,128)(2,1)S(1)} %collective-permute-done.14.refs_2_, bf16[32,512]{1,0:T(8,128)(2,1)S(1)} %get-tuple-element.34.refs_3_), custom_call_target="tpu_custom_call" | custom-call | tf_op jit(solution)/shard_map/pallas_call | solution.py:329
  (6 shorter events, 0.1 us)
Async XLA Ops:
  1.7 1.6 %collective-permute-start = (bf16[128,512]{1,0:T(8,128)(2,1)S(1)}, bf16[128,512]{1,0:T(8,128)(2,1)S(1)}, u32[]{:S(2)}, u32[]{:S(2)}) collective-permute-start(bf16[128,512]{1,0:T(8,128)(2,1)S(1)} %get-tuple-element.23), channel_id=1, source_target_pairs={{0,2},{2,0},{1,3},{3,1},{4,6},{6,4},{5,7},{7,5},{8,10},{10,8},{9,1... | collective-permute-start | bytes 393224 | tf_op jit(solution)/shard_map/ppermute | solution.py:346
  2.2 4.0 %collective-permute-start.3 = (bf16[128,512]{1,0:T(8,128)(2,1)S(1)}, bf16[128,512]{1,0:T(8,128)(2,1)S(1)}, u32[]{:S(2)}, u32[]{:S(2)}) collective-permute-start(bf16[128,512]{1,0:T(8,128)(2,1)S(1)} %get-tuple-element.28), channel_id=1, source_target_pairs={{0,2},{2,0},{1,3},{3,1},{4,6},{6,4},{5,7},{7,5},{8,10},{10,8},{9,1... | collective-permute-start | bytes 393224 | tf_op jit(solution)/shard_map/ppermute | solution.py:346
  2.7 5.4 %collective-permute-start.1 = (bf16[256,512]{1,0:T(8,128)(2,1)S(1)}, bf16[256,512]{1,0:T(8,128)(2,1)S(1)}, u32[]{:S(2)}, u32[]{:S(2)}) collective-permute-start(bf16[256,512]{1,0:T(8,128)(2,1)S(1)} %get-tuple-element.25), channel_id=1, source_target_pairs={{0,2},{2,0},{1,3},{3,1},{4,6},{6,4},{5,7},{7,5},{8,10},{10,8},{9,1... | collective-permute-start | bytes 786440 | tf_op jit(solution)/shard_map/ppermute | solution.py:346
  3.3 6.8 %collective-permute-start.5 = (bf16[128,512]{1,0:T(8,128)(2,1)S(1)}, bf16[128,512]{1,0:T(8,128)(2,1)S(1)}, u32[]{:S(2)}, u32[]{:S(2)}) collective-permute-start(bf16[128,512]{1,0:T(8,128)(2,1)S(1)} %add_convert_fusion.2.refs_0_), channel_id=1, source_target_pairs={{0,8},{8,0},{16,24},{24,16},{1,9},{9,1},{17,25},{25,17},{2,10},{10... | collective-permute-start | bytes 393224 | tf_op jit(solution)/shard_map/ppermute | solution.py:346
  6.3 8.2 %collective-permute-start.4 = (bf16[128,512]{1,0:T(8,128)(2,1)S(1)}, bf16[128,512]{1,0:T(8,128)(2,1)S(1)}, u32[]{:S(2)}, u32[]{:S(2)}) collective-permute-start(bf16[128,512]{1,0:T(8,128)(2,1)S(1)} %add_convert_fusion), channel_id=1, source_target_pairs={{0,4},{4,0},{1,5},{5,1},{2,6},{6,2},{3,7},{7,3},{8,12},{12,8},{9,1... | collective-permute-start | bytes 393224 | tf_op jit(solution)/shard_map/ppermute | solution.py:346
  8.2 6.2 %collective-permute-start.2 = (bf16[128,512]{1,0:T(8,128)(2,1)S(1)}, bf16[128,512]{1,0:T(8,128)(2,1)S(1)}, u32[]{:S(2)}, u32[]{:S(2)}) collective-permute-start(bf16[128,512]{1,0:T(8,128)(2,1)S(1)} %get-tuple-element.35), channel_id=1, source_target_pairs={{0,12},{4,8},{8,4},{12,0},{16,28},{20,24},{24,20},{28,16},{1,13},{... | collective-permute-start | bytes 393224 | tf_op jit(solution)/shard_map/ppermute | solution.py:350
  14.5 7.3 %collective-permute-start.6 = (bf16[128,384]{1,0:T(8,128)(2,1)S(1)}, bf16[128,384]{1,0:T(8,128)(2,1)S(1)}, u32[]{:S(2)}, u32[]{:S(2)}) collective-permute-start(bf16[128,384]{1,0:T(8,128)(2,1)S(1)} %get-tuple-element.30), channel_id=1, source_target_pairs={{0,16},{8,24},{16,0},{24,8},{1,17},{9,25},{17,1},{25,9},{2,18},{10... | collective-permute-start | bytes 294920 | tf_op jit(solution)/shard_map/ppermute | solution.py:346
  17.2 5.6 %collective-permute-start.9 = (bf16[128,128]{1,0:T(8,128)(2,1)S(1)}, bf16[128,128]{1,0:T(8,128)(2,1)S(1)}, u32[]{:S(2)}, u32[]{:S(2)}) collective-permute-start(bf16[128,128]{1,0:T(8,128)(2,1)S(1)} %get-tuple-element.32), channel_id=1, source_target_pairs={{0,16},{8,24},{16,0},{24,8},{1,17},{9,25},{17,1},{25,9},{2,18},{10... | collective-permute-start | bytes 98312 | tf_op jit(solution)/shard_map/ppermute | solution.py:346
  21.9 4.7 %collective-permute-start.7 = (bf16[128,384]{1,0:T(8,128)(2,1)S(1)}, bf16[128,384]{1,0:T(8,128)(2,1)S(1)}, u32[]{:S(2)}, u32[]{:S(2)}) collective-permute-start(bf16[128,384]{1,0:T(8,128)(2,1)S(1)} %add_convert_fusion.3.refs_0_), channel_id=1, source_target_pairs={{0,8},{8,0},{16,24},{24,16},{1,9},{9,1},{17,25},{25,17},{2,10},{10... | collective-permute-start | bytes 294920 | tf_op jit(solution)/shard_map/ppermute | solution.py:346
  22.8 4.2 %collective-permute-start.10 = (bf16[128,128]{1,0:T(8,128)(2,1)S(1)}, bf16[128,128]{1,0:T(8,128)(2,1)S(1)}, u32[]{:S(2)}, u32[]{:S(2)}) collective-permute-start(bf16[128,128]{1,0:T(8,128)(2,1)S(1)} %add_convert_fusion.4.refs_3_), channel_id=1, source_target_pairs={{0,8},{8,0},{16,24},{24,16},{1,9},{9,1},{17,25},{25,17},{2,10},{10... | collective-permute-start | bytes 98312 | tf_op jit(solution)/shard_map/ppermute | solution.py:346
  26.6 1.6 %collective-permute-start.8 = (bf16[256,384]{1,0:T(8,128)(2,1)S(1)}, bf16[256,384]{1,0:T(8,128)(2,1)S(1)}, u32[]{:S(2)}, u32[]{:S(2)}) collective-permute-start(bf16[256,384]{1,0:T(8,128)(2,1)S(1)} %pad_maximum_fusion), channel_id=1, source_target_pairs={{0,2},{2,0},{1,3},{3,1},{4,6},{6,4},{5,7},{7,5},{8,10},{10,8},{9,1... | collective-permute-start | bytes 589832 | tf_op jit(solution)/shard_map/ppermute | solution.py:346
  26.9 1.3 %collective-permute-start.11 = (bf16[256,128]{1,0:T(8,128)(2,1)S(1)}, bf16[256,128]{1,0:T(8,128)(2,1)S(1)}, u32[]{:S(2)}, u32[]{:S(2)}) collective-permute-start(bf16[256,128]{1,0:T(8,128)(2,1)S(1)} %pad_maximum_fusion.1), channel_id=1, source_target_pairs={{0,2},{2,0},{1,3},{3,1},{4,6},{6,4},{5,7},{7,5},{8,10},{10,8},{9,1... | collective-permute-start | bytes 196616 | tf_op jit(solution)/shard_map/ppermute | solution.py:346
  34.4 4.9 %collective-permute-start.14 = (bf16[32,512]{1,0:T(8,128)(2,1)S(1)}, bf16[32,512]{1,0:T(8,128)(2,1)S(1)}, u32[]{:S(2)}, u32[]{:S(2)}) collective-permute-start(bf16[32,512]{1,0:T(8,128)(2,1)S(1)} %get-tuple-element.33), channel_id=1, source_target_pairs={{0,5},{1,4},{4,1},{5,0},{2,7},{3,6},{6,3},{7,2},{8,13},{9,12},{12,... | collective-permute-start | bytes 98312 | tf_op jit(solution)/shard_map/ppermute | solution.py:396
  37.4 3.9 %collective-permute-start.12 = (bf16[32,512]{1,0:T(8,128)(2,1)S(1)}, bf16[32,512]{1,0:T(8,128)(2,1)S(1)}, u32[]{:S(2)}, u32[]{:S(2)}) collective-permute-start(bf16[32,512]{1,0:T(8,128)(2,1)S(1)} %get-tuple-element.33), channel_id=1, source_target_pairs={{0,4},{1,5},{4,0},{5,1},{2,6},{3,7},{6,2},{7,3},{8,12},{9,13},{12,... | collective-permute-start | bytes 98312 | tf_op jit(solution)/shard_map/ppermute | solution.py:396
  37.4 3.9 %collective-permute-start.13 = (bf16[32,512]{1,0:T(8,128)(2,1)S(1)}, bf16[32,512]{1,0:T(8,128)(2,1)S(1)}, u32[]{:S(2)}, u32[]{:S(2)}) collective-permute-start(bf16[32,512]{1,0:T(8,128)(2,1)S(1)} %get-tuple-element.34.refs_3_), channel_id=1, source_target_pairs={{0,1},{1,0},{4,5},{5,4},{2,3},{3,2},{6,7},{7,6},{8,9},{9,8},{12,13... | collective-permute-start | bytes 98312 | tf_op jit(solution)/shard_map/ppermute | solution.py:396

commit v21 on v20

--- a/solution.py
+++ b/solution.py
@@ -366,7 +366,7 @@
     to_line = add(kept_line, came_line).astype(BF16)
     from_line = swap(to_line, "z")
     kept_diagonal, own = sums(
-        scale, patch, cot, (to_line,), (F32, ((1, 0, 1),)), (F32, ((0, 0, 0),))
+        scale, patch, cot, (to_column,), (F32, ((1, 0, 1),)), (F32, ((0, 0, 0),))
     )
     quarter = own.shape[0]
     to_diagonal = add(kept_diagonal, came_rest[:quarter]).astype(BF16)

time: 42.2 us -> 42.2 us (level)
    ppermute x1, waiting for transfers between devices: 0.01 us -> 1.68 us  [swap_diagonal(): return lax.ppermute(array, ('z', 'x'), moves)]
    ppermute x11, waiting for transfers between devices: 14.1 us -> 12.5 us  [swap(): lax.ppermute(array, axis, [(i, i ^ mask) for i in range(lax.axis_size(axi...]
  transfers between devices with their start and end apart: 15 -> 15, of which waited for: 8 -> 10; matrix products, arithmetic and copies ran while one was open for 0% -> 0% of each run, Pallas kernels for 2% -> 2%
where the time goes in v21:
time: 42.2 us; the launch traced here: 42.1 us
  waiting for transfers between devices  17.6 us (42%)
  starting transfers between devices  14.9 us (35%)
  Pallas kernels  9.35 us (22%)
    ppermute x11, waiting for transfers between devices, swap(): lax.ppermute(array, axis, [(i, i ^ mask) for i in range(lax.axis_size(axi...  12.5 us
    ppermute x11, starting transfers between devices, swap(): lax.ppermute(array, axis, [(i, i ^ mask) for i in range(lax.axis_size(axi...  11.1 us
    pallas_call x1, Pallas kernels, root(): pl.pallas_call(functools.partial(root_kernel, most), out_shape=[out, out]...  6.15 us
    ppermute x3, starting transfers between devices, pass_on(): return lax.ppermute(send if flip else keep, ('x', 'group'), moves)  3.55 us
    ppermute x3, waiting for transfers between devices, pass_on(): return lax.ppermute(send if flip else keep, ('x', 'group'), moves)  3.41 us
    ppermute x1, waiting for transfers between devices, swap_diagonal(): return lax.ppermute(array, ('z', 'x'), moves)  1.68 us
    pallas_call x1, Pallas kernels, load(): pl.pallas_call(functools.partial(load_kernel, scale), out_shape=[jax.Shap...  1.67 us
  transfers between devices with their start and end apart: 15, of which 10 were waited for; matrix products, arithmetic and copies ran while one was open for 0% of the time, Pallas kernels for 2%

profile of v21, /device:TPU:0, one launch (start us, length us, event | category | flops | bytes accessed | tf_op | source)
XLA Modules:
  0.0 42.1 jit_solution(9145749461368784082)
XLA Ops:
  0.0 1.7 %shard_map.37 = (bf16[128,512]{1,0:T(8,128)(2,1)S(1)}, bf16[128,512]{1,0:T(8,128)(2,1)S(1)}, bf16[2,2,512,256]{3,2,1,0:T(8,128)(2,1)S(1)}, bf16[2,512,512]{2,1,0:T(8,128)(2,1)S(1)}) custom-call(bf16[2,512,512]{2,1,0:T(8,128)(2,1)} %patch_hbm.1, bf16[2,512,512]{2,1,0:T(8,128)(2,1)} %cot_hbm.1), custom_call_target="tpu_custom_call" | custom-call | tf_op jit(solution)/shard_map/pallas_call | solution.py:70
  1.7 0.5 %collective-permute-start = (bf16[128,512]{1,0:T(8,128)(2,1)S(1)}, bf16[128,512]{1,0:T(8,128)(2,1)S(1)}, u32[]{:S(2)}, u32[]{:S(2)}) collective-permute-start(bf16[128,512]{1,0:T(8,128)(2,1)S(1)} %get-tuple-element.23), channel_id=1, source_target_pairs={{0,2},{2,0},{1,3},{3,1},{4,6},{6,4},{5,7},{7,5},{8,10},{10,8},{9,1... | collective-permute-start | bytes 393224 | tf_op jit(solution)/shard_map/ppermute | solution.py:346
  2.2 0.1 collective-permute-start.4
  2.3 0.5 %shard_map.38 = (f32[128,512]{1,0:T(8,128)S(1)}, f32[128,512]{1,0:T(8,128)S(1)}, bf16[256,512]{1,0:T(8,128)(2,1)S(1)}) custom-call(bf16[2,2,512,256]{3,2,1,0:T(8,128)(2,1)S(1)} %get-tuple-element.20.patch, bf16[2,512,512]{2,1,0:T(8,128)(2,1)S(1)} %get-tuple-element.21.cot), custom_call_target="tpu_custom_call" | custom-call | flops 402653184 | bytes 1048576 | tf_op jit(solution)/shard_map/pallas_call | solution.py:98
  2.7 0.5 %collective-permute-start.1 = (bf16[256,512]{1,0:T(8,128)(2,1)S(1)}, bf16[256,512]{1,0:T(8,128)(2,1)S(1)}, u32[]{:S(2)}, u32[]{:S(2)}) collective-permute-start(bf16[256,512]{1,0:T(8,128)(2,1)S(1)} %get-tuple-element.25), channel_id=1, source_target_pairs={{0,2},{2,0},{1,3},{3,1},{4,6},{6,4},{5,7},{7,5},{8,10},{10,8},{9,1... | collective-permute-start | bytes 786440 | tf_op jit(solution)/shard_map/ppermute | solution.py:346
  3.2 0.0 collective-permute-done
  3.3 2.9 %collective-permute-start.3 = (bf16[128,512]{1,0:T(8,128)(2,1)S(1)}, bf16[128,512]{1,0:T(8,128)(2,1)S(1)}, u32[]{:S(2)}, u32[]{:S(2)}) collective-permute-start(bf16[128,512]{1,0:T(8,128)(2,1)S(1)} %add_convert_fusion.2.refs_0_), channel_id=1, source_target_pairs={{0,4},{4,0},{1,5},{5,1},{2,6},{6,2},{3,7},{7,3},{8,12},{12,8},{9,1... | collective-permute-start | bytes 393224 | tf_op jit(solution)/shard_map/ppermute | solution.py:346
  6.1 0.0 collective-permute-done.4
  6.2 1.6 %collective-permute-start.5 = (bf16[128,512]{1,0:T(8,128)(2,1)S(1)}, bf16[128,512]{1,0:T(8,128)(2,1)S(1)}, u32[]{:S(2)}, u32[]{:S(2)}) collective-permute-start(bf16[128,512]{1,0:T(8,128)(2,1)S(1)} %add_convert_fusion), channel_id=1, source_target_pairs={{0,8},{8,0},{16,24},{24,16},{1,9},{9,1},{17,25},{25,17},{2,10},{10... | collective-permute-start | bytes 393224 | tf_op jit(solution)/shard_map/ppermute | solution.py:346
  7.8 0.3 shard_map.39
  8.1 0.0 collective-permute-done.1
  8.1 0.1 add_convert_fusion.1
  8.2 0.2 collective-permute-start.2
  8.4 1.6 %collective-permute-done.3.refs_1_ = bf16[128,512]{1,0:T(8,128)(2,1)S(1)} collective-permute-done((bf16[128,512]{1,0:T(8,128)(2,1)S(1)}, bf16[128,512]{1,0:T(8,128)(2,1)S(1)}, u32[]{:S(2)}, u32[]{:S(2)}) %collective-permute-start.3) | collective-permute-done | bytes 131104 | tf_op jit(solution)/shard_map/ppermute | solution.py:346
  10.0 2.6 %collective-permute-done.5.refs_2_ = bf16[128,512]{1,0:T(8,128)(2,1)S(1)} collective-permute-done((bf16[128,512]{1,0:T(8,128)(2,1)S(1)}, bf16[128,512]{1,0:T(8,128)(2,1)S(1)}, u32[]{:S(2)}, u32[]{:S(2)}) %collective-permute-start.5) | collective-permute-done | bytes 131104 | tf_op jit(solution)/shard_map/ppermute | solution.py:346
  12.6 1.7 %collective-permute-done.2.refs_0_ = bf16[128,512]{1,0:T(8,128)(2,1)S(1)} collective-permute-done((bf16[128,512]{1,0:T(8,128)(2,1)S(1)}, bf16[128,512]{1,0:T(8,128)(2,1)S(1)}, u32[]{:S(2)}, u32[]{:S(2)}) %collective-permute-start.2) | collective-permute-done | bytes 131104 | tf_op jit(solution)/shard_map/ppermute | solution.py:350
  14.3 0.1 shard_map.40
  14.4 2.7 %collective-permute-start.6 = (bf16[128,384]{1,0:T(8,128)(2,1)S(1)}, bf16[128,384]{1,0:T(8,128)(2,1)S(1)}, u32[]{:S(2)}, u32[]{:S(2)}) collective-permute-start(bf16[128,384]{1,0:T(8,128)(2,1)S(1)} %get-tuple-element.30), channel_id=1, source_target_pairs={{0,16},{8,24},{16,0},{24,8},{1,17},{9,25},{17,1},{25,9},{2,18},{10... | collective-permute-start | bytes 294920 | tf_op jit(solution)/shard_map/ppermute | solution.py:346
  17.1 0.3 collective-permute-start.9
  17.3 4.6 %collective-permute-done.6 = bf16[128,384]{1,0:T(8,128)(2,1)S(1)} collective-permute-done((bf16[128,384]{1,0:T(8,128)(2,1)S(1)}, bf16[128,384]{1,0:T(8,128)(2,1)S(1)}, u32[]{:S(2)}, u32[]{:S(2)}) %collective-permute-start.6) | collective-permute-done | bytes 98336 | tf_op jit(solution)/shard_map/ppermute | solution.py:346
  21.9 0.9 %collective-permute-start.7 = (bf16[128,384]{1,0:T(8,128)(2,1)S(1)}, bf16[128,384]{1,0:T(8,128)(2,1)S(1)}, u32[]{:S(2)}, u32[]{:S(2)}) collective-permute-start(bf16[128,384]{1,0:T(8,128)(2,1)S(1)} %add_convert_fusion.3.refs_0_), channel_id=1, source_target_pairs={{0,8},{8,0},{16,24},{24,16},{1,9},{9,1},{17,25},{25,17},{2,10},{10... | collective-permute-start | bytes 294920 | tf_op jit(solution)/shard_map/ppermute | solution.py:346
  22.9 0.0 collective-permute-done.9
  22.9 1.2 %collective-permute-start.10 = (bf16[128,128]{1,0:T(8,128)(2,1)S(1)}, bf16[128,128]{1,0:T(8,128)(2,1)S(1)}, u32[]{:S(2)}, u32[]{:S(2)}) collective-permute-start(bf16[128,128]{1,0:T(8,128)(2,1)S(1)} %add_convert_fusion.4.refs_3_), channel_id=1, source_target_pairs={{0,8},{8,0},{16,24},{24,16},{1,9},{9,1},{17,25},{25,17},{2,10},{10... | collective-permute-start | bytes 98312 | tf_op jit(solution)/shard_map/ppermute | solution.py:346
  24.1 2.5 %collective-permute-done.7.refs_1_ = bf16[128,384]{1,0:T(8,128)(2,1)S(1)} collective-permute-done((bf16[128,384]{1,0:T(8,128)(2,1)S(1)}, bf16[128,384]{1,0:T(8,128)(2,1)S(1)}, u32[]{:S(2)}, u32[]{:S(2)}) %collective-permute-start.7) | collective-permute-done | bytes 98336 | tf_op jit(solution)/shard_map/ppermute | solution.py:346
  26.6 0.1 collective-permute-start.8
  26.7 0.2 collective-permute-done.10.refs_4_
  27.0 0.3 collective-permute-start.11
  27.3 0.9 %collective-permute-done.11.refs_5_ = bf16[256,128]{1,0:T(8,128)(2,1)S(1)} collective-permute-done((bf16[256,128]{1,0:T(8,128)(2,1)S(1)}, bf16[256,128]{1,0:T(8,128)(2,1)S(1)}, u32[]{:S(2)}, u32[]{:S(2)}) %collective-permute-start.11) | collective-permute-done | bytes 65568 | tf_op jit(solution)/shard_map/ppermute | solution.py:346
  28.3 0.0 collective-permute-done.8.refs_2_
  28.3 6.1 %shard_map.41 = (bf16[32,512]{1,0:T(8,128)(2,1)S(1)}, bf16[32,512]{1,0:T(8,128)(2,1)S(1)}) custom-call(s32[2,2]{1,0:T(2,128)} %counts_hbm.1, bf16[128,384]{1,0:T(8,128)(2,1)S(1)} %add_convert_fusion.3.refs_0_, bf16[128,384]{1,0:T(8,128)(2,1)S(1)} %collective-permute-done.7.refs_1_, bf16[256,384]{1,0:T(8,128)(2,1)S(1)} %collective-permute-done.8.refs_2_, ...), custom_call_target="tpu_custom_call" | custom-call | tf_op jit(solution)/shard_map/pallas_call | solution.py:293
  34.4 2.6 %collective-permute-start.14 = (bf16[32,512]{1,0:T(8,128)(2,1)S(1)}, bf16[32,512]{1,0:T(8,128)(2,1)S(1)}, u32[]{:S(2)}, u32[]{:S(2)}) collective-permute-start(bf16[32,512]{1,0:T(8,128)(2,1)S(1)} %get-tuple-element.33), channel_id=1, source_target_pairs={{0,5},{1,4},{4,1},{5,0},{2,7},{3,6},{6,3},{7,2},{8,13},{9,12},{12,... | collective-permute-start | bytes 98312 | tf_op jit(solution)/shard_map/ppermute | solution.py:396
  37.0 0.5 %collective-permute-start.12 = (bf16[32,512]{1,0:T(8,128)(2,1)S(1)}, bf16[32,512]{1,0:T(8,128)(2,1)S(1)}, u32[]{:S(2)}, u32[]{:S(2)}) collective-permute-start(bf16[32,512]{1,0:T(8,128)(2,1)S(1)} %get-tuple-element.33), channel_id=1, source_target_pairs={{0,4},{1,5},{4,0},{5,1},{2,6},{3,7},{6,2},{7,3},{8,12},{9,13},{12,... | collective-permute-start | bytes 98312 | tf_op jit(solution)/shard_map/ppermute | solution.py:396
  37.5 0.5 %collective-permute-start.13 = (bf16[32,512]{1,0:T(8,128)(2,1)S(1)}, bf16[32,512]{1,0:T(8,128)(2,1)S(1)}, u32[]{:S(2)}, u32[]{:S(2)}) collective-permute-start(bf16[32,512]{1,0:T(8,128)(2,1)S(1)} %get-tuple-element.34.refs_3_), channel_id=1, source_target_pairs={{0,1},{1,0},{4,5},{5,4},{2,3},{3,2},{6,7},{7,6},{8,9},{9,8},{12,13... | collective-permute-start | bytes 98312 | tf_op jit(solution)/shard_map/ppermute | solution.py:396
  38.0 1.3 %collective-permute-done.14.refs_2_ = bf16[32,512]{1,0:T(8,128)(2,1)S(1)} collective-permute-done((bf16[32,512]{1,0:T(8,128)(2,1)S(1)}, bf16[32,512]{1,0:T(8,128)(2,1)S(1)}, u32[]{:S(2)}, u32[]{:S(2)}) %collective-permute-start.14) | collective-permute-done | bytes 32800 | tf_op jit(solution)/shard_map/ppermute | solution.py:396
  39.3 1.6 %collective-permute-done.12.refs_0_ = bf16[32,512]{1,0:T(8,128)(2,1)S(1)} collective-permute-done((bf16[32,512]{1,0:T(8,128)(2,1)S(1)}, bf16[32,512]{1,0:T(8,128)(2,1)S(1)}, u32[]{:S(2)}, u32[]{:S(2)}) %collective-permute-start.12) | collective-permute-done | bytes 32800 | tf_op jit(solution)/shard_map/ppermute | solution.py:396
  40.9 0.5 %collective-permute-done.13.refs_1_ = bf16[32,512]{1,0:T(8,128)(2,1)S(1)} collective-permute-done((bf16[32,512]{1,0:T(8,128)(2,1)S(1)}, bf16[32,512]{1,0:T(8,128)(2,1)S(1)}, u32[]{:S(2)}, u32[]{:S(2)}) %collective-permute-start.13) | collective-permute-done | bytes 32800 | tf_op jit(solution)/shard_map/ppermute | solution.py:396
  41.4 0.7 %shard_map.42 = bf16[4,32,512]{2,1,0:T(8,128)(2,1)} custom-call(bf16[32,512]{1,0:T(8,128)(2,1)S(1)} %collective-permute-done.12.refs_0_, bf16[32,512]{1,0:T(8,128)(2,1)S(1)} %collective-permute-done.13.refs_1_, bf16[32,512]{1,0:T(8,128)(2,1)S(1)} %collective-permute-done.14.refs_2_, bf16[32,512]{1,0:T(8,128)(2,1)S(1)} %get-tuple-element.34.refs_3_), custom_call_target="tpu_custom_call" | custom-call | tf_op jit(solution)/shard_map/pallas_call | solution.py:329
  (6 shorter events, 0.1 us)
Async XLA Ops:
  1.7 1.6 %collective-permute-start = (bf16[128,512]{1,0:T(8,128)(2,1)S(1)}, bf16[128,512]{1,0:T(8,128)(2,1)S(1)}, u32[]{:S(2)}, u32[]{:S(2)}) collective-permute-start(bf16[128,512]{1,0:T(8,128)(2,1)S(1)} %get-tuple-element.23), channel_id=1, source_target_pairs={{0,2},{2,0},{1,3},{3,1},{4,6},{6,4},{5,7},{7,5},{8,10},{10,8},{9,1... | collective-permute-start | bytes 393224 | tf_op jit(solution)/shard_map/ppermute | solution.py:346
  2.2 3.9 %collective-permute-start.4 = (bf16[128,512]{1,0:T(8,128)(2,1)S(1)}, bf16[128,512]{1,0:T(8,128)(2,1)S(1)}, u32[]{:S(2)}, u32[]{:S(2)}) collective-permute-start(bf16[128,512]{1,0:T(8,128)(2,1)S(1)} %get-tuple-element.28), channel_id=1, source_target_pairs={{0,2},{2,0},{1,3},{3,1},{4,6},{6,4},{5,7},{7,5},{8,10},{10,8},{9,1... | collective-permute-start | bytes 393224 | tf_op jit(solution)/shard_map/ppermute | solution.py:346
  2.7 5.4 %collective-permute-start.1 = (bf16[256,512]{1,0:T(8,128)(2,1)S(1)}, bf16[256,512]{1,0:T(8,128)(2,1)S(1)}, u32[]{:S(2)}, u32[]{:S(2)}) collective-permute-start(bf16[256,512]{1,0:T(8,128)(2,1)S(1)} %get-tuple-element.25), channel_id=1, source_target_pairs={{0,2},{2,0},{1,3},{3,1},{4,6},{6,4},{5,7},{7,5},{8,10},{10,8},{9,1... | collective-permute-start | bytes 786440 | tf_op jit(solution)/shard_map/ppermute | solution.py:346
  3.3 6.7 %collective-permute-start.3 = (bf16[128,512]{1,0:T(8,128)(2,1)S(1)}, bf16[128,512]{1,0:T(8,128)(2,1)S(1)}, u32[]{:S(2)}, u32[]{:S(2)}) collective-permute-start(bf16[128,512]{1,0:T(8,128)(2,1)S(1)} %add_convert_fusion.2.refs_0_), channel_id=1, source_target_pairs={{0,4},{4,0},{1,5},{5,1},{2,6},{6,2},{3,7},{7,3},{8,12},{12,8},{9,1... | collective-permute-start | bytes 393224 | tf_op jit(solution)/shard_map/ppermute | solution.py:346
  6.2 6.4 %collective-permute-start.5 = (bf16[128,512]{1,0:T(8,128)(2,1)S(1)}, bf16[128,512]{1,0:T(8,128)(2,1)S(1)}, u32[]{:S(2)}, u32[]{:S(2)}) collective-permute-start(bf16[128,512]{1,0:T(8,128)(2,1)S(1)} %add_convert_fusion), channel_id=1, source_target_pairs={{0,8},{8,0},{16,24},{24,16},{1,9},{9,1},{17,25},{25,17},{2,10},{10... | collective-permute-start | bytes 393224 | tf_op jit(solution)/shard_map/ppermute | solution.py:346
  8.2 6.1 %collective-permute-start.2 = (bf16[128,512]{1,0:T(8,128)(2,1)S(1)}, bf16[128,512]{1,0:T(8,128)(2,1)S(1)}, u32[]{:S(2)}, u32[]{:S(2)}) collective-permute-start(bf16[128,512]{1,0:T(8,128)(2,1)S(1)} %get-tuple-element.35), channel_id=1, source_target_pairs={{0,12},{4,8},{8,4},{12,0},{16,28},{20,24},{24,20},{28,16},{1,13},{... | collective-permute-start | bytes 393224 | tf_op jit(solution)/shard_map/ppermute | solution.py:350
  14.4 7.6 %collective-permute-start.6 = (bf16[128,384]{1,0:T(8,128)(2,1)S(1)}, bf16[128,384]{1,0:T(8,128)(2,1)S(1)}, u32[]{:S(2)}, u32[]{:S(2)}) collective-permute-start(bf16[128,384]{1,0:T(8,128)(2,1)S(1)} %get-tuple-element.30), channel_id=1, source_target_pairs={{0,16},{8,24},{16,0},{24,8},{1,17},{9,25},{17,1},{25,9},{2,18},{10... | collective-permute-start | bytes 294920 | tf_op jit(solution)/shard_map/ppermute | solution.py:346
  17.1 5.8 %collective-permute-start.9 = (bf16[128,128]{1,0:T(8,128)(2,1)S(1)}, bf16[128,128]{1,0:T(8,128)(2,1)S(1)}, u32[]{:S(2)}, u32[]{:S(2)}) collective-permute-start(bf16[128,128]{1,0:T(8,128)(2,1)S(1)} %get-tuple-element.32), channel_id=1, source_target_pairs={{0,16},{8,24},{16,0},{24,8},{1,17},{9,25},{17,1},{25,9},{2,18},{10... | collective-permute-start | bytes 98312 | tf_op jit(solution)/shard_map/ppermute | solution.py:346
  21.9 4.7 %collective-permute-start.7 = (bf16[128,384]{1,0:T(8,128)(2,1)S(1)}, bf16[128,384]{1,0:T(8,128)(2,1)S(1)}, u32[]{:S(2)}, u32[]{:S(2)}) collective-permute-start(bf16[128,384]{1,0:T(8,128)(2,1)S(1)} %add_convert_fusion.3.refs_0_), channel_id=1, source_target_pairs={{0,8},{8,0},{16,24},{24,16},{1,9},{9,1},{17,25},{25,17},{2,10},{10... | collective-permute-start | bytes 294920 | tf_op jit(solution)/shard_map/ppermute | solution.py:346
  22.9 4.1 %collective-permute-start.10 = (bf16[128,128]{1,0:T(8,128)(2,1)S(1)}, bf16[128,128]{1,0:T(8,128)(2,1)S(1)}, u32[]{:S(2)}, u32[]{:S(2)}) collective-permute-start(bf16[128,128]{1,0:T(8,128)(2,1)S(1)} %add_convert_fusion.4.refs_3_), channel_id=1, source_target_pairs={{0,8},{8,0},{16,24},{24,16},{1,9},{9,1},{17,25},{25,17},{2,10},{10... | collective-permute-start | bytes 98312 | tf_op jit(solution)/shard_map/ppermute | solution.py:346
  26.6 1.6 %collective-permute-start.8 = (bf16[256,384]{1,0:T(8,128)(2,1)S(1)}, bf16[256,384]{1,0:T(8,128)(2,1)S(1)}, u32[]{:S(2)}, u32[]{:S(2)}) collective-permute-start(bf16[256,384]{1,0:T(8,128)(2,1)S(1)} %pad_maximum_fusion), channel_id=1, source_target_pairs={{0,2},{2,0},{1,3},{3,1},{4,6},{6,4},{5,7},{7,5},{8,10},{10,8},{9,1... | collective-permute-start | bytes 589832 | tf_op jit(solution)/shard_map/ppermute | solution.py:346
  27.0 1.3 %collective-permute-start.11 = (bf16[256,128]{1,0:T(8,128)(2,1)S(1)}, bf16[256,128]{1,0:T(8,128)(2,1)S(1)}, u32[]{:S(2)}, u32[]{:S(2)}) collective-permute-start(bf16[256,128]{1,0:T(8,128)(2,1)S(1)} %pad_maximum_fusion.1), channel_id=1, source_target_pairs={{0,2},{2,0},{1,3},{3,1},{4,6},{6,4},{5,7},{7,5},{8,10},{10,8},{9,1... | collective-permute-start | bytes 196616 | tf_op jit(solution)/shard_map/ppermute | solution.py:346
  34.4 4.9 %collective-permute-start.14 = (bf16[32,512]{1,0:T(8,128)(2,1)S(1)}, bf16[32,512]{1,0:T(8,128)(2,1)S(1)}, u32[]{:S(2)}, u32[]{:S(2)}) collective-permute-start(bf16[32,512]{1,0:T(8,128)(2,1)S(1)} %get-tuple-element.33), channel_id=1, source_target_pairs={{0,5},{1,4},{4,1},{5,0},{2,7},{3,6},{6,3},{7,2},{8,13},{9,12},{12,... | collective-permute-start | bytes 98312 | tf_op jit(solution)/shard_map/ppermute | solution.py:396
  37.0 3.9 %collective-permute-start.12 = (bf16[32,512]{1,0:T(8,128)(2,1)S(1)}, bf16[32,512]{1,0:T(8,128)(2,1)S(1)}, u32[]{:S(2)}, u32[]{:S(2)}) collective-permute-start(bf16[32,512]{1,0:T(8,128)(2,1)S(1)} %get-tuple-element.33), channel_id=1, source_target_pairs={{0,4},{1,5},{4,0},{5,1},{2,6},{3,7},{6,2},{7,3},{8,12},{9,13},{12,... | collective-permute-start | bytes 98312 | tf_op jit(solution)/shard_map/ppermute | solution.py:396
  37.5 3.9 %collective-permute-start.13 = (bf16[32,512]{1,0:T(8,128)(2,1)S(1)}, bf16[32,512]{1,0:T(8,128)(2,1)S(1)}, u32[]{:S(2)}, u32[]{:S(2)}) collective-permute-start(bf16[32,512]{1,0:T(8,128)(2,1)S(1)} %get-tuple-element.34.refs_3_), channel_id=1, source_target_pairs={{0,1},{1,0},{4,5},{5,4},{2,3},{3,2},{6,7},{7,6},{8,9},{9,8},{12,13... | collective-permute-start | bytes 98312 | tf_op jit(solution)/shard_map/ppermute | solution.py:396

commit v22 on v20

--- a/solution.py
+++ b/solution.py
@@ -230,8 +230,9 @@
     for index in range(1, most):
         q_left, q_right = left.at[picked:, :], right.at[width:, :]
         if index == 1:
-            fill(s_left, 0, square(q_left))
-            fill(s_right, 0, square(q_right))
+            seconds = square(q_left), square(q_right)
+            fill(s_left, 0, seconds[0])
+            fill(s_right, 0, seconds[1])
         else:
             by_high = dot(left[...], q_left[:, high])
             by_low = dot(left[: picked + half, :], q_left[:, low])
@@ -259,15 +260,16 @@
         fourths = square(s_left), square(s_right)
         fill(s_left, 0, fourths[0])
         fill(s_right, 0, fourths[1])
-        for fourth, moment_ref, ref, start in (
-            (s_left, m_left, left, picked),
-            (s_right, m_right, right, width),
-        ):
+        moments = []
+        for fourth, moment_ref in ((s_left, m_left), (s_right, m_right)):
             by_high = dot(fourth[...], moment_ref[:, high])
-            tiles = (dot(fourth[low, :], moment_ref[:, low]), by_high[low], by_high[high])
-            if index < most - 1:
-                fill(moment_ref, 0, tiles)
-            fill(ref, start, factor(tiles))
+            by_low = dot(fourth[low, :], moment_ref[:, low])
+            moments.append((by_low, by_high[low], by_high[high]))
+        fill(left, picked, factor(moments[0]))
+        fill(right, width, factor(moments[1]))
+        if index < most - 1:
+            fill(m_left, 0, moments[0])
+            fill(m_right, 0, moments[1])
     final_left = dot(left[:picked, :], left[picked:, :]).astype(BF16)
     final_left = jnp.where(most <= count_left, final_left, left[:picked, :])
     by_high = dot(right[:width, :], right[width:, high])

time: 42.2 us -> 42.2 us (level)
  no operation moved by 1% of the time
where the time goes in v22:
time: 42.2 us; the launch traced here: 42 us
  waiting for transfers between devices  17.4 us (41%)
  starting transfers between devices  15 us (36%)
  Pallas kernels  9.35 us (22%)
    ppermute x11, waiting for transfers between devices, swap(): lax.ppermute(array, axis, [(i, i ^ mask) for i in range(lax.axis_size(axi...  14.1 us
    ppermute x11, starting transfers between devices, swap(): lax.ppermute(array, axis, [(i, i ^ mask) for i in range(lax.axis_size(axi...  11.1 us
    pallas_call x1, Pallas kernels, root(): pl.pallas_call(functools.partial(root_kernel, most), out_shape=[out, out]...  6.15 us
    ppermute x3, starting transfers between devices, pass_on(): return lax.ppermute(send if flip else keep, ('x', 'group'), moves)  3.69 us
    ppermute x3, waiting for transfers between devices, pass_on(): return lax.ppermute(send if flip else keep, ('x', 'group'), moves)  3.27 us
    pallas_call x1, Pallas kernels, load(): pl.pallas_call(functools.partial(load_kernel, scale), out_shape=[jax.Shap...  1.67 us
  transfers between devices with their start and end apart: 15, of which 8 were waited for; matrix products, arithmetic and copies ran while one was open for 0% of the time, Pallas kernels for 2%

profile of v22, /device:TPU:0, one launch (start us, length us, event | category | flops | bytes accessed | tf_op | source)
XLA Modules:
  0.0 42.0 jit_solution(11698426008746785249)
XLA Ops:
  0.0 1.7 %shard_map.37 = (bf16[128,512]{1,0:T(8,128)(2,1)S(1)}, bf16[128,512]{1,0:T(8,128)(2,1)S(1)}, bf16[2,2,512,256]{3,2,1,0:T(8,128)(2,1)S(1)}, bf16[2,512,512]{2,1,0:T(8,128)(2,1)S(1)}) custom-call(bf16[2,512,512]{2,1,0:T(8,128)(2,1)} %patch_hbm.1, bf16[2,512,512]{2,1,0:T(8,128)(2,1)} %cot_hbm.1), custom_call_target="tpu_custom_call" | custom-call | tf_op jit(solution)/shard_map/pallas_call | solution.py:70
  1.7 0.5 %collective-permute-start = (bf16[128,512]{1,0:T(8,128)(2,1)S(1)}, bf16[128,512]{1,0:T(8,128)(2,1)S(1)}, u32[]{:S(2)}, u32[]{:S(2)}) collective-permute-start(bf16[128,512]{1,0:T(8,128)(2,1)S(1)} %get-tuple-element.23), channel_id=1, source_target_pairs={{0,2},{2,0},{1,3},{3,1},{4,6},{6,4},{5,7},{7,5},{8,10},{10,8},{9,1... | collective-permute-start | bytes 393224 | tf_op jit(solution)/shard_map/ppermute | solution.py:348
  2.2 0.1 collective-permute-start.3
  2.3 0.5 %shard_map.38 = (f32[128,512]{1,0:T(8,128)S(1)}, f32[128,512]{1,0:T(8,128)S(1)}, bf16[256,512]{1,0:T(8,128)(2,1)S(1)}) custom-call(bf16[2,2,512,256]{3,2,1,0:T(8,128)(2,1)S(1)} %get-tuple-element.20.patch, bf16[2,512,512]{2,1,0:T(8,128)(2,1)S(1)} %get-tuple-element.21.cot), custom_call_target="tpu_custom_call" | custom-call | flops 402653184 | bytes 1048576 | tf_op jit(solution)/shard_map/pallas_call | solution.py:98
  2.7 0.5 %collective-permute-start.1 = (bf16[256,512]{1,0:T(8,128)(2,1)S(1)}, bf16[256,512]{1,0:T(8,128)(2,1)S(1)}, u32[]{:S(2)}, u32[]{:S(2)}) collective-permute-start(bf16[256,512]{1,0:T(8,128)(2,1)S(1)} %get-tuple-element.25), channel_id=1, source_target_pairs={{0,2},{2,0},{1,3},{3,1},{4,6},{6,4},{5,7},{7,5},{8,10},{10,8},{9,1... | collective-permute-start | bytes 786440 | tf_op jit(solution)/shard_map/ppermute | solution.py:348
  3.2 0.0 collective-permute-done
  3.3 2.9 %collective-permute-start.5 = (bf16[128,512]{1,0:T(8,128)(2,1)S(1)}, bf16[128,512]{1,0:T(8,128)(2,1)S(1)}, u32[]{:S(2)}, u32[]{:S(2)}) collective-permute-start(bf16[128,512]{1,0:T(8,128)(2,1)S(1)} %add_convert_fusion.2.refs_0_), channel_id=1, source_target_pairs={{0,8},{8,0},{16,24},{24,16},{1,9},{9,1},{17,25},{25,17},{2,10},{10... | collective-permute-start | bytes 393224 | tf_op jit(solution)/shard_map/ppermute | solution.py:348
  6.2 0.0 collective-permute-done.3
  6.3 1.6 %collective-permute-start.4 = (bf16[128,512]{1,0:T(8,128)(2,1)S(1)}, bf16[128,512]{1,0:T(8,128)(2,1)S(1)}, u32[]{:S(2)}, u32[]{:S(2)}) collective-permute-start(bf16[128,512]{1,0:T(8,128)(2,1)S(1)} %add_convert_fusion), channel_id=1, source_target_pairs={{0,4},{4,0},{1,5},{5,1},{2,6},{6,2},{3,7},{7,3},{8,12},{12,8},{9,1... | collective-permute-start | bytes 393224 | tf_op jit(solution)/shard_map/ppermute | solution.py:348
  7.8 0.3 shard_map.39
  8.1 0.0 collective-permute-done.1
  8.1 0.1 add_convert_fusion.1
  8.2 0.2 collective-permute-start.2
  8.4 1.7 %collective-permute-done.5.refs_2_ = bf16[128,512]{1,0:T(8,128)(2,1)S(1)} collective-permute-done((bf16[128,512]{1,0:T(8,128)(2,1)S(1)}, bf16[128,512]{1,0:T(8,128)(2,1)S(1)}, u32[]{:S(2)}, u32[]{:S(2)}) %collective-permute-start.5) | collective-permute-done | bytes 131104 | tf_op jit(solution)/shard_map/ppermute | solution.py:348
  10.1 4.4 %collective-permute-done.4.refs_1_ = bf16[128,512]{1,0:T(8,128)(2,1)S(1)} collective-permute-done((bf16[128,512]{1,0:T(8,128)(2,1)S(1)}, bf16[128,512]{1,0:T(8,128)(2,1)S(1)}, u32[]{:S(2)}, u32[]{:S(2)}) %collective-permute-start.4) | collective-permute-done | bytes 131104 | tf_op jit(solution)/shard_map/ppermute | solution.py:348
  14.5 0.0 collective-permute-done.2.refs_0_
  14.5 0.1 shard_map.40
  14.5 2.7 %collective-permute-start.6 = (bf16[128,384]{1,0:T(8,128)(2,1)S(1)}, bf16[128,384]{1,0:T(8,128)(2,1)S(1)}, u32[]{:S(2)}, u32[]{:S(2)}) collective-permute-start(bf16[128,384]{1,0:T(8,128)(2,1)S(1)} %get-tuple-element.30), channel_id=1, source_target_pairs={{0,16},{8,24},{16,0},{24,8},{1,17},{9,25},{17,1},{25,9},{2,18},{10... | collective-permute-start | bytes 294920 | tf_op jit(solution)/shard_map/ppermute | solution.py:348
  17.2 0.3 collective-permute-start.9
  17.5 4.4 %collective-permute-done.6 = bf16[128,384]{1,0:T(8,128)(2,1)S(1)} collective-permute-done((bf16[128,384]{1,0:T(8,128)(2,1)S(1)}, bf16[128,384]{1,0:T(8,128)(2,1)S(1)}, u32[]{:S(2)}, u32[]{:S(2)}) %collective-permute-start.6) | collective-permute-done | bytes 98336 | tf_op jit(solution)/shard_map/ppermute | solution.py:348
  21.9 0.8 %collective-permute-start.7 = (bf16[128,384]{1,0:T(8,128)(2,1)S(1)}, bf16[128,384]{1,0:T(8,128)(2,1)S(1)}, u32[]{:S(2)}, u32[]{:S(2)}) collective-permute-start(bf16[128,384]{1,0:T(8,128)(2,1)S(1)} %add_convert_fusion.3.refs_0_), channel_id=1, source_target_pairs={{0,8},{8,0},{16,24},{24,16},{1,9},{9,1},{17,25},{25,17},{2,10},{10... | collective-permute-start | bytes 294920 | tf_op jit(solution)/shard_map/ppermute | solution.py:348
  22.7 0.0 collective-permute-done.9
  22.8 1.3 %collective-permute-start.10 = (bf16[128,128]{1,0:T(8,128)(2,1)S(1)}, bf16[128,128]{1,0:T(8,128)(2,1)S(1)}, u32[]{:S(2)}, u32[]{:S(2)}) collective-permute-start(bf16[128,128]{1,0:T(8,128)(2,1)S(1)} %add_convert_fusion.4.refs_3_), channel_id=1, source_target_pairs={{0,8},{8,0},{16,24},{24,16},{1,9},{9,1},{17,25},{25,17},{2,10},{10... | collective-permute-start | bytes 98312 | tf_op jit(solution)/shard_map/ppermute | solution.py:348
  24.1 2.5 %collective-permute-done.7.refs_1_ = bf16[128,384]{1,0:T(8,128)(2,1)S(1)} collective-permute-done((bf16[128,384]{1,0:T(8,128)(2,1)S(1)}, bf16[128,384]{1,0:T(8,128)(2,1)S(1)}, u32[]{:S(2)}, u32[]{:S(2)}) %collective-permute-start.7) | collective-permute-done | bytes 98336 | tf_op jit(solution)/shard_map/ppermute | solution.py:348
  26.6 0.1 collective-permute-start.8
  26.7 0.2 collective-permute-done.10.refs_4_
  26.9 0.3 collective-permute-start.11
  27.3 0.9 %collective-permute-done.11.refs_5_ = bf16[256,128]{1,0:T(8,128)(2,1)S(1)} collective-permute-done((bf16[256,128]{1,0:T(8,128)(2,1)S(1)}, bf16[256,128]{1,0:T(8,128)(2,1)S(1)}, u32[]{:S(2)}, u32[]{:S(2)}) %collective-permute-start.11) | collective-permute-done | bytes 65568 | tf_op jit(solution)/shard_map/ppermute | solution.py:348
  28.2 0.0 collective-permute-done.8.refs_2_
  28.2 6.1 %shard_map.41 = (bf16[32,512]{1,0:T(8,128)(2,1)S(1)}, bf16[32,512]{1,0:T(8,128)(2,1)S(1)}) custom-call(s32[2,2]{1,0:T(2,128)} %counts_hbm.1, bf16[128,384]{1,0:T(8,128)(2,1)S(1)} %add_convert_fusion.3.refs_0_, bf16[128,384]{1,0:T(8,128)(2,1)S(1)} %collective-permute-done.7.refs_1_, bf16[256,384]{1,0:T(8,128)(2,1)S(1)} %collective-permute-done.8.refs_2_, ...), custom_call_target="tpu_custom_call" | custom-call | tf_op jit(solution)/shard_map/pallas_call | solution.py:295
  34.4 3.1 %collective-permute-start.14 = (bf16[32,512]{1,0:T(8,128)(2,1)S(1)}, bf16[32,512]{1,0:T(8,128)(2,1)S(1)}, u32[]{:S(2)}, u32[]{:S(2)}) collective-permute-start(bf16[32,512]{1,0:T(8,128)(2,1)S(1)} %get-tuple-element.33), channel_id=1, source_target_pairs={{0,5},{1,4},{4,1},{5,0},{2,7},{3,6},{6,3},{7,2},{8,13},{9,12},{12,... | collective-permute-start | bytes 98312 | tf_op jit(solution)/shard_map/ppermute | solution.py:398
  37.4 0.0 collective-permute-start.12
  37.4 0.6 %collective-permute-start.13 = (bf16[32,512]{1,0:T(8,128)(2,1)S(1)}, bf16[32,512]{1,0:T(8,128)(2,1)S(1)}, u32[]{:S(2)}, u32[]{:S(2)}) collective-permute-start(bf16[32,512]{1,0:T(8,128)(2,1)S(1)} %get-tuple-element.34.refs_3_), channel_id=1, source_target_pairs={{0,1},{1,0},{4,5},{5,4},{2,3},{3,2},{6,7},{7,6},{8,9},{9,8},{12,13... | collective-permute-start | bytes 98312 | tf_op jit(solution)/shard_map/ppermute | solution.py:398
  38.1 1.3 %collective-permute-done.14.refs_2_ = bf16[32,512]{1,0:T(8,128)(2,1)S(1)} collective-permute-done((bf16[32,512]{1,0:T(8,128)(2,1)S(1)}, bf16[32,512]{1,0:T(8,128)(2,1)S(1)}, u32[]{:S(2)}, u32[]{:S(2)}) %collective-permute-start.14) | collective-permute-done | bytes 32800 | tf_op jit(solution)/shard_map/ppermute | solution.py:398
  39.3 2.0 %collective-permute-done.12.refs_0_ = bf16[32,512]{1,0:T(8,128)(2,1)S(1)} collective-permute-done((bf16[32,512]{1,0:T(8,128)(2,1)S(1)}, bf16[32,512]{1,0:T(8,128)(2,1)S(1)}, u32[]{:S(2)}, u32[]{:S(2)}) %collective-permute-start.12) | collective-permute-done | bytes 32800 | tf_op jit(solution)/shard_map/ppermute | solution.py:398
  41.3 0.0 collective-permute-done.13.refs_1_
  41.3 0.7 %shard_map.42 = bf16[4,32,512]{2,1,0:T(8,128)(2,1)} custom-call(bf16[32,512]{1,0:T(8,128)(2,1)S(1)} %collective-permute-done.12.refs_0_, bf16[32,512]{1,0:T(8,128)(2,1)S(1)} %collective-permute-done.13.refs_1_, bf16[32,512]{1,0:T(8,128)(2,1)S(1)} %collective-permute-done.14.refs_2_, bf16[32,512]{1,0:T(8,128)(2,1)S(1)} %get-tuple-element.34.refs_3_), custom_call_target="tpu_custom_call" | custom-call | tf_op jit(solution)/shard_map/pallas_call | solution.py:331
  (6 shorter events, 0.1 us)
Async XLA Ops:
  1.7 1.6 %collective-permute-start = (bf16[128,512]{1,0:T(8,128)(2,1)S(1)}, bf16[128,512]{1,0:T(8,128)(2,1)S(1)}, u32[]{:S(2)}, u32[]{:S(2)}) collective-permute-start(bf16[128,512]{1,0:T(8,128)(2,1)S(1)} %get-tuple-element.23), channel_id=1, source_target_pairs={{0,2},{2,0},{1,3},{3,1},{4,6},{6,4},{5,7},{7,5},{8,10},{10,8},{9,1... | collective-permute-start | bytes 393224 | tf_op jit(solution)/shard_map/ppermute | solution.py:348
  2.2 4.0 %collective-permute-start.3 = (bf16[128,512]{1,0:T(8,128)(2,1)S(1)}, bf16[128,512]{1,0:T(8,128)(2,1)S(1)}, u32[]{:S(2)}, u32[]{:S(2)}) collective-permute-start(bf16[128,512]{1,0:T(8,128)(2,1)S(1)} %get-tuple-element.28), channel_id=1, source_target_pairs={{0,2},{2,0},{1,3},{3,1},{4,6},{6,4},{5,7},{7,5},{8,10},{10,8},{9,1... | collective-permute-start | bytes 393224 | tf_op jit(solution)/shard_map/ppermute | solution.py:348
  2.7 5.4 %collective-permute-start.1 = (bf16[256,512]{1,0:T(8,128)(2,1)S(1)}, bf16[256,512]{1,0:T(8,128)(2,1)S(1)}, u32[]{:S(2)}, u32[]{:S(2)}) collective-permute-start(bf16[256,512]{1,0:T(8,128)(2,1)S(1)} %get-tuple-element.25), channel_id=1, source_target_pairs={{0,2},{2,0},{1,3},{3,1},{4,6},{6,4},{5,7},{7,5},{8,10},{10,8},{9,1... | collective-permute-start | bytes 786440 | tf_op jit(solution)/shard_map/ppermute | solution.py:348
  3.3 6.8 %collective-permute-start.5 = (bf16[128,512]{1,0:T(8,128)(2,1)S(1)}, bf16[128,512]{1,0:T(8,128)(2,1)S(1)}, u32[]{:S(2)}, u32[]{:S(2)}) collective-permute-start(bf16[128,512]{1,0:T(8,128)(2,1)S(1)} %add_convert_fusion.2.refs_0_), channel_id=1, source_target_pairs={{0,8},{8,0},{16,24},{24,16},{1,9},{9,1},{17,25},{25,17},{2,10},{10... | collective-permute-start | bytes 393224 | tf_op jit(solution)/shard_map/ppermute | solution.py:348
  6.3 8.2 %collective-permute-start.4 = (bf16[128,512]{1,0:T(8,128)(2,1)S(1)}, bf16[128,512]{1,0:T(8,128)(2,1)S(1)}, u32[]{:S(2)}, u32[]{:S(2)}) collective-permute-start(bf16[128,512]{1,0:T(8,128)(2,1)S(1)} %add_convert_fusion), channel_id=1, source_target_pairs={{0,4},{4,0},{1,5},{5,1},{2,6},{6,2},{3,7},{7,3},{8,12},{12,8},{9,1... | collective-permute-start | bytes 393224 | tf_op jit(solution)/shard_map/ppermute | solution.py:348
  8.2 6.2 %collective-permute-start.2 = (bf16[128,512]{1,0:T(8,128)(2,1)S(1)}, bf16[128,512]{1,0:T(8,128)(2,1)S(1)}, u32[]{:S(2)}, u32[]{:S(2)}) collective-permute-start(bf16[128,512]{1,0:T(8,128)(2,1)S(1)} %get-tuple-element.35), channel_id=1, source_target_pairs={{0,12},{4,8},{8,4},{12,0},{16,28},{20,24},{24,20},{28,16},{1,13},{... | collective-permute-start | bytes 393224 | tf_op jit(solution)/shard_map/ppermute | solution.py:352
  14.5 7.3 %collective-permute-start.6 = (bf16[128,384]{1,0:T(8,128)(2,1)S(1)}, bf16[128,384]{1,0:T(8,128)(2,1)S(1)}, u32[]{:S(2)}, u32[]{:S(2)}) collective-permute-start(bf16[128,384]{1,0:T(8,128)(2,1)S(1)} %get-tuple-element.30), channel_id=1, source_target_pairs={{0,16},{8,24},{16,0},{24,8},{1,17},{9,25},{17,1},{25,9},{2,18},{10... | collective-permute-start | bytes 294920 | tf_op jit(solution)/shard_map/ppermute | solution.py:348
  17.2 5.6 %collective-permute-start.9 = (bf16[128,128]{1,0:T(8,128)(2,1)S(1)}, bf16[128,128]{1,0:T(8,128)(2,1)S(1)}, u32[]{:S(2)}, u32[]{:S(2)}) collective-permute-start(bf16[128,128]{1,0:T(8,128)(2,1)S(1)} %get-tuple-element.32), channel_id=1, source_target_pairs={{0,16},{8,24},{16,0},{24,8},{1,17},{9,25},{17,1},{25,9},{2,18},{10... | collective-permute-start | bytes 98312 | tf_op jit(solution)/shard_map/ppermute | solution.py:348
  21.9 4.7 %collective-permute-start.7 = (bf16[128,384]{1,0:T(8,128)(2,1)S(1)}, bf16[128,384]{1,0:T(8,128)(2,1)S(1)}, u32[]{:S(2)}, u32[]{:S(2)}) collective-permute-start(bf16[128,384]{1,0:T(8,128)(2,1)S(1)} %add_convert_fusion.3.refs_0_), channel_id=1, source_target_pairs={{0,8},{8,0},{16,24},{24,16},{1,9},{9,1},{17,25},{25,17},{2,10},{10... | collective-permute-start | bytes 294920 | tf_op jit(solution)/shard_map/ppermute | solution.py:348
  22.8 4.2 %collective-permute-start.10 = (bf16[128,128]{1,0:T(8,128)(2,1)S(1)}, bf16[128,128]{1,0:T(8,128)(2,1)S(1)}, u32[]{:S(2)}, u32[]{:S(2)}) collective-permute-start(bf16[128,128]{1,0:T(8,128)(2,1)S(1)} %add_convert_fusion.4.refs_3_), channel_id=1, source_target_pairs={{0,8},{8,0},{16,24},{24,16},{1,9},{9,1},{17,25},{25,17},{2,10},{10... | collective-permute-start | bytes 98312 | tf_op jit(solution)/shard_map/ppermute | solution.py:348
  26.6 1.6 %collective-permute-start.8 = (bf16[256,384]{1,0:T(8,128)(2,1)S(1)}, bf16[256,384]{1,0:T(8,128)(2,1)S(1)}, u32[]{:S(2)}, u32[]{:S(2)}) collective-permute-start(bf16[256,384]{1,0:T(8,128)(2,1)S(1)} %pad_maximum_fusion), channel_id=1, source_target_pairs={{0,2},{2,0},{1,3},{3,1},{4,6},{6,4},{5,7},{7,5},{8,10},{10,8},{9,1... | collective-permute-start | bytes 589832 | tf_op jit(solution)/shard_map/ppermute | solution.py:348
  26.9 1.3 %collective-permute-start.11 = (bf16[256,128]{1,0:T(8,128)(2,1)S(1)}, bf16[256,128]{1,0:T(8,128)(2,1)S(1)}, u32[]{:S(2)}, u32[]{:S(2)}) collective-permute-start(bf16[256,128]{1,0:T(8,128)(2,1)S(1)} %pad_maximum_fusion.1), channel_id=1, source_target_pairs={{0,2},{2,0},{1,3},{3,1},{4,6},{6,4},{5,7},{7,5},{8,10},{10,8},{9,1... | collective-permute-start | bytes 196616 | tf_op jit(solution)/shard_map/ppermute | solution.py:348
  34.4 4.9 %collective-permute-start.14 = (bf16[32,512]{1,0:T(8,128)(2,1)S(1)}, bf16[32,512]{1,0:T(8,128)(2,1)S(1)}, u32[]{:S(2)}, u32[]{:S(2)}) collective-permute-start(bf16[32,512]{1,0:T(8,128)(2,1)S(1)} %get-tuple-element.33), channel_id=1, source_target_pairs={{0,5},{1,4},{4,1},{5,0},{2,7},{3,6},{6,3},{7,2},{8,13},{9,12},{12,... | collective-permute-start | bytes 98312 | tf_op jit(solution)/shard_map/ppermute | solution.py:398
  37.4 3.9 %collective-permute-start.12 = (bf16[32,512]{1,0:T(8,128)(2,1)S(1)}, bf16[32,512]{1,0:T(8,128)(2,1)S(1)}, u32[]{:S(2)}, u32[]{:S(2)}) collective-permute-start(bf16[32,512]{1,0:T(8,128)(2,1)S(1)} %get-tuple-element.33), channel_id=1, source_target_pairs={{0,4},{1,5},{4,0},{5,1},{2,6},{3,7},{6,2},{7,3},{8,12},{9,13},{12,... | collective-permute-start | bytes 98312 | tf_op jit(solution)/shard_map/ppermute | solution.py:398
  37.4 3.9 %collective-permute-start.13 = (bf16[32,512]{1,0:T(8,128)(2,1)S(1)}, bf16[32,512]{1,0:T(8,128)(2,1)S(1)}, u32[]{:S(2)}, u32[]{:S(2)}) collective-permute-start(bf16[32,512]{1,0:T(8,128)(2,1)S(1)} %get-tuple-element.34.refs_3_), channel_id=1, source_target_pairs={{0,1},{1,0},{4,5},{5,4},{2,3},{3,2},{6,7},{7,6},{8,9},{9,8},{12,13... | collective-permute-start | bytes 98312 | tf_op jit(solution)/shard_map/ppermute | solution.py:398

commit v23 on v22

--- a/solution.py
+++ b/solution.py
@@ -397,7 +397,7 @@
         ]
         return lax.ppermute(send if flip else keep, ("x", "group"), moves)
 
-    others = [(turn, flip) for turn in range(groups) for flip in range(2) if turn or flip]
+    others = [(turn, flip) for flip in (1, 0) for turn in range(groups - 1, -1, -1) if turn or flip]
     found = {(turn, flip): pass_on(turn, flip) for turn, flip in others}
     found[0, 0] = keep
     return place(found)

time: 42.2 us -> 42.5 us (level)
  transfers between devices with their start and end apart: 15 -> 15, of which waited for: 8 -> 9; matrix products, arithmetic and copies ran while one was open for 0% -> 0% of each run, Pallas kernels for 2% -> 2%
where the time goes in v23:
time: 42.5 us; the launch traced here: 42.3 us
  waiting for transfers between devices  17.7 us (42%)
  starting transfers between devices  15 us (35%)
  Pallas kernels  9.35 us (22%)
    ppermute x11, waiting for transfers between devices, swap(): lax.ppermute(array, axis, [(i, i ^ mask) for i in range(lax.axis_size(axi...  14.1 us
    ppermute x11, starting transfers between devices, swap(): lax.ppermute(array, axis, [(i, i ^ mask) for i in range(lax.axis_size(axi...  11.1 us
    pallas_call x1, Pallas kernels, root(): pl.pallas_call(functools.partial(root_kernel, most), out_shape=[out, out]...  6.15 us
    ppermute x3, starting transfers between devices, pass_on(): return lax.ppermute(send if flip else keep, ('x', 'group'), moves)  3.64 us
    ppermute x3, waiting for transfers between devices, pass_on(): return lax.ppermute(send if flip else keep, ('x', 'group'), moves)  3.62 us
    pallas_call x1, Pallas kernels, load(): pl.pallas_call(functools.partial(load_kernel, scale), out_shape=[jax.Shap...  1.67 us
  transfers between devices with their start and end apart: 15, of which 9 were waited for; matrix products, arithmetic and copies ran while one was open for 0% of the time, Pallas kernels for 2%

profile of v23, /device:TPU:0, one launch (start us, length us, event | category | flops | bytes accessed | tf_op | source)
XLA Modules:
  0.0 42.3 jit_solution(15797517837772836045)
XLA Ops:
  0.0 1.7 %shard_map.37 = (bf16[128,512]{1,0:T(8,128)(2,1)S(1)}, bf16[128,512]{1,0:T(8,128)(2,1)S(1)}, bf16[2,2,512,256]{3,2,1,0:T(8,128)(2,1)S(1)}, bf16[2,512,512]{2,1,0:T(8,128)(2,1)S(1)}) custom-call(bf16[2,512,512]{2,1,0:T(8,128)(2,1)} %patch_hbm.1, bf16[2,512,512]{2,1,0:T(8,128)(2,1)} %cot_hbm.1), custom_call_target="tpu_custom_call" | custom-call | tf_op jit(solution)/shard_map/pallas_call | solution.py:70
  1.7 0.5 %collective-permute-start = (bf16[128,512]{1,0:T(8,128)(2,1)S(1)}, bf16[128,512]{1,0:T(8,128)(2,1)S(1)}, u32[]{:S(2)}, u32[]{:S(2)}) collective-permute-start(bf16[128,512]{1,0:T(8,128)(2,1)S(1)} %get-tuple-element.23), channel_id=1, source_target_pairs={{0,2},{2,0},{1,3},{3,1},{4,6},{6,4},{5,7},{7,5},{8,10},{10,8},{9,1... | collective-permute-start | bytes 393224 | tf_op jit(solution)/shard_map/ppermute | solution.py:348
  2.2 0.1 collective-permute-start.3
  2.3 0.5 %shard_map.38 = (f32[128,512]{1,0:T(8,128)S(1)}, f32[128,512]{1,0:T(8,128)S(1)}, bf16[256,512]{1,0:T(8,128)(2,1)S(1)}) custom-call(bf16[2,2,512,256]{3,2,1,0:T(8,128)(2,1)S(1)} %get-tuple-element.20.patch, bf16[2,512,512]{2,1,0:T(8,128)(2,1)S(1)} %get-tuple-element.21.cot), custom_call_target="tpu_custom_call" | custom-call | flops 402653184 | bytes 1048576 | tf_op jit(solution)/shard_map/pallas_call | solution.py:98
  2.7 0.5 %collective-permute-start.1 = (bf16[256,512]{1,0:T(8,128)(2,1)S(1)}, bf16[256,512]{1,0:T(8,128)(2,1)S(1)}, u32[]{:S(2)}, u32[]{:S(2)}) collective-permute-start(bf16[256,512]{1,0:T(8,128)(2,1)S(1)} %get-tuple-element.25), channel_id=1, source_target_pairs={{0,2},{2,0},{1,3},{3,1},{4,6},{6,4},{5,7},{7,5},{8,10},{10,8},{9,1... | collective-permute-start | bytes 786440 | tf_op jit(solution)/shard_map/ppermute | solution.py:348
  3.2 0.0 collective-permute-done
  3.3 2.9 %collective-permute-start.5 = (bf16[128,512]{1,0:T(8,128)(2,1)S(1)}, bf16[128,512]{1,0:T(8,128)(2,1)S(1)}, u32[]{:S(2)}, u32[]{:S(2)}) collective-permute-start(bf16[128,512]{1,0:T(8,128)(2,1)S(1)} %add_convert_fusion.2.refs_0_), channel_id=1, source_target_pairs={{0,8},{8,0},{16,24},{24,16},{1,9},{9,1},{17,25},{25,17},{2,10},{10... | collective-permute-start | bytes 393224 | tf_op jit(solution)/shard_map/ppermute | solution.py:348
  6.2 0.0 collective-permute-done.3
  6.3 1.6 %collective-permute-start.4 = (bf16[128,512]{1,0:T(8,128)(2,1)S(1)}, bf16[128,512]{1,0:T(8,128)(2,1)S(1)}, u32[]{:S(2)}, u32[]{:S(2)}) collective-permute-start(bf16[128,512]{1,0:T(8,128)(2,1)S(1)} %add_convert_fusion), channel_id=1, source_target_pairs={{0,4},{4,0},{1,5},{5,1},{2,6},{6,2},{3,7},{7,3},{8,12},{12,8},{9,1... | collective-permute-start | bytes 393224 | tf_op jit(solution)/shard_map/ppermute | solution.py:348
  7.8 0.3 shard_map.39
  8.1 0.0 collective-permute-done.1
  8.1 0.1 add_convert_fusion.1
  8.2 0.2 collective-permute-start.2
  8.4 1.7 %collective-permute-done.5.refs_2_ = bf16[128,512]{1,0:T(8,128)(2,1)S(1)} collective-permute-done((bf16[128,512]{1,0:T(8,128)(2,1)S(1)}, bf16[128,512]{1,0:T(8,128)(2,1)S(1)}, u32[]{:S(2)}, u32[]{:S(2)}) %collective-permute-start.5) | collective-permute-done | bytes 131104 | tf_op jit(solution)/shard_map/ppermute | solution.py:348
  10.1 4.4 %collective-permute-done.4.refs_1_ = bf16[128,512]{1,0:T(8,128)(2,1)S(1)} collective-permute-done((bf16[128,512]{1,0:T(8,128)(2,1)S(1)}, bf16[128,512]{1,0:T(8,128)(2,1)S(1)}, u32[]{:S(2)}, u32[]{:S(2)}) %collective-permute-start.4) | collective-permute-done | bytes 131104 | tf_op jit(solution)/shard_map/ppermute | solution.py:348
  14.5 0.0 collective-permute-done.2.refs_0_
  14.5 0.1 shard_map.40
  14.5 2.7 %collective-permute-start.6 = (bf16[128,384]{1,0:T(8,128)(2,1)S(1)}, bf16[128,384]{1,0:T(8,128)(2,1)S(1)}, u32[]{:S(2)}, u32[]{:S(2)}) collective-permute-start(bf16[128,384]{1,0:T(8,128)(2,1)S(1)} %get-tuple-element.30), channel_id=1, source_target_pairs={{0,16},{8,24},{16,0},{24,8},{1,17},{9,25},{17,1},{25,9},{2,18},{10... | collective-permute-start | bytes 294920 | tf_op jit(solution)/shard_map/ppermute | solution.py:348
  17.2 0.3 collective-permute-start.9
  17.5 4.4 %collective-permute-done.6 = bf16[128,384]{1,0:T(8,128)(2,1)S(1)} collective-permute-done((bf16[128,384]{1,0:T(8,128)(2,1)S(1)}, bf16[128,384]{1,0:T(8,128)(2,1)S(1)}, u32[]{:S(2)}, u32[]{:S(2)}) %collective-permute-start.6) | collective-permute-done | bytes 98336 | tf_op jit(solution)/shard_map/ppermute | solution.py:348
  21.9 0.8 %collective-permute-start.7 = (bf16[128,384]{1,0:T(8,128)(2,1)S(1)}, bf16[128,384]{1,0:T(8,128)(2,1)S(1)}, u32[]{:S(2)}, u32[]{:S(2)}) collective-permute-start(bf16[128,384]{1,0:T(8,128)(2,1)S(1)} %add_convert_fusion.3.refs_0_), channel_id=1, source_target_pairs={{0,8},{8,0},{16,24},{24,16},{1,9},{9,1},{17,25},{25,17},{2,10},{10... | collective-permute-start | bytes 294920 | tf_op jit(solution)/shard_map/ppermute | solution.py:348
  22.7 0.0 collective-permute-done.9
  22.8 1.3 %collective-permute-start.10 = (bf16[128,128]{1,0:T(8,128)(2,1)S(1)}, bf16[128,128]{1,0:T(8,128)(2,1)S(1)}, u32[]{:S(2)}, u32[]{:S(2)}) collective-permute-start(bf16[128,128]{1,0:T(8,128)(2,1)S(1)} %add_convert_fusion.4.refs_3_), channel_id=1, source_target_pairs={{0,8},{8,0},{16,24},{24,16},{1,9},{9,1},{17,25},{25,17},{2,10},{10... | collective-permute-start | bytes 98312 | tf_op jit(solution)/shard_map/ppermute | solution.py:348
  24.1 2.5 %collective-permute-done.7.refs_1_ = bf16[128,384]{1,0:T(8,128)(2,1)S(1)} collective-permute-done((bf16[128,384]{1,0:T(8,128)(2,1)S(1)}, bf16[128,384]{1,0:T(8,128)(2,1)S(1)}, u32[]{:S(2)}, u32[]{:S(2)}) %collective-permute-start.7) | collective-permute-done | bytes 98336 | tf_op jit(solution)/shard_map/ppermute | solution.py:348
  26.6 0.1 collective-permute-start.8
  26.7 0.2 collective-permute-done.10.refs_4_
  26.9 0.3 collective-permute-start.11
  27.3 0.9 %collective-permute-done.11.refs_5_ = bf16[256,128]{1,0:T(8,128)(2,1)S(1)} collective-permute-done((bf16[256,128]{1,0:T(8,128)(2,1)S(1)}, bf16[256,128]{1,0:T(8,128)(2,1)S(1)}, u32[]{:S(2)}, u32[]{:S(2)}) %collective-permute-start.11) | collective-permute-done | bytes 65568 | tf_op jit(solution)/shard_map/ppermute | solution.py:348
  28.2 0.0 collective-permute-done.8.refs_2_
  28.2 6.1 %shard_map.41 = (bf16[32,512]{1,0:T(8,128)(2,1)S(1)}, bf16[32,512]{1,0:T(8,128)(2,1)S(1)}) custom-call(s32[2,2]{1,0:T(2,128)} %counts_hbm.1, bf16[128,384]{1,0:T(8,128)(2,1)S(1)} %add_convert_fusion.3.refs_0_, bf16[128,384]{1,0:T(8,128)(2,1)S(1)} %collective-permute-done.7.refs_1_, bf16[256,384]{1,0:T(8,128)(2,1)S(1)} %collective-permute-done.8.refs_2_, ...), custom_call_target="tpu_custom_call" | custom-call | tf_op jit(solution)/shard_map/pallas_call | solution.py:295
  34.4 2.1 %collective-permute-start.13 = (bf16[32,512]{1,0:T(8,128)(2,1)S(1)}, bf16[32,512]{1,0:T(8,128)(2,1)S(1)}, u32[]{:S(2)}, u32[]{:S(2)}) collective-permute-start(bf16[32,512]{1,0:T(8,128)(2,1)S(1)} %get-tuple-element.33), channel_id=1, source_target_pairs={{0,4},{1,5},{4,0},{5,1},{2,6},{3,7},{6,2},{7,3},{8,12},{9,13},{12,... | collective-permute-start | bytes 98312 | tf_op jit(solution)/shard_map/ppermute | solution.py:398
  36.5 1.0 %collective-permute-start.12 = (bf16[32,512]{1,0:T(8,128)(2,1)S(1)}, bf16[32,512]{1,0:T(8,128)(2,1)S(1)}, u32[]{:S(2)}, u32[]{:S(2)}) collective-permute-start(bf16[32,512]{1,0:T(8,128)(2,1)S(1)} %get-tuple-element.33), channel_id=1, source_target_pairs={{0,5},{1,4},{4,1},{5,0},{2,7},{3,6},{6,3},{7,2},{8,13},{9,12},{12,... | collective-permute-start | bytes 98312 | tf_op jit(solution)/shard_map/ppermute | solution.py:398
  37.5 0.5 %collective-permute-start.14 = (bf16[32,512]{1,0:T(8,128)(2,1)S(1)}, bf16[32,512]{1,0:T(8,128)(2,1)S(1)}, u32[]{:S(2)}, u32[]{:S(2)}) collective-permute-start(bf16[32,512]{1,0:T(8,128)(2,1)S(1)} %get-tuple-element.34.refs_3_), channel_id=1, source_target_pairs={{0,1},{1,0},{4,5},{5,4},{2,3},{3,2},{6,7},{7,6},{8,9},{9,8},{12,13... | collective-permute-start | bytes 98312 | tf_op jit(solution)/shard_map/ppermute | solution.py:398
  38.0 0.4 collective-permute-done.13.refs_1_
  38.4 2.9 %collective-permute-done.12.refs_0_ = bf16[32,512]{1,0:T(8,128)(2,1)S(1)} collective-permute-done((bf16[32,512]{1,0:T(8,128)(2,1)S(1)}, bf16[32,512]{1,0:T(8,128)(2,1)S(1)}, u32[]{:S(2)}, u32[]{:S(2)}) %collective-permute-start.12) | collective-permute-done | bytes 32800 | tf_op jit(solution)/shard_map/ppermute | solution.py:398
  41.3 0.3 collective-permute-done.14.refs_2_
  41.6 0.7 %shard_map.42 = bf16[4,32,512]{2,1,0:T(8,128)(2,1)} custom-call(bf16[32,512]{1,0:T(8,128)(2,1)S(1)} %collective-permute-done.12.refs_0_, bf16[32,512]{1,0:T(8,128)(2,1)S(1)} %collective-permute-done.13.refs_1_, bf16[32,512]{1,0:T(8,128)(2,1)S(1)} %collective-permute-done.14.refs_2_, bf16[32,512]{1,0:T(8,128)(2,1)S(1)} %get-tuple-element.34.refs_3_), custom_call_target="tpu_custom_call" | custom-call | tf_op jit(solution)/shard_map/pallas_call | solution.py:331
  (6 shorter events, 0.1 us)
Async XLA Ops:
  1.7 1.6 %collective-permute-start = (bf16[128,512]{1,0:T(8,128)(2,1)S(1)}, bf16[128,512]{1,0:T(8,128)(2,1)S(1)}, u32[]{:S(2)}, u32[]{:S(2)}) collective-permute-start(bf16[128,512]{1,0:T(8,128)(2,1)S(1)} %get-tuple-element.23), channel_id=1, source_target_pairs={{0,2},{2,0},{1,3},{3,1},{4,6},{6,4},{5,7},{7,5},{8,10},{10,8},{9,1... | collective-permute-start | bytes 393224 | tf_op jit(solution)/shard_map/ppermute | solution.py:348
  2.2 4.0 %collective-permute-start.3 = (bf16[128,512]{1,0:T(8,128)(2,1)S(1)}, bf16[128,512]{1,0:T(8,128)(2,1)S(1)}, u32[]{:S(2)}, u32[]{:S(2)}) collective-permute-start(bf16[128,512]{1,0:T(8,128)(2,1)S(1)} %get-tuple-element.28), channel_id=1, source_target_pairs={{0,2},{2,0},{1,3},{3,1},{4,6},{6,4},{5,7},{7,5},{8,10},{10,8},{9,1... | collective-permute-start | bytes 393224 | tf_op jit(solution)/shard_map/ppermute | solution.py:348
  2.7 5.4 %collective-permute-start.1 = (bf16[256,512]{1,0:T(8,128)(2,1)S(1)}, bf16[256,512]{1,0:T(8,128)(2,1)S(1)}, u32[]{:S(2)}, u32[]{:S(2)}) collective-permute-start(bf16[256,512]{1,0:T(8,128)(2,1)S(1)} %get-tuple-element.25), channel_id=1, source_target_pairs={{0,2},{2,0},{1,3},{3,1},{4,6},{6,4},{5,7},{7,5},{8,10},{10,8},{9,1... | collective-permute-start | bytes 786440 | tf_op jit(solution)/shard_map/ppermute | solution.py:348
  3.3 6.8 %collective-permute-start.5 = (bf16[128,512]{1,0:T(8,128)(2,1)S(1)}, bf16[128,512]{1,0:T(8,128)(2,1)S(1)}, u32[]{:S(2)}, u32[]{:S(2)}) collective-permute-start(bf16[128,512]{1,0:T(8,128)(2,1)S(1)} %add_convert_fusion.2.refs_0_), channel_id=1, source_target_pairs={{0,8},{8,0},{16,24},{24,16},{1,9},{9,1},{17,25},{25,17},{2,10},{10... | collective-permute-start | bytes 393224 | tf_op jit(solution)/shard_map/ppermute | solution.py:348
  6.3 8.2 %collective-permute-start.4 = (bf16[128,512]{1,0:T(8,128)(2,1)S(1)}, bf16[128,512]{1,0:T(8,128)(2,1)S(1)}, u32[]{:S(2)}, u32[]{:S(2)}) collective-permute-start(bf16[128,512]{1,0:T(8,128)(2,1)S(1)} %add_convert_fusion), channel_id=1, source_target_pairs={{0,4},{4,0},{1,5},{5,1},{2,6},{6,2},{3,7},{7,3},{8,12},{12,8},{9,1... | collective-permute-start | bytes 393224 | tf_op jit(solution)/shard_map/ppermute | solution.py:348
  8.2 6.2 %collective-permute-start.2 = (bf16[128,512]{1,0:T(8,128)(2,1)S(1)}, bf16[128,512]{1,0:T(8,128)(2,1)S(1)}, u32[]{:S(2)}, u32[]{:S(2)}) collective-permute-start(bf16[128,512]{1,0:T(8,128)(2,1)S(1)} %get-tuple-element.35), channel_id=1, source_target_pairs={{0,12},{4,8},{8,4},{12,0},{16,28},{20,24},{24,20},{28,16},{1,13},{... | collective-permute-start | bytes 393224 | tf_op jit(solution)/shard_map/ppermute | solution.py:352
  14.5 7.3 %collective-permute-start.6 = (bf16[128,384]{1,0:T(8,128)(2,1)S(1)}, bf16[128,384]{1,0:T(8,128)(2,1)S(1)}, u32[]{:S(2)}, u32[]{:S(2)}) collective-permute-start(bf16[128,384]{1,0:T(8,128)(2,1)S(1)} %get-tuple-element.30), channel_id=1, source_target_pairs={{0,16},{8,24},{16,0},{24,8},{1,17},{9,25},{17,1},{25,9},{2,18},{10... | collective-permute-start | bytes 294920 | tf_op jit(solution)/shard_map/ppermute | solution.py:348
  17.2 5.6 %collective-permute-start.9 = (bf16[128,128]{1,0:T(8,128)(2,1)S(1)}, bf16[128,128]{1,0:T(8,128)(2,1)S(1)}, u32[]{:S(2)}, u32[]{:S(2)}) collective-permute-start(bf16[128,128]{1,0:T(8,128)(2,1)S(1)} %get-tuple-element.32), channel_id=1, source_target_pairs={{0,16},{8,24},{16,0},{24,8},{1,17},{9,25},{17,1},{25,9},{2,18},{10... | collective-permute-start | bytes 98312 | tf_op jit(solution)/shard_map/ppermute | solution.py:348
  21.9 4.7 %collective-permute-start.7 = (bf16[128,384]{1,0:T(8,128)(2,1)S(1)}, bf16[128,384]{1,0:T(8,128)(2,1)S(1)}, u32[]{:S(2)}, u32[]{:S(2)}) collective-permute-start(bf16[128,384]{1,0:T(8,128)(2,1)S(1)} %add_convert_fusion.3.refs_0_), channel_id=1, source_target_pairs={{0,8},{8,0},{16,24},{24,16},{1,9},{9,1},{17,25},{25,17},{2,10},{10... | collective-permute-start | bytes 294920 | tf_op jit(solution)/shard_map/ppermute | solution.py:348
  22.8 4.2 %collective-permute-start.10 = (bf16[128,128]{1,0:T(8,128)(2,1)S(1)}, bf16[128,128]{1,0:T(8,128)(2,1)S(1)}, u32[]{:S(2)}, u32[]{:S(2)}) collective-permute-start(bf16[128,128]{1,0:T(8,128)(2,1)S(1)} %add_convert_fusion.4.refs_3_), channel_id=1, source_target_pairs={{0,8},{8,0},{16,24},{24,16},{1,9},{9,1},{17,25},{25,17},{2,10},{10... | collective-permute-start | bytes 98312 | tf_op jit(solution)/shard_map/ppermute | solution.py:348
  26.6 1.6 %collective-permute-start.8 = (bf16[256,384]{1,0:T(8,128)(2,1)S(1)}, bf16[256,384]{1,0:T(8,128)(2,1)S(1)}, u32[]{:S(2)}, u32[]{:S(2)}) collective-permute-start(bf16[256,384]{1,0:T(8,128)(2,1)S(1)} %pad_maximum_fusion), channel_id=1, source_target_pairs={{0,2},{2,0},{1,3},{3,1},{4,6},{6,4},{5,7},{7,5},{8,10},{10,8},{9,1... | collective-permute-start | bytes 589832 | tf_op jit(solution)/shard_map/ppermute | solution.py:348
  26.9 1.3 %collective-permute-start.11 = (bf16[256,128]{1,0:T(8,128)(2,1)S(1)}, bf16[256,128]{1,0:T(8,128)(2,1)S(1)}, u32[]{:S(2)}, u32[]{:S(2)}) collective-permute-start(bf16[256,128]{1,0:T(8,128)(2,1)S(1)} %pad_maximum_fusion.1), channel_id=1, source_target_pairs={{0,2},{2,0},{1,3},{3,1},{4,6},{6,4},{5,7},{7,5},{8,10},{10,8},{9,1... | collective-permute-start | bytes 196616 | tf_op jit(solution)/shard_map/ppermute | solution.py:348
  34.4 4.0 %collective-permute-start.13 = (bf16[32,512]{1,0:T(8,128)(2,1)S(1)}, bf16[32,512]{1,0:T(8,128)(2,1)S(1)}, u32[]{:S(2)}, u32[]{:S(2)}) collective-permute-start(bf16[32,512]{1,0:T(8,128)(2,1)S(1)} %get-tuple-element.33), channel_id=1, source_target_pairs={{0,4},{1,5},{4,0},{5,1},{2,6},{3,7},{6,2},{7,3},{8,12},{9,13},{12,... | collective-permute-start | bytes 98312 | tf_op jit(solution)/shard_map/ppermute | solution.py:398
  36.5 4.8 %collective-permute-start.12 = (bf16[32,512]{1,0:T(8,128)(2,1)S(1)}, bf16[32,512]{1,0:T(8,128)(2,1)S(1)}, u32[]{:S(2)}, u32[]{:S(2)}) collective-permute-start(bf16[32,512]{1,0:T(8,128)(2,1)S(1)} %get-tuple-element.33), channel_id=1, source_target_pairs={{0,5},{1,4},{4,1},{5,0},{2,7},{3,6},{6,3},{7,2},{8,13},{9,12},{12,... | collective-permute-start | bytes 98312 | tf_op jit(solution)/shard_map/ppermute | solution.py:398
  37.5 4.1 %collective-permute-start.14 = (bf16[32,512]{1,0:T(8,128)(2,1)S(1)}, bf16[32,512]{1,0:T(8,128)(2,1)S(1)}, u32[]{:S(2)}, u32[]{:S(2)}) collective-permute-start(bf16[32,512]{1,0:T(8,128)(2,1)S(1)} %get-tuple-element.34.refs_3_), channel_id=1, source_target_pairs={{0,1},{1,0},{4,5},{5,4},{2,3},{3,2},{6,7},{7,6},{8,9},{9,8},{12,13... | collective-permute-start | bytes 98312 | tf_op jit(solution)/shard_map/ppermute | solution.py:398

commit v24 on v22

--- a/solution.py
+++ b/solution.py
@@ -375,7 +375,7 @@
     own = add(own, came_rest[quarter:])
     from_diagonal = swap_diagonal(to_diagonal)
     left, right, send_left, send_right = collect(
-        width * 3 // 4, own, from_diagonal, from_column, from_line
+        width // 2, own, from_diagonal, from_column, from_line
     )
     pieces = []
     for own, send in ((left, send_left), (right, send_right)):

time: 42.2 us -> 43 us (1.019)
  waiting for transfers between devices: 17.4 us -> 19.6 us
  starting transfers between devices: 15 us -> 13.7 us
    ppermute x11, waiting for transfers between devices: 14.1 us -> 16.2 us  [swap(): lax.ppermute(array, axis, [(i, i ^ mask) for i in range(lax.axis_size(axi...]
    ppermute x11, starting transfers between devices: 11.1 us -> 9.93 us  [swap(): lax.ppermute(array, axis, [(i, i ^ mask) for i in range(lax.axis_size(axi...]
  transfers between devices with their start and end apart: 15 -> 15, of which waited for: 8 -> 10; matrix products, arithmetic and copies ran while one was open for 0% -> 0% of each run, Pallas kernels for 2% -> 2%
where the time goes in v24:
time: 43 us; the launch traced here: 42.9 us
  waiting for transfers between devices  19.6 us (46%)
  starting transfers between devices  13.7 us (32%)
  Pallas kernels  9.36 us (22%)
    ppermute x11, waiting for transfers between devices, swap(): lax.ppermute(array, axis, [(i, i ^ mask) for i in range(lax.axis_size(axi...  16.2 us
    ppermute x11, starting transfers between devices, swap(): lax.ppermute(array, axis, [(i, i ^ mask) for i in range(lax.axis_size(axi...  9.93 us
    pallas_call x1, Pallas kernels, root(): pl.pallas_call(functools.partial(root_kernel, most), out_shape=[out, out]...  6.17 us
    ppermute x3, starting transfers between devices, pass_on(): return lax.ppermute(send if flip else keep, ('x', 'group'), moves)  3.55 us
    ppermute x3, waiting for transfers between devices, pass_on(): return lax.ppermute(send if flip else keep, ('x', 'group'), moves)  3.4 us
    pallas_call x1, Pallas kernels, load(): pl.pallas_call(functools.partial(load_kernel, scale), out_shape=[jax.Shap...  1.67 us
  transfers between devices with their start and end apart: 15, of which 10 were waited for; matrix products, arithmetic and copies ran while one was open for 0% of the time, Pallas kernels for 2%

profile of v24, /device:TPU:0, one launch (start us, length us, event | category | flops | bytes accessed | tf_op | source)
XLA Modules:
  0.0 42.9 jit_solution(10748623182878754586)
XLA Ops:
  0.0 1.7 %shard_map.37 = (bf16[128,512]{1,0:T(8,128)(2,1)S(1)}, bf16[128,512]{1,0:T(8,128)(2,1)S(1)}, bf16[2,2,512,256]{3,2,1,0:T(8,128)(2,1)S(1)}, bf16[2,512,512]{2,1,0:T(8,128)(2,1)S(1)}) custom-call(bf16[2,512,512]{2,1,0:T(8,128)(2,1)} %patch_hbm.1, bf16[2,512,512]{2,1,0:T(8,128)(2,1)} %cot_hbm.1), custom_call_target="tpu_custom_call" | custom-call | tf_op jit(solution)/shard_map/pallas_call | solution.py:70
  1.7 0.5 %collective-permute-start = (bf16[128,512]{1,0:T(8,128)(2,1)S(1)}, bf16[128,512]{1,0:T(8,128)(2,1)S(1)}, u32[]{:S(2)}, u32[]{:S(2)}) collective-permute-start(bf16[128,512]{1,0:T(8,128)(2,1)S(1)} %get-tuple-element.23), channel_id=1, source_target_pairs={{0,2},{2,0},{1,3},{3,1},{4,6},{6,4},{5,7},{7,5},{8,10},{10,8},{9,1... | collective-permute-start | bytes 393224 | tf_op jit(solution)/shard_map/ppermute | solution.py:348
  2.2 0.1 collective-permute-start.3
  2.3 0.5 %shard_map.38 = (f32[128,512]{1,0:T(8,128)S(1)}, f32[128,512]{1,0:T(8,128)S(1)}, bf16[256,512]{1,0:T(8,128)(2,1)S(1)}) custom-call(bf16[2,2,512,256]{3,2,1,0:T(8,128)(2,1)S(1)} %get-tuple-element.20.patch, bf16[2,512,512]{2,1,0:T(8,128)(2,1)S(1)} %get-tuple-element.21.cot), custom_call_target="tpu_custom_call" | custom-call | flops 402653184 | bytes 1048576 | tf_op jit(solution)/shard_map/pallas_call | solution.py:98
  2.7 0.5 %collective-permute-start.1 = (bf16[256,512]{1,0:T(8,128)(2,1)S(1)}, bf16[256,512]{1,0:T(8,128)(2,1)S(1)}, u32[]{:S(2)}, u32[]{:S(2)}) collective-permute-start(bf16[256,512]{1,0:T(8,128)(2,1)S(1)} %get-tuple-element.25), channel_id=1, source_target_pairs={{0,2},{2,0},{1,3},{3,1},{4,6},{6,4},{5,7},{7,5},{8,10},{10,8},{9,1... | collective-permute-start | bytes 786440 | tf_op jit(solution)/shard_map/ppermute | solution.py:348
  3.2 0.0 collective-permute-done
  3.3 2.9 %collective-permute-start.5 = (bf16[128,512]{1,0:T(8,128)(2,1)S(1)}, bf16[128,512]{1,0:T(8,128)(2,1)S(1)}, u32[]{:S(2)}, u32[]{:S(2)}) collective-permute-start(bf16[128,512]{1,0:T(8,128)(2,1)S(1)} %add_convert_fusion.2.refs_0_), channel_id=1, source_target_pairs={{0,8},{8,0},{16,24},{24,16},{1,9},{9,1},{17,25},{25,17},{2,10},{10... | collective-permute-start | bytes 393224 | tf_op jit(solution)/shard_map/ppermute | solution.py:348
  6.2 0.0 collective-permute-done.3
  6.3 1.6 %collective-permute-start.4 = (bf16[128,512]{1,0:T(8,128)(2,1)S(1)}, bf16[128,512]{1,0:T(8,128)(2,1)S(1)}, u32[]{:S(2)}, u32[]{:S(2)}) collective-permute-start(bf16[128,512]{1,0:T(8,128)(2,1)S(1)} %add_convert_fusion), channel_id=1, source_target_pairs={{0,4},{4,0},{1,5},{5,1},{2,6},{6,2},{3,7},{7,3},{8,12},{12,8},{9,1... | collective-permute-start | bytes 393224 | tf_op jit(solution)/shard_map/ppermute | solution.py:348
  7.8 0.3 shard_map.39
  8.1 0.0 collective-permute-done.1
  8.1 0.1 add_convert_fusion.1
  8.2 0.2 collective-permute-start.2
  8.4 1.7 %collective-permute-done.5.refs_2_ = bf16[128,512]{1,0:T(8,128)(2,1)S(1)} collective-permute-done((bf16[128,512]{1,0:T(8,128)(2,1)S(1)}, bf16[128,512]{1,0:T(8,128)(2,1)S(1)}, u32[]{:S(2)}, u32[]{:S(2)}) %collective-permute-start.5) | collective-permute-done | bytes 131104 | tf_op jit(solution)/shard_map/ppermute | solution.py:348
  10.1 4.4 %collective-permute-done.4.refs_1_ = bf16[128,512]{1,0:T(8,128)(2,1)S(1)} collective-permute-done((bf16[128,512]{1,0:T(8,128)(2,1)S(1)}, bf16[128,512]{1,0:T(8,128)(2,1)S(1)}, u32[]{:S(2)}, u32[]{:S(2)}) %collective-permute-start.4) | collective-permute-done | bytes 131104 | tf_op jit(solution)/shard_map/ppermute | solution.py:348
  14.5 0.0 collective-permute-done.2.refs_0_
  14.5 0.1 shard_map.40
  14.5 2.7 %collective-permute-start.6 = (bf16[128,256]{1,0:T(8,128)(2,1)S(1)}, bf16[128,256]{1,0:T(8,128)(2,1)S(1)}, u32[]{:S(2)}, u32[]{:S(2)}) collective-permute-start(bf16[128,256]{1,0:T(8,128)(2,1)S(1)} %get-tuple-element.30), channel_id=1, source_target_pairs={{0,16},{8,24},{16,0},{24,8},{1,17},{9,25},{17,1},{25,9},{2,18},{10... | collective-permute-start | bytes 196616 | tf_op jit(solution)/shard_map/ppermute | solution.py:348
  17.2 0.3 collective-permute-start.9
  17.5 4.4 %collective-permute-done.6 = bf16[128,256]{1,0:T(8,128)(2,1)S(1)} collective-permute-done((bf16[128,256]{1,0:T(8,128)(2,1)S(1)}, bf16[128,256]{1,0:T(8,128)(2,1)S(1)}, u32[]{:S(2)}, u32[]{:S(2)}) %collective-permute-start.6) | collective-permute-done | bytes 65568 | tf_op jit(solution)/shard_map/ppermute | solution.py:348
  21.9 0.4 collective-permute-start.7
  22.3 1.0 %collective-permute-done.9 = bf16[128,256]{1,0:T(8,128)(2,1)S(1)} collective-permute-done((bf16[128,256]{1,0:T(8,128)(2,1)S(1)}, bf16[128,256]{1,0:T(8,128)(2,1)S(1)}, u32[]{:S(2)}, u32[]{:S(2)}) %collective-permute-start.9) | collective-permute-done | bytes 65568 | tf_op jit(solution)/shard_map/ppermute | solution.py:348
  23.3 0.8 %collective-permute-start.10 = (bf16[128,256]{1,0:T(8,128)(2,1)S(1)}, bf16[128,256]{1,0:T(8,128)(2,1)S(1)}, u32[]{:S(2)}, u32[]{:S(2)}) collective-permute-start(bf16[128,256]{1,0:T(8,128)(2,1)S(1)} %add_convert_fusion.3.refs_3_), channel_id=1, source_target_pairs={{0,8},{8,0},{16,24},{24,16},{1,9},{9,1},{17,25},{25,17},{2,10},{10... | collective-permute-start | bytes 196616 | tf_op jit(solution)/shard_map/ppermute | solution.py:348
  24.1 2.2 %collective-permute-done.7.refs_1_ = bf16[128,256]{1,0:T(8,128)(2,1)S(1)} collective-permute-done((bf16[128,256]{1,0:T(8,128)(2,1)S(1)}, bf16[128,256]{1,0:T(8,128)(2,1)S(1)}, u32[]{:S(2)}, u32[]{:S(2)}) %collective-permute-start.7) | collective-permute-done | bytes 65568 | tf_op jit(solution)/shard_map/ppermute | solution.py:348
  26.3 0.1 collective-permute-start.8
  26.4 1.3 %collective-permute-done.10.refs_4_ = bf16[128,256]{1,0:T(8,128)(2,1)S(1)} collective-permute-done((bf16[128,256]{1,0:T(8,128)(2,1)S(1)}, bf16[128,256]{1,0:T(8,128)(2,1)S(1)}, u32[]{:S(2)}, u32[]{:S(2)}) %collective-permute-start.10) | collective-permute-done | bytes 65568 | tf_op jit(solution)/shard_map/ppermute | solution.py:348
  27.6 0.1 collective-permute-start.11
  27.7 0.0 collective-permute-done.8.refs_2_
  27.7 1.3 %collective-permute-done.11.refs_5_ = bf16[256,256]{1,0:T(8,128)(2,1)S(1)} collective-permute-done((bf16[256,256]{1,0:T(8,128)(2,1)S(1)}, bf16[256,256]{1,0:T(8,128)(2,1)S(1)}, u32[]{:S(2)}, u32[]{:S(2)}) %collective-permute-start.11) | collective-permute-done | bytes 131104 | tf_op jit(solution)/shard_map/ppermute | solution.py:348
  29.1 6.2 %shard_map.41 = (bf16[32,512]{1,0:T(8,128)(2,1)S(1)}, bf16[32,512]{1,0:T(8,128)(2,1)S(1)}) custom-call(s32[2,2]{1,0:T(2,128)} %counts_hbm.1, bf16[128,256]{1,0:T(8,128)(2,1)S(1)} %add_convert_fusion.4.refs_0_, bf16[128,256]{1,0:T(8,128)(2,1)S(1)} %collective-permute-done.7.refs_1_, bf16[256,256]{1,0:T(8,128)(2,1)S(1)} %collective-permute-done.8.refs_2_, ...), custom_call_target="tpu_custom_call" | custom-call | tf_op jit(solution)/shard_map/pallas_call | solution.py:295
  35.2 2.4 %collective-permute-start.14 = (bf16[32,512]{1,0:T(8,128)(2,1)S(1)}, bf16[32,512]{1,0:T(8,128)(2,1)S(1)}, u32[]{:S(2)}, u32[]{:S(2)}) collective-permute-start(bf16[32,512]{1,0:T(8,128)(2,1)S(1)} %get-tuple-element.33), channel_id=1, source_target_pairs={{0,5},{1,4},{4,1},{5,0},{2,7},{3,6},{6,3},{7,2},{8,13},{9,12},{12,... | collective-permute-start | bytes 98312 | tf_op jit(solution)/shard_map/ppermute | solution.py:398
  37.6 0.6 %collective-permute-start.12 = (bf16[32,512]{1,0:T(8,128)(2,1)S(1)}, bf16[32,512]{1,0:T(8,128)(2,1)S(1)}, u32[]{:S(2)}, u32[]{:S(2)}) collective-permute-start(bf16[32,512]{1,0:T(8,128)(2,1)S(1)} %get-tuple-element.33), channel_id=1, source_target_pairs={{0,4},{1,5},{4,0},{5,1},{2,6},{3,7},{6,2},{7,3},{8,12},{9,13},{12,... | collective-permute-start | bytes 98312 | tf_op jit(solution)/shard_map/ppermute | solution.py:398
  38.3 0.5 %collective-permute-start.13 = (bf16[32,512]{1,0:T(8,128)(2,1)S(1)}, bf16[32,512]{1,0:T(8,128)(2,1)S(1)}, u32[]{:S(2)}, u32[]{:S(2)}) collective-permute-start(bf16[32,512]{1,0:T(8,128)(2,1)S(1)} %get-tuple-element.34.refs_3_), channel_id=1, source_target_pairs={{0,1},{1,0},{4,5},{5,4},{2,3},{3,2},{6,7},{7,6},{8,9},{9,8},{12,13... | collective-permute-start | bytes 98312 | tf_op jit(solution)/shard_map/ppermute | solution.py:398
  38.8 1.4 %collective-permute-done.14.refs_2_ = bf16[32,512]{1,0:T(8,128)(2,1)S(1)} collective-permute-done((bf16[32,512]{1,0:T(8,128)(2,1)S(1)}, bf16[32,512]{1,0:T(8,128)(2,1)S(1)}, u32[]{:S(2)}, u32[]{:S(2)}) %collective-permute-start.14) | collective-permute-done | bytes 32800 | tf_op jit(solution)/shard_map/ppermute | solution.py:398
  40.2 1.4 %collective-permute-done.12.refs_0_ = bf16[32,512]{1,0:T(8,128)(2,1)S(1)} collective-permute-done((bf16[32,512]{1,0:T(8,128)(2,1)S(1)}, bf16[32,512]{1,0:T(8,128)(2,1)S(1)}, u32[]{:S(2)}, u32[]{:S(2)}) %collective-permute-start.12) | collective-permute-done | bytes 32800 | tf_op jit(solution)/shard_map/ppermute | solution.py:398
  41.6 0.6 %collective-permute-done.13.refs_1_ = bf16[32,512]{1,0:T(8,128)(2,1)S(1)} collective-permute-done((bf16[32,512]{1,0:T(8,128)(2,1)S(1)}, bf16[32,512]{1,0:T(8,128)(2,1)S(1)}, u32[]{:S(2)}, u32[]{:S(2)}) %collective-permute-start.13) | collective-permute-done | bytes 32800 | tf_op jit(solution)/shard_map/ppermute | solution.py:398
  42.2 0.7 %shard_map.42 = bf16[4,32,512]{2,1,0:T(8,128)(2,1)} custom-call(bf16[32,512]{1,0:T(8,128)(2,1)S(1)} %collective-permute-done.12.refs_0_, bf16[32,512]{1,0:T(8,128)(2,1)S(1)} %collective-permute-done.13.refs_1_, bf16[32,512]{1,0:T(8,128)(2,1)S(1)} %collective-permute-done.14.refs_2_, bf16[32,512]{1,0:T(8,128)(2,1)S(1)} %get-tuple-element.34.refs_3_), custom_call_target="tpu_custom_call" | custom-call | tf_op jit(solution)/shard_map/pallas_call | solution.py:331
  (6 shorter events, 0.1 us)
Async XLA Ops:
  1.7 1.6 %collective-permute-start = (bf16[128,512]{1,0:T(8,128)(2,1)S(1)}, bf16[128,512]{1,0:T(8,128)(2,1)S(1)}, u32[]{:S(2)}, u32[]{:S(2)}) collective-permute-start(bf16[128,512]{1,0:T(8,128)(2,1)S(1)} %get-tuple-element.23), channel_id=1, source_target_pairs={{0,2},{2,0},{1,3},{3,1},{4,6},{6,4},{5,7},{7,5},{8,10},{10,8},{9,1... | collective-permute-start | bytes 393224 | tf_op jit(solution)/shard_map/ppermute | solution.py:348
  2.2 4.0 %collective-permute-start.3 = (bf16[128,512]{1,0:T(8,128)(2,1)S(1)}, bf16[128,512]{1,0:T(8,128)(2,1)S(1)}, u32[]{:S(2)}, u32[]{:S(2)}) collective-permute-start(bf16[128,512]{1,0:T(8,128)(2,1)S(1)} %get-tuple-element.28), channel_id=1, source_target_pairs={{0,2},{2,0},{1,3},{3,1},{4,6},{6,4},{5,7},{7,5},{8,10},{10,8},{9,1... | collective-permute-start | bytes 393224 | tf_op jit(solution)/shard_map/ppermute | solution.py:348
  2.7 5.4 %collective-permute-start.1 = (bf16[256,512]{1,0:T(8,128)(2,1)S(1)}, bf16[256,512]{1,0:T(8,128)(2,1)S(1)}, u32[]{:S(2)}, u32[]{:S(2)}) collective-permute-start(bf16[256,512]{1,0:T(8,128)(2,1)S(1)} %get-tuple-element.25), channel_id=1, source_target_pairs={{0,2},{2,0},{1,3},{3,1},{4,6},{6,4},{5,7},{7,5},{8,10},{10,8},{9,1... | collective-permute-start | bytes 786440 | tf_op jit(solution)/shard_map/ppermute | solution.py:348
  3.3 6.8 %collective-permute-start.5 = (bf16[128,512]{1,0:T(8,128)(2,1)S(1)}, bf16[128,512]{1,0:T(8,128)(2,1)S(1)}, u32[]{:S(2)}, u32[]{:S(2)}) collective-permute-start(bf16[128,512]{1,0:T(8,128)(2,1)S(1)} %add_convert_fusion.2.refs_0_), channel_id=1, source_target_pairs={{0,8},{8,0},{16,24},{24,16},{1,9},{9,1},{17,25},{25,17},{2,10},{10... | collective-permute-start | bytes 393224 | tf_op jit(solution)/shard_map/ppermute | solution.py:348
  6.3 8.2 %collective-permute-start.4 = (bf16[128,512]{1,0:T(8,128)(2,1)S(1)}, bf16[128,512]{1,0:T(8,128)(2,1)S(1)}, u32[]{:S(2)}, u32[]{:S(2)}) collective-permute-start(bf16[128,512]{1,0:T(8,128)(2,1)S(1)} %add_convert_fusion), channel_id=1, source_target_pairs={{0,4},{4,0},{1,5},{5,1},{2,6},{6,2},{3,7},{7,3},{8,12},{12,8},{9,1... | collective-permute-start | bytes 393224 | tf_op jit(solution)/shard_map/ppermute | solution.py:348
  8.2 6.2 %collective-permute-start.2 = (bf16[128,512]{1,0:T(8,128)(2,1)S(1)}, bf16[128,512]{1,0:T(8,128)(2,1)S(1)}, u32[]{:S(2)}, u32[]{:S(2)}) collective-permute-start(bf16[128,512]{1,0:T(8,128)(2,1)S(1)} %get-tuple-element.35), channel_id=1, source_target_pairs={{0,12},{4,8},{8,4},{12,0},{16,28},{20,24},{24,20},{28,16},{1,13},{... | collective-permute-start | bytes 393224 | tf_op jit(solution)/shard_map/ppermute | solution.py:352
  14.5 7.4 %collective-permute-start.6 = (bf16[128,256]{1,0:T(8,128)(2,1)S(1)}, bf16[128,256]{1,0:T(8,128)(2,1)S(1)}, u32[]{:S(2)}, u32[]{:S(2)}) collective-permute-start(bf16[128,256]{1,0:T(8,128)(2,1)S(1)} %get-tuple-element.30), channel_id=1, source_target_pairs={{0,16},{8,24},{16,0},{24,8},{1,17},{9,25},{17,1},{25,9},{2,18},{10... | collective-permute-start | bytes 196616 | tf_op jit(solution)/shard_map/ppermute | solution.py:348
  17.2 6.1 %collective-permute-start.9 = (bf16[128,256]{1,0:T(8,128)(2,1)S(1)}, bf16[128,256]{1,0:T(8,128)(2,1)S(1)}, u32[]{:S(2)}, u32[]{:S(2)}) collective-permute-start(bf16[128,256]{1,0:T(8,128)(2,1)S(1)} %get-tuple-element.32), channel_id=1, source_target_pairs={{0,16},{8,24},{16,0},{24,8},{1,17},{9,25},{17,1},{25,9},{2,18},{10... | collective-permute-start | bytes 196616 | tf_op jit(solution)/shard_map/ppermute | solution.py:348
  21.9 4.3 %collective-permute-start.7 = (bf16[128,256]{1,0:T(8,128)(2,1)S(1)}, bf16[128,256]{1,0:T(8,128)(2,1)S(1)}, u32[]{:S(2)}, u32[]{:S(2)}) collective-permute-start(bf16[128,256]{1,0:T(8,128)(2,1)S(1)} %add_convert_fusion.4.refs_0_), channel_id=1, source_target_pairs={{0,8},{8,0},{16,24},{24,16},{1,9},{9,1},{17,25},{25,17},{2,10},{10... | collective-permute-start | bytes 196616 | tf_op jit(solution)/shard_map/ppermute | solution.py:348
  23.3 4.3 %collective-permute-start.10 = (bf16[128,256]{1,0:T(8,128)(2,1)S(1)}, bf16[128,256]{1,0:T(8,128)(2,1)S(1)}, u32[]{:S(2)}, u32[]{:S(2)}) collective-permute-start(bf16[128,256]{1,0:T(8,128)(2,1)S(1)} %add_convert_fusion.3.refs_3_), channel_id=1, source_target_pairs={{0,8},{8,0},{16,24},{24,16},{1,9},{9,1},{17,25},{25,17},{2,10},{10... | collective-permute-start | bytes 196616 | tf_op jit(solution)/shard_map/ppermute | solution.py:348
  26.3 1.4 %collective-permute-start.8 = (bf16[256,256]{1,0:T(8,128)(2,1)S(1)}, bf16[256,256]{1,0:T(8,128)(2,1)S(1)}, u32[]{:S(2)}, u32[]{:S(2)}) collective-permute-start(bf16[256,256]{1,0:T(8,128)(2,1)S(1)} %pad_maximum_fusion), channel_id=1, source_target_pairs={{0,2},{2,0},{1,3},{3,1},{4,6},{6,4},{5,7},{7,5},{8,10},{10,8},{9,1... | collective-permute-start | bytes 393224 | tf_op jit(solution)/shard_map/ppermute | solution.py:348
  27.6 1.4 %collective-permute-start.11 = (bf16[256,256]{1,0:T(8,128)(2,1)S(1)}, bf16[256,256]{1,0:T(8,128)(2,1)S(1)}, u32[]{:S(2)}, u32[]{:S(2)}) collective-permute-start(bf16[256,256]{1,0:T(8,128)(2,1)S(1)} %pad_maximum_fusion.1), channel_id=1, source_target_pairs={{0,2},{2,0},{1,3},{3,1},{4,6},{6,4},{5,7},{7,5},{8,10},{10,8},{9,1... | collective-permute-start | bytes 393224 | tf_op jit(solution)/shard_map/ppermute | solution.py:348
  35.2 4.9 %collective-permute-start.14 = (bf16[32,512]{1,0:T(8,128)(2,1)S(1)}, bf16[32,512]{1,0:T(8,128)(2,1)S(1)}, u32[]{:S(2)}, u32[]{:S(2)}) collective-permute-start(bf16[32,512]{1,0:T(8,128)(2,1)S(1)} %get-tuple-element.33), channel_id=1, source_target_pairs={{0,5},{1,4},{4,1},{5,0},{2,7},{3,6},{6,3},{7,2},{8,13},{9,12},{12,... | collective-permute-start | bytes 98312 | tf_op jit(solution)/shard_map/ppermute | solution.py:398
  37.6 3.9 %collective-permute-start.12 = (bf16[32,512]{1,0:T(8,128)(2,1)S(1)}, bf16[32,512]{1,0:T(8,128)(2,1)S(1)}, u32[]{:S(2)}, u32[]{:S(2)}) collective-permute-start(bf16[32,512]{1,0:T(8,128)(2,1)S(1)} %get-tuple-element.33), channel_id=1, source_target_pairs={{0,4},{1,5},{4,0},{5,1},{2,6},{3,7},{6,2},{7,3},{8,12},{9,13},{12,... | collective-permute-start | bytes 98312 | tf_op jit(solution)/shard_map/ppermute | solution.py:398
  38.3 3.9 %collective-permute-start.13 = (bf16[32,512]{1,0:T(8,128)(2,1)S(1)}, bf16[32,512]{1,0:T(8,128)(2,1)S(1)}, u32[]{:S(2)}, u32[]{:S(2)}) collective-permute-start(bf16[32,512]{1,0:T(8,128)(2,1)S(1)} %get-tuple-element.34.refs_3_), channel_id=1, source_target_pairs={{0,1},{1,0},{4,5},{5,4},{2,3},{3,2},{6,7},{7,6},{8,9},{9,8},{12,13... | collective-permute-start | bytes 98312 | tf_op jit(solution)/shard_map/ppermute | solution.py:398

commit v25 on v18

--- a/solution.py
+++ b/solution.py
@@ -226,8 +226,9 @@
     for index in range(1, most):
         q_left, q_right = left.at[picked:, :], right.at[width:, :]
         if index == 1:
-            fill(s_left, 0, square(q_left))
-            fill(s_right, 0, square(q_right))
+            seconds = square(q_left), square(q_right)
+            fill(s_left, 0, seconds[0])
+            fill(s_right, 0, seconds[1])
         else:
             by_high = dot(left[...], q_left[:, high])
             by_low = dot(left[: picked + half, :], q_left[:, low])
@@ -255,15 +256,16 @@
         fourths = square(s_left), square(s_right)
         fill(s_left, 0, fourths[0])
         fill(s_right, 0, fourths[1])
-        for fourth, moment_ref, ref, start in (
-            (s_left, m_left, left, picked),
-            (s_right, m_right, right, width),
-        ):
+        moments = []
+        for fourth, moment_ref in ((s_left, m_left), (s_right, m_right)):
             by_high = dot(fourth[...], moment_ref[:, high])
-            tiles = (dot(fourth[low, :], moment_ref[:, low]), by_high[low], by_high[high])
-            if index < most - 1:
-                fill(moment_ref, 0, tiles)
-            fill(ref, start, factor(tiles))
+            by_low = dot(fourth[low, :], moment_ref[:, low])
+            moments.append((by_low, by_high[low], by_high[high]))
+        fill(left, picked, factor(moments[0]))
+        fill(right, width, factor(moments[1]))
+        if index < most - 1:
+            fill(m_left, 0, moments[0])
+            fill(m_right, 0, moments[1])
     final_left = dot(left[:picked, :], left[picked:, :]).astype(BF16)
     final_left = jnp.where(most <= count_left, final_left, left[:picked, :])
     by_high = dot(right[:width, :], right[width:, high])
@@ -381,7 +383,7 @@
         ]
         return lax.ppermute(send if flip else keep, ("x", "group"), moves)
 
-    others = [(turn, flip) for flip in (0, 1) for turn in range(groups) if turn or flip]
+    others = [(turn, flip) for turn in range(groups) for flip in range(2) if turn or flip]
     found = {(turn, flip): pass_on(turn, flip) for turn, flip in others}
     found[0, 0] = keep
     return place(found)

time: 42.3 us -> 42.3 us (level)
  no operation moved by 1% of the time
where the time goes in v25:
time: 42.3 us; the launch traced here: 42.2 us
  waiting for transfers between devices  17.8 us (42%)
  starting transfers between devices  14.8 us (35%)
  Pallas kernels  9.29 us (22%)
    ppermute x11, waiting for transfers between devices, swap(): lax.ppermute(array, axis, [(i, i ^ mask) for i in range(lax.axis_size(axi...  13.3 us
    ppermute x11, starting transfers between devices, swap(): lax.ppermute(array, axis, [(i, i ^ mask) for i in range(lax.axis_size(axi...  9.59 us
    pallas_call x1, Pallas kernels, root(): pl.pallas_call(functools.partial(root_kernel, most), out_shape=[out, out]...  6.15 us
    ppermute x3, starting transfers between devices, pass_on(): return lax.ppermute(send if flip else keep, ('x', 'group'), moves)  3.55 us
    ppermute x3, waiting for transfers between devices, pass_on(): return lax.ppermute(send if flip else keep, ('x', 'group'), moves)  3.12 us
    ppermute x1, starting transfers between devices, swap_diagonal(): return lax.ppermute(array, ('z', 'x'), moves)  1.61 us
    pallas_call x1, Pallas kernels, load(): pl.pallas_call(functools.partial(load_kernel, scale), out_shape=[jax.Shap...  1.61 us
    ppermute x1, waiting for transfers between devices, swap_diagonal(): return lax.ppermute(array, ('z', 'x'), moves)  1.39 us
  transfers between devices with their start and end apart: 15, of which 10 were waited for; matrix products, arithmetic and copies ran while one was open for 0% of the time, Pallas kernels for 2%

profile of v25, /device:TPU:0, one launch (start us, length us, event | category | flops | bytes accessed | tf_op | source)
XLA Modules:
  0.0 42.2 jit_solution(7205289697617958939)
XLA Ops:
  0.0 1.6 %shard_map.37 = (bf16[128,512]{1,0:T(8,128)(2,1)S(1)}, bf16[128,512]{1,0:T(8,128)(2,1)S(1)}, bf16[2,2,512,256]{3,2,1,0:T(8,128)(2,1)S(1)}, bf16[2,512,512]{2,1,0:T(8,128)(2,1)S(1)}) custom-call(bf16[2,512,512]{2,1,0:T(8,128)(2,1)} %patch_hbm.1, bf16[2,512,512]{2,1,0:T(8,128)(2,1)} %cot_hbm.1), custom_call_target="tpu_custom_call" | custom-call | tf_op jit(solution)/shard_map/pallas_call | solution.py:69
  1.6 0.5 %collective-permute-start = (bf16[128,512]{1,0:T(8,128)(2,1)S(1)}, bf16[128,512]{1,0:T(8,128)(2,1)S(1)}, u32[]{:S(2)}, u32[]{:S(2)}) collective-permute-start(bf16[128,512]{1,0:T(8,128)(2,1)S(1)} %get-tuple-element.21), channel_id=1, source_target_pairs={{0,2},{2,0},{1,3},{3,1},{4,6},{6,4},{5,7},{7,5},{8,10},{10,8},{9,1... | collective-permute-start | bytes 393224 | tf_op jit(solution)/shard_map/ppermute | solution.py:344
  2.1 0.1 collective-permute-start.2
  2.2 0.5 %shard_map.38 = (f32[128,512]{1,0:T(8,128)S(1)}, f32[128,512]{1,0:T(8,128)S(1)}, bf16[256,512]{1,0:T(8,128)(2,1)S(1)}) custom-call(bf16[2,2,512,256]{3,2,1,0:T(8,128)(2,1)S(1)} %get-tuple-element.18.patch, bf16[2,512,512]{2,1,0:T(8,128)(2,1)S(1)} %get-tuple-element.19.cot), custom_call_target="tpu_custom_call" | custom-call | flops 402653184 | bytes 1048576 | tf_op jit(solution)/shard_map/pallas_call | solution.py:94
  2.7 0.5 %collective-permute-start.1 = (bf16[256,512]{1,0:T(8,128)(2,1)S(1)}, bf16[256,512]{1,0:T(8,128)(2,1)S(1)}, u32[]{:S(2)}, u32[]{:S(2)}) collective-permute-start(bf16[256,512]{1,0:T(8,128)(2,1)S(1)} %get-tuple-element.22), channel_id=1, source_target_pairs={{0,2},{2,0},{1,3},{3,1},{4,6},{6,4},{5,7},{7,5},{8,10},{10,8},{9,1... | collective-permute-start | bytes 786440 | tf_op jit(solution)/shard_map/ppermute | solution.py:344
  3.2 0.0 collective-permute-done
  3.2 2.9 %collective-permute-start.4 = (bf16[128,512]{1,0:T(8,128)(2,1)S(1)}, bf16[128,512]{1,0:T(8,128)(2,1)S(1)}, u32[]{:S(2)}, u32[]{:S(2)}) collective-permute-start(bf16[128,512]{1,0:T(8,128)(2,1)S(1)} %add_convert_fusion.1.refs_0_), channel_id=1, source_target_pairs={{0,4},{4,0},{1,5},{5,1},{2,6},{6,2},{3,7},{7,3},{8,12},{12,8},{9,1... | collective-permute-start | bytes 393224 | tf_op jit(solution)/shard_map/ppermute | solution.py:344
  6.1 0.0 collective-permute-done.2
  6.1 1.6 %collective-permute-start.3 = (bf16[128,512]{1,0:T(8,128)(2,1)S(1)}, bf16[128,512]{1,0:T(8,128)(2,1)S(1)}, u32[]{:S(2)}, u32[]{:S(2)}) collective-permute-start(bf16[128,512]{1,0:T(8,128)(2,1)S(1)} %add_convert_fusion), channel_id=1, source_target_pairs={{0,12},{4,8},{8,4},{12,0},{16,28},{20,24},{24,20},{28,16},{1,13},{... | collective-permute-start | bytes 393224 | tf_op jit(solution)/shard_map/ppermute | solution.py:348
  7.7 0.3 shard_map.39
  8.0 0.0 collective-permute-done.1
  8.0 0.1 convert_add_fusion.own
  8.2 0.1 collective-permute-start.5
  8.3 3.8 %collective-permute-done.4.refs_1_ = bf16[128,512]{1,0:T(8,128)(2,1)S(1)} collective-permute-done((bf16[128,512]{1,0:T(8,128)(2,1)S(1)}, bf16[128,512]{1,0:T(8,128)(2,1)S(1)}, u32[]{:S(2)}, u32[]{:S(2)}) %collective-permute-start.4) | collective-permute-done | bytes 131104 | tf_op jit(solution)/shard_map/ppermute | solution.py:344
  12.1 1.4 %collective-permute-done.3.refs_0_ = bf16[128,512]{1,0:T(8,128)(2,1)S(1)} collective-permute-done((bf16[128,512]{1,0:T(8,128)(2,1)S(1)}, bf16[128,512]{1,0:T(8,128)(2,1)S(1)}, u32[]{:S(2)}, u32[]{:S(2)}) %collective-permute-start.3) | collective-permute-done | bytes 131104 | tf_op jit(solution)/shard_map/ppermute | solution.py:348
  13.4 0.8 %collective-permute-done.5.refs_2_ = bf16[128,512]{1,0:T(8,128)(2,1)S(1)} collective-permute-done((bf16[128,512]{1,0:T(8,128)(2,1)S(1)}, bf16[128,512]{1,0:T(8,128)(2,1)S(1)}, u32[]{:S(2)}, u32[]{:S(2)}) %collective-permute-start.5) | collective-permute-done | bytes 131104 | tf_op jit(solution)/shard_map/ppermute | solution.py:344
  14.3 0.1 shard_map.40
  14.3 2.7 %collective-permute-start.6 = (bf16[128,384]{1,0:T(8,128)(2,1)S(1)}, bf16[128,384]{1,0:T(8,128)(2,1)S(1)}, u32[]{:S(2)}, u32[]{:S(2)}) collective-permute-start(bf16[128,384]{1,0:T(8,128)(2,1)S(1)} %get-tuple-element.26), channel_id=1, source_target_pairs={{0,16},{8,24},{16,0},{24,8},{1,17},{9,25},{17,1},{25,9},{2,18},{10... | collective-permute-start | bytes 294920 | tf_op jit(solution)/shard_map/ppermute | solution.py:344
  17.0 0.3 collective-permute-start.9
  17.3 5.0 %collective-permute-done.6 = bf16[128,384]{1,0:T(8,128)(2,1)S(1)} collective-permute-done((bf16[128,384]{1,0:T(8,128)(2,1)S(1)}, bf16[128,384]{1,0:T(8,128)(2,1)S(1)}, u32[]{:S(2)}, u32[]{:S(2)}) %collective-permute-start.6) | collective-permute-done | bytes 98336 | tf_op jit(solution)/shard_map/ppermute | solution.py:344
  22.3 0.8 %collective-permute-start.7 = (bf16[128,384]{1,0:T(8,128)(2,1)S(1)}, bf16[128,384]{1,0:T(8,128)(2,1)S(1)}, u32[]{:S(2)}, u32[]{:S(2)}) collective-permute-start(bf16[128,384]{1,0:T(8,128)(2,1)S(1)} %add_convert_fusion.2.refs_0_), channel_id=1, source_target_pairs={{0,8},{8,0},{16,24},{24,16},{1,9},{9,1},{17,25},{25,17},{2,10},{10... | collective-permute-start | bytes 294920 | tf_op jit(solution)/shard_map/ppermute | solution.py:344
  23.1 0.0 collective-permute-done.9
  23.1 1.4 %collective-permute-start.10 = (bf16[128,128]{1,0:T(8,128)(2,1)S(1)}, bf16[128,128]{1,0:T(8,128)(2,1)S(1)}, u32[]{:S(2)}, u32[]{:S(2)}) collective-permute-start(bf16[128,128]{1,0:T(8,128)(2,1)S(1)} %add_convert_fusion.3.refs_3_), channel_id=1, source_target_pairs={{0,8},{8,0},{16,24},{24,16},{1,9},{9,1},{17,25},{25,17},{2,10},{10... | collective-permute-start | bytes 98312 | tf_op jit(solution)/shard_map/ppermute | solution.py:344
  24.5 2.5 %collective-permute-done.7.refs_1_ = bf16[128,384]{1,0:T(8,128)(2,1)S(1)} collective-permute-done((bf16[128,384]{1,0:T(8,128)(2,1)S(1)}, bf16[128,384]{1,0:T(8,128)(2,1)S(1)}, u32[]{:S(2)}, u32[]{:S(2)}) %collective-permute-start.7) | collective-permute-done | bytes 98336 | tf_op jit(solution)/shard_map/ppermute | solution.py:344
  27.0 0.1 collective-permute-start.8
  27.1 0.2 collective-permute-done.10.refs_4_
  27.4 0.3 collective-permute-start.11
  27.7 0.9 %collective-permute-done.11.refs_5_ = bf16[256,128]{1,0:T(8,128)(2,1)S(1)} collective-permute-done((bf16[256,128]{1,0:T(8,128)(2,1)S(1)}, bf16[256,128]{1,0:T(8,128)(2,1)S(1)}, u32[]{:S(2)}, u32[]{:S(2)}) %collective-permute-start.11) | collective-permute-done | bytes 65568 | tf_op jit(solution)/shard_map/ppermute | solution.py:344
  28.6 0.0 collective-permute-done.8.refs_2_
  28.6 6.2 %shard_map.41 = (bf16[32,512]{1,0:T(8,128)(2,1)S(1)}, bf16[32,512]{1,0:T(8,128)(2,1)S(1)}) custom-call(s32[2,2]{1,0:T(2,128)} %counts_hbm.1, bf16[128,384]{1,0:T(8,128)(2,1)S(1)} %add_convert_fusion.2.refs_0_, bf16[128,384]{1,0:T(8,128)(2,1)S(1)} %collective-permute-done.7.refs_1_, bf16[256,384]{1,0:T(8,128)(2,1)S(1)} %collective-permute-done.8.refs_2_, ...), custom_call_target="tpu_custom_call" | custom-call | tf_op jit(solution)/shard_map/pallas_call | solution.py:291
  34.8 2.2 %collective-permute-start.14 = (bf16[32,512]{1,0:T(8,128)(2,1)S(1)}, bf16[32,512]{1,0:T(8,128)(2,1)S(1)}, u32[]{:S(2)}, u32[]{:S(2)}) collective-permute-start(bf16[32,512]{1,0:T(8,128)(2,1)S(1)} %get-tuple-element.29), channel_id=1, source_target_pairs={{0,5},{1,4},{4,1},{5,0},{2,7},{3,6},{6,3},{7,2},{8,13},{9,12},{12,... | collective-permute-start | bytes 98312 | tf_op jit(solution)/shard_map/ppermute | solution.py:384
  37.0 0.5 %collective-permute-start.12 = (bf16[32,512]{1,0:T(8,128)(2,1)S(1)}, bf16[32,512]{1,0:T(8,128)(2,1)S(1)}, u32[]{:S(2)}, u32[]{:S(2)}) collective-permute-start(bf16[32,512]{1,0:T(8,128)(2,1)S(1)} %get-tuple-element.29), channel_id=1, source_target_pairs={{0,4},{1,5},{4,0},{5,1},{2,6},{3,7},{6,2},{7,3},{8,12},{9,13},{12,... | collective-permute-start | bytes 98312 | tf_op jit(solution)/shard_map/ppermute | solution.py:384
  37.6 0.8 %collective-permute-start.13 = (bf16[32,512]{1,0:T(8,128)(2,1)S(1)}, bf16[32,512]{1,0:T(8,128)(2,1)S(1)}, u32[]{:S(2)}, u32[]{:S(2)}) collective-permute-start(bf16[32,512]{1,0:T(8,128)(2,1)S(1)} %get-tuple-element.30.refs_3_), channel_id=1, source_target_pairs={{0,1},{1,0},{4,5},{5,4},{2,3},{3,2},{6,7},{7,6},{8,9},{9,8},{12,13... | collective-permute-start | bytes 98312 | tf_op jit(solution)/shard_map/ppermute | solution.py:384
  38.4 1.4 %collective-permute-done.14.refs_2_ = bf16[32,512]{1,0:T(8,128)(2,1)S(1)} collective-permute-done((bf16[32,512]{1,0:T(8,128)(2,1)S(1)}, bf16[32,512]{1,0:T(8,128)(2,1)S(1)}, u32[]{:S(2)}, u32[]{:S(2)}) %collective-permute-start.14) | collective-permute-done | bytes 32800 | tf_op jit(solution)/shard_map/ppermute | solution.py:384
  39.8 1.1 %collective-permute-done.12.refs_0_ = bf16[32,512]{1,0:T(8,128)(2,1)S(1)} collective-permute-done((bf16[32,512]{1,0:T(8,128)(2,1)S(1)}, bf16[32,512]{1,0:T(8,128)(2,1)S(1)}, u32[]{:S(2)}, u32[]{:S(2)}) %collective-permute-start.12) | collective-permute-done | bytes 32800 | tf_op jit(solution)/shard_map/ppermute | solution.py:384
  40.9 0.5 %collective-permute-done.13.refs_1_ = bf16[32,512]{1,0:T(8,128)(2,1)S(1)} collective-permute-done((bf16[32,512]{1,0:T(8,128)(2,1)S(1)}, bf16[32,512]{1,0:T(8,128)(2,1)S(1)}, u32[]{:S(2)}, u32[]{:S(2)}) %collective-permute-start.13) | collective-permute-done | bytes 32800 | tf_op jit(solution)/shard_map/ppermute | solution.py:384
  41.5 0.7 %shard_map.42 = bf16[4,32,512]{2,1,0:T(8,128)(2,1)} custom-call(bf16[32,512]{1,0:T(8,128)(2,1)S(1)} %collective-permute-done.12.refs_0_, bf16[32,512]{1,0:T(8,128)(2,1)S(1)} %collective-permute-done.13.refs_1_, bf16[32,512]{1,0:T(8,128)(2,1)S(1)} %collective-permute-done.14.refs_2_, bf16[32,512]{1,0:T(8,128)(2,1)S(1)} %get-tuple-element.30.refs_3_), custom_call_target="tpu_custom_call" | custom-call | tf_op jit(solution)/shard_map/pallas_call | solution.py:327
  (7 shorter events, 0.1 us)
Async XLA Ops:
  1.6 1.6 %collective-permute-start = (bf16[128,512]{1,0:T(8,128)(2,1)S(1)}, bf16[128,512]{1,0:T(8,128)(2,1)S(1)}, u32[]{:S(2)}, u32[]{:S(2)}) collective-permute-start(bf16[128,512]{1,0:T(8,128)(2,1)S(1)} %get-tuple-element.21), channel_id=1, source_target_pairs={{0,2},{2,0},{1,3},{3,1},{4,6},{6,4},{5,7},{7,5},{8,10},{10,8},{9,1... | collective-permute-start | bytes 393224 | tf_op jit(solution)/shard_map/ppermute | solution.py:344
  2.1 3.9 %collective-permute-start.2 = (bf16[128,512]{1,0:T(8,128)(2,1)S(1)}, bf16[128,512]{1,0:T(8,128)(2,1)S(1)}, u32[]{:S(2)}, u32[]{:S(2)}) collective-permute-start(bf16[128,512]{1,0:T(8,128)(2,1)S(1)} %get-tuple-element.24), channel_id=1, source_target_pairs={{0,2},{2,0},{1,3},{3,1},{4,6},{6,4},{5,7},{7,5},{8,10},{10,8},{9,1... | collective-permute-start | bytes 393224 | tf_op jit(solution)/shard_map/ppermute | solution.py:344
  2.7 5.4 %collective-permute-start.1 = (bf16[256,512]{1,0:T(8,128)(2,1)S(1)}, bf16[256,512]{1,0:T(8,128)(2,1)S(1)}, u32[]{:S(2)}, u32[]{:S(2)}) collective-permute-start(bf16[256,512]{1,0:T(8,128)(2,1)S(1)} %get-tuple-element.22), channel_id=1, source_target_pairs={{0,2},{2,0},{1,3},{3,1},{4,6},{6,4},{5,7},{7,5},{8,10},{10,8},{9,1... | collective-permute-start | bytes 786440 | tf_op jit(solution)/shard_map/ppermute | solution.py:344
  3.2 8.8 %collective-permute-start.4 = (bf16[128,512]{1,0:T(8,128)(2,1)S(1)}, bf16[128,512]{1,0:T(8,128)(2,1)S(1)}, u32[]{:S(2)}, u32[]{:S(2)}) collective-permute-start(bf16[128,512]{1,0:T(8,128)(2,1)S(1)} %add_convert_fusion.1.refs_0_), channel_id=1, source_target_pairs={{0,4},{4,0},{1,5},{5,1},{2,6},{6,2},{3,7},{7,3},{8,12},{12,8},{9,1... | collective-permute-start | bytes 393224 | tf_op jit(solution)/shard_map/ppermute | solution.py:344
  6.1 7.3 %collective-permute-start.3 = (bf16[128,512]{1,0:T(8,128)(2,1)S(1)}, bf16[128,512]{1,0:T(8,128)(2,1)S(1)}, u32[]{:S(2)}, u32[]{:S(2)}) collective-permute-start(bf16[128,512]{1,0:T(8,128)(2,1)S(1)} %add_convert_fusion), channel_id=1, source_target_pairs={{0,12},{4,8},{8,4},{12,0},{16,28},{20,24},{24,20},{28,16},{1,13},{... | collective-permute-start | bytes 393224 | tf_op jit(solution)/shard_map/ppermute | solution.py:348
  8.2 6.1 %collective-permute-start.5 = (bf16[128,512]{1,0:T(8,128)(2,1)S(1)}, bf16[128,512]{1,0:T(8,128)(2,1)S(1)}, u32[]{:S(2)}, u32[]{:S(2)}) collective-permute-start(bf16[128,512]{1,0:T(8,128)(2,1)S(1)} %slice.7), channel_id=1, source_target_pairs={{0,8},{8,0},{16,24},{24,16},{1,9},{9,1},{17,25},{25,17},{2,10},{10... | collective-permute-start | bytes 393224 | tf_op jit(solution)/shard_map/ppermute | solution.py:344
  14.3 8.0 %collective-permute-start.6 = (bf16[128,384]{1,0:T(8,128)(2,1)S(1)}, bf16[128,384]{1,0:T(8,128)(2,1)S(1)}, u32[]{:S(2)}, u32[]{:S(2)}) collective-permute-start(bf16[128,384]{1,0:T(8,128)(2,1)S(1)} %get-tuple-element.26), channel_id=1, source_target_pairs={{0,16},{8,24},{16,0},{24,8},{1,17},{9,25},{17,1},{25,9},{2,18},{10... | collective-permute-start | bytes 294920 | tf_op jit(solution)/shard_map/ppermute | solution.py:344
  17.0 6.0 %collective-permute-start.9 = (bf16[128,128]{1,0:T(8,128)(2,1)S(1)}, bf16[128,128]{1,0:T(8,128)(2,1)S(1)}, u32[]{:S(2)}, u32[]{:S(2)}) collective-permute-start(bf16[128,128]{1,0:T(8,128)(2,1)S(1)} %get-tuple-element.28), channel_id=1, source_target_pairs={{0,16},{8,24},{16,0},{24,8},{1,17},{9,25},{17,1},{25,9},{2,18},{10... | collective-permute-start | bytes 98312 | tf_op jit(solution)/shard_map/ppermute | solution.py:344
  22.3 4.7 %collective-permute-start.7 = (bf16[128,384]{1,0:T(8,128)(2,1)S(1)}, bf16[128,384]{1,0:T(8,128)(2,1)S(1)}, u32[]{:S(2)}, u32[]{:S(2)}) collective-permute-start(bf16[128,384]{1,0:T(8,128)(2,1)S(1)} %add_convert_fusion.2.refs_0_), channel_id=1, source_target_pairs={{0,8},{8,0},{16,24},{24,16},{1,9},{9,1},{17,25},{25,17},{2,10},{10... | collective-permute-start | bytes 294920 | tf_op jit(solution)/shard_map/ppermute | solution.py:344
  23.1 4.2 %collective-permute-start.10 = (bf16[128,128]{1,0:T(8,128)(2,1)S(1)}, bf16[128,128]{1,0:T(8,128)(2,1)S(1)}, u32[]{:S(2)}, u32[]{:S(2)}) collective-permute-start(bf16[128,128]{1,0:T(8,128)(2,1)S(1)} %add_convert_fusion.3.refs_3_), channel_id=1, source_target_pairs={{0,8},{8,0},{16,24},{24,16},{1,9},{9,1},{17,25},{25,17},{2,10},{10... | collective-permute-start | bytes 98312 | tf_op jit(solution)/shard_map/ppermute | solution.py:344
  27.0 1.6 %collective-permute-start.8 = (bf16[256,384]{1,0:T(8,128)(2,1)S(1)}, bf16[256,384]{1,0:T(8,128)(2,1)S(1)}, u32[]{:S(2)}, u32[]{:S(2)}) collective-permute-start(bf16[256,384]{1,0:T(8,128)(2,1)S(1)} %pad_maximum_fusion), channel_id=1, source_target_pairs={{0,2},{2,0},{1,3},{3,1},{4,6},{6,4},{5,7},{7,5},{8,10},{10,8},{9,1... | collective-permute-start | bytes 589832 | tf_op jit(solution)/shard_map/ppermute | solution.py:344
  27.4 1.3 %collective-permute-start.11 = (bf16[256,128]{1,0:T(8,128)(2,1)S(1)}, bf16[256,128]{1,0:T(8,128)(2,1)S(1)}, u32[]{:S(2)}, u32[]{:S(2)}) collective-permute-start(bf16[256,128]{1,0:T(8,128)(2,1)S(1)} %pad_maximum_fusion.1), channel_id=1, source_target_pairs={{0,2},{2,0},{1,3},{3,1},{4,6},{6,4},{5,7},{7,5},{8,10},{10,8},{9,1... | collective-permute-start | bytes 196616 | tf_op jit(solution)/shard_map/ppermute | solution.py:344
  34.8 5.0 %collective-permute-start.14 = (bf16[32,512]{1,0:T(8,128)(2,1)S(1)}, bf16[32,512]{1,0:T(8,128)(2,1)S(1)}, u32[]{:S(2)}, u32[]{:S(2)}) collective-permute-start(bf16[32,512]{1,0:T(8,128)(2,1)S(1)} %get-tuple-element.29), channel_id=1, source_target_pairs={{0,5},{1,4},{4,1},{5,0},{2,7},{3,6},{6,3},{7,2},{8,13},{9,12},{12,... | collective-permute-start | bytes 98312 | tf_op jit(solution)/shard_map/ppermute | solution.py:384
  37.0 3.9 %collective-permute-start.12 = (bf16[32,512]{1,0:T(8,128)(2,1)S(1)}, bf16[32,512]{1,0:T(8,128)(2,1)S(1)}, u32[]{:S(2)}, u32[]{:S(2)}) collective-permute-start(bf16[32,512]{1,0:T(8,128)(2,1)S(1)} %get-tuple-element.29), channel_id=1, source_target_pairs={{0,4},{1,5},{4,0},{5,1},{2,6},{3,7},{6,2},{7,3},{8,12},{9,13},{12,... | collective-permute-start | bytes 98312 | tf_op jit(solution)/shard_map/ppermute | solution.py:384
  37.6 3.9 %collective-permute-start.13 = (bf16[32,512]{1,0:T(8,128)(2,1)S(1)}, bf16[32,512]{1,0:T(8,128)(2,1)S(1)}, u32[]{:S(2)}, u32[]{:S(2)}) collective-permute-start(bf16[32,512]{1,0:T(8,128)(2,1)S(1)} %get-tuple-element.30.refs_3_), channel_id=1, source_target_pairs={{0,1},{1,0},{4,5},{5,4},{2,3},{3,2},{6,7},{7,6},{8,9},{9,8},{12,13... | collective-permute-start | bytes 98312 | tf_op jit(solution)/shard_map/ppermute | solution.py:384

commit v26 on v23

--- a/solution.py
+++ b/solution.py
@@ -316,8 +316,11 @@
 def place_kernel(origins, *refs):
     *pieces, out, sems = refs
     column, group = lax.axis_index("x"), lax.axis_index("group")
+    core = lax.axis_index("core")
     copies = []
-    for index, (piece, (turn, flip)) in enumerate(zip(pieces, origins)):
+    for index, (piece, (turn, flip, by_core)) in enumerate(zip(pieces, origins)):
+        if by_core:
+            turn, flip = turn ^ core, flip ^ core
         number = 2 * (group ^ turn) + (column ^ flip)
         copies.append(pltpu.make_async_copy(piece, out.at[number], sems.at[index]))
         copies[-1].start()
@@ -397,9 +400,22 @@
         ]
         return lax.ppermute(send if flip else keep, ("x", "group"), moves)
 
-    others = [(turn, flip) for flip in (1, 0) for turn in range(groups - 1, -1, -1) if turn or flip]
-    found = {(turn, flip): pass_on(turn, flip) for turn, flip in others}
-    found[0, 0] = keep
+    if groups == 2:
+        first_core = lax.axis_index("core") == 0
+        payloads = jnp.where(first_core, send, keep), jnp.where(first_core, keep, send)
+        found = {(1, 1, False): pass_on(1, 1)}
+        for order, payload in enumerate(payloads):
+            moves = []
+            for c in range(2):
+                for core in range(2):
+                    for g in range(2):
+                        to = (c ^ 1, g) if core == order else (c, g ^ 1)
+                        moves.append((4 * c + 2 * core + g, 4 * to[0] + 2 * core + to[1]))
+            found[order, 1 - order, True] = lax.ppermute(payload, ("x", "core", "group"), moves)
+    else:
+        others = [(turn, flip) for turn in range(groups) for flip in range(2) if turn or flip]
+        found = {(turn, flip, False): pass_on(turn, flip) for turn, flip in others}
+    found[0, 0, False] = keep
     return place(found)
 
 

time: 42.5 us -> 42.8 us (level)
    ppermute x0 -> x2, waiting for transfers between devices: none -> 2.6 us  [shards(): lax.ppermute(payload, ('x', 'core', 'group'), moves)]
    ppermute x3 -> x1, waiting for transfers between devices: 3.62 us -> 1.23 us  [pass_on(): return lax.ppermute(send if flip else keep, ('x', 'group'), moves)]
    ppermute x0 -> x2, starting transfers between devices: none -> 0.65 us  [shards(): lax.ppermute(payload, ('x', 'core', 'group'), moves)]
    ppermute x3 -> x1, starting transfers between devices: 3.64 us -> 3.05 us  [pass_on(): return lax.ppermute(send if flip else keep, ('x', 'group'), moves)]
where the time goes in v26:
time: 42.8 us; the launch traced here: 42.6 us
  waiting for transfers between devices  18 us (42%)
  starting transfers between devices  15 us (35%)
  Pallas kernels  9.35 us (22%)
    ppermute x11, waiting for transfers between devices, swap(): lax.ppermute(array, axis, [(i, i ^ mask) for i in range(lax.axis_size(axi...  14.1 us
    ppermute x11, starting transfers between devices, swap(): lax.ppermute(array, axis, [(i, i ^ mask) for i in range(lax.axis_size(axi...  11.1 us
    pallas_call x1, Pallas kernels, root(): pl.pallas_call(functools.partial(root_kernel, most), out_shape=[out, out]...  6.15 us
    ppermute x1, starting transfers between devices, pass_on(): return lax.ppermute(send if flip else keep, ('x', 'group'), moves)  3.05 us
    ppermute x2, waiting for transfers between devices, shards(): lax.ppermute(payload, ('x', 'core', 'group'), moves)  2.6 us
    pallas_call x1, Pallas kernels, load(): pl.pallas_call(functools.partial(load_kernel, scale), out_shape=[jax.Shap...  1.67 us
    ppermute x1, waiting for transfers between devices, pass_on(): return lax.ppermute(send if flip else keep, ('x', 'group'), moves)  1.23 us
  transfers between devices with their start and end apart: 15, of which 9 were waited for; matrix products, arithmetic and copies ran while one was open for 0% of the time, Pallas kernels for 2%

profile of v26, /device:TPU:0, one launch (start us, length us, event | category | flops | bytes accessed | tf_op | source)
XLA Modules:
  0.0 42.6 jit_solution(10280047717785048636)
XLA Ops:
  0.0 1.7 %shard_map.37 = (bf16[128,512]{1,0:T(8,128)(2,1)S(1)}, bf16[128,512]{1,0:T(8,128)(2,1)S(1)}, bf16[2,2,512,256]{3,2,1,0:T(8,128)(2,1)S(1)}, bf16[2,512,512]{2,1,0:T(8,128)(2,1)S(1)}) custom-call(bf16[2,512,512]{2,1,0:T(8,128)(2,1)} %patch_hbm.1, bf16[2,512,512]{2,1,0:T(8,128)(2,1)} %cot_hbm.1), custom_call_target="tpu_custom_call" | custom-call | tf_op jit(solution)/shard_map/pallas_call | solution.py:70
  1.7 0.5 %collective-permute-start = (bf16[128,512]{1,0:T(8,128)(2,1)S(1)}, bf16[128,512]{1,0:T(8,128)(2,1)S(1)}, u32[]{:S(2)}, u32[]{:S(2)}) collective-permute-start(bf16[128,512]{1,0:T(8,128)(2,1)S(1)} %get-tuple-element.23), channel_id=1, source_target_pairs={{0,2},{2,0},{1,3},{3,1},{4,6},{6,4},{5,7},{7,5},{8,10},{10,8},{9,1... | collective-permute-start | bytes 393224 | tf_op jit(solution)/shard_map/ppermute | solution.py:351
  2.2 0.1 collective-permute-start.3
  2.3 0.5 %shard_map.38 = (f32[128,512]{1,0:T(8,128)S(1)}, f32[128,512]{1,0:T(8,128)S(1)}, bf16[256,512]{1,0:T(8,128)(2,1)S(1)}) custom-call(bf16[2,2,512,256]{3,2,1,0:T(8,128)(2,1)S(1)} %get-tuple-element.20.patch, bf16[2,512,512]{2,1,0:T(8,128)(2,1)S(1)} %get-tuple-element.21.cot), custom_call_target="tpu_custom_call" | custom-call | flops 402653184 | bytes 1048576 | tf_op jit(solution)/shard_map/pallas_call | solution.py:98
  2.7 0.5 %collective-permute-start.1 = (bf16[256,512]{1,0:T(8,128)(2,1)S(1)}, bf16[256,512]{1,0:T(8,128)(2,1)S(1)}, u32[]{:S(2)}, u32[]{:S(2)}) collective-permute-start(bf16[256,512]{1,0:T(8,128)(2,1)S(1)} %get-tuple-element.25), channel_id=1, source_target_pairs={{0,2},{2,0},{1,3},{3,1},{4,6},{6,4},{5,7},{7,5},{8,10},{10,8},{9,1... | collective-permute-start | bytes 786440 | tf_op jit(solution)/shard_map/ppermute | solution.py:351
  3.2 0.0 collective-permute-done
  3.3 2.9 %collective-permute-start.5 = (bf16[128,512]{1,0:T(8,128)(2,1)S(1)}, bf16[128,512]{1,0:T(8,128)(2,1)S(1)}, u32[]{:S(2)}, u32[]{:S(2)}) collective-permute-start(bf16[128,512]{1,0:T(8,128)(2,1)S(1)} %add_convert_fusion.2.refs_0_), channel_id=1, source_target_pairs={{0,8},{8,0},{16,24},{24,16},{1,9},{9,1},{17,25},{25,17},{2,10},{10... | collective-permute-start | bytes 393224 | tf_op jit(solution)/shard_map/ppermute | solution.py:351
  6.2 0.0 collective-permute-done.3
  6.3 1.6 %collective-permute-start.4 = (bf16[128,512]{1,0:T(8,128)(2,1)S(1)}, bf16[128,512]{1,0:T(8,128)(2,1)S(1)}, u32[]{:S(2)}, u32[]{:S(2)}) collective-permute-start(bf16[128,512]{1,0:T(8,128)(2,1)S(1)} %add_convert_fusion), channel_id=1, source_target_pairs={{0,4},{4,0},{1,5},{5,1},{2,6},{6,2},{3,7},{7,3},{8,12},{12,8},{9,1... | collective-permute-start | bytes 393224 | tf_op jit(solution)/shard_map/ppermute | solution.py:351
  7.8 0.3 shard_map.39
  8.1 0.0 collective-permute-done.1
  8.1 0.1 add_convert_fusion.1
  8.2 0.2 collective-permute-start.2
  8.4 1.7 %collective-permute-done.5.refs_2_ = bf16[128,512]{1,0:T(8,128)(2,1)S(1)} collective-permute-done((bf16[128,512]{1,0:T(8,128)(2,1)S(1)}, bf16[128,512]{1,0:T(8,128)(2,1)S(1)}, u32[]{:S(2)}, u32[]{:S(2)}) %collective-permute-start.5) | collective-permute-done | bytes 131104 | tf_op jit(solution)/shard_map/ppermute | solution.py:351
  10.1 4.4 %collective-permute-done.4.refs_1_ = bf16[128,512]{1,0:T(8,128)(2,1)S(1)} collective-permute-done((bf16[128,512]{1,0:T(8,128)(2,1)S(1)}, bf16[128,512]{1,0:T(8,128)(2,1)S(1)}, u32[]{:S(2)}, u32[]{:S(2)}) %collective-permute-start.4) | collective-permute-done | bytes 131104 | tf_op jit(solution)/shard_map/ppermute | solution.py:351
  14.5 0.0 collective-permute-done.2.refs_0_
  14.5 0.1 shard_map.40
  14.5 2.7 %collective-permute-start.6 = (bf16[128,384]{1,0:T(8,128)(2,1)S(1)}, bf16[128,384]{1,0:T(8,128)(2,1)S(1)}, u32[]{:S(2)}, u32[]{:S(2)}) collective-permute-start(bf16[128,384]{1,0:T(8,128)(2,1)S(1)} %get-tuple-element.30), channel_id=1, source_target_pairs={{0,16},{8,24},{16,0},{24,8},{1,17},{9,25},{17,1},{25,9},{2,18},{10... | collective-permute-start | bytes 294920 | tf_op jit(solution)/shard_map/ppermute | solution.py:351
  17.2 0.3 collective-permute-start.9
  17.5 4.4 %collective-permute-done.6 = bf16[128,384]{1,0:T(8,128)(2,1)S(1)} collective-permute-done((bf16[128,384]{1,0:T(8,128)(2,1)S(1)}, bf16[128,384]{1,0:T(8,128)(2,1)S(1)}, u32[]{:S(2)}, u32[]{:S(2)}) %collective-permute-start.6) | collective-permute-done | bytes 98336 | tf_op jit(solution)/shard_map/ppermute | solution.py:351
  21.9 0.8 %collective-permute-start.7 = (bf16[128,384]{1,0:T(8,128)(2,1)S(1)}, bf16[128,384]{1,0:T(8,128)(2,1)S(1)}, u32[]{:S(2)}, u32[]{:S(2)}) collective-permute-start(bf16[128,384]{1,0:T(8,128)(2,1)S(1)} %add_convert_fusion.3.refs_0_), channel_id=1, source_target_pairs={{0,8},{8,0},{16,24},{24,16},{1,9},{9,1},{17,25},{25,17},{2,10},{10... | collective-permute-start | bytes 294920 | tf_op jit(solution)/shard_map/ppermute | solution.py:351
  22.7 0.0 collective-permute-done.9
  22.8 1.3 %collective-permute-start.10 = (bf16[128,128]{1,0:T(8,128)(2,1)S(1)}, bf16[128,128]{1,0:T(8,128)(2,1)S(1)}, u32[]{:S(2)}, u32[]{:S(2)}) collective-permute-start(bf16[128,128]{1,0:T(8,128)(2,1)S(1)} %add_convert_fusion.4.refs_3_), channel_id=1, source_target_pairs={{0,8},{8,0},{16,24},{24,16},{1,9},{9,1},{17,25},{25,17},{2,10},{10... | collective-permute-start | bytes 98312 | tf_op jit(solution)/shard_map/ppermute | solution.py:351
  24.1 2.5 %collective-permute-done.7.refs_1_ = bf16[128,384]{1,0:T(8,128)(2,1)S(1)} collective-permute-done((bf16[128,384]{1,0:T(8,128)(2,1)S(1)}, bf16[128,384]{1,0:T(8,128)(2,1)S(1)}, u32[]{:S(2)}, u32[]{:S(2)}) %collective-permute-start.7) | collective-permute-done | bytes 98336 | tf_op jit(solution)/shard_map/ppermute | solution.py:351
  26.6 0.1 collective-permute-start.8
  26.7 0.2 collective-permute-done.10.refs_4_
  26.9 0.3 collective-permute-start.11
  27.3 0.9 %collective-permute-done.11.refs_5_ = bf16[256,128]{1,0:T(8,128)(2,1)S(1)} collective-permute-done((bf16[256,128]{1,0:T(8,128)(2,1)S(1)}, bf16[256,128]{1,0:T(8,128)(2,1)S(1)}, u32[]{:S(2)}, u32[]{:S(2)}) %collective-permute-start.11) | collective-permute-done | bytes 65568 | tf_op jit(solution)/shard_map/ppermute | solution.py:351
  28.2 0.0 collective-permute-done.8.refs_2_
  28.2 6.2 %shard_map.41 = (bf16[32,512]{1,0:T(8,128)(2,1)S(1)}, bf16[32,512]{1,0:T(8,128)(2,1)S(1)}) custom-call(s32[2,2]{1,0:T(2,128)} %counts_hbm.1, bf16[128,384]{1,0:T(8,128)(2,1)S(1)} %add_convert_fusion.3.refs_0_, bf16[128,384]{1,0:T(8,128)(2,1)S(1)} %collective-permute-done.7.refs_1_, bf16[256,384]{1,0:T(8,128)(2,1)S(1)} %collective-permute-done.8.refs_2_, ...), custom_call_target="tpu_custom_call" | custom-call | tf_op jit(solution)/shard_map/pallas_call | solution.py:295
  34.4 3.1 %collective-permute-start.12 = (bf16[32,512]{1,0:T(8,128)(2,1)S(1)}, bf16[32,512]{1,0:T(8,128)(2,1)S(1)}, u32[]{:S(2)}, u32[]{:S(2)}) collective-permute-start(bf16[32,512]{1,0:T(8,128)(2,1)S(1)} %get-tuple-element.33), channel_id=1, source_target_pairs={{0,5},{1,4},{4,1},{5,0},{2,7},{3,6},{6,3},{7,2},{8,13},{9,12},{12,... | collective-permute-start | bytes 98312 | tf_op jit(solution)/shard_map/ppermute | solution.py:401
  37.4 0.6 %collective-permute-start.14 = (bf16[32,512]{1,0:T(8,128)(2,1)S(1)}, bf16[32,512]{1,0:T(8,128)(2,1)S(1)}, u32[]{:S(2)}, u32[]{:S(2)}) collective-permute-start(bf16[32,512]{1,0:T(8,128)(2,1)S(1)} %get-tuple-element.37), channel_id=1, source_target_pairs={{0,1},{1,0},{2,6},{3,7},{4,5},{5,4},{6,2},{7,3},{8,9},{9,8},{10,14... | collective-permute-start | bytes 98312 | tf_op jit(solution)/shard_map/ppermute | solution.py:414
  38.0 0.1 collective-permute-start.13
  38.1 1.2 %collective-permute-done.12.refs_0_ = bf16[32,512]{1,0:T(8,128)(2,1)S(1)} collective-permute-done((bf16[32,512]{1,0:T(8,128)(2,1)S(1)}, bf16[32,512]{1,0:T(8,128)(2,1)S(1)}, u32[]{:S(2)}, u32[]{:S(2)}) %collective-permute-start.12) | collective-permute-done | bytes 32800 | tf_op jit(solution)/shard_map/ppermute | solution.py:401
  39.3 2.1 %collective-permute-done.14.refs_2_ = bf16[32,512]{1,0:T(8,128)(2,1)S(1)} collective-permute-done((bf16[32,512]{1,0:T(8,128)(2,1)S(1)}, bf16[32,512]{1,0:T(8,128)(2,1)S(1)}, u32[]{:S(2)}, u32[]{:S(2)}) %collective-permute-start.14) | collective-permute-done | bytes 32800 | tf_op jit(solution)/shard_map/ppermute | solution.py:414
  41.4 0.5 %collective-permute-done.13.refs_1_ = bf16[32,512]{1,0:T(8,128)(2,1)S(1)} collective-permute-done((bf16[32,512]{1,0:T(8,128)(2,1)S(1)}, bf16[32,512]{1,0:T(8,128)(2,1)S(1)}, u32[]{:S(2)}, u32[]{:S(2)}) %collective-permute-start.13) | collective-permute-done | bytes 32800 | tf_op jit(solution)/shard_map/ppermute | solution.py:414
  41.9 0.7 %shard_map.42 = bf16[4,32,512]{2,1,0:T(8,128)(2,1)} custom-call(bf16[32,512]{1,0:T(8,128)(2,1)S(1)} %collective-permute-done.12.refs_0_, bf16[32,512]{1,0:T(8,128)(2,1)S(1)} %collective-permute-done.13.refs_1_, bf16[32,512]{1,0:T(8,128)(2,1)S(1)} %collective-permute-done.14.refs_2_, bf16[32,512]{1,0:T(8,128)(2,1)S(1)} %get-tuple-element.34.refs_3_), custom_call_target="tpu_custom_call" | custom-call | tf_op jit(solution)/shard_map/pallas_call | solution.py:334
  (7 shorter events, 0.1 us)
Async XLA Ops:
  1.7 1.6 %collective-permute-start = (bf16[128,512]{1,0:T(8,128)(2,1)S(1)}, bf16[128,512]{1,0:T(8,128)(2,1)S(1)}, u32[]{:S(2)}, u32[]{:S(2)}) collective-permute-start(bf16[128,512]{1,0:T(8,128)(2,1)S(1)} %get-tuple-element.23), channel_id=1, source_target_pairs={{0,2},{2,0},{1,3},{3,1},{4,6},{6,4},{5,7},{7,5},{8,10},{10,8},{9,1... | collective-permute-start | bytes 393224 | tf_op jit(solution)/shard_map/ppermute | solution.py:351
  2.2 4.0 %collective-permute-start.3 = (bf16[128,512]{1,0:T(8,128)(2,1)S(1)}, bf16[128,512]{1,0:T(8,128)(2,1)S(1)}, u32[]{:S(2)}, u32[]{:S(2)}) collective-permute-start(bf16[128,512]{1,0:T(8,128)(2,1)S(1)} %get-tuple-element.28), channel_id=1, source_target_pairs={{0,2},{2,0},{1,3},{3,1},{4,6},{6,4},{5,7},{7,5},{8,10},{10,8},{9,1... | collective-permute-start | bytes 393224 | tf_op jit(solution)/shard_map/ppermute | solution.py:351
  2.7 5.4 %collective-permute-start.1 = (bf16[256,512]{1,0:T(8,128)(2,1)S(1)}, bf16[256,512]{1,0:T(8,128)(2,1)S(1)}, u32[]{:S(2)}, u32[]{:S(2)}) collective-permute-start(bf16[256,512]{1,0:T(8,128)(2,1)S(1)} %get-tuple-element.25), channel_id=1, source_target_pairs={{0,2},{2,0},{1,3},{3,1},{4,6},{6,4},{5,7},{7,5},{8,10},{10,8},{9,1... | collective-permute-start | bytes 786440 | tf_op jit(solution)/shard_map/ppermute | solution.py:351
  3.3 6.8 %collective-permute-start.5 = (bf16[128,512]{1,0:T(8,128)(2,1)S(1)}, bf16[128,512]{1,0:T(8,128)(2,1)S(1)}, u32[]{:S(2)}, u32[]{:S(2)}) collective-permute-start(bf16[128,512]{1,0:T(8,128)(2,1)S(1)} %add_convert_fusion.2.refs_0_), channel_id=1, source_target_pairs={{0,8},{8,0},{16,24},{24,16},{1,9},{9,1},{17,25},{25,17},{2,10},{10... | collective-permute-start | bytes 393224 | tf_op jit(solution)/shard_map/ppermute | solution.py:351
  6.3 8.2 %collective-permute-start.4 = (bf16[128,512]{1,0:T(8,128)(2,1)S(1)}, bf16[128,512]{1,0:T(8,128)(2,1)S(1)}, u32[]{:S(2)}, u32[]{:S(2)}) collective-permute-start(bf16[128,512]{1,0:T(8,128)(2,1)S(1)} %add_convert_fusion), channel_id=1, source_target_pairs={{0,4},{4,0},{1,5},{5,1},{2,6},{6,2},{3,7},{7,3},{8,12},{12,8},{9,1... | collective-permute-start | bytes 393224 | tf_op jit(solution)/shard_map/ppermute | solution.py:351
  8.2 6.2 %collective-permute-start.2 = (bf16[128,512]{1,0:T(8,128)(2,1)S(1)}, bf16[128,512]{1,0:T(8,128)(2,1)S(1)}, u32[]{:S(2)}, u32[]{:S(2)}) collective-permute-start(bf16[128,512]{1,0:T(8,128)(2,1)S(1)} %get-tuple-element.35), channel_id=1, source_target_pairs={{0,12},{4,8},{8,4},{12,0},{16,28},{20,24},{24,20},{28,16},{1,13},{... | collective-permute-start | bytes 393224 | tf_op jit(solution)/shard_map/ppermute | solution.py:355
  14.5 7.3 %collective-permute-start.6 = (bf16[128,384]{1,0:T(8,128)(2,1)S(1)}, bf16[128,384]{1,0:T(8,128)(2,1)S(1)}, u32[]{:S(2)}, u32[]{:S(2)}) collective-permute-start(bf16[128,384]{1,0:T(8,128)(2,1)S(1)} %get-tuple-element.30), channel_id=1, source_target_pairs={{0,16},{8,24},{16,0},{24,8},{1,17},{9,25},{17,1},{25,9},{2,18},{10... | collective-permute-start | bytes 294920 | tf_op jit(solution)/shard_map/ppermute | solution.py:351
  17.2 5.6 %collective-permute-start.9 = (bf16[128,128]{1,0:T(8,128)(2,1)S(1)}, bf16[128,128]{1,0:T(8,128)(2,1)S(1)}, u32[]{:S(2)}, u32[]{:S(2)}) collective-permute-start(bf16[128,128]{1,0:T(8,128)(2,1)S(1)} %get-tuple-element.32), channel_id=1, source_target_pairs={{0,16},{8,24},{16,0},{24,8},{1,17},{9,25},{17,1},{25,9},{2,18},{10... | collective-permute-start | bytes 98312 | tf_op jit(solution)/shard_map/ppermute | solution.py:351
  21.9 4.7 %collective-permute-start.7 = (bf16[128,384]{1,0:T(8,128)(2,1)S(1)}, bf16[128,384]{1,0:T(8,128)(2,1)S(1)}, u32[]{:S(2)}, u32[]{:S(2)}) collective-permute-start(bf16[128,384]{1,0:T(8,128)(2,1)S(1)} %add_convert_fusion.3.refs_0_), channel_id=1, source_target_pairs={{0,8},{8,0},{16,24},{24,16},{1,9},{9,1},{17,25},{25,17},{2,10},{10... | collective-permute-start | bytes 294920 | tf_op jit(solution)/shard_map/ppermute | solution.py:351
  22.8 4.2 %collective-permute-start.10 = (bf16[128,128]{1,0:T(8,128)(2,1)S(1)}, bf16[128,128]{1,0:T(8,128)(2,1)S(1)}, u32[]{:S(2)}, u32[]{:S(2)}) collective-permute-start(bf16[128,128]{1,0:T(8,128)(2,1)S(1)} %add_convert_fusion.4.refs_3_), channel_id=1, source_target_pairs={{0,8},{8,0},{16,24},{24,16},{1,9},{9,1},{17,25},{25,17},{2,10},{10... | collective-permute-start | bytes 98312 | tf_op jit(solution)/shard_map/ppermute | solution.py:351
  26.6 1.6 %collective-permute-start.8 = (bf16[256,384]{1,0:T(8,128)(2,1)S(1)}, bf16[256,384]{1,0:T(8,128)(2,1)S(1)}, u32[]{:S(2)}, u32[]{:S(2)}) collective-permute-start(bf16[256,384]{1,0:T(8,128)(2,1)S(1)} %pad_maximum_fusion), channel_id=1, source_target_pairs={{0,2},{2,0},{1,3},{3,1},{4,6},{6,4},{5,7},{7,5},{8,10},{10,8},{9,1... | collective-permute-start | bytes 589832 | tf_op jit(solution)/shard_map/ppermute | solution.py:351
  26.9 1.3 %collective-permute-start.11 = (bf16[256,128]{1,0:T(8,128)(2,1)S(1)}, bf16[256,128]{1,0:T(8,128)(2,1)S(1)}, u32[]{:S(2)}, u32[]{:S(2)}) collective-permute-start(bf16[256,128]{1,0:T(8,128)(2,1)S(1)} %pad_maximum_fusion.1), channel_id=1, source_target_pairs={{0,2},{2,0},{1,3},{3,1},{4,6},{6,4},{5,7},{7,5},{8,10},{10,8},{9,1... | collective-permute-start | bytes 196616 | tf_op jit(solution)/shard_map/ppermute | solution.py:351
  34.4 4.9 %collective-permute-start.12 = (bf16[32,512]{1,0:T(8,128)(2,1)S(1)}, bf16[32,512]{1,0:T(8,128)(2,1)S(1)}, u32[]{:S(2)}, u32[]{:S(2)}) collective-permute-start(bf16[32,512]{1,0:T(8,128)(2,1)S(1)} %get-tuple-element.33), channel_id=1, source_target_pairs={{0,5},{1,4},{4,1},{5,0},{2,7},{3,6},{6,3},{7,2},{8,13},{9,12},{12,... | collective-permute-start | bytes 98312 | tf_op jit(solution)/shard_map/ppermute | solution.py:401
  37.4 4.0 %collective-permute-start.14 = (bf16[32,512]{1,0:T(8,128)(2,1)S(1)}, bf16[32,512]{1,0:T(8,128)(2,1)S(1)}, u32[]{:S(2)}, u32[]{:S(2)}) collective-permute-start(bf16[32,512]{1,0:T(8,128)(2,1)S(1)} %get-tuple-element.37), channel_id=1, source_target_pairs={{0,1},{1,0},{2,6},{3,7},{4,5},{5,4},{6,2},{7,3},{8,9},{9,8},{10,14... | collective-permute-start | bytes 98312 | tf_op jit(solution)/shard_map/ppermute | solution.py:414
  38.0 3.9 %collective-permute-start.13 = (bf16[32,512]{1,0:T(8,128)(2,1)S(1)}, bf16[32,512]{1,0:T(8,128)(2,1)S(1)}, u32[]{:S(2)}, u32[]{:S(2)}) collective-permute-start(bf16[32,512]{1,0:T(8,128)(2,1)S(1)} %get-tuple-element.38), channel_id=1, source_target_pairs={{0,4},{1,5},{2,3},{3,2},{4,0},{5,1},{6,7},{7,6},{8,12},{9,13},{10,... | collective-permute-start | bytes 98312 | tf_op jit(solution)/shard_map/ppermute | solution.py:414

commit v27 on v22

--- a/solution.py
+++ b/solution.py
@@ -147,8 +147,8 @@
 
 
 def root_kernel(most, counts_hbm, *refs):
-    pieces = refs[:6]
-    keep_ref, send_ref, grad, turned, left, right, m_left, m_right, s_left, s_right, counts, sem = refs[6:]
+    pieces, far = refs[:4], refs[4]
+    keep_ref, send_ref, grad, turned, left, right, m_left, m_right, s_left, s_right, counts, sem = refs[5:]
     counts_copy = pltpu.make_async_copy(counts_hbm, counts, sem)
     counts_copy.start()
     width = grad.shape[0]
@@ -157,13 +157,12 @@
     low, high = slice(0, half), slice(half, width)
     place, column, core = (lax.axis_index(name) for name in ("z", "x", "core"))
     column_start = 0
-    for index in range(2):
-        own, other, far = pieces[3 * index : 3 * index + 3]
+    for own, other in (pieces[:2], pieces[2:]):
         columns = slice(column_start, column_start + own.shape[1])
         column_start += own.shape[1]
         grad[:quarter, columns] = own[...]
         grad[quarter:half, columns] = other[...]
-        grad[half:, columns] = far[...]
+    grad[half:, :] = far[...]
     turned[...] = grad[...].T
     diagonal = lax.broadcasted_iota(jnp.int32, (half, half), 0) == lax.broadcasted_iota(
         jnp.int32, (half, half), 1
@@ -295,7 +294,7 @@
     return pl.pallas_call(
         functools.partial(root_kernel, most),
         out_shape=[out, out],
-        in_specs=[HBM] + [VMEM] * 6,
+        in_specs=[HBM] + [VMEM] * 5,
         out_specs=[VMEM] * 2,
         scratch_shapes=[
             square,
@@ -386,7 +385,9 @@
             mask *= 2
         own = send
         other = swap(own, "z")
-        pieces += [own, other, swap(jnp.concatenate([own, other], 0), "core")]
+        pieces += [own, other]
+    far = swap(jnp.concatenate([jnp.concatenate(pieces[i : i + 2], 0) for i in (0, 2)], 1), "core")
+    pieces.append(far)
     keep, send = root(newton_counts, pieces, rows)
 
     def pass_on(turn, flip):

time: 42.2 us -> 42.5 us (level)
  waiting for transfers between devices: 17.4 us -> 18.1 us
    ppermute x11 -> x10, waiting for transfers between devices: 14.1 us -> 14.8 us  [swap(): lax.ppermute(array, axis, [(i, i ^ mask) for i in range(lax.axis_size(axi...]
    ppermute x11 -> x10, starting transfers between devices: 11.1 us -> 10.8 us  [swap(): lax.ppermute(array, axis, [(i, i ^ mask) for i in range(lax.axis_size(axi...]
  transfers between devices with their start and end apart: 15 -> 14, of which waited for: 8 -> 7; matrix products, arithmetic and copies ran while one was open for 0% -> 0% of each run, Pallas kernels for 2% -> 2%
where the time goes in v27:
time: 42.5 us; the launch traced here: 42.4 us
  waiting for transfers between devices  18.1 us (43%)
  starting transfers between devices  14.7 us (35%)
  Pallas kernels  9.35 us (22%)
    ppermute x10, waiting for transfers between devices, swap(): lax.ppermute(array, axis, [(i, i ^ mask) for i in range(lax.axis_size(axi...  14.8 us
    ppermute x10, starting transfers between devices, swap(): lax.ppermute(array, axis, [(i, i ^ mask) for i in range(lax.axis_size(axi...  10.8 us
    pallas_call x1, Pallas kernels, root(): pl.pallas_call(functools.partial(root_kernel, most), out_shape=[out, out]...  6.15 us
    ppermute x3, starting transfers between devices, pass_on(): return lax.ppermute(send if flip else keep, ('x', 'group'), moves)  3.69 us
    ppermute x3, waiting for transfers between devices, pass_on(): return lax.ppermute(send if flip else keep, ('x', 'group'), moves)  3.27 us
    pallas_call x1, Pallas kernels, load(): pl.pallas_call(functools.partial(load_kernel, scale), out_shape=[jax.Shap...  1.67 us
  transfers between devices with their start and end apart: 14, of which 7 were waited for; matrix products, arithmetic and copies ran while one was open for 0% of the time, Pallas kernels for 2%

profile of v27, /device:TPU:0, one launch (start us, length us, event | category | flops | bytes accessed | tf_op | source)
XLA Modules:
  0.0 42.4 jit_solution(4775996698509155309)
XLA Ops:
  0.0 1.7 %shard_map.37 = (bf16[128,512]{1,0:T(8,128)(2,1)S(1)}, bf16[128,512]{1,0:T(8,128)(2,1)S(1)}, bf16[2,2,512,256]{3,2,1,0:T(8,128)(2,1)S(1)}, bf16[2,512,512]{2,1,0:T(8,128)(2,1)S(1)}) custom-call(bf16[2,512,512]{2,1,0:T(8,128)(2,1)} %patch_hbm.1, bf16[2,512,512]{2,1,0:T(8,128)(2,1)} %cot_hbm.1), custom_call_target="tpu_custom_call" | custom-call | tf_op jit(solution)/shard_map/pallas_call | solution.py:70
  1.7 0.5 %collective-permute-start = (bf16[128,512]{1,0:T(8,128)(2,1)S(1)}, bf16[128,512]{1,0:T(8,128)(2,1)S(1)}, u32[]{:S(2)}, u32[]{:S(2)}) collective-permute-start(bf16[128,512]{1,0:T(8,128)(2,1)S(1)} %get-tuple-element.23), channel_id=1, source_target_pairs={{0,2},{2,0},{1,3},{3,1},{4,6},{6,4},{5,7},{7,5},{8,10},{10,8},{9,1... | collective-permute-start | bytes 393224 | tf_op jit(solution)/shard_map/ppermute | solution.py:347
  2.2 0.1 collective-permute-start.3
  2.3 0.5 %shard_map.38 = (f32[128,512]{1,0:T(8,128)S(1)}, f32[128,512]{1,0:T(8,128)S(1)}, bf16[256,512]{1,0:T(8,128)(2,1)S(1)}) custom-call(bf16[2,2,512,256]{3,2,1,0:T(8,128)(2,1)S(1)} %get-tuple-element.20.patch, bf16[2,512,512]{2,1,0:T(8,128)(2,1)S(1)} %get-tuple-element.21.cot), custom_call_target="tpu_custom_call" | custom-call | flops 402653184 | bytes 1048576 | tf_op jit(solution)/shard_map/pallas_call | solution.py:98
  2.7 0.5 %collective-permute-start.1 = (bf16[256,512]{1,0:T(8,128)(2,1)S(1)}, bf16[256,512]{1,0:T(8,128)(2,1)S(1)}, u32[]{:S(2)}, u32[]{:S(2)}) collective-permute-start(bf16[256,512]{1,0:T(8,128)(2,1)S(1)} %get-tuple-element.25), channel_id=1, source_target_pairs={{0,2},{2,0},{1,3},{3,1},{4,6},{6,4},{5,7},{7,5},{8,10},{10,8},{9,1... | collective-permute-start | bytes 786440 | tf_op jit(solution)/shard_map/ppermute | solution.py:347
  3.2 0.0 collective-permute-done
  3.3 2.9 %collective-permute-start.5 = (bf16[128,512]{1,0:T(8,128)(2,1)S(1)}, bf16[128,512]{1,0:T(8,128)(2,1)S(1)}, u32[]{:S(2)}, u32[]{:S(2)}) collective-permute-start(bf16[128,512]{1,0:T(8,128)(2,1)S(1)} %add_convert_fusion.2.refs_0_), channel_id=1, source_target_pairs={{0,8},{8,0},{16,24},{24,16},{1,9},{9,1},{17,25},{25,17},{2,10},{10... | collective-permute-start | bytes 393224 | tf_op jit(solution)/shard_map/ppermute | solution.py:347
  6.2 0.0 collective-permute-done.3
  6.3 1.6 %collective-permute-start.4 = (bf16[128,512]{1,0:T(8,128)(2,1)S(1)}, bf16[128,512]{1,0:T(8,128)(2,1)S(1)}, u32[]{:S(2)}, u32[]{:S(2)}) collective-permute-start(bf16[128,512]{1,0:T(8,128)(2,1)S(1)} %add_convert_fusion), channel_id=1, source_target_pairs={{0,4},{4,0},{1,5},{5,1},{2,6},{6,2},{3,7},{7,3},{8,12},{12,8},{9,1... | collective-permute-start | bytes 393224 | tf_op jit(solution)/shard_map/ppermute | solution.py:347
  7.8 0.3 shard_map.39
  8.1 0.0 collective-permute-done.1
  8.1 0.1 add_convert_fusion.1
  8.2 0.2 collective-permute-start.2
  8.4 1.7 %collective-permute-done.5.refs_2_ = bf16[128,512]{1,0:T(8,128)(2,1)S(1)} collective-permute-done((bf16[128,512]{1,0:T(8,128)(2,1)S(1)}, bf16[128,512]{1,0:T(8,128)(2,1)S(1)}, u32[]{:S(2)}, u32[]{:S(2)}) %collective-permute-start.5) | collective-permute-done | bytes 131104 | tf_op jit(solution)/shard_map/ppermute | solution.py:347
  10.1 4.4 %collective-permute-done.4.refs_1_ = bf16[128,512]{1,0:T(8,128)(2,1)S(1)} collective-permute-done((bf16[128,512]{1,0:T(8,128)(2,1)S(1)}, bf16[128,512]{1,0:T(8,128)(2,1)S(1)}, u32[]{:S(2)}, u32[]{:S(2)}) %collective-permute-start.4) | collective-permute-done | bytes 131104 | tf_op jit(solution)/shard_map/ppermute | solution.py:347
  14.5 0.0 collective-permute-done.2.refs_0_
  14.5 0.1 shard_map.40
  14.5 2.7 %collective-permute-start.6 = (bf16[128,384]{1,0:T(8,128)(2,1)S(1)}, bf16[128,384]{1,0:T(8,128)(2,1)S(1)}, u32[]{:S(2)}, u32[]{:S(2)}) collective-permute-start(bf16[128,384]{1,0:T(8,128)(2,1)S(1)} %get-tuple-element.30), channel_id=1, source_target_pairs={{0,16},{8,24},{16,0},{24,8},{1,17},{9,25},{17,1},{25,9},{2,18},{10... | collective-permute-start | bytes 294920 | tf_op jit(solution)/shard_map/ppermute | solution.py:347
  17.2 0.3 collective-permute-start.8
  17.5 4.4 %collective-permute-done.6 = bf16[128,384]{1,0:T(8,128)(2,1)S(1)} collective-permute-done((bf16[128,384]{1,0:T(8,128)(2,1)S(1)}, bf16[128,384]{1,0:T(8,128)(2,1)S(1)}, u32[]{:S(2)}, u32[]{:S(2)}) %collective-permute-start.6) | collective-permute-done | bytes 98336 | tf_op jit(solution)/shard_map/ppermute | solution.py:347
  21.9 0.8 %collective-permute-start.7 = (bf16[128,384]{1,0:T(8,128)(2,1)S(1)}, bf16[128,384]{1,0:T(8,128)(2,1)S(1)}, u32[]{:S(2)}, u32[]{:S(2)}) collective-permute-start(bf16[128,384]{1,0:T(8,128)(2,1)S(1)} %add_convert_fusion.3.refs_0_), channel_id=1, source_target_pairs={{0,8},{8,0},{16,24},{24,16},{1,9},{9,1},{17,25},{25,17},{2,10},{10... | collective-permute-start | bytes 294920 | tf_op jit(solution)/shard_map/ppermute | solution.py:347
  22.7 0.0 collective-permute-done.8
  22.8 1.3 %collective-permute-start.9 = (bf16[128,128]{1,0:T(8,128)(2,1)S(1)}, bf16[128,128]{1,0:T(8,128)(2,1)S(1)}, u32[]{:S(2)}, u32[]{:S(2)}) collective-permute-start(bf16[128,128]{1,0:T(8,128)(2,1)S(1)} %add_convert_fusion.4.refs_2_), channel_id=1, source_target_pairs={{0,8},{8,0},{16,24},{24,16},{1,9},{9,1},{17,25},{25,17},{2,10},{10... | collective-permute-start | bytes 98312 | tf_op jit(solution)/shard_map/ppermute | solution.py:347
  24.1 2.9 %collective-permute-done.9.refs_3_ = bf16[128,128]{1,0:T(8,128)(2,1)S(1)} collective-permute-done((bf16[128,128]{1,0:T(8,128)(2,1)S(1)}, bf16[128,128]{1,0:T(8,128)(2,1)S(1)}, u32[]{:S(2)}, u32[]{:S(2)}) %collective-permute-start.9) | collective-permute-done | bytes 32800 | tf_op jit(solution)/shard_map/ppermute | solution.py:347
  26.9 0.0 collective-permute-done.7.refs_1_
  27.0 0.1 collective-permute-start.10
  27.1 1.5 %collective-permute-done.10.refs_4_ = bf16[256,512]{1,0:T(8,128)(2,1)S(1)} collective-permute-done((bf16[256,512]{1,0:T(8,128)(2,1)S(1)}, bf16[256,512]{1,0:T(8,128)(2,1)S(1)}, u32[]{:S(2)}, u32[]{:S(2)}) %collective-permute-start.10) | collective-permute-done | bytes 262176 | tf_op jit(solution)/shard_map/ppermute | solution.py:347
  28.6 6.1 %shard_map.41 = (bf16[32,512]{1,0:T(8,128)(2,1)S(1)}, bf16[32,512]{1,0:T(8,128)(2,1)S(1)}) custom-call(s32[2,2]{1,0:T(2,128)} %counts_hbm.1, bf16[128,384]{1,0:T(8,128)(2,1)S(1)} %add_convert_fusion.3.refs_0_, bf16[128,384]{1,0:T(8,128)(2,1)S(1)} %collective-permute-done.7.refs_1_, bf16[128,128]{1,0:T(8,128)(2,1)S(1)} %add_convert_fusion.4.refs_2_, ...), custom_call_target="tpu_custom_call" | custom-call | tf_op jit(solution)/shard_map/pallas_call | solution.py:294
  34.7 3.0 %collective-permute-start.13 = (bf16[32,512]{1,0:T(8,128)(2,1)S(1)}, bf16[32,512]{1,0:T(8,128)(2,1)S(1)}, u32[]{:S(2)}, u32[]{:S(2)}) collective-permute-start(bf16[32,512]{1,0:T(8,128)(2,1)S(1)} %get-tuple-element.33), channel_id=1, source_target_pairs={{0,5},{1,4},{4,1},{5,0},{2,7},{3,6},{6,3},{7,2},{8,13},{9,12},{12,... | collective-permute-start | bytes 98312 | tf_op jit(solution)/shard_map/ppermute | solution.py:399
  37.8 0.0 collective-permute-start.11
  37.8 0.6 %collective-permute-start.12 = (bf16[32,512]{1,0:T(8,128)(2,1)S(1)}, bf16[32,512]{1,0:T(8,128)(2,1)S(1)}, u32[]{:S(2)}, u32[]{:S(2)}) collective-permute-start(bf16[32,512]{1,0:T(8,128)(2,1)S(1)} %get-tuple-element.34.refs_3_), channel_id=1, source_target_pairs={{0,1},{1,0},{4,5},{5,4},{2,3},{3,2},{6,7},{7,6},{8,9},{9,8},{12,13... | collective-permute-start | bytes 98312 | tf_op jit(solution)/shard_map/ppermute | solution.py:399
  38.4 1.3 %collective-permute-done.13.refs_2_ = bf16[32,512]{1,0:T(8,128)(2,1)S(1)} collective-permute-done((bf16[32,512]{1,0:T(8,128)(2,1)S(1)}, bf16[32,512]{1,0:T(8,128)(2,1)S(1)}, u32[]{:S(2)}, u32[]{:S(2)}) %collective-permute-start.13) | collective-permute-done | bytes 32800 | tf_op jit(solution)/shard_map/ppermute | solution.py:399
  39.7 2.0 %collective-permute-done.11.refs_0_ = bf16[32,512]{1,0:T(8,128)(2,1)S(1)} collective-permute-done((bf16[32,512]{1,0:T(8,128)(2,1)S(1)}, bf16[32,512]{1,0:T(8,128)(2,1)S(1)}, u32[]{:S(2)}, u32[]{:S(2)}) %collective-permute-start.11) | collective-permute-done | bytes 32800 | tf_op jit(solution)/shard_map/ppermute | solution.py:399
  41.7 0.0 collective-permute-done.12.refs_1_
  41.7 0.7 %shard_map.42 = bf16[4,32,512]{2,1,0:T(8,128)(2,1)} custom-call(bf16[32,512]{1,0:T(8,128)(2,1)S(1)} %collective-permute-done.11.refs_0_, bf16[32,512]{1,0:T(8,128)(2,1)S(1)} %collective-permute-done.12.refs_1_, bf16[32,512]{1,0:T(8,128)(2,1)S(1)} %collective-permute-done.13.refs_2_, bf16[32,512]{1,0:T(8,128)(2,1)S(1)} %get-tuple-element.34.refs_3_), custom_call_target="tpu_custom_call" | custom-call | tf_op jit(solution)/shard_map/pallas_call | solution.py:330
  (5 shorter events, 0.1 us)
Async XLA Ops:
  1.7 1.6 %collective-permute-start = (bf16[128,512]{1,0:T(8,128)(2,1)S(1)}, bf16[128,512]{1,0:T(8,128)(2,1)S(1)}, u32[]{:S(2)}, u32[]{:S(2)}) collective-permute-start(bf16[128,512]{1,0:T(8,128)(2,1)S(1)} %get-tuple-element.23), channel_id=1, source_target_pairs={{0,2},{2,0},{1,3},{3,1},{4,6},{6,4},{5,7},{7,5},{8,10},{10,8},{9,1... | collective-permute-start | bytes 393224 | tf_op jit(solution)/shard_map/ppermute | solution.py:347
  2.2 4.0 %collective-permute-start.3 = (bf16[128,512]{1,0:T(8,128)(2,1)S(1)}, bf16[128,512]{1,0:T(8,128)(2,1)S(1)}, u32[]{:S(2)}, u32[]{:S(2)}) collective-permute-start(bf16[128,512]{1,0:T(8,128)(2,1)S(1)} %get-tuple-element.28), channel_id=1, source_target_pairs={{0,2},{2,0},{1,3},{3,1},{4,6},{6,4},{5,7},{7,5},{8,10},{10,8},{9,1... | collective-permute-start | bytes 393224 | tf_op jit(solution)/shard_map/ppermute | solution.py:347
  2.7 5.4 %collective-permute-start.1 = (bf16[256,512]{1,0:T(8,128)(2,1)S(1)}, bf16[256,512]{1,0:T(8,128)(2,1)S(1)}, u32[]{:S(2)}, u32[]{:S(2)}) collective-permute-start(bf16[256,512]{1,0:T(8,128)(2,1)S(1)} %get-tuple-element.25), channel_id=1, source_target_pairs={{0,2},{2,0},{1,3},{3,1},{4,6},{6,4},{5,7},{7,5},{8,10},{10,8},{9,1... | collective-permute-start | bytes 786440 | tf_op jit(solution)/shard_map/ppermute | solution.py:347
  3.3 6.8 %collective-permute-start.5 = (bf16[128,512]{1,0:T(8,128)(2,1)S(1)}, bf16[128,512]{1,0:T(8,128)(2,1)S(1)}, u32[]{:S(2)}, u32[]{:S(2)}) collective-permute-start(bf16[128,512]{1,0:T(8,128)(2,1)S(1)} %add_convert_fusion.2.refs_0_), channel_id=1, source_target_pairs={{0,8},{8,0},{16,24},{24,16},{1,9},{9,1},{17,25},{25,17},{2,10},{10... | collective-permute-start | bytes 393224 | tf_op jit(solution)/shard_map/ppermute | solution.py:347
  6.3 8.2 %collective-permute-start.4 = (bf16[128,512]{1,0:T(8,128)(2,1)S(1)}, bf16[128,512]{1,0:T(8,128)(2,1)S(1)}, u32[]{:S(2)}, u32[]{:S(2)}) collective-permute-start(bf16[128,512]{1,0:T(8,128)(2,1)S(1)} %add_convert_fusion), channel_id=1, source_target_pairs={{0,4},{4,0},{1,5},{5,1},{2,6},{6,2},{3,7},{7,3},{8,12},{12,8},{9,1... | collective-permute-start | bytes 393224 | tf_op jit(solution)/shard_map/ppermute | solution.py:347
  8.2 6.2 %collective-permute-start.2 = (bf16[128,512]{1,0:T(8,128)(2,1)S(1)}, bf16[128,512]{1,0:T(8,128)(2,1)S(1)}, u32[]{:S(2)}, u32[]{:S(2)}) collective-permute-start(bf16[128,512]{1,0:T(8,128)(2,1)S(1)} %get-tuple-element.35), channel_id=1, source_target_pairs={{0,12},{4,8},{8,4},{12,0},{16,28},{20,24},{24,20},{28,16},{1,13},{... | collective-permute-start | bytes 393224 | tf_op jit(solution)/shard_map/ppermute | solution.py:351
  14.5 7.3 %collective-permute-start.6 = (bf16[128,384]{1,0:T(8,128)(2,1)S(1)}, bf16[128,384]{1,0:T(8,128)(2,1)S(1)}, u32[]{:S(2)}, u32[]{:S(2)}) collective-permute-start(bf16[128,384]{1,0:T(8,128)(2,1)S(1)} %get-tuple-element.30), channel_id=1, source_target_pairs={{0,16},{8,24},{16,0},{24,8},{1,17},{9,25},{17,1},{25,9},{2,18},{10... | collective-permute-start | bytes 294920 | tf_op jit(solution)/shard_map/ppermute | solution.py:347
  17.2 5.6 %collective-permute-start.8 = (bf16[128,128]{1,0:T(8,128)(2,1)S(1)}, bf16[128,128]{1,0:T(8,128)(2,1)S(1)}, u32[]{:S(2)}, u32[]{:S(2)}) collective-permute-start(bf16[128,128]{1,0:T(8,128)(2,1)S(1)} %get-tuple-element.32), channel_id=1, source_target_pairs={{0,16},{8,24},{16,0},{24,8},{1,17},{9,25},{17,1},{25,9},{2,18},{10... | collective-permute-start | bytes 98312 | tf_op jit(solution)/shard_map/ppermute | solution.py:347
  21.9 5.0 %collective-permute-start.7 = (bf16[128,384]{1,0:T(8,128)(2,1)S(1)}, bf16[128,384]{1,0:T(8,128)(2,1)S(1)}, u32[]{:S(2)}, u32[]{:S(2)}) collective-permute-start(bf16[128,384]{1,0:T(8,128)(2,1)S(1)} %add_convert_fusion.3.refs_0_), channel_id=1, source_target_pairs={{0,8},{8,0},{16,24},{24,16},{1,9},{9,1},{17,25},{25,17},{2,10},{10... | collective-permute-start | bytes 294920 | tf_op jit(solution)/shard_map/ppermute | solution.py:347
  22.8 4.2 %collective-permute-start.9 = (bf16[128,128]{1,0:T(8,128)(2,1)S(1)}, bf16[128,128]{1,0:T(8,128)(2,1)S(1)}, u32[]{:S(2)}, u32[]{:S(2)}) collective-permute-start(bf16[128,128]{1,0:T(8,128)(2,1)S(1)} %add_convert_fusion.4.refs_2_), channel_id=1, source_target_pairs={{0,8},{8,0},{16,24},{24,16},{1,9},{9,1},{17,25},{25,17},{2,10},{10... | collective-permute-start | bytes 98312 | tf_op jit(solution)/shard_map/ppermute | solution.py:347
  27.0 1.6 %collective-permute-start.10 = (bf16[256,512]{1,0:T(8,128)(2,1)S(1)}, bf16[256,512]{1,0:T(8,128)(2,1)S(1)}, u32[]{:S(2)}, u32[]{:S(2)}) collective-permute-start(bf16[256,512]{1,0:T(8,128)(2,1)S(1)} %maximum_maximum_fusion), channel_id=1, source_target_pairs={{0,2},{2,0},{1,3},{3,1},{4,6},{6,4},{5,7},{7,5},{8,10},{10,8},{9,1... | collective-permute-start | bytes 786440 | tf_op jit(solution)/shard_map/ppermute | solution.py:347
  34.7 4.9 %collective-permute-start.13 = (bf16[32,512]{1,0:T(8,128)(2,1)S(1)}, bf16[32,512]{1,0:T(8,128)(2,1)S(1)}, u32[]{:S(2)}, u32[]{:S(2)}) collective-permute-start(bf16[32,512]{1,0:T(8,128)(2,1)S(1)} %get-tuple-element.33), channel_id=1, source_target_pairs={{0,5},{1,4},{4,1},{5,0},{2,7},{3,6},{6,3},{7,2},{8,13},{9,12},{12,... | collective-permute-start | bytes 98312 | tf_op jit(solution)/shard_map/ppermute | solution.py:399
  37.8 3.9 %collective-permute-start.11 = (bf16[32,512]{1,0:T(8,128)(2,1)S(1)}, bf16[32,512]{1,0:T(8,128)(2,1)S(1)}, u32[]{:S(2)}, u32[]{:S(2)}) collective-permute-start(bf16[32,512]{1,0:T(8,128)(2,1)S(1)} %get-tuple-element.33), channel_id=1, source_target_pairs={{0,4},{1,5},{4,0},{5,1},{2,6},{3,7},{6,2},{7,3},{8,12},{9,13},{12,... | collective-permute-start | bytes 98312 | tf_op jit(solution)/shard_map/ppermute | solution.py:399
  37.8 3.9 %collective-permute-start.12 = (bf16[32,512]{1,0:T(8,128)(2,1)S(1)}, bf16[32,512]{1,0:T(8,128)(2,1)S(1)}, u32[]{:S(2)}, u32[]{:S(2)}) collective-permute-start(bf16[32,512]{1,0:T(8,128)(2,1)S(1)} %get-tuple-element.34.refs_3_), channel_id=1, source_target_pairs={{0,1},{1,0},{4,5},{5,4},{2,3},{3,2},{6,7},{7,6},{8,9},{9,8},{12,13... | collective-permute-start | bytes 98312 | tf_op jit(solution)/shard_map/ppermute | solution.py:399

commit v28 on v20

--- a/solution.py
+++ b/solution.py
@@ -312,7 +312,7 @@
 
 
 def place_kernel(origins, *refs):
-    *pieces, out, sems = refs
+    pieces, out, sems = refs[: len(origins)], refs[-2], refs[-1]
     column, group = lax.axis_index("x"), lax.axis_index("group")
     copies = []
     for index, (piece, (turn, flip)) in enumerate(zip(pieces, origins)):
@@ -323,17 +323,18 @@
         copy.wait()
 
 
-def place(found):
+def place(found, total, begun=()):
     origins, pieces = zip(*found.items())
     rows, width = pieces[0].shape
     return pl.pallas_call(
         functools.partial(place_kernel, origins),
-        out_shape=jax.ShapeDtypeStruct((len(pieces), rows, width), BF16),
-        in_specs=[VMEM] * len(pieces),
+        out_shape=jax.ShapeDtypeStruct((total, rows, width), BF16),
+        in_specs=[VMEM] * len(pieces) + [HBM] * len(begun),
         out_specs=HBM,
+        input_output_aliases={len(pieces): 0} if begun else {},
         scratch_shapes=[pltpu.SemaphoreType.DMA((len(pieces),))],
         compiler_params=params(16),
-    )(*pieces)
+    )(*pieces, *begun)
 
 
 def shards(line, groups, patches, cotangents, newton_counts):
@@ -397,8 +398,9 @@
 
     others = [(turn, flip) for turn in range(groups) for flip in range(2) if turn or flip]
     found = {(turn, flip): pass_on(turn, flip) for turn, flip in others}
+    last = {(1, 0): found.pop((1, 0))}
     found[0, 0] = keep
-    return place(found)
+    return place(last, 2 * groups, (place(found, 2 * groups),))
 
 
 def solution(mesh):

time: 42.2 us -> 42.8 us (1.014)
  Pallas kernels: 9.35 us -> 9.97 us
    pallas_call x1 -> x2, Pallas kernels: 0.68 us -> 1.3 us  [place(): pl.pallas_call(functools.partial(place_kernel, origins), out_shape=jax.Sh...]
  transfers between devices with their start and end apart: 15 -> 15, of which waited for: 8 -> 8; matrix products, arithmetic and copies ran while one was open for 0% -> 0% of each run, Pallas kernels for 2% -> 3%
where the time goes in v28:
time: 42.8 us; the launch traced here: 42.7 us
  waiting for transfers between devices  17.4 us (41%)
  starting transfers between devices  15 us (35%)
  Pallas kernels  9.97 us (23%)
    ppermute x11, waiting for transfers between devices, swap(): lax.ppermute(array, axis, [(i, i ^ mask) for i in range(lax.axis_size(axi...  14.1 us
    ppermute x11, starting transfers between devices, swap(): lax.ppermute(array, axis, [(i, i ^ mask) for i in range(lax.axis_size(axi...  11.1 us
    pallas_call x1, Pallas kernels, root(): pl.pallas_call(functools.partial(root_kernel, most), out_shape=[out, out]...  6.15 us
    ppermute x3, starting transfers between devices, pass_on(): return lax.ppermute(send if flip else keep, ('x', 'group'), moves)  3.69 us
    ppermute x3, waiting for transfers between devices, pass_on(): return lax.ppermute(send if flip else keep, ('x', 'group'), moves)  3.27 us
    pallas_call x1, Pallas kernels, load(): pl.pallas_call(functools.partial(load_kernel, scale), out_shape=[jax.Shap...  1.67 us
    pallas_call x2, Pallas kernels, place(): pl.pallas_call(functools.partial(place_kernel, origins), out_shape=jax.Sh...  1.3 us
  transfers between devices with their start and end apart: 15, of which 8 were waited for; matrix products, arithmetic and copies ran while one was open for 0% of the time, Pallas kernels for 3%

profile of v28, /device:TPU:0, one launch (start us, length us, event | category | flops | bytes accessed | tf_op | source)
XLA Modules:
  0.0 42.7 jit_solution(12946683165887605985)
XLA Ops:
  0.0 1.7 %shard_map.37 = (bf16[128,512]{1,0:T(8,128)(2,1)S(1)}, bf16[128,512]{1,0:T(8,128)(2,1)S(1)}, bf16[2,2,512,256]{3,2,1,0:T(8,128)(2,1)S(1)}, bf16[2,512,512]{2,1,0:T(8,128)(2,1)S(1)}) custom-call(bf16[2,512,512]{2,1,0:T(8,128)(2,1)} %patch_hbm.1, bf16[2,512,512]{2,1,0:T(8,128)(2,1)} %cot_hbm.1), custom_call_target="tpu_custom_call" | custom-call | tf_op jit(solution)/shard_map/pallas_call | solution.py:70
  1.7 0.5 %collective-permute-start = (bf16[128,512]{1,0:T(8,128)(2,1)S(1)}, bf16[128,512]{1,0:T(8,128)(2,1)S(1)}, u32[]{:S(2)}, u32[]{:S(2)}) collective-permute-start(bf16[128,512]{1,0:T(8,128)(2,1)S(1)} %get-tuple-element.23), channel_id=1, source_target_pairs={{0,2},{2,0},{1,3},{3,1},{4,6},{6,4},{5,7},{7,5},{8,10},{10,8},{9,1... | collective-permute-start | bytes 393224 | tf_op jit(solution)/shard_map/ppermute | solution.py:347
  2.2 0.1 collective-permute-start.3
  2.3 0.5 %shard_map.38 = (f32[128,512]{1,0:T(8,128)S(1)}, f32[128,512]{1,0:T(8,128)S(1)}, bf16[256,512]{1,0:T(8,128)(2,1)S(1)}) custom-call(bf16[2,2,512,256]{3,2,1,0:T(8,128)(2,1)S(1)} %get-tuple-element.20.patch, bf16[2,512,512]{2,1,0:T(8,128)(2,1)S(1)} %get-tuple-element.21.cot), custom_call_target="tpu_custom_call" | custom-call | flops 402653184 | bytes 1048576 | tf_op jit(solution)/shard_map/pallas_call | solution.py:98
  2.7 0.5 %collective-permute-start.1 = (bf16[256,512]{1,0:T(8,128)(2,1)S(1)}, bf16[256,512]{1,0:T(8,128)(2,1)S(1)}, u32[]{:S(2)}, u32[]{:S(2)}) collective-permute-start(bf16[256,512]{1,0:T(8,128)(2,1)S(1)} %get-tuple-element.25), channel_id=1, source_target_pairs={{0,2},{2,0},{1,3},{3,1},{4,6},{6,4},{5,7},{7,5},{8,10},{10,8},{9,1... | collective-permute-start | bytes 786440 | tf_op jit(solution)/shard_map/ppermute | solution.py:347
  3.2 0.0 collective-permute-done
  3.3 2.9 %collective-permute-start.5 = (bf16[128,512]{1,0:T(8,128)(2,1)S(1)}, bf16[128,512]{1,0:T(8,128)(2,1)S(1)}, u32[]{:S(2)}, u32[]{:S(2)}) collective-permute-start(bf16[128,512]{1,0:T(8,128)(2,1)S(1)} %add_convert_fusion.2.refs_0_), channel_id=1, source_target_pairs={{0,8},{8,0},{16,24},{24,16},{1,9},{9,1},{17,25},{25,17},{2,10},{10... | collective-permute-start | bytes 393224 | tf_op jit(solution)/shard_map/ppermute | solution.py:347
  6.2 0.0 collective-permute-done.3
  6.3 1.6 %collective-permute-start.4 = (bf16[128,512]{1,0:T(8,128)(2,1)S(1)}, bf16[128,512]{1,0:T(8,128)(2,1)S(1)}, u32[]{:S(2)}, u32[]{:S(2)}) collective-permute-start(bf16[128,512]{1,0:T(8,128)(2,1)S(1)} %add_convert_fusion), channel_id=1, source_target_pairs={{0,4},{4,0},{1,5},{5,1},{2,6},{6,2},{3,7},{7,3},{8,12},{12,8},{9,1... | collective-permute-start | bytes 393224 | tf_op jit(solution)/shard_map/ppermute | solution.py:347
  7.8 0.3 shard_map.39
  8.1 0.0 collective-permute-done.1
  8.1 0.1 add_convert_fusion.1
  8.2 0.2 collective-permute-start.2
  8.4 1.7 %collective-permute-done.5.refs_2_ = bf16[128,512]{1,0:T(8,128)(2,1)S(1)} collective-permute-done((bf16[128,512]{1,0:T(8,128)(2,1)S(1)}, bf16[128,512]{1,0:T(8,128)(2,1)S(1)}, u32[]{:S(2)}, u32[]{:S(2)}) %collective-permute-start.5) | collective-permute-done | bytes 131104 | tf_op jit(solution)/shard_map/ppermute | solution.py:347
  10.1 4.4 %collective-permute-done.4.refs_1_ = bf16[128,512]{1,0:T(8,128)(2,1)S(1)} collective-permute-done((bf16[128,512]{1,0:T(8,128)(2,1)S(1)}, bf16[128,512]{1,0:T(8,128)(2,1)S(1)}, u32[]{:S(2)}, u32[]{:S(2)}) %collective-permute-start.4) | collective-permute-done | bytes 131104 | tf_op jit(solution)/shard_map/ppermute | solution.py:347
  14.5 0.0 collective-permute-done.2.refs_0_
  14.5 0.1 shard_map.40
  14.5 2.7 %collective-permute-start.6 = (bf16[128,384]{1,0:T(8,128)(2,1)S(1)}, bf16[128,384]{1,0:T(8,128)(2,1)S(1)}, u32[]{:S(2)}, u32[]{:S(2)}) collective-permute-start(bf16[128,384]{1,0:T(8,128)(2,1)S(1)} %get-tuple-element.30), channel_id=1, source_target_pairs={{0,16},{8,24},{16,0},{24,8},{1,17},{9,25},{17,1},{25,9},{2,18},{10... | collective-permute-start | bytes 294920 | tf_op jit(solution)/shard_map/ppermute | solution.py:347
  17.2 0.3 collective-permute-start.9
  17.5 4.4 %collective-permute-done.6 = bf16[128,384]{1,0:T(8,128)(2,1)S(1)} collective-permute-done((bf16[128,384]{1,0:T(8,128)(2,1)S(1)}, bf16[128,384]{1,0:T(8,128)(2,1)S(1)}, u32[]{:S(2)}, u32[]{:S(2)}) %collective-permute-start.6) | collective-permute-done | bytes 98336 | tf_op jit(solution)/shard_map/ppermute | solution.py:347
  21.9 0.8 %collective-permute-start.7 = (bf16[128,384]{1,0:T(8,128)(2,1)S(1)}, bf16[128,384]{1,0:T(8,128)(2,1)S(1)}, u32[]{:S(2)}, u32[]{:S(2)}) collective-permute-start(bf16[128,384]{1,0:T(8,128)(2,1)S(1)} %add_convert_fusion.3.refs_0_), channel_id=1, source_target_pairs={{0,8},{8,0},{16,24},{24,16},{1,9},{9,1},{17,25},{25,17},{2,10},{10... | collective-permute-start | bytes 294920 | tf_op jit(solution)/shard_map/ppermute | solution.py:347
  22.7 0.0 collective-permute-done.9
  22.8 1.3 %collective-permute-start.10 = (bf16[128,128]{1,0:T(8,128)(2,1)S(1)}, bf16[128,128]{1,0:T(8,128)(2,1)S(1)}, u32[]{:S(2)}, u32[]{:S(2)}) collective-permute-start(bf16[128,128]{1,0:T(8,128)(2,1)S(1)} %add_convert_fusion.4.refs_3_), channel_id=1, source_target_pairs={{0,8},{8,0},{16,24},{24,16},{1,9},{9,1},{17,25},{25,17},{2,10},{10... | collective-permute-start | bytes 98312 | tf_op jit(solution)/shard_map/ppermute | solution.py:347
  24.1 2.5 %collective-permute-done.7.refs_1_ = bf16[128,384]{1,0:T(8,128)(2,1)S(1)} collective-permute-done((bf16[128,384]{1,0:T(8,128)(2,1)S(1)}, bf16[128,384]{1,0:T(8,128)(2,1)S(1)}, u32[]{:S(2)}, u32[]{:S(2)}) %collective-permute-start.7) | collective-permute-done | bytes 98336 | tf_op jit(solution)/shard_map/ppermute | solution.py:347
  26.6 0.1 collective-permute-start.8
  26.7 0.2 collective-permute-done.10.refs_4_
  26.9 0.3 collective-permute-start.11
  27.3 0.9 %collective-permute-done.11.refs_5_ = bf16[256,128]{1,0:T(8,128)(2,1)S(1)} collective-permute-done((bf16[256,128]{1,0:T(8,128)(2,1)S(1)}, bf16[256,128]{1,0:T(8,128)(2,1)S(1)}, u32[]{:S(2)}, u32[]{:S(2)}) %collective-permute-start.11) | collective-permute-done | bytes 65568 | tf_op jit(solution)/shard_map/ppermute | solution.py:347
  28.2 0.0 collective-permute-done.8.refs_2_
  28.2 6.1 %shard_map.41 = (bf16[32,512]{1,0:T(8,128)(2,1)S(1)}, bf16[32,512]{1,0:T(8,128)(2,1)S(1)}) custom-call(s32[2,2]{1,0:T(2,128)} %counts_hbm.1, bf16[128,384]{1,0:T(8,128)(2,1)S(1)} %add_convert_fusion.3.refs_0_, bf16[128,384]{1,0:T(8,128)(2,1)S(1)} %collective-permute-done.7.refs_1_, bf16[256,384]{1,0:T(8,128)(2,1)S(1)} %collective-permute-done.8.refs_2_, ...), custom_call_target="tpu_custom_call" | custom-call | tf_op jit(solution)/shard_map/pallas_call | solution.py:293
  34.4 3.1 %collective-permute-start.14 = (bf16[32,512]{1,0:T(8,128)(2,1)S(1)}, bf16[32,512]{1,0:T(8,128)(2,1)S(1)}, u32[]{:S(2)}, u32[]{:S(2)}) collective-permute-start(bf16[32,512]{1,0:T(8,128)(2,1)S(1)} %get-tuple-element.34), channel_id=1, source_target_pairs={{0,5},{1,4},{4,1},{5,0},{2,7},{3,6},{6,3},{7,2},{8,13},{9,12},{12,... | collective-permute-start | bytes 98312 | tf_op jit(solution)/shard_map/ppermute | solution.py:397
  37.4 0.0 collective-permute-start.13
  37.4 0.6 %collective-permute-start.12 = (bf16[32,512]{1,0:T(8,128)(2,1)S(1)}, bf16[32,512]{1,0:T(8,128)(2,1)S(1)}, u32[]{:S(2)}, u32[]{:S(2)}) collective-permute-start(bf16[32,512]{1,0:T(8,128)(2,1)S(1)} %get-tuple-element.33.refs_2_), channel_id=1, source_target_pairs={{0,1},{1,0},{4,5},{5,4},{2,3},{3,2},{6,7},{7,6},{8,9},{9,8},{12,13... | collective-permute-start | bytes 98312 | tf_op jit(solution)/shard_map/ppermute | solution.py:397
  38.1 1.3 %collective-permute-done.14.refs_1_ = bf16[32,512]{1,0:T(8,128)(2,1)S(1)} collective-permute-done((bf16[32,512]{1,0:T(8,128)(2,1)S(1)}, bf16[32,512]{1,0:T(8,128)(2,1)S(1)}, u32[]{:S(2)}, u32[]{:S(2)}) %collective-permute-start.14) | collective-permute-done | bytes 32800 | tf_op jit(solution)/shard_map/ppermute | solution.py:397
  39.3 2.0 %collective-permute-done.13.refs_0_ = bf16[32,512]{1,0:T(8,128)(2,1)S(1)} collective-permute-done((bf16[32,512]{1,0:T(8,128)(2,1)S(1)}, bf16[32,512]{1,0:T(8,128)(2,1)S(1)}, u32[]{:S(2)}, u32[]{:S(2)}) %collective-permute-start.13) | collective-permute-done | bytes 32800 | tf_op jit(solution)/shard_map/ppermute | solution.py:397
  41.3 0.7 %shard_map.42.refs_1_ = bf16[4,32,512]{2,1,0:T(8,128)(2,1)} custom-call(bf16[32,512]{1,0:T(8,128)(2,1)S(1)} %collective-permute-done.13.refs_0_, bf16[32,512]{1,0:T(8,128)(2,1)S(1)} %collective-permute-done.14.refs_1_, bf16[32,512]{1,0:T(8,128)(2,1)S(1)} %get-tuple-element.33.refs_2_), custom_call_target="tpu_custom_call" | custom-call | tf_op jit(solution)/shard_map/pallas_call | solution.py:329
  42.0 0.0 collective-permute-done.12.refs_0_
  42.0 0.6 %shard_map.43 = bf16[4,32,512]{2,1,0:T(8,128)(2,1)} custom-call(bf16[32,512]{1,0:T(8,128)(2,1)S(1)} %collective-permute-done.12.refs_0_, bf16[4,32,512]{2,1,0:T(8,128)(2,1)} %shard_map.42.refs_1_), custom_call_target="tpu_custom_call", output_to_operand_aliasing={{}: (1, {})} | custom-call | tf_op jit(solution)/shard_map/pallas_call | solution.py:329
  (6 shorter events, 0.1 us)
Async XLA Ops:
  1.7 1.6 %collective-permute-start = (bf16[128,512]{1,0:T(8,128)(2,1)S(1)}, bf16[128,512]{1,0:T(8,128)(2,1)S(1)}, u32[]{:S(2)}, u32[]{:S(2)}) collective-permute-start(bf16[128,512]{1,0:T(8,128)(2,1)S(1)} %get-tuple-element.23), channel_id=1, source_target_pairs={{0,2},{2,0},{1,3},{3,1},{4,6},{6,4},{5,7},{7,5},{8,10},{10,8},{9,1... | collective-permute-start | bytes 393224 | tf_op jit(solution)/shard_map/ppermute | solution.py:347
  2.2 4.0 %collective-permute-start.3 = (bf16[128,512]{1,0:T(8,128)(2,1)S(1)}, bf16[128,512]{1,0:T(8,128)(2,1)S(1)}, u32[]{:S(2)}, u32[]{:S(2)}) collective-permute-start(bf16[128,512]{1,0:T(8,128)(2,1)S(1)} %get-tuple-element.28), channel_id=1, source_target_pairs={{0,2},{2,0},{1,3},{3,1},{4,6},{6,4},{5,7},{7,5},{8,10},{10,8},{9,1... | collective-permute-start | bytes 393224 | tf_op jit(solution)/shard_map/ppermute | solution.py:347
  2.7 5.4 %collective-permute-start.1 = (bf16[256,512]{1,0:T(8,128)(2,1)S(1)}, bf16[256,512]{1,0:T(8,128)(2,1)S(1)}, u32[]{:S(2)}, u32[]{:S(2)}) collective-permute-start(bf16[256,512]{1,0:T(8,128)(2,1)S(1)} %get-tuple-element.25), channel_id=1, source_target_pairs={{0,2},{2,0},{1,3},{3,1},{4,6},{6,4},{5,7},{7,5},{8,10},{10,8},{9,1... | collective-permute-start | bytes 786440 | tf_op jit(solution)/shard_map/ppermute | solution.py:347
  3.3 6.8 %collective-permute-start.5 = (bf16[128,512]{1,0:T(8,128)(2,1)S(1)}, bf16[128,512]{1,0:T(8,128)(2,1)S(1)}, u32[]{:S(2)}, u32[]{:S(2)}) collective-permute-start(bf16[128,512]{1,0:T(8,128)(2,1)S(1)} %add_convert_fusion.2.refs_0_), channel_id=1, source_target_pairs={{0,8},{8,0},{16,24},{24,16},{1,9},{9,1},{17,25},{25,17},{2,10},{10... | collective-permute-start | bytes 393224 | tf_op jit(solution)/shard_map/ppermute | solution.py:347
  6.3 8.2 %collective-permute-start.4 = (bf16[128,512]{1,0:T(8,128)(2,1)S(1)}, bf16[128,512]{1,0:T(8,128)(2,1)S(1)}, u32[]{:S(2)}, u32[]{:S(2)}) collective-permute-start(bf16[128,512]{1,0:T(8,128)(2,1)S(1)} %add_convert_fusion), channel_id=1, source_target_pairs={{0,4},{4,0},{1,5},{5,1},{2,6},{6,2},{3,7},{7,3},{8,12},{12,8},{9,1... | collective-permute-start | bytes 393224 | tf_op jit(solution)/shard_map/ppermute | solution.py:347
  8.2 6.2 %collective-permute-start.2 = (bf16[128,512]{1,0:T(8,128)(2,1)S(1)}, bf16[128,512]{1,0:T(8,128)(2,1)S(1)}, u32[]{:S(2)}, u32[]{:S(2)}) collective-permute-start(bf16[128,512]{1,0:T(8,128)(2,1)S(1)} %get-tuple-element.35), channel_id=1, source_target_pairs={{0,12},{4,8},{8,4},{12,0},{16,28},{20,24},{24,20},{28,16},{1,13},{... | collective-permute-start | bytes 393224 | tf_op jit(solution)/shard_map/ppermute | solution.py:351
  14.5 7.3 %collective-permute-start.6 = (bf16[128,384]{1,0:T(8,128)(2,1)S(1)}, bf16[128,384]{1,0:T(8,128)(2,1)S(1)}, u32[]{:S(2)}, u32[]{:S(2)}) collective-permute-start(bf16[128,384]{1,0:T(8,128)(2,1)S(1)} %get-tuple-element.30), channel_id=1, source_target_pairs={{0,16},{8,24},{16,0},{24,8},{1,17},{9,25},{17,1},{25,9},{2,18},{10... | collective-permute-start | bytes 294920 | tf_op jit(solution)/shard_map/ppermute | solution.py:347
  17.2 5.6 %collective-permute-start.9 = (bf16[128,128]{1,0:T(8,128)(2,1)S(1)}, bf16[128,128]{1,0:T(8,128)(2,1)S(1)}, u32[]{:S(2)}, u32[]{:S(2)}) collective-permute-start(bf16[128,128]{1,0:T(8,128)(2,1)S(1)} %get-tuple-element.32), channel_id=1, source_target_pairs={{0,16},{8,24},{16,0},{24,8},{1,17},{9,25},{17,1},{25,9},{2,18},{10... | collective-permute-start | bytes 98312 | tf_op jit(solution)/shard_map/ppermute | solution.py:347
  21.9 4.7 %collective-permute-start.7 = (bf16[128,384]{1,0:T(8,128)(2,1)S(1)}, bf16[128,384]{1,0:T(8,128)(2,1)S(1)}, u32[]{:S(2)}, u32[]{:S(2)}) collective-permute-start(bf16[128,384]{1,0:T(8,128)(2,1)S(1)} %add_convert_fusion.3.refs_0_), channel_id=1, source_target_pairs={{0,8},{8,0},{16,24},{24,16},{1,9},{9,1},{17,25},{25,17},{2,10},{10... | collective-permute-start | bytes 294920 | tf_op jit(solution)/shard_map/ppermute | solution.py:347
  22.8 4.2 %collective-permute-start.10 = (bf16[128,128]{1,0:T(8,128)(2,1)S(1)}, bf16[128,128]{1,0:T(8,128)(2,1)S(1)}, u32[]{:S(2)}, u32[]{:S(2)}) collective-permute-start(bf16[128,128]{1,0:T(8,128)(2,1)S(1)} %add_convert_fusion.4.refs_3_), channel_id=1, source_target_pairs={{0,8},{8,0},{16,24},{24,16},{1,9},{9,1},{17,25},{25,17},{2,10},{10... | collective-permute-start | bytes 98312 | tf_op jit(solution)/shard_map/ppermute | solution.py:347
  26.6 1.6 %collective-permute-start.8 = (bf16[256,384]{1,0:T(8,128)(2,1)S(1)}, bf16[256,384]{1,0:T(8,128)(2,1)S(1)}, u32[]{:S(2)}, u32[]{:S(2)}) collective-permute-start(bf16[256,384]{1,0:T(8,128)(2,1)S(1)} %pad_maximum_fusion), channel_id=1, source_target_pairs={{0,2},{2,0},{1,3},{3,1},{4,6},{6,4},{5,7},{7,5},{8,10},{10,8},{9,1... | collective-permute-start | bytes 589832 | tf_op jit(solution)/shard_map/ppermute | solution.py:347
  26.9 1.3 %collective-permute-start.11 = (bf16[256,128]{1,0:T(8,128)(2,1)S(1)}, bf16[256,128]{1,0:T(8,128)(2,1)S(1)}, u32[]{:S(2)}, u32[]{:S(2)}) collective-permute-start(bf16[256,128]{1,0:T(8,128)(2,1)S(1)} %pad_maximum_fusion.1), channel_id=1, source_target_pairs={{0,2},{2,0},{1,3},{3,1},{4,6},{6,4},{5,7},{7,5},{8,10},{10,8},{9,1... | collective-permute-start | bytes 196616 | tf_op jit(solution)/shard_map/ppermute | solution.py:347
  34.4 4.9 %collective-permute-start.14 = (bf16[32,512]{1,0:T(8,128)(2,1)S(1)}, bf16[32,512]{1,0:T(8,128)(2,1)S(1)}, u32[]{:S(2)}, u32[]{:S(2)}) collective-permute-start(bf16[32,512]{1,0:T(8,128)(2,1)S(1)} %get-tuple-element.34), channel_id=1, source_target_pairs={{0,5},{1,4},{4,1},{5,0},{2,7},{3,6},{6,3},{7,2},{8,13},{9,12},{12,... | collective-permute-start | bytes 98312 | tf_op jit(solution)/shard_map/ppermute | solution.py:397
  37.4 3.9 %collective-permute-start.13 = (bf16[32,512]{1,0:T(8,128)(2,1)S(1)}, bf16[32,512]{1,0:T(8,128)(2,1)S(1)}, u32[]{:S(2)}, u32[]{:S(2)}) collective-permute-start(bf16[32,512]{1,0:T(8,128)(2,1)S(1)} %get-tuple-element.34), channel_id=1, source_target_pairs={{0,4},{1,5},{4,0},{5,1},{2,6},{3,7},{6,2},{7,3},{8,12},{9,13},{12,... | collective-permute-start | bytes 98312 | tf_op jit(solution)/shard_map/ppermute | solution.py:397
  37.4 4.6 %collective-permute-start.12 = (bf16[32,512]{1,0:T(8,128)(2,1)S(1)}, bf16[32,512]{1,0:T(8,128)(2,1)S(1)}, u32[]{:S(2)}, u32[]{:S(2)}) collective-permute-start(bf16[32,512]{1,0:T(8,128)(2,1)S(1)} %get-tuple-element.33.refs_2_), channel_id=1, source_target_pairs={{0,1},{1,0},{4,5},{5,4},{2,3},{3,2},{6,7},{7,6},{8,9},{9,8},{12,13... | collective-permute-start | bytes 98312 | tf_op jit(solution)/shard_map/ppermute | solution.py:397

commit v29 on v20

--- a/solution.py
+++ b/solution.py
@@ -270,18 +270,11 @@
             fill(ref, start, factor(tiles))
     final_left = dot(left[:picked, :], left[picked:, :]).astype(BF16)
     final_left = jnp.where(most <= count_left, final_left, left[:picked, :])
-    by_high = dot(right[:width, :], right[width:, high])
-    by_low = dot(right[half:width, :], right[width:, low])
-    goes_on = most <= count_right
-    upper_right = jnp.where(goes_on, by_high[half:].astype(BF16), right[half:width, high])
-    right[half:width, low] = jnp.where(goes_on, by_low.astype(BF16), right[half:width, low])
-    right[half:width, high] = upper_right
-    right[:half, low] = upper_right.T
-    right[:half, high] = jnp.where(goes_on, by_high[:half].astype(BF16), right[:half, high])
     partial_value = dot(final_left, grad[...]).astype(BF16)
     update = dot(partial_value[:, low], right[half:width, :]) + dot(
         partial_value[:, high], right[:half, :]
     )
+    update = jnp.where(most <= count_right, dot(update.astype(BF16), right[width:, :]), update)
     keep_ref[...] = update[:rows, :].astype(BF16)
     send_ref[...] = update[rows:, :].astype(BF16)
 

time: 42.2 us -> 42.1 us (level)
  no operation moved by 1% of the time
where the time goes in v29:
time: 42.1 us; the launch traced here: 41.9 us
  waiting for transfers between devices  17.4 us (41%)
  starting transfers between devices  15 us (36%)
  Pallas kernels  9.26 us (22%)
    ppermute x11, waiting for transfers between devices, swap(): lax.ppermute(array, axis, [(i, i ^ mask) for i in range(lax.axis_size(axi...  14.1 us
    ppermute x11, starting transfers between devices, swap(): lax.ppermute(array, axis, [(i, i ^ mask) for i in range(lax.axis_size(axi...  11.1 us
    pallas_call x1, Pallas kernels, root(): pl.pallas_call(functools.partial(root_kernel, most), out_shape=[out, out]...  6.06 us
    ppermute x3, starting transfers between devices, pass_on(): return lax.ppermute(send if flip else keep, ('x', 'group'), moves)  3.69 us
    ppermute x3, waiting for transfers between devices, pass_on(): return lax.ppermute(send if flip else keep, ('x', 'group'), moves)  3.27 us
    pallas_call x1, Pallas kernels, load(): pl.pallas_call(functools.partial(load_kernel, scale), out_shape=[jax.Shap...  1.67 us
  transfers between devices with their start and end apart: 15, of which 8 were waited for; matrix products, arithmetic and copies ran while one was open for 0% of the time, Pallas kernels for 2%

profile of v29, /device:TPU:0, one launch (start us, length us, event | category | flops | bytes accessed | tf_op | source)
XLA Modules:
  0.0 41.9 jit_solution(2657314074550980540)
XLA Ops:
  0.0 1.7 %shard_map.37 = (bf16[128,512]{1,0:T(8,128)(2,1)S(1)}, bf16[128,512]{1,0:T(8,128)(2,1)S(1)}, bf16[2,2,512,256]{3,2,1,0:T(8,128)(2,1)S(1)}, bf16[2,512,512]{2,1,0:T(8,128)(2,1)S(1)}) custom-call(bf16[2,512,512]{2,1,0:T(8,128)(2,1)} %patch_hbm.1, bf16[2,512,512]{2,1,0:T(8,128)(2,1)} %cot_hbm.1), custom_call_target="tpu_custom_call" | custom-call | tf_op jit(solution)/shard_map/pallas_call | solution.py:70
  1.7 0.5 %collective-permute-start = (bf16[128,512]{1,0:T(8,128)(2,1)S(1)}, bf16[128,512]{1,0:T(8,128)(2,1)S(1)}, u32[]{:S(2)}, u32[]{:S(2)}) collective-permute-start(bf16[128,512]{1,0:T(8,128)(2,1)S(1)} %get-tuple-element.23), channel_id=1, source_target_pairs={{0,2},{2,0},{1,3},{3,1},{4,6},{6,4},{5,7},{7,5},{8,10},{10,8},{9,1... | collective-permute-start | bytes 393224 | tf_op jit(solution)/shard_map/ppermute | solution.py:339
  2.2 0.1 collective-permute-start.3
  2.3 0.5 %shard_map.38 = (f32[128,512]{1,0:T(8,128)S(1)}, f32[128,512]{1,0:T(8,128)S(1)}, bf16[256,512]{1,0:T(8,128)(2,1)S(1)}) custom-call(bf16[2,2,512,256]{3,2,1,0:T(8,128)(2,1)S(1)} %get-tuple-element.20.patch, bf16[2,512,512]{2,1,0:T(8,128)(2,1)S(1)} %get-tuple-element.21.cot), custom_call_target="tpu_custom_call" | custom-call | flops 402653184 | bytes 1048576 | tf_op jit(solution)/shard_map/pallas_call | solution.py:98
  2.7 0.5 %collective-permute-start.1 = (bf16[256,512]{1,0:T(8,128)(2,1)S(1)}, bf16[256,512]{1,0:T(8,128)(2,1)S(1)}, u32[]{:S(2)}, u32[]{:S(2)}) collective-permute-start(bf16[256,512]{1,0:T(8,128)(2,1)S(1)} %get-tuple-element.25), channel_id=1, source_target_pairs={{0,2},{2,0},{1,3},{3,1},{4,6},{6,4},{5,7},{7,5},{8,10},{10,8},{9,1... | collective-permute-start | bytes 786440 | tf_op jit(solution)/shard_map/ppermute | solution.py:339
  3.2 0.0 collective-permute-done
  3.3 2.9 %collective-permute-start.5 = (bf16[128,512]{1,0:T(8,128)(2,1)S(1)}, bf16[128,512]{1,0:T(8,128)(2,1)S(1)}, u32[]{:S(2)}, u32[]{:S(2)}) collective-permute-start(bf16[128,512]{1,0:T(8,128)(2,1)S(1)} %add_convert_fusion.2.refs_0_), channel_id=1, source_target_pairs={{0,8},{8,0},{16,24},{24,16},{1,9},{9,1},{17,25},{25,17},{2,10},{10... | collective-permute-start | bytes 393224 | tf_op jit(solution)/shard_map/ppermute | solution.py:339
  6.2 0.0 collective-permute-done.3
  6.3 1.6 %collective-permute-start.4 = (bf16[128,512]{1,0:T(8,128)(2,1)S(1)}, bf16[128,512]{1,0:T(8,128)(2,1)S(1)}, u32[]{:S(2)}, u32[]{:S(2)}) collective-permute-start(bf16[128,512]{1,0:T(8,128)(2,1)S(1)} %add_convert_fusion), channel_id=1, source_target_pairs={{0,4},{4,0},{1,5},{5,1},{2,6},{6,2},{3,7},{7,3},{8,12},{12,8},{9,1... | collective-permute-start | bytes 393224 | tf_op jit(solution)/shard_map/ppermute | solution.py:339
  7.8 0.3 shard_map.39
  8.1 0.0 collective-permute-done.1
  8.1 0.1 add_convert_fusion.1
  8.2 0.2 collective-permute-start.2
  8.4 1.7 %collective-permute-done.5.refs_2_ = bf16[128,512]{1,0:T(8,128)(2,1)S(1)} collective-permute-done((bf16[128,512]{1,0:T(8,128)(2,1)S(1)}, bf16[128,512]{1,0:T(8,128)(2,1)S(1)}, u32[]{:S(2)}, u32[]{:S(2)}) %collective-permute-start.5) | collective-permute-done | bytes 131104 | tf_op jit(solution)/shard_map/ppermute | solution.py:339
  10.1 4.4 %collective-permute-done.4.refs_1_ = bf16[128,512]{1,0:T(8,128)(2,1)S(1)} collective-permute-done((bf16[128,512]{1,0:T(8,128)(2,1)S(1)}, bf16[128,512]{1,0:T(8,128)(2,1)S(1)}, u32[]{:S(2)}, u32[]{:S(2)}) %collective-permute-start.4) | collective-permute-done | bytes 131104 | tf_op jit(solution)/shard_map/ppermute | solution.py:339
  14.5 0.0 collective-permute-done.2.refs_0_
  14.5 0.1 shard_map.40
  14.5 2.7 %collective-permute-start.6 = (bf16[128,384]{1,0:T(8,128)(2,1)S(1)}, bf16[128,384]{1,0:T(8,128)(2,1)S(1)}, u32[]{:S(2)}, u32[]{:S(2)}) collective-permute-start(bf16[128,384]{1,0:T(8,128)(2,1)S(1)} %get-tuple-element.30), channel_id=1, source_target_pairs={{0,16},{8,24},{16,0},{24,8},{1,17},{9,25},{17,1},{25,9},{2,18},{10... | collective-permute-start | bytes 294920 | tf_op jit(solution)/shard_map/ppermute | solution.py:339
  17.2 0.3 collective-permute-start.9
  17.5 4.4 %collective-permute-done.6 = bf16[128,384]{1,0:T(8,128)(2,1)S(1)} collective-permute-done((bf16[128,384]{1,0:T(8,128)(2,1)S(1)}, bf16[128,384]{1,0:T(8,128)(2,1)S(1)}, u32[]{:S(2)}, u32[]{:S(2)}) %collective-permute-start.6) | collective-permute-done | bytes 98336 | tf_op jit(solution)/shard_map/ppermute | solution.py:339
  21.9 0.8 %collective-permute-start.7 = (bf16[128,384]{1,0:T(8,128)(2,1)S(1)}, bf16[128,384]{1,0:T(8,128)(2,1)S(1)}, u32[]{:S(2)}, u32[]{:S(2)}) collective-permute-start(bf16[128,384]{1,0:T(8,128)(2,1)S(1)} %add_convert_fusion.3.refs_0_), channel_id=1, source_target_pairs={{0,8},{8,0},{16,24},{24,16},{1,9},{9,1},{17,25},{25,17},{2,10},{10... | collective-permute-start | bytes 294920 | tf_op jit(solution)/shard_map/ppermute | solution.py:339
  22.7 0.0 collective-permute-done.9
  22.8 1.3 %collective-permute-start.10 = (bf16[128,128]{1,0:T(8,128)(2,1)S(1)}, bf16[128,128]{1,0:T(8,128)(2,1)S(1)}, u32[]{:S(2)}, u32[]{:S(2)}) collective-permute-start(bf16[128,128]{1,0:T(8,128)(2,1)S(1)} %add_convert_fusion.4.refs_3_), channel_id=1, source_target_pairs={{0,8},{8,0},{16,24},{24,16},{1,9},{9,1},{17,25},{25,17},{2,10},{10... | collective-permute-start | bytes 98312 | tf_op jit(solution)/shard_map/ppermute | solution.py:339
  24.1 2.5 %collective-permute-done.7.refs_1_ = bf16[128,384]{1,0:T(8,128)(2,1)S(1)} collective-permute-done((bf16[128,384]{1,0:T(8,128)(2,1)S(1)}, bf16[128,384]{1,0:T(8,128)(2,1)S(1)}, u32[]{:S(2)}, u32[]{:S(2)}) %collective-permute-start.7) | collective-permute-done | bytes 98336 | tf_op jit(solution)/shard_map/ppermute | solution.py:339
  26.6 0.1 collective-permute-start.8
  26.7 0.2 collective-permute-done.10.refs_4_
  26.9 0.3 collective-permute-start.11
  27.3 0.9 %collective-permute-done.11.refs_5_ = bf16[256,128]{1,0:T(8,128)(2,1)S(1)} collective-permute-done((bf16[256,128]{1,0:T(8,128)(2,1)S(1)}, bf16[256,128]{1,0:T(8,128)(2,1)S(1)}, u32[]{:S(2)}, u32[]{:S(2)}) %collective-permute-start.11) | collective-permute-done | bytes 65568 | tf_op jit(solution)/shard_map/ppermute | solution.py:339
  28.2 0.0 collective-permute-done.8.refs_2_
  28.2 6.1 %shard_map.41 = (bf16[32,512]{1,0:T(8,128)(2,1)S(1)}, bf16[32,512]{1,0:T(8,128)(2,1)S(1)}) custom-call(s32[2,2]{1,0:T(2,128)} %counts_hbm.1, bf16[128,384]{1,0:T(8,128)(2,1)S(1)} %add_convert_fusion.3.refs_0_, bf16[128,384]{1,0:T(8,128)(2,1)S(1)} %collective-permute-done.7.refs_1_, bf16[256,384]{1,0:T(8,128)(2,1)S(1)} %collective-permute-done.8.refs_2_, ...), custom_call_target="tpu_custom_call" | custom-call | tf_op jit(solution)/shard_map/pallas_call | solution.py:286
  34.3 3.0 %collective-permute-start.14 = (bf16[32,512]{1,0:T(8,128)(2,1)S(1)}, bf16[32,512]{1,0:T(8,128)(2,1)S(1)}, u32[]{:S(2)}, u32[]{:S(2)}) collective-permute-start(bf16[32,512]{1,0:T(8,128)(2,1)S(1)} %get-tuple-element.33), channel_id=1, source_target_pairs={{0,5},{1,4},{4,1},{5,0},{2,7},{3,6},{6,3},{7,2},{8,13},{9,12},{12,... | collective-permute-start | bytes 98312 | tf_op jit(solution)/shard_map/ppermute | solution.py:389
  37.3 0.0 collective-permute-start.12
  37.3 0.6 %collective-permute-start.13 = (bf16[32,512]{1,0:T(8,128)(2,1)S(1)}, bf16[32,512]{1,0:T(8,128)(2,1)S(1)}, u32[]{:S(2)}, u32[]{:S(2)}) collective-permute-start(bf16[32,512]{1,0:T(8,128)(2,1)S(1)} %get-tuple-element.34.refs_3_), channel_id=1, source_target_pairs={{0,1},{1,0},{4,5},{5,4},{2,3},{3,2},{6,7},{7,6},{8,9},{9,8},{12,13... | collective-permute-start | bytes 98312 | tf_op jit(solution)/shard_map/ppermute | solution.py:389
  38.0 1.3 %collective-permute-done.14.refs_2_ = bf16[32,512]{1,0:T(8,128)(2,1)S(1)} collective-permute-done((bf16[32,512]{1,0:T(8,128)(2,1)S(1)}, bf16[32,512]{1,0:T(8,128)(2,1)S(1)}, u32[]{:S(2)}, u32[]{:S(2)}) %collective-permute-start.14) | collective-permute-done | bytes 32800 | tf_op jit(solution)/shard_map/ppermute | solution.py:389
  39.2 2.0 %collective-permute-done.12.refs_0_ = bf16[32,512]{1,0:T(8,128)(2,1)S(1)} collective-permute-done((bf16[32,512]{1,0:T(8,128)(2,1)S(1)}, bf16[32,512]{1,0:T(8,128)(2,1)S(1)}, u32[]{:S(2)}, u32[]{:S(2)}) %collective-permute-start.12) | collective-permute-done | bytes 32800 | tf_op jit(solution)/shard_map/ppermute | solution.py:389
  41.3 0.0 collective-permute-done.13.refs_1_
  41.3 0.7 %shard_map.42 = bf16[4,32,512]{2,1,0:T(8,128)(2,1)} custom-call(bf16[32,512]{1,0:T(8,128)(2,1)S(1)} %collective-permute-done.12.refs_0_, bf16[32,512]{1,0:T(8,128)(2,1)S(1)} %collective-permute-done.13.refs_1_, bf16[32,512]{1,0:T(8,128)(2,1)S(1)} %collective-permute-done.14.refs_2_, bf16[32,512]{1,0:T(8,128)(2,1)S(1)} %get-tuple-element.34.refs_3_), custom_call_target="tpu_custom_call" | custom-call | tf_op jit(solution)/shard_map/pallas_call | solution.py:322
  (6 shorter events, 0.1 us)
Async XLA Ops:
  1.7 1.6 %collective-permute-start = (bf16[128,512]{1,0:T(8,128)(2,1)S(1)}, bf16[128,512]{1,0:T(8,128)(2,1)S(1)}, u32[]{:S(2)}, u32[]{:S(2)}) collective-permute-start(bf16[128,512]{1,0:T(8,128)(2,1)S(1)} %get-tuple-element.23), channel_id=1, source_target_pairs={{0,2},{2,0},{1,3},{3,1},{4,6},{6,4},{5,7},{7,5},{8,10},{10,8},{9,1... | collective-permute-start | bytes 393224 | tf_op jit(solution)/shard_map/ppermute | solution.py:339
  2.2 4.0 %collective-permute-start.3 = (bf16[128,512]{1,0:T(8,128)(2,1)S(1)}, bf16[128,512]{1,0:T(8,128)(2,1)S(1)}, u32[]{:S(2)}, u32[]{:S(2)}) collective-permute-start(bf16[128,512]{1,0:T(8,128)(2,1)S(1)} %get-tuple-element.28), channel_id=1, source_target_pairs={{0,2},{2,0},{1,3},{3,1},{4,6},{6,4},{5,7},{7,5},{8,10},{10,8},{9,1... | collective-permute-start | bytes 393224 | tf_op jit(solution)/shard_map/ppermute | solution.py:339
  2.7 5.4 %collective-permute-start.1 = (bf16[256,512]{1,0:T(8,128)(2,1)S(1)}, bf16[256,512]{1,0:T(8,128)(2,1)S(1)}, u32[]{:S(2)}, u32[]{:S(2)}) collective-permute-start(bf16[256,512]{1,0:T(8,128)(2,1)S(1)} %get-tuple-element.25), channel_id=1, source_target_pairs={{0,2},{2,0},{1,3},{3,1},{4,6},{6,4},{5,7},{7,5},{8,10},{10,8},{9,1... | collective-permute-start | bytes 786440 | tf_op jit(solution)/shard_map/ppermute | solution.py:339
  3.3 6.8 %collective-permute-start.5 = (bf16[128,512]{1,0:T(8,128)(2,1)S(1)}, bf16[128,512]{1,0:T(8,128)(2,1)S(1)}, u32[]{:S(2)}, u32[]{:S(2)}) collective-permute-start(bf16[128,512]{1,0:T(8,128)(2,1)S(1)} %add_convert_fusion.2.refs_0_), channel_id=1, source_target_pairs={{0,8},{8,0},{16,24},{24,16},{1,9},{9,1},{17,25},{25,17},{2,10},{10... | collective-permute-start | bytes 393224 | tf_op jit(solution)/shard_map/ppermute | solution.py:339
  6.3 8.2 %collective-permute-start.4 = (bf16[128,512]{1,0:T(8,128)(2,1)S(1)}, bf16[128,512]{1,0:T(8,128)(2,1)S(1)}, u32[]{:S(2)}, u32[]{:S(2)}) collective-permute-start(bf16[128,512]{1,0:T(8,128)(2,1)S(1)} %add_convert_fusion), channel_id=1, source_target_pairs={{0,4},{4,0},{1,5},{5,1},{2,6},{6,2},{3,7},{7,3},{8,12},{12,8},{9,1... | collective-permute-start | bytes 393224 | tf_op jit(solution)/shard_map/ppermute | solution.py:339
  8.2 6.2 %collective-permute-start.2 = (bf16[128,512]{1,0:T(8,128)(2,1)S(1)}, bf16[128,512]{1,0:T(8,128)(2,1)S(1)}, u32[]{:S(2)}, u32[]{:S(2)}) collective-permute-start(bf16[128,512]{1,0:T(8,128)(2,1)S(1)} %get-tuple-element.35), channel_id=1, source_target_pairs={{0,12},{4,8},{8,4},{12,0},{16,28},{20,24},{24,20},{28,16},{1,13},{... | collective-permute-start | bytes 393224 | tf_op jit(solution)/shard_map/ppermute | solution.py:343
  14.5 7.3 %collective-permute-start.6 = (bf16[128,384]{1,0:T(8,128)(2,1)S(1)}, bf16[128,384]{1,0:T(8,128)(2,1)S(1)}, u32[]{:S(2)}, u32[]{:S(2)}) collective-permute-start(bf16[128,384]{1,0:T(8,128)(2,1)S(1)} %get-tuple-element.30), channel_id=1, source_target_pairs={{0,16},{8,24},{16,0},{24,8},{1,17},{9,25},{17,1},{25,9},{2,18},{10... | collective-permute-start | bytes 294920 | tf_op jit(solution)/shard_map/ppermute | solution.py:339
  17.2 5.6 %collective-permute-start.9 = (bf16[128,128]{1,0:T(8,128)(2,1)S(1)}, bf16[128,128]{1,0:T(8,128)(2,1)S(1)}, u32[]{:S(2)}, u32[]{:S(2)}) collective-permute-start(bf16[128,128]{1,0:T(8,128)(2,1)S(1)} %get-tuple-element.32), channel_id=1, source_target_pairs={{0,16},{8,24},{16,0},{24,8},{1,17},{9,25},{17,1},{25,9},{2,18},{10... | collective-permute-start | bytes 98312 | tf_op jit(solution)/shard_map/ppermute | solution.py:339
  21.9 4.7 %collective-permute-start.7 = (bf16[128,384]{1,0:T(8,128)(2,1)S(1)}, bf16[128,384]{1,0:T(8,128)(2,1)S(1)}, u32[]{:S(2)}, u32[]{:S(2)}) collective-permute-start(bf16[128,384]{1,0:T(8,128)(2,1)S(1)} %add_convert_fusion.3.refs_0_), channel_id=1, source_target_pairs={{0,8},{8,0},{16,24},{24,16},{1,9},{9,1},{17,25},{25,17},{2,10},{10... | collective-permute-start | bytes 294920 | tf_op jit(solution)/shard_map/ppermute | solution.py:339
  22.8 4.2 %collective-permute-start.10 = (bf16[128,128]{1,0:T(8,128)(2,1)S(1)}, bf16[128,128]{1,0:T(8,128)(2,1)S(1)}, u32[]{:S(2)}, u32[]{:S(2)}) collective-permute-start(bf16[128,128]{1,0:T(8,128)(2,1)S(1)} %add_convert_fusion.4.refs_3_), channel_id=1, source_target_pairs={{0,8},{8,0},{16,24},{24,16},{1,9},{9,1},{17,25},{25,17},{2,10},{10... | collective-permute-start | bytes 98312 | tf_op jit(solution)/shard_map/ppermute | solution.py:339
  26.6 1.6 %collective-permute-start.8 = (bf16[256,384]{1,0:T(8,128)(2,1)S(1)}, bf16[256,384]{1,0:T(8,128)(2,1)S(1)}, u32[]{:S(2)}, u32[]{:S(2)}) collective-permute-start(bf16[256,384]{1,0:T(8,128)(2,1)S(1)} %pad_maximum_fusion), channel_id=1, source_target_pairs={{0,2},{2,0},{1,3},{3,1},{4,6},{6,4},{5,7},{7,5},{8,10},{10,8},{9,1... | collective-permute-start | bytes 589832 | tf_op jit(solution)/shard_map/ppermute | solution.py:339
  26.9 1.3 %collective-permute-start.11 = (bf16[256,128]{1,0:T(8,128)(2,1)S(1)}, bf16[256,128]{1,0:T(8,128)(2,1)S(1)}, u32[]{:S(2)}, u32[]{:S(2)}) collective-permute-start(bf16[256,128]{1,0:T(8,128)(2,1)S(1)} %pad_maximum_fusion.1), channel_id=1, source_target_pairs={{0,2},{2,0},{1,3},{3,1},{4,6},{6,4},{5,7},{7,5},{8,10},{10,8},{9,1... | collective-permute-start | bytes 196616 | tf_op jit(solution)/shard_map/ppermute | solution.py:339
  34.3 4.9 %collective-permute-start.14 = (bf16[32,512]{1,0:T(8,128)(2,1)S(1)}, bf16[32,512]{1,0:T(8,128)(2,1)S(1)}, u32[]{:S(2)}, u32[]{:S(2)}) collective-permute-start(bf16[32,512]{1,0:T(8,128)(2,1)S(1)} %get-tuple-element.33), channel_id=1, source_target_pairs={{0,5},{1,4},{4,1},{5,0},{2,7},{3,6},{6,3},{7,2},{8,13},{9,12},{12,... | collective-permute-start | bytes 98312 | tf_op jit(solution)/shard_map/ppermute | solution.py:389
  37.3 3.9 %collective-permute-start.12 = (bf16[32,512]{1,0:T(8,128)(2,1)S(1)}, bf16[32,512]{1,0:T(8,128)(2,1)S(1)}, u32[]{:S(2)}, u32[]{:S(2)}) collective-permute-start(bf16[32,512]{1,0:T(8,128)(2,1)S(1)} %get-tuple-element.33), channel_id=1, source_target_pairs={{0,4},{1,5},{4,0},{5,1},{2,6},{3,7},{6,2},{7,3},{8,12},{9,13},{12,... | collective-permute-start | bytes 98312 | tf_op jit(solution)/shard_map/ppermute | solution.py:389
  37.3 3.9 %collective-permute-start.13 = (bf16[32,512]{1,0:T(8,128)(2,1)S(1)}, bf16[32,512]{1,0:T(8,128)(2,1)S(1)}, u32[]{:S(2)}, u32[]{:S(2)}) collective-permute-start(bf16[32,512]{1,0:T(8,128)(2,1)S(1)} %get-tuple-element.34.refs_3_), channel_id=1, source_target_pairs={{0,1},{1,0},{4,5},{5,4},{2,3},{3,2},{6,7},{7,6},{8,9},{9,8},{12,13... | collective-permute-start | bytes 98312 | tf_op jit(solution)/shard_map/ppermute | solution.py:389

commit v30 on v29

--- a/solution.py
+++ b/solution.py
@@ -267,10 +267,11 @@
             tiles = (dot(fourth[low, :], moment_ref[:, low]), by_high[low], by_high[high])
             if index < most - 1:
                 fill(moment_ref, 0, tiles)
+            elif ref is right:
+                final_left = dot(left[:picked, :], left[picked:, :]).astype(BF16)
+                final_left = jnp.where(most <= count_left, final_left, left[:picked, :])
+                partial_value = dot(final_left, grad[...]).astype(BF16)
             fill(ref, start, factor(tiles))
-    final_left = dot(left[:picked, :], left[picked:, :]).astype(BF16)
-    final_left = jnp.where(most <= count_left, final_left, left[:picked, :])
-    partial_value = dot(final_left, grad[...]).astype(BF16)
     update = dot(partial_value[:, low], right[half:width, :]) + dot(
         partial_value[:, high], right[:half, :]
     )

time: 42.1 us -> 42.1 us (level)
  no operation moved by 1% of the time
where the time goes in v30:
time: 42.1 us; the launch traced here: 41.9 us
  waiting for transfers between devices  17.4 us (41%)
  starting transfers between devices  15 us (36%)
  Pallas kernels  9.26 us (22%)
    ppermute x11, waiting for transfers between devices, swap(): lax.ppermute(array, axis, [(i, i ^ mask) for i in range(lax.axis_size(axi...  14.1 us
    ppermute x11, starting transfers between devices, swap(): lax.ppermute(array, axis, [(i, i ^ mask) for i in range(lax.axis_size(axi...  11.1 us
    pallas_call x1, Pallas kernels, root(): pl.pallas_call(functools.partial(root_kernel, most), out_shape=[out, out]...  6.06 us
    ppermute x3, starting transfers between devices, pass_on(): return lax.ppermute(send if flip else keep, ('x', 'group'), moves)  3.69 us
    ppermute x3, waiting for transfers between devices, pass_on(): return lax.ppermute(send if flip else keep, ('x', 'group'), moves)  3.27 us
    pallas_call x1, Pallas kernels, load(): pl.pallas_call(functools.partial(load_kernel, scale), out_shape=[jax.Shap...  1.67 us
  transfers between devices with their start and end apart: 15, of which 8 were waited for; matrix products, arithmetic and copies ran while one was open for 0% of the time, Pallas kernels for 2%

profile of v30, /device:TPU:0, one launch (start us, length us, event | category | flops | bytes accessed | tf_op | source)
XLA Modules:
  0.0 41.9 jit_solution(2657314074550980540)
XLA Ops:
  0.0 1.7 %shard_map.37 = (bf16[128,512]{1,0:T(8,128)(2,1)S(1)}, bf16[128,512]{1,0:T(8,128)(2,1)S(1)}, bf16[2,2,512,256]{3,2,1,0:T(8,128)(2,1)S(1)}, bf16[2,512,512]{2,1,0:T(8,128)(2,1)S(1)}) custom-call(bf16[2,512,512]{2,1,0:T(8,128)(2,1)} %patch_hbm.1, bf16[2,512,512]{2,1,0:T(8,128)(2,1)} %cot_hbm.1), custom_call_target="tpu_custom_call" | custom-call | tf_op jit(solution)/shard_map/pallas_call | solution.py:70
  1.7 0.5 %collective-permute-start = (bf16[128,512]{1,0:T(8,128)(2,1)S(1)}, bf16[128,512]{1,0:T(8,128)(2,1)S(1)}, u32[]{:S(2)}, u32[]{:S(2)}) collective-permute-start(bf16[128,512]{1,0:T(8,128)(2,1)S(1)} %get-tuple-element.23), channel_id=1, source_target_pairs={{0,2},{2,0},{1,3},{3,1},{4,6},{6,4},{5,7},{7,5},{8,10},{10,8},{9,1... | collective-permute-start | bytes 393224 | tf_op jit(solution)/shard_map/ppermute | solution.py:340
  2.2 0.1 collective-permute-start.3
  2.3 0.5 %shard_map.38 = (f32[128,512]{1,0:T(8,128)S(1)}, f32[128,512]{1,0:T(8,128)S(1)}, bf16[256,512]{1,0:T(8,128)(2,1)S(1)}) custom-call(bf16[2,2,512,256]{3,2,1,0:T(8,128)(2,1)S(1)} %get-tuple-element.20.patch, bf16[2,512,512]{2,1,0:T(8,128)(2,1)S(1)} %get-tuple-element.21.cot), custom_call_target="tpu_custom_call" | custom-call | flops 402653184 | bytes 1048576 | tf_op jit(solution)/shard_map/pallas_call | solution.py:98
  2.7 0.5 %collective-permute-start.1 = (bf16[256,512]{1,0:T(8,128)(2,1)S(1)}, bf16[256,512]{1,0:T(8,128)(2,1)S(1)}, u32[]{:S(2)}, u32[]{:S(2)}) collective-permute-start(bf16[256,512]{1,0:T(8,128)(2,1)S(1)} %get-tuple-element.25), channel_id=1, source_target_pairs={{0,2},{2,0},{1,3},{3,1},{4,6},{6,4},{5,7},{7,5},{8,10},{10,8},{9,1... | collective-permute-start | bytes 786440 | tf_op jit(solution)/shard_map/ppermute | solution.py:340
  3.2 0.0 collective-permute-done
  3.3 2.9 %collective-permute-start.5 = (bf16[128,512]{1,0:T(8,128)(2,1)S(1)}, bf16[128,512]{1,0:T(8,128)(2,1)S(1)}, u32[]{:S(2)}, u32[]{:S(2)}) collective-permute-start(bf16[128,512]{1,0:T(8,128)(2,1)S(1)} %add_convert_fusion.2.refs_0_), channel_id=1, source_target_pairs={{0,8},{8,0},{16,24},{24,16},{1,9},{9,1},{17,25},{25,17},{2,10},{10... | collective-permute-start | bytes 393224 | tf_op jit(solution)/shard_map/ppermute | solution.py:340
  6.2 0.0 collective-permute-done.3
  6.3 1.6 %collective-permute-start.4 = (bf16[128,512]{1,0:T(8,128)(2,1)S(1)}, bf16[128,512]{1,0:T(8,128)(2,1)S(1)}, u32[]{:S(2)}, u32[]{:S(2)}) collective-permute-start(bf16[128,512]{1,0:T(8,128)(2,1)S(1)} %add_convert_fusion), channel_id=1, source_target_pairs={{0,4},{4,0},{1,5},{5,1},{2,6},{6,2},{3,7},{7,3},{8,12},{12,8},{9,1... | collective-permute-start | bytes 393224 | tf_op jit(solution)/shard_map/ppermute | solution.py:340
  7.8 0.3 shard_map.39
  8.1 0.0 collective-permute-done.1
  8.1 0.1 add_convert_fusion.1
  8.2 0.2 collective-permute-start.2
  8.4 1.7 %collective-permute-done.5.refs_2_ = bf16[128,512]{1,0:T(8,128)(2,1)S(1)} collective-permute-done((bf16[128,512]{1,0:T(8,128)(2,1)S(1)}, bf16[128,512]{1,0:T(8,128)(2,1)S(1)}, u32[]{:S(2)}, u32[]{:S(2)}) %collective-permute-start.5) | collective-permute-done | bytes 131104 | tf_op jit(solution)/shard_map/ppermute | solution.py:340
  10.1 4.4 %collective-permute-done.4.refs_1_ = bf16[128,512]{1,0:T(8,128)(2,1)S(1)} collective-permute-done((bf16[128,512]{1,0:T(8,128)(2,1)S(1)}, bf16[128,512]{1,0:T(8,128)(2,1)S(1)}, u32[]{:S(2)}, u32[]{:S(2)}) %collective-permute-start.4) | collective-permute-done | bytes 131104 | tf_op jit(solution)/shard_map/ppermute | solution.py:340
  14.5 0.0 collective-permute-done.2.refs_0_
  14.5 0.1 shard_map.40
  14.5 2.7 %collective-permute-start.6 = (bf16[128,384]{1,0:T(8,128)(2,1)S(1)}, bf16[128,384]{1,0:T(8,128)(2,1)S(1)}, u32[]{:S(2)}, u32[]{:S(2)}) collective-permute-start(bf16[128,384]{1,0:T(8,128)(2,1)S(1)} %get-tuple-element.30), channel_id=1, source_target_pairs={{0,16},{8,24},{16,0},{24,8},{1,17},{9,25},{17,1},{25,9},{2,18},{10... | collective-permute-start | bytes 294920 | tf_op jit(solution)/shard_map/ppermute | solution.py:340
  17.2 0.3 collective-permute-start.9
  17.5 4.4 %collective-permute-done.6 = bf16[128,384]{1,0:T(8,128)(2,1)S(1)} collective-permute-done((bf16[128,384]{1,0:T(8,128)(2,1)S(1)}, bf16[128,384]{1,0:T(8,128)(2,1)S(1)}, u32[]{:S(2)}, u32[]{:S(2)}) %collective-permute-start.6) | collective-permute-done | bytes 98336 | tf_op jit(solution)/shard_map/ppermute | solution.py:340
  21.9 0.8 %collective-permute-start.7 = (bf16[128,384]{1,0:T(8,128)(2,1)S(1)}, bf16[128,384]{1,0:T(8,128)(2,1)S(1)}, u32[]{:S(2)}, u32[]{:S(2)}) collective-permute-start(bf16[128,384]{1,0:T(8,128)(2,1)S(1)} %add_convert_fusion.3.refs_0_), channel_id=1, source_target_pairs={{0,8},{8,0},{16,24},{24,16},{1,9},{9,1},{17,25},{25,17},{2,10},{10... | collective-permute-start | bytes 294920 | tf_op jit(solution)/shard_map/ppermute | solution.py:340
  22.7 0.0 collective-permute-done.9
  22.8 1.3 %collective-permute-start.10 = (bf16[128,128]{1,0:T(8,128)(2,1)S(1)}, bf16[128,128]{1,0:T(8,128)(2,1)S(1)}, u32[]{:S(2)}, u32[]{:S(2)}) collective-permute-start(bf16[128,128]{1,0:T(8,128)(2,1)S(1)} %add_convert_fusion.4.refs_3_), channel_id=1, source_target_pairs={{0,8},{8,0},{16,24},{24,16},{1,9},{9,1},{17,25},{25,17},{2,10},{10... | collective-permute-start | bytes 98312 | tf_op jit(solution)/shard_map/ppermute | solution.py:340
  24.1 2.5 %collective-permute-done.7.refs_1_ = bf16[128,384]{1,0:T(8,128)(2,1)S(1)} collective-permute-done((bf16[128,384]{1,0:T(8,128)(2,1)S(1)}, bf16[128,384]{1,0:T(8,128)(2,1)S(1)}, u32[]{:S(2)}, u32[]{:S(2)}) %collective-permute-start.7) | collective-permute-done | bytes 98336 | tf_op jit(solution)/shard_map/ppermute | solution.py:340
  26.6 0.1 collective-permute-start.8
  26.7 0.2 collective-permute-done.10.refs_4_
  26.9 0.3 collective-permute-start.11
  27.3 0.9 %collective-permute-done.11.refs_5_ = bf16[256,128]{1,0:T(8,128)(2,1)S(1)} collective-permute-done((bf16[256,128]{1,0:T(8,128)(2,1)S(1)}, bf16[256,128]{1,0:T(8,128)(2,1)S(1)}, u32[]{:S(2)}, u32[]{:S(2)}) %collective-permute-start.11) | collective-permute-done | bytes 65568 | tf_op jit(solution)/shard_map/ppermute | solution.py:340
  28.2 0.0 collective-permute-done.8.refs_2_
  28.2 6.1 %shard_map.41 = (bf16[32,512]{1,0:T(8,128)(2,1)S(1)}, bf16[32,512]{1,0:T(8,128)(2,1)S(1)}) custom-call(s32[2,2]{1,0:T(2,128)} %counts_hbm.1, bf16[128,384]{1,0:T(8,128)(2,1)S(1)} %add_convert_fusion.3.refs_0_, bf16[128,384]{1,0:T(8,128)(2,1)S(1)} %collective-permute-done.7.refs_1_, bf16[256,384]{1,0:T(8,128)(2,1)S(1)} %collective-permute-done.8.refs_2_, ...), custom_call_target="tpu_custom_call" | custom-call | tf_op jit(solution)/shard_map/pallas_call | solution.py:287
  34.3 3.0 %collective-permute-start.14 = (bf16[32,512]{1,0:T(8,128)(2,1)S(1)}, bf16[32,512]{1,0:T(8,128)(2,1)S(1)}, u32[]{:S(2)}, u32[]{:S(2)}) collective-permute-start(bf16[32,512]{1,0:T(8,128)(2,1)S(1)} %get-tuple-element.33), channel_id=1, source_target_pairs={{0,5},{1,4},{4,1},{5,0},{2,7},{3,6},{6,3},{7,2},{8,13},{9,12},{12,... | collective-permute-start | bytes 98312 | tf_op jit(solution)/shard_map/ppermute | solution.py:390
  37.3 0.0 collective-permute-start.12
  37.3 0.6 %collective-permute-start.13 = (bf16[32,512]{1,0:T(8,128)(2,1)S(1)}, bf16[32,512]{1,0:T(8,128)(2,1)S(1)}, u32[]{:S(2)}, u32[]{:S(2)}) collective-permute-start(bf16[32,512]{1,0:T(8,128)(2,1)S(1)} %get-tuple-element.34.refs_3_), channel_id=1, source_target_pairs={{0,1},{1,0},{4,5},{5,4},{2,3},{3,2},{6,7},{7,6},{8,9},{9,8},{12,13... | collective-permute-start | bytes 98312 | tf_op jit(solution)/shard_map/ppermute | solution.py:390
  38.0 1.3 %collective-permute-done.14.refs_2_ = bf16[32,512]{1,0:T(8,128)(2,1)S(1)} collective-permute-done((bf16[32,512]{1,0:T(8,128)(2,1)S(1)}, bf16[32,512]{1,0:T(8,128)(2,1)S(1)}, u32[]{:S(2)}, u32[]{:S(2)}) %collective-permute-start.14) | collective-permute-done | bytes 32800 | tf_op jit(solution)/shard_map/ppermute | solution.py:390
  39.2 2.0 %collective-permute-done.12.refs_0_ = bf16[32,512]{1,0:T(8,128)(2,1)S(1)} collective-permute-done((bf16[32,512]{1,0:T(8,128)(2,1)S(1)}, bf16[32,512]{1,0:T(8,128)(2,1)S(1)}, u32[]{:S(2)}, u32[]{:S(2)}) %collective-permute-start.12) | collective-permute-done | bytes 32800 | tf_op jit(solution)/shard_map/ppermute | solution.py:390
  41.3 0.0 collective-permute-done.13.refs_1_
  41.3 0.7 %shard_map.42 = bf16[4,32,512]{2,1,0:T(8,128)(2,1)} custom-call(bf16[32,512]{1,0:T(8,128)(2,1)S(1)} %collective-permute-done.12.refs_0_, bf16[32,512]{1,0:T(8,128)(2,1)S(1)} %collective-permute-done.13.refs_1_, bf16[32,512]{1,0:T(8,128)(2,1)S(1)} %collective-permute-done.14.refs_2_, bf16[32,512]{1,0:T(8,128)(2,1)S(1)} %get-tuple-element.34.refs_3_), custom_call_target="tpu_custom_call" | custom-call | tf_op jit(solution)/shard_map/pallas_call | solution.py:323
  (6 shorter events, 0.1 us)
Async XLA Ops:
  1.7 1.6 %collective-permute-start = (bf16[128,512]{1,0:T(8,128)(2,1)S(1)}, bf16[128,512]{1,0:T(8,128)(2,1)S(1)}, u32[]{:S(2)}, u32[]{:S(2)}) collective-permute-start(bf16[128,512]{1,0:T(8,128)(2,1)S(1)} %get-tuple-element.23), channel_id=1, source_target_pairs={{0,2},{2,0},{1,3},{3,1},{4,6},{6,4},{5,7},{7,5},{8,10},{10,8},{9,1... | collective-permute-start | bytes 393224 | tf_op jit(solution)/shard_map/ppermute | solution.py:340
  2.2 4.0 %collective-permute-start.3 = (bf16[128,512]{1,0:T(8,128)(2,1)S(1)}, bf16[128,512]{1,0:T(8,128)(2,1)S(1)}, u32[]{:S(2)}, u32[]{:S(2)}) collective-permute-start(bf16[128,512]{1,0:T(8,128)(2,1)S(1)} %get-tuple-element.28), channel_id=1, source_target_pairs={{0,2},{2,0},{1,3},{3,1},{4,6},{6,4},{5,7},{7,5},{8,10},{10,8},{9,1... | collective-permute-start | bytes 393224 | tf_op jit(solution)/shard_map/ppermute | solution.py:340
  2.7 5.4 %collective-permute-start.1 = (bf16[256,512]{1,0:T(8,128)(2,1)S(1)}, bf16[256,512]{1,0:T(8,128)(2,1)S(1)}, u32[]{:S(2)}, u32[]{:S(2)}) collective-permute-start(bf16[256,512]{1,0:T(8,128)(2,1)S(1)} %get-tuple-element.25), channel_id=1, source_target_pairs={{0,2},{2,0},{1,3},{3,1},{4,6},{6,4},{5,7},{7,5},{8,10},{10,8},{9,1... | collective-permute-start | bytes 786440 | tf_op jit(solution)/shard_map/ppermute | solution.py:340
  3.3 6.8 %collective-permute-start.5 = (bf16[128,512]{1,0:T(8,128)(2,1)S(1)}, bf16[128,512]{1,0:T(8,128)(2,1)S(1)}, u32[]{:S(2)}, u32[]{:S(2)}) collective-permute-start(bf16[128,512]{1,0:T(8,128)(2,1)S(1)} %add_convert_fusion.2.refs_0_), channel_id=1, source_target_pairs={{0,8},{8,0},{16,24},{24,16},{1,9},{9,1},{17,25},{25,17},{2,10},{10... | collective-permute-start | bytes 393224 | tf_op jit(solution)/shard_map/ppermute | solution.py:340
  6.3 8.2 %collective-permute-start.4 = (bf16[128,512]{1,0:T(8,128)(2,1)S(1)}, bf16[128,512]{1,0:T(8,128)(2,1)S(1)}, u32[]{:S(2)}, u32[]{:S(2)}) collective-permute-start(bf16[128,512]{1,0:T(8,128)(2,1)S(1)} %add_convert_fusion), channel_id=1, source_target_pairs={{0,4},{4,0},{1,5},{5,1},{2,6},{6,2},{3,7},{7,3},{8,12},{12,8},{9,1... | collective-permute-start | bytes 393224 | tf_op jit(solution)/shard_map/ppermute | solution.py:340
  8.2 6.2 %collective-permute-start.2 = (bf16[128,512]{1,0:T(8,128)(2,1)S(1)}, bf16[128,512]{1,0:T(8,128)(2,1)S(1)}, u32[]{:S(2)}, u32[]{:S(2)}) collective-permute-start(bf16[128,512]{1,0:T(8,128)(2,1)S(1)} %get-tuple-element.35), channel_id=1, source_target_pairs={{0,12},{4,8},{8,4},{12,0},{16,28},{20,24},{24,20},{28,16},{1,13},{... | collective-permute-start | bytes 393224 | tf_op jit(solution)/shard_map/ppermute | solution.py:344
  14.5 7.3 %collective-permute-start.6 = (bf16[128,384]{1,0:T(8,128)(2,1)S(1)}, bf16[128,384]{1,0:T(8,128)(2,1)S(1)}, u32[]{:S(2)}, u32[]{:S(2)}) collective-permute-start(bf16[128,384]{1,0:T(8,128)(2,1)S(1)} %get-tuple-element.30), channel_id=1, source_target_pairs={{0,16},{8,24},{16,0},{24,8},{1,17},{9,25},{17,1},{25,9},{2,18},{10... | collective-permute-start | bytes 294920 | tf_op jit(solution)/shard_map/ppermute | solution.py:340
  17.2 5.6 %collective-permute-start.9 = (bf16[128,128]{1,0:T(8,128)(2,1)S(1)}, bf16[128,128]{1,0:T(8,128)(2,1)S(1)}, u32[]{:S(2)}, u32[]{:S(2)}) collective-permute-start(bf16[128,128]{1,0:T(8,128)(2,1)S(1)} %get-tuple-element.32), channel_id=1, source_target_pairs={{0,16},{8,24},{16,0},{24,8},{1,17},{9,25},{17,1},{25,9},{2,18},{10... | collective-permute-start | bytes 98312 | tf_op jit(solution)/shard_map/ppermute | solution.py:340
  21.9 4.7 %collective-permute-start.7 = (bf16[128,384]{1,0:T(8,128)(2,1)S(1)}, bf16[128,384]{1,0:T(8,128)(2,1)S(1)}, u32[]{:S(2)}, u32[]{:S(2)}) collective-permute-start(bf16[128,384]{1,0:T(8,128)(2,1)S(1)} %add_convert_fusion.3.refs_0_), channel_id=1, source_target_pairs={{0,8},{8,0},{16,24},{24,16},{1,9},{9,1},{17,25},{25,17},{2,10},{10... | collective-permute-start | bytes 294920 | tf_op jit(solution)/shard_map/ppermute | solution.py:340
  22.8 4.2 %collective-permute-start.10 = (bf16[128,128]{1,0:T(8,128)(2,1)S(1)}, bf16[128,128]{1,0:T(8,128)(2,1)S(1)}, u32[]{:S(2)}, u32[]{:S(2)}) collective-permute-start(bf16[128,128]{1,0:T(8,128)(2,1)S(1)} %add_convert_fusion.4.refs_3_), channel_id=1, source_target_pairs={{0,8},{8,0},{16,24},{24,16},{1,9},{9,1},{17,25},{25,17},{2,10},{10... | collective-permute-start | bytes 98312 | tf_op jit(solution)/shard_map/ppermute | solution.py:340
  26.6 1.6 %collective-permute-start.8 = (bf16[256,384]{1,0:T(8,128)(2,1)S(1)}, bf16[256,384]{1,0:T(8,128)(2,1)S(1)}, u32[]{:S(2)}, u32[]{:S(2)}) collective-permute-start(bf16[256,384]{1,0:T(8,128)(2,1)S(1)} %pad_maximum_fusion), channel_id=1, source_target_pairs={{0,2},{2,0},{1,3},{3,1},{4,6},{6,4},{5,7},{7,5},{8,10},{10,8},{9,1... | collective-permute-start | bytes 589832 | tf_op jit(solution)/shard_map/ppermute | solution.py:340
  26.9 1.3 %collective-permute-start.11 = (bf16[256,128]{1,0:T(8,128)(2,1)S(1)}, bf16[256,128]{1,0:T(8,128)(2,1)S(1)}, u32[]{:S(2)}, u32[]{:S(2)}) collective-permute-start(bf16[256,128]{1,0:T(8,128)(2,1)S(1)} %pad_maximum_fusion.1), channel_id=1, source_target_pairs={{0,2},{2,0},{1,3},{3,1},{4,6},{6,4},{5,7},{7,5},{8,10},{10,8},{9,1... | collective-permute-start | bytes 196616 | tf_op jit(solution)/shard_map/ppermute | solution.py:340
  34.3 4.9 %collective-permute-start.14 = (bf16[32,512]{1,0:T(8,128)(2,1)S(1)}, bf16[32,512]{1,0:T(8,128)(2,1)S(1)}, u32[]{:S(2)}, u32[]{:S(2)}) collective-permute-start(bf16[32,512]{1,0:T(8,128)(2,1)S(1)} %get-tuple-element.33), channel_id=1, source_target_pairs={{0,5},{1,4},{4,1},{5,0},{2,7},{3,6},{6,3},{7,2},{8,13},{9,12},{12,... | collective-permute-start | bytes 98312 | tf_op jit(solution)/shard_map/ppermute | solution.py:390
  37.3 3.9 %collective-permute-start.12 = (bf16[32,512]{1,0:T(8,128)(2,1)S(1)}, bf16[32,512]{1,0:T(8,128)(2,1)S(1)}, u32[]{:S(2)}, u32[]{:S(2)}) collective-permute-start(bf16[32,512]{1,0:T(8,128)(2,1)S(1)} %get-tuple-element.33), channel_id=1, source_target_pairs={{0,4},{1,5},{4,0},{5,1},{2,6},{3,7},{6,2},{7,3},{8,12},{9,13},{12,... | collective-permute-start | bytes 98312 | tf_op jit(solution)/shard_map/ppermute | solution.py:390
  37.3 3.9 %collective-permute-start.13 = (bf16[32,512]{1,0:T(8,128)(2,1)S(1)}, bf16[32,512]{1,0:T(8,128)(2,1)S(1)}, u32[]{:S(2)}, u32[]{:S(2)}) collective-permute-start(bf16[32,512]{1,0:T(8,128)(2,1)S(1)} %get-tuple-element.34.refs_3_), channel_id=1, source_target_pairs={{0,1},{1,0},{4,5},{5,4},{2,3},{3,2},{6,7},{7,6},{8,9},{9,8},{12,13... | collective-permute-start | bytes 98312 | tf_op jit(solution)/shard_map/ppermute | solution.py:390

commit v31 on v29

--- a/solution.py
+++ b/solution.py
@@ -230,8 +230,9 @@
     for index in range(1, most):
         q_left, q_right = left.at[picked:, :], right.at[width:, :]
         if index == 1:
-            fill(s_left, 0, square(q_left))
-            fill(s_right, 0, square(q_right))
+            seconds = square(q_left), square(q_right)
+            fill(s_left, 0, seconds[0])
+            fill(s_right, 0, seconds[1])
         else:
             by_high = dot(left[...], q_left[:, high])
             by_low = dot(left[: picked + half, :], q_left[:, low])

time: 42.1 us -> 42.1 us (level)
  no operation moved by 1% of the time
where the time goes in v31:
time: 42.1 us; the launch traced here: 41.9 us
  waiting for transfers between devices  17.4 us (41%)
  starting transfers between devices  15 us (36%)
  Pallas kernels  9.26 us (22%)
    ppermute x11, waiting for transfers between devices, swap(): lax.ppermute(array, axis, [(i, i ^ mask) for i in range(lax.axis_size(axi...  14.1 us
    ppermute x11, starting transfers between devices, swap(): lax.ppermute(array, axis, [(i, i ^ mask) for i in range(lax.axis_size(axi...  11.1 us
    pallas_call x1, Pallas kernels, root(): pl.pallas_call(functools.partial(root_kernel, most), out_shape=[out, out]...  6.06 us
    ppermute x3, starting transfers between devices, pass_on(): return lax.ppermute(send if flip else keep, ('x', 'group'), moves)  3.69 us
    ppermute x3, waiting for transfers between devices, pass_on(): return lax.ppermute(send if flip else keep, ('x', 'group'), moves)  3.27 us
    pallas_call x1, Pallas kernels, load(): pl.pallas_call(functools.partial(load_kernel, scale), out_shape=[jax.Shap...  1.67 us
  transfers between devices with their start and end apart: 15, of which 8 were waited for; matrix products, arithmetic and copies ran while one was open for 0% of the time, Pallas kernels for 2%

profile of v31, /device:TPU:0, one launch (start us, length us, event | category | flops | bytes accessed | tf_op | source)
XLA Modules:
  0.0 41.9 jit_solution(2657314074550980540)
XLA Ops:
  0.0 1.7 %shard_map.37 = (bf16[128,512]{1,0:T(8,128)(2,1)S(1)}, bf16[128,512]{1,0:T(8,128)(2,1)S(1)}, bf16[2,2,512,256]{3,2,1,0:T(8,128)(2,1)S(1)}, bf16[2,512,512]{2,1,0:T(8,128)(2,1)S(1)}) custom-call(bf16[2,512,512]{2,1,0:T(8,128)(2,1)} %patch_hbm.1, bf16[2,512,512]{2,1,0:T(8,128)(2,1)} %cot_hbm.1), custom_call_target="tpu_custom_call" | custom-call | tf_op jit(solution)/shard_map/pallas_call | solution.py:70
  1.7 0.5 %collective-permute-start = (bf16[128,512]{1,0:T(8,128)(2,1)S(1)}, bf16[128,512]{1,0:T(8,128)(2,1)S(1)}, u32[]{:S(2)}, u32[]{:S(2)}) collective-permute-start(bf16[128,512]{1,0:T(8,128)(2,1)S(1)} %get-tuple-element.23), channel_id=1, source_target_pairs={{0,2},{2,0},{1,3},{3,1},{4,6},{6,4},{5,7},{7,5},{8,10},{10,8},{9,1... | collective-permute-start | bytes 393224 | tf_op jit(solution)/shard_map/ppermute | solution.py:340
  2.2 0.1 collective-permute-start.3
  2.3 0.5 %shard_map.38 = (f32[128,512]{1,0:T(8,128)S(1)}, f32[128,512]{1,0:T(8,128)S(1)}, bf16[256,512]{1,0:T(8,128)(2,1)S(1)}) custom-call(bf16[2,2,512,256]{3,2,1,0:T(8,128)(2,1)S(1)} %get-tuple-element.20.patch, bf16[2,512,512]{2,1,0:T(8,128)(2,1)S(1)} %get-tuple-element.21.cot), custom_call_target="tpu_custom_call" | custom-call | flops 402653184 | bytes 1048576 | tf_op jit(solution)/shard_map/pallas_call | solution.py:98
  2.7 0.5 %collective-permute-start.1 = (bf16[256,512]{1,0:T(8,128)(2,1)S(1)}, bf16[256,512]{1,0:T(8,128)(2,1)S(1)}, u32[]{:S(2)}, u32[]{:S(2)}) collective-permute-start(bf16[256,512]{1,0:T(8,128)(2,1)S(1)} %get-tuple-element.25), channel_id=1, source_target_pairs={{0,2},{2,0},{1,3},{3,1},{4,6},{6,4},{5,7},{7,5},{8,10},{10,8},{9,1... | collective-permute-start | bytes 786440 | tf_op jit(solution)/shard_map/ppermute | solution.py:340
  3.2 0.0 collective-permute-done
  3.3 2.9 %collective-permute-start.5 = (bf16[128,512]{1,0:T(8,128)(2,1)S(1)}, bf16[128,512]{1,0:T(8,128)(2,1)S(1)}, u32[]{:S(2)}, u32[]{:S(2)}) collective-permute-start(bf16[128,512]{1,0:T(8,128)(2,1)S(1)} %add_convert_fusion.2.refs_0_), channel_id=1, source_target_pairs={{0,8},{8,0},{16,24},{24,16},{1,9},{9,1},{17,25},{25,17},{2,10},{10... | collective-permute-start | bytes 393224 | tf_op jit(solution)/shard_map/ppermute | solution.py:340
  6.2 0.0 collective-permute-done.3
  6.3 1.6 %collective-permute-start.4 = (bf16[128,512]{1,0:T(8,128)(2,1)S(1)}, bf16[128,512]{1,0:T(8,128)(2,1)S(1)}, u32[]{:S(2)}, u32[]{:S(2)}) collective-permute-start(bf16[128,512]{1,0:T(8,128)(2,1)S(1)} %add_convert_fusion), channel_id=1, source_target_pairs={{0,4},{4,0},{1,5},{5,1},{2,6},{6,2},{3,7},{7,3},{8,12},{12,8},{9,1... | collective-permute-start | bytes 393224 | tf_op jit(solution)/shard_map/ppermute | solution.py:340
  7.8 0.3 shard_map.39
  8.1 0.0 collective-permute-done.1
  8.1 0.1 add_convert_fusion.1
  8.2 0.2 collective-permute-start.2
  8.4 1.7 %collective-permute-done.5.refs_2_ = bf16[128,512]{1,0:T(8,128)(2,1)S(1)} collective-permute-done((bf16[128,512]{1,0:T(8,128)(2,1)S(1)}, bf16[128,512]{1,0:T(8,128)(2,1)S(1)}, u32[]{:S(2)}, u32[]{:S(2)}) %collective-permute-start.5) | collective-permute-done | bytes 131104 | tf_op jit(solution)/shard_map/ppermute | solution.py:340
  10.1 4.4 %collective-permute-done.4.refs_1_ = bf16[128,512]{1,0:T(8,128)(2,1)S(1)} collective-permute-done((bf16[128,512]{1,0:T(8,128)(2,1)S(1)}, bf16[128,512]{1,0:T(8,128)(2,1)S(1)}, u32[]{:S(2)}, u32[]{:S(2)}) %collective-permute-start.4) | collective-permute-done | bytes 131104 | tf_op jit(solution)/shard_map/ppermute | solution.py:340
  14.5 0.0 collective-permute-done.2.refs_0_
  14.5 0.1 shard_map.40
  14.5 2.7 %collective-permute-start.6 = (bf16[128,384]{1,0:T(8,128)(2,1)S(1)}, bf16[128,384]{1,0:T(8,128)(2,1)S(1)}, u32[]{:S(2)}, u32[]{:S(2)}) collective-permute-start(bf16[128,384]{1,0:T(8,128)(2,1)S(1)} %get-tuple-element.30), channel_id=1, source_target_pairs={{0,16},{8,24},{16,0},{24,8},{1,17},{9,25},{17,1},{25,9},{2,18},{10... | collective-permute-start | bytes 294920 | tf_op jit(solution)/shard_map/ppermute | solution.py:340
  17.2 0.3 collective-permute-start.9
  17.5 4.4 %collective-permute-done.6 = bf16[128,384]{1,0:T(8,128)(2,1)S(1)} collective-permute-done((bf16[128,384]{1,0:T(8,128)(2,1)S(1)}, bf16[128,384]{1,0:T(8,128)(2,1)S(1)}, u32[]{:S(2)}, u32[]{:S(2)}) %collective-permute-start.6) | collective-permute-done | bytes 98336 | tf_op jit(solution)/shard_map/ppermute | solution.py:340
  21.9 0.8 %collective-permute-start.7 = (bf16[128,384]{1,0:T(8,128)(2,1)S(1)}, bf16[128,384]{1,0:T(8,128)(2,1)S(1)}, u32[]{:S(2)}, u32[]{:S(2)}) collective-permute-start(bf16[128,384]{1,0:T(8,128)(2,1)S(1)} %add_convert_fusion.3.refs_0_), channel_id=1, source_target_pairs={{0,8},{8,0},{16,24},{24,16},{1,9},{9,1},{17,25},{25,17},{2,10},{10... | collective-permute-start | bytes 294920 | tf_op jit(solution)/shard_map/ppermute | solution.py:340
  22.7 0.0 collective-permute-done.9
  22.8 1.3 %collective-permute-start.10 = (bf16[128,128]{1,0:T(8,128)(2,1)S(1)}, bf16[128,128]{1,0:T(8,128)(2,1)S(1)}, u32[]{:S(2)}, u32[]{:S(2)}) collective-permute-start(bf16[128,128]{1,0:T(8,128)(2,1)S(1)} %add_convert_fusion.4.refs_3_), channel_id=1, source_target_pairs={{0,8},{8,0},{16,24},{24,16},{1,9},{9,1},{17,25},{25,17},{2,10},{10... | collective-permute-start | bytes 98312 | tf_op jit(solution)/shard_map/ppermute | solution.py:340
  24.1 2.5 %collective-permute-done.7.refs_1_ = bf16[128,384]{1,0:T(8,128)(2,1)S(1)} collective-permute-done((bf16[128,384]{1,0:T(8,128)(2,1)S(1)}, bf16[128,384]{1,0:T(8,128)(2,1)S(1)}, u32[]{:S(2)}, u32[]{:S(2)}) %collective-permute-start.7) | collective-permute-done | bytes 98336 | tf_op jit(solution)/shard_map/ppermute | solution.py:340
  26.6 0.1 collective-permute-start.8
  26.7 0.2 collective-permute-done.10.refs_4_
  26.9 0.3 collective-permute-start.11
  27.3 0.9 %collective-permute-done.11.refs_5_ = bf16[256,128]{1,0:T(8,128)(2,1)S(1)} collective-permute-done((bf16[256,128]{1,0:T(8,128)(2,1)S(1)}, bf16[256,128]{1,0:T(8,128)(2,1)S(1)}, u32[]{:S(2)}, u32[]{:S(2)}) %collective-permute-start.11) | collective-permute-done | bytes 65568 | tf_op jit(solution)/shard_map/ppermute | solution.py:340
  28.2 0.0 collective-permute-done.8.refs_2_
  28.2 6.1 %shard_map.41 = (bf16[32,512]{1,0:T(8,128)(2,1)S(1)}, bf16[32,512]{1,0:T(8,128)(2,1)S(1)}) custom-call(s32[2,2]{1,0:T(2,128)} %counts_hbm.1, bf16[128,384]{1,0:T(8,128)(2,1)S(1)} %add_convert_fusion.3.refs_0_, bf16[128,384]{1,0:T(8,128)(2,1)S(1)} %collective-permute-done.7.refs_1_, bf16[256,384]{1,0:T(8,128)(2,1)S(1)} %collective-permute-done.8.refs_2_, ...), custom_call_target="tpu_custom_call" | custom-call | tf_op jit(solution)/shard_map/pallas_call | solution.py:287
  34.3 3.0 %collective-permute-start.14 = (bf16[32,512]{1,0:T(8,128)(2,1)S(1)}, bf16[32,512]{1,0:T(8,128)(2,1)S(1)}, u32[]{:S(2)}, u32[]{:S(2)}) collective-permute-start(bf16[32,512]{1,0:T(8,128)(2,1)S(1)} %get-tuple-element.33), channel_id=1, source_target_pairs={{0,5},{1,4},{4,1},{5,0},{2,7},{3,6},{6,3},{7,2},{8,13},{9,12},{12,... | collective-permute-start | bytes 98312 | tf_op jit(solution)/shard_map/ppermute | solution.py:390
  37.3 0.0 collective-permute-start.12
  37.3 0.6 %collective-permute-start.13 = (bf16[32,512]{1,0:T(8,128)(2,1)S(1)}, bf16[32,512]{1,0:T(8,128)(2,1)S(1)}, u32[]{:S(2)}, u32[]{:S(2)}) collective-permute-start(bf16[32,512]{1,0:T(8,128)(2,1)S(1)} %get-tuple-element.34.refs_3_), channel_id=1, source_target_pairs={{0,1},{1,0},{4,5},{5,4},{2,3},{3,2},{6,7},{7,6},{8,9},{9,8},{12,13... | collective-permute-start | bytes 98312 | tf_op jit(solution)/shard_map/ppermute | solution.py:390
  38.0 1.3 %collective-permute-done.14.refs_2_ = bf16[32,512]{1,0:T(8,128)(2,1)S(1)} collective-permute-done((bf16[32,512]{1,0:T(8,128)(2,1)S(1)}, bf16[32,512]{1,0:T(8,128)(2,1)S(1)}, u32[]{:S(2)}, u32[]{:S(2)}) %collective-permute-start.14) | collective-permute-done | bytes 32800 | tf_op jit(solution)/shard_map/ppermute | solution.py:390
  39.2 2.0 %collective-permute-done.12.refs_0_ = bf16[32,512]{1,0:T(8,128)(2,1)S(1)} collective-permute-done((bf16[32,512]{1,0:T(8,128)(2,1)S(1)}, bf16[32,512]{1,0:T(8,128)(2,1)S(1)}, u32[]{:S(2)}, u32[]{:S(2)}) %collective-permute-start.12) | collective-permute-done | bytes 32800 | tf_op jit(solution)/shard_map/ppermute | solution.py:390
  41.3 0.0 collective-permute-done.13.refs_1_
  41.3 0.7 %shard_map.42 = bf16[4,32,512]{2,1,0:T(8,128)(2,1)} custom-call(bf16[32,512]{1,0:T(8,128)(2,1)S(1)} %collective-permute-done.12.refs_0_, bf16[32,512]{1,0:T(8,128)(2,1)S(1)} %collective-permute-done.13.refs_1_, bf16[32,512]{1,0:T(8,128)(2,1)S(1)} %collective-permute-done.14.refs_2_, bf16[32,512]{1,0:T(8,128)(2,1)S(1)} %get-tuple-element.34.refs_3_), custom_call_target="tpu_custom_call" | custom-call | tf_op jit(solution)/shard_map/pallas_call | solution.py:323
  (6 shorter events, 0.1 us)
Async XLA Ops:
  1.7 1.6 %collective-permute-start = (bf16[128,512]{1,0:T(8,128)(2,1)S(1)}, bf16[128,512]{1,0:T(8,128)(2,1)S(1)}, u32[]{:S(2)}, u32[]{:S(2)}) collective-permute-start(bf16[128,512]{1,0:T(8,128)(2,1)S(1)} %get-tuple-element.23), channel_id=1, source_target_pairs={{0,2},{2,0},{1,3},{3,1},{4,6},{6,4},{5,7},{7,5},{8,10},{10,8},{9,1... | collective-permute-start | bytes 393224 | tf_op jit(solution)/shard_map/ppermute | solution.py:340
  2.2 4.0 %collective-permute-start.3 = (bf16[128,512]{1,0:T(8,128)(2,1)S(1)}, bf16[128,512]{1,0:T(8,128)(2,1)S(1)}, u32[]{:S(2)}, u32[]{:S(2)}) collective-permute-start(bf16[128,512]{1,0:T(8,128)(2,1)S(1)} %get-tuple-element.28), channel_id=1, source_target_pairs={{0,2},{2,0},{1,3},{3,1},{4,6},{6,4},{5,7},{7,5},{8,10},{10,8},{9,1... | collective-permute-start | bytes 393224 | tf_op jit(solution)/shard_map/ppermute | solution.py:340
  2.7 5.4 %collective-permute-start.1 = (bf16[256,512]{1,0:T(8,128)(2,1)S(1)}, bf16[256,512]{1,0:T(8,128)(2,1)S(1)}, u32[]{:S(2)}, u32[]{:S(2)}) collective-permute-start(bf16[256,512]{1,0:T(8,128)(2,1)S(1)} %get-tuple-element.25), channel_id=1, source_target_pairs={{0,2},{2,0},{1,3},{3,1},{4,6},{6,4},{5,7},{7,5},{8,10},{10,8},{9,1... | collective-permute-start | bytes 786440 | tf_op jit(solution)/shard_map/ppermute | solution.py:340
  3.3 6.8 %collective-permute-start.5 = (bf16[128,512]{1,0:T(8,128)(2,1)S(1)}, bf16[128,512]{1,0:T(8,128)(2,1)S(1)}, u32[]{:S(2)}, u32[]{:S(2)}) collective-permute-start(bf16[128,512]{1,0:T(8,128)(2,1)S(1)} %add_convert_fusion.2.refs_0_), channel_id=1, source_target_pairs={{0,8},{8,0},{16,24},{24,16},{1,9},{9,1},{17,25},{25,17},{2,10},{10... | collective-permute-start | bytes 393224 | tf_op jit(solution)/shard_map/ppermute | solution.py:340
  6.3 8.2 %collective-permute-start.4 = (bf16[128,512]{1,0:T(8,128)(2,1)S(1)}, bf16[128,512]{1,0:T(8,128)(2,1)S(1)}, u32[]{:S(2)}, u32[]{:S(2)}) collective-permute-start(bf16[128,512]{1,0:T(8,128)(2,1)S(1)} %add_convert_fusion), channel_id=1, source_target_pairs={{0,4},{4,0},{1,5},{5,1},{2,6},{6,2},{3,7},{7,3},{8,12},{12,8},{9,1... | collective-permute-start | bytes 393224 | tf_op jit(solution)/shard_map/ppermute | solution.py:340
  8.2 6.2 %collective-permute-start.2 = (bf16[128,512]{1,0:T(8,128)(2,1)S(1)}, bf16[128,512]{1,0:T(8,128)(2,1)S(1)}, u32[]{:S(2)}, u32[]{:S(2)}) collective-permute-start(bf16[128,512]{1,0:T(8,128)(2,1)S(1)} %get-tuple-element.35), channel_id=1, source_target_pairs={{0,12},{4,8},{8,4},{12,0},{16,28},{20,24},{24,20},{28,16},{1,13},{... | collective-permute-start | bytes 393224 | tf_op jit(solution)/shard_map/ppermute | solution.py:344
  14.5 7.3 %collective-permute-start.6 = (bf16[128,384]{1,0:T(8,128)(2,1)S(1)}, bf16[128,384]{1,0:T(8,128)(2,1)S(1)}, u32[]{:S(2)}, u32[]{:S(2)}) collective-permute-start(bf16[128,384]{1,0:T(8,128)(2,1)S(1)} %get-tuple-element.30), channel_id=1, source_target_pairs={{0,16},{8,24},{16,0},{24,8},{1,17},{9,25},{17,1},{25,9},{2,18},{10... | collective-permute-start | bytes 294920 | tf_op jit(solution)/shard_map/ppermute | solution.py:340
  17.2 5.6 %collective-permute-start.9 = (bf16[128,128]{1,0:T(8,128)(2,1)S(1)}, bf16[128,128]{1,0:T(8,128)(2,1)S(1)}, u32[]{:S(2)}, u32[]{:S(2)}) collective-permute-start(bf16[128,128]{1,0:T(8,128)(2,1)S(1)} %get-tuple-element.32), channel_id=1, source_target_pairs={{0,16},{8,24},{16,0},{24,8},{1,17},{9,25},{17,1},{25,9},{2,18},{10... | collective-permute-start | bytes 98312 | tf_op jit(solution)/shard_map/ppermute | solution.py:340
  21.9 4.7 %collective-permute-start.7 = (bf16[128,384]{1,0:T(8,128)(2,1)S(1)}, bf16[128,384]{1,0:T(8,128)(2,1)S(1)}, u32[]{:S(2)}, u32[]{:S(2)}) collective-permute-start(bf16[128,384]{1,0:T(8,128)(2,1)S(1)} %add_convert_fusion.3.refs_0_), channel_id=1, source_target_pairs={{0,8},{8,0},{16,24},{24,16},{1,9},{9,1},{17,25},{25,17},{2,10},{10... | collective-permute-start | bytes 294920 | tf_op jit(solution)/shard_map/ppermute | solution.py:340
  22.8 4.2 %collective-permute-start.10 = (bf16[128,128]{1,0:T(8,128)(2,1)S(1)}, bf16[128,128]{1,0:T(8,128)(2,1)S(1)}, u32[]{:S(2)}, u32[]{:S(2)}) collective-permute-start(bf16[128,128]{1,0:T(8,128)(2,1)S(1)} %add_convert_fusion.4.refs_3_), channel_id=1, source_target_pairs={{0,8},{8,0},{16,24},{24,16},{1,9},{9,1},{17,25},{25,17},{2,10},{10... | collective-permute-start | bytes 98312 | tf_op jit(solution)/shard_map/ppermute | solution.py:340
  26.6 1.6 %collective-permute-start.8 = (bf16[256,384]{1,0:T(8,128)(2,1)S(1)}, bf16[256,384]{1,0:T(8,128)(2,1)S(1)}, u32[]{:S(2)}, u32[]{:S(2)}) collective-permute-start(bf16[256,384]{1,0:T(8,128)(2,1)S(1)} %pad_maximum_fusion), channel_id=1, source_target_pairs={{0,2},{2,0},{1,3},{3,1},{4,6},{6,4},{5,7},{7,5},{8,10},{10,8},{9,1... | collective-permute-start | bytes 589832 | tf_op jit(solution)/shard_map/ppermute | solution.py:340
  26.9 1.3 %collective-permute-start.11 = (bf16[256,128]{1,0:T(8,128)(2,1)S(1)}, bf16[256,128]{1,0:T(8,128)(2,1)S(1)}, u32[]{:S(2)}, u32[]{:S(2)}) collective-permute-start(bf16[256,128]{1,0:T(8,128)(2,1)S(1)} %pad_maximum_fusion.1), channel_id=1, source_target_pairs={{0,2},{2,0},{1,3},{3,1},{4,6},{6,4},{5,7},{7,5},{8,10},{10,8},{9,1... | collective-permute-start | bytes 196616 | tf_op jit(solution)/shard_map/ppermute | solution.py:340
  34.3 4.9 %collective-permute-start.14 = (bf16[32,512]{1,0:T(8,128)(2,1)S(1)}, bf16[32,512]{1,0:T(8,128)(2,1)S(1)}, u32[]{:S(2)}, u32[]{:S(2)}) collective-permute-start(bf16[32,512]{1,0:T(8,128)(2,1)S(1)} %get-tuple-element.33), channel_id=1, source_target_pairs={{0,5},{1,4},{4,1},{5,0},{2,7},{3,6},{6,3},{7,2},{8,13},{9,12},{12,... | collective-permute-start | bytes 98312 | tf_op jit(solution)/shard_map/ppermute | solution.py:390
  37.3 3.9 %collective-permute-start.12 = (bf16[32,512]{1,0:T(8,128)(2,1)S(1)}, bf16[32,512]{1,0:T(8,128)(2,1)S(1)}, u32[]{:S(2)}, u32[]{:S(2)}) collective-permute-start(bf16[32,512]{1,0:T(8,128)(2,1)S(1)} %get-tuple-element.33), channel_id=1, source_target_pairs={{0,4},{1,5},{4,0},{5,1},{2,6},{3,7},{6,2},{7,3},{8,12},{9,13},{12,... | collective-permute-start | bytes 98312 | tf_op jit(solution)/shard_map/ppermute | solution.py:390
  37.3 3.9 %collective-permute-start.13 = (bf16[32,512]{1,0:T(8,128)(2,1)S(1)}, bf16[32,512]{1,0:T(8,128)(2,1)S(1)}, u32[]{:S(2)}, u32[]{:S(2)}) collective-permute-start(bf16[32,512]{1,0:T(8,128)(2,1)S(1)} %get-tuple-element.34.refs_3_), channel_id=1, source_target_pairs={{0,1},{1,0},{4,5},{5,4},{2,3},{3,2},{6,7},{7,6},{8,9},{9,8},{12,13... | collective-permute-start | bytes 98312 | tf_op jit(solution)/shard_map/ppermute | solution.py:390
